TPU v7x, 32 devices: a whole 2x2x4 slice. The times are simulated.
32 devices in a mesh: blk: 8 (over y, x, core), grp: 4 (over z).
Axes of the slice: x: 2, y: 2, z: 4, core: 2. Of those that a mesh axis runs over, the one named last changes fastest.
Arguments:
- latent: bfloat16 [16384, 128], P(('blk', 'grp')), may hold values from -6 to 6
- positions: float32 [3, 16384], P(None, ('blk', 'grp')), may hold values from -6 to 6
- tile_send: int32 [8, 4, 16], P('blk', 'grp'), may hold values from 0 to 15, as said below
- tile_recv: int32 [8, 4, 16], P('blk', 'grp'), may hold values from 0 to 11
- tile_mask: int32 [8, 4, 16, 128, 128], P('blk', 'grp'), may hold values 0 or 1
- tile_count: int32 [8, 4], P('blk', 'grp'), may hold values from 1 to 16
- w_send: bfloat16 [128, 128], replicated, may hold values from -0.5 to 0.5
- w_recv: bfloat16 [128, 128], replicated, may hold values from -0.5 to 0.5
- pos_weight: float32 [3, 128], replicated, may hold values from -3.5 to 3.5
- edge_bias: float32 [128], replicated, may hold values from -3 to 3
- w_edge_out: bfloat16 [128, 128], replicated, may hold values from -0.125 to 0.125
- w_node_self: bfloat16 [128, 128], replicated, may hold values from -0.375 to 0.375
- w_node_msg: bfloat16 [128, 128], replicated, may hold values from -0.375 to 0.375
- node_bias: float32 [128], replicated, may hold values from -3 to 3
- w_node_out: bfloat16 [128, 128], replicated, may hold values from -0.5 to 0.5
- gain: float32 [128], replicated, may hold values from 0.5 to 1.5
- cotangent: bfloat16 [16384, 128], P(('blk', 'grp')), may hold values from -6 to 6
Outputs:
- new_latent: bfloat16 [16384, 128], P(('blk', 'grp'))
- latent_grad: float32 [16384, 128], P(('blk', 'grp'))
- weight_grads: float32 [6, 128, 128], replicated
Inputs may be any that keep to these rules, and one draw needn't show every extreme that they name: `tile_send`: the sender block of every tile lies in the same slab; tile 0 of member g names a block of member (g + 2) mod 4.
All inputs are finite; a program needn't handle non-finite values. No bound on the sum of `tile_mask` on one device may be relied on, other than what follows from the above.
Results may differ from a plain program's by a relative error of at most 0.012.
Values may be sent and summed in bfloat16 or wider, within the bound.
No kernel may reach another device: no remote copies, remote signals or barrier semaphores. Data moves between devices by JAX's collectives and lax.ppermute only.
A program may use at most 64 MiB of HBM per device.

v0:
```python
import jax
import jax.numpy as jnp
from jax import lax
from jax.sharding import PartitionSpec as P


def shifted(value, axis, steps):
    count = lax.axis_size(axis)
    pairs = [(source, (source + steps) % count) for source in range(count)]
    return lax.ppermute(value, axis, pairs)


def contract_rows(left_rows, right_rows):
    return lax.dot_general(
        left_rows, right_rows, (((0,), (0,)), ((), ())), preferred_element_type=jnp.float32
    )


def edge_forward(send_block, recv_block, edge_mask):
    size_rows = recv_block.shape[0]
    width = recv_block.shape[1]
    group_rows = min(32, size_rows)
    group_count = size_rows // group_rows
    sender_values = send_block.astype(jnp.float32)

    def one_group(pieces):
        recv_part, mask_part = pieces
        preact = recv_part.astype(jnp.float32)[:, None, :] + sender_values[None, :, :]
        summed = jnp.sum(mask_part[:, :, None] * jnp.maximum(preact, 0.0), axis=1)
        return (summed,)

    results = lax.map(
        one_group,
        (
            recv_block.reshape(group_count, group_rows, width),
            edge_mask.reshape(group_count, group_rows, size_rows),
        ),
    )
    return tuple((item.reshape(size_rows, width) for item in results))


def edge_backward(send_block, recv_block, edge_mask, grad_block):
    size_rows = recv_block.shape[0]
    width = recv_block.shape[1]
    group_rows = min(32, size_rows)
    group_count = size_rows // group_rows
    sender_values = send_block.astype(jnp.float32)

    def one_group(running, pieces):
        recv_part, mask_part, grad_part = pieces
        preact = recv_part.astype(jnp.float32)[:, None, :] + sender_values[None, :, :]
        terms = mask_part[:, :, None] * (preact > 0.0).astype(jnp.float32) * grad_part[:, None, :]
        running = running + jnp.sum(terms, axis=0)
        return (running, jnp.sum(terms, axis=1))

    pieces = (
        recv_block.reshape(group_count, group_rows, width),
        edge_mask.reshape(group_count, group_rows, size_rows),
        grad_block.reshape(group_count, group_rows, width),
    )
    send_grad, recv_grad = lax.scan(one_group, jnp.zeros((size_rows, width), jnp.float32), pieces)
    recv_grad = recv_grad.reshape(size_rows, width)
    return (send_grad, recv_grad)


def node_update(
    latent, aggregate, cotangent, w_edge_out, w_node_self, w_node_msg, node_bias, w_node_out, gain
):
    aggregate_b = aggregate.astype(jnp.bfloat16)
    message = jnp.dot(aggregate_b, w_edge_out, preferred_element_type=jnp.float32).astype(
        jnp.bfloat16
    )
    hidden_pre = (
        jnp.dot(latent, w_node_self, preferred_element_type=jnp.float32)
        + jnp.dot(message, w_node_msg, preferred_element_type=jnp.float32)
        + node_bias
    )
    logistic = jax.nn.sigmoid(hidden_pre)
    hidden = (hidden_pre * logistic).astype(jnp.bfloat16)
    update = jnp.dot(hidden, w_node_out, preferred_element_type=jnp.float32)
    average = jnp.mean(update, axis=-1, keepdims=True)
    centred = update - average
    variance = jnp.mean(centred * centred, axis=-1, keepdims=True)
    inv_std = lax.rsqrt(variance + 1e-05)
    normed = centred * inv_std
    new_latent = (latent.astype(jnp.float32) + normed * gain).astype(jnp.bfloat16)
    cot_float = cotangent.astype(jnp.float32)
    d_normed = cot_float * gain
    d_update = (
        inv_std
        * (
            d_normed
            - jnp.mean(d_normed, axis=-1, keepdims=True)
            - normed * jnp.mean(d_normed * normed, axis=-1, keepdims=True)
        )
    ).astype(jnp.bfloat16)
    d_hidden = jnp.dot(d_update, w_node_out.T, preferred_element_type=jnp.float32)
    d_hidden_pre = (d_hidden * logistic * (1.0 + hidden_pre * (1.0 - logistic))).astype(
        jnp.bfloat16
    )
    d_message = jnp.dot(d_hidden_pre, w_node_msg.T, preferred_element_type=jnp.float32).astype(
        jnp.bfloat16
    )
    d_aggregate = jnp.dot(d_message, w_edge_out.T, preferred_element_type=jnp.float32)
    direct = cot_float + jnp.dot(d_hidden_pre, w_node_self.T, preferred_element_type=jnp.float32)
    grad_list = [
        contract_rows(aggregate_b, d_message),
        contract_rows(latent, d_hidden_pre),
        contract_rows(message, d_hidden_pre),
        contract_rows(hidden, d_update),
    ]
    return (new_latent, d_aggregate, d_message, direct, grad_list)


def from_slab(values, offset):
    return shifted(values, "blk", offset)


def to_slab(values, offset):
    return shifted(values, "blk", offset)


def add_rows(buffer, start, size_rows, added_rows):
    current = lax.dynamic_slice_in_dim(buffer, start, size_rows, 0)
    return lax.dynamic_update_slice_in_dim(buffer, current + added_rows, start, 0)


def body(
    latent,
    positions,
    tile_send,
    tile_recv,
    tile_mask,
    tile_count,
    w_send,
    w_recv,
    pos_weight,
    edge_bias,
    w_edge_out,
    w_node_self,
    w_node_msg,
    node_bias,
    w_node_out,
    gain,
    cotangent,
):
    own_rows = latent.shape[0]
    width = latent.shape[1]
    block_size = tile_mask.shape[-1]
    tiles_here = tile_mask.shape[2]
    placed = lax.dot_general(
        positions,
        pos_weight,
        (((0,), (0,)), ((), ())),
        precision=lax.Precision.HIGHEST,
        preferred_element_type=jnp.float32,
    )
    send_rows = (jnp.dot(latent, w_send, preferred_element_type=jnp.float32) + placed).astype(
        jnp.bfloat16
    )
    recv_rows = (
        jnp.dot(latent, w_recv, preferred_element_type=jnp.float32) - placed + edge_bias
    ).astype(jnp.bfloat16)
    senders = lax.all_gather(send_rows, "grp", axis=0, tiled=True)
    receivers = jnp.concatenate([from_slab(recv_rows, 1), recv_rows, from_slab(recv_rows, -1)], 0)
    send_table = tile_send[0, 0]
    recv_table = tile_recv[0, 0]
    mask_table = tile_mask[0, 0]
    live_count = tile_count[0, 0]

    def locate(tile_step):
        send_start = send_table[tile_step] * block_size
        recv_start = recv_table[tile_step] * block_size
        tile_alive = (tile_step < live_count).astype(jnp.float32)
        edge_mask = mask_table[tile_step].astype(jnp.float32) * tile_alive
        send_block = lax.dynamic_slice_in_dim(senders, send_start, block_size, 0)
        recv_block = lax.dynamic_slice_in_dim(receivers, recv_start, block_size, 0)
        return (send_start, recv_start, send_block, recv_block, edge_mask)

    window = jnp.zeros((3 * own_rows, width), jnp.float32)

    def forward_tile(tile_step, running):
        send_start, recv_start, send_block, recv_block, edge_mask = locate(tile_step)
        results = edge_forward(send_block, recv_block, edge_mask)
        return tuple(
            (
                add_rows(buffer, recv_start, block_size, added)
                for buffer, added in zip(running, results)
            )
        )

    start_state = (window,)
    sums = lax.fori_loop(0, tiles_here, forward_tile, start_state)
    partial_value = sums[0]
    aggregate = (
        partial_value[own_rows : 2 * own_rows]
        + to_slab(partial_value[:own_rows], -1)
        + to_slab(partial_value[2 * own_rows :], 1)
    )
    new_latent, d_aggregate, d_message, direct, grad_list = node_update(
        latent,
        aggregate,
        cotangent,
        w_edge_out,
        w_node_self,
        w_node_msg,
        node_bias,
        w_node_out,
        gain,
    )
    grad_window = jnp.concatenate(
        [to_slab(d_aggregate, 1), d_aggregate, to_slab(d_aggregate, -1)], 0
    )

    def backward_tile(tile_step, running):
        send_start, recv_start, send_block, recv_block, edge_mask = locate(tile_step)
        grad_block = lax.dynamic_slice_in_dim(grad_window, recv_start, block_size, 0)
        send_part, recv_part = edge_backward(send_block, recv_block, edge_mask, grad_block)
        send_buffer = add_rows(running[0], send_start, block_size, send_part)
        return (send_buffer, add_rows(running[1], recv_start, block_size, recv_part))

    send_zero = jnp.zeros(senders.shape, jnp.float32)
    back_state = (send_zero, window)
    grads_out = lax.fori_loop(0, tiles_here, backward_tile, back_state)
    send_grad = lax.psum_scatter(
        grads_out[0].astype(jnp.bfloat16), "grp", scatter_dimension=0, tiled=True
    )
    recv_window = grads_out[1]
    recv_grad = (
        recv_window[own_rows : 2 * own_rows]
        + to_slab(recv_window[:own_rows], -1)
        + to_slab(recv_window[2 * own_rows :], 1)
    )
    recv_bf = recv_grad.astype(jnp.bfloat16)
    latent_grad = (
        direct
        + jnp.dot(send_grad, w_send.T, preferred_element_type=jnp.float32)
        + jnp.dot(recv_bf, w_recv.T, preferred_element_type=jnp.float32)
    )
    local_grads = jnp.stack(
        [contract_rows(latent, send_grad), contract_rows(latent, recv_bf)] + grad_list
    )
    weight_grads = lax.psum(local_grads, ("blk", "grp"))
    return (new_latent, latent_grad, weight_grads)


def solution(mesh):
    in_specs = (
        P(("blk", "grp"), None),
        P(None, ("blk", "grp")),
        P("blk", "grp", None),
        P("blk", "grp", None),
        P("blk", "grp", None, None, None),
        P("blk", "grp"),
        P(),
        P(),
        P(),
        P(),
        P(),
        P(),
        P(),
        P(),
        P(),
        P(),
        P(("blk", "grp"), None),
    )
    out_specs = (P(("blk", "grp"), None), P(("blk", "grp"), None), P())
    return jax.shard_map(body, mesh=mesh, in_specs=in_specs, out_specs=out_specs, check_vma=False)
```

profile of v0, /device:TPU:0, one launch (start us, length us, event | category | flops | bytes accessed | tf_op | source)
XLA Modules:
  0.0 487.5 jit_solution(2873636590985350596)
XLA Ops:
  7.2 1.3 fusion.26
  8.5 1.1 fusion.5
  10.1 2.9 collective-permute-start.1
  14.2 15.8 %all_gather.3 = bf16[2048,128]{1,0:T(8,128)(2,1)S(1)} all-gather(bf16[512,128]{1,0:T(8,128)(2,1)S(1)} %fusion.6), channel_id=1, replica_groups=mesh['blk'=8,'grp'=4] {'grp'}, dimensions={0}, use_global_device_ids=true | all-gather | bytes 655360 | tf_op jit(solution)/shard_map/all_gather | solution.py:164
  30.9 127.0 %while.80 = (s32[]{:T(128)}, f32[1536,128]{1,0:T(8,128)S(1)}, s32[16]{0:T(128)S(1)}, bf16[1536,128]{1,0:T(8,128)(2,1)}, s32[16,128,128]{2,1,0:T(8,128)}, /*index...) while((s32[]{:T(128)}, f32[1536,128]{1,0:T(8,128)S(1)}, ...), condition=%wide.region_4.5_spmd, body=%wide.region_0.4_spmd.sunk | while | flops 2162702 | bytes 696740 | solution.py:193
  35.7 3.1 while.83
  43.6 3.1 while.83
  51.5 3.1 while.83
  59.5 3.1 while.83
  67.4 3.1 while.83
  75.3 3.1 while.83
  83.3 3.1 while.83
  91.2 3.1 while.83
  99.1 3.1 while.83
  107.1 3.1 while.83
  115.0 3.1 while.83
  123.0 3.1 while.83
  130.9 3.1 while.83
  138.8 3.1 while.83
  146.8 3.1 while.83
  154.7 3.1 while.83
  159.3 4.5 collective-permute-done.2
  163.8 2.8 collective-permute-done.3
  170.5 2.6 collective-permute-start.5
  173.2 6.0 %collective-permute-done.4 = f32[512,128]{1,0:T(8,128)S(1)} collective-permute-done((f32[512,128]{1,0:T(8,128)S(1)}, f32[512,128]{1,0:T(8,128)S(1)}, u32[]{:S(2)}, u32[]{:S(2)}) %collective-permute-start.4) | collective-permute-done | bytes 262176 | tf_op jit(solution)/shard_map/ppermute | solution.py:10
  179.3 143.6 %while.82 = (s32[]{:T(128)}, f32[2048,128]{1,0:T(8,128)S(1)}, f32[1536,128]{1,0:T(8,128)S(1)}, s32[16]{0:T(128)S(1)}, s32[16]{0:T(128)S(1)}, /*index=5*/bf16[153...) while((s32[]{:T(128)}, f32[2048,128]{1,0:T(8,128)S(1)}, ...), condition=%wide.region_14.15_spmd, body=%wide.region_9.14_spmd.sunk | while | flops 3244047 | bytes 1335806 | solution.py:224
  184.9 3.3 while.84
  193.9 3.3 while.84
  202.9 3.3 while.84
  211.9 3.3 while.84
  220.8 3.3 while.84
  229.8 3.3 while.84
  238.8 3.3 while.84
  247.7 3.3 while.84
  256.7 3.3 while.84
  265.7 3.3 while.84
  274.7 3.3 while.84
  283.6 3.3 while.84
  292.6 3.3 while.84
  301.6 3.3 while.84
  310.6 3.3 while.84
  319.5 3.3 while.84
  325.8 4.9 %collective-permute-done.6 = f32[512,128]{1,0:T(8,128)S(1)} collective-permute-done((f32[512,128]{1,0:T(8,128)S(1)}, f32[512,128]{1,0:T(8,128)S(1)}, u32[]{:S(2)}, u32[]{:S(2)}) %collective-permute-start.6) | collective-permute-done | bytes 262176 | tf_op jit(solution)/shard_map/ppermute | solution.py:10
  330.7 3.0 collective-permute-done.7
  333.8 13.3 %reduce-scatter.2.cloned.1.call-done = bf16[512,128]{1,0:T(8,128)(2,1)} async-done(((bf16[2048,128]{1,0:T(8,128)(2,1)}), bf16[512,128]{1,0:T(8,128)(2,1)}) %reduce-scatter.2.cloned.1.call-update) | async-done | bytes 131088 | tf_op jit(solution)/shard_map/reduce_scatter | solution.py:225
  347.1 1.1 fusion.13
  351.5 127.3 %all-reduce.2.cloned.1.call-done = f32[6,128,128]{1,2,0:T(8,128)} async-done(((f32[6,128,128]{1,2,0:T(8,128)}), f32[6,128,128]{1,2,0:T(8,128)}) %all-reduce.2.cloned.1.call-update) | async-done | bytes 393232 | tf_op jit(solution)/shard_map/psum | solution.py:243
  478.8 1.9 copy.41
  (917 shorter events, 214.0 us)
Async XLA Ops:
  7.2 160.4 %copy-start = (bf16[128,128]{1,0:T(8,128)(2,1)S(1)}, bf16[128,128]{1,0:T(8,128)(2,1)}, u32[]{:S(2)}) copy-start(bf16[128,128]{1,0:T(8,128)(2,1)} %param.39) | copy-start | bytes 98308
  7.2 339.9 %reduce-scatter.2.cloned.1.call-start = ((), (), s32[]{:S(2)}) async-start(), calls=%async_computation.1 | async-start | bytes 655360 | tf_op jit(solution)/shard_map/reduce_scatter | solution.py:225
  9.6 20.4 %collective-permute-start = (bf16[512,128]{1,0:T(8,128)(2,1)S(1)}, bf16[512,128]{1,0:T(8,128)(2,1)S(1)}, u32[]{:S(2)}, u32[]{:S(2)}) collective-permute-start(bf16[512,128]{1,0:T(8,128)(2,1)S(1)} %fusion.5), channel_id=1, source_target_pairs={{0,4},{4,8},{8,12},{12,16},{16,20},{20,24},{24,28},{28,0},{1,5},{5... | collective-permute-start | bytes 393224 | tf_op jit(solution)/shard_map/ppermute | solution.py:10
  10.1 19.9 %collective-permute-start.1 = (bf16[512,128]{1,0:T(8,128)(2,1)S(1)}, bf16[512,128]{1,0:T(8,128)(2,1)S(1)}, u32[]{:S(2)}, u32[]{:S(2)}) collective-permute-start(bf16[512,128]{1,0:T(8,128)(2,1)S(1)} %fusion.5), channel_id=1, source_target_pairs={{0,28},{4,0},{8,4},{12,8},{16,12},{20,16},{24,20},{28,24},{1,29},{... | collective-permute-start | bytes 393224 | tf_op jit(solution)/shard_map/ppermute | solution.py:10
  14.2 16.7 %copy-start.24 = (s32[1,1,16]{2,1,0:T(1,128)S(1)}, s32[1,1,16]{2,1,0:T(1,128)}, u32[]{:S(2)}) copy-start(s32[1,1,16]{2,1,0:T(1,128)} %param.28) | copy-start | bytes 196
  14.2 16.7 %copy-start.25 = (s32[1,1,16]{2,1,0:T(1,128)S(1)}, s32[1,1,16]{2,1,0:T(1,128)}, u32[]{:S(2)}) copy-start(s32[1,1,16]{2,1,0:T(1,128)} %param.27) | copy-start | bytes 196
  157.9 8.8 %copy-start.2 = (bf16[2048,128]{1,0:T(8,128)(2,1)}, bf16[2048,128]{1,0:T(8,128)(2,1)S(1)}, u32[]{:S(2)}) copy-start(bf16[2048,128]{1,0:T(8,128)(2,1)S(1)} %get-tuple-element.864) | copy-start | bytes 1572868
  157.9 1.0 copy-start.1
  157.9 1.2 copy-start.15
  157.9 1.3 copy-start.19
  157.9 8.8 %copy-start.18 = (bf16[128,128]{1,0:T(8,128)(2,1)S(1)}, bf16[128,128]{1,0:T(8,128)(2,1)}, u32[]{:S(2)}) copy-start(bf16[128,128]{1,0:T(8,128)(2,1)} %param.35) | copy-start | bytes 98308
  158.0 5.9 %collective-permute-start.2 = (f32[512,128]{1,0:T(8,128)S(1)}, f32[512,128]{1,0:T(8,128)S(1)}, u32[]{:S(2)}, u32[]{:S(2)}) collective-permute-start(f32[512,128]{1,0:T(8,128)S(1)} %get-tuple-element.482), channel_id=1, source_target_pairs={{0,28},{4,0},{8,4},{12,8},{16,12},{20,16},{24,20},{28,24},{1,29},{... | collective-permute-start | bytes 786440 | tf_op jit(solution)/shard_map/ppermute | solution.py:10
  158.0 9.3 %copy-start.14 = (bf16[128,128]{1,0:T(8,128)(2,1)S(1)}, bf16[128,128]{1,0:T(8,128)(2,1)}, u32[]{:S(2)}) copy-start(bf16[128,128]{1,0:T(8,128)(2,1)} %param.37) | copy-start | bytes 98308
  158.0 9.3 %copy-start.23 = (f32[128]{0:T(128)S(1)}, f32[128]{0:T(128)}, u32[]{:S(2)}) copy-start(f32[128]{0:T(128)} %param.38) | copy-start | bytes 1540
  158.0 8.6 %collective-permute-start.3 = (f32[512,128]{1,0:T(8,128)S(1)}, f32[512,128]{1,0:T(8,128)S(1)}, u32[]{:S(2)}, u32[]{:S(2)}) collective-permute-start(f32[512,128]{1,0:T(8,128)S(1)} %get-tuple-element.483), channel_id=1, source_target_pairs={{0,4},{4,8},{8,12},{12,16},{16,20},{20,24},{24,28},{28,0},{1,5},{5... | collective-permute-start | bytes 786440 | tf_op jit(solution)/shard_map/ppermute | solution.py:10
  166.7 0.6 copy-start.3
  167.4 0.7 copy-start.7
  167.4 0.7 copy-start.22
  167.6 1.4 copy-start.12
  169.0 0.6 copy-start.16
  169.6 0.7 copy-start.5
  170.5 8.7 %collective-permute-start.4 = (f32[512,128]{1,0:T(8,128)S(1)}, f32[512,128]{1,0:T(8,128)S(1)}, u32[]{:S(2)}, u32[]{:S(2)}) collective-permute-start(f32[512,128]{1,0:T(8,128)S(1)} %fusion.27), channel_id=1, source_target_pairs={{0,4},{4,8},{8,12},{12,16},{16,20},{20,24},{24,28},{28,0},{1,5},{5... | collective-permute-start | bytes 786440 | tf_op jit(solution)/shard_map/ppermute | solution.py:10
  170.5 8.6 %collective-permute-start.5 = (f32[512,128]{1,0:T(8,128)S(1)}, f32[512,128]{1,0:T(8,128)S(1)}, u32[]{:S(2)}, u32[]{:S(2)}) collective-permute-start(f32[512,128]{1,0:T(8,128)S(1)} %fusion.27), channel_id=1, source_target_pairs={{0,28},{4,0},{8,4},{12,8},{16,12},{20,16},{24,20},{28,24},{1,29},{... | collective-permute-start | bytes 786440 | tf_op jit(solution)/shard_map/ppermute | solution.py:10
  323.8 1.0 copy-start.10
  323.8 155.0 %all-reduce.2.cloned.1.call-start = ((), (), s32[]{:S(2)}) async-start(), calls=%async_computation.2 | async-start | bytes 786432 | tf_op jit(solution)/shard_map/psum | solution.py:243
  323.9 6.8 %collective-permute-start.6 = (f32[512,128]{1,0:T(8,128)S(1)}, f32[512,128]{1,0:T(8,128)S(1)}, u32[]{:S(2)}, u32[]{:S(2)}) collective-permute-start(f32[512,128]{1,0:T(8,128)S(1)} %get-tuple-element.480), channel_id=1, source_target_pairs={{0,28},{4,0},{8,4},{12,8},{16,12},{20,16},{24,20},{28,24},{1,29},{... | collective-permute-start | bytes 786440 | tf_op jit(solution)/shard_map/ppermute | solution.py:10
  324.8 8.9 %collective-permute-start.7 = (f32[512,128]{1,0:T(8,128)S(1)}, f32[512,128]{1,0:T(8,128)S(1)}, u32[]{:S(2)}, u32[]{:S(2)}) collective-permute-start(f32[512,128]{1,0:T(8,128)S(1)} %get-tuple-element.481), channel_id=1, source_target_pairs={{0,4},{4,8},{8,12},{12,16},{16,20},{20,24},{24,28},{28,0},{1,5},{5... | collective-permute-start | bytes 786440 | tf_op jit(solution)/shard_map/ppermute | solution.py:10
  325.5 22.9 %copy-start.4 = (bf16[512,128]{1,0:T(8,128)(2,1)S(1)}, bf16[512,128]{1,0:T(8,128)(2,1)}, u32[]{:S(2)}) copy-start(bf16[512,128]{1,0:T(8,128)(2,1)} %copy-done.3) | copy-start | bytes 393220
  325.5 22.9 %copy-start.6 = (bf16[512,128]{1,0:T(8,128)(2,1)S(1)}, bf16[512,128]{1,0:T(8,128)(2,1)}, u32[]{:S(2)}) copy-start(bf16[512,128]{1,0:T(8,128)(2,1)} %copy-done.5) | copy-start | bytes 393220
  325.7 23.2 %copy-start.8 = (bf16[512,128]{1,0:T(8,128)(2,1)S(1)}, bf16[512,128]{1,0:T(8,128)(2,1)}, u32[]{:S(2)}) copy-start(bf16[512,128]{1,0:T(8,128)(2,1)} %copy-done.7) | copy-start | bytes 393220
  333.8 15.4 %copy-start.13 = (f32[512,128]{1,0:T(8,128)S(1)}, f32[512,128]{1,0:T(8,128)}, u32[]{:S(2)}) copy-start(f32[512,128]{1,0:T(8,128)} %copy-done.12) | copy-start | bytes 786436
  333.8 15.4 %copy-start.17 = (bf16[512,128]{0,1:T(8,128)(2,1)S(1)}, bf16[512,128]{0,1:T(8,128)(2,1)}, u32[]{:S(2)}) copy-start(bf16[512,128]{0,1:T(8,128)(2,1)} %copy-done.16) | copy-start | bytes 393220
  348.9 1.3 copy-start.11
  348.9 1.3 copy-start.20
  349.2 1.2 copy-start.21
  349.4 0.7 copy-start.9
Sparse Core Ops, SparseCore 0:
  323.9 23.0 reduce-scatter.1
  352.9 125.8 all-reduce.1
where the time goes:
time: 493 us; the launch traced here: 488 us
  waiting for transfers between devices  162 us (33%)
  other arithmetic  150 us (30%)
  loops' own time  70.3 us (14%)
  local copies, waits for them, and re-layouts  59.9 us (12%)
  blocking collectives  15.8 us (3%)
  between operations  14.6 us (3%)
  starting transfers between devices  7.65 us (2%)
  matrix products  7.65 us (2%)
    psum x1, waiting for transfers between devices, body(): weight_grads = lax.psum(local_grads, ('blk', 'grp'))  127 us
    reduce_sum x64, other arithmetic, one_group(): return (running, jnp.sum(terms, axis=1))  46.5 us
    reduce_sum x64, other arithmetic, one_group(): summed = jnp.sum(mask_part[:, :, None] * jnp.maximum(preact, 0.0), axis=1)  45.5 us
    another operation x1, loops' own time, body(): sums = lax.fori_loop(0, tiles_here, forward_tile, start_state)  32 us
    another operation x1, loops' own time, body(): grads_out = lax.fori_loop(0, tiles_here, backward_tile, back_state)  31.9 us
    mul x32, other arithmetic, locate(): edge_mask = mask_table[tile_step].astype(jnp.float32) * tile_alive  27.2 us
    ppermute x8, waiting for transfers between devices, shifted(): return lax.ppermute(value, axis, pairs)  21.2 us
    dynamic_slice x32, local copies, waits for them, and re-layouts, locate(): recv_start = recv_table[tile_step] * block_size  19.2 us
  transfers between devices with their start and end apart: 10, of which 7 were waited for; matrix products, arithmetic and copies ran while one was open for 1% of the time, Pallas kernels for 0%

commit v1 on v0

v1 whole, which is shorter than its diff:
```python
import jax
import jax.numpy as jnp
from jax import lax
from jax.experimental import pallas as pl
from jax.experimental.pallas import tpu as pltpu
from jax.sharding import PartitionSpec as P

F32 = jnp.float32
BF16 = jnp.bfloat16
RANKS = 4
DIRECT = 8


def shifted(value, axis, steps):
    count = lax.axis_size(axis)
    pairs = [(source, (source + steps) % count) for source in range(count)]
    return lax.ppermute(value, axis, pairs)


def dot(left, right):
    return jnp.dot(left, right, preferred_element_type=F32)


def dot_t(left, right):
    return lax.dot_general(left, right, (((1,), (1,)), ((), ())), preferred_element_type=F32)


def contract_rows(left_rows, right_rows):
    return lax.dot_general(
        left_rows, right_rows, (((0,), (0,)), ((), ())), preferred_element_type=F32
    )


def call(kernel, outs, args, scalars=(), scratch=(), flops=0, smem_outs=()):
    vmem = pl.BlockSpec(memory_space=pltpu.VMEM)
    smem = pl.BlockSpec(memory_space=pltpu.SMEM)
    moved = sum(a.size * a.dtype.itemsize for a in list(args) + list(outs))
    return pl.pallas_call(
        kernel,
        out_shape=[jax.ShapeDtypeStruct(o.shape, o.dtype) for o in list(outs) + list(smem_outs)],
        in_specs=[smem] * len(scalars) + [vmem] * len(args),
        out_specs=[vmem] * len(outs) + [smem] * len(smem_outs),
        scratch_shapes=list(scratch),
        compiler_params=pltpu.CompilerParams(vmem_limit_bytes=32 * 2**20),
        cost_estimate=pl.CostEstimate(flops=flops, bytes_accessed=moved, transcendentals=0),
    )(*scalars, *args)


def like(shape, dtype):
    return jax.ShapeDtypeStruct(tuple(shape), dtype)


def rows_kernel(latent, positions, w_send, w_recv, pos_weight, edge_bias, send_out, recv_out):
    count = positions.shape[1]
    padded = jnp.concatenate([positions[...], jnp.zeros((5, count), F32)], 0)
    columns = jnp.transpose(padded)
    placed = columns[:, 0:1] * pos_weight[0:1, :]
    placed = placed + columns[:, 1:2] * pos_weight[1:2, :]
    placed = placed + columns[:, 2:3] * pos_weight[2:3, :]
    rows = latent[...]
    send_out[...] = (dot(rows, w_send[...]) + placed).astype(BF16)
    recv_out[...] = (dot(rows, w_recv[...]) - placed + edge_bias[...]).astype(BF16)


def ranks_kernel(tile_count, mask, row_rank, row_degree, col_rank, row_most, col_most):
    size = mask.shape[-1]
    row_index = lax.broadcasted_iota(jnp.int32, (size, size), 0)
    col_index = lax.broadcasted_iota(jnp.int32, (size, size), 1)
    upper = (row_index <= col_index).astype(F32).astype(BF16)
    eye = (row_index == col_index).astype(F32).astype(BF16)
    ones = jnp.ones((size, size), BF16)
    for_rows = jnp.concatenate([upper, ones], 1)
    for_cols = jnp.concatenate([upper, eye], 1)

    def one_tile(tile, carry):
        values = mask[tile].astype(F32)
        values_b = values.astype(BF16)
        found = dot(values_b, for_rows)
        row_rank[tile] = (found[:, :size] * values).astype(BF16)
        row_degree[tile] = found[:, size:].astype(BF16)
        row_most[tile] = jnp.max(found[:, size:]).astype(jnp.int32)
        found = contract_rows(values_b, for_cols)
        col_rank[tile] = (found[:, :size] * found[:, size:]).astype(BF16)
        col_most[tile] = jnp.max(found[:, :size]).astype(jnp.int32)
        return carry

    lax.fori_loop(0, tile_count[0, 0], one_tile, 0)


def one_hots(rank_block, step, unit):
    found = []
    for item in range(RANKS):
        rank = (step * RANKS + item + 1).astype(F32).astype(BF16)
        hot = jnp.where(rank_block == rank, jnp.ones_like(unit), jnp.zeros_like(unit))
        found.append(jnp.concatenate([hot, unit], 1))
    return found


def eye_of(size):
    row_index = lax.broadcasted_iota(jnp.int32, (size, size), 0)
    col_index = lax.broadcasted_iota(jnp.int32, (size, size), 1)
    return (row_index == col_index).astype(F32).astype(BF16)


def lay_blocks(table, parts):
    size = table.shape[1]
    place = 0
    for part in parts:
        for block in range(part.shape[0] // size):
            table[place] = part[block * size : (block + 1) * size, :]
            place += 1


def sender_place(block, member, members, blocks):
    distance = lax.rem(member - block // blocks + members, members)
    return distance * blocks + lax.rem(block, blocks)


def make_forward(members, blocks):
    def kernel(tile_send, tile_recv, tile_count, row_most, row_rank, row_degree, *refs):
        send_parts, refs = refs[:members], refs[members:]
        recv_parts, refs = refs[:3], refs[3:]
        sums_out, counts_out, refs = refs[:3], refs[3:6], refs[6:]
        senders, receivers, sums, counts = refs
        size = senders.shape[1]
        member = lax.axis_index("grp")
        lay_blocks(senders, send_parts)
        lay_blocks(receivers, recv_parts)
        sums[...] = jnp.zeros_like(sums)
        counts[...] = jnp.zeros_like(counts)
        unit = eye_of(size)

        def one_tile(tile, carry):
            recv_place = tile_recv[0, 0, tile]
            recv_rows = receivers[recv_place]
            send_rows = senders[sender_place(tile_send[0, 0, tile], member, members, blocks)]
            right = jnp.concatenate([send_rows, recv_rows], 0)
            rank_block = row_rank[tile]
            steps = (row_most[tile] + RANKS - 1) // RANKS

            def one_step(step, running):
                total, count = running
                for left in one_hots(rank_block, step, unit):
                    preact = dot(left, right)
                    total = total + jnp.maximum(preact, 0.0)
                    count = count + jnp.where(preact > 0.0, 1.0, 0.0)
                return (total, count)

            zero = jnp.zeros((size, size), F32)
            total, count = lax.fori_loop(0, steps, one_step, (zero, zero))
            spare = (steps * RANKS).astype(F32) - row_degree[tile].astype(F32)
            recv_float = recv_rows.astype(F32)
            sums[recv_place] += total - spare * jnp.maximum(recv_float, 0.0)
            counts[recv_place] += count - jnp.where(recv_float > 0.0, spare, 0.0)
            return carry

        lax.fori_loop(0, tile_count[0, 0], one_tile, 0)
        for table, outs in ((sums, sums_out), (counts, counts_out)):
            for side, out in enumerate(outs):
                for block in range(blocks):
                    out[block * size : (block + 1) * size, :] = table[side * blocks + block].astype(
                        out.dtype
                    )

    return kernel


def node_kernel(
    latent,
    cotangent,
    sum_own,
    sum_low,
    sum_high,
    w_edge_out,
    w_node_self,
    w_node_msg,
    node_bias,
    w_node_out,
    gain,
    new_latent,
    d_aggregate_out,
    aggregate_out,
    message_out,
    hidden_out,
    d_update_out,
    d_hidden_out,
    d_message_out,
):
    rows = latent[...]
    aggregate = (sum_own[...] + sum_low[...].astype(F32) + sum_high[...].astype(F32)).astype(BF16)
    message = dot(aggregate, w_edge_out[...]).astype(BF16)
    hidden_pre = dot(rows, w_node_self[...]) + dot(message, w_node_msg[...]) + node_bias[...]
    logistic = 1.0 / (1.0 + jnp.exp(-hidden_pre))
    hidden = (hidden_pre * logistic).astype(BF16)
    update = dot(hidden, w_node_out[...])
    centred = update - jnp.mean(update, axis=-1, keepdims=True)
    variance = jnp.mean(centred * centred, axis=-1, keepdims=True)
    inv_std = lax.rsqrt(variance + 1e-05)
    normed = centred * inv_std
    new_latent[...] = (rows.astype(F32) + normed * gain[...]).astype(BF16)
    d_normed = cotangent[...].astype(F32) * gain[...]
    d_update = (
        inv_std
        * (
            d_normed
            - jnp.mean(d_normed, axis=-1, keepdims=True)
            - normed * jnp.mean(d_normed * normed, axis=-1, keepdims=True)
        )
    ).astype(BF16)
    d_hidden = dot_t(d_update, w_node_out[...])
    d_hidden_pre = (d_hidden * logistic * (1.0 + hidden_pre * (1.0 - logistic))).astype(BF16)
    d_message = dot_t(d_hidden_pre, w_node_msg[...]).astype(BF16)
    d_aggregate_out[...] = dot_t(d_message, w_edge_out[...]).astype(BF16)
    aggregate_out[...] = aggregate
    message_out[...] = message
    hidden_out[...] = hidden
    d_update_out[...] = d_update
    d_hidden_out[...] = d_hidden_pre
    d_message_out[...] = d_message


def make_early(members):
    def kernel(
        latent,
        cotangent,
        count_own,
        count_low,
        count_high,
        aggregate,
        message,
        hidden,
        d_update,
        d_hidden_pre,
        d_message,
        w_edge_out,
        w_node_self,
        w_recv,
        direct_out,
        *refs,
    ):
        share_outs, grads = refs[:members], refs[members]
        width = latent.shape[1]
        rows = latent[...]
        count = count_own[...] + count_low[...].astype(F32) + count_high[...].astype(F32)
        d_recv = (dot_t(d_message[...], w_edge_out[...]) * count).astype(BF16)
        direct_out[...] = (
            cotangent[...].astype(F32)
            + dot_t(d_hidden_pre[...], w_node_self[...])
            + dot_t(d_recv, w_recv[...])
        )
        grads[0:width, :] = contract_rows(rows, d_recv)
        grads[width : 2 * width, :] = contract_rows(aggregate[...], d_message[...])
        grads[2 * width : 3 * width, :] = contract_rows(rows, d_hidden_pre[...])
        grads[3 * width : 4 * width, :] = contract_rows(message[...], d_hidden_pre[...])
        grads[4 * width : 5 * width, :] = contract_rows(hidden[...], d_update[...])
        member = lax.axis_index("grp")
        share = grads.shape[0] // members
        for distance, out in enumerate(share_outs):
            start = pl.multiple_of(lax.rem(member + distance, members) * share, share)
            out[...] = grads[pl.ds(start, share), :].astype(out.dtype)

    return kernel


def make_backward(members, blocks):
    def kernel(tile_send, tile_recv, tile_count, col_most, col_rank, *refs):
        send_parts, refs = refs[:members], refs[members:]
        recv_parts, refs = refs[:3], refs[3:]
        grad_parts, refs = refs[:3], refs[3:]
        latent_parts, refs = refs[:members], refs[members:]
        grads_out, refs = refs[:members], refs[members:]
        weight_out, senders, receivers, d_sums, grads = refs
        size = senders.shape[1]
        member = lax.axis_index("grp")
        lay_blocks(senders, send_parts)
        lay_blocks(receivers, recv_parts)
        lay_blocks(d_sums, grad_parts)
        grads[...] = jnp.zeros_like(grads)
        unit = eye_of(size)
        nothing = jnp.zeros((size, size), BF16)

        def one_tile(tile, carry):
            recv_place = tile_recv[0, 0, tile]
            send_place = sender_place(tile_send[0, 0, tile], member, members, blocks)
            upper = jnp.concatenate([receivers[recv_place], d_sums[recv_place]], 1)
            lower = jnp.concatenate([senders[send_place], nothing], 1)
            right = jnp.concatenate([upper, lower], 0)
            rank_block = col_rank[tile]
            steps = (col_most[tile] + RANKS - 1) // RANKS

            def one_step(step, total):
                for left in one_hots(rank_block, step, unit):
                    found = dot(left, right)
                    total = total + jnp.where(found[:, :size] > 0.0, found[:, size:], 0.0)
                return total

            total = lax.fori_loop(0, steps, one_step, jnp.zeros((size, size), F32))
            grads[send_place] += total
            return carry

        lax.fori_loop(0, tile_count[0, 0], one_tile, 0)
        weight = jnp.zeros((size, size), F32)
        for distance, out in enumerate(grads_out):
            for block in range(blocks):
                span = slice(block * size, (block + 1) * size)
                found = grads[distance * blocks + block]
                out[span, :] = found.astype(out.dtype)
                weight = weight + contract_rows(
                    latent_parts[distance][span, :], found.astype(BF16)
                )
        weight_out[...] = weight.astype(weight_out.dtype)

    return kernel


def make_sum(axis, count):
    def kernel(*refs):
        parts, out, table = refs[:count], refs[count], refs[count + 1]
        place = lax.axis_index(axis)
        for distance, part in enumerate(parts):
            table[lax.rem(place - distance + count, count)] = part[...]
        total = table[0].astype(F32)
        for item in range(1, count):
            total = total + table[item].astype(F32)
        out[...] = total.astype(out.dtype)

    return kernel


def sum_over(value, axis):
    count = lax.axis_size(axis)
    if count > DIRECT:
        return lax.psum(value.astype(F32), axis).astype(BF16)
    parts = [value] + [shifted(value, axis, distance) for distance in range(1, count)]
    return call(
        make_sum(axis, count),
        [like(value.shape, BF16)],
        parts,
        scratch=[pltpu.VMEM((count, *value.shape), BF16)],
        flops=value.size * count,
    )[0]


def make_last(members):
    def kernel(*refs):
        direct, w_send, refs = refs[0], refs[1], refs[2:]
        send_grads, refs = refs[:members], refs[members:]
        shares, refs = refs[:members], refs[members:]
        lates, refs = refs[:members], refs[members:]
        latent_grad, weight_grads, table, late_table = refs
        member = lax.axis_index("grp")
        d_send = send_grads[0][...]
        for part in send_grads[1:]:
            d_send = d_send + part[...].astype(F32)
        latent_grad[...] = direct[...] + dot_t(d_send.astype(BF16), w_send[...])
        share = shares[0].shape[0]
        width = table.shape[1]
        for distance, part in enumerate(shares):
            place = lax.rem(member - distance + members, members)
            start = pl.multiple_of(place * share, share)
            table[pl.ds(start, share), :] = part[...].astype(F32)
        for distance, part in enumerate(lates):
            late_table[lax.rem(member - distance + members, members)] = part[...]
        late = late_table[0].astype(F32)
        for item in range(1, members):
            late = late + late_table[item].astype(F32)
        weight_grads[0] = late
        for item in range(weight_grads.shape[0] - 1):
            weight_grads[item + 1] = table[item * width : (item + 1) * width, :]

    return kernel


def body(
    latent,
    positions,
    tile_send,
    tile_recv,
    tile_mask,
    tile_count,
    w_send,
    w_recv,
    pos_weight,
    edge_bias,
    w_edge_out,
    w_node_self,
    w_node_msg,
    node_bias,
    w_node_out,
    gain,
    cotangent,
):
    own_rows, width = latent.shape
    tiles, size = tile_mask.shape[2], tile_mask.shape[3]
    blocks = own_rows // size
    members = lax.axis_size("grp")
    node_like = like((own_rows, width), BF16)
    node_float = like((own_rows, width), F32)
    tile_like = like((tiles, size, size), BF16)
    most_like = like((tiles,), jnp.int32)
    send_rows, recv_rows = call(
        rows_kernel,
        [node_like] * 2,
        [latent, positions, w_send, w_recv, pos_weight, edge_bias.reshape(1, width)],
        flops=4 * own_rows * width * width,
    )
    recv_parts = [shifted(recv_rows, "blk", 1), recv_rows, shifted(recv_rows, "blk", -1)]
    send_parts = [send_rows] + [
        shifted(send_rows, "grp", distance) for distance in range(1, members)
    ]
    row_rank, row_degree, col_rank, row_most, col_most = call(
        ranks_kernel,
        [tile_like] * 3,
        [tile_mask.reshape(tiles, size, size)],
        scalars=[tile_count],
        smem_outs=[most_like] * 2,
        flops=8 * tiles * size * size * size,
    )
    window = pltpu.VMEM((3 * blocks, size, width), F32)
    sum_low, sum_own, sum_high, count_low, count_own, count_high = call(
        make_forward(members, blocks),
        [node_like, node_float, node_like] * 2,
        [row_rank, row_degree, *send_parts, *recv_parts],
        scalars=[tile_send, tile_recv, tile_count, row_most],
        scratch=[
            pltpu.VMEM((members * blocks, size, width), BF16),
            pltpu.VMEM((3 * blocks, size, width), BF16),
            window,
            window,
        ],
        flops=64 * tiles * size * size * width,
    )
    from_high = shifted(sum_low, "blk", -1)
    from_low = shifted(sum_high, "blk", 1)
    counts_from_high = shifted(count_low, "blk", -1)
    counts_from_low = shifted(count_high, "blk", 1)
    (
        new_latent,
        d_aggregate,
        aggregate,
        message,
        hidden,
        d_update,
        d_hidden_pre,
        d_message,
    ) = call(
        node_kernel,
        [node_like] * 8,
        [
            latent,
            cotangent,
            sum_own,
            from_low,
            from_high,
            w_edge_out,
            w_node_self,
            w_node_msg,
            node_bias.reshape(1, width),
            w_node_out,
            gain.reshape(1, width),
        ],
        flops=14 * own_rows * width * width,
    )
    grad_parts = [shifted(d_aggregate, "blk", 1), d_aggregate, shifted(d_aggregate, "blk", -1)]
    share_rows = 5 * width // members
    direct, *shares = call(
        make_early(members),
        [node_float, like((share_rows, width), F32)]
        + [like((share_rows, width), BF16)] * (members - 1),
        [
            latent,
            cotangent,
            count_own,
            counts_from_low,
            counts_from_high,
            aggregate,
            message,
            hidden,
            d_update,
            d_hidden_pre,
            d_message,
            w_edge_out,
            w_node_self,
            w_recv,
        ],
        scratch=[pltpu.VMEM((5 * width, width), F32)],
        flops=16 * own_rows * width * width,
    )
    latent_parts = [latent] + [shifted(latent, "grp", distance) for distance in range(1, members)]
    *send_grads, late = call(
        make_backward(members, blocks),
        [node_float] + [node_like] * (members - 1) + [like((width, width), BF16)],
        [col_rank, *send_parts, *recv_parts, *grad_parts, *latent_parts],
        scalars=[tile_send, tile_recv, tile_count, col_most],
        scratch=[
            pltpu.VMEM((members * blocks, size, width), BF16),
            pltpu.VMEM((3 * blocks, size, width), BF16),
            pltpu.VMEM((3 * blocks, size, width), BF16),
            pltpu.VMEM((members * blocks, size, width), F32),
        ],
        flops=64 * tiles * size * size * width,
    )
    share = shares[0]
    for distance in range(1, members):
        share = share + shifted(shares[distance], "grp", distance).astype(F32)
    share = sum_over(share.astype(BF16), "blk")
    share_parts = [share] + [shifted(share, "grp", distance) for distance in range(1, members)]
    sent_back = [send_grads[0]] + [
        shifted(send_grads[distance], "grp", -distance) for distance in range(1, members)
    ]
    late = sum_over(late, "blk")
    late_parts = [late] + [shifted(late, "grp", distance) for distance in range(1, members)]
    latent_grad, weight_grads = call(
        make_last(members),
        [node_float, like((6, width, width), F32)],
        [direct, w_send, *sent_back, *share_parts, *late_parts],
        scratch=[
            pltpu.VMEM((5 * width, width), F32),
            pltpu.VMEM((members, width, width), BF16),
        ],
        flops=2 * own_rows * width * width,
    )
    return (new_latent, latent_grad, weight_grads)


def solution(mesh):
    in_specs = (
        P(("blk", "grp"), None),
        P(None, ("blk", "grp")),
        P("blk", "grp", None),
        P("blk", "grp", None),
        P("blk", "grp", None, None, None),
        P("blk", "grp"),
        P(),
        P(),
        P(),
        P(),
        P(),
        P(),
        P(),
        P(),
        P(),
        P(),
        P(("blk", "grp"), None),
    )
    out_specs = (P(("blk", "grp"), None), P(("blk", "grp"), None), P())
    return jax.shard_map(body, mesh=mesh, in_specs=in_specs, out_specs=out_specs, check_vma=False)
```

time: 493 us -> 128 us (0.26)
  other arithmetic: 150 us -> 0.03 us
  waiting for transfers between devices: 162 us -> 27.7 us
  loops' own time: 70.3 us -> 0 us
  local copies, waits for them, and re-layouts: 59.9 us -> 6.97 us
  Pallas kernels: 0 us -> 44.7 us
  starting transfers between devices: 7.65 us -> 46.1 us
  blocking collectives: 15.8 us -> 0 us
  between operations: 14.6 us -> 1.58 us
  matrix products: 7.65 us -> 0 us
    psum x1 -> x0, waiting for transfers between devices: 127 us -> none  [body(): weight_grads = lax.psum(local_grads, ('blk', 'grp'))]
    reduce_sum x130 -> x0, other arithmetic: 92.1 us -> none  [the longest x64 46.5 us: one_group(): return (running, jnp.sum(terms, axis=1))]
    another operation x34 -> x0, loops' own time: 70.3 us -> none  [the longest x1 32 us: body(): sums = lax.fori_loop(0, tiles_here, forward_tile, start_state)]
    dynamic_slice x96 -> x0, local copies, waits for them, and re-layouts: 50.9 us -> none  [the longest x32 19.2 us: locate(): recv_start = recv_table[tile_step] * block_size]
    pallas_call x0 -> x9, Pallas kernels: none -> 44.7 us  [call(): pl.pallas_call(kernel, out_shape=[jax.ShapeDtypeStruct(o.shape, o.dtype)...]
    ppermute x8 -> x40, starting transfers between devices: 7.57 us -> 46.1 us  [shifted(): return lax.ppermute(value, axis, pairs)]
    convert_element_type x164 -> x1, other arithmetic: 27.7 us -> 0.03 us  [body(): share = sum_over(share.astype(BF16), 'blk')]
    mul x32 -> x0, other arithmetic: 27.2 us -> none  [locate(): edge_mask = mask_table[tile_step].astype(jnp.float32) * tile_alive]
  transfers between devices with their start and end apart: 10 -> 40, of which waited for: 7 -> 12; matrix products, arithmetic and copies ran while one was open for 1% -> 0% of each run, Pallas kernels for 0% -> 20%
where the time goes in v1:
time: 128 us; the launch traced here: 127 us
  starting transfers between devices  46.1 us (36%)
  Pallas kernels  44.7 us (35%)
  waiting for transfers between devices  27.7 us (22%)
  local copies, waits for them, and re-layouts  6.97 us (5%)
  between operations  1.58 us (1%)
    ppermute x40, starting transfers between devices, shifted(): return lax.ppermute(value, axis, pairs)  46.1 us
    pallas_call x9, Pallas kernels, call(): pl.pallas_call(kernel, out_shape=[jax.ShapeDtypeStruct(o.shape, o.dtype)...  44.7 us
    ppermute x40, waiting for transfers between devices, shifted(): return lax.ppermute(value, axis, pairs)  27.7 us
    unnamed x38, local copies, waits for them, and re-layouts  6.97 us
  transfers between devices with their start and end apart: 40, of which 12 were waited for; matrix products, arithmetic and copies ran while one was open for 0% of the time, Pallas kernels for 20%

profile of v1, /device:TPU:0, one launch (start us, length us, event | category | flops | bytes accessed | tf_op | source)
XLA Modules:
  0.0 127.1 jit_solution(12982982372985965680)
XLA Ops:
  0.6 0.6 copy-done.14
  1.3 0.9 copy-done
  2.2 0.8 copy-done.4
  3.0 0.8 copy-done.8
  3.7 0.7 copy-done.12
  4.4 0.7 copy-done.13
  5.5 3.1 %collective-permute-start = (bf16[512,128]{1,0:T(8,128)(2,1)S(1)}, bf16[512,128]{1,0:T(8,128)(2,1)S(1)}, u32[]{:S(2)}, u32[]{:S(2)}) collective-permute-start(bf16[512,128]{1,0:T(8,128)(2,1)S(1)} %get-tuple-element.39.refs_0_), channel_id=1, source_target_pairs={{0,1},{1,2},{2,3},{3,0},{4,5},{5,6},{6,7},{7,4},{8,9},{9,10},{10,1... | collective-permute-start | bytes 393224 | tf_op jit(solution)/shard_map/ppermute | solution.py:17
  8.6 2.6 %collective-permute-start.1 = (bf16[512,128]{1,0:T(8,128)(2,1)S(1)}, bf16[512,128]{1,0:T(8,128)(2,1)S(1)}, u32[]{:S(2)}, u32[]{:S(2)}) collective-permute-start(bf16[512,128]{1,0:T(8,128)(2,1)S(1)} %get-tuple-element.39.refs_0_), channel_id=1, source_target_pairs={{0,2},{1,3},{2,0},{3,1},{4,6},{5,7},{6,4},{7,5},{8,10},{9,11},{10,... | collective-permute-start | bytes 393224 | tf_op jit(solution)/shard_map/ppermute | solution.py:17
  11.2 1.4 %collective-permute-start.2 = (bf16[512,128]{1,0:T(8,128)(2,1)S(1)}, bf16[512,128]{1,0:T(8,128)(2,1)S(1)}, u32[]{:S(2)}, u32[]{:S(2)}) collective-permute-start(bf16[512,128]{1,0:T(8,128)(2,1)S(1)} %get-tuple-element.39.refs_0_), channel_id=1, source_target_pairs={{0,3},{1,0},{2,1},{3,2},{4,7},{5,4},{6,5},{7,6},{8,11},{9,8},{10,9... | collective-permute-start | bytes 393224 | tf_op jit(solution)/shard_map/ppermute | solution.py:17
  12.5 2.6 %collective-permute-start.4 = (bf16[512,128]{1,0:T(8,128)(2,1)S(1)}, bf16[512,128]{1,0:T(8,128)(2,1)S(1)}, u32[]{:S(2)}, u32[]{:S(2)}) collective-permute-start(bf16[512,128]{1,0:T(8,128)(2,1)S(1)} %get-tuple-element.40.refs_5_), channel_id=1, source_target_pairs={{0,28},{4,0},{8,4},{12,8},{16,12},{20,16},{24,20},{28,24},{1,29},{... | collective-permute-start | bytes 393224 | tf_op jit(solution)/shard_map/ppermute | solution.py:17
  15.9 1.2 copy-done.2
  17.1 5.9 %shard_map.184 = (bf16[16,128,128]{2,1,0:T(8,128)(2,1)S(1)}, bf16[16,128,128]{2,1,0:T(8,128)(2,1)S(1)}, bf16[16,128,128]{2,1,0:T(8,128)(2,1)S(1)}, s32[16]{0:T(128)S(1)}, s32[16]{0:T(128)S(1)}) custom-call(s32[1,1]{1,0:T(1,128)S(6)} %copy.20.tile_count, s32[16,128,128]{2,1,0:T(8,128)S(1)} %bitcast.4), custom_call_target="tpu_custom_call" | custom-call | flops 268435456 | bytes 2621440 | tf_op jit(solution)/shard_map/pallas_call | solution.py:38
  23.7 16.8 %shard_map.186 = (bf16[512,128]{1,0:T(8,128)(2,1)S(1)}, f32[512,128]{1,0:T(8,128)S(1)}, bf16[512,128]{1,0:T(8,128)(2,1)S(1)}, bf16[512,128]{1,0:T(8,128)(2,1)S(1...) custom-call(s32[1,1,16]{2,1,0:T(1,128)S(1)} %copy-done.17, s32[1,1,16]{2,1,0:T(1,128)S(1)} %copy-done.18, ...), custom_call_target="tpu_custom_call" | custom-call | flops 2147483648 | bytes 3014656 | tf_op jit(solution)/shard_map/pallas_call | solution.py:38
  40.5 2.6 %collective-permute-start.6 = (bf16[512,128]{1,0:T(8,128)(2,1)S(1)}, bf16[512,128]{1,0:T(8,128)(2,1)S(1)}, u32[]{:S(2)}, u32[]{:S(2)}) collective-permute-start(bf16[512,128]{1,0:T(8,128)(2,1)S(1)} %get-tuple-element.43), channel_id=1, source_target_pairs={{0,28},{4,0},{8,4},{12,8},{16,12},{20,16},{24,20},{28,24},{1,29},{... | collective-permute-start | bytes 393224 | tf_op jit(solution)/shard_map/ppermute | solution.py:17
  43.2 2.6 %collective-permute-start.8 = (bf16[512,128]{1,0:T(8,128)(2,1)S(1)}, bf16[512,128]{1,0:T(8,128)(2,1)S(1)}, u32[]{:S(2)}, u32[]{:S(2)}) collective-permute-start(bf16[512,128]{1,0:T(8,128)(2,1)S(1)} %get-tuple-element.47), channel_id=1, source_target_pairs={{0,28},{4,0},{8,4},{12,8},{16,12},{20,16},{24,20},{28,24},{1,29},{... | collective-permute-start | bytes 393224 | tf_op jit(solution)/shard_map/ppermute | solution.py:17
  45.8 0.7 collective-permute-done.5.sum_low
  47.2 1.7 %shard_map.187 = (bf16[512,128]{1,0:T(8,128)(2,1)}, bf16[512,128]{1,0:T(8,128)(2,1)S(1)}, bf16[512,128]{1,0:T(8,128)(2,1)S(1)}, bf16[512,128]{1,0:T(8,128)(2,1)S...) custom-call(bf16[512,128]{1,0:T(8,128)(2,1)S(1)} %copy-done.1, ...), custom_call_target="tpu_custom_call" | custom-call | flops 117440512 | bytes 1967104 | tf_op jit(solution)/shard_map/pallas_call | solution.py:38
  49.5 0.7 collective-permute-start.19
  50.2 1.4 %collective-permute-start.17 = (bf16[160,128]{1,0:T(8,128)(2,1)S(1)}, bf16[160,128]{1,0:T(8,128)(2,1)S(1)}, u32[]{:S(2)}, u32[]{:S(2)}) collective-permute-start(bf16[160,128]{1,0:T(8,128)(2,1)S(1)} %get-tuple-element.63), channel_id=1, source_target_pairs={{0,1},{1,2},{2,3},{3,0},{4,5},{5,6},{6,7},{7,4},{8,9},{9,10},{10,1... | collective-permute-start | bytes 122888 | tf_op jit(solution)/shard_map/ppermute | solution.py:17
  51.6 2.4 %collective-permute-done.19 = bf16[160,128]{1,0:T(8,128)(2,1)S(1)} collective-permute-done((bf16[160,128]{1,0:T(8,128)(2,1)S(1)}, bf16[160,128]{1,0:T(8,128)(2,1)S(1)}, u32[]{:S(2)}, u32[]{:S(2)}) %collective-permute-start.19) | collective-permute-done | bytes 40992 | tf_op jit(solution)/shard_map/ppermute | solution.py:17
  54.0 1.1 collective-permute-done.18
  55.1 1.2 collective-permute-done.17
  56.5 0.7 collective-permute-start.22
  57.2 2.5 %collective-permute-start.23 = (bf16[160,128]{1,0:T(8,128)(2,1)S(1)}, bf16[160,128]{1,0:T(8,128)(2,1)S(1)}, u32[]{:S(2)}, u32[]{:S(2)}) collective-permute-start(bf16[160,128]{1,0:T(8,128)(2,1)S(1)} %add_convert_fusion.refs_0_), channel_id=1, source_target_pairs={{0,16},{4,20},{8,24},{12,28},{16,0},{20,4},{24,8},{28,12},{1,17},{... | collective-permute-start | bytes 122888 | tf_op jit(solution)/shard_map/ppermute | solution.py:17
  59.7 1.1 collective-permute-done.20.refs_1_
  60.8 1.6 %collective-permute-start.25 = (bf16[160,128]{1,0:T(8,128)(2,1)S(1)}, bf16[160,128]{1,0:T(8,128)(2,1)S(1)}, u32[]{:S(2)}, u32[]{:S(2)}) collective-permute-start(bf16[160,128]{1,0:T(8,128)(2,1)S(1)} %add_convert_fusion.refs_0_), channel_id=1, source_target_pairs={{0,24},{4,28},{8,0},{12,4},{16,8},{20,12},{24,16},{28,20},{1,25},{... | collective-permute-start | bytes 122888 | tf_op jit(solution)/shard_map/ppermute | solution.py:17
  62.4 0.9 collective-permute-start.26
  63.4 2.0 %collective-permute-start.12 = (bf16[512,128]{1,0:T(8,128)(2,1)S(1)}, bf16[512,128]{1,0:T(8,128)(2,1)S(1)}, u32[]{:S(2)}, u32[]{:S(2)}) collective-permute-start(bf16[512,128]{1,0:T(8,128)(2,1)S(1)} %copy-done.1), channel_id=1, source_target_pairs={{0,2},{1,3},{2,0},{3,1},{4,6},{5,7},{6,4},{7,5},{8,10},{9,11},{10,... | collective-permute-start | bytes 393224 | tf_op jit(solution)/shard_map/ppermute | solution.py:17
  65.4 1.7 %collective-permute-start.13 = (bf16[512,128]{1,0:T(8,128)(2,1)S(1)}, bf16[512,128]{1,0:T(8,128)(2,1)S(1)}, u32[]{:S(2)}, u32[]{:S(2)}) collective-permute-start(bf16[512,128]{1,0:T(8,128)(2,1)S(1)} %copy-done.1), channel_id=1, source_target_pairs={{0,3},{1,0},{2,1},{3,2},{4,7},{5,4},{6,5},{7,6},{8,11},{9,8},{10,9... | collective-permute-start | bytes 393224 | tf_op jit(solution)/shard_map/ppermute | solution.py:17
  67.1 2.6 %collective-permute-start.10 = (bf16[512,128]{1,0:T(8,128)(2,1)S(1)}, bf16[512,128]{1,0:T(8,128)(2,1)S(1)}, u32[]{:S(2)}, u32[]{:S(2)}) collective-permute-start(bf16[512,128]{1,0:T(8,128)(2,1)S(1)} %get-tuple-element.57.refs_8_), channel_id=1, source_target_pairs={{0,28},{4,0},{8,4},{12,8},{16,12},{20,16},{24,20},{28,24},{1,29},{... | collective-permute-start | bytes 393224 | tf_op jit(solution)/shard_map/ppermute | solution.py:17
  69.9 1.6 %collective-permute-done.11.refs_11_ = bf16[512,128]{1,0:T(8,128)(2,1)S(1)} collective-permute-done((bf16[512,128]{1,0:T(8,128)(2,1)S(1)}, bf16[512,128]{1,0:T(8,128)(2,1)S(1)}, u32[]{:S(2)}, u32[]{:S(2)}) %collective-permute-start.11) | collective-permute-done | bytes 131104 | tf_op jit(solution)/shard_map/ppermute | solution.py:17
  71.5 4.7 %collective-permute-done.12.refs_12_ = bf16[512,128]{1,0:T(8,128)(2,1)S(1)} collective-permute-done((bf16[512,128]{1,0:T(8,128)(2,1)S(1)}, bf16[512,128]{1,0:T(8,128)(2,1)S(1)}, u32[]{:S(2)}, u32[]{:S(2)}) %collective-permute-start.12) | collective-permute-done | bytes 131104 | tf_op jit(solution)/shard_map/ppermute | solution.py:17
  76.2 18.2 %shard_map.189 = (f32[512,128]{1,0:T(8,128)S(1)}, bf16[512,128]{1,0:T(8,128)(2,1)S(1)}, bf16[512,128]{1,0:T(8,128)(2,1)S(1)}, bf16[512,128]{1,0:T(8,128)(2,1)S(1)}, bf16[128,128]{1,0:T(8,128)(2,1)S(1)}) custom-call(s32[1,1,16]{2,1,0:T(1,128)S(1)} %copy-done.17, s32[1,1,16]{2,1,0:T(1,128)S(1)} %copy-done.18, s32[1,1]{1,0:T(1,128)S(6)} %copy.20.tile_count, ...), custom_call_target="tpu_custom_call" | custom-call | flops 2147483648 | bytes 3047424 | tf_op jit(solution)/shard_map/pallas_call | solution.py:38
  94.7 3.1 %collective-permute-start.33 = (bf16[128,128]{1,0:T(8,128)(2,1)S(1)}, bf16[128,128]{1,0:T(8,128)(2,1)S(1)}, u32[]{:S(2)}, u32[]{:S(2)}) collective-permute-start(bf16[128,128]{1,0:T(8,128)(2,1)S(1)} %get-tuple-element.66.refs_0_), channel_id=1, source_target_pairs={{0,16},{4,20},{8,24},{12,28},{16,0},{20,4},{24,8},{28,12},{1,17},{... | collective-permute-start | bytes 98312 | tf_op jit(solution)/shard_map/ppermute | solution.py:17
  97.8 1.0 collective-permute-done.30.refs_1_
  98.8 1.7 %collective-permute-start.35 = (bf16[128,128]{1,0:T(8,128)(2,1)S(1)}, bf16[128,128]{1,0:T(8,128)(2,1)S(1)}, u32[]{:S(2)}, u32[]{:S(2)}) collective-permute-start(bf16[128,128]{1,0:T(8,128)(2,1)S(1)} %get-tuple-element.66.refs_0_), channel_id=1, source_target_pairs={{0,24},{4,28},{8,0},{12,4},{16,8},{20,12},{24,16},{28,20},{1,25},{... | collective-permute-start | bytes 98312 | tf_op jit(solution)/shard_map/ppermute | solution.py:17
  100.4 1.5 %collective-permute-start.15 = (bf16[512,128]{1,0:T(8,128)(2,1)S(1)}, bf16[512,128]{1,0:T(8,128)(2,1)S(1)}, u32[]{:S(2)}, u32[]{:S(2)}) collective-permute-start(bf16[512,128]{1,0:T(8,128)(2,1)S(1)} %get-tuple-element.60), channel_id=1, source_target_pairs={{0,2},{1,3},{2,0},{3,1},{4,6},{5,7},{6,4},{7,5},{8,10},{9,11},{10,... | collective-permute-start | bytes 393224 | tf_op jit(solution)/shard_map/ppermute | solution.py:17
  102.0 2.0 %collective-permute-start.16 = (bf16[512,128]{1,0:T(8,128)(2,1)S(1)}, bf16[512,128]{1,0:T(8,128)(2,1)S(1)}, u32[]{:S(2)}, u32[]{:S(2)}) collective-permute-start(bf16[512,128]{1,0:T(8,128)(2,1)S(1)} %get-tuple-element.61), channel_id=1, source_target_pairs={{0,1},{1,2},{2,3},{3,0},{4,5},{5,6},{6,7},{7,4},{8,9},{9,10},{10,1... | collective-permute-start | bytes 393224 | tf_op jit(solution)/shard_map/ppermute | solution.py:17
  103.9 0.7 collective-permute-start.36
  104.6 0.9 collective-permute-start.28
  105.5 0.7 collective-permute-done.36.refs_7_
  106.2 2.4 %collective-permute-start.29 = (bf16[160,128]{1,0:T(8,128)(2,1)S(1)}, bf16[160,128]{1,0:T(8,128)(2,1)S(1)}, u32[]{:S(2)}, u32[]{:S(2)}) collective-permute-start(bf16[160,128]{1,0:T(8,128)(2,1)S(1)} %shard_map.190.refs_6_), channel_id=1, source_target_pairs={{0,3},{1,0},{2,1},{3,2},{4,7},{5,4},{6,5},{7,6},{8,11},{9,8},{10,9... | collective-permute-start | bytes 122888 | tf_op jit(solution)/shard_map/ppermute | solution.py:17
  108.7 7.7 %collective-permute-done.28.refs_8_ = bf16[160,128]{1,0:T(8,128)(2,1)S(1)} collective-permute-done((bf16[160,128]{1,0:T(8,128)(2,1)S(1)}, bf16[160,128]{1,0:T(8,128)(2,1)S(1)}, u32[]{:S(2)}, u32[]{:S(2)}) %collective-permute-start.28) | collective-permute-done | bytes 40992 | tf_op jit(solution)/shard_map/ppermute | solution.py:17
  116.4 3.3 %collective-permute-start.38 = (bf16[128,128]{1,0:T(8,128)(2,1)S(1)}, bf16[128,128]{1,0:T(8,128)(2,1)S(1)}, u32[]{:S(2)}, u32[]{:S(2)}) collective-permute-start(bf16[128,128]{1,0:T(8,128)(2,1)S(1)} %shard_map.191.refs_10_), channel_id=1, source_target_pairs={{0,2},{1,3},{2,0},{3,1},{4,6},{5,7},{6,4},{7,5},{8,10},{9,11},{10,... | collective-permute-start | bytes 98312 | tf_op jit(solution)/shard_map/ppermute | solution.py:17
  119.7 2.5 %collective-permute-done.37.refs_11_ = bf16[128,128]{1,0:T(8,128)(2,1)S(1)} collective-permute-done((bf16[128,128]{1,0:T(8,128)(2,1)S(1)}, bf16[128,128]{1,0:T(8,128)(2,1)S(1)}, u32[]{:S(2)}, u32[]{:S(2)}) %collective-permute-start.37) | collective-permute-done | bytes 32800 | tf_op jit(solution)/shard_map/ppermute | solution.py:17
  122.2 1.1 collective-permute-start.39
  123.3 2.8 %collective-permute-done.39.refs_13_ = bf16[128,128]{1,0:T(8,128)(2,1)S(1)} collective-permute-done((bf16[128,128]{1,0:T(8,128)(2,1)S(1)}, bf16[128,128]{1,0:T(8,128)(2,1)S(1)}, u32[]{:S(2)}, u32[]{:S(2)}) %collective-permute-start.39) | collective-permute-done | bytes 32800 | tf_op jit(solution)/shard_map/ppermute | solution.py:17
  126.1 1.0 shard_map.192
  (80 shorter events, 3.1 us)
Async XLA Ops:
  5.5 17.4 %collective-permute-start = (bf16[512,128]{1,0:T(8,128)(2,1)S(1)}, bf16[512,128]{1,0:T(8,128)(2,1)S(1)}, u32[]{:S(2)}, u32[]{:S(2)}) collective-permute-start(bf16[512,128]{1,0:T(8,128)(2,1)S(1)} %get-tuple-element.39.refs_0_), channel_id=1, source_target_pairs={{0,1},{1,2},{2,3},{3,0},{4,5},{5,6},{6,7},{7,4},{8,9},{9,10},{10,1... | collective-permute-start | bytes 393224 | tf_op jit(solution)/shard_map/ppermute | solution.py:17
  8.6 14.3 %collective-permute-start.1 = (bf16[512,128]{1,0:T(8,128)(2,1)S(1)}, bf16[512,128]{1,0:T(8,128)(2,1)S(1)}, u32[]{:S(2)}, u32[]{:S(2)}) collective-permute-start(bf16[512,128]{1,0:T(8,128)(2,1)S(1)} %get-tuple-element.39.refs_0_), channel_id=1, source_target_pairs={{0,2},{1,3},{2,0},{3,1},{4,6},{5,7},{6,4},{7,5},{8,10},{9,11},{10,... | collective-permute-start | bytes 393224 | tf_op jit(solution)/shard_map/ppermute | solution.py:17
  11.2 11.8 %collective-permute-start.2 = (bf16[512,128]{1,0:T(8,128)(2,1)S(1)}, bf16[512,128]{1,0:T(8,128)(2,1)S(1)}, u32[]{:S(2)}, u32[]{:S(2)}) collective-permute-start(bf16[512,128]{1,0:T(8,128)(2,1)S(1)} %get-tuple-element.39.refs_0_), channel_id=1, source_target_pairs={{0,3},{1,0},{2,1},{3,2},{4,7},{5,4},{6,5},{7,6},{8,11},{9,8},{10,9... | collective-permute-start | bytes 393224 | tf_op jit(solution)/shard_map/ppermute | solution.py:17
  12.5 10.4 %collective-permute-start.3 = (bf16[512,128]{1,0:T(8,128)(2,1)S(1)}, bf16[512,128]{1,0:T(8,128)(2,1)S(1)}, u32[]{:S(2)}, u32[]{:S(2)}) collective-permute-start(bf16[512,128]{1,0:T(8,128)(2,1)S(1)} %get-tuple-element.40.refs_5_), channel_id=1, source_target_pairs={{0,4},{4,8},{8,12},{12,16},{16,20},{20,24},{24,28},{28,0},{1,5},{5... | collective-permute-start | bytes 393224 | tf_op jit(solution)/shard_map/ppermute | solution.py:17
  12.5 10.4 %collective-permute-start.4 = (bf16[512,128]{1,0:T(8,128)(2,1)S(1)}, bf16[512,128]{1,0:T(8,128)(2,1)S(1)}, u32[]{:S(2)}, u32[]{:S(2)}) collective-permute-start(bf16[512,128]{1,0:T(8,128)(2,1)S(1)} %get-tuple-element.40.refs_5_), channel_id=1, source_target_pairs={{0,28},{4,0},{8,4},{12,8},{16,12},{20,16},{24,20},{28,24},{1,29},{... | collective-permute-start | bytes 393224 | tf_op jit(solution)/shard_map/ppermute | solution.py:17
  23.7 22.9 %copy-start.1 = (bf16[512,128]{1,0:T(8,128)(2,1)S(1)}, bf16[512,128]{1,0:T(8,128)(2,1)}, u32[]{:S(2)}) copy-start(bf16[512,128]{1,0:T(8,128)(2,1)} %refs_10_.1) | copy-start | bytes 393220
  23.7 22.9 %copy-start.3 = (bf16[512,128]{1,0:T(8,128)(2,1)S(1)}, bf16[512,128]{1,0:T(8,128)(2,1)}, u32[]{:S(2)}) copy-start(bf16[512,128]{1,0:T(8,128)(2,1)} %cotangent.3) | copy-start | bytes 393220
  23.7 22.9 %copy-start.6 = (bf16[128,128]{1,0:T(8,128)(2,1)S(1)}, bf16[128,128]{1,0:T(8,128)(2,1)}, u32[]{:S(2)}) copy-start(bf16[128,128]{1,0:T(8,128)(2,1)} %w_edge_out.3) | copy-start | bytes 98308
  23.7 22.9 %copy-start.7 = (bf16[128,128]{1,0:T(8,128)(2,1)S(1)}, bf16[128,128]{1,0:T(8,128)(2,1)}, u32[]{:S(2)}) copy-start(bf16[128,128]{1,0:T(8,128)(2,1)} %w_node_self.3) | copy-start | bytes 98308
  23.7 22.9 %copy-start.10 = (bf16[128,128]{1,0:T(8,128)(2,1)S(1)}, bf16[128,128]{1,0:T(8,128)(2,1)}, u32[]{:S(2)}) copy-start(bf16[128,128]{1,0:T(8,128)(2,1)} %w_node_msg.1) | copy-start | bytes 98308
  23.7 22.9 %copy-start.11 = (bf16[128,128]{1,0:T(8,128)(2,1)S(1)}, bf16[128,128]{1,0:T(8,128)(2,1)}, u32[]{:S(2)}) copy-start(bf16[128,128]{1,0:T(8,128)(2,1)} %w_node_out.1) | copy-start | bytes 98308
  40.5 6.1 %collective-permute-start.5 = (bf16[512,128]{1,0:T(8,128)(2,1)S(1)}, bf16[512,128]{1,0:T(8,128)(2,1)S(1)}, u32[]{:S(2)}, u32[]{:S(2)}) collective-permute-start(bf16[512,128]{1,0:T(8,128)(2,1)S(1)} %get-tuple-element.42), channel_id=1, source_target_pairs={{0,4},{4,8},{8,12},{12,16},{16,20},{20,24},{24,28},{28,0},{1,5},{5... | collective-permute-start | bytes 393224 | tf_op jit(solution)/shard_map/ppermute | solution.py:17
  40.5 6.0 %collective-permute-start.6 = (bf16[512,128]{1,0:T(8,128)(2,1)S(1)}, bf16[512,128]{1,0:T(8,128)(2,1)S(1)}, u32[]{:S(2)}, u32[]{:S(2)}) collective-permute-start(bf16[512,128]{1,0:T(8,128)(2,1)S(1)} %get-tuple-element.43), channel_id=1, source_target_pairs={{0,28},{4,0},{8,4},{12,8},{16,12},{20,16},{24,20},{28,24},{1,29},{... | collective-permute-start | bytes 393224 | tf_op jit(solution)/shard_map/ppermute | solution.py:17
  43.2 5.7 %collective-permute-start.7 = (bf16[512,128]{1,0:T(8,128)(2,1)S(1)}, bf16[512,128]{1,0:T(8,128)(2,1)S(1)}, u32[]{:S(2)}, u32[]{:S(2)}) collective-permute-start(bf16[512,128]{1,0:T(8,128)(2,1)S(1)} %get-tuple-element.46), channel_id=1, source_target_pairs={{0,4},{4,8},{8,12},{12,16},{16,20},{20,24},{24,28},{28,0},{1,5},{5... | collective-permute-start | bytes 393224 | tf_op jit(solution)/shard_map/ppermute | solution.py:17
  43.2 5.7 %collective-permute-start.8 = (bf16[512,128]{1,0:T(8,128)(2,1)S(1)}, bf16[512,128]{1,0:T(8,128)(2,1)S(1)}, u32[]{:S(2)}, u32[]{:S(2)}) collective-permute-start(bf16[512,128]{1,0:T(8,128)(2,1)S(1)} %get-tuple-element.47), channel_id=1, source_target_pairs={{0,28},{4,0},{8,4},{12,8},{16,12},{20,16},{24,20},{28,24},{1,29},{... | collective-permute-start | bytes 393224 | tf_op jit(solution)/shard_map/ppermute | solution.py:17
  47.2 1.7 %copy-start.5 = (bf16[128,128]{1,0:T(8,128)(2,1)S(1)}, bf16[128,128]{1,0:T(8,128)(2,1)}, u32[]{:S(2)}) copy-start(bf16[128,128]{1,0:T(8,128)(2,1)} %w_recv.3) | copy-start | bytes 98308
  49.5 4.5 %collective-permute-start.19 = (bf16[160,128]{1,0:T(8,128)(2,1)S(1)}, bf16[160,128]{1,0:T(8,128)(2,1)S(1)}, u32[]{:S(2)}, u32[]{:S(2)}) collective-permute-start(bf16[160,128]{1,0:T(8,128)(2,1)S(1)} %get-tuple-element.65), channel_id=1, source_target_pairs={{0,3},{1,0},{2,1},{3,2},{4,7},{5,4},{6,5},{7,6},{8,11},{9,8},{10,9... | collective-permute-start | bytes 122888 | tf_op jit(solution)/shard_map/ppermute | solution.py:17
  50.2 4.9 %collective-permute-start.18 = (bf16[160,128]{1,0:T(8,128)(2,1)S(1)}, bf16[160,128]{1,0:T(8,128)(2,1)S(1)}, u32[]{:S(2)}, u32[]{:S(2)}) collective-permute-start(bf16[160,128]{1,0:T(8,128)(2,1)S(1)} %get-tuple-element.64), channel_id=1, source_target_pairs={{0,2},{1,3},{2,0},{3,1},{4,6},{5,7},{6,4},{7,5},{8,10},{9,11},{10,... | collective-permute-start | bytes 122888 | tf_op jit(solution)/shard_map/ppermute | solution.py:17
  50.2 6.1 %collective-permute-start.17 = (bf16[160,128]{1,0:T(8,128)(2,1)S(1)}, bf16[160,128]{1,0:T(8,128)(2,1)S(1)}, u32[]{:S(2)}, u32[]{:S(2)}) collective-permute-start(bf16[160,128]{1,0:T(8,128)(2,1)S(1)} %get-tuple-element.63), channel_id=1, source_target_pairs={{0,1},{1,2},{2,3},{3,0},{4,5},{5,6},{6,7},{7,4},{8,9},{9,10},{10,1... | collective-permute-start | bytes 122888 | tf_op jit(solution)/shard_map/ppermute | solution.py:17
  56.4 4.4 %collective-permute-start.20 = (bf16[160,128]{1,0:T(8,128)(2,1)S(1)}, bf16[160,128]{1,0:T(8,128)(2,1)S(1)}, u32[]{:S(2)}, u32[]{:S(2)}) collective-permute-start(bf16[160,128]{1,0:T(8,128)(2,1)S(1)} %add_convert_fusion.refs_0_), channel_id=1, source_target_pairs={{0,4},{4,8},{8,12},{12,16},{16,20},{20,24},{24,28},{28,0},{1,5},{5... | collective-permute-start | bytes 122888 | tf_op jit(solution)/shard_map/ppermute | solution.py:17
  56.5 5.9 %collective-permute-start.21 = (bf16[160,128]{1,0:T(8,128)(2,1)S(1)}, bf16[160,128]{1,0:T(8,128)(2,1)S(1)}, u32[]{:S(2)}, u32[]{:S(2)}) collective-permute-start(bf16[160,128]{1,0:T(8,128)(2,1)S(1)} %add_convert_fusion.refs_0_), channel_id=1, source_target_pairs={{0,8},{4,12},{8,16},{12,20},{16,24},{20,28},{24,0},{28,4},{1,9},{5... | collective-permute-start | bytes 122888 | tf_op jit(solution)/shard_map/ppermute | solution.py:17
  56.5 6.7 %collective-permute-start.22 = (bf16[160,128]{1,0:T(8,128)(2,1)S(1)}, bf16[160,128]{1,0:T(8,128)(2,1)S(1)}, u32[]{:S(2)}, u32[]{:S(2)}) collective-permute-start(bf16[160,128]{1,0:T(8,128)(2,1)S(1)} %add_convert_fusion.refs_0_), channel_id=1, source_target_pairs={{0,12},{4,16},{8,20},{12,24},{16,28},{20,0},{24,4},{28,8},{1,13},{... | collective-permute-start | bytes 122888 | tf_op jit(solution)/shard_map/ppermute | solution.py:17
  57.2 6.1 %collective-permute-start.23 = (bf16[160,128]{1,0:T(8,128)(2,1)S(1)}, bf16[160,128]{1,0:T(8,128)(2,1)S(1)}, u32[]{:S(2)}, u32[]{:S(2)}) collective-permute-start(bf16[160,128]{1,0:T(8,128)(2,1)S(1)} %add_convert_fusion.refs_0_), channel_id=1, source_target_pairs={{0,16},{4,20},{8,24},{12,28},{16,0},{20,4},{24,8},{28,12},{1,17},{... | collective-permute-start | bytes 122888 | tf_op jit(solution)/shard_map/ppermute | solution.py:17
  59.7 5.7 %collective-permute-start.24 = (bf16[160,128]{1,0:T(8,128)(2,1)S(1)}, bf16[160,128]{1,0:T(8,128)(2,1)S(1)}, u32[]{:S(2)}, u32[]{:S(2)}) collective-permute-start(bf16[160,128]{1,0:T(8,128)(2,1)S(1)} %add_convert_fusion.refs_0_), channel_id=1, source_target_pairs={{0,20},{4,24},{8,28},{12,0},{16,4},{20,8},{24,12},{28,16},{1,21},{... | collective-permute-start | bytes 122888 | tf_op jit(solution)/shard_map/ppermute | solution.py:17
  60.8 6.3 %collective-permute-start.25 = (bf16[160,128]{1,0:T(8,128)(2,1)S(1)}, bf16[160,128]{1,0:T(8,128)(2,1)S(1)}, u32[]{:S(2)}, u32[]{:S(2)}) collective-permute-start(bf16[160,128]{1,0:T(8,128)(2,1)S(1)} %add_convert_fusion.refs_0_), channel_id=1, source_target_pairs={{0,24},{4,28},{8,0},{12,4},{16,8},{20,12},{24,16},{28,20},{1,25},{... | collective-permute-start | bytes 122888 | tf_op jit(solution)/shard_map/ppermute | solution.py:17
  62.4 4.8 %collective-permute-start.26 = (bf16[160,128]{1,0:T(8,128)(2,1)S(1)}, bf16[160,128]{1,0:T(8,128)(2,1)S(1)}, u32[]{:S(2)}, u32[]{:S(2)}) collective-permute-start(bf16[160,128]{1,0:T(8,128)(2,1)S(1)} %add_convert_fusion.refs_0_), channel_id=1, source_target_pairs={{0,28},{4,0},{8,4},{12,8},{16,12},{20,16},{24,20},{28,24},{1,29},{... | collective-permute-start | bytes 122888 | tf_op jit(solution)/shard_map/ppermute | solution.py:17
  63.2 8.3 %collective-permute-start.11 = (bf16[512,128]{1,0:T(8,128)(2,1)S(1)}, bf16[512,128]{1,0:T(8,128)(2,1)S(1)}, u32[]{:S(2)}, u32[]{:S(2)}) collective-permute-start(bf16[512,128]{1,0:T(8,128)(2,1)S(1)} %copy-done.1), channel_id=1, source_target_pairs={{0,1},{1,2},{2,3},{3,0},{4,5},{5,6},{6,7},{7,4},{8,9},{9,10},{10,1... | collective-permute-start | bytes 393224 | tf_op jit(solution)/shard_map/ppermute | solution.py:17
  63.4 12.9 %collective-permute-start.12 = (bf16[512,128]{1,0:T(8,128)(2,1)S(1)}, bf16[512,128]{1,0:T(8,128)(2,1)S(1)}, u32[]{:S(2)}, u32[]{:S(2)}) collective-permute-start(bf16[512,128]{1,0:T(8,128)(2,1)S(1)} %copy-done.1), channel_id=1, source_target_pairs={{0,2},{1,3},{2,0},{3,1},{4,6},{5,7},{6,4},{7,5},{8,10},{9,11},{10,... | collective-permute-start | bytes 393224 | tf_op jit(solution)/shard_map/ppermute | solution.py:17
  65.4 10.8 %collective-permute-start.13 = (bf16[512,128]{1,0:T(8,128)(2,1)S(1)}, bf16[512,128]{1,0:T(8,128)(2,1)S(1)}, u32[]{:S(2)}, u32[]{:S(2)}) collective-permute-start(bf16[512,128]{1,0:T(8,128)(2,1)S(1)} %copy-done.1), channel_id=1, source_target_pairs={{0,3},{1,0},{2,1},{3,2},{4,7},{5,4},{6,5},{7,6},{8,11},{9,8},{10,9... | collective-permute-start | bytes 393224 | tf_op jit(solution)/shard_map/ppermute | solution.py:17
  67.1 9.1 %collective-permute-start.9 = (bf16[512,128]{1,0:T(8,128)(2,1)S(1)}, bf16[512,128]{1,0:T(8,128)(2,1)S(1)}, u32[]{:S(2)}, u32[]{:S(2)}) collective-permute-start(bf16[512,128]{1,0:T(8,128)(2,1)S(1)} %get-tuple-element.57.refs_8_), channel_id=1, source_target_pairs={{0,4},{4,8},{8,12},{12,16},{16,20},{20,24},{24,28},{28,0},{1,5},{5... | collective-permute-start | bytes 393224 | tf_op jit(solution)/shard_map/ppermute | solution.py:17
  67.1 9.1 %collective-permute-start.10 = (bf16[512,128]{1,0:T(8,128)(2,1)S(1)}, bf16[512,128]{1,0:T(8,128)(2,1)S(1)}, u32[]{:S(2)}, u32[]{:S(2)}) collective-permute-start(bf16[512,128]{1,0:T(8,128)(2,1)S(1)} %get-tuple-element.57.refs_8_), channel_id=1, source_target_pairs={{0,28},{4,0},{8,4},{12,8},{16,12},{20,16},{24,20},{28,24},{1,29},{... | collective-permute-start | bytes 393224 | tf_op jit(solution)/shard_map/ppermute | solution.py:17
  71.5 26.3 %collective-permute-start.27 = (bf16[160,128]{1,0:T(8,128)(2,1)S(1)}, bf16[160,128]{1,0:T(8,128)(2,1)S(1)}, u32[]{:S(2)}, u32[]{:S(2)}) collective-permute-start(bf16[160,128]{1,0:T(8,128)(2,1)S(1)} %shard_map.190.refs_6_), channel_id=1, source_target_pairs={{0,1},{1,2},{2,3},{3,0},{4,5},{5,6},{6,7},{7,4},{8,9},{9,10},{10,1... | collective-permute-start | bytes 122888 | tf_op jit(solution)/shard_map/ppermute | solution.py:17
  94.5 4.3 %collective-permute-start.30 = (bf16[128,128]{1,0:T(8,128)(2,1)S(1)}, bf16[128,128]{1,0:T(8,128)(2,1)S(1)}, u32[]{:S(2)}, u32[]{:S(2)}) collective-permute-start(bf16[128,128]{1,0:T(8,128)(2,1)S(1)} %get-tuple-element.66.refs_0_), channel_id=1, source_target_pairs={{0,4},{4,8},{8,12},{12,16},{16,20},{20,24},{24,28},{28,0},{1,5},{5... | collective-permute-start | bytes 98312 | tf_op jit(solution)/shard_map/ppermute | solution.py:17
  94.5 5.9 %collective-permute-start.31 = (bf16[128,128]{1,0:T(8,128)(2,1)S(1)}, bf16[128,128]{1,0:T(8,128)(2,1)S(1)}, u32[]{:S(2)}, u32[]{:S(2)}) collective-permute-start(bf16[128,128]{1,0:T(8,128)(2,1)S(1)} %get-tuple-element.66.refs_0_), channel_id=1, source_target_pairs={{0,8},{4,12},{8,16},{12,20},{16,24},{20,28},{24,0},{28,4},{1,9},{5... | collective-permute-start | bytes 98312 | tf_op jit(solution)/shard_map/ppermute | solution.py:17
  94.6 5.9 %collective-permute-start.32 = (bf16[128,128]{1,0:T(8,128)(2,1)S(1)}, bf16[128,128]{1,0:T(8,128)(2,1)S(1)}, u32[]{:S(2)}, u32[]{:S(2)}) collective-permute-start(bf16[128,128]{1,0:T(8,128)(2,1)S(1)} %get-tuple-element.66.refs_0_), channel_id=1, source_target_pairs={{0,12},{4,16},{8,20},{12,24},{16,28},{20,0},{24,4},{28,8},{1,13},{... | collective-permute-start | bytes 98312 | tf_op jit(solution)/shard_map/ppermute | solution.py:17
  94.7 7.3 %collective-permute-start.33 = (bf16[128,128]{1,0:T(8,128)(2,1)S(1)}, bf16[128,128]{1,0:T(8,128)(2,1)S(1)}, u32[]{:S(2)}, u32[]{:S(2)}) collective-permute-start(bf16[128,128]{1,0:T(8,128)(2,1)S(1)} %get-tuple-element.66.refs_0_), channel_id=1, source_target_pairs={{0,16},{4,20},{8,24},{12,28},{16,0},{20,4},{24,8},{28,12},{1,17},{... | collective-permute-start | bytes 98312 | tf_op jit(solution)/shard_map/ppermute | solution.py:17
  97.8 6.2 %collective-permute-start.34 = (bf16[128,128]{1,0:T(8,128)(2,1)S(1)}, bf16[128,128]{1,0:T(8,128)(2,1)S(1)}, u32[]{:S(2)}, u32[]{:S(2)}) collective-permute-start(bf16[128,128]{1,0:T(8,128)(2,1)S(1)} %get-tuple-element.66.refs_0_), channel_id=1, source_target_pairs={{0,20},{4,24},{8,28},{12,0},{16,4},{20,8},{24,12},{28,16},{1,21},{... | collective-permute-start | bytes 98312 | tf_op jit(solution)/shard_map/ppermute | solution.py:17
  98.8 5.8 %collective-permute-start.35 = (bf16[128,128]{1,0:T(8,128)(2,1)S(1)}, bf16[128,128]{1,0:T(8,128)(2,1)S(1)}, u32[]{:S(2)}, u32[]{:S(2)}) collective-permute-start(bf16[128,128]{1,0:T(8,128)(2,1)S(1)} %get-tuple-element.66.refs_0_), channel_id=1, source_target_pairs={{0,24},{4,28},{8,0},{12,4},{16,8},{20,12},{24,16},{28,20},{1,25},{... | collective-permute-start | bytes 98312 | tf_op jit(solution)/shard_map/ppermute | solution.py:17
  100.4 25.7 %collective-permute-start.14 = (bf16[512,128]{1,0:T(8,128)(2,1)S(1)}, bf16[512,128]{1,0:T(8,128)(2,1)S(1)}, u32[]{:S(2)}, u32[]{:S(2)}) collective-permute-start(bf16[512,128]{1,0:T(8,128)(2,1)S(1)} %get-tuple-element.59), channel_id=1, source_target_pairs={{0,3},{1,0},{2,1},{3,2},{4,7},{5,4},{6,5},{7,6},{8,11},{9,8},{10,9... | collective-permute-start | bytes 393224 | tf_op jit(solution)/shard_map/ppermute | solution.py:17
  100.4 25.7 %collective-permute-start.15 = (bf16[512,128]{1,0:T(8,128)(2,1)S(1)}, bf16[512,128]{1,0:T(8,128)(2,1)S(1)}, u32[]{:S(2)}, u32[]{:S(2)}) collective-permute-start(bf16[512,128]{1,0:T(8,128)(2,1)S(1)} %get-tuple-element.60), channel_id=1, source_target_pairs={{0,2},{1,3},{2,0},{3,1},{4,6},{5,7},{6,4},{7,5},{8,10},{9,11},{10,... | collective-permute-start | bytes 393224 | tf_op jit(solution)/shard_map/ppermute | solution.py:17
  102.0 24.1 %copy-start.9 = (bf16[128,128]{1,0:T(8,128)(2,1)S(1)}, bf16[128,128]{1,0:T(8,128)(2,1)}, u32[]{:S(2)}) copy-start(bf16[128,128]{1,0:T(8,128)(2,1)} %refs_1_.1) | copy-start | bytes 98308
  102.0 24.1 %collective-permute-start.16 = (bf16[512,128]{1,0:T(8,128)(2,1)S(1)}, bf16[512,128]{1,0:T(8,128)(2,1)S(1)}, u32[]{:S(2)}, u32[]{:S(2)}) collective-permute-start(bf16[512,128]{1,0:T(8,128)(2,1)S(1)} %get-tuple-element.61), channel_id=1, source_target_pairs={{0,1},{1,2},{2,3},{3,0},{4,5},{5,6},{6,7},{7,4},{8,9},{9,10},{10,1... | collective-permute-start | bytes 393224 | tf_op jit(solution)/shard_map/ppermute | solution.py:17
  103.9 2.3 %collective-permute-start.36 = (bf16[128,128]{1,0:T(8,128)(2,1)S(1)}, bf16[128,128]{1,0:T(8,128)(2,1)S(1)}, u32[]{:S(2)}, u32[]{:S(2)}) collective-permute-start(bf16[128,128]{1,0:T(8,128)(2,1)S(1)} %get-tuple-element.66.refs_0_), channel_id=1, source_target_pairs={{0,28},{4,0},{8,4},{12,8},{16,12},{20,16},{24,20},{28,24},{1,29},{... | collective-permute-start | bytes 98312 | tf_op jit(solution)/shard_map/ppermute | solution.py:17
  104.6 11.8 %collective-permute-start.28 = (bf16[160,128]{1,0:T(8,128)(2,1)S(1)}, bf16[160,128]{1,0:T(8,128)(2,1)S(1)}, u32[]{:S(2)}, u32[]{:S(2)}) collective-permute-start(bf16[160,128]{1,0:T(8,128)(2,1)S(1)} %shard_map.190.refs_6_), channel_id=1, source_target_pairs={{0,2},{1,3},{2,0},{3,1},{4,6},{5,7},{6,4},{7,5},{8,10},{9,11},{10,... | collective-permute-start | bytes 122888 | tf_op jit(solution)/shard_map/ppermute | solution.py:17
  106.2 10.2 %collective-permute-start.29 = (bf16[160,128]{1,0:T(8,128)(2,1)S(1)}, bf16[160,128]{1,0:T(8,128)(2,1)S(1)}, u32[]{:S(2)}, u32[]{:S(2)}) collective-permute-start(bf16[160,128]{1,0:T(8,128)(2,1)S(1)} %shard_map.190.refs_6_), channel_id=1, source_target_pairs={{0,3},{1,0},{2,1},{3,2},{4,7},{5,4},{6,5},{7,6},{8,11},{9,8},{10,9... | collective-permute-start | bytes 122888 | tf_op jit(solution)/shard_map/ppermute | solution.py:17
  116.4 5.8 %collective-permute-start.37 = (bf16[128,128]{1,0:T(8,128)(2,1)S(1)}, bf16[128,128]{1,0:T(8,128)(2,1)S(1)}, u32[]{:S(2)}, u32[]{:S(2)}) collective-permute-start(bf16[128,128]{1,0:T(8,128)(2,1)S(1)} %shard_map.191.refs_10_), channel_id=1, source_target_pairs={{0,1},{1,2},{2,3},{3,0},{4,5},{5,6},{6,7},{7,4},{8,9},{9,10},{10,1... | collective-permute-start | bytes 98312 | tf_op jit(solution)/shard_map/ppermute | solution.py:17
  116.4 6.9 %collective-permute-start.38 = (bf16[128,128]{1,0:T(8,128)(2,1)S(1)}, bf16[128,128]{1,0:T(8,128)(2,1)S(1)}, u32[]{:S(2)}, u32[]{:S(2)}) collective-permute-start(bf16[128,128]{1,0:T(8,128)(2,1)S(1)} %shard_map.191.refs_10_), channel_id=1, source_target_pairs={{0,2},{1,3},{2,0},{3,1},{4,6},{5,7},{6,4},{7,5},{8,10},{9,11},{10,... | collective-permute-start | bytes 98312 | tf_op jit(solution)/shard_map/ppermute | solution.py:17
  122.2 3.9 %collective-permute-start.39 = (bf16[128,128]{1,0:T(8,128)(2,1)S(1)}, bf16[128,128]{1,0:T(8,128)(2,1)S(1)}, u32[]{:S(2)}, u32[]{:S(2)}) collective-permute-start(bf16[128,128]{1,0:T(8,128)(2,1)S(1)} %shard_map.191.refs_10_), channel_id=1, source_target_pairs={{0,3},{1,0},{2,1},{3,2},{4,7},{5,4},{6,5},{7,6},{8,11},{9,8},{10,9... | collective-permute-start | bytes 98312 | tf_op jit(solution)/shard_map/ppermute | solution.py:17
  (11 other events, 8.3 us)

commit v2 on v1

v2 whole, which is shorter than its diff:
```python
import jax
import jax.numpy as jnp
from jax import lax
from jax.experimental import pallas as pl
from jax.experimental.pallas import tpu as pltpu
from jax.sharding import PartitionSpec as P

F32 = jnp.float32
BF16 = jnp.bfloat16
RANKS = 4
FIRST = 3
TOGETHER = 4


def shifted(value, axis, steps):
    count = lax.axis_size(axis)
    pairs = [(source, (source + steps) % count) for source in range(count)]
    return lax.ppermute(value, axis, pairs)


def dot(left, right):
    return jnp.dot(left, right, preferred_element_type=F32)


def dot_t(left, right):
    return lax.dot_general(left, right, (((1,), (1,)), ((), ())), preferred_element_type=F32)


def contract_rows(left_rows, right_rows):
    return lax.dot_general(
        left_rows, right_rows, (((0,), (0,)), ((), ())), preferred_element_type=F32
    )


def call(kernel, outs, args, scalars=(), scratch=(), flops=0, smem_outs=(), grant=32):
    vmem = pl.BlockSpec(memory_space=pltpu.VMEM)
    smem = pl.BlockSpec(memory_space=pltpu.SMEM)
    moved = sum(a.size * a.dtype.itemsize for a in list(args) + list(outs))
    return pl.pallas_call(
        kernel,
        out_shape=[jax.ShapeDtypeStruct(o.shape, o.dtype) for o in list(outs) + list(smem_outs)],
        in_specs=[smem] * len(scalars) + [vmem] * len(args),
        out_specs=[vmem] * len(outs) + [smem] * len(smem_outs),
        scratch_shapes=list(scratch),
        compiler_params=pltpu.CompilerParams(vmem_limit_bytes=grant * 2**20),
        cost_estimate=pl.CostEstimate(flops=flops, bytes_accessed=moved, transcendentals=0),
    )(*scalars, *args)


def like(shape, dtype):
    return jax.ShapeDtypeStruct(tuple(shape), dtype)


def rows_kernel(latent, positions, w_send, w_recv, pos_weight, edge_bias, send_out, recv_out):
    count = positions.shape[1]
    padded = jnp.concatenate([positions[...], jnp.zeros((5, count), F32)], 0)
    columns = jnp.transpose(padded)
    placed = columns[:, 0:1] * pos_weight[0:1, :]
    placed = placed + columns[:, 1:2] * pos_weight[1:2, :]
    placed = placed + columns[:, 2:3] * pos_weight[2:3, :]
    rows = latent[...]
    send_out[...] = (dot(rows, w_send[...]) + placed).astype(BF16)
    recv_out[...] = (dot(rows, w_recv[...]) - placed + edge_bias[...]).astype(BF16)


def ranks_kernel(tile_count, mask, row_rank, row_degree, col_rank, row_most, col_most):
    size = mask.shape[-1]
    row_index = lax.broadcasted_iota(jnp.int32, (size, size), 0)
    col_index = lax.broadcasted_iota(jnp.int32, (size, size), 1)
    upper = (row_index <= col_index).astype(F32).astype(BF16)
    eye = (row_index == col_index).astype(F32).astype(BF16)
    ones = jnp.ones((size, size), BF16)
    for_rows = jnp.concatenate([upper, ones], 1)
    for_cols = jnp.concatenate([upper, eye], 1)

    def one_tile(tile):
        values = mask[tile].astype(F32)
        values_b = values.astype(BF16)
        found = dot(values_b, for_rows)
        row_rank[tile] = (found[:, :size] * values).astype(BF16)
        row_degree[tile] = found[:, size:].astype(BF16)
        row_most[tile] = jnp.max(found[:, size:]).astype(jnp.int32)
        found = contract_rows(values_b, for_cols)
        col_rank[tile] = (found[:, :size] * found[:, size:]).astype(BF16)
        col_most[tile] = jnp.max(found[:, :size]).astype(jnp.int32)

    tiles = mask.shape[0]
    together = TOGETHER if tiles % TOGETHER == 0 else 1

    def some_tiles(step, carry):
        for item in range(together):
            one_tile(step * together + item)
        return carry

    lax.fori_loop(0, (tile_count[0, 0] + together - 1) // together, some_tiles, 0)


def one_hots(rank_block, step, unit):
    found = []
    for item in range(RANKS):
        rank = jnp.asarray(step * RANKS + item + 1, jnp.int32).astype(F32).astype(BF16)
        hot = jnp.where(rank_block == rank, jnp.ones_like(unit), jnp.zeros_like(unit))
        found.append(jnp.concatenate([hot, unit], 1))
    return jnp.concatenate(found, 0)


def run_steps(one_step, most, start):
    running = start
    for step in range(FIRST):
        running = one_step(step, running)
    steps = jnp.maximum((most + RANKS - 1) // RANKS, FIRST)
    return steps, lax.fori_loop(FIRST, steps, one_step, running)


def eye_of(size):
    row_index = lax.broadcasted_iota(jnp.int32, (size, size), 0)
    col_index = lax.broadcasted_iota(jnp.int32, (size, size), 1)
    return (row_index == col_index).astype(F32).astype(BF16)


def lay_blocks(table, parts):
    size = table.shape[1]
    place = 0
    for part in parts:
        for block in range(part.shape[0] // size):
            table[place] = part[block * size : (block + 1) * size, :]
            place += 1


def sender_place(block, member, members, blocks):
    distance = lax.rem(member - block // blocks + members, members)
    return distance * blocks + lax.rem(block, blocks)


def make_forward(members, blocks):
    def kernel(tile_send, tile_recv, tile_count, row_most, row_rank, row_degree, *refs):
        send_parts, refs = refs[:members], refs[members:]
        recv_parts, refs = refs[:3], refs[3:]
        sums_out, counts_out, refs = refs[:3], refs[3:6], refs[6:]
        senders, receivers, sums, counts = refs
        size = senders.shape[1]
        member = lax.axis_index("grp")
        lay_blocks(senders, send_parts)
        lay_blocks(receivers, recv_parts)
        sums[...] = jnp.zeros_like(sums)
        counts[...] = jnp.zeros_like(counts)
        unit = eye_of(size)

        def one_tile(tile, carry):
            recv_place = tile_recv[0, 0, tile]
            recv_rows = receivers[recv_place]
            send_rows = senders[sender_place(tile_send[0, 0, tile], member, members, blocks)]
            right = jnp.concatenate([send_rows, recv_rows], 0)
            rank_block = row_rank[tile]

            def one_step(step, running):
                total, count = running
                found = dot(one_hots(rank_block, step, unit), right)
                for item in range(RANKS):
                    preact = found[item * size : (item + 1) * size, :]
                    total = total + jnp.maximum(preact, 0.0)
                    count = count + jnp.where(preact > 0.0, 1.0, 0.0)
                return (total, count)

            zero = jnp.zeros((size, right.shape[1]), F32)
            steps, (total, count) = run_steps(one_step, row_most[tile], (zero, zero))
            spare = (steps * RANKS).astype(F32) - row_degree[tile].astype(F32)
            recv_float = recv_rows.astype(F32)
            sums[recv_place] += total - spare * jnp.maximum(recv_float, 0.0)
            counts[recv_place] += count - jnp.where(recv_float > 0.0, spare, 0.0)
            return carry

        lax.fori_loop(0, tile_count[0, 0], one_tile, 0)
        for table, outs in ((sums, sums_out), (counts, counts_out)):
            for side, out in enumerate(outs):
                for block in range(blocks):
                    out[block * size : (block + 1) * size, :] = table[side * blocks + block].astype(
                        out.dtype
                    )

    return kernel


def node_kernel(
    latent,
    cotangent,
    sum_own,
    sum_low,
    sum_high,
    count_low,
    count_high,
    w_edge_out,
    w_node_self,
    w_node_msg,
    node_bias,
    w_node_out,
    gain,
    new_latent,
    to_low,
    to_high,
    aggregate_out,
    message_out,
    hidden_out,
    d_update_out,
    d_hidden_out,
    d_message_out,
):
    rows = latent[...]
    aggregate = (sum_own[...] + sum_low[...].astype(F32) + sum_high[...].astype(F32)).astype(BF16)
    message = dot(aggregate, w_edge_out[...]).astype(BF16)
    hidden_pre = dot(rows, w_node_self[...]) + dot(message, w_node_msg[...]) + node_bias[...]
    logistic = 1.0 / (1.0 + jnp.exp(-hidden_pre))
    hidden = (hidden_pre * logistic).astype(BF16)
    update = dot(hidden, w_node_out[...])
    centred = update - jnp.mean(update, axis=-1, keepdims=True)
    variance = jnp.mean(centred * centred, axis=-1, keepdims=True)
    inv_std = lax.rsqrt(variance + 1e-05)
    normed = centred * inv_std
    new_latent[...] = (rows.astype(F32) + normed * gain[...]).astype(BF16)
    d_normed = cotangent[...].astype(F32) * gain[...]
    d_update = (
        inv_std
        * (
            d_normed
            - jnp.mean(d_normed, axis=-1, keepdims=True)
            - normed * jnp.mean(d_normed * normed, axis=-1, keepdims=True)
        )
    ).astype(BF16)
    d_hidden = dot_t(d_update, w_node_out[...])
    d_hidden_pre = (d_hidden * logistic * (1.0 + hidden_pre * (1.0 - logistic))).astype(BF16)
    d_message = dot_t(d_hidden_pre, w_node_msg[...]).astype(BF16)
    d_aggregate = dot_t(d_message, w_edge_out[...]).astype(BF16)
    own_rows = latent.shape[0]
    to_low[0:own_rows, :] = d_aggregate
    to_low[own_rows:, :] = count_low[...]
    to_high[0:own_rows, :] = d_aggregate
    to_high[own_rows:, :] = count_high[...]
    aggregate_out[...] = aggregate
    message_out[...] = message
    hidden_out[...] = hidden
    d_update_out[...] = d_update
    d_hidden_out[...] = d_hidden_pre
    d_message_out[...] = d_message


def early_kernel(
    latent,
    cotangent,
    count_own,
    from_low,
    from_high,
    aggregate,
    message,
    hidden,
    d_update,
    d_hidden_pre,
    d_message,
    w_edge_out,
    w_node_self,
    w_recv,
    direct_out,
    shares_out,
    grads,
):
    own_rows, width = latent.shape
    rows = latent[...]
    count = count_own[...] + from_low[own_rows:, :].astype(F32)
    count = count + from_high[own_rows:, :].astype(F32)
    d_recv = (dot_t(d_message[...], w_edge_out[...]) * count).astype(BF16)
    direct_out[...] = (
        cotangent[...].astype(F32)
        + dot_t(d_hidden_pre[...], w_node_self[...])
        + dot_t(d_recv, w_recv[...])
    )
    grads[0:width, :] = contract_rows(rows, d_recv)
    grads[width : 2 * width, :] = contract_rows(aggregate[...], d_message[...])
    grads[2 * width : 3 * width, :] = contract_rows(rows, d_hidden_pre[...])
    grads[3 * width : 4 * width, :] = contract_rows(message[...], d_hidden_pre[...])
    grads[4 * width : 5 * width, :] = contract_rows(hidden[...], d_update[...])
    share = shares_out.shape[1]
    for place in range(shares_out.shape[0]):
        shares_out[place] = grads[place * share : (place + 1) * share, :].astype(BF16)


def make_backward(members, blocks):
    def kernel(tile_send, tile_recv, tile_count, col_most, col_rank, *refs):
        send_parts, refs = refs[:members], refs[members:]
        recv_parts, refs = refs[:3], refs[3:]
        grad_parts, refs = refs[:3], refs[3:]
        shares, away_out, refs = refs[0], refs[1], refs[2:]
        senders, receivers, d_sums, grads = refs
        size, width = senders.shape[1:]
        member = lax.axis_index("grp")
        lay_blocks(senders, send_parts)
        lay_blocks(receivers, recv_parts)
        lay_blocks(d_sums, [part.at[0 : blocks * size, :] for part in grad_parts])
        grads[...] = jnp.zeros_like(grads)
        unit = eye_of(size)
        nothing = jnp.zeros((size, width), BF16)

        def one_tile(tile, carry):
            recv_place = tile_recv[0, 0, tile]
            send_place = sender_place(tile_send[0, 0, tile], member, members, blocks)
            upper = jnp.concatenate([receivers[recv_place], d_sums[recv_place]], 1)
            lower = jnp.concatenate([senders[send_place], nothing], 1)
            right = jnp.concatenate([upper, lower], 0)
            rank_block = col_rank[tile]

            def one_step(step, total):
                found = dot(one_hots(rank_block, step, unit), right)
                for item in range(RANKS):
                    part = found[item * size : (item + 1) * size, :]
                    total = total + jnp.where(part[:, :width] > 0.0, part[:, width:], 0.0)
                return total

            zero = jnp.zeros((size, width), F32)
            unused, total = run_steps(one_step, col_most[tile], zero)
            grads[send_place] += total
            return carry

        lax.fori_loop(0, tile_count[0, 0], one_tile, 0)
        rows = blocks * size
        for distance in range(members):
            place = lax.rem(member - distance + members, members)
            for block in range(blocks):
                span = slice(block * size, (block + 1) * size)
                away_out[place, span, :] = grads[distance * blocks + block].astype(BF16)
            away_out[place, rows:, :] = shares[place]

    return kernel


def return_kernel(direct, latent, w_send, back, latent_grad, part_out):
    rows = direct.shape[0]
    share = part_out.shape[0] - latent.shape[1]
    total = back[0].astype(F32)
    for place in range(1, back.shape[0]):
        total = total + back[place].astype(F32)
    d_send = total[:rows, :].astype(BF16)
    latent_grad[...] = direct[...] + dot_t(d_send, w_send[...])
    part_out[0:share, :] = total[rows:, :].astype(BF16)
    part_out[share:, :] = contract_rows(latent[...], d_send).astype(BF16)


def sum_kernel(parts, out):
    def add(place, total):
        return total + parts[place].astype(F32)

    total = lax.fori_loop(1, parts.shape[0], add, parts[0].astype(F32))
    out[...] = total.astype(BF16)


def last_kernel(parts, weight_grads, table):
    members = parts.shape[0]
    width = table.shape[1]
    share = parts.shape[1] - width
    late = jnp.zeros((width, width), F32)
    for place in range(members):
        table[place * share : (place + 1) * share, :] = parts[place, 0:share, :].astype(F32)
        late = late + parts[place, share:, :].astype(F32)
    weight_grads[0] = late
    for item in range(weight_grads.shape[0] - 1):
        weight_grads[item + 1] = table[item * width : (item + 1) * width, :]


def body(
    latent,
    positions,
    tile_send,
    tile_recv,
    tile_mask,
    tile_count,
    w_send,
    w_recv,
    pos_weight,
    edge_bias,
    w_edge_out,
    w_node_self,
    w_node_msg,
    node_bias,
    w_node_out,
    gain,
    cotangent,
):
    own_rows, width = latent.shape
    tiles, size = tile_mask.shape[2], tile_mask.shape[3]
    blocks = own_rows // size
    members = lax.axis_size("grp")
    share = 5 * width // members
    node_like = like((own_rows, width), BF16)
    node_float = like((own_rows, width), F32)
    pair_like = like((2 * own_rows, width), BF16)
    tile_like = like((tiles, size, size), BF16)
    most_like = like((tiles,), jnp.int32)
    send_rows, recv_rows = call(
        rows_kernel,
        [node_like] * 2,
        [latent, positions, w_send, w_recv, pos_weight, edge_bias.reshape(1, width)],
        flops=4 * own_rows * width * width,
        grant=60,
    )
    send_parts = [send_rows] + [
        shifted(send_rows, "grp", distance) for distance in range(1, members)
    ]
    recv_parts = [shifted(recv_rows, "blk", 1), recv_rows, shifted(recv_rows, "blk", -1)]
    row_rank, row_degree, col_rank, row_most, col_most = call(
        ranks_kernel,
        [tile_like] * 3,
        [tile_mask.reshape(tiles, size, size)],
        scalars=[tile_count],
        smem_outs=[most_like] * 2,
        flops=8 * tiles * size * size * size,
        grant=56,
    )
    window = pltpu.VMEM((3 * blocks, size, width), F32)
    sum_low, sum_own, sum_high, count_low, count_own, count_high = call(
        make_forward(members, blocks),
        [node_like, node_float, node_like] * 2,
        [row_rank, row_degree, *send_parts, *recv_parts],
        scalars=[tile_send, tile_recv, tile_count, row_most],
        scratch=[
            pltpu.VMEM((members * blocks, size, width), BF16),
            pltpu.VMEM((3 * blocks, size, width), BF16),
            window,
            window,
        ],
        flops=64 * tiles * size * size * width,
    )
    (
        new_latent,
        to_low,
        to_high,
        aggregate,
        message,
        hidden,
        d_update,
        d_hidden_pre,
        d_message,
    ) = call(
        node_kernel,
        [node_like] + [pair_like] * 2 + [node_like] * 6,
        [
            latent,
            cotangent,
            sum_own,
            shifted(sum_high, "blk", 1),
            shifted(sum_low, "blk", -1),
            count_low,
            count_high,
            w_edge_out,
            w_node_self,
            w_node_msg,
            node_bias.reshape(1, width),
            w_node_out,
            gain.reshape(1, width),
        ],
        flops=14 * own_rows * width * width,
    )
    from_low = shifted(to_high, "blk", 1)
    from_high = shifted(to_low, "blk", -1)
    direct, shares = call(
        early_kernel,
        [node_float, like((members, share, width), BF16)],
        [
            latent,
            cotangent,
            count_own,
            from_low,
            from_high,
            aggregate,
            message,
            hidden,
            d_update,
            d_hidden_pre,
            d_message,
            w_edge_out,
            w_node_self,
            w_recv,
        ],
        scratch=[pltpu.VMEM((5 * width, width), F32)],
        flops=16 * own_rows * width * width,
    )
    (away,) = call(
        make_backward(members, blocks),
        [like((members, own_rows + share, width), BF16)],
        [col_rank, *send_parts, *recv_parts, from_low, to_low, from_high, shares],
        scalars=[tile_send, tile_recv, tile_count, col_most],
        scratch=[
            pltpu.VMEM((members * blocks, size, width), BF16),
            pltpu.VMEM((3 * blocks, size, width), BF16),
            pltpu.VMEM((3 * blocks, size, width), BF16),
            pltpu.VMEM((members * blocks, size, width), F32),
        ],
        flops=64 * tiles * size * size * width,
    )
    back = lax.all_to_all(away, "grp", split_axis=0, concat_axis=0, tiled=True)
    latent_grad, part = call(
        return_kernel,
        [node_float, like((share + width, width), BF16)],
        [direct, latent, w_send, back],
        flops=4 * own_rows * width * width,
    )
    parts = lax.all_gather(part, "blk")
    (part,) = call(sum_kernel, [like(part.shape, BF16)], [parts], flops=parts.size)
    (weight_grads,) = call(
        last_kernel,
        [like((6, width, width), F32)],
        [lax.all_gather(part, "grp")],
        scratch=[pltpu.VMEM((5 * width, width), F32)],
        flops=6 * width * width,
    )
    return (new_latent, latent_grad, weight_grads)


def solution(mesh):
    in_specs = (
        P(("blk", "grp"), None),
        P(None, ("blk", "grp")),
        P("blk", "grp", None),
        P("blk", "grp", None),
        P("blk", "grp", None, None, None),
        P("blk", "grp"),
        P(),
        P(),
        P(),
        P(),
        P(),
        P(),
        P(),
        P(),
        P(),
        P(),
        P(("blk", "grp"), None),
    )
    out_specs = (P(("blk", "grp"), None), P(("blk", "grp"), None), P())
    return jax.shard_map(body, mesh=mesh, in_specs=in_specs, out_specs=out_specs, check_vma=False)
```

time: 128 us -> 110 us (0.86); the launches traced: 127 us -> 110 us
  blocking collectives: 0 us -> 42.6 us
  starting transfers between devices: 46.1 us -> 13.4 us
  waiting for transfers between devices: 27.7 us -> 14.5 us
  Pallas kernels: 44.7 us -> 34.4 us
  local copies, waits for them, and re-layouts: 6.97 us -> 4.05 us
    ppermute x40 -> x9, starting transfers between devices: 46.1 us -> 13.4 us  [shifted(): return lax.ppermute(value, axis, pairs)]
    all_gather x0 -> x2, blocking collectives: none -> 25.2 us  [the longest x1 14.1 us: body(): lax.all_gather(part, 'grp')]
    all_to_all x0 -> x1, blocking collectives: none -> 17.3 us  [body(): back = lax.all_to_all(away, 'grp', split_axis=0, concat_axis=0, tiled=True)]
    ppermute x40 -> x9, waiting for transfers between devices: 27.7 us -> 14.5 us  [shifted(): return lax.ppermute(value, axis, pairs)]
    pallas_call x9, Pallas kernels: 44.7 us -> 34.4 us  [call(): pl.pallas_call(kernel, out_shape=[jax.ShapeDtypeStruct(o.shape, o.dtype)...]
    unnamed x38, local copies, waits for them, and re-layouts: 6.97 us -> 4.05 us
  transfers between devices with their start and end apart: 40 -> 9, of which waited for: 12 -> 4; matrix products, arithmetic and copies ran while one was open for 0% -> 0% of each run, Pallas kernels for 20% -> 4%
where the time goes in v2:
time: 110 us
  blocking collectives  42.6 us (39%)
  Pallas kernels  34.4 us (31%)
  waiting for transfers between devices  14.5 us (13%)
  starting transfers between devices  13.4 us (12%)
  local copies, waits for them, and re-layouts  4.05 us (4%)
  between operations  1.48 us (1%)
    pallas_call x9, Pallas kernels, call(): pl.pallas_call(kernel, out_shape=[jax.ShapeDtypeStruct(o.shape, o.dtype)...  34.4 us
    all_to_all x1, blocking collectives, body(): back = lax.all_to_all(away, 'grp', split_axis=0, concat_axis=0, tiled=True)  17.3 us
    ppermute x9, waiting for transfers between devices, shifted(): return lax.ppermute(value, axis, pairs)  14.5 us
    all_gather x1, blocking collectives, body(): lax.all_gather(part, 'grp')  14.1 us
    ppermute x9, starting transfers between devices, shifted(): return lax.ppermute(value, axis, pairs)  13.4 us
    all_gather x1, blocking collectives, body(): parts = lax.all_gather(part, 'blk')  11.1 us
    unnamed x38, local copies, waits for them, and re-layouts  4.05 us
  transfers between devices with their start and end apart: 9, of which 4 were waited for; matrix products, arithmetic and copies ran while one was open for 0% of the time, Pallas kernels for 4%

profile of v2, /device:TPU:0, one launch (start us, length us, event | category | flops | bytes accessed | tf_op | source)
XLA Modules:
  0.0 110.4 jit_solution(4097395673540746318)
XLA Ops:
  0.6 2.1 %shard_map.185 = (bf16[512,128]{1,0:T(8,128)(2,1)}, bf16[512,128]{1,0:T(8,128)(2,1)}) custom-call(bf16[512,128]{1,0:T(8,128)(2,1)} %latent.7, f32[3,512]{1,0:T(4,128)} %positions.1, bf16[128,128]{1,0:T(8,128)(2,1)} %w_send.3, bf16[128,128]{1,0:T(8,128)(2,1)} %w_recv.3, f32[3,128]{1,0:T(4,128)} %pos_weight.1, f32[1,128]{1,0:T(1,128)} %bitcast.11), custom_call_target="tpu_custom_call" | custom-call | flops 33554432 | bytes 466944 | tf_op jit(solution)/shard_map/pallas_call | solution.py:39
  2.7 3.3 %collective-permute-start.4 = (bf16[512,128]{1,0:T(8,128)(2,1)}, bf16[512,128]{1,0:T(8,128)(2,1)S(1)}, u32[]{:S(2)}, u32[]{:S(2)}) collective-permute-start(bf16[512,128]{1,0:T(8,128)(2,1)} %get-tuple-element.33.refs_5_), channel_id=1, source_target_pairs={{0,28},{4,0},{8,4},{12,8},{16,12},{20,16},{24,20},{28,24},{1,29},{... | collective-permute-start | bytes 393224 | tf_op jit(solution)/shard_map/ppermute | solution.py:18
  6.0 0.0 collective-permute-start.3
  6.0 3.6 %collective-permute-start.2 = (bf16[512,128]{1,0:T(8,128)(2,1)}, bf16[512,128]{1,0:T(8,128)(2,1)S(1)}, u32[]{:S(2)}, u32[]{:S(2)}) collective-permute-start(bf16[512,128]{1,0:T(8,128)(2,1)} %get-tuple-element.32.refs_0_), channel_id=1, source_target_pairs={{0,3},{1,0},{2,1},{3,2},{4,7},{5,4},{6,5},{7,6},{8,11},{9,8},{10,9... | collective-permute-start | bytes 393224 | tf_op jit(solution)/shard_map/ppermute | solution.py:18
  9.6 0.0 collective-permute-start.1
  9.6 1.0 collective-permute-start
  11.3 0.0 copy-start.13
  11.3 0.0 copy-start.14
  11.3 4.3 %shard_map.184 = (bf16[16,128,128]{2,1,0:T(8,128)(2,1)}, bf16[16,128,128]{2,1,0:T(8,128)(2,1)}, bf16[16,128,128]{2,1,0:T(8,128)(2,1)}, s32[16]{0:T(128)}, s32[16]{0:T(128)}) custom-call(s32[1,1]{1,0:T(1,128)S(6)} %copy.20.tile_count, s32[16,128,128]{2,1,0:T(8,128)} %bitcast.10), custom_call_target="tpu_custom_call" | custom-call | flops 268435456 | bytes 2621440 | tf_op jit(solution)/shard_map/pallas_call | solution.py:39
  15.6 0.0 collective-permute-done.4.refs_6_
  15.6 0.0 collective-permute-done.3.refs_4_
  15.6 0.0 collective-permute-done.2.refs_3_
  15.6 5.2 %collective-permute-done.1.refs_2_ = bf16[512,128]{1,0:T(8,128)(2,1)S(1)} collective-permute-done((bf16[512,128]{1,0:T(8,128)(2,1)}, bf16[512,128]{1,0:T(8,128)(2,1)S(1)}, u32[]{:S(2)}, u32[]{:S(2)}) %collective-permute-start.1) | collective-permute-done | bytes 131104 | tf_op jit(solution)/shard_map/ppermute | solution.py:18
  20.9 0.0 collective-permute-done.refs_1_
  20.9 0.0 copy-done.13
  20.9 0.0 copy-done.14
  20.9 0.6 copy-done.15
  21.5 0.0 copy-done.16
  21.6 0.0 copy-done.18
  21.6 1.0 copy-done.11
  22.6 1.0 copy-done.12
  23.7 0.0 copy-start.6
  23.7 0.0 copy-start.7
  23.7 12.2 %shard_map.186 = (bf16[512,128]{1,0:T(8,128)(2,1)S(1)}, f32[512,128]{1,0:T(8,128)S(1)}, bf16[512,128]{1,0:T(8,128)(2,1)S(1)}, bf16[512,128]{1,0:T(8,128)(2,1)S(1...) custom-call(s32[1,1,16]{2,1,0:T(1,128)S(1)} %copy-done.15, s32[1,1,16]{2,1,0:T(1,128)S(1)} %copy-done.16, ...), custom_call_target="tpu_custom_call" | custom-call | flops 2147483648 | bytes 3014656 | tf_op jit(solution)/shard_map/pallas_call | solution.py:39
  35.9 0.1 collective-permute-start.5
  36.0 2.6 %collective-permute-start.6 = (bf16[512,128]{1,0:T(8,128)(2,1)S(1)}, bf16[512,128]{1,0:T(8,128)(2,1)S(1)}, u32[]{:S(2)}, u32[]{:S(2)}) collective-permute-start(bf16[512,128]{1,0:T(8,128)(2,1)S(1)} %get-tuple-element.36), channel_id=1, source_target_pairs={{0,28},{4,0},{8,4},{12,8},{16,12},{20,16},{24,20},{28,24},{1,29},{... | collective-permute-start | bytes 393224 | tf_op jit(solution)/shard_map/ppermute | solution.py:18
  38.6 2.6 %collective-permute-done.5.sum_low = bf16[512,128]{1,0:T(8,128)(2,1)S(1)} collective-permute-done((bf16[512,128]{1,0:T(8,128)(2,1)S(1)}, bf16[512,128]{1,0:T(8,128)(2,1)S(1)}, u32[]{:S(2)}, u32[]{:S(2)}) %collective-permute-start.5) | collective-permute-done | bytes 131104 | tf_op jit(solution)/shard_map/ppermute | solution.py:18
  41.2 0.4 collective-permute-done.6.sum_high
  41.6 0.0 copy-done
  41.6 0.0 copy-done.1
  41.7 0.6 copy-done.8
  42.3 0.0 copy-done.9
  42.3 1.6 %shard_map.187 = (bf16[512,128]{1,0:T(8,128)(2,1)}, bf16[1024,128]{1,0:T(8,128)(2,1)S(1)}, bf16[1024,128]{1,0:T(8,128)(2,1)S(1)}, bf16[512,128]{1,0:T(8,128)(2,1...) custom-call(bf16[512,128]{1,0:T(8,128)(2,1)S(1)} %copy-done, ...), custom_call_target="tpu_custom_call" | custom-call | flops 117440512 | bytes 2622464 | tf_op jit(solution)/shard_map/pallas_call | solution.py:39
  43.9 0.0 collective-permute-start.7
  43.9 2.8 %collective-permute-start.8 = (bf16[1024,128]{1,0:T(8,128)(2,1)S(1)}, bf16[1024,128]{1,0:T(8,128)(2,1)S(1)}, u32[]{:S(2)}, u32[]{:S(2)}) collective-permute-start(bf16[1024,128]{1,0:T(8,128)(2,1)S(1)} %get-tuple-element.42.refs_8_), channel_id=1, source_target_pairs={{0,28},{4,0},{8,4},{12,8},{16,12},{20,16},{24,20},{28,24},{1,29},{... | collective-permute-start | bytes 786440 | tf_op jit(solution)/shard_map/ppermute | solution.py:18
  46.7 6.2 %collective-permute-done.7.from_low.refs_7_ = bf16[1024,128]{1,0:T(8,128)(2,1)S(1)} collective-permute-done((bf16[1024,128]{1,0:T(8,128)(2,1)S(1)}, bf16[1024,128]{1,0:T(8,128)(2,1)S(1)}, u32[]{:S(2)}, u32[]{:S(2)}) %collective-permute-start.7) | collective-permute-done | bytes 262176 | tf_op jit(solution)/shard_map/ppermute | solution.py:18
  52.9 0.0 collective-permute-done.8.from_high.refs_9_
  52.9 0.5 shard_map.188
  53.4 0.5 copy-done.10
  53.9 0.1 copy-done.17
  54.1 11.9 %shard_map.189 = bf16[4,672,128]{2,1,0:T(8,128)(2,1)S(1)} custom-call(s32[1,1,16]{2,1,0:T(1,128)S(1)} %copy-done.15, s32[1,1,16]{2,1,0:T(1,128)S(1)} %copy-done.16, s32[1,1]{1,0:T(1,128)S(6)} %copy.20.tile_count, s32[16]{0:T(128)S(1)} %copy-done.17, bf16[16,128,128]{2,1,0:T(8,128)(2,1)S(1)} %copy-done.10, bf16[512,128]{1,0:T(8,128)(2,1)S(1)} %copy-done.13, ...), custom_call_target="tpu_custom_call" | custom-call | flops 2147483648 | bytes 3080192 | tf_op jit(solution)/shard_map/pallas_call | solution.py:39
  65.9 0.0 copy-start.5
  65.9 17.3 %all_to_all.5.back = bf16[4,672,128]{2,1,0:T(8,128)(2,1)S(1)} all-to-all(bf16[4,672,128]{2,1,0:T(8,128)(2,1)S(1)} %shard_map.189), channel_id=1, replica_groups=mesh['blk'=8,'grp'=4] {'grp'}, dimensions={0} | all-to-all | bytes 1376256 | tf_op jit(solution)/shard_map/all_to_all | solution.py:496
  83.3 0.9 shard_map.190
  84.2 11.1 %all-gather = bf16[2304,128]{1,0:T(8,128)(2,1)S(1)} all-gather(bf16[288,128]{1,0:T(8,128)(2,1)S(1)} %get-tuple-element.54), channel_id=2, replica_groups=mesh['blk'=8,'grp'=4] {'blk'}, dimensions={0}, use_global_device_ids=true | all-gather | bytes 663552 | tf_op jit(solution)/shard_map/all_gather | solution.py:503
  95.3 0.2 shard_map.191
  95.5 14.1 %all-gather.1 = bf16[1152,128]{1,0:T(8,128)(2,1)S(1)} all-gather(bf16[288,128]{1,0:T(8,128)(2,1)S(1)} %shard_map.191), channel_id=3, replica_groups=mesh['blk'=8,'grp'=4] {'grp'}, dimensions={0}, use_global_device_ids=true | all-gather | bytes 368640 | tf_op jit(solution)/shard_map/all_gather | solution.py:508
  109.6 0.8 shard_map.192
  (20 shorter events, 0.0 us)
Async XLA Ops:
  2.7 12.9 %collective-permute-start.4 = (bf16[512,128]{1,0:T(8,128)(2,1)}, bf16[512,128]{1,0:T(8,128)(2,1)S(1)}, u32[]{:S(2)}, u32[]{:S(2)}) collective-permute-start(bf16[512,128]{1,0:T(8,128)(2,1)} %get-tuple-element.33.refs_5_), channel_id=1, source_target_pairs={{0,28},{4,0},{8,4},{12,8},{16,12},{20,16},{24,20},{28,24},{1,29},{... | collective-permute-start | bytes 393224 | tf_op jit(solution)/shard_map/ppermute | solution.py:18
  6.0 9.6 %collective-permute-start.3 = (bf16[512,128]{1,0:T(8,128)(2,1)}, bf16[512,128]{1,0:T(8,128)(2,1)S(1)}, u32[]{:S(2)}, u32[]{:S(2)}) collective-permute-start(bf16[512,128]{1,0:T(8,128)(2,1)} %get-tuple-element.33.refs_5_), channel_id=1, source_target_pairs={{0,4},{4,8},{8,12},{12,16},{16,20},{20,24},{24,28},{28,0},{1,5},{5... | collective-permute-start | bytes 393224 | tf_op jit(solution)/shard_map/ppermute | solution.py:18
  6.0 9.6 %collective-permute-start.2 = (bf16[512,128]{1,0:T(8,128)(2,1)}, bf16[512,128]{1,0:T(8,128)(2,1)S(1)}, u32[]{:S(2)}, u32[]{:S(2)}) collective-permute-start(bf16[512,128]{1,0:T(8,128)(2,1)} %get-tuple-element.32.refs_0_), channel_id=1, source_target_pairs={{0,3},{1,0},{2,1},{3,2},{4,7},{5,4},{6,5},{7,6},{8,11},{9,8},{10,9... | collective-permute-start | bytes 393224 | tf_op jit(solution)/shard_map/ppermute | solution.py:18
  9.6 11.2 %collective-permute-start.1 = (bf16[512,128]{1,0:T(8,128)(2,1)}, bf16[512,128]{1,0:T(8,128)(2,1)S(1)}, u32[]{:S(2)}, u32[]{:S(2)}) collective-permute-start(bf16[512,128]{1,0:T(8,128)(2,1)} %get-tuple-element.32.refs_0_), channel_id=1, source_target_pairs={{0,2},{1,3},{2,0},{3,1},{4,6},{5,7},{6,4},{7,5},{8,10},{9,11},{10,... | collective-permute-start | bytes 393224 | tf_op jit(solution)/shard_map/ppermute | solution.py:18
  9.6 11.2 %collective-permute-start = (bf16[512,128]{1,0:T(8,128)(2,1)}, bf16[512,128]{1,0:T(8,128)(2,1)S(1)}, u32[]{:S(2)}, u32[]{:S(2)}) collective-permute-start(bf16[512,128]{1,0:T(8,128)(2,1)} %get-tuple-element.32.refs_0_), channel_id=1, source_target_pairs={{0,1},{1,2},{2,3},{3,0},{4,5},{5,6},{6,7},{7,4},{8,9},{9,10},{10,1... | collective-permute-start | bytes 393224 | tf_op jit(solution)/shard_map/ppermute | solution.py:18
  11.3 9.6 %copy-start.13 = (bf16[512,128]{1,0:T(8,128)(2,1)S(1)}, bf16[512,128]{1,0:T(8,128)(2,1)}, u32[]{:S(2)}) copy-start(bf16[512,128]{1,0:T(8,128)(2,1)} %get-tuple-element.32.refs_0_) | copy-start | bytes 393220
  11.3 9.6 %copy-start.14 = (bf16[512,128]{1,0:T(8,128)(2,1)S(1)}, bf16[512,128]{1,0:T(8,128)(2,1)}, u32[]{:S(2)}) copy-start(bf16[512,128]{1,0:T(8,128)(2,1)} %get-tuple-element.33.refs_5_) | copy-start | bytes 393220
  20.9 0.7 copy-start.15
  20.9 0.7 copy-start.16
  20.9 0.7 copy-start.18
  21.6 1.0 copy-start.11
  22.6 1.0 copy-start.12
  23.6 18.0 %copy-start = (bf16[512,128]{1,0:T(8,128)(2,1)S(1)}, bf16[512,128]{1,0:T(8,128)(2,1)}, u32[]{:S(2)}) copy-start(bf16[512,128]{1,0:T(8,128)(2,1)} %latent.7) | copy-start | bytes 393220
  23.7 18.0 %copy-start.1 = (bf16[512,128]{1,0:T(8,128)(2,1)S(1)}, bf16[512,128]{1,0:T(8,128)(2,1)}, u32[]{:S(2)}) copy-start(bf16[512,128]{1,0:T(8,128)(2,1)} %cotangent.3) | copy-start | bytes 393220
  23.7 18.0 %copy-start.3 = (bf16[128,128]{1,0:T(8,128)(2,1)S(1)}, bf16[128,128]{1,0:T(8,128)(2,1)}, u32[]{:S(2)}) copy-start(bf16[128,128]{1,0:T(8,128)(2,1)} %w_edge_out.3) | copy-start | bytes 98308
  23.7 18.0 %copy-start.4 = (bf16[128,128]{1,0:T(8,128)(2,1)S(1)}, bf16[128,128]{1,0:T(8,128)(2,1)}, u32[]{:S(2)}) copy-start(bf16[128,128]{1,0:T(8,128)(2,1)} %w_node_self.3) | copy-start | bytes 98308
  23.7 18.0 %copy-start.6 = (bf16[128,128]{1,0:T(8,128)(2,1)S(1)}, bf16[128,128]{1,0:T(8,128)(2,1)}, u32[]{:S(2)}) copy-start(bf16[128,128]{1,0:T(8,128)(2,1)} %w_node_msg.1) | copy-start | bytes 98308
  23.7 18.0 %copy-start.7 = (bf16[128,128]{1,0:T(8,128)(2,1)S(1)}, bf16[128,128]{1,0:T(8,128)(2,1)}, u32[]{:S(2)}) copy-start(bf16[128,128]{1,0:T(8,128)(2,1)} %w_node_out.1) | copy-start | bytes 98308
  35.9 5.3 %collective-permute-start.5 = (bf16[512,128]{1,0:T(8,128)(2,1)S(1)}, bf16[512,128]{1,0:T(8,128)(2,1)S(1)}, u32[]{:S(2)}, u32[]{:S(2)}) collective-permute-start(bf16[512,128]{1,0:T(8,128)(2,1)S(1)} %get-tuple-element.35), channel_id=1, source_target_pairs={{0,4},{4,8},{8,12},{12,16},{16,20},{20,24},{24,28},{28,0},{1,5},{5... | collective-permute-start | bytes 393224 | tf_op jit(solution)/shard_map/ppermute | solution.py:18
  36.0 5.7 %collective-permute-start.6 = (bf16[512,128]{1,0:T(8,128)(2,1)S(1)}, bf16[512,128]{1,0:T(8,128)(2,1)S(1)}, u32[]{:S(2)}, u32[]{:S(2)}) collective-permute-start(bf16[512,128]{1,0:T(8,128)(2,1)S(1)} %get-tuple-element.36), channel_id=1, source_target_pairs={{0,28},{4,0},{8,4},{12,8},{16,12},{20,16},{24,20},{28,24},{1,29},{... | collective-permute-start | bytes 393224 | tf_op jit(solution)/shard_map/ppermute | solution.py:18
  41.6 0.7 copy-start.8
  41.6 0.7 copy-start.9
  42.3 10.6 %copy-start.2 = (bf16[128,128]{1,0:T(8,128)(2,1)S(1)}, bf16[128,128]{1,0:T(8,128)(2,1)}, u32[]{:S(2)}) copy-start(bf16[128,128]{1,0:T(8,128)(2,1)} %w_recv.3) | copy-start | bytes 98308
  43.9 9.0 %collective-permute-start.7 = (bf16[1024,128]{1,0:T(8,128)(2,1)S(1)}, bf16[1024,128]{1,0:T(8,128)(2,1)S(1)}, u32[]{:S(2)}, u32[]{:S(2)}) collective-permute-start(bf16[1024,128]{1,0:T(8,128)(2,1)S(1)} %get-tuple-element.41), channel_id=1, source_target_pairs={{0,4},{4,8},{8,12},{12,16},{16,20},{20,24},{24,28},{28,0},{1,5},{5... | collective-permute-start | bytes 786440 | tf_op jit(solution)/shard_map/ppermute | solution.py:18
  43.9 9.0 %collective-permute-start.8 = (bf16[1024,128]{1,0:T(8,128)(2,1)S(1)}, bf16[1024,128]{1,0:T(8,128)(2,1)S(1)}, u32[]{:S(2)}, u32[]{:S(2)}) collective-permute-start(bf16[1024,128]{1,0:T(8,128)(2,1)S(1)} %get-tuple-element.42.refs_8_), channel_id=1, source_target_pairs={{0,28},{4,0},{8,4},{12,8},{16,12},{20,16},{24,20},{28,24},{1,29},{... | collective-permute-start | bytes 786440 | tf_op jit(solution)/shard_map/ppermute | solution.py:18
  52.9 1.0 copy-start.10
  53.4 0.6 copy-start.17
  65.9 17.4 %copy-start.5 = (bf16[128,128]{1,0:T(8,128)(2,1)S(1)}, bf16[128,128]{1,0:T(8,128)(2,1)}, u32[]{:S(2)}) copy-start(bf16[128,128]{1,0:T(8,128)(2,1)} %w_send.3) | copy-start | bytes 98308

commit v3 on v2

v3 whole, which is shorter than its diff:
```python
import jax
import jax.numpy as jnp
from jax import lax
from jax.experimental import pallas as pl
from jax.experimental.pallas import tpu as pltpu
from jax.sharding import PartitionSpec as P

F32 = jnp.float32
BF16 = jnp.bfloat16
GROUPS = (6, 6)
LOOPED = 4
CHUNK = 32
PARTS = 16


def shifted(value, axis, steps):
    count = lax.axis_size(axis)
    pairs = [(source, (source + steps) % count) for source in range(count)]
    return lax.ppermute(value, axis, pairs)


def dot(left, right):
    return jnp.dot(left, right, preferred_element_type=F32)


def dot_t(left, right):
    return lax.dot_general(left, right, (((1,), (1,)), ((), ())), preferred_element_type=F32)


def contract_rows(left_rows, right_rows):
    return lax.dot_general(
        left_rows, right_rows, (((0,), (0,)), ((), ())), preferred_element_type=F32
    )


def call(kernel, outs, args, scalars=(), far=(), scratch=(), flops=0, smem_outs=(), grant=20):
    vmem = pl.BlockSpec(memory_space=pltpu.VMEM)
    smem = pl.BlockSpec(memory_space=pltpu.SMEM)
    hbm = pl.BlockSpec(memory_space=pltpu.HBM)
    moved = sum(a.size * a.dtype.itemsize for a in list(far) + list(args) + list(outs))
    return pl.pallas_call(
        kernel,
        out_shape=[jax.ShapeDtypeStruct(o.shape, o.dtype) for o in list(outs) + list(smem_outs)],
        in_specs=[smem] * len(scalars) + [hbm] * len(far) + [vmem] * len(args),
        out_specs=[vmem] * len(outs) + [smem] * len(smem_outs),
        scratch_shapes=list(scratch),
        compiler_params=pltpu.CompilerParams(vmem_limit_bytes=grant * 2**20),
        cost_estimate=pl.CostEstimate(flops=flops, bytes_accessed=moved, transcendentals=0),
    )(*scalars, *far, *args)


def like(shape, dtype):
    return jax.ShapeDtypeStruct(tuple(shape), dtype)


def bf16_parts(value):
    parts, rest = [], value
    for unused in range(3):
        part = rest.astype(BF16)
        parts.append(part)
        rest = rest - part.astype(F32)
    return parts


def pack_kernel(latent, positions, pos_weight, message, weight_parts):
    rows, width = latent.shape
    blocks = (message.shape[0] - rows) // PARTS
    message[0:rows, :] = latent[...]
    parts = [part.astype(F32) for part in bf16_parts(positions[...])]
    filler = jnp.zeros((PARTS - 9, rows), F32)
    table = jnp.concatenate([*parts, filler], 0).astype(BF16)
    size = rows // blocks
    for block in range(blocks):
        start = rows + block * PARTS
        message[start : start + PARTS, :] = table[:, block * size : (block + 1) * size]
    filler = jnp.zeros((PARTS - 9, width), F32)
    for item, part in enumerate(bf16_parts(pos_weight[...])):
        part = part.astype(F32)
        stacked = jnp.concatenate([part, part, part, filler], 0)
        weight_parts[:, item * width : (item + 1) * width] = stacked.astype(BF16)


def ranks_kernel(tile_count, mask_far, row_rank, row_degree, col_rank, row_most, col_most, mask, sem):
    tiles, size = mask.shape[0], mask.shape[-1]
    copies = [
        pltpu.make_async_copy(mask_far.at[tile], mask.at[tile], sem.at[tile])
        for tile in range(tiles)
    ]
    for copy in copies:
        copy.start()
    row_index = lax.broadcasted_iota(jnp.int32, (size, size), 0)
    col_index = lax.broadcasted_iota(jnp.int32, (size, size), 1)
    upper = (row_index <= col_index).astype(F32).astype(BF16)
    eye = (row_index == col_index).astype(F32).astype(BF16)
    ones = jnp.ones((size, size), BF16)
    for_rows = jnp.concatenate([upper, ones], 1)
    for_cols = jnp.concatenate([upper, eye], 1)
    for tile in range(tiles):
        copies[tile].wait()
        live = (tile < tile_count[0, 0]).astype(F32)
        values = mask[tile].astype(F32) * live
        values_b = values.astype(BF16)
        found = dot(values_b, for_rows)
        row_rank[tile] = (found[:, :size] * values).astype(BF16)
        row_degree[tile] = found[:, size:].astype(BF16)
        row_most[tile] = jnp.max(found[:, size:]).astype(jnp.int32)
        found = contract_rows(values_b, for_cols)
        col_rank[tile] = (found[:, :size] * found[:, size:]).astype(BF16)
        col_most[tile] = jnp.max(found[:, :size]).astype(jnp.int32)


def one_hots(rank_block, first, ranks):
    one, nothing = jnp.ones_like(rank_block), jnp.zeros_like(rank_block)
    found = []
    for item in range(ranks):
        rank = jnp.asarray(first + item + 1, jnp.int32).astype(F32).astype(BF16)
        found.append(jnp.where(rank_block == rank, one, nothing))
    return found


def run_groups(one_group, most):
    first = 0
    for place, ranks in enumerate(GROUPS):
        one_group(first, ranks, place == 0)
        first += ranks
    steps = jnp.maximum((most - first + LOOPED - 1) // LOOPED, 0)

    def one_step(step, carry):
        one_group(first + step * LOOPED, LOOPED, False)
        return carry

    lax.fori_loop(0, steps, one_step, 0)
    return first + steps * LOOPED


def eye_of(size):
    row_index = lax.broadcasted_iota(jnp.int32, (size, size), 0)
    col_index = lax.broadcasted_iota(jnp.int32, (size, size), 1)
    return (row_index == col_index).astype(F32).astype(BF16)


def lay_blocks(table, parts):
    size = table.shape[1]
    place = 0
    for part in parts:
        for block in range(part.shape[0] // size):
            table[place] = part[block * size : (block + 1) * size, :]
            place += 1


def sender_place(block, member, members, blocks):
    distance = lax.rem(member - block // blocks + members, members)
    return distance * blocks + lax.rem(block, blocks)


def start_copies(sources, targets, sem):
    copies = [
        pltpu.make_async_copy(source, target, sem.at[item])
        for item, (source, target) in enumerate(zip(sources, targets))
    ]
    for copy in copies:
        copy.start()
    return copies


def make_forward(members, blocks):
    def kernel(tile_count, send_far, recv_far, most_far, *refs):
        row_rank, row_degree, w_send, w_recv, weight_parts, edge_bias, refs = *refs[:6], refs[6:]
        messages, sides, refs = refs[:members], refs[members : members + 2], refs[members + 2 :]
        sums_out, counts_out, refs = refs[:3], refs[3:6], refs[6:]
        senders, receivers, refs = refs[0], refs[1], refs[2:]
        sums, counts, total, count, tile_send, tile_recv, row_most, sem = refs
        size, width = senders.shape[1:]
        rows = blocks * size
        copies = start_copies(
            (send_far, recv_far, most_far), (tile_send, tile_recv, row_most), sem
        )
        member = lax.axis_index("grp")
        sums[...] = jnp.zeros_like(sums)
        counts[...] = jnp.zeros_like(counts)

        def placed_of(message):
            found = []
            for block in range(blocks):
                start = rows + block * PARTS
                parts = contract_rows(message[start : start + PARTS, :], weight_parts[...])
                found.append(parts[:, :width] + parts[:, width : 2 * width] + parts[:, 2 * width :])
            return jnp.concatenate(found, 0)

        def lay(table, place, found):
            for block in range(blocks):
                span = slice(block * size, (block + 1) * size)
                table[place * blocks + block] = found[span, :].astype(BF16)

        for distance, message in enumerate(messages):
            placed = placed_of(message)
            lay(senders, distance, dot(message[0:rows, :], w_send[...]) + placed)
            if distance == 0:
                lay(receivers, 1, dot(message[0:rows, :], w_recv[...]) - placed + edge_bias[...])
        for place, message in ((0, sides[0]), (2, sides[1])):
            placed = placed_of(message)
            lay(receivers, place, dot(message[0:rows, :], w_recv[...]) - placed + edge_bias[...])
        for copy in copies:
            copy.wait()

        def one_pair(pair, carry):
            tiles = (2 * pair, 2 * pair + 1)
            recv_places = [tile_recv[0, 0, tile] for tile in tiles]
            send_rows = [
                senders[sender_place(tile_send[0, 0, tile], member, members, blocks)]
                for tile in tiles
            ]
            nothing = jnp.zeros((size, width), BF16)
            upper = jnp.concatenate([send_rows[0], nothing], 1)
            lower = jnp.concatenate([nothing, send_rows[1]], 1)
            right = jnp.concatenate([upper, lower], 0)
            recv_rows = jnp.concatenate([receivers[place] for place in recv_places], 1).astype(F32)
            ranks_of = [row_rank[tile] for tile in tiles]

            def one_group(first, ranks, fresh):
                hots = [one_hots(rank_block, first, ranks) for rank_block in ranks_of]
                left = jnp.concatenate([jnp.concatenate(two, 1) for two in zip(*hots)], 0)
                found = dot(left, right)
                for chunk in range(0, size, CHUNK):
                    span = slice(chunk, chunk + CHUNK)
                    added = jnp.zeros((CHUNK, 2 * width), F32)
                    seen = jnp.zeros((CHUNK, 2 * width), F32)
                    for item in range(ranks):
                        start = item * size + chunk
                        preact = found[start : start + CHUNK, :] + recv_rows[span, :]
                        added = added + jnp.maximum(preact, 0.0)
                        seen = seen + jnp.where(preact > 0.0, 1.0, 0.0)
                    total[span, :] = added if fresh else total[span, :] + added
                    count[span, :] = seen if fresh else count[span, :] + seen

            most = jnp.maximum(row_most[tiles[0]], row_most[tiles[1]])
            done = jnp.asarray(run_groups(one_group, most), jnp.int32).astype(F32)
            for item, tile in enumerate(tiles):
                half = slice(item * width, (item + 1) * width)
                spare = done - row_degree[tile].astype(F32)
                rows_here = recv_rows[:, half]
                place = recv_places[item]
                sums[place] += total[:, half] - spare * jnp.maximum(rows_here, 0.0)
                counts[place] += count[:, half] - jnp.where(rows_here > 0.0, spare, 0.0)
            return carry

        lax.fori_loop(0, (tile_count[0, 0] + 1) // 2, one_pair, 0)
        for table, outs in ((sums, sums_out), (counts, counts_out)):
            for side, out in enumerate(outs):
                for block in range(blocks):
                    out[block * size : (block + 1) * size, :] = table[side * blocks + block].astype(
                        out.dtype
                    )

    return kernel


def node_kernel(
    bias_far,
    gain_far,
    latent,
    cotangent,
    sum_own,
    sum_low,
    sum_high,
    count_low,
    count_high,
    w_edge_out,
    w_node_self,
    w_node_msg,
    w_node_out,
    new_latent,
    to_low,
    to_high,
    aggregate_out,
    message_out,
    hidden_out,
    d_update_out,
    d_hidden_out,
    d_message_out,
    node_bias,
    gain,
    sem,
):
    copies = start_copies((bias_far, gain_far), (node_bias, gain), sem)
    rows = latent[...]
    aggregate = (sum_own[...] + sum_low[...].astype(F32) + sum_high[...].astype(F32)).astype(BF16)
    message = dot(aggregate, w_edge_out[...]).astype(BF16)
    for copy in copies:
        copy.wait()
    hidden_pre = dot(rows, w_node_self[...]) + dot(message, w_node_msg[...]) + node_bias[...]
    logistic = 1.0 / (1.0 + jnp.exp(-hidden_pre))
    hidden = (hidden_pre * logistic).astype(BF16)
    update = dot(hidden, w_node_out[...])
    centred = update - jnp.mean(update, axis=-1, keepdims=True)
    variance = jnp.mean(centred * centred, axis=-1, keepdims=True)
    inv_std = lax.rsqrt(variance + 1e-05)
    normed = centred * inv_std
    new_latent[...] = (rows.astype(F32) + normed * gain[...]).astype(BF16)
    d_normed = cotangent[...].astype(F32) * gain[...]
    d_update = (
        inv_std
        * (
            d_normed
            - jnp.mean(d_normed, axis=-1, keepdims=True)
            - normed * jnp.mean(d_normed * normed, axis=-1, keepdims=True)
        )
    ).astype(BF16)
    d_hidden = dot_t(d_update, w_node_out[...])
    d_hidden_pre = (d_hidden * logistic * (1.0 + hidden_pre * (1.0 - logistic))).astype(BF16)
    d_message = dot_t(d_hidden_pre, w_node_msg[...]).astype(BF16)
    d_aggregate = dot_t(d_message, w_edge_out[...]).astype(BF16)
    own_rows = latent.shape[0]
    to_low[0:own_rows, :] = d_aggregate
    to_low[own_rows:, :] = count_low[...]
    to_high[0:own_rows, :] = d_aggregate
    to_high[own_rows:, :] = count_high[...]
    aggregate_out[...] = aggregate
    message_out[...] = message
    hidden_out[...] = hidden
    d_update_out[...] = d_update
    d_hidden_out[...] = d_hidden_pre
    d_message_out[...] = d_message


def early_kernel(
    latent,
    cotangent,
    count_own,
    from_low,
    from_high,
    aggregate,
    message,
    hidden,
    d_update,
    d_hidden_pre,
    d_message,
    w_edge_out,
    w_node_self,
    w_recv,
    direct_out,
    grads,
):
    own_rows, width = latent.shape
    rows = latent[...]
    count = count_own[...] + from_low[own_rows:, :].astype(F32)
    count = count + from_high[own_rows:, :].astype(F32)
    d_recv = (dot_t(d_message[...], w_edge_out[...]) * count).astype(BF16)
    direct_out[...] = (
        cotangent[...].astype(F32)
        + dot_t(d_hidden_pre[...], w_node_self[...])
        + dot_t(d_recv, w_recv[...])
    )
    grads[0:width, :] = contract_rows(rows, d_recv)
    grads[width : 2 * width, :] = contract_rows(aggregate[...], d_message[...])
    grads[2 * width : 3 * width, :] = contract_rows(rows, d_hidden_pre[...])
    grads[3 * width : 4 * width, :] = contract_rows(message[...], d_hidden_pre[...])
    grads[4 * width : 5 * width, :] = contract_rows(hidden[...], d_update[...])


def make_backward(members, blocks):
    def kernel(tile_count, send_far, recv_far, most_far, *refs):
        col_rank, senders, receivers, refs = *refs[:3], refs[3:]
        grad_parts, refs = refs[:3], refs[3:]
        messages, refs = refs[:members], refs[members:]
        grads_out, refs = refs[:members], refs[members:]
        late_out, d_sums, grads, totals, tile_send, tile_recv, col_most, sem = refs
        size, width = senders.shape[1:]
        rows = blocks * size
        copies = start_copies(
            (send_far, recv_far, most_far), (tile_send, tile_recv, col_most), sem
        )
        member = lax.axis_index("grp")
        lay_blocks(d_sums, [part.at[0:rows, :] for part in grad_parts])
        grads[...] = jnp.zeros_like(grads)
        unit = eye_of(size)
        nothing = jnp.zeros((size, width), BF16)
        for copy in copies:
            copy.wait()

        def one_pair(pair, carry):
            tiles = (2 * pair, 2 * pair + 1)
            send_places = [
                sender_place(tile_send[0, 0, tile], member, members, blocks) for tile in tiles
            ]
            rights = []
            for tile, send_place in zip(tiles, send_places):
                recv_place = tile_recv[0, 0, tile]
                upper = jnp.concatenate([receivers[recv_place], d_sums[recv_place]], 1)
                lower = jnp.concatenate([senders[send_place], nothing], 1)
                rights.append(jnp.concatenate([upper, lower], 0))
            ranks_of = [col_rank[tile] for tile in tiles]

            def one_group(first, ranks, fresh):
                for place in range(2):
                    hots = one_hots(ranks_of[place], first, ranks)
                    left = jnp.concatenate([jnp.concatenate([hot, unit], 1) for hot in hots], 0)
                    found = dot(left, rights[place])
                    for chunk in range(0, size, CHUNK):
                        span = slice(chunk, chunk + CHUNK)
                        added = jnp.zeros((CHUNK, width), F32)
                        for item in range(ranks):
                            part = found[item * size + chunk : item * size + chunk + CHUNK, :]
                            added = added + jnp.where(part[:, :width] > 0.0, part[:, width:], 0.0)
                        totals[place, span, :] = added if fresh else totals[place, span, :] + added

            run_groups(one_group, jnp.maximum(col_most[tiles[0]], col_most[tiles[1]]))
            for item, send_place in enumerate(send_places):
                grads[send_place] += totals[item]
            return carry

        lax.fori_loop(0, (tile_count[0, 0] + 1) // 2, one_pair, 0)
        late = jnp.zeros((width, width), F32)
        for distance, out in enumerate(grads_out):
            for block in range(blocks):
                span = slice(block * size, (block + 1) * size)
                found = grads[distance * blocks + block]
                out[span, :] = found.astype(out.dtype)
                late = late + contract_rows(messages[distance][span, :], found.astype(BF16))
        late_out[...] = late.astype(BF16)

    return kernel


def pairwise_sum(value, axis):
    count = lax.axis_size(axis)
    if count & (count - 1):
        return lax.psum(value.astype(F32), axis).astype(BF16)
    step = 1
    while step < count:
        pairs = [(source, source ^ step) for source in range(count)]
        other = lax.ppermute(value, axis, pairs)
        value = (value.astype(F32) + other.astype(F32)).astype(BF16)
        step *= 2
    return value


def return_kernel(direct, w_send, own, *refs):
    back, latent_grad = refs[:-1], refs[-1]
    d_send = own[...]
    for part in back:
        d_send = d_send + part[...].astype(F32)
    latent_grad[...] = direct[...] + dot_t(d_send.astype(BF16), w_send[...])


def last_kernel(early, late, weight_grads):
    width = late.shape[1]
    weight_grads[0] = late[...].astype(F32)
    for item in range(weight_grads.shape[0] - 1):
        weight_grads[item + 1] = early[item * width : (item + 1) * width, :]


def body(
    latent,
    positions,
    tile_send,
    tile_recv,
    tile_mask,
    tile_count,
    w_send,
    w_recv,
    pos_weight,
    edge_bias,
    w_edge_out,
    w_node_self,
    w_node_msg,
    node_bias,
    w_node_out,
    gain,
    cotangent,
):
    own_rows, width = latent.shape
    tiles, size = tile_mask.shape[2], tile_mask.shape[3]
    blocks = own_rows // size
    members = lax.axis_size("grp")
    node_like = like((own_rows, width), BF16)
    node_float = like((own_rows, width), F32)
    pair_like = like((2 * own_rows, width), BF16)
    tile_like = like((tiles, size, size), BF16)
    most_like = like((tiles,), jnp.int32)
    slab_like = like((members * blocks, size, width), BF16)
    near_like = like((3 * blocks, size, width), BF16)
    message, weight_parts = call(
        pack_kernel,
        [like((own_rows + blocks * PARTS, width), BF16), like((PARTS, 3 * width), BF16)],
        [latent, positions, pos_weight],
        grant=60,
    )
    messages = [message] + [shifted(message, "grp", distance) for distance in range(1, members)]
    sides = [shifted(message, "blk", 1), shifted(message, "blk", -1)]
    row_rank, row_degree, col_rank, row_most, col_most = call(
        ranks_kernel,
        [tile_like] * 3,
        [],
        scalars=[tile_count],
        far=[tile_mask.reshape(tiles, size, size)],
        smem_outs=[most_like] * 2,
        scratch=[
            pltpu.VMEM((tiles, size, size), jnp.int32),
            pltpu.SemaphoreType.DMA((tiles,)),
        ],
        flops=8 * tiles * size * size * size,
    )
    tables = [
        pltpu.SMEM(tile_send.shape, jnp.int32),
        pltpu.SMEM(tile_recv.shape, jnp.int32),
        pltpu.SMEM((tiles,), jnp.int32),
        pltpu.SemaphoreType.DMA((3,)),
    ]
    window = pltpu.VMEM((3 * blocks, size, width), F32)
    sum_low, sum_own, sum_high, count_low, count_own, count_high, senders, receivers = call(
        make_forward(members, blocks),
        [node_like, node_float, node_like] * 2 + [slab_like, near_like],
        [
            row_rank,
            row_degree,
            w_send,
            w_recv,
            weight_parts,
            edge_bias.reshape(1, width),
            *messages,
            *sides,
        ],
        scalars=[tile_count],
        far=[tile_send, tile_recv, row_most],
        scratch=[
            window,
            window,
            pltpu.VMEM((size, 2 * width), F32),
            pltpu.VMEM((size, 2 * width), F32),
            *tables,
        ],
        flops=64 * tiles * size * size * width,
    )
    (
        new_latent,
        to_low,
        to_high,
        aggregate,
        message_out,
        hidden,
        d_update,
        d_hidden_pre,
        d_message,
    ) = call(
        node_kernel,
        [node_like] + [pair_like] * 2 + [node_like] * 6,
        [
            latent,
            cotangent,
            sum_own,
            shifted(sum_high, "blk", 1),
            shifted(sum_low, "blk", -1),
            count_low,
            count_high,
            w_edge_out,
            w_node_self,
            w_node_msg,
            w_node_out,
        ],
        far=[node_bias.reshape(1, width), gain.reshape(1, width)],
        scratch=[
            pltpu.VMEM((1, width), F32),
            pltpu.VMEM((1, width), F32),
            pltpu.SemaphoreType.DMA((2,)),
        ],
        flops=14 * own_rows * width * width,
    )
    from_low = shifted(to_high, "blk", 1)
    from_high = shifted(to_low, "blk", -1)
    direct, early = call(
        early_kernel,
        [node_float, like((5 * width, width), F32)],
        [
            latent,
            cotangent,
            count_own,
            from_low,
            from_high,
            aggregate,
            message_out,
            hidden,
            d_update,
            d_hidden_pre,
            d_message,
            w_edge_out,
            w_node_self,
            w_recv,
        ],
        flops=16 * own_rows * width * width,
    )
    early = lax.psum(lax.optimization_barrier(lax.psum(early, "blk")), "grp")
    *send_grads, late = call(
        make_backward(members, blocks),
        [node_float] + [node_like] * (members - 1) + [like((width, width), BF16)],
        [col_rank, senders, receivers, from_low, to_low, from_high, *messages],
        scalars=[tile_count],
        far=[tile_send, tile_recv, col_most],
        scratch=[
            pltpu.VMEM((3 * blocks, size, width), BF16),
            pltpu.VMEM((members * blocks, size, width), F32),
            pltpu.VMEM((2, size, width), F32),
            *tables,
        ],
        flops=64 * tiles * size * size * width,
    )
    back = [shifted(send_grads[distance], "grp", -distance) for distance in range(1, members)]
    late = pairwise_sum(pairwise_sum(late, "blk"), "grp")
    (latent_grad,) = call(
        return_kernel,
        [node_float],
        [direct, w_send, send_grads[0], *back],
        flops=2 * own_rows * width * width,
    )
    (weight_grads,) = call(last_kernel, [like((6, width, width), F32)], [early, late])
    return (new_latent, latent_grad, weight_grads)


def solution(mesh):
    in_specs = (
        P(("blk", "grp"), None),
        P(None, ("blk", "grp")),
        P("blk", "grp", None),
        P("blk", "grp", None),
        P("blk", "grp", None, None, None),
        P("blk", "grp"),
        P(),
        P(),
        P(),
        P(),
        P(),
        P(),
        P(),
        P(),
        P(),
        P(),
        P(("blk", "grp"), None),
    )
    out_specs = (P(("blk", "grp"), None), P(("blk", "grp"), None), P())
    return jax.shard_map(body, mesh=mesh, in_specs=in_specs, out_specs=out_specs, check_vma=False)
```

time: 110 us -> 171 us (1.55)
  waiting for transfers between devices: 14.5 us -> 97.6 us
  blocking collectives: 42.6 us -> 0 us
  between operations: 1.48 us -> 15 us
  starting transfers between devices: 13.4 us -> 21.5 us
    psum x0 -> x2, waiting for transfers between devices: none -> 78.7 us  [body(): early = lax.psum(lax.optimization_barrier(lax.psum(early, 'blk')), 'grp')]
    all_gather x2 -> x0, blocking collectives: 25.2 us -> none  [the longest x1 14.1 us: body(): lax.all_gather(part, 'grp')]
    all_to_all x1 -> x0, blocking collectives: 17.3 us -> none  [body(): back = lax.all_to_all(away, 'grp', split_axis=0, concat_axis=0, tiled=True)]
    ppermute x0 -> x5, waiting for transfers between devices: none -> 8.95 us  [pairwise_sum(): other = lax.ppermute(value, axis, pairs)]
    ppermute x9 -> x12, starting transfers between devices: 13.4 us -> 18.5 us  [shifted(): return lax.ppermute(value, axis, pairs)]
    ppermute x9 -> x12, waiting for transfers between devices: 14.5 us -> 9.88 us  [shifted(): return lax.ppermute(value, axis, pairs)]
    ppermute x0 -> x5, starting transfers between devices: none -> 2.98 us  [pairwise_sum(): other = lax.ppermute(value, axis, pairs)]
    pallas_call x9 -> x8, Pallas kernels: 34.4 us -> 32.8 us  [call(): pl.pallas_call(kernel, out_shape=[jax.ShapeDtypeStruct(o.shape, o.dtype)...]
  transfers between devices with their start and end apart: 9 -> 19, of which waited for: 4 -> 8; matrix products, arithmetic and copies ran while one was open for 0% -> 0% of each run, Pallas kernels for 4% -> 6%
where the time goes in v3:
time: 171 us; the launch traced here: 170 us
  waiting for transfers between devices  97.6 us (57%)
  Pallas kernels  32.8 us (19%)
  starting transfers between devices  21.5 us (13%)
  between operations  15 us (9%)
  local copies, waits for them, and re-layouts  3.47 us (2%)
    psum x2, waiting for transfers between devices, body(): early = lax.psum(lax.optimization_barrier(lax.psum(early, 'blk')), 'grp')  78.7 us
    pallas_call x8, Pallas kernels, call(): pl.pallas_call(kernel, out_shape=[jax.ShapeDtypeStruct(o.shape, o.dtype)...  32.8 us
    ppermute x12, starting transfers between devices, shifted(): return lax.ppermute(value, axis, pairs)  18.5 us
    ppermute x12, waiting for transfers between devices, shifted(): return lax.ppermute(value, axis, pairs)  9.88 us
    ppermute x5, waiting for transfers between devices, pairwise_sum(): other = lax.ppermute(value, axis, pairs)  8.95 us
    unnamed x34, local copies, waits for them, and re-layouts  3.47 us
  transfers between devices with their start and end apart: 19, of which 8 were waited for; matrix products, arithmetic and copies ran while one was open for 0% of the time, Pallas kernels for 6%

profile of v3, /device:TPU:0, one launch (start us, length us, event | category | flops | bytes accessed | tf_op | source)
XLA Modules:
  0.0 170.4 jit_solution(2987445323901419506)
XLA Ops:
  7.2 0.0 all-reduce.3.cloned.1.call-start
  7.2 1.6 shard_map.185
  8.8 3.0 %collective-permute-start = (bf16[576,128]{1,0:T(8,128)(2,1)}, bf16[576,128]{1,0:T(8,128)(2,1)S(1)}, u32[]{:S(2)}, u32[]{:S(2)}) collective-permute-start(bf16[576,128]{1,0:T(8,128)(2,1)} %get-tuple-element.38.refs_6_), channel_id=1, source_target_pairs={{0,1},{1,2},{2,3},{3,0},{4,5},{5,6},{6,7},{7,4},{8,9},{9,10},{10,1... | collective-permute-start | bytes 442376 | tf_op jit(solution)/shard_map/ppermute | solution.py:19
  11.8 2.6 %collective-permute-start.1 = (bf16[576,128]{1,0:T(8,128)(2,1)}, bf16[576,128]{1,0:T(8,128)(2,1)S(1)}, u32[]{:S(2)}, u32[]{:S(2)}) collective-permute-start(bf16[576,128]{1,0:T(8,128)(2,1)} %get-tuple-element.38.refs_6_), channel_id=1, source_target_pairs={{0,2},{1,3},{2,0},{3,1},{4,6},{5,7},{6,4},{7,5},{8,10},{9,11},{10,... | collective-permute-start | bytes 442376 | tf_op jit(solution)/shard_map/ppermute | solution.py:19
  14.4 1.3 collective-permute-start.2
  15.8 2.6 %collective-permute-start.4 = (bf16[576,128]{1,0:T(8,128)(2,1)}, bf16[576,128]{1,0:T(8,128)(2,1)S(1)}, u32[]{:S(2)}, u32[]{:S(2)}) collective-permute-start(bf16[576,128]{1,0:T(8,128)(2,1)} %get-tuple-element.38.refs_6_), channel_id=1, source_target_pairs={{0,28},{4,0},{8,4},{12,8},{16,12},{20,16},{24,20},{28,24},{1,29},{... | collective-permute-start | bytes 442376 | tf_op jit(solution)/shard_map/ppermute | solution.py:19
  19.1 0.0 copy-start.1
  19.1 1.2 copy-done.1
  20.3 7.4 %shard_map.184 = (bf16[16,128,128]{2,1,0:T(8,128)(2,1)S(1)}, bf16[16,128,128]{2,1,0:T(8,128)(2,1)S(1)}, bf16[16,128,128]{2,1,0:T(8,128)(2,1)S(1)}, s32[16]{0:T(128)S(1)}, s32[16]{0:T(128)S(1)}) custom-call(s32[1,1]{1,0:T(1,128)S(6)} %copy.22.tile_count, s32[16,128,128]{2,1,0:T(8,128)S(1)} %bitcast.4), custom_call_target="tpu_custom_call" | custom-call | flops 268435456 | bytes 2621440 | tf_op jit(solution)/shard_map/pallas_call | solution.py:41
  27.7 0.0 copy-start.14
  27.8 0.0 copy-start.15
  27.8 0.0 copy-start.16
  27.8 0.6 copy-done.14
  28.4 0.0 copy-done.15
  28.4 0.0 copy-done.16
  28.4 0.0 copy-start.7
  28.5 0.0 copy-start.8
  28.5 9.7 %shard_map.186 = (bf16[512,128]{1,0:T(8,128)(2,1)S(1)}, f32[512,128]{1,0:T(8,128)S(1)}, bf16[512,128]{1,0:T(8,128)(2,1)S(1)}, bf16[512,128]{1,0:T(8,128)(2,1)S(1...) custom-call(s32[1,1]{1,0:T(1,128)S(6)} %copy.22.tile_count, ...), custom_call_target="tpu_custom_call" | custom-call | flops 2147483648 | bytes 3977920 | tf_op jit(solution)/shard_map/pallas_call | solution.py:41
  38.2 0.1 collective-permute-start.5
  38.2 2.6 %collective-permute-start.6 = (bf16[512,128]{1,0:T(8,128)(2,1)S(1)}, bf16[512,128]{1,0:T(8,128)(2,1)S(1)}, u32[]{:S(2)}, u32[]{:S(2)}) collective-permute-start(bf16[512,128]{1,0:T(8,128)(2,1)S(1)} %get-tuple-element.41), channel_id=1, source_target_pairs={{0,28},{4,0},{8,4},{12,8},{16,12},{20,16},{24,20},{28,24},{1,29},{... | collective-permute-start | bytes 393224 | tf_op jit(solution)/shard_map/ppermute | solution.py:19
  40.8 3.2 %collective-permute-done.5.sum_low = bf16[512,128]{1,0:T(8,128)(2,1)S(1)} collective-permute-done((bf16[512,128]{1,0:T(8,128)(2,1)S(1)}, bf16[512,128]{1,0:T(8,128)(2,1)S(1)}, u32[]{:S(2)}, u32[]{:S(2)}) %collective-permute-start.5) | collective-permute-done | bytes 131104 | tf_op jit(solution)/shard_map/ppermute | solution.py:19
  44.1 0.6 copy-done.10
  44.7 0.0 copy-done.11
  44.7 1.8 %shard_map.187 = (bf16[512,128]{1,0:T(8,128)(2,1)}, bf16[1024,128]{1,0:T(8,128)(2,1)S(1)}, bf16[1024,128]{1,0:T(8,128)(2,1)S(1)}, bf16[512,128]{1,0:T(8,128)(2,1...) custom-call(f32[1,128]{1,0:T(1,128)S(1)} %bitcast.5, ...), custom_call_target="tpu_custom_call" | custom-call | flops 117440512 | bytes 2622464 | tf_op jit(solution)/shard_map/pallas_call | solution.py:41
  46.5 0.1 collective-permute-start.7
  46.6 2.6 %collective-permute-start.8 = (bf16[1024,128]{1,0:T(8,128)(2,1)S(1)}, bf16[1024,128]{1,0:T(8,128)(2,1)S(1)}, u32[]{:S(2)}, u32[]{:S(2)}) collective-permute-start(bf16[1024,128]{1,0:T(8,128)(2,1)S(1)} %get-tuple-element.47.refs_4_), channel_id=1, source_target_pairs={{0,28},{4,0},{8,4},{12,8},{16,12},{20,16},{24,20},{28,24},{1,29},{... | collective-permute-start | bytes 786440 | tf_op jit(solution)/shard_map/ppermute | solution.py:19
  49.2 6.7 %collective-permute-done.7.from_low.refs_3_ = bf16[1024,128]{1,0:T(8,128)(2,1)S(1)} collective-permute-done((bf16[1024,128]{1,0:T(8,128)(2,1)S(1)}, bf16[1024,128]{1,0:T(8,128)(2,1)S(1)}, u32[]{:S(2)}, u32[]{:S(2)}) %collective-permute-start.7) | collective-permute-done | bytes 262176 | tf_op jit(solution)/shard_map/ppermute | solution.py:19
  55.9 9.4 %shard_map.189 = (f32[512,128]{1,0:T(8,128)S(1)}, bf16[512,128]{1,0:T(8,128)(2,1)S(1)}, bf16[512,128]{1,0:T(8,128)(2,1)S(1)}, bf16[512,128]{1,0:T(8,128)(2,1)S(1)}, bf16[128,128]{1,0:T(8,128)(2,1)S(1)}) custom-call(s32[1,1]{1,0:T(1,128)S(6)} %copy.22.tile_count, s32[1,1,16]{2,1,0:T(1,128)S(1)} %copy-done.15, s32[1,1,16]{2,1,0:T(1,128)S(1)} %copy-done.16, ...), custom_call_target="tpu_custom_call" | custom-call | flops 2147483648 | bytes 3506368 | tf_op jit(solution)/shard_map/pallas_call | solution.py:41
  65.3 0.1 collective-permute-start.12
  65.4 1.2 collective-permute-done.12
  66.6 0.1 collective-permute-start.13
  66.7 3.9 %collective-permute-done.13 = bf16[128,128]{1,0:T(8,128)(2,1)S(1)} collective-permute-done((bf16[128,128]{1,0:T(8,128)(2,1)S(1)}, bf16[128,128]{1,0:T(8,128)(2,1)S(1)}, u32[]{:S(2)}, u32[]{:S(2)}) %collective-permute-start.13) | collective-permute-done | bytes 32800 | tf_op jit(solution)/shard_map/ppermute | solution.py:432
  70.6 0.3 collective-permute-start.14
  70.9 1.3 shard_map.188
  72.1 0.0 all-reduce.3.cloned.1.call-update
  72.2 0.0 all-reduce.5.cloned.1.call-start
  72.2 2.4 %collective-permute-done.14 = bf16[128,128]{1,0:T(8,128)(2,1)S(1)} collective-permute-done((bf16[128,128]{1,0:T(8,128)(2,1)S(1)}, bf16[128,128]{1,0:T(8,128)(2,1)S(1)}, u32[]{:S(2)}, u32[]{:S(2)}) %collective-permute-start.14) | collective-permute-done | bytes 32800 | tf_op jit(solution)/shard_map/ppermute | solution.py:432
  74.6 0.1 collective-permute-start.15
  74.7 0.1 collective-permute-start.9
  74.7 3.4 %collective-permute-start.10 = (bf16[512,128]{1,0:T(8,128)(2,1)S(1)}, bf16[512,128]{1,0:T(8,128)(2,1)S(1)}, u32[]{:S(2)}, u32[]{:S(2)}) collective-permute-start(bf16[512,128]{1,0:T(8,128)(2,1)S(1)} %get-tuple-element.61), channel_id=1, source_target_pairs={{0,2},{1,3},{2,0},{3,1},{4,6},{5,7},{6,4},{7,5},{8,10},{9,11},{10,... | collective-permute-start | bytes 393224 | tf_op jit(solution)/shard_map/ppermute | solution.py:19
  78.1 45.6 %all-reduce.3.cloned.1.call-done = f32[640,128]{1,0:T(8,128)} async-done(((f32[640,128]{1,0:T(8,128)}), f32[640,128]{1,0:T(8,128)}) %all-reduce.3.cloned.1.call-update) | async-done | bytes 327696 | tf_op jit(solution)/shard_map/psum | solution.py:592
  123.8 0.0 all-reduce.5.cloned.1.call-update
  123.8 2.5 %collective-permute-start.16 = (bf16[128,128]{1,0:T(8,128)(2,1)S(1)}, bf16[128,128]{1,0:T(8,128)(2,1)S(1)}, u32[]{:S(2)}, u32[]{:S(2)}) collective-permute-start(bf16[128,128]{1,0:T(8,128)(2,1)S(1)} %add_convert_fusion.1), channel_id=1, source_target_pairs={{0,2},{1,3},{2,0},{3,1},{4,6},{5,7},{6,4},{7,5},{8,10},{9,11},{10,... | collective-permute-start | bytes 98312 | tf_op jit(solution)/shard_map/ppermute | solution.py:432
  126.3 0.9 shard_map.190
  127.2 1.5 collective-permute-done.16
  128.7 33.1 %all-reduce.5.cloned.1.call-done.early = f32[640,128]{1,0:T(8,128)} async-done(((f32[640,128]{1,0:T(8,128)}), f32[640,128]{1,0:T(8,128)}) %all-reduce.5.cloned.1.call-update) | async-done | bytes 327696 | tf_op jit(solution)/shard_map/psum | solution.py:592
  161.8 1.0 copy-done.3
  162.8 0.8 shard_map.191
  (39 shorter events, 0.1 us)
Async XLA Ops:
  7.2 116.6 %all-reduce.3.cloned.1.call-start = ((), (), s32[]{:S(2)}) async-start(), calls=%async_computation | async-start | bytes 655360 | tf_op jit(solution)/shard_map/psum | solution.py:592
  8.8 18.9 %collective-permute-start = (bf16[576,128]{1,0:T(8,128)(2,1)}, bf16[576,128]{1,0:T(8,128)(2,1)S(1)}, u32[]{:S(2)}, u32[]{:S(2)}) collective-permute-start(bf16[576,128]{1,0:T(8,128)(2,1)} %get-tuple-element.38.refs_6_), channel_id=1, source_target_pairs={{0,1},{1,2},{2,3},{3,0},{4,5},{5,6},{6,7},{7,4},{8,9},{9,10},{10,1... | collective-permute-start | bytes 442376 | tf_op jit(solution)/shard_map/ppermute | solution.py:19
  11.8 15.9 %collective-permute-start.1 = (bf16[576,128]{1,0:T(8,128)(2,1)}, bf16[576,128]{1,0:T(8,128)(2,1)S(1)}, u32[]{:S(2)}, u32[]{:S(2)}) collective-permute-start(bf16[576,128]{1,0:T(8,128)(2,1)} %get-tuple-element.38.refs_6_), channel_id=1, source_target_pairs={{0,2},{1,3},{2,0},{3,1},{4,6},{5,7},{6,4},{7,5},{8,10},{9,11},{10,... | collective-permute-start | bytes 442376 | tf_op jit(solution)/shard_map/ppermute | solution.py:19
  14.4 13.3 %collective-permute-start.2 = (bf16[576,128]{1,0:T(8,128)(2,1)}, bf16[576,128]{1,0:T(8,128)(2,1)S(1)}, u32[]{:S(2)}, u32[]{:S(2)}) collective-permute-start(bf16[576,128]{1,0:T(8,128)(2,1)} %get-tuple-element.38.refs_6_), channel_id=1, source_target_pairs={{0,3},{1,0},{2,1},{3,2},{4,7},{5,4},{6,5},{7,6},{8,11},{9,8},{10,9... | collective-permute-start | bytes 442376 | tf_op jit(solution)/shard_map/ppermute | solution.py:19
  15.8 11.9 %collective-permute-start.3 = (bf16[576,128]{1,0:T(8,128)(2,1)}, bf16[576,128]{1,0:T(8,128)(2,1)S(1)}, u32[]{:S(2)}, u32[]{:S(2)}) collective-permute-start(bf16[576,128]{1,0:T(8,128)(2,1)} %get-tuple-element.38.refs_6_), channel_id=1, source_target_pairs={{0,4},{4,8},{8,12},{12,16},{16,20},{20,24},{24,28},{28,0},{1,5},{5... | collective-permute-start | bytes 442376 | tf_op jit(solution)/shard_map/ppermute | solution.py:19
  15.8 11.9 %collective-permute-start.4 = (bf16[576,128]{1,0:T(8,128)(2,1)}, bf16[576,128]{1,0:T(8,128)(2,1)S(1)}, u32[]{:S(2)}, u32[]{:S(2)}) collective-permute-start(bf16[576,128]{1,0:T(8,128)(2,1)} %get-tuple-element.38.refs_6_), channel_id=1, source_target_pairs={{0,28},{4,0},{8,4},{12,8},{16,12},{20,16},{24,20},{28,24},{1,29},{... | collective-permute-start | bytes 442376 | tf_op jit(solution)/shard_map/ppermute | solution.py:19
  19.1 1.2 copy-start.1
  20.3 7.5 %copy-start.6 = (bf16[128,128]{1,0:T(8,128)(2,1)S(1)}, bf16[128,128]{1,0:T(8,128)(2,1)}, u32[]{:S(2)}) copy-start(bf16[128,128]{1,0:T(8,128)(2,1)} %w_recv.1) | copy-start | bytes 98308
  20.3 7.5 %copy-start.9 = (bf16[128,128]{1,0:T(8,128)(2,1)S(1)}, bf16[128,128]{1,0:T(8,128)(2,1)}, u32[]{:S(2)}) copy-start(bf16[128,128]{1,0:T(8,128)(2,1)} %w_send.1) | copy-start | bytes 98308
  20.3 7.5 %copy-start.12 = (bf16[576,128]{1,0:T(8,128)(2,1)S(1)}, bf16[576,128]{1,0:T(8,128)(2,1)}, u32[]{:S(2)}) copy-start(bf16[576,128]{1,0:T(8,128)(2,1)} %get-tuple-element.38.refs_6_) | copy-start | bytes 442372
  20.3 7.5 %copy-start.13 = (bf16[16,384]{1,0:T(8,128)(2,1)S(1)}, bf16[16,384]{1,0:T(8,128)(2,1)}, u32[]{:S(2)}) copy-start(bf16[16,384]{1,0:T(8,128)(2,1)} %get-tuple-element.37.refs_4_) | copy-start | bytes 36868
  27.7 0.7 copy-start.14
  27.8 0.7 copy-start.15
  27.8 0.7 copy-start.16
  28.4 15.6 %copy-start = (bf16[512,128]{1,0:T(8,128)(2,1)S(1)}, bf16[512,128]{1,0:T(8,128)(2,1)}, u32[]{:S(2)}) copy-start(bf16[512,128]{1,0:T(8,128)(2,1)} %latent.5) | copy-start | bytes 393220
  28.4 15.6 %copy-start.2 = (bf16[512,128]{1,0:T(8,128)(2,1)S(1)}, bf16[512,128]{1,0:T(8,128)(2,1)}, u32[]{:S(2)}) copy-start(bf16[512,128]{1,0:T(8,128)(2,1)} %cotangent.3) | copy-start | bytes 393220
  28.4 15.6 %copy-start.4 = (bf16[128,128]{1,0:T(8,128)(2,1)S(1)}, bf16[128,128]{1,0:T(8,128)(2,1)}, u32[]{:S(2)}) copy-start(bf16[128,128]{1,0:T(8,128)(2,1)} %w_edge_out.3) | copy-start | bytes 98308
  28.4 15.6 %copy-start.5 = (bf16[128,128]{1,0:T(8,128)(2,1)S(1)}, bf16[128,128]{1,0:T(8,128)(2,1)}, u32[]{:S(2)}) copy-start(bf16[128,128]{1,0:T(8,128)(2,1)} %w_node_self.3) | copy-start | bytes 98308
  28.4 15.6 %copy-start.7 = (bf16[128,128]{1,0:T(8,128)(2,1)S(1)}, bf16[128,128]{1,0:T(8,128)(2,1)}, u32[]{:S(2)}) copy-start(bf16[128,128]{1,0:T(8,128)(2,1)} %w_node_msg.1) | copy-start | bytes 98308
  28.5 15.6 %copy-start.8 = (bf16[128,128]{1,0:T(8,128)(2,1)S(1)}, bf16[128,128]{1,0:T(8,128)(2,1)}, u32[]{:S(2)}) copy-start(bf16[128,128]{1,0:T(8,128)(2,1)} %w_node_out.1) | copy-start | bytes 98308
  38.2 5.9 %collective-permute-start.5 = (bf16[512,128]{1,0:T(8,128)(2,1)S(1)}, bf16[512,128]{1,0:T(8,128)(2,1)S(1)}, u32[]{:S(2)}, u32[]{:S(2)}) collective-permute-start(bf16[512,128]{1,0:T(8,128)(2,1)S(1)} %get-tuple-element.40), channel_id=1, source_target_pairs={{0,4},{4,8},{8,12},{12,16},{16,20},{20,24},{24,28},{28,0},{1,5},{5... | collective-permute-start | bytes 393224 | tf_op jit(solution)/shard_map/ppermute | solution.py:19
  38.2 5.8 %collective-permute-start.6 = (bf16[512,128]{1,0:T(8,128)(2,1)S(1)}, bf16[512,128]{1,0:T(8,128)(2,1)S(1)}, u32[]{:S(2)}, u32[]{:S(2)}) collective-permute-start(bf16[512,128]{1,0:T(8,128)(2,1)S(1)} %get-tuple-element.41), channel_id=1, source_target_pairs={{0,28},{4,0},{8,4},{12,8},{16,12},{20,16},{24,20},{28,24},{1,29},{... | collective-permute-start | bytes 393224 | tf_op jit(solution)/shard_map/ppermute | solution.py:19
  44.0 0.7 copy-start.10
  44.0 0.7 copy-start.11
  46.5 9.4 %collective-permute-start.7 = (bf16[1024,128]{1,0:T(8,128)(2,1)S(1)}, bf16[1024,128]{1,0:T(8,128)(2,1)S(1)}, u32[]{:S(2)}, u32[]{:S(2)}) collective-permute-start(bf16[1024,128]{1,0:T(8,128)(2,1)S(1)} %get-tuple-element.46), channel_id=1, source_target_pairs={{0,4},{4,8},{8,12},{12,16},{16,20},{20,24},{24,28},{28,0},{1,5},{5... | collective-permute-start | bytes 786440 | tf_op jit(solution)/shard_map/ppermute | solution.py:19
  46.6 9.3 %collective-permute-start.8 = (bf16[1024,128]{1,0:T(8,128)(2,1)S(1)}, bf16[1024,128]{1,0:T(8,128)(2,1)S(1)}, u32[]{:S(2)}, u32[]{:S(2)}) collective-permute-start(bf16[1024,128]{1,0:T(8,128)(2,1)S(1)} %get-tuple-element.47.refs_4_), channel_id=1, source_target_pairs={{0,28},{4,0},{8,4},{12,8},{16,12},{20,16},{24,20},{28,24},{1,29},{... | collective-permute-start | bytes 786440 | tf_op jit(solution)/shard_map/ppermute | solution.py:19
  65.3 1.3 collective-permute-start.12
  66.6 4.0 %collective-permute-start.13 = (bf16[128,128]{1,0:T(8,128)(2,1)S(1)}, bf16[128,128]{1,0:T(8,128)(2,1)S(1)}, u32[]{:S(2)}, u32[]{:S(2)}) collective-permute-start(bf16[128,128]{1,0:T(8,128)(2,1)S(1)} %add_convert_fusion.4), channel_id=1, source_target_pairs={{0,8},{4,12},{8,0},{12,4},{16,24},{20,28},{24,16},{28,20},{1,9},{5... | collective-permute-start | bytes 98312 | tf_op jit(solution)/shard_map/ppermute | solution.py:432
  70.6 4.0 %collective-permute-start.14 = (bf16[128,128]{1,0:T(8,128)(2,1)S(1)}, bf16[128,128]{1,0:T(8,128)(2,1)S(1)}, u32[]{:S(2)}, u32[]{:S(2)}) collective-permute-start(bf16[128,128]{1,0:T(8,128)(2,1)S(1)} %add_convert_fusion.3), channel_id=1, source_target_pairs={{0,16},{4,20},{8,24},{12,28},{16,0},{20,4},{24,8},{28,12},{1,17},{... | collective-permute-start | bytes 98312 | tf_op jit(solution)/shard_map/ppermute | solution.py:432
  72.2 89.6 %all-reduce.5.cloned.1.call-start = ((), (), s32[]{:S(2)}) async-start(), calls=%async_computation.1 | async-start | bytes 655360 | tf_op jit(solution)/shard_map/psum | solution.py:592
  74.6 49.2 %collective-permute-start.15 = (bf16[128,128]{1,0:T(8,128)(2,1)S(1)}, bf16[128,128]{1,0:T(8,128)(2,1)S(1)}, u32[]{:S(2)}, u32[]{:S(2)}) collective-permute-start(bf16[128,128]{1,0:T(8,128)(2,1)S(1)} %add_convert_fusion.2), channel_id=1, source_target_pairs={{0,1},{1,0},{2,3},{3,2},{4,5},{5,4},{6,7},{7,6},{8,9},{9,8},{10,11... | collective-permute-start | bytes 98312 | tf_op jit(solution)/shard_map/ppermute | solution.py:432
  74.7 51.6 %collective-permute-start.9 = (bf16[512,128]{1,0:T(8,128)(2,1)S(1)}, bf16[512,128]{1,0:T(8,128)(2,1)S(1)}, u32[]{:S(2)}, u32[]{:S(2)}) collective-permute-start(bf16[512,128]{1,0:T(8,128)(2,1)S(1)} %get-tuple-element.60), channel_id=1, source_target_pairs={{0,3},{1,0},{2,1},{3,2},{4,7},{5,4},{6,5},{7,6},{8,11},{9,8},{10,9... | collective-permute-start | bytes 393224 | tf_op jit(solution)/shard_map/ppermute | solution.py:19
  74.7 51.6 %collective-permute-start.10 = (bf16[512,128]{1,0:T(8,128)(2,1)S(1)}, bf16[512,128]{1,0:T(8,128)(2,1)S(1)}, u32[]{:S(2)}, u32[]{:S(2)}) collective-permute-start(bf16[512,128]{1,0:T(8,128)(2,1)S(1)} %get-tuple-element.61), channel_id=1, source_target_pairs={{0,2},{1,3},{2,0},{3,1},{4,6},{5,7},{6,4},{7,5},{8,10},{9,11},{10,... | collective-permute-start | bytes 393224 | tf_op jit(solution)/shard_map/ppermute | solution.py:19
  78.1 48.2 %collective-permute-start.11 = (bf16[512,128]{1,0:T(8,128)(2,1)S(1)}, bf16[512,128]{1,0:T(8,128)(2,1)S(1)}, u32[]{:S(2)}, u32[]{:S(2)}) collective-permute-start(bf16[512,128]{1,0:T(8,128)(2,1)S(1)} %get-tuple-element.62), channel_id=1, source_target_pairs={{0,1},{1,2},{2,3},{3,0},{4,5},{5,6},{6,7},{7,4},{8,9},{9,10},{10,1... | collective-permute-start | bytes 393224 | tf_op jit(solution)/shard_map/ppermute | solution.py:19
  123.8 4.9 %collective-permute-start.16 = (bf16[128,128]{1,0:T(8,128)(2,1)S(1)}, bf16[128,128]{1,0:T(8,128)(2,1)S(1)}, u32[]{:S(2)}, u32[]{:S(2)}) collective-permute-start(bf16[128,128]{1,0:T(8,128)(2,1)S(1)} %add_convert_fusion.1), channel_id=1, source_target_pairs={{0,2},{1,3},{2,0},{3,1},{4,6},{5,7},{6,4},{7,5},{8,10},{9,11},{10,... | collective-permute-start | bytes 98312 | tf_op jit(solution)/shard_map/ppermute | solution.py:432
  161.8 1.0 copy-start.3
Sparse Core Ops, SparseCore 0:
  72.3 51.4 all-reduce.2
  126.1 35.6 all-reduce.4

commit v4 on v3

--- a/solution.py
+++ b/solution.py
@@ -7,8 +7,9 @@
 
 F32 = jnp.float32
 BF16 = jnp.bfloat16
-GROUPS = (6, 6)
+GROUPS = (8, 8)
 LOOPED = 4
+TOGETHER = 4
 CHUNK = 32
 PARTS = 16
 
@@ -80,14 +81,8 @@
         weight_parts[:, item * width : (item + 1) * width] = stacked.astype(BF16)
 
 
-def ranks_kernel(tile_count, mask_far, row_rank, row_degree, col_rank, row_most, col_most, mask, sem):
+def ranks_kernel(tile_count, mask, row_rank, row_degree, col_rank, most):
     tiles, size = mask.shape[0], mask.shape[-1]
-    copies = [
-        pltpu.make_async_copy(mask_far.at[tile], mask.at[tile], sem.at[tile])
-        for tile in range(tiles)
-    ]
-    for copy in copies:
-        copy.start()
     row_index = lax.broadcasted_iota(jnp.int32, (size, size), 0)
     col_index = lax.broadcasted_iota(jnp.int32, (size, size), 1)
     upper = (row_index <= col_index).astype(F32).astype(BF16)
@@ -95,18 +90,48 @@
     ones = jnp.ones((size, size), BF16)
     for_rows = jnp.concatenate([upper, ones], 1)
     for_cols = jnp.concatenate([upper, eye], 1)
+    most[...] = jnp.zeros_like(most)
+    for table in (row_rank, row_degree, col_rank):
+        table[tiles] = jnp.zeros((size, size), BF16)
+    for start in range(0, tiles, TOGETHER):
+        here = range(start, min(start + TOGETHER, tiles))
+        values = []
+        for tile in here:
+            live = (tile < tile_count[0, 0]).astype(F32)
+            values.append(mask[tile].astype(F32) * live)
+        values_b = [value.astype(BF16) for value in values]
+        found = dot(jnp.concatenate(values_b, 0), for_rows)
+        for item, tile in enumerate(here):
+            span = slice(item * size, (item + 1) * size)
+            row_rank[tile] = (found[span, :size] * values[item]).astype(BF16)
+            degree = found[span, size:]
+            row_degree[tile] = degree.astype(BF16)
+            most[0, tile : tile + 1, :] = jnp.max(degree, axis=0, keepdims=True).astype(jnp.int32)
+        for item, tile in enumerate(here):
+            found = contract_rows(values_b[item], for_cols)
+            ranks = found[:, :size]
+            col_rank[tile] = (ranks * found[:, size:]).astype(BF16)
+            most[1, tile : tile + 1, :] = jnp.max(ranks, axis=0, keepdims=True).astype(jnp.int32)
+
+
+def list_tiles(order, tile_recv, tile_count, blocks, own):
+    tiles = tile_recv.shape[-1]
+    found = jnp.int32(0)
     for tile in range(tiles):
-        copies[tile].wait()
-        live = (tile < tile_count[0, 0]).astype(F32)
-        values = mask[tile].astype(F32) * live
-        values_b = values.astype(BF16)
-        found = dot(values_b, for_rows)
-        row_rank[tile] = (found[:, :size] * values).astype(BF16)
-        row_degree[tile] = found[:, size:].astype(BF16)
-        row_most[tile] = jnp.max(found[:, size:]).astype(jnp.int32)
-        found = contract_rows(values_b, for_cols)
-        col_rank[tile] = (found[:, :size] * found[:, size:]).astype(BF16)
-        col_most[tile] = jnp.max(found[:, :size]).astype(jnp.int32)
+        mine = (tile_recv[0, 0, tile] // blocks == 1) == own
+        order[found] = tile
+        found = found + (mine & (tile < tile_count[0, 0])).astype(jnp.int32)
+    order[found] = tiles
+    return (found + 1) // 2
+
+
+def pair_of(pair, order, tile_send, tile_recv, member, members, blocks):
+    last = tile_recv.shape[-1] - 1
+    tiles = [order[2 * pair], order[2 * pair + 1]]
+    named = [tiles[0], jnp.where(tiles[1] > last, tiles[0], tiles[1])]
+    recv_places = [tile_recv[0, 0, tile] for tile in named]
+    send_places = [sender_place(tile_send[0, 0, tile], member, members, blocks) for tile in named]
+    return tiles, recv_places, send_places
 
 
 def one_hots(rank_block, first, ranks):
@@ -163,56 +188,67 @@
     return copies
 
 
-def make_forward(members, blocks):
-    def kernel(tile_count, send_far, recv_far, most_far, *refs):
-        row_rank, row_degree, w_send, w_recv, weight_parts, edge_bias, refs = *refs[:6], refs[6:]
-        messages, sides, refs = refs[:members], refs[members : members + 2], refs[members + 2 :]
-        sums_out, counts_out, refs = refs[:3], refs[3:6], refs[6:]
-        senders, receivers, refs = refs[0], refs[1], refs[2:]
-        sums, counts, total, count, tile_send, tile_recv, row_most, sem = refs
+def make_rows(members, blocks, size, width):
+    rows = blocks * size
+
+    def placed_of(message, weight_parts):
+        found = []
+        for block in range(blocks):
+            start = rows + block * PARTS
+            parts = contract_rows(message[start : start + PARTS, :], weight_parts[...])
+            found.append(parts[:, :width] + parts[:, width : 2 * width] + parts[:, 2 * width :])
+        return jnp.concatenate(found, 0)
+
+    def lay(table, place, found):
+        for block in range(blocks):
+            span = slice(block * size, (block + 1) * size)
+            table[place * blocks + block] = found[span, :].astype(BF16)
+
+    def lay_rows(messages, sides, w_send, w_recv, weight_parts, edge_bias, senders, receivers):
+        for distance, message in enumerate(messages):
+            placed = placed_of(message, weight_parts)
+            lay(senders, distance, dot(message[0:rows, :], w_send[...]) + placed)
+            if distance == 0:
+                lay(receivers, 1, dot(message[0:rows, :], w_recv[...]) - placed + edge_bias[...])
+        for place, message in ((0, sides[0]), (2, sides[1])):
+            placed = placed_of(message, weight_parts)
+            lay(receivers, place, dot(message[0:rows, :], w_recv[...]) - placed + edge_bias[...])
+
+    return lay_rows
+
+
+def make_forward(members, blocks, own):
+    def kernel(tile_count, send_far, recv_far, most_far, row_rank, row_degree, *refs):
+        if own:
+            senders, receivers, sums_out, counts_out, refs = *refs[:4], refs[4:]
+            sides = ((1, sums_out, counts_out),)
+        else:
+            weights, refs = refs[:4], refs[4:]
+            messages, refs = refs[:members], refs[members:]
+            beside, refs = refs[:2], refs[2:]
+            sides = ((0, refs[0], refs[2]), (2, refs[1], refs[3]))
+            senders, receivers, refs = refs[4], refs[5], refs[6:]
+        sums, counts, total, count, tile_send, tile_recv, row_most, order, sem = refs
         size, width = senders.shape[1:]
-        rows = blocks * size
         copies = start_copies(
-            (send_far, recv_far, most_far), (tile_send, tile_recv, row_most), sem
+            (send_far, recv_far, most_far.at[0]), (tile_send, tile_recv, row_most), sem
         )
         member = lax.axis_index("grp")
         sums[...] = jnp.zeros_like(sums)
         counts[...] = jnp.zeros_like(counts)
-
-        def placed_of(message):
-            found = []
-            for block in range(blocks):
-                start = rows + block * PARTS
-                parts = contract_rows(message[start : start + PARTS, :], weight_parts[...])
-                found.append(parts[:, :width] + parts[:, width : 2 * width] + parts[:, 2 * width :])
-            return jnp.concatenate(found, 0)
-
-        def lay(table, place, found):
-            for block in range(blocks):
-                span = slice(block * size, (block + 1) * size)
-                table[place * blocks + block] = found[span, :].astype(BF16)
-
-        for distance, message in enumerate(messages):
-            placed = placed_of(message)
-            lay(senders, distance, dot(message[0:rows, :], w_send[...]) + placed)
-            if distance == 0:
-                lay(receivers, 1, dot(message[0:rows, :], w_recv[...]) - placed + edge_bias[...])
-        for place, message in ((0, sides[0]), (2, sides[1])):
-            placed = placed_of(message)
-            lay(receivers, place, dot(message[0:rows, :], w_recv[...]) - placed + edge_bias[...])
+        if not own:
+            lay_rows = make_rows(members, blocks, size, width)
+            lay_rows(messages, beside, *weights, senders, receivers)
         for copy in copies:
             copy.wait()
 
         def one_pair(pair, carry):
-            tiles = (2 * pair, 2 * pair + 1)
-            recv_places = [tile_recv[0, 0, tile] for tile in tiles]
-            send_rows = [
-                senders[sender_place(tile_send[0, 0, tile], member, members, blocks)]
-                for tile in tiles
-            ]
+            tiles, recv_places, send_places = pair_of(
+                pair, order, tile_send, tile_recv, member, members, blocks
+            )
             nothing = jnp.zeros((size, width), BF16)
-            upper = jnp.concatenate([send_rows[0], nothing], 1)
-            lower = jnp.concatenate([nothing, send_rows[1]], 1)
+            upper = jnp.concatenate([senders[send_places[0]], nothing], 1)
+            lower = jnp.concatenate([nothing, senders[send_places[1]]], 1)
             right = jnp.concatenate([upper, lower], 0)
             recv_rows = jnp.concatenate([receivers[place] for place in recv_places], 1).astype(F32)
             ranks_of = [row_rank[tile] for tile in tiles]
@@ -233,7 +269,7 @@
                     total[span, :] = added if fresh else total[span, :] + added
                     count[span, :] = seen if fresh else count[span, :] + seen
 
-            most = jnp.maximum(row_most[tiles[0]], row_most[tiles[1]])
+            most = jnp.maximum(row_most[tiles[0], size - 1], row_most[tiles[1], size - 1])
             done = jnp.asarray(run_groups(one_group, most), jnp.int32).astype(F32)
             for item, tile in enumerate(tiles):
                 half = slice(item * width, (item + 1) * width)
@@ -244,9 +280,10 @@
                 counts[place] += count[:, half] - jnp.where(rows_here > 0.0, spare, 0.0)
             return carry
 
-        lax.fori_loop(0, (tile_count[0, 0] + 1) // 2, one_pair, 0)
-        for table, outs in ((sums, sums_out), (counts, counts_out)):
-            for side, out in enumerate(outs):
+        pairs = list_tiles(order, tile_recv, tile_count, blocks, own)
+        lax.fori_loop(0, pairs, one_pair, 0)
+        for side, *outs in sides:
+            for table, out in zip((sums, counts), outs):
                 for block in range(blocks):
                     out[block * size : (block + 1) * size, :] = table[side * blocks + block].astype(
                         out.dtype
@@ -324,25 +361,34 @@
 
 
 def early_kernel(
+    latent, aggregate, message, hidden, d_update, d_hidden_pre, d_message, keep, give, grads
+):
+    width = latent.shape[1]
+    grads[0:width, :] = contract_rows(aggregate[...], d_message[...])
+    grads[width : 2 * width, :] = contract_rows(latent[...], d_hidden_pre[...])
+    grads[2 * width : 3 * width, :] = contract_rows(message[...], d_hidden_pre[...])
+    grads[3 * width : 4 * width, :] = contract_rows(hidden[...], d_update[...])
+    half = keep.shape[0]
+    bit = lax.axis_index("grp") & 1
+    keep[...] = grads[pl.ds(pl.multiple_of(bit * half, half), half), :]
+    give[...] = grads[pl.ds(pl.multiple_of((1 - bit) * half, half), half), :].astype(BF16)
+
+
+def recv_kernel(
     latent,
     cotangent,
     count_own,
     from_low,
     from_high,
-    aggregate,
-    message,
-    hidden,
-    d_update,
     d_hidden_pre,
     d_message,
     w_edge_out,
     w_node_self,
     w_recv,
     direct_out,
-    grads,
+    grad_out,
 ):
-    own_rows, width = latent.shape
-    rows = latent[...]
+    own_rows = latent.shape[0]
     count = count_own[...] + from_low[own_rows:, :].astype(F32)
     count = count + from_high[own_rows:, :].astype(F32)
     d_recv = (dot_t(d_message[...], w_edge_out[...]) * count).astype(BF16)
@@ -351,41 +397,43 @@
         + dot_t(d_hidden_pre[...], w_node_self[...])
         + dot_t(d_recv, w_recv[...])
     )
-    grads[0:width, :] = contract_rows(rows, d_recv)
-    grads[width : 2 * width, :] = contract_rows(aggregate[...], d_message[...])
-    grads[2 * width : 3 * width, :] = contract_rows(rows, d_hidden_pre[...])
-    grads[3 * width : 4 * width, :] = contract_rows(message[...], d_hidden_pre[...])
-    grads[4 * width : 5 * width, :] = contract_rows(hidden[...], d_update[...])
-
-
-def make_backward(members, blocks):
-    def kernel(tile_count, send_far, recv_far, most_far, *refs):
-        col_rank, senders, receivers, refs = *refs[:3], refs[3:]
-        grad_parts, refs = refs[:3], refs[3:]
-        messages, refs = refs[:members], refs[members:]
-        grads_out, refs = refs[:members], refs[members:]
-        late_out, d_sums, grads, totals, tile_send, tile_recv, col_most, sem = refs
+    grad_out[...] = contract_rows(latent[...], d_recv).astype(BF16)
+
+
+def make_backward(members, blocks, own):
+    def kernel(tile_count, send_far, recv_far, most_far, col_rank, senders, receivers, *refs):
+        if own:
+            grad_parts, grads, refs = (None, refs[0], None), refs[1], refs[2:]
+            d_sums = refs[0]
+        else:
+            grad_parts, started, refs = (refs[0], None, refs[1]), refs[2], refs[3:]
+            messages, refs = refs[:members], refs[members:]
+            grads_out, late_out, refs = refs[:members], refs[members], refs[members + 1 :]
+            d_sums, grads = refs[0], refs[-1]
+        totals, tile_send, tile_recv, col_most, order, sem = refs[1:7]
         size, width = senders.shape[1:]
         rows = blocks * size
         copies = start_copies(
-            (send_far, recv_far, most_far), (tile_send, tile_recv, col_most), sem
+            (send_far, recv_far, most_far.at[1]), (tile_send, tile_recv, col_most), sem
         )
         member = lax.axis_index("grp")
-        lay_blocks(d_sums, [part.at[0:rows, :] for part in grad_parts])
-        grads[...] = jnp.zeros_like(grads)
+        for side, part in enumerate(grad_parts):
+            if part is not None:
+                for block in range(blocks):
+                    span = slice(block * size, (block + 1) * size)
+                    d_sums[side * blocks + block] = part[span, :]
+        grads[...] = jnp.zeros_like(grads) if own else started[...]
         unit = eye_of(size)
         nothing = jnp.zeros((size, width), BF16)
         for copy in copies:
             copy.wait()
 
         def one_pair(pair, carry):
-            tiles = (2 * pair, 2 * pair + 1)
-            send_places = [
-                sender_place(tile_send[0, 0, tile], member, members, blocks) for tile in tiles
-            ]
+            tiles, recv_places, send_places = pair_of(
+                pair, order, tile_send, tile_recv, member, members, blocks
+            )
             rights = []
-            for tile, send_place in zip(tiles, send_places):
-                recv_place = tile_recv[0, 0, tile]
+            for recv_place, send_place in zip(recv_places, send_places):
                 upper = jnp.concatenate([receivers[recv_place], d_sums[recv_place]], 1)
                 lower = jnp.concatenate([senders[send_place], nothing], 1)
                 rights.append(jnp.concatenate([upper, lower], 0))
@@ -404,12 +452,16 @@
                             added = added + jnp.where(part[:, :width] > 0.0, part[:, width:], 0.0)
                         totals[place, span, :] = added if fresh else totals[place, span, :] + added
 
-            run_groups(one_group, jnp.maximum(col_most[tiles[0]], col_most[tiles[1]]))
+            most = jnp.maximum(col_most[tiles[0], size - 1], col_most[tiles[1], size - 1])
+            run_groups(one_group, most)
             for item, send_place in enumerate(send_places):
                 grads[send_place] += totals[item]
             return carry
 
-        lax.fori_loop(0, (tile_count[0, 0] + 1) // 2, one_pair, 0)
+        pairs = list_tiles(order, tile_recv, tile_count, blocks, own)
+        lax.fori_loop(0, pairs, one_pair, 0)
+        if own:
+            return
         late = jnp.zeros((width, width), F32)
         for distance, out in enumerate(grads_out):
             for block in range(blocks):
@@ -422,15 +474,22 @@
     return kernel
 
 
+def exchanged(value, axis, step):
+    count = lax.axis_size(axis)
+    return lax.ppermute(value, axis, [(source, source ^ step) for source in range(count)])
+
+
+def bit_set(axis, step):
+    return (lax.axis_index(axis) & step) != 0
+
+
 def pairwise_sum(value, axis):
     count = lax.axis_size(axis)
     if count & (count - 1):
         return lax.psum(value.astype(F32), axis).astype(BF16)
     step = 1
     while step < count:
-        pairs = [(source, source ^ step) for source in range(count)]
-        other = lax.ppermute(value, axis, pairs)
-        value = (value.astype(F32) + other.astype(F32)).astype(BF16)
+        value = (value.astype(F32) + exchanged(value, axis, step).astype(F32)).astype(BF16)
         step *= 2
     return value
 
@@ -443,11 +502,18 @@
     latent_grad[...] = direct[...] + dot_t(d_send.astype(BF16), w_send[...])
 
 
-def last_kernel(early, late, weight_grads):
-    width = late.shape[1]
-    weight_grads[0] = late[...].astype(F32)
-    for item in range(weight_grads.shape[0] - 1):
-        weight_grads[item + 1] = early[item * width : (item + 1) * width, :]
+def last_kernel(mine, other, weight_grads, table):
+    summed = mine.shape[0] - table.shape[0] // 2
+    half = table.shape[0] // 2
+    width = mine.shape[1]
+    bit = lax.axis_index("grp") & 1
+    table[pl.ds(pl.multiple_of(bit * half, half), half), :] = mine[0:half, :].astype(F32)
+    table[pl.ds(pl.multiple_of((1 - bit) * half, half), half), :] = other[0:half, :].astype(F32)
+    for item in range(summed // width):
+        span = slice(half + item * width, half + (item + 1) * width)
+        weight_grads[item] = mine[span, :].astype(F32) + other[span, :].astype(F32)
+    for item in range(table.shape[0] // width):
+        weight_grads[summed // width + item] = table[item * width : (item + 1) * width, :]
 
 
 def body(
@@ -476,8 +542,8 @@
     node_like = like((own_rows, width), BF16)
     node_float = like((own_rows, width), F32)
     pair_like = like((2 * own_rows, width), BF16)
-    tile_like = like((tiles, size, size), BF16)
-    most_like = like((tiles,), jnp.int32)
+    tile_like = like((tiles + 1, size, size), BF16)
+    most_like = like((2, tiles + 8, size), jnp.int32)
     slab_like = like((members * blocks, size, width), BF16)
     near_like = like((3 * blocks, size, width), BF16)
     message, weight_parts = call(
@@ -488,29 +554,26 @@
     )
     messages = [message] + [shifted(message, "grp", distance) for distance in range(1, members)]
     sides = [shifted(message, "blk", 1), shifted(message, "blk", -1)]
-    row_rank, row_degree, col_rank, row_most, col_most = call(
+    row_rank, row_degree, col_rank, most = call(
         ranks_kernel,
-        [tile_like] * 3,
-        [],
+        [tile_like] * 3 + [most_like],
+        [tile_mask.reshape(tiles, size, size)],
         scalars=[tile_count],
-        far=[tile_mask.reshape(tiles, size, size)],
-        smem_outs=[most_like] * 2,
-        scratch=[
-            pltpu.VMEM((tiles, size, size), jnp.int32),
-            pltpu.SemaphoreType.DMA((tiles,)),
-        ],
         flops=8 * tiles * size * size * size,
     )
     tables = [
         pltpu.SMEM(tile_send.shape, jnp.int32),
         pltpu.SMEM(tile_recv.shape, jnp.int32),
-        pltpu.SMEM((tiles,), jnp.int32),
+        pltpu.SMEM(most.shape[1:], jnp.int32),
+        pltpu.SMEM((tiles + 2,), jnp.int32),
         pltpu.SemaphoreType.DMA((3,)),
     ]
     window = pltpu.VMEM((3 * blocks, size, width), F32)
-    sum_low, sum_own, sum_high, count_low, count_own, count_high, senders, receivers = call(
-        make_forward(members, blocks),
-        [node_like, node_float, node_like] * 2 + [slab_like, near_like],
+    sums_scratch = [window] * 2 + [pltpu.VMEM((size, 2 * width), F32)] * 2 + tables
+    tile_flops = 64 * tiles * size * size * width
+    sum_low, sum_high, count_low, count_high, senders, receivers = call(
+        make_forward(members, blocks, False),
+        [node_like] * 4 + [slab_like, near_like],
         [
             row_rank,
             row_degree,
@@ -522,15 +585,19 @@
             *sides,
         ],
         scalars=[tile_count],
-        far=[tile_send, tile_recv, row_most],
-        scratch=[
-            window,
-            window,
-            pltpu.VMEM((size, 2 * width), F32),
-            pltpu.VMEM((size, 2 * width), F32),
-            *tables,
-        ],
-        flops=64 * tiles * size * size * width,
+        far=[tile_send, tile_recv, most],
+        scratch=sums_scratch,
+        flops=tile_flops,
+    )
+    from_low, from_high = shifted(sum_high, "blk", 1), shifted(sum_low, "blk", -1)
+    sum_own, count_own = call(
+        make_forward(members, blocks, True),
+        [node_float] * 2,
+        [row_rank, row_degree, senders, receivers],
+        scalars=[tile_count],
+        far=[tile_send, tile_recv, most],
+        scratch=sums_scratch,
+        flops=tile_flops // 2,
     )
     (
         new_latent,
@@ -549,8 +616,8 @@
             latent,
             cotangent,
             sum_own,
-            shifted(sum_high, "blk", 1),
-            shifted(sum_low, "blk", -1),
+            from_low,
+            from_high,
             count_low,
             count_high,
             w_edge_out,
@@ -566,53 +633,92 @@
         ],
         flops=14 * own_rows * width * width,
     )
-    from_low = shifted(to_high, "blk", 1)
-    from_high = shifted(to_low, "blk", -1)
-    direct, early = call(
+    from_low, from_high = shifted(to_high, "blk", 1), shifted(to_low, "blk", -1)
+    half = 4 * width // 2
+    share, given = call(
         early_kernel,
-        [node_float, like((5 * width, width), F32)],
+        [like((half, width), F32), like((half, width), BF16)],
+        [latent, aggregate, message_out, hidden, d_update, d_hidden_pre, d_message],
+        scratch=[pltpu.VMEM((2 * half, width), F32)],
+        flops=8 * own_rows * width * width,
+    )
+    share = share + exchanged(given, "grp", 1).astype(F32)
+    step = 2
+    while step < members:
+        half = share.shape[0] // 2
+        high = bit_set("grp", step)
+        given = jnp.where(high, share[:half], share[half:]).astype(BF16)
+        share = jnp.where(high, share[half:], share[:half])
+        share = share + exchanged(given, "grp", step).astype(F32)
+        step *= 2
+    back_scratch = [
+        pltpu.VMEM((3 * blocks, size, width), BF16),
+        pltpu.VMEM((2, size, width), F32),
+        *tables,
+    ]
+    (started,) = call(
+        make_backward(members, blocks, True),
+        [like((members * blocks, size, width), F32)],
+        [col_rank, senders, receivers, to_low],
+        scalars=[tile_count],
+        far=[tile_send, tile_recv, most],
+        scratch=back_scratch,
+        flops=tile_flops // 2,
+    )
+    direct, recv_grad = call(
+        recv_kernel,
+        [node_float, like((width, width), BF16)],
         [
             latent,
             cotangent,
             count_own,
             from_low,
             from_high,
-            aggregate,
-            message_out,
-            hidden,
-            d_update,
             d_hidden_pre,
             d_message,
             w_edge_out,
             w_node_self,
             w_recv,
         ],
-        flops=16 * own_rows * width * width,
-    )
-    early = lax.psum(lax.optimization_barrier(lax.psum(early, "blk")), "grp")
+        flops=8 * own_rows * width * width,
+    )
     *send_grads, late = call(
-        make_backward(members, blocks),
+        make_backward(members, blocks, False),
         [node_float] + [node_like] * (members - 1) + [like((width, width), BF16)],
-        [col_rank, senders, receivers, from_low, to_low, from_high, *messages],
+        [col_rank, senders, receivers, from_low, from_high, started, *messages],
         scalars=[tile_count],
-        far=[tile_send, tile_recv, col_most],
-        scratch=[
-            pltpu.VMEM((3 * blocks, size, width), BF16),
-            pltpu.VMEM((members * blocks, size, width), F32),
-            pltpu.VMEM((2, size, width), F32),
-            *tables,
-        ],
-        flops=64 * tiles * size * size * width,
+        far=[tile_send, tile_recv, most],
+        scratch=back_scratch + [pltpu.VMEM((members * blocks, size, width), F32)],
+        flops=tile_flops,
     )
     back = [shifted(send_grads[distance], "grp", -distance) for distance in range(1, members)]
-    late = pairwise_sum(pairwise_sum(late, "blk"), "grp")
+    chain = jnp.concatenate([share.astype(BF16), late, recv_grad], 0)
+    chain = pairwise_sum(chain, "blk")
+    share, summed = chain[: -2 * width], chain[-2 * width :]
+    step = members // 2
+    while step > 1:
+        other = exchanged(jnp.concatenate([share, summed], 0), "grp", step)
+        others = other[: -2 * width]
+        high = bit_set("grp", step)
+        share = jnp.concatenate(
+            [jnp.where(high, others, share), jnp.where(high, share, others)], 0
+        )
+        summed = (summed.astype(F32) + other[-2 * width :].astype(F32)).astype(BF16)
+        step //= 2
+    chain = jnp.concatenate([share, summed], 0)
+    other = exchanged(chain, "grp", 1)
     (latent_grad,) = call(
         return_kernel,
         [node_float],
         [direct, w_send, send_grads[0], *back],
         flops=2 * own_rows * width * width,
     )
-    (weight_grads,) = call(last_kernel, [like((6, width, width), F32)], [early, late])
+    (weight_grads,) = call(
+        last_kernel,
+        [like((6, width, width), F32)],
+        [chain, other],
+        scratch=[pltpu.VMEM((4 * width, width), F32)],
+    )
     return (new_latent, latent_grad, weight_grads)
 
 

time: 171 us -> 85.3 us (0.50)
  waiting for transfers between devices: 97.6 us -> 33.4 us
  between operations: 15 us -> 1.68 us
  Pallas kernels: 32.8 us -> 26.8 us
    psum x2 -> x0, waiting for transfers between devices: 78.7 us -> none  [body(): early = lax.psum(lax.optimization_barrier(lax.psum(early, 'blk')), 'grp')]
    ppermute x5 -> x7, waiting for transfers between devices: 8.95 us -> 20.9 us  [exchanged(): lax.ppermute(value, axis, [(source, source ^ step) for source in range(co...]
    pallas_call x8 -> x11, Pallas kernels: 32.8 us -> 26.8 us  [call(): pl.pallas_call(kernel, out_shape=[jax.ShapeDtypeStruct(o.shape, o.dtype)...]
    ppermute x12, waiting for transfers between devices: 9.88 us -> 12.5 us  [shifted(): return lax.ppermute(value, axis, pairs)]
    ppermute x5 -> x7, starting transfers between devices: 2.98 us -> 4.75 us  [exchanged(): lax.ppermute(value, axis, [(source, source ^ step) for source in range(co...]
    ppermute x12, starting transfers between devices: 18.5 us -> 16.7 us  [shifted(): return lax.ppermute(value, axis, pairs)]
    unnamed x34 -> x36, local copies, waits for them, and re-layouts: 3.47 us -> 2.51 us
  transfers between devices with their start and end apart: 19 -> 19, of which waited for: 8 -> 9; matrix products, arithmetic and copies ran while one was open for 0% -> 0% of each run, Pallas kernels for 6% -> 11%
where the time goes in v4:
time: 85.3 us; the launch traced here: 86 us
  waiting for transfers between devices  33.4 us (39%)
  Pallas kernels  26.8 us (31%)
  starting transfers between devices  21.5 us (25%)
  local copies, waits for them, and re-layouts  2.51 us (3%)
  between operations  1.68 us (2%)
    pallas_call x11, Pallas kernels, call(): pl.pallas_call(kernel, out_shape=[jax.ShapeDtypeStruct(o.shape, o.dtype)...  26.8 us
    ppermute x7, waiting for transfers between devices, exchanged(): lax.ppermute(value, axis, [(source, source ^ step) for source in range(co...  20.9 us
    ppermute x12, starting transfers between devices, shifted(): return lax.ppermute(value, axis, pairs)  16.7 us
    ppermute x12, waiting for transfers between devices, shifted(): return lax.ppermute(value, axis, pairs)  12.5 us
    ppermute x7, starting transfers between devices, exchanged(): lax.ppermute(value, axis, [(source, source ^ step) for source in range(co...  4.75 us
    unnamed x36, local copies, waits for them, and re-layouts  2.51 us
  transfers between devices with their start and end apart: 19, of which 9 were waited for; matrix products, arithmetic and copies ran while one was open for 0% of the time, Pallas kernels for 11%

profile of v4, /device:TPU:0, one launch (start us, length us, event | category | flops | bytes accessed | tf_op | source)
XLA Modules:
  0.0 86.0 jit_solution(7289127075000102332)
XLA Ops:
  0.6 1.6 %shard_map.185 = (bf16[576,128]{1,0:T(8,128)(2,1)}, bf16[16,384]{1,0:T(8,128)(2,1)}) custom-call(bf16[512,128]{1,0:T(8,128)(2,1)} %latent.7, f32[3,512]{1,0:T(4,128)} %positions.1, f32[3,128]{1,0:T(4,128)} %pos_weight.1), custom_call_target="tpu_custom_call" | custom-call | bytes 298496 | tf_op jit(solution)/shard_map/pallas_call | solution.py:42
  2.2 3.3 %collective-permute-start.4 = (bf16[576,128]{1,0:T(8,128)(2,1)}, bf16[576,128]{1,0:T(8,128)(2,1)S(1)}, u32[]{:S(2)}, u32[]{:S(2)}) collective-permute-start(bf16[576,128]{1,0:T(8,128)(2,1)} %get-tuple-element.39.refs_4_.refs_3_), channel_id=1, source_target_pairs={{0,28},{4,0},{8,4},{12,8},{16,12},{20,16},{24,20},{28,24},{1,29},{... | collective-permute-start | bytes 442376 | tf_op jit(solution)/shard_map/ppermute | solution.py:20
  5.6 3.6 %collective-permute-start.2 = (bf16[576,128]{1,0:T(8,128)(2,1)}, bf16[576,128]{1,0:T(8,128)(2,1)S(1)}, u32[]{:S(2)}, u32[]{:S(2)}) collective-permute-start(bf16[576,128]{1,0:T(8,128)(2,1)} %get-tuple-element.39.refs_4_.refs_3_), channel_id=1, source_target_pairs={{0,3},{1,0},{2,1},{3,2},{4,7},{5,4},{6,5},{7,6},{8,11},{9,8},{10,9... | collective-permute-start | bytes 442376 | tf_op jit(solution)/shard_map/ppermute | solution.py:20
  9.2 1.0 %collective-permute-start = (bf16[576,128]{1,0:T(8,128)(2,1)}, bf16[576,128]{1,0:T(8,128)(2,1)S(1)}, u32[]{:S(2)}, u32[]{:S(2)}) collective-permute-start(bf16[576,128]{1,0:T(8,128)(2,1)} %get-tuple-element.39.refs_4_.refs_3_), channel_id=1, source_target_pairs={{0,1},{1,2},{2,3},{3,0},{4,5},{5,6},{6,7},{7,4},{8,9},{9,10},{10,1... | collective-permute-start | bytes 442376 | tf_op jit(solution)/shard_map/ppermute | solution.py:20
  10.8 0.0 copy-start.1
  10.9 1.2 %copy-done.1 = s32[1,1,16,128,128]{4,3,2,1,0:T(8,128)S(1)} copy-done((s32[1,1,16,128,128]{4,3,2,1,0:T(8,128)S(1)}, s32[1,1,16,128,128]{4,3,2,1,0:T(8,128)}, u32[]{:S(2)}) %copy-start.1) | copy-done | bytes 1048600
  12.1 0.7 shard_map.184
  12.8 0.9 %collective-permute-done.2.refs_7_.refs_6_ = bf16[576,128]{1,0:T(8,128)(2,1)S(1)} collective-permute-done((bf16[576,128]{1,0:T(8,128)(2,1)}, bf16[576,128]{1,0:T(8,128)(2,1)S(1)}, u32[]{:S(2)}, u32[]{:S(2)}) %collective-permute-start.2) | collective-permute-done | bytes 147488 | tf_op jit(solution)/shard_map/ppermute | solution.py:20
  13.8 8.0 %collective-permute-done.1.refs_6_.refs_5_ = bf16[576,128]{1,0:T(8,128)(2,1)S(1)} collective-permute-done((bf16[576,128]{1,0:T(8,128)(2,1)}, bf16[576,128]{1,0:T(8,128)(2,1)S(1)}, u32[]{:S(2)}, u32[]{:S(2)}) %collective-permute-start.1) | collective-permute-done | bytes 147488 | tf_op jit(solution)/shard_map/ppermute | solution.py:20
  21.8 0.6 copy-done.13
  22.4 0.0 copy-done.14
  22.4 0.0 copy-done.15
  22.4 6.1 %shard_map.186 = (bf16[512,128]{1,0:T(8,128)(2,1)S(1)}, bf16[512,128]{1,0:T(8,128)(2,1)S(1)}, bf16[512,128]{1,0:T(8,128)(2,1)S(1)}, bf16[512,128]{1,0:T(8,128)(2...) custom-call(s32[1,1]{1,0:T(1,128)S(6)} %copy.20.tile_count, s32[1,1,16]{2,1,0:T(1,128)S(1)} %copy-done.14, ...), custom_call_target="tpu_custom_call" | custom-call | flops 2147483648 | bytes 3543680 | tf_op jit(solution)/shard_map/pallas_call | solution.py:42
  28.6 0.0 copy-start.16
  28.6 0.1 collective-permute-start.5
  28.7 2.6 %collective-permute-start.6 = (bf16[512,128]{1,0:T(8,128)(2,1)S(1)}, bf16[512,128]{1,0:T(8,128)(2,1)S(1)}, u32[]{:S(2)}, u32[]{:S(2)}) collective-permute-start(bf16[512,128]{1,0:T(8,128)(2,1)S(1)} %get-tuple-element.44), channel_id=1, source_target_pairs={{0,28},{4,0},{8,4},{12,8},{16,12},{20,16},{24,20},{28,24},{1,29},{... | collective-permute-start | bytes 393224 | tf_op jit(solution)/shard_map/ppermute | solution.py:20
  31.3 0.0 copy-start.5
  31.3 4.1 %shard_map.187 = (f32[512,128]{1,0:T(8,128)S(1)}, f32[512,128]{1,0:T(8,128)S(1)}) custom-call(s32[1,1]{1,0:T(1,128)S(6)} %copy.20.tile_count, s32[1,1,16]{2,1,0:T(1,128)S(1)} %copy-done.14, s32[1,1,16]{2,1,0:T(1,128)S(1)} %copy-done.15, s32[2,24,128]{2,1,0:T(8,128)S(1)} %get-tuple-element.35.most_far, bf16[17,128,128]{2,1,0:T(8,128)(2,1)S(1)} %get-tuple-element.36.row_rank, ...), custom_call_target="tpu_custom_call" | custom-call | flops 1073741824 | bytes 2580608 | tf_op jit(solution)/shard_map/pallas_call | solution.py:42
  35.5 0.0 copy-start.9
  35.6 0.6 copy-done.9
  36.2 0.0 copy-done.10
  36.2 1.8 %shard_map.188 = (bf16[512,128]{1,0:T(8,128)(2,1)}, bf16[1024,128]{1,0:T(8,128)(2,1)S(1)}, bf16[1024,128]{1,0:T(8,128)(2,1)S(1)}, bf16[512,128]{1,0:T(8,128)(2,1...) custom-call(f32[1,128]{1,0:T(1,128)S(1)} %bitcast.5, ...), custom_call_target="tpu_custom_call" | custom-call | flops 117440512 | bytes 2622464 | tf_op jit(solution)/shard_map/pallas_call | solution.py:42
  38.0 0.4 shard_map.193
  38.4 0.1 collective-permute-start.12
  38.5 0.0 copy-start.17
  38.5 0.4 collective-permute-start.7
  38.9 2.3 %collective-permute-start.8 = (bf16[1024,128]{1,0:T(8,128)(2,1)S(1)}, bf16[1024,128]{1,0:T(8,128)(2,1)S(1)}, u32[]{:S(2)}, u32[]{:S(2)}) collective-permute-start(bf16[1024,128]{1,0:T(8,128)(2,1)S(1)} %get-tuple-element.50.refs_0_), channel_id=1, source_target_pairs={{0,28},{4,0},{8,4},{12,8},{16,12},{20,16},{24,20},{28,24},{1,29},{... | collective-permute-start | bytes 786440 | tf_op jit(solution)/shard_map/ppermute | solution.py:20
  41.2 1.6 %collective-permute-done.12 = bf16[256,128]{1,0:T(8,128)(2,1)S(1)} collective-permute-done((bf16[256,128]{1,0:T(8,128)(2,1)S(1)}, bf16[256,128]{1,0:T(8,128)(2,1)S(1)}, u32[]{:S(2)}, u32[]{:S(2)}) %collective-permute-start.12) | collective-permute-done | bytes 65568 | tf_op jit(solution)/shard_map/ppermute | solution.py:479
  42.8 2.7 %collective-permute-start.13 = (bf16[128,128]{1,0:T(8,128)(2,1)S(1)}, bf16[128,128]{1,0:T(8,128)(2,1)S(1)}, u32[]{:S(2)}, u32[]{:S(2)}) collective-permute-start(bf16[128,128]{1,0:T(8,128)(2,1)S(1)} %select_convert_fusion), channel_id=1, source_target_pairs={{0,2},{1,3},{2,0},{3,1},{4,6},{5,7},{6,4},{7,5},{8,10},{9,11},{10,... | collective-permute-start | bytes 98312 | tf_op jit(solution)/shard_map/ppermute | solution.py:479
  45.6 3.7 %shard_map.190.refs_2_ = f32[16,128,128]{2,1,0:T(8,128)S(1)} custom-call(s32[1,1]{1,0:T(1,128)S(6)} %copy.20.tile_count, s32[1,1,16]{2,1,0:T(1,128)S(1)} %copy-done.14, s32[1,1,16]{2,1,0:T(1,128)S(1)} %copy-done.15, s32[2,24,128]{2,1,0:T(8,128)S(1)} %get-tuple-element.35.most_far, bf16[17,128,128]{2,1,0:T(8,128)(2,1)S(1)} %get-tuple-element.54.col_rank, ...), custom_call_target="tpu_custom_call" | custom-call | flops 1073741824 | bytes 2809984 | tf_op jit(solution)/shard_map/pallas_call | solution.py:42
  49.3 0.4 shard_map.189
  49.7 6.2 %shard_map.191 = (f32[512,128]{1,0:T(8,128)S(1)}, bf16[512,128]{1,0:T(8,128)(2,1)S(1)}, bf16[512,128]{1,0:T(8,128)(2,1)S(1)}, bf16[512,128]{1,0:T(8,128)(2,1)S(1)}, bf16[128,128]{1,0:T(8,128)(2,1)S(1)}) custom-call(s32[1,1]{1,0:T(1,128)S(6)} %copy.20.tile_count, s32[1,1,16]{2,1,0:T(1,128)S(1)} %copy-done.14, s32[1,1,16]{2,1,0:T(1,128)S(1)} %copy-done.15, ...), custom_call_target="tpu_custom_call" | custom-call | flops 2147483648 | bytes 4350080 | tf_op jit(solution)/shard_map/pallas_call | solution.py:42
  55.9 0.1 collective-permute-start.14
  56.0 1.3 %collective-permute-done.14 = bf16[384,128]{1,0:T(8,128)(2,1)S(1)} collective-permute-done((bf16[384,128]{1,0:T(8,128)(2,1)S(1)}, bf16[384,128]{1,0:T(8,128)(2,1)S(1)}, u32[]{:S(2)}, u32[]{:S(2)}) %collective-permute-start.14) | collective-permute-done | bytes 98336 | tf_op jit(solution)/shard_map/ppermute | solution.py:479
  57.3 0.1 collective-permute-start.15
  57.4 4.8 %collective-permute-done.15 = bf16[384,128]{1,0:T(8,128)(2,1)S(1)} collective-permute-done((bf16[384,128]{1,0:T(8,128)(2,1)S(1)}, bf16[384,128]{1,0:T(8,128)(2,1)S(1)}, u32[]{:S(2)}, u32[]{:S(2)}) %collective-permute-start.15) | collective-permute-done | bytes 98336 | tf_op jit(solution)/shard_map/ppermute | solution.py:479
  62.3 0.1 collective-permute-start.16
  62.3 4.6 %collective-permute-done.16 = bf16[384,128]{1,0:T(8,128)(2,1)S(1)} collective-permute-done((bf16[384,128]{1,0:T(8,128)(2,1)S(1)}, bf16[384,128]{1,0:T(8,128)(2,1)S(1)}, u32[]{:S(2)}, u32[]{:S(2)}) %collective-permute-start.16) | collective-permute-done | bytes 98336 | tf_op jit(solution)/shard_map/ppermute | solution.py:479
  67.0 1.6 %collective-permute-start.17 = (bf16[384,128]{1,0:T(8,128)(2,1)S(1)}, bf16[384,128]{1,0:T(8,128)(2,1)S(1)}, u32[]{:S(2)}, u32[]{:S(2)}) collective-permute-start(bf16[384,128]{1,0:T(8,128)(2,1)S(1)} %add_convert_fusion), channel_id=1, source_target_pairs={{0,2},{1,3},{2,0},{3,1},{4,6},{5,7},{6,4},{7,5},{8,10},{9,11},{10,... | collective-permute-start | bytes 294920 | tf_op jit(solution)/shard_map/ppermute | solution.py:479
  68.6 0.6 collective-permute-start.9
  69.3 2.0 %collective-permute-start.10 = (bf16[512,128]{1,0:T(8,128)(2,1)S(1)}, bf16[512,128]{1,0:T(8,128)(2,1)S(1)}, u32[]{:S(2)}, u32[]{:S(2)}) collective-permute-start(bf16[512,128]{1,0:T(8,128)(2,1)S(1)} %get-tuple-element.57), channel_id=1, source_target_pairs={{0,2},{1,3},{2,0},{3,1},{4,6},{5,7},{6,4},{7,5},{8,10},{9,11},{10,... | collective-permute-start | bytes 393224 | tf_op jit(solution)/shard_map/ppermute | solution.py:20
  71.2 0.8 collective-permute-start.11
  72.0 8.1 %collective-permute-done.17 = bf16[384,128]{1,0:T(8,128)(2,1)S(1)} collective-permute-done((bf16[384,128]{1,0:T(8,128)(2,1)S(1)}, bf16[384,128]{1,0:T(8,128)(2,1)S(1)}, u32[]{:S(2)}, u32[]{:S(2)}) %collective-permute-start.17) | collective-permute-done | bytes 98336 | tf_op jit(solution)/shard_map/ppermute | solution.py:479
  80.1 0.1 collective-permute-start.18
  80.2 3.6 %collective-permute-done.10.refs_1_ = bf16[512,128]{1,0:T(8,128)(2,1)S(1)} collective-permute-done((bf16[512,128]{1,0:T(8,128)(2,1)S(1)}, bf16[512,128]{1,0:T(8,128)(2,1)S(1)}, u32[]{:S(2)}, u32[]{:S(2)}) %collective-permute-start.10) | collective-permute-done | bytes 131104 | tf_op jit(solution)/shard_map/ppermute | solution.py:20
  83.8 0.9 %shard_map.192 = f32[512,128]{1,0:T(8,128)} custom-call(f32[512,128]{1,0:T(8,128)S(1)} %get-tuple-element.53.direct, bf16[128,128]{1,0:T(8,128)(2,1)S(1)} %copy-done.8, f32[512,128]{1,0:T(8,128)S(1)} %get-tuple-element.55.own, bf16[512,128]{1,0:T(8,128)(2,1)S(1)} %collective-permute-done.9.refs_0_, bf16[512,128]{1,0:T(8,128)(2,1)S(1)} %collective-permute-done.10.refs_1_, ...), custom_call_target="tpu_custom_call" | custom-call | flops 16777216 | bytes 1212416 | tf_op jit(solution)/shard_map/pallas_call | solution.py:42
  84.7 0.5 collective-permute-done.18.other
  85.2 0.8 shard_map.194
  (47 shorter events, 0.3 us)
Async XLA Ops:
  2.2 10.6 %collective-permute-start.4 = (bf16[576,128]{1,0:T(8,128)(2,1)}, bf16[576,128]{1,0:T(8,128)(2,1)S(1)}, u32[]{:S(2)}, u32[]{:S(2)}) collective-permute-start(bf16[576,128]{1,0:T(8,128)(2,1)} %get-tuple-element.39.refs_4_.refs_3_), channel_id=1, source_target_pairs={{0,28},{4,0},{8,4},{12,8},{16,12},{20,16},{24,20},{28,24},{1,29},{... | collective-permute-start | bytes 442376 | tf_op jit(solution)/shard_map/ppermute | solution.py:20
  5.6 7.3 %collective-permute-start.3 = (bf16[576,128]{1,0:T(8,128)(2,1)}, bf16[576,128]{1,0:T(8,128)(2,1)S(1)}, u32[]{:S(2)}, u32[]{:S(2)}) collective-permute-start(bf16[576,128]{1,0:T(8,128)(2,1)} %get-tuple-element.39.refs_4_.refs_3_), channel_id=1, source_target_pairs={{0,4},{4,8},{8,12},{12,16},{16,20},{20,24},{24,28},{28,0},{1,5},{5... | collective-permute-start | bytes 442376 | tf_op jit(solution)/shard_map/ppermute | solution.py:20
  5.6 8.2 %collective-permute-start.2 = (bf16[576,128]{1,0:T(8,128)(2,1)}, bf16[576,128]{1,0:T(8,128)(2,1)S(1)}, u32[]{:S(2)}, u32[]{:S(2)}) collective-permute-start(bf16[576,128]{1,0:T(8,128)(2,1)} %get-tuple-element.39.refs_4_.refs_3_), channel_id=1, source_target_pairs={{0,3},{1,0},{2,1},{3,2},{4,7},{5,4},{6,5},{7,6},{8,11},{9,8},{10,9... | collective-permute-start | bytes 442376 | tf_op jit(solution)/shard_map/ppermute | solution.py:20
  9.2 12.6 %collective-permute-start.1 = (bf16[576,128]{1,0:T(8,128)(2,1)}, bf16[576,128]{1,0:T(8,128)(2,1)S(1)}, u32[]{:S(2)}, u32[]{:S(2)}) collective-permute-start(bf16[576,128]{1,0:T(8,128)(2,1)} %get-tuple-element.39.refs_4_.refs_3_), channel_id=1, source_target_pairs={{0,2},{1,3},{2,0},{3,1},{4,6},{5,7},{6,4},{7,5},{8,10},{9,11},{10,... | collective-permute-start | bytes 442376 | tf_op jit(solution)/shard_map/ppermute | solution.py:20
  9.2 12.6 %collective-permute-start = (bf16[576,128]{1,0:T(8,128)(2,1)}, bf16[576,128]{1,0:T(8,128)(2,1)S(1)}, u32[]{:S(2)}, u32[]{:S(2)}) collective-permute-start(bf16[576,128]{1,0:T(8,128)(2,1)} %get-tuple-element.39.refs_4_.refs_3_), channel_id=1, source_target_pairs={{0,1},{1,2},{2,3},{3,0},{4,5},{5,6},{6,7},{7,4},{8,9},{9,10},{10,1... | collective-permute-start | bytes 442376 | tf_op jit(solution)/shard_map/ppermute | solution.py:20
  10.8 1.2 %copy-start.1 = (s32[1,1,16,128,128]{4,3,2,1,0:T(8,128)S(1)}, s32[1,1,16,128,128]{4,3,2,1,0:T(8,128)}, u32[]{:S(2)}) copy-start(s32[1,1,16,128,128]{4,3,2,1,0:T(8,128)} %param.21) | copy-start | bytes 3145732
  12.1 9.7 %copy-start.7 = (bf16[128,128]{1,0:T(8,128)(2,1)S(1)}, bf16[128,128]{1,0:T(8,128)(2,1)}, u32[]{:S(2)}) copy-start(bf16[128,128]{1,0:T(8,128)(2,1)} %w_recv.1) | copy-start | bytes 98308
  12.1 9.7 %copy-start.8 = (bf16[128,128]{1,0:T(8,128)(2,1)S(1)}, bf16[128,128]{1,0:T(8,128)(2,1)}, u32[]{:S(2)}) copy-start(bf16[128,128]{1,0:T(8,128)(2,1)} %w_send.1) | copy-start | bytes 98308
  12.1 9.7 %copy-start.11 = (bf16[576,128]{1,0:T(8,128)(2,1)S(1)}, bf16[576,128]{1,0:T(8,128)(2,1)}, u32[]{:S(2)}) copy-start(bf16[576,128]{1,0:T(8,128)(2,1)} %get-tuple-element.39.refs_4_.refs_3_) | copy-start | bytes 442372
  12.1 9.7 %copy-start.12 = (bf16[16,384]{1,0:T(8,128)(2,1)S(1)}, bf16[16,384]{1,0:T(8,128)(2,1)}, u32[]{:S(2)}) copy-start(bf16[16,384]{1,0:T(8,128)(2,1)} %get-tuple-element.38.refs_2_) | copy-start | bytes 36868
  21.8 0.7 copy-start.13
  21.8 0.7 copy-start.14
  21.8 0.7 copy-start.15
  28.6 6.9 %copy-start.16 = (bf16[12,128,128]{2,1,0:T(8,128)(2,1)}, bf16[12,128,128]{2,1,0:T(8,128)(2,1)S(1)}, u32[]{:S(2)}) copy-start(bf16[12,128,128]{2,1,0:T(8,128)(2,1)S(1)} %get-tuple-element.41.refs_1_.receivers) | copy-start | bytes 1179652
  28.6 6.9 %collective-permute-start.5 = (bf16[512,128]{1,0:T(8,128)(2,1)S(1)}, bf16[512,128]{1,0:T(8,128)(2,1)S(1)}, u32[]{:S(2)}, u32[]{:S(2)}) collective-permute-start(bf16[512,128]{1,0:T(8,128)(2,1)S(1)} %get-tuple-element.43), channel_id=1, source_target_pairs={{0,4},{4,8},{8,12},{12,16},{16,20},{20,24},{24,28},{28,0},{1,5},{5... | collective-permute-start | bytes 393224 | tf_op jit(solution)/shard_map/ppermute | solution.py:20
  28.7 6.8 %collective-permute-start.6 = (bf16[512,128]{1,0:T(8,128)(2,1)S(1)}, bf16[512,128]{1,0:T(8,128)(2,1)S(1)}, u32[]{:S(2)}, u32[]{:S(2)}) collective-permute-start(bf16[512,128]{1,0:T(8,128)(2,1)S(1)} %get-tuple-element.44), channel_id=1, source_target_pairs={{0,28},{4,0},{8,4},{12,8},{16,12},{20,16},{24,20},{28,24},{1,29},{... | collective-permute-start | bytes 393224 | tf_op jit(solution)/shard_map/ppermute | solution.py:20
  31.3 4.2 %copy-start = (bf16[512,128]{1,0:T(8,128)(2,1)S(1)}, bf16[512,128]{1,0:T(8,128)(2,1)}, u32[]{:S(2)}) copy-start(bf16[512,128]{1,0:T(8,128)(2,1)} %latent.7) | copy-start | bytes 393220
  31.3 4.3 %copy-start.2 = (bf16[512,128]{1,0:T(8,128)(2,1)S(1)}, bf16[512,128]{1,0:T(8,128)(2,1)}, u32[]{:S(2)}) copy-start(bf16[512,128]{1,0:T(8,128)(2,1)} %cotangent.3) | copy-start | bytes 393220
  31.3 4.3 %copy-start.3 = (bf16[128,128]{1,0:T(8,128)(2,1)S(1)}, bf16[128,128]{1,0:T(8,128)(2,1)}, u32[]{:S(2)}) copy-start(bf16[128,128]{1,0:T(8,128)(2,1)} %w_edge_out.3) | copy-start | bytes 98308
  31.3 4.3 %copy-start.4 = (bf16[128,128]{1,0:T(8,128)(2,1)S(1)}, bf16[128,128]{1,0:T(8,128)(2,1)}, u32[]{:S(2)}) copy-start(bf16[128,128]{1,0:T(8,128)(2,1)} %w_node_self.3) | copy-start | bytes 98308
  31.3 4.3 %copy-start.5 = (bf16[128,128]{1,0:T(8,128)(2,1)S(1)}, bf16[128,128]{1,0:T(8,128)(2,1)}, u32[]{:S(2)}) copy-start(bf16[128,128]{1,0:T(8,128)(2,1)} %w_node_msg.1) | copy-start | bytes 98308
  31.3 4.3 %copy-start.6 = (bf16[128,128]{1,0:T(8,128)(2,1)S(1)}, bf16[128,128]{1,0:T(8,128)(2,1)}, u32[]{:S(2)}) copy-start(bf16[128,128]{1,0:T(8,128)(2,1)} %w_node_out.1) | copy-start | bytes 98308
  35.5 0.7 copy-start.9
  35.5 0.7 copy-start.10
  38.4 4.4 %collective-permute-start.12 = (bf16[256,128]{1,0:T(8,128)(2,1)S(1)}, bf16[256,128]{1,0:T(8,128)(2,1)S(1)}, u32[]{:S(2)}, u32[]{:S(2)}) collective-permute-start(bf16[256,128]{1,0:T(8,128)(2,1)S(1)} %get-tuple-element.64), channel_id=1, source_target_pairs={{0,1},{1,0},{2,3},{3,2},{4,5},{5,4},{6,7},{7,6},{8,9},{9,8},{10,11... | collective-permute-start | bytes 196616 | tf_op jit(solution)/shard_map/ppermute | solution.py:479
  38.5 7.1 %copy-start.17 = (bf16[12,128,128]{2,1,0:T(8,128)(2,1)S(1)}, bf16[12,128,128]{2,1,0:T(8,128)(2,1)}, u32[]{:S(2)}) copy-start(bf16[12,128,128]{2,1,0:T(8,128)(2,1)} %copy-done.16) | copy-start | bytes 1179652
  38.5 10.8 %collective-permute-start.7 = (bf16[1024,128]{1,0:T(8,128)(2,1)S(1)}, bf16[1024,128]{1,0:T(8,128)(2,1)S(1)}, u32[]{:S(2)}, u32[]{:S(2)}) collective-permute-start(bf16[1024,128]{1,0:T(8,128)(2,1)S(1)} %get-tuple-element.49), channel_id=1, source_target_pairs={{0,4},{4,8},{8,12},{12,16},{16,20},{20,24},{24,28},{28,0},{1,5},{5... | collective-permute-start | bytes 786440 | tf_op jit(solution)/shard_map/ppermute | solution.py:20
  38.9 10.5 %collective-permute-start.8 = (bf16[1024,128]{1,0:T(8,128)(2,1)S(1)}, bf16[1024,128]{1,0:T(8,128)(2,1)S(1)}, u32[]{:S(2)}, u32[]{:S(2)}) collective-permute-start(bf16[1024,128]{1,0:T(8,128)(2,1)S(1)} %get-tuple-element.50.refs_0_), channel_id=1, source_target_pairs={{0,28},{4,0},{8,4},{12,8},{16,12},{20,16},{24,20},{28,24},{1,29},{... | collective-permute-start | bytes 786440 | tf_op jit(solution)/shard_map/ppermute | solution.py:20
  42.8 6.5 %collective-permute-start.13 = (bf16[128,128]{1,0:T(8,128)(2,1)S(1)}, bf16[128,128]{1,0:T(8,128)(2,1)S(1)}, u32[]{:S(2)}, u32[]{:S(2)}) collective-permute-start(bf16[128,128]{1,0:T(8,128)(2,1)S(1)} %select_convert_fusion), channel_id=1, source_target_pairs={{0,2},{1,3},{2,0},{3,1},{4,6},{5,7},{6,4},{7,5},{8,10},{9,11},{10,... | collective-permute-start | bytes 98312 | tf_op jit(solution)/shard_map/ppermute | solution.py:479
  55.9 1.4 %collective-permute-start.14 = (bf16[384,128]{1,0:T(8,128)(2,1)S(1)}, bf16[384,128]{1,0:T(8,128)(2,1)S(1)}, u32[]{:S(2)}, u32[]{:S(2)}) collective-permute-start(bf16[384,128]{1,0:T(8,128)(2,1)S(1)} %pad_maximum_fusion.1), channel_id=1, source_target_pairs={{0,4},{4,0},{8,12},{12,8},{16,20},{20,16},{24,28},{28,24},{1,5},{5... | collective-permute-start | bytes 294920 | tf_op jit(solution)/shard_map/ppermute | solution.py:479
  57.3 4.9 %collective-permute-start.15 = (bf16[384,128]{1,0:T(8,128)(2,1)S(1)}, bf16[384,128]{1,0:T(8,128)(2,1)S(1)}, u32[]{:S(2)}, u32[]{:S(2)}) collective-permute-start(bf16[384,128]{1,0:T(8,128)(2,1)S(1)} %add_convert_fusion.2), channel_id=1, source_target_pairs={{0,8},{4,12},{8,0},{12,4},{16,24},{20,28},{24,16},{28,20},{1,9},{5... | collective-permute-start | bytes 294920 | tf_op jit(solution)/shard_map/ppermute | solution.py:479
  62.3 4.7 %collective-permute-start.16 = (bf16[384,128]{1,0:T(8,128)(2,1)S(1)}, bf16[384,128]{1,0:T(8,128)(2,1)S(1)}, u32[]{:S(2)}, u32[]{:S(2)}) collective-permute-start(bf16[384,128]{1,0:T(8,128)(2,1)S(1)} %add_convert_fusion.1), channel_id=1, source_target_pairs={{0,16},{4,20},{8,24},{12,28},{16,0},{20,4},{24,8},{28,12},{1,17},{... | collective-permute-start | bytes 294920 | tf_op jit(solution)/shard_map/ppermute | solution.py:479
  67.0 13.1 %collective-permute-start.17 = (bf16[384,128]{1,0:T(8,128)(2,1)S(1)}, bf16[384,128]{1,0:T(8,128)(2,1)S(1)}, u32[]{:S(2)}, u32[]{:S(2)}) collective-permute-start(bf16[384,128]{1,0:T(8,128)(2,1)S(1)} %add_convert_fusion), channel_id=1, source_target_pairs={{0,2},{1,3},{2,0},{3,1},{4,6},{5,7},{6,4},{7,5},{8,10},{9,11},{10,... | collective-permute-start | bytes 294920 | tf_op jit(solution)/shard_map/ppermute | solution.py:479
  68.6 11.6 %collective-permute-start.9 = (bf16[512,128]{1,0:T(8,128)(2,1)S(1)}, bf16[512,128]{1,0:T(8,128)(2,1)S(1)}, u32[]{:S(2)}, u32[]{:S(2)}) collective-permute-start(bf16[512,128]{1,0:T(8,128)(2,1)S(1)} %get-tuple-element.56), channel_id=1, source_target_pairs={{0,3},{1,0},{2,1},{3,2},{4,7},{5,4},{6,5},{7,6},{8,11},{9,8},{10,9... | collective-permute-start | bytes 393224 | tf_op jit(solution)/shard_map/ppermute | solution.py:20
  69.3 14.5 %collective-permute-start.10 = (bf16[512,128]{1,0:T(8,128)(2,1)S(1)}, bf16[512,128]{1,0:T(8,128)(2,1)S(1)}, u32[]{:S(2)}, u32[]{:S(2)}) collective-permute-start(bf16[512,128]{1,0:T(8,128)(2,1)S(1)} %get-tuple-element.57), channel_id=1, source_target_pairs={{0,2},{1,3},{2,0},{3,1},{4,6},{5,7},{6,4},{7,5},{8,10},{9,11},{10,... | collective-permute-start | bytes 393224 | tf_op jit(solution)/shard_map/ppermute | solution.py:20
  71.2 12.5 %collective-permute-start.11 = (bf16[512,128]{1,0:T(8,128)(2,1)S(1)}, bf16[512,128]{1,0:T(8,128)(2,1)S(1)}, u32[]{:S(2)}, u32[]{:S(2)}) collective-permute-start(bf16[512,128]{1,0:T(8,128)(2,1)S(1)} %get-tuple-element.58), channel_id=1, source_target_pairs={{0,1},{1,2},{2,3},{3,0},{4,5},{5,6},{6,7},{7,4},{8,9},{9,10},{10,1... | collective-permute-start | bytes 393224 | tf_op jit(solution)/shard_map/ppermute | solution.py:20
  80.1 5.1 %collective-permute-start.18 = (bf16[512,128]{1,0:T(8,128)(2,1)S(1)}, bf16[512,128]{1,0:T(8,128)(2,1)S(1)}, u32[]{:S(2)}, u32[]{:S(2)}) collective-permute-start(bf16[512,128]{1,0:T(8,128)(2,1)S(1)} %pad_maximum_fusion.mine), channel_id=1, source_target_pairs={{0,1},{1,0},{2,3},{3,2},{4,5},{5,4},{6,7},{7,6},{8,9},{9,8},{10,11... | collective-permute-start | bytes 393224 | tf_op jit(solution)/shard_map/ppermute | solution.py:479

commit v5 on v4

--- a/solution.py
+++ b/solution.py
@@ -7,8 +7,11 @@
 
 F32 = jnp.float32
 BF16 = jnp.bfloat16
-GROUPS = (8, 8)
+FORWARD = (4, 4, 4, 4)
+BACKWARD = (2, 2, 2, 2, 2, 2, 2, 2)
 LOOPED = 4
+ROWS, COLUMNS, TABLES = 0, 1, 2
+SENDERS, RECEIVERS = 0, 1
 TOGETHER = 4
 CHUNK = 32
 PARTS = 16
@@ -81,7 +84,20 @@
         weight_parts[:, item * width : (item + 1) * width] = stacked.astype(BF16)
 
 
-def ranks_kernel(tile_count, mask, row_rank, row_degree, col_rank, most):
+def ranks_kernel(
+    tile_count,
+    mask,
+    tile_send,
+    tile_recv,
+    edge_bias,
+    node_bias,
+    gain,
+    row_rank,
+    row_degree,
+    col_rank,
+    most,
+    vectors,
+):
     tiles, size = mask.shape[0], mask.shape[-1]
     row_index = lax.broadcasted_iota(jnp.int32, (size, size), 0)
     col_index = lax.broadcasted_iota(jnp.int32, (size, size), 1)
@@ -91,6 +107,11 @@
     for_rows = jnp.concatenate([upper, ones], 1)
     for_cols = jnp.concatenate([upper, eye], 1)
     most[...] = jnp.zeros_like(most)
+    most[2, SENDERS : SENDERS + 1, 0:tiles] = tile_send[0]
+    most[2, RECEIVERS : RECEIVERS + 1, 0:tiles] = tile_recv[0]
+    vectors[...] = jnp.zeros_like(vectors)
+    for place, vector in enumerate((edge_bias, node_bias, gain)):
+        vectors[place : place + 1, :] = vector[...]
     for table in (row_rank, row_degree, col_rank):
         table[tiles] = jnp.zeros((size, size), BF16)
     for start in range(0, tiles, TOGETHER):
@@ -114,24 +135,35 @@
             most[1, tile : tile + 1, :] = jnp.max(ranks, axis=0, keepdims=True).astype(jnp.int32)
 
 
-def list_tiles(order, tile_recv, tile_count, blocks, own):
-    tiles = tile_recv.shape[-1]
+def list_tiles(order, table, tile_count, tiles, wanted):
     found = jnp.int32(0)
     for tile in range(tiles):
-        mine = (tile_recv[0, 0, tile] // blocks == 1) == own
+        match = wanted(table[SENDERS, tile], table[RECEIVERS, tile]) & (tile < tile_count[0, 0])
         order[found] = tile
-        found = found + (mine & (tile < tile_count[0, 0])).astype(jnp.int32)
+        found = found + match.astype(jnp.int32)
     order[found] = tiles
     return (found + 1) // 2
 
 
-def pair_of(pair, order, tile_send, tile_recv, member, members, blocks):
-    last = tile_recv.shape[-1] - 1
-    tiles = [order[2 * pair], order[2 * pair + 1]]
-    named = [tiles[0], jnp.where(tiles[1] > last, tiles[0], tiles[1])]
-    recv_places = [tile_recv[0, 0, tile] for tile in named]
-    send_places = [sender_place(tile_send[0, 0, tile], member, members, blocks) for tile in named]
-    return tiles, recv_places, send_places
+def pair_of(pair, order, table, tiles, member, members, blocks):
+    pair_tiles = [order[2 * pair], order[2 * pair + 1]]
+    named = [pair_tiles[0], jnp.where(pair_tiles[1] == tiles, pair_tiles[0], pair_tiles[1])]
+    recv_places = [table[RECEIVERS, tile] for tile in named]
+    send_places = [
+        sender_place(table[SENDERS, tile], member, members, blocks) for tile in named
+    ]
+    return pair_tiles, recv_places, send_places
+
+
+def start_tables(most, part, extremes, table, sem):
+    sources = (most.at[part], most.at[TABLES, 0 : table.shape[0]])
+    copies = [
+        pltpu.make_async_copy(source, target, sem.at[item])
+        for item, (source, target) in enumerate(zip(sources, (extremes, table)))
+    ]
+    for copy in copies:
+        copy.start()
+    return copies
 
 
 def one_hots(rank_block, first, ranks):
@@ -143,9 +175,9 @@
     return found
 
 
-def run_groups(one_group, most):
+def run_groups(groups, one_group, most):
     first = 0
-    for place, ranks in enumerate(GROUPS):
+    for place, ranks in enumerate(groups):
         one_group(first, ranks, place == 0)
         first += ranks
     steps = jnp.maximum((most - first + LOOPED - 1) // LOOPED, 0)
@@ -178,123 +210,173 @@
     return distance * blocks + lax.rem(block, blocks)
 
 
-def start_copies(sources, targets, sem):
-    copies = [
-        pltpu.make_async_copy(source, target, sem.at[item])
-        for item, (source, target) in enumerate(zip(sources, targets))
-    ]
-    for copy in copies:
-        copy.start()
-    return copies
-
-
-def make_rows(members, blocks, size, width):
-    rows = blocks * size
-
-    def placed_of(message, weight_parts):
-        found = []
-        for block in range(blocks):
-            start = rows + block * PARTS
-            parts = contract_rows(message[start : start + PARTS, :], weight_parts[...])
-            found.append(parts[:, :width] + parts[:, width : 2 * width] + parts[:, 2 * width :])
-        return jnp.concatenate(found, 0)
-
-    def lay(table, place, found):
-        for block in range(blocks):
-            span = slice(block * size, (block + 1) * size)
-            table[place * blocks + block] = found[span, :].astype(BF16)
-
-    def lay_rows(messages, sides, w_send, w_recv, weight_parts, edge_bias, senders, receivers):
-        for distance, message in enumerate(messages):
-            placed = placed_of(message, weight_parts)
-            lay(senders, distance, dot(message[0:rows, :], w_send[...]) + placed)
-            if distance == 0:
-                lay(receivers, 1, dot(message[0:rows, :], w_recv[...]) - placed + edge_bias[...])
-        for place, message in ((0, sides[0]), (2, sides[1])):
-            placed = placed_of(message, weight_parts)
-            lay(receivers, place, dot(message[0:rows, :], w_recv[...]) - placed + edge_bias[...])
-
-    return lay_rows
-
-
-def make_forward(members, blocks, own):
-    def kernel(tile_count, send_far, recv_far, most_far, row_rank, row_degree, *refs):
-        if own:
-            senders, receivers, sums_out, counts_out, refs = *refs[:4], refs[4:]
-            sides = ((1, sums_out, counts_out),)
-        else:
-            weights, refs = refs[:4], refs[4:]
-            messages, refs = refs[:members], refs[members:]
-            beside, refs = refs[:2], refs[2:]
-            sides = ((0, refs[0], refs[2]), (2, refs[1], refs[3]))
-            senders, receivers, refs = refs[4], refs[5], refs[6:]
-        sums, counts, total, count, tile_send, tile_recv, row_most, order, sem = refs
-        size, width = senders.shape[1:]
-        copies = start_copies(
-            (send_far, recv_far, most_far.at[0]), (tile_send, tile_recv, row_most), sem
+def placed_of(message, weight_parts, blocks):
+    width = message.shape[1]
+    rows = message.shape[0] - blocks * PARTS
+    found = []
+    for block in range(blocks):
+        start = rows + block * PARTS
+        parts = contract_rows(message[start : start + PARTS, :], weight_parts[...])
+        found.append(parts[:, :width] + parts[:, width : 2 * width] + parts[:, 2 * width :])
+    return jnp.concatenate(found, 0)
+
+
+def lay(table, start, found):
+    size = table.shape[1]
+    for block in range(found.shape[0] // size):
+        table[start + block] = found[block * size : (block + 1) * size, :].astype(BF16)
+
+
+def forward_tiles(member, members, tables, ranks_in, rows_in, sums, counts, wanted):
+    tile_count, row_most, table, order, total, count = tables
+    row_rank, row_degree = ranks_in
+    senders, receivers = rows_in
+    size, width = senders.shape[1:]
+    blocks = receivers.shape[0] // 3
+    tiles = row_rank.shape[0] - 1
+
+    def one_pair(pair, carry):
+        pair_tiles, recv_places, send_places = pair_of(
+            pair, order, table, tiles, member, members, blocks
         )
-        member = lax.axis_index("grp")
+        nothing = jnp.zeros((size, width), BF16)
+        upper = jnp.concatenate([senders[send_places[0]], nothing], 1)
+        lower = jnp.concatenate([nothing, senders[send_places[1]]], 1)
+        right = jnp.concatenate([upper, lower], 0)
+        recv_rows = jnp.concatenate([receivers[place] for place in recv_places], 1).astype(F32)
+        ranks_of = [row_rank[tile] for tile in pair_tiles]
+
+        def one_group(first, ranks, fresh):
+            hots = [one_hots(rank_block, first, ranks) for rank_block in ranks_of]
+            left = jnp.concatenate([jnp.concatenate(two, 1) for two in zip(*hots)], 0)
+            found = dot(left, right)
+            for chunk in range(0, size, CHUNK):
+                span = slice(chunk, chunk + CHUNK)
+                added = jnp.zeros((CHUNK, 2 * width), F32)
+                seen = jnp.zeros((CHUNK, 2 * width), F32)
+                for item in range(ranks):
+                    start = item * size + chunk
+                    preact = found[start : start + CHUNK, :] + recv_rows[span, :]
+                    added = added + jnp.maximum(preact, 0.0)
+                    seen = seen + jnp.where(preact > 0.0, 1.0, 0.0)
+                total[span, :] = added if fresh else total[span, :] + added
+                count[span, :] = seen if fresh else count[span, :] + seen
+
+        most = jnp.maximum(row_most[pair_tiles[0], size - 1], row_most[pair_tiles[1], size - 1])
+        done = jnp.asarray(run_groups(FORWARD, one_group, most), jnp.int32).astype(F32)
+        for item, tile in enumerate(pair_tiles):
+            half = slice(item * width, (item + 1) * width)
+            spare = done - row_degree[tile].astype(F32)
+            rows_here = recv_rows[:, half]
+            place = recv_places[item]
+            sums[place] += total[:, half] - spare * jnp.maximum(rows_here, 0.0)
+            counts[place] += count[:, half] - jnp.where(rows_here > 0.0, spare, 0.0)
+        return carry
+
+    pairs = list_tiles(order, table, tile_count, tiles, wanted)
+    lax.fori_loop(0, pairs, one_pair, 0)
+
+
+def make_first(members):
+    def kernel(
+        tile_count,
+        most,
+        row_rank,
+        row_degree,
+        w_send,
+        w_recv,
+        weight_parts,
+        vectors,
+        message,
+        low,
+        high,
+        senders,
+        receivers,
+        sums,
+        counts,
+        total,
+        count,
+        row_most,
+        table,
+        order,
+        sem,
+    ):
+        copies = start_tables(most, ROWS, row_most, table, sem)
+        blocks = senders.shape[0]
+        rows = blocks * senders.shape[1]
         sums[...] = jnp.zeros_like(sums)
         counts[...] = jnp.zeros_like(counts)
-        if not own:
-            lay_rows = make_rows(members, blocks, size, width)
-            lay_rows(messages, beside, *weights, senders, receivers)
+        for side, here in enumerate((low, message, high)):
+            placed = placed_of(here, weight_parts, blocks)
+            latents = here[0:rows, :]
+            lay(receivers, side * blocks, dot(latents, w_recv[...]) - placed + vectors[0:1, :])
+            if side == 1:
+                lay(senders, 0, dot(latents, w_send[...]) + placed)
         for copy in copies:
             copy.wait()
-
-        def one_pair(pair, carry):
-            tiles, recv_places, send_places = pair_of(
-                pair, order, tile_send, tile_recv, member, members, blocks
-            )
-            nothing = jnp.zeros((size, width), BF16)
-            upper = jnp.concatenate([senders[send_places[0]], nothing], 1)
-            lower = jnp.concatenate([nothing, senders[send_places[1]]], 1)
-            right = jnp.concatenate([upper, lower], 0)
-            recv_rows = jnp.concatenate([receivers[place] for place in recv_places], 1).astype(F32)
-            ranks_of = [row_rank[tile] for tile in tiles]
-
-            def one_group(first, ranks, fresh):
-                hots = [one_hots(rank_block, first, ranks) for rank_block in ranks_of]
-                left = jnp.concatenate([jnp.concatenate(two, 1) for two in zip(*hots)], 0)
-                found = dot(left, right)
-                for chunk in range(0, size, CHUNK):
-                    span = slice(chunk, chunk + CHUNK)
-                    added = jnp.zeros((CHUNK, 2 * width), F32)
-                    seen = jnp.zeros((CHUNK, 2 * width), F32)
-                    for item in range(ranks):
-                        start = item * size + chunk
-                        preact = found[start : start + CHUNK, :] + recv_rows[span, :]
-                        added = added + jnp.maximum(preact, 0.0)
-                        seen = seen + jnp.where(preact > 0.0, 1.0, 0.0)
-                    total[span, :] = added if fresh else total[span, :] + added
-                    count[span, :] = seen if fresh else count[span, :] + seen
-
-            most = jnp.maximum(row_most[tiles[0], size - 1], row_most[tiles[1], size - 1])
-            done = jnp.asarray(run_groups(one_group, most), jnp.int32).astype(F32)
-            for item, tile in enumerate(tiles):
-                half = slice(item * width, (item + 1) * width)
-                spare = done - row_degree[tile].astype(F32)
-                rows_here = recv_rows[:, half]
-                place = recv_places[item]
-                sums[place] += total[:, half] - spare * jnp.maximum(rows_here, 0.0)
-                counts[place] += count[:, half] - jnp.where(rows_here > 0.0, spare, 0.0)
-            return carry
-
-        pairs = list_tiles(order, tile_recv, tile_count, blocks, own)
-        lax.fori_loop(0, pairs, one_pair, 0)
+        member = lax.axis_index("grp")
+        forward_tiles(
+            member,
+            members,
+            (tile_count, row_most, table, order, total, count),
+            (row_rank, row_degree),
+            (senders, receivers),
+            sums,
+            counts,
+            lambda send, recv: send // blocks == member,
+        )
+
+    return kernel
+
+
+def make_forward(members, own):
+    def kernel(tile_count, most, row_rank, row_degree, receivers, sums_in, counts_in, *refs):
+        if own:
+            senders, sum_own, count_own, refs = *refs[:3], refs[3:]
+            sides = ((1, sum_own, count_own),)
+        else:
+            own_senders, w_send, weight_parts, refs = *refs[:3], refs[3:]
+            messages, refs = refs[: members - 1], refs[members - 1 :]
+            sides = ((0, refs[0], refs[2]), (2, refs[1], refs[3]))
+            senders, refs = refs[4], refs[5:]
+        total, count, row_most, table, order, sem, sums, counts = refs
+        copies = start_tables(most, ROWS, row_most, table, sem)
+        blocks = receivers.shape[0] // 3
+        size = receivers.shape[1]
+        for side, *unused in sides:
+            span = slice(side * blocks, (side + 1) * blocks)
+            sums[span] = sums_in[span]
+            counts[span] = counts_in[span]
+        if not own:
+            senders[0:blocks] = own_senders[...]
+            for distance, message in enumerate(messages):
+                placed = placed_of(message, weight_parts, blocks)
+                rows = dot(message[0 : blocks * size, :], w_send[...]) + placed
+                lay(senders, (distance + 1) * blocks, rows)
+        for copy in copies:
+            copy.wait()
+        member = lax.axis_index("grp")
+        forward_tiles(
+            member,
+            members,
+            (tile_count, row_most, table, order, total, count),
+            (row_rank, row_degree),
+            (senders, receivers),
+            sums,
+            counts,
+            lambda send, recv: (send // blocks != member) & ((recv // blocks == 1) == own),
+        )
         for side, *outs in sides:
-            for table, out in zip((sums, counts), outs):
+            for values, out in zip((sums, counts), outs):
                 for block in range(blocks):
-                    out[block * size : (block + 1) * size, :] = table[side * blocks + block].astype(
-                        out.dtype
-                    )
+                    span = slice(block * size, (block + 1) * size)
+                    out[span, :] = values[side * blocks + block].astype(out.dtype)
 
     return kernel
 
 
 def node_kernel(
-    bias_far,
-    gain_far,
+    vectors,
     latent,
     cotangent,
     sum_own,
@@ -315,17 +397,12 @@
     d_update_out,
     d_hidden_out,
     d_message_out,
-    node_bias,
-    gain,
-    sem,
 ):
-    copies = start_copies((bias_far, gain_far), (node_bias, gain), sem)
+    node_bias, gain = vectors[1:2, :], vectors[2:3, :]
     rows = latent[...]
     aggregate = (sum_own[...] + sum_low[...].astype(F32) + sum_high[...].astype(F32)).astype(BF16)
     message = dot(aggregate, w_edge_out[...]).astype(BF16)
-    for copy in copies:
-        copy.wait()
-    hidden_pre = dot(rows, w_node_self[...]) + dot(message, w_node_msg[...]) + node_bias[...]
+    hidden_pre = dot(rows, w_node_self[...]) + dot(message, w_node_msg[...]) + node_bias
     logistic = 1.0 / (1.0 + jnp.exp(-hidden_pre))
     hidden = (hidden_pre * logistic).astype(BF16)
     update = dot(hidden, w_node_out[...])
@@ -333,8 +410,8 @@
     variance = jnp.mean(centred * centred, axis=-1, keepdims=True)
     inv_std = lax.rsqrt(variance + 1e-05)
     normed = centred * inv_std
-    new_latent[...] = (rows.astype(F32) + normed * gain[...]).astype(BF16)
-    d_normed = cotangent[...].astype(F32) * gain[...]
+    new_latent[...] = (rows.astype(F32) + normed * gain).astype(BF16)
+    d_normed = cotangent[...].astype(F32) * gain
     d_update = (
         inv_std
         * (
@@ -401,7 +478,7 @@
 
 
 def make_backward(members, blocks, own):
-    def kernel(tile_count, send_far, recv_far, most_far, col_rank, senders, receivers, *refs):
+    def kernel(tile_count, most, col_rank, senders, receivers, *refs):
         if own:
             grad_parts, grads, refs = (None, refs[0], None), refs[1], refs[2:]
             d_sums = refs[0]
@@ -410,12 +487,11 @@
             messages, refs = refs[:members], refs[members:]
             grads_out, late_out, refs = refs[:members], refs[members], refs[members + 1 :]
             d_sums, grads = refs[0], refs[-1]
-        totals, tile_send, tile_recv, col_most, order, sem = refs[1:7]
+        totals, col_most, table, order, sem = refs[1:6]
         size, width = senders.shape[1:]
         rows = blocks * size
-        copies = start_copies(
-            (send_far, recv_far, most_far.at[1]), (tile_send, tile_recv, col_most), sem
-        )
+        tiles = col_rank.shape[0] - 1
+        copies = start_tables(most, COLUMNS, col_most, table, sem)
         member = lax.axis_index("grp")
         for side, part in enumerate(grad_parts):
             if part is not None:
@@ -429,15 +505,15 @@
             copy.wait()
 
         def one_pair(pair, carry):
-            tiles, recv_places, send_places = pair_of(
-                pair, order, tile_send, tile_recv, member, members, blocks
+            pair_tiles, recv_places, send_places = pair_of(
+                pair, order, table, tiles, member, members, blocks
             )
             rights = []
             for recv_place, send_place in zip(recv_places, send_places):
                 upper = jnp.concatenate([receivers[recv_place], d_sums[recv_place]], 1)
                 lower = jnp.concatenate([senders[send_place], nothing], 1)
                 rights.append(jnp.concatenate([upper, lower], 0))
-            ranks_of = [col_rank[tile] for tile in tiles]
+            ranks_of = [col_rank[tile] for tile in pair_tiles]
 
             def one_group(first, ranks, fresh):
                 for place in range(2):
@@ -452,13 +528,16 @@
                             added = added + jnp.where(part[:, :width] > 0.0, part[:, width:], 0.0)
                         totals[place, span, :] = added if fresh else totals[place, span, :] + added
 
-            most = jnp.maximum(col_most[tiles[0], size - 1], col_most[tiles[1], size - 1])
-            run_groups(one_group, most)
+            last = size - 1
+            most = jnp.maximum(col_most[pair_tiles[0], last], col_most[pair_tiles[1], last])
+            run_groups(BACKWARD, one_group, most)
             for item, send_place in enumerate(send_places):
                 grads[send_place] += totals[item]
             return carry
 
-        pairs = list_tiles(order, tile_recv, tile_count, blocks, own)
+        pairs = list_tiles(
+            order, table, tile_count, tiles, lambda send, recv: (recv // blocks == 1) == own
+        )
         lax.fori_loop(0, pairs, one_pair, 0)
         if own:
             return
@@ -543,7 +622,8 @@
     node_float = like((own_rows, width), F32)
     pair_like = like((2 * own_rows, width), BF16)
     tile_like = like((tiles + 1, size, size), BF16)
-    most_like = like((2, tiles + 8, size), jnp.int32)
+    most_like = like((3, tiles + 8, size), jnp.int32)
+    vectors_like = like((8, width), F32)
     slab_like = like((members * blocks, size, width), BF16)
     near_like = like((3 * blocks, size, width), BF16)
     message, weight_parts = call(
@@ -553,50 +633,67 @@
         grant=60,
     )
     messages = [message] + [shifted(message, "grp", distance) for distance in range(1, members)]
-    sides = [shifted(message, "blk", 1), shifted(message, "blk", -1)]
-    row_rank, row_degree, col_rank, most = call(
+    row_rank, row_degree, col_rank, most, vectors = call(
         ranks_kernel,
-        [tile_like] * 3 + [most_like],
-        [tile_mask.reshape(tiles, size, size)],
+        [tile_like] * 3 + [most_like, vectors_like],
+        [
+            tile_mask.reshape(tiles, size, size),
+            tile_send,
+            tile_recv,
+            edge_bias.reshape(1, width),
+            node_bias.reshape(1, width),
+            gain.reshape(1, width),
+        ],
         scalars=[tile_count],
         flops=8 * tiles * size * size * size,
     )
+    near, most = lax.optimization_barrier((message, most))
+    sides = [shifted(near, "blk", 1), shifted(near, "blk", -1)]
     tables = [
-        pltpu.SMEM(tile_send.shape, jnp.int32),
-        pltpu.SMEM(tile_recv.shape, jnp.int32),
         pltpu.SMEM(most.shape[1:], jnp.int32),
+        pltpu.SMEM((8, size), jnp.int32),
         pltpu.SMEM((tiles + 2,), jnp.int32),
-        pltpu.SemaphoreType.DMA((3,)),
+        pltpu.SemaphoreType.DMA((2,)),
     ]
+    pair_scratch = [pltpu.VMEM((size, 2 * width), F32)] * 2 + tables
     window = pltpu.VMEM((3 * blocks, size, width), F32)
-    sums_scratch = [window] * 2 + [pltpu.VMEM((size, 2 * width), F32)] * 2 + tables
     tile_flops = 64 * tiles * size * size * width
-    sum_low, sum_high, count_low, count_high, senders, receivers = call(
-        make_forward(members, blocks, False),
-        [node_like] * 4 + [slab_like, near_like],
+    own_senders, receivers, sums, counts = call(
+        make_first(members),
+        [like((blocks, size, width), BF16), near_like] + [like(window.shape, F32)] * 2,
+        [row_rank, row_degree, w_send, w_recv, weight_parts, vectors, message, *sides],
+        scalars=[tile_count],
+        far=[most],
+        scratch=pair_scratch,
+        flops=tile_flops // 2,
+    )
+    sum_low, sum_high, count_low, count_high, senders = call(
+        make_forward(members, False),
+        [node_like] * 4 + [slab_like],
         [
             row_rank,
             row_degree,
+            receivers,
+            sums,
+            counts,
+            own_senders,
             w_send,
-            w_recv,
             weight_parts,
-            edge_bias.reshape(1, width),
-            *messages,
-            *sides,
+            *messages[1:],
         ],
         scalars=[tile_count],
-        far=[tile_send, tile_recv, most],
-        scratch=sums_scratch,
+        far=[most],
+        scratch=pair_scratch + [window] * 2,
         flops=tile_flops,
     )
     from_low, from_high = shifted(sum_high, "blk", 1), shifted(sum_low, "blk", -1)
     sum_own, count_own = call(
-        make_forward(members, blocks, True),
+        make_forward(members, True),
         [node_float] * 2,
-        [row_rank, row_degree, senders, receivers],
+        [row_rank, row_degree, receivers, sums, counts, senders],
         scalars=[tile_count],
-        far=[tile_send, tile_recv, most],
-        scratch=sums_scratch,
+        far=[most],
+        scratch=pair_scratch + [window] * 2,
         flops=tile_flops // 2,
     )
     (
@@ -613,6 +710,7 @@
         node_kernel,
         [node_like] + [pair_like] * 2 + [node_like] * 6,
         [
+            vectors,
             latent,
             cotangent,
             sum_own,
@@ -624,12 +722,6 @@
             w_node_self,
             w_node_msg,
             w_node_out,
-        ],
-        far=[node_bias.reshape(1, width), gain.reshape(1, width)],
-        scratch=[
-            pltpu.VMEM((1, width), F32),
-            pltpu.VMEM((1, width), F32),
-            pltpu.SemaphoreType.DMA((2,)),
         ],
         flops=14 * own_rows * width * width,
     )
@@ -661,7 +753,7 @@
         [like((members * blocks, size, width), F32)],
         [col_rank, senders, receivers, to_low],
         scalars=[tile_count],
-        far=[tile_send, tile_recv, most],
+        far=[most],
         scratch=back_scratch,
         flops=tile_flops // 2,
     )
@@ -687,13 +779,20 @@
         [node_float] + [node_like] * (members - 1) + [like((width, width), BF16)],
         [col_rank, senders, receivers, from_low, from_high, started, *messages],
         scalars=[tile_count],
-        far=[tile_send, tile_recv, most],
+        far=[most],
         scratch=back_scratch + [pltpu.VMEM((members * blocks, size, width), F32)],
         flops=tile_flops,
     )
     back = [shifted(send_grads[distance], "grp", -distance) for distance in range(1, members)]
     chain = jnp.concatenate([share.astype(BF16), late, recv_grad], 0)
     chain = pairwise_sum(chain, "blk")
+    (latent_grad,) = call(
+        return_kernel,
+        [node_float],
+        [direct, w_send, send_grads[0], *back],
+        flops=2 * own_rows * width * width,
+    )
+    chain, latent_grad = lax.optimization_barrier((chain, latent_grad))
     share, summed = chain[: -2 * width], chain[-2 * width :]
     step = members // 2
     while step > 1:
@@ -707,12 +806,6 @@
         step //= 2
     chain = jnp.concatenate([share, summed], 0)
     other = exchanged(chain, "grp", 1)
-    (latent_grad,) = call(
-        return_kernel,
-        [node_float],
-        [direct, w_send, send_grads[0], *back],
-        flops=2 * own_rows * width * width,
-    )
     (weight_grads,) = call(
         last_kernel,
         [like((6, width, width), F32)],

time: 85.3 us -> 84.6 us (level)
  waiting for transfers between devices: 33.4 us -> 26.8 us
  starting transfers between devices: 21.5 us -> 26.6 us
  Pallas kernels: 26.8 us -> 27.9 us
    ppermute x7, waiting for transfers between devices: 20.9 us -> 14 us  [exchanged(): lax.ppermute(value, axis, [(source, source ^ step) for source in range(co...]
    ppermute x7, starting transfers between devices: 4.75 us -> 7.6 us  [exchanged(): lax.ppermute(value, axis, [(source, source ^ step) for source in range(co...]
    ppermute x12, starting transfers between devices: 16.7 us -> 19 us  [shifted(): return lax.ppermute(value, axis, pairs)]
    pallas_call x11 -> x12, Pallas kernels: 26.8 us -> 27.9 us  [call(): pl.pallas_call(kernel, out_shape=[jax.ShapeDtypeStruct(o.shape, o.dtype)...]
  transfers between devices with their start and end apart: 19 -> 19, of which waited for: 9 -> 8; matrix products, arithmetic and copies ran while one was open for 0% -> 0% of each run, Pallas kernels for 11% -> 13%
where the time goes in v5:
time: 84.6 us; the launch traced here: 85.2 us
  Pallas kernels  27.9 us (33%)
  waiting for transfers between devices  26.8 us (32%)
  starting transfers between devices  26.6 us (31%)
  local copies, waits for them, and re-layouts  2.13 us (3%)
  between operations  1.61 us (2%)
    pallas_call x12, Pallas kernels, call(): pl.pallas_call(kernel, out_shape=[jax.ShapeDtypeStruct(o.shape, o.dtype)...  27.9 us
    ppermute x12, starting transfers between devices, shifted(): return lax.ppermute(value, axis, pairs)  19 us
    ppermute x7, waiting for transfers between devices, exchanged(): lax.ppermute(value, axis, [(source, source ^ step) for source in range(co...  14 us
    ppermute x12, waiting for transfers between devices, shifted(): return lax.ppermute(value, axis, pairs)  12.7 us
    ppermute x7, starting transfers between devices, exchanged(): lax.ppermute(value, axis, [(source, source ^ step) for source in range(co...  7.6 us
    unnamed x36, local copies, waits for them, and re-layouts  2.13 us
  transfers between devices with their start and end apart: 19, of which 8 were waited for; matrix products, arithmetic and copies ran while one was open for 0% of the time, Pallas kernels for 13%

profile of v5, /device:TPU:0, one launch (start us, length us, event | category | flops | bytes accessed | tf_op | source)
XLA Modules:
  0.0 85.2 jit_solution(5935022315345120907)
XLA Ops:
  1.3 1.6 %shard_map.185 = (bf16[576,128]{1,0:T(8,128)(2,1)}, bf16[16,384]{1,0:T(8,128)(2,1)}) custom-call(bf16[512,128]{1,0:T(8,128)(2,1)} %latent.7, f32[3,512]{1,0:T(4,128)} %positions.1, f32[3,128]{1,0:T(4,128)} %pos_weight.1), custom_call_target="tpu_custom_call" | custom-call | bytes 298496 | tf_op jit(solution)/shard_map/pallas_call | solution.py:45
  2.9 0.0 copy-start.10
  2.9 0.6 copy-done.12
  3.5 0.0 copy-done.13
  3.6 0.0 copy-done.9
  3.6 0.0 copy-done.10
  3.6 0.0 copy-done.11
  3.6 1.2 %copy-done.1 = s32[1,1,16,128,128]{4,3,2,1,0:T(8,128)S(1)} copy-done((s32[1,1,16,128,128]{4,3,2,1,0:T(8,128)S(1)}, s32[1,1,16,128,128]{4,3,2,1,0:T(8,128)}, u32[]{:S(2)}) %copy-start.1) | copy-done | bytes 1048600
  4.8 0.7 shard_map.184
  5.6 0.2 copy-done.14
  5.7 0.5 collective-permute-start
  6.2 2.9 %collective-permute-start.1 = (bf16[576,128]{1,0:T(8,128)(2,1)S(1)}, bf16[576,128]{1,0:T(8,128)(2,1)S(1)}, u32[]{:S(2)}, u32[]{:S(2)}) collective-permute-start(bf16[576,128]{1,0:T(8,128)(2,1)S(1)} %copy-done.14), channel_id=1, source_target_pairs={{0,28},{4,0},{8,4},{12,8},{16,12},{20,16},{24,20},{28,24},{1,29},{... | collective-permute-start | bytes 442376 | tf_op jit(solution)/shard_map/ppermute | solution.py:23
  9.1 2.3 %collective-permute-start.2 = (bf16[576,128]{1,0:T(8,128)(2,1)S(1)}, bf16[576,128]{1,0:T(8,128)(2,1)S(1)}, u32[]{:S(2)}, u32[]{:S(2)}) collective-permute-start(bf16[576,128]{1,0:T(8,128)(2,1)S(1)} %copy-done.14), channel_id=1, source_target_pairs={{0,1},{1,2},{2,3},{3,0},{4,5},{5,6},{6,7},{7,4},{8,9},{9,10},{10,1... | collective-permute-start | bytes 442376 | tf_op jit(solution)/shard_map/ppermute | solution.py:23
  11.4 2.6 %collective-permute-start.3 = (bf16[576,128]{1,0:T(8,128)(2,1)S(1)}, bf16[576,128]{1,0:T(8,128)(2,1)S(1)}, u32[]{:S(2)}, u32[]{:S(2)}) collective-permute-start(bf16[576,128]{1,0:T(8,128)(2,1)S(1)} %copy-done.14), channel_id=1, source_target_pairs={{0,2},{1,3},{2,0},{3,1},{4,6},{5,7},{6,4},{7,5},{8,10},{9,11},{10,... | collective-permute-start | bytes 442376 | tf_op jit(solution)/shard_map/ppermute | solution.py:23
  14.0 1.3 %collective-permute-start.4 = (bf16[576,128]{1,0:T(8,128)(2,1)S(1)}, bf16[576,128]{1,0:T(8,128)(2,1)S(1)}, u32[]{:S(2)}, u32[]{:S(2)}) collective-permute-start(bf16[576,128]{1,0:T(8,128)(2,1)S(1)} %copy-done.14), channel_id=1, source_target_pairs={{0,3},{1,0},{2,1},{3,2},{4,7},{5,4},{6,5},{7,6},{8,11},{9,8},{10,9... | collective-permute-start | bytes 442376 | tf_op jit(solution)/shard_map/ppermute | solution.py:23
  15.4 3.2 %shard_map.186 = (bf16[4,128,128]{2,1,0:T(8,128)(2,1)S(1)}, bf16[12,128,128]{2,1,0:T(8,128)(2,1)S(1)}, f32[12,128,128]{2,1,0:T(8,128)S(1)}, f32[12,128,128]{2,1,0:T(8,128)S(1)}) custom-call(s32[1,1]{1,0:T(1,128)S(6)} %copy.20.tile_count, s32[3,24,128]{2,1,0:T(8,128)S(1)} %get-tuple-element.46.most, bf16[17,128,128]{2,1,0:T(8,128)(2,1)S(1)} %get-tuple-element.47.row_rank, ...), custom_call_target="tpu_custom_call" | custom-call | flops 1073741824 | bytes 3772416 | tf_op jit(solution)/shard_map/pallas_call | solution.py:45
  18.6 4.2 %collective-permute-done.3.refs_4_.refs_5_ = bf16[576,128]{1,0:T(8,128)(2,1)S(1)} collective-permute-done((bf16[576,128]{1,0:T(8,128)(2,1)S(1)}, bf16[576,128]{1,0:T(8,128)(2,1)S(1)}, u32[]{:S(2)}, u32[]{:S(2)}) %collective-permute-start.3) | collective-permute-done | bytes 147488 | tf_op jit(solution)/shard_map/ppermute | solution.py:23
  22.8 5.4 %shard_map.187 = (bf16[512,128]{1,0:T(8,128)(2,1)S(1)}, bf16[512,128]{1,0:T(8,128)(2,1)S(1)}, bf16[512,128]{1,0:T(8,128)(2,1)S(1)}, bf16[512,128]{1,0:T(8,128)(2,1)S(1)}, bf16[16,128,128]{2,1,0:T(8,128)(2,1)S(1)}) custom-call(s32[1,1]{1,0:T(1,128)S(6)} %copy.20.tile_count, s32[3,24,128]{2,1,0:T(8,128)S(1)} %get-tuple-element.46.most, ...), custom_call_target="tpu_custom_call" | custom-call | flops 2147483648 | bytes 4784128 | tf_op jit(solution)/shard_map/pallas_call | solution.py:45
  28.2 0.1 collective-permute-start.5
  28.3 2.6 %collective-permute-start.6 = (bf16[512,128]{1,0:T(8,128)(2,1)S(1)}, bf16[512,128]{1,0:T(8,128)(2,1)S(1)}, u32[]{:S(2)}, u32[]{:S(2)}) collective-permute-start(bf16[512,128]{1,0:T(8,128)(2,1)S(1)} %get-tuple-element.58), channel_id=1, source_target_pairs={{0,28},{4,0},{8,4},{12,8},{16,12},{20,16},{24,20},{28,24},{1,29},{... | collective-permute-start | bytes 393224 | tf_op jit(solution)/shard_map/ppermute | solution.py:23
  30.9 0.0 copy-start.4
  30.9 0.0 copy-start.5
  31.0 4.0 %shard_map.188 = (f32[512,128]{1,0:T(8,128)S(1)}, f32[512,128]{1,0:T(8,128)S(1)}) custom-call(s32[1,1]{1,0:T(1,128)S(6)} %copy.20.tile_count, s32[3,24,128]{2,1,0:T(8,128)S(1)} %get-tuple-element.46.most, bf16[17,128,128]{2,1,0:T(8,128)(2,1)S(1)} %get-tuple-element.47.row_rank, bf16[17,128,128]{2,1,0:T(8,128)(2,1)S(1)} %get-tuple-element.48.row_degree, ...), custom_call_target="tpu_custom_call" | custom-call | flops 1073741824 | bytes 4165632 | tf_op jit(solution)/shard_map/pallas_call | solution.py:45
  35.0 1.4 %shard_map.189 = (bf16[512,128]{1,0:T(8,128)(2,1)}, bf16[1024,128]{1,0:T(8,128)(2,1)S(1)}, bf16[1024,128]{1,0:T(8,128)(2,1)S(1)}, bf16[512,128]{1,0:T(8,128)(2,1...) custom-call(f32[8,128]{1,0:T(8,128)S(1)} %get-tuple-element.43.vecto, ...), custom_call_target="tpu_custom_call" | custom-call | flops 117440512 | bytes 2625536 | tf_op jit(solution)/shard_map/pallas_call | solution.py:45
  36.4 0.4 shard_map.190
  36.8 0.1 collective-permute-start.7
  36.9 2.3 %collective-permute-start.10 = (bf16[1024,128]{1,0:T(8,128)(2,1)S(1)}, bf16[1024,128]{1,0:T(8,128)(2,1)S(1)}, u32[]{:S(2)}, u32[]{:S(2)}) collective-permute-start(bf16[1024,128]{1,0:T(8,128)(2,1)S(1)} %get-tuple-element.72.refs_0_), channel_id=1, source_target_pairs={{0,28},{4,0},{8,4},{12,8},{16,12},{20,16},{24,20},{28,24},{1,29},{... | collective-permute-start | bytes 786440 | tf_op jit(solution)/shard_map/ppermute | solution.py:23
  39.3 1.9 %collective-permute-done.7 = bf16[256,128]{1,0:T(8,128)(2,1)S(1)} collective-permute-done((bf16[256,128]{1,0:T(8,128)(2,1)S(1)}, bf16[256,128]{1,0:T(8,128)(2,1)S(1)}, u32[]{:S(2)}, u32[]{:S(2)}) %collective-permute-start.7) | collective-permute-done | bytes 65568 | tf_op jit(solution)/shard_map/ppermute | solution.py:558
  41.2 3.5 %collective-permute-start.8 = (bf16[128,128]{1,0:T(8,128)(2,1)S(1)}, bf16[128,128]{1,0:T(8,128)(2,1)S(1)}, u32[]{:S(2)}, u32[]{:S(2)}) collective-permute-start(bf16[128,128]{1,0:T(8,128)(2,1)S(1)} %select_convert_fusion), channel_id=1, source_target_pairs={{0,2},{1,3},{2,0},{3,1},{4,6},{5,7},{6,4},{7,5},{8,10},{9,11},{10,... | collective-permute-start | bytes 98312 | tf_op jit(solution)/shard_map/ppermute | solution.py:558
  44.6 3.2 %shard_map.191.refs_2_ = f32[16,128,128]{2,1,0:T(8,128)S(1)} custom-call(s32[1,1]{1,0:T(1,128)S(6)} %copy.20.tile_count, s32[3,24,128]{2,1,0:T(8,128)S(1)} %get-tuple-element.46.most, bf16[17,128,128]{2,1,0:T(8,128)(2,1)S(1)} %get-tuple-element.70.col_rank, bf16[16,128,128]{2,1,0:T(8,128)(2,1)S(1)} %get-tuple-element.55.refs_0_.senders, ...), custom_call_target="tpu_custom_call" | custom-call | flops 1073741824 | bytes 2822144 | tf_op jit(solution)/shard_map/pallas_call | solution.py:45
  47.9 0.8 collective-permute-done.9.refs_0_.from_low
  48.7 5.9 %shard_map.192 = (f32[512,128]{1,0:T(8,128)S(1)}, bf16[512,128]{1,0:T(8,128)(2,1)S(1)}, bf16[512,128]{1,0:T(8,128)(2,1)S(1)}, bf16[512,128]{1,0:T(8,128)(2,1)S(1)}, bf16[128,128]{1,0:T(8,128)(2,1)S(1)}) custom-call(s32[1,1]{1,0:T(1,128)S(6)} %copy.20.tile_count, s32[3,24,128]{2,1,0:T(8,128)S(1)} %get-tuple-element.46.most, ...), custom_call_target="tpu_custom_call" | custom-call | flops 2147483648 | bytes 4362240 | tf_op jit(solution)/shard_map/pallas_call | solution.py:45
  54.6 0.4 shard_map.193
  55.0 0.1 collective-permute-start.11
  55.1 1.3 %collective-permute-done.11 = bf16[384,128]{1,0:T(8,128)(2,1)S(1)} collective-permute-done((bf16[384,128]{1,0:T(8,128)(2,1)S(1)}, bf16[384,128]{1,0:T(8,128)(2,1)S(1)}, u32[]{:S(2)}, u32[]{:S(2)}) %collective-permute-start.11) | collective-permute-done | bytes 98336 | tf_op jit(solution)/shard_map/ppermute | solution.py:558
  56.4 0.3 collective-permute-start.12
  56.8 1.0 %collective-permute-start.14 = (bf16[512,128]{1,0:T(8,128)(2,1)S(1)}, bf16[512,128]{1,0:T(8,128)(2,1)S(1)}, u32[]{:S(2)}, u32[]{:S(2)}) collective-permute-start(bf16[512,128]{1,0:T(8,128)(2,1)S(1)} %get-tuple-element.78), channel_id=1, source_target_pairs={{0,3},{1,0},{2,1},{3,2},{4,7},{5,4},{6,5},{7,6},{8,11},{9,8},{10,9... | collective-permute-start | bytes 393224 | tf_op jit(solution)/shard_map/ppermute | solution.py:23
  57.8 1.4 %collective-permute-start.15 = (bf16[512,128]{1,0:T(8,128)(2,1)S(1)}, bf16[512,128]{1,0:T(8,128)(2,1)S(1)}, u32[]{:S(2)}, u32[]{:S(2)}) collective-permute-start(bf16[512,128]{1,0:T(8,128)(2,1)S(1)} %get-tuple-element.79), channel_id=1, source_target_pairs={{0,2},{1,3},{2,0},{3,1},{4,6},{5,7},{6,4},{7,5},{8,10},{9,11},{10,... | collective-permute-start | bytes 393224 | tf_op jit(solution)/shard_map/ppermute | solution.py:23
  59.2 1.9 %collective-permute-start.16 = (bf16[512,128]{1,0:T(8,128)(2,1)S(1)}, bf16[512,128]{1,0:T(8,128)(2,1)S(1)}, u32[]{:S(2)}, u32[]{:S(2)}) collective-permute-start(bf16[512,128]{1,0:T(8,128)(2,1)S(1)} %get-tuple-element.80), channel_id=1, source_target_pairs={{0,1},{1,2},{2,3},{3,0},{4,5},{5,6},{6,7},{7,4},{8,9},{9,10},{10,1... | collective-permute-start | bytes 393224 | tf_op jit(solution)/shard_map/ppermute | solution.py:23
  61.1 0.2 collective-permute-done.12
  61.4 2.2 %collective-permute-start.13 = (bf16[384,128]{1,0:T(8,128)(2,1)S(1)}, bf16[384,128]{1,0:T(8,128)(2,1)S(1)}, u32[]{:S(2)}, u32[]{:S(2)}) collective-permute-start(bf16[384,128]{1,0:T(8,128)(2,1)S(1)} %add_convert_fusion.1), channel_id=1, source_target_pairs={{0,16},{4,20},{8,24},{12,28},{16,0},{20,4},{24,8},{28,12},{1,17},{... | collective-permute-start | bytes 294920 | tf_op jit(solution)/shard_map/ppermute | solution.py:558
  63.6 7.7 %collective-permute-done.15.refs_1_ = bf16[512,128]{1,0:T(8,128)(2,1)S(1)} collective-permute-done((bf16[512,128]{1,0:T(8,128)(2,1)S(1)}, bf16[512,128]{1,0:T(8,128)(2,1)S(1)}, u32[]{:S(2)}, u32[]{:S(2)}) %collective-permute-start.15) | collective-permute-done | bytes 131104 | tf_op jit(solution)/shard_map/ppermute | solution.py:23
  71.4 0.9 %shard_map.194 = f32[512,128]{1,0:T(8,128)} custom-call(f32[512,128]{1,0:T(8,128)S(1)} %get-tuple-element.76.direct, bf16[128,128]{1,0:T(8,128)(2,1)S(1)} %copy-done.8, f32[512,128]{1,0:T(8,128)S(1)} %get-tuple-element.77.own, bf16[512,128]{1,0:T(8,128)(2,1)S(1)} %collective-permute-done.14.refs_0_, bf16[512,128]{1,0:T(8,128)(2,1)S(1)} %collective-permute-done.15.refs_1_, ...), custom_call_target="tpu_custom_call" | custom-call | flops 16777216 | bytes 1212416 | tf_op jit(solution)/shard_map/pallas_call | solution.py:45
  72.3 1.3 %collective-permute-start.17 = (bf16[384,128]{1,0:T(8,128)(2,1)S(1)}, bf16[384,128]{1,0:T(8,128)(2,1)S(1)}, u32[]{:S(2)}, u32[]{:S(2)}) collective-permute-start(bf16[384,128]{1,0:T(8,128)(2,1)S(1)} %add_convert_fusion), channel_id=1, source_target_pairs={{0,2},{1,3},{2,0},{3,1},{4,6},{5,7},{6,4},{7,5},{8,10},{9,11},{10,... | collective-permute-start | bytes 294920 | tf_op jit(solution)/shard_map/ppermute | solution.py:558
  73.6 5.2 %collective-permute-done.17 = bf16[384,128]{1,0:T(8,128)(2,1)S(1)} collective-permute-done((bf16[384,128]{1,0:T(8,128)(2,1)S(1)}, bf16[384,128]{1,0:T(8,128)(2,1)S(1)}, u32[]{:S(2)}, u32[]{:S(2)}) %collective-permute-start.17) | collective-permute-done | bytes 98336 | tf_op jit(solution)/shard_map/ppermute | solution.py:558
  78.9 0.1 collective-permute-start.18
  79.0 5.4 %collective-permute-done.18.other = bf16[512,128]{1,0:T(8,128)(2,1)S(1)} collective-permute-done((bf16[512,128]{1,0:T(8,128)(2,1)S(1)}, bf16[512,128]{1,0:T(8,128)(2,1)S(1)}, u32[]{:S(2)}, u32[]{:S(2)}) %collective-permute-start.18) | collective-permute-done | bytes 131104 | tf_op jit(solution)/shard_map/ppermute | solution.py:558
  84.4 0.8 shard_map.195
  (48 shorter events, 0.3 us)
Async XLA Ops:
  2.9 0.7 copy-start.12
  2.9 0.7 copy-start.13
  2.9 0.7 copy-start.9
  2.9 0.7 copy-start.10
  2.9 0.7 copy-start.11
  3.6 1.2 %copy-start.1 = (s32[1,1,16,128,128]{4,3,2,1,0:T(8,128)S(1)}, s32[1,1,16,128,128]{4,3,2,1,0:T(8,128)}, u32[]{:S(2)}) copy-start(s32[1,1,16,128,128]{4,3,2,1,0:T(8,128)} %param.21) | copy-start | bytes 3145732
  4.8 0.9 %copy-start.14 = (bf16[576,128]{1,0:T(8,128)(2,1)S(1)}, bf16[576,128]{1,0:T(8,128)(2,1)}, u32[]{:S(2)}) copy-start(bf16[576,128]{1,0:T(8,128)(2,1)} %get-tuple-element.50.message.refs_3_) | copy-start | bytes 442372
  4.8 10.5 %copy-start.7 = (bf16[128,128]{1,0:T(8,128)(2,1)S(1)}, bf16[128,128]{1,0:T(8,128)(2,1)}, u32[]{:S(2)}) copy-start(bf16[128,128]{1,0:T(8,128)(2,1)} %w_recv.3) | copy-start | bytes 98308
  4.8 10.5 %copy-start.8 = (bf16[128,128]{1,0:T(8,128)(2,1)S(1)}, bf16[128,128]{1,0:T(8,128)(2,1)}, u32[]{:S(2)}) copy-start(bf16[128,128]{1,0:T(8,128)(2,1)} %w_send.3) | copy-start | bytes 98308
  4.8 10.5 %copy-start.15 = (bf16[16,384]{1,0:T(8,128)(2,1)S(1)}, bf16[16,384]{1,0:T(8,128)(2,1)}, u32[]{:S(2)}) copy-start(bf16[16,384]{1,0:T(8,128)(2,1)} %get-tuple-element.49.weight_parts.refs_2_) | copy-start | bytes 36868
  5.7 9.6 %collective-permute-start = (bf16[576,128]{1,0:T(8,128)(2,1)S(1)}, bf16[576,128]{1,0:T(8,128)(2,1)S(1)}, u32[]{:S(2)}, u32[]{:S(2)}) collective-permute-start(bf16[576,128]{1,0:T(8,128)(2,1)S(1)} %copy-done.14), channel_id=1, source_target_pairs={{0,4},{4,8},{8,12},{12,16},{16,20},{20,24},{24,28},{28,0},{1,5},{5... | collective-permute-start | bytes 442376 | tf_op jit(solution)/shard_map/ppermute | solution.py:23
  6.2 9.2 %collective-permute-start.1 = (bf16[576,128]{1,0:T(8,128)(2,1)S(1)}, bf16[576,128]{1,0:T(8,128)(2,1)S(1)}, u32[]{:S(2)}, u32[]{:S(2)}) collective-permute-start(bf16[576,128]{1,0:T(8,128)(2,1)S(1)} %copy-done.14), channel_id=1, source_target_pairs={{0,28},{4,0},{8,4},{12,8},{16,12},{20,16},{24,20},{28,24},{1,29},{... | collective-permute-start | bytes 442376 | tf_op jit(solution)/shard_map/ppermute | solution.py:23
  9.1 9.6 %collective-permute-start.2 = (bf16[576,128]{1,0:T(8,128)(2,1)S(1)}, bf16[576,128]{1,0:T(8,128)(2,1)S(1)}, u32[]{:S(2)}, u32[]{:S(2)}) collective-permute-start(bf16[576,128]{1,0:T(8,128)(2,1)S(1)} %copy-done.14), channel_id=1, source_target_pairs={{0,1},{1,2},{2,3},{3,0},{4,5},{5,6},{6,7},{7,4},{8,9},{9,10},{10,1... | collective-permute-start | bytes 442376 | tf_op jit(solution)/shard_map/ppermute | solution.py:23
  11.4 11.4 %collective-permute-start.3 = (bf16[576,128]{1,0:T(8,128)(2,1)S(1)}, bf16[576,128]{1,0:T(8,128)(2,1)S(1)}, u32[]{:S(2)}, u32[]{:S(2)}) collective-permute-start(bf16[576,128]{1,0:T(8,128)(2,1)S(1)} %copy-done.14), channel_id=1, source_target_pairs={{0,2},{1,3},{2,0},{3,1},{4,6},{5,7},{6,4},{7,5},{8,10},{9,11},{10,... | collective-permute-start | bytes 442376 | tf_op jit(solution)/shard_map/ppermute | solution.py:23
  14.0 8.8 %collective-permute-start.4 = (bf16[576,128]{1,0:T(8,128)(2,1)S(1)}, bf16[576,128]{1,0:T(8,128)(2,1)S(1)}, u32[]{:S(2)}, u32[]{:S(2)}) collective-permute-start(bf16[576,128]{1,0:T(8,128)(2,1)S(1)} %copy-done.14), channel_id=1, source_target_pairs={{0,3},{1,0},{2,1},{3,2},{4,7},{5,4},{6,5},{7,6},{8,11},{9,8},{10,9... | collective-permute-start | bytes 442376 | tf_op jit(solution)/shard_map/ppermute | solution.py:23
  18.6 12.3 %copy-start.16 = (bf16[12,128,128]{2,1,0:T(8,128)(2,1)}, bf16[12,128,128]{2,1,0:T(8,128)(2,1)S(1)}, u32[]{:S(2)}) copy-start(bf16[12,128,128]{2,1,0:T(8,128)(2,1)S(1)} %get-tuple-element.51.receivers) | copy-start | bytes 1179652
  28.2 6.8 %collective-permute-start.5 = (bf16[512,128]{1,0:T(8,128)(2,1)S(1)}, bf16[512,128]{1,0:T(8,128)(2,1)S(1)}, u32[]{:S(2)}, u32[]{:S(2)}) collective-permute-start(bf16[512,128]{1,0:T(8,128)(2,1)S(1)} %get-tuple-element.57), channel_id=1, source_target_pairs={{0,4},{4,8},{8,12},{12,16},{16,20},{20,24},{24,28},{28,0},{1,5},{5... | collective-permute-start | bytes 393224 | tf_op jit(solution)/shard_map/ppermute | solution.py:23
  28.3 6.7 %collective-permute-start.6 = (bf16[512,128]{1,0:T(8,128)(2,1)S(1)}, bf16[512,128]{1,0:T(8,128)(2,1)S(1)}, u32[]{:S(2)}, u32[]{:S(2)}) collective-permute-start(bf16[512,128]{1,0:T(8,128)(2,1)S(1)} %get-tuple-element.58), channel_id=1, source_target_pairs={{0,28},{4,0},{8,4},{12,8},{16,12},{20,16},{24,20},{28,24},{1,29},{... | collective-permute-start | bytes 393224 | tf_op jit(solution)/shard_map/ppermute | solution.py:23
  30.9 4.1 %copy-start = (bf16[512,128]{1,0:T(8,128)(2,1)S(1)}, bf16[512,128]{1,0:T(8,128)(2,1)}, u32[]{:S(2)}) copy-start(bf16[512,128]{1,0:T(8,128)(2,1)} %latent.7) | copy-start | bytes 393220
  30.9 4.1 %copy-start.2 = (bf16[512,128]{1,0:T(8,128)(2,1)S(1)}, bf16[512,128]{1,0:T(8,128)(2,1)}, u32[]{:S(2)}) copy-start(bf16[512,128]{1,0:T(8,128)(2,1)} %cotangent.3) | copy-start | bytes 393220
  30.9 4.1 %copy-start.3 = (bf16[128,128]{1,0:T(8,128)(2,1)S(1)}, bf16[128,128]{1,0:T(8,128)(2,1)}, u32[]{:S(2)}) copy-start(bf16[128,128]{1,0:T(8,128)(2,1)} %w_edge_out.3) | copy-start | bytes 98308
  30.9 4.1 %copy-start.4 = (bf16[128,128]{1,0:T(8,128)(2,1)S(1)}, bf16[128,128]{1,0:T(8,128)(2,1)}, u32[]{:S(2)}) copy-start(bf16[128,128]{1,0:T(8,128)(2,1)} %w_node_self.3) | copy-start | bytes 98308
  30.9 4.1 %copy-start.5 = (bf16[128,128]{1,0:T(8,128)(2,1)S(1)}, bf16[128,128]{1,0:T(8,128)(2,1)}, u32[]{:S(2)}) copy-start(bf16[128,128]{1,0:T(8,128)(2,1)} %w_node_msg.1) | copy-start | bytes 98308
  30.9 4.1 %copy-start.6 = (bf16[128,128]{1,0:T(8,128)(2,1)S(1)}, bf16[128,128]{1,0:T(8,128)(2,1)}, u32[]{:S(2)}) copy-start(bf16[128,128]{1,0:T(8,128)(2,1)} %w_node_out.1) | copy-start | bytes 98308
  36.8 4.3 %collective-permute-start.7 = (bf16[256,128]{1,0:T(8,128)(2,1)S(1)}, bf16[256,128]{1,0:T(8,128)(2,1)S(1)}, u32[]{:S(2)}, u32[]{:S(2)}) collective-permute-start(bf16[256,128]{1,0:T(8,128)(2,1)S(1)} %get-tuple-element.69), channel_id=1, source_target_pairs={{0,1},{1,0},{2,3},{3,2},{4,5},{5,4},{6,7},{7,6},{8,9},{9,8},{10,11... | collective-permute-start | bytes 196616 | tf_op jit(solution)/shard_map/ppermute | solution.py:558
  36.9 7.7 %copy-start.17 = (bf16[12,128,128]{2,1,0:T(8,128)(2,1)S(1)}, bf16[12,128,128]{2,1,0:T(8,128)(2,1)}, u32[]{:S(2)}) copy-start(bf16[12,128,128]{2,1,0:T(8,128)(2,1)} %copy-done.16) | copy-start | bytes 1179652
  36.9 11.0 %collective-permute-start.10 = (bf16[1024,128]{1,0:T(8,128)(2,1)S(1)}, bf16[1024,128]{1,0:T(8,128)(2,1)S(1)}, u32[]{:S(2)}, u32[]{:S(2)}) collective-permute-start(bf16[1024,128]{1,0:T(8,128)(2,1)S(1)} %get-tuple-element.72.refs_0_), channel_id=1, source_target_pairs={{0,28},{4,0},{8,4},{12,8},{16,12},{20,16},{24,20},{28,24},{1,29},{... | collective-permute-start | bytes 786440 | tf_op jit(solution)/shard_map/ppermute | solution.py:23
  39.2 9.5 %collective-permute-start.9 = (bf16[1024,128]{1,0:T(8,128)(2,1)S(1)}, bf16[1024,128]{1,0:T(8,128)(2,1)S(1)}, u32[]{:S(2)}, u32[]{:S(2)}) collective-permute-start(bf16[1024,128]{1,0:T(8,128)(2,1)S(1)} %get-tuple-element.71), channel_id=1, source_target_pairs={{0,4},{4,8},{8,12},{12,16},{16,20},{20,24},{24,28},{28,0},{1,5},{5... | collective-permute-start | bytes 786440 | tf_op jit(solution)/shard_map/ppermute | solution.py:23
  41.2 6.7 %collective-permute-start.8 = (bf16[128,128]{1,0:T(8,128)(2,1)S(1)}, bf16[128,128]{1,0:T(8,128)(2,1)S(1)}, u32[]{:S(2)}, u32[]{:S(2)}) collective-permute-start(bf16[128,128]{1,0:T(8,128)(2,1)S(1)} %select_convert_fusion), channel_id=1, source_target_pairs={{0,2},{1,3},{2,0},{3,1},{4,6},{5,7},{6,4},{7,5},{8,10},{9,11},{10,... | collective-permute-start | bytes 98312 | tf_op jit(solution)/shard_map/ppermute | solution.py:558
  55.0 1.4 %collective-permute-start.11 = (bf16[384,128]{1,0:T(8,128)(2,1)S(1)}, bf16[384,128]{1,0:T(8,128)(2,1)S(1)}, u32[]{:S(2)}, u32[]{:S(2)}) collective-permute-start(bf16[384,128]{1,0:T(8,128)(2,1)S(1)} %pad_maximum_fusion.1), channel_id=1, source_target_pairs={{0,4},{4,0},{8,12},{12,8},{16,20},{20,16},{24,28},{28,24},{1,5},{5... | collective-permute-start | bytes 294920 | tf_op jit(solution)/shard_map/ppermute | solution.py:558
  56.4 4.9 %collective-permute-start.12 = (bf16[384,128]{1,0:T(8,128)(2,1)S(1)}, bf16[384,128]{1,0:T(8,128)(2,1)S(1)}, u32[]{:S(2)}, u32[]{:S(2)}) collective-permute-start(bf16[384,128]{1,0:T(8,128)(2,1)S(1)} %add_convert_fusion.2), channel_id=1, source_target_pairs={{0,8},{4,12},{8,0},{12,4},{16,24},{20,28},{24,16},{28,20},{1,9},{5... | collective-permute-start | bytes 294920 | tf_op jit(solution)/shard_map/ppermute | solution.py:558
  56.8 6.8 %collective-permute-start.14 = (bf16[512,128]{1,0:T(8,128)(2,1)S(1)}, bf16[512,128]{1,0:T(8,128)(2,1)S(1)}, u32[]{:S(2)}, u32[]{:S(2)}) collective-permute-start(bf16[512,128]{1,0:T(8,128)(2,1)S(1)} %get-tuple-element.78), channel_id=1, source_target_pairs={{0,3},{1,0},{2,1},{3,2},{4,7},{5,4},{6,5},{7,6},{8,11},{9,8},{10,9... | collective-permute-start | bytes 393224 | tf_op jit(solution)/shard_map/ppermute | solution.py:23
  57.8 13.5 %collective-permute-start.15 = (bf16[512,128]{1,0:T(8,128)(2,1)S(1)}, bf16[512,128]{1,0:T(8,128)(2,1)S(1)}, u32[]{:S(2)}, u32[]{:S(2)}) collective-permute-start(bf16[512,128]{1,0:T(8,128)(2,1)S(1)} %get-tuple-element.79), channel_id=1, source_target_pairs={{0,2},{1,3},{2,0},{3,1},{4,6},{5,7},{6,4},{7,5},{8,10},{9,11},{10,... | collective-permute-start | bytes 393224 | tf_op jit(solution)/shard_map/ppermute | solution.py:23
  59.2 12.2 %collective-permute-start.16 = (bf16[512,128]{1,0:T(8,128)(2,1)S(1)}, bf16[512,128]{1,0:T(8,128)(2,1)S(1)}, u32[]{:S(2)}, u32[]{:S(2)}) collective-permute-start(bf16[512,128]{1,0:T(8,128)(2,1)S(1)} %get-tuple-element.80), channel_id=1, source_target_pairs={{0,1},{1,2},{2,3},{3,0},{4,5},{5,6},{6,7},{7,4},{8,9},{9,10},{10,1... | collective-permute-start | bytes 393224 | tf_op jit(solution)/shard_map/ppermute | solution.py:23
  61.4 10.9 %collective-permute-start.13 = (bf16[384,128]{1,0:T(8,128)(2,1)S(1)}, bf16[384,128]{1,0:T(8,128)(2,1)S(1)}, u32[]{:S(2)}, u32[]{:S(2)}) collective-permute-start(bf16[384,128]{1,0:T(8,128)(2,1)S(1)} %add_convert_fusion.1), channel_id=1, source_target_pairs={{0,16},{4,20},{8,24},{12,28},{16,0},{20,4},{24,8},{28,12},{1,17},{... | collective-permute-start | bytes 294920 | tf_op jit(solution)/shard_map/ppermute | solution.py:558
  72.3 6.6 %collective-permute-start.17 = (bf16[384,128]{1,0:T(8,128)(2,1)S(1)}, bf16[384,128]{1,0:T(8,128)(2,1)S(1)}, u32[]{:S(2)}, u32[]{:S(2)}) collective-permute-start(bf16[384,128]{1,0:T(8,128)(2,1)S(1)} %add_convert_fusion), channel_id=1, source_target_pairs={{0,2},{1,3},{2,0},{3,1},{4,6},{5,7},{6,4},{7,5},{8,10},{9,11},{10,... | collective-permute-start | bytes 294920 | tf_op jit(solution)/shard_map/ppermute | solution.py:558
  78.9 5.5 %collective-permute-start.18 = (bf16[512,128]{1,0:T(8,128)(2,1)S(1)}, bf16[512,128]{1,0:T(8,128)(2,1)S(1)}, u32[]{:S(2)}, u32[]{:S(2)}) collective-permute-start(bf16[512,128]{1,0:T(8,128)(2,1)S(1)} %pad_maximum_fusion.mine), channel_id=1, source_target_pairs={{0,1},{1,0},{2,3},{3,2},{4,5},{5,4},{6,7},{7,6},{8,9},{9,8},{10,11... | collective-permute-start | bytes 393224 | tf_op jit(solution)/shard_map/ppermute | solution.py:558

commit v6 on v5

--- a/solution.py
+++ b/solution.py
@@ -7,8 +7,8 @@
 
 F32 = jnp.float32
 BF16 = jnp.bfloat16
-FORWARD = (4, 4, 4, 4)
-BACKWARD = (2, 2, 2, 2, 2, 2, 2, 2)
+FORWARD = (8, 8)
+BACKWARD = (16,)
 LOOPED = 4
 ROWS, COLUMNS, TABLES = 0, 1, 2
 SENDERS, RECEIVERS = 0, 1
@@ -382,15 +382,12 @@
     sum_own,
     sum_low,
     sum_high,
-    count_low,
-    count_high,
     w_edge_out,
     w_node_self,
     w_node_msg,
     w_node_out,
     new_latent,
-    to_low,
-    to_high,
+    d_aggregate_out,
     aggregate_out,
     message_out,
     hidden_out,
@@ -423,12 +420,7 @@
     d_hidden = dot_t(d_update, w_node_out[...])
     d_hidden_pre = (d_hidden * logistic * (1.0 + hidden_pre * (1.0 - logistic))).astype(BF16)
     d_message = dot_t(d_hidden_pre, w_node_msg[...]).astype(BF16)
-    d_aggregate = dot_t(d_message, w_edge_out[...]).astype(BF16)
-    own_rows = latent.shape[0]
-    to_low[0:own_rows, :] = d_aggregate
-    to_low[own_rows:, :] = count_low[...]
-    to_high[0:own_rows, :] = d_aggregate
-    to_high[own_rows:, :] = count_high[...]
+    d_aggregate_out[...] = dot_t(d_message, w_edge_out[...]).astype(BF16)
     aggregate_out[...] = aggregate
     message_out[...] = message
     hidden_out[...] = hidden
@@ -451,8 +443,15 @@
     give[...] = grads[pl.ds(pl.multiple_of((1 - bit) * half, half), half), :].astype(BF16)
 
 
-def recv_kernel(
-    latent,
+def recv_kernel(low, own, high, d_low, d_own, d_high, n_low, n_own, n_high, grad_out):
+    total = jnp.zeros(grad_out.shape, F32)
+    for latents, grads, counts in ((low, d_low, n_low), (own, d_own, n_own), (high, d_high, n_high)):
+        part = (grads[...].astype(F32) * counts[...].astype(F32)).astype(BF16)
+        total = total + contract_rows(latents[0 : part.shape[0], :], part)
+    grad_out[...] = total.astype(BF16)
+
+
+def direct_kernel(
     cotangent,
     count_own,
     from_low,
@@ -463,18 +462,14 @@
     w_node_self,
     w_recv,
     direct_out,
-    grad_out,
 ):
-    own_rows = latent.shape[0]
-    count = count_own[...] + from_low[own_rows:, :].astype(F32)
-    count = count + from_high[own_rows:, :].astype(F32)
+    count = count_own[...] + from_low[...].astype(F32) + from_high[...].astype(F32)
     d_recv = (dot_t(d_message[...], w_edge_out[...]) * count).astype(BF16)
     direct_out[...] = (
         cotangent[...].astype(F32)
         + dot_t(d_hidden_pre[...], w_node_self[...])
         + dot_t(d_recv, w_recv[...])
     )
-    grad_out[...] = contract_rows(latent[...], d_recv).astype(BF16)
 
 
 def make_backward(members, blocks, own):
@@ -562,11 +557,10 @@
     return (lax.axis_index(axis) & step) != 0
 
 
-def pairwise_sum(value, axis):
+def pairwise_sum(value, axis, step=1):
     count = lax.axis_size(axis)
     if count & (count - 1):
         return lax.psum(value.astype(F32), axis).astype(BF16)
-    step = 1
     while step < count:
         value = (value.astype(F32) + exchanged(value, axis, step).astype(F32)).astype(BF16)
         step *= 2
@@ -581,18 +575,54 @@
     latent_grad[...] = direct[...] + dot_t(d_send.astype(BF16), w_send[...])
 
 
-def last_kernel(mine, other, weight_grads, table):
-    summed = mine.shape[0] - table.shape[0] // 2
-    half = table.shape[0] // 2
-    width = mine.shape[1]
-    bit = lax.axis_index("grp") & 1
-    table[pl.ds(pl.multiple_of(bit * half, half), half), :] = mine[0:half, :].astype(F32)
-    table[pl.ds(pl.multiple_of((1 - bit) * half, half), half), :] = other[0:half, :].astype(F32)
-    for item in range(summed // width):
-        span = slice(half + item * width, half + (item + 1) * width)
-        weight_grads[item] = mine[span, :].astype(F32) + other[span, :].astype(F32)
-    for item in range(table.shape[0] // width):
-        weight_grads[summed // width + item] = table[item * width : (item + 1) * width, :]
+def make_last(members):
+    def kernel(mine, other, weight_grads):
+        bit = lax.axis_index("blk") & 1
+        for part, place in ((mine, bit), (other, 1 - bit)):
+            early = 2 * weight_grads.shape[0] // 6
+            half = (weight_grads.shape[0] - early) // (2 * members)
+            quarter = early // 4
+            for item in range(members):
+                start = pl.multiple_of(early + (2 * item + place) * half, half)
+                span = slice(item * half, (item + 1) * half)
+                weight_grads[pl.ds(start, half), :] = part[span, :].astype(F32)
+            for item in range(2):
+                start = pl.multiple_of((2 * item + place) * quarter, quarter)
+                first = members * half + item * quarter
+                weight_grads[pl.ds(start, quarter), :] = part[
+                    first : first + quarter, :
+                ].astype(F32)
+
+    return kernel
+
+
+def halves(value, pieces):
+    rows, width = value.shape
+    parts = []
+    start = 0
+    for piece in pieces:
+        parts.append((value[start : start + piece // 2], value[start + piece // 2 : start + piece]))
+        start += piece
+    high = bit_set("blk", 1)
+    lows = jnp.concatenate([part[0] for part in parts], 0)
+    highs = jnp.concatenate([part[1] for part in parts], 0)
+    return jnp.where(high, highs, lows), jnp.where(high, lows, highs)
+
+
+def gather_shares(share, summed, tied):
+    step = lax.axis_size("grp") // 2
+    rows = share.shape[0]
+    while step:
+        if step == 1:
+            share, summed, tied = lax.optimization_barrier((share, summed, tied))
+        other = exchanged(jnp.concatenate([share, summed], 0), "grp", step)
+        others = other[:rows]
+        high = bit_set("grp", step)
+        share = jnp.concatenate([jnp.where(high, others, share), jnp.where(high, share, others)], 0)
+        summed = (summed.astype(F32) + other[rows:].astype(F32)).astype(BF16)
+        rows *= 2
+        step //= 2
+    return share, summed, tied
 
 
 def body(
@@ -620,7 +650,6 @@
     members = lax.axis_size("grp")
     node_like = like((own_rows, width), BF16)
     node_float = like((own_rows, width), F32)
-    pair_like = like((2 * own_rows, width), BF16)
     tile_like = like((tiles + 1, size, size), BF16)
     most_like = like((3, tiles + 8, size), jnp.int32)
     vectors_like = like((8, width), F32)
@@ -647,8 +676,7 @@
         scalars=[tile_count],
         flops=8 * tiles * size * size * size,
     )
-    near, most = lax.optimization_barrier((message, most))
-    sides = [shifted(near, "blk", 1), shifted(near, "blk", -1)]
+    sides = [shifted(message, "blk", 1), shifted(message, "blk", -1)]
     tables = [
         pltpu.SMEM(most.shape[1:], jnp.int32),
         pltpu.SMEM((8, size), jnp.int32),
@@ -698,8 +726,7 @@
     )
     (
         new_latent,
-        to_low,
-        to_high,
+        d_aggregate,
         aggregate,
         message_out,
         hidden,
@@ -708,7 +735,7 @@
         d_message,
     ) = call(
         node_kernel,
-        [node_like] + [pair_like] * 2 + [node_like] * 6,
+        [node_like] * 8,
         [
             vectors,
             latent,
@@ -716,8 +743,6 @@
             sum_own,
             from_low,
             from_high,
-            count_low,
-            count_high,
             w_edge_out,
             w_node_self,
             w_node_msg,
@@ -725,7 +750,7 @@
         ],
         flops=14 * own_rows * width * width,
     )
-    from_low, from_high = shifted(to_high, "blk", 1), shifted(to_low, "blk", -1)
+    d_low, d_high = shifted(d_aggregate, "blk", 1), shifted(d_aggregate, "blk", -1)
     half = 4 * width // 2
     share, given = call(
         early_kernel,
@@ -751,68 +776,80 @@
     (started,) = call(
         make_backward(members, blocks, True),
         [like((members * blocks, size, width), F32)],
-        [col_rank, senders, receivers, to_low],
+        [col_rank, senders, receivers, d_aggregate],
         scalars=[tile_count],
         far=[most],
         scratch=back_scratch,
         flops=tile_flops // 2,
     )
-    direct, recv_grad = call(
+    (recv_grad,) = call(
         recv_kernel,
-        [node_float, like((width, width), BF16)],
+        [like((width, width), BF16)],
         [
-            latent,
+            sides[0],
+            message,
+            sides[1],
+            d_low,
+            d_aggregate,
+            d_high,
+            count_low,
+            count_own,
+            count_high,
+        ],
+        flops=6 * own_rows * width * width,
+    )
+    *send_grads, late = call(
+        make_backward(members, blocks, False),
+        [node_float] + [node_like] * (members - 1) + [like((width, width), BF16)],
+        [col_rank, senders, receivers, d_low, d_high, started, *messages],
+        scalars=[tile_count],
+        far=[most],
+        scratch=back_scratch + [pltpu.VMEM((members * blocks, size, width), F32)],
+        flops=tile_flops,
+    )
+    back = [shifted(send_grads[distance], "grp", -distance) for distance in range(1, members)]
+    count_low, count_high, late = lax.optimization_barrier((count_low, count_high, late))
+    (direct,) = call(
+        direct_kernel,
+        [node_float],
+        [
             cotangent,
             count_own,
-            from_low,
-            from_high,
+            shifted(count_high, "blk", 1),
+            shifted(count_low, "blk", -1),
             d_hidden_pre,
             d_message,
             w_edge_out,
             w_node_self,
             w_recv,
         ],
-        flops=8 * own_rows * width * width,
-    )
-    *send_grads, late = call(
-        make_backward(members, blocks, False),
-        [node_float] + [node_like] * (members - 1) + [like((width, width), BF16)],
-        [col_rank, senders, receivers, from_low, from_high, started, *messages],
-        scalars=[tile_count],
-        far=[most],
-        scratch=back_scratch + [pltpu.VMEM((members * blocks, size, width), F32)],
-        flops=tile_flops,
-    )
-    back = [shifted(send_grads[distance], "grp", -distance) for distance in range(1, members)]
-    chain = jnp.concatenate([share.astype(BF16), late, recv_grad], 0)
-    chain = pairwise_sum(chain, "blk")
+        flops=6 * own_rows * width * width,
+    )
     (latent_grad,) = call(
         return_kernel,
         [node_float],
         [direct, w_send, send_grads[0], *back],
         flops=2 * own_rows * width * width,
     )
-    chain, latent_grad = lax.optimization_barrier((chain, latent_grad))
-    share, summed = chain[: -2 * width], chain[-2 * width :]
-    step = members // 2
-    while step > 1:
-        other = exchanged(jnp.concatenate([share, summed], 0), "grp", step)
-        others = other[: -2 * width]
-        high = bit_set("grp", step)
-        share = jnp.concatenate(
-            [jnp.where(high, others, share), jnp.where(high, share, others)], 0
+    share = share.astype(BF16)
+    chain = jnp.concatenate([share, late, recv_grad], 0)
+    slabs = lax.axis_size("blk")
+    if slabs & (slabs - 1) or slabs == 1:
+        chain = pairwise_sum(chain, "blk")
+        rows = share.shape[0]
+        share, summed, latent_grad = gather_shares(chain[:rows], chain[rows:], latent_grad)
+        weight_grads = jnp.concatenate([summed, share], 0).astype(F32)
+    else:
+        mine, given = halves(chain, (share.shape[0], width, width))
+        mine = (mine.astype(F32) + exchanged(given, "blk", 1).astype(F32)).astype(BF16)
+        chain = pairwise_sum(mine, "blk", 2)
+        rows = share.shape[0] // 2
+        share, summed, latent_grad = gather_shares(chain[:rows], chain[rows:], latent_grad)
+        mine = jnp.concatenate([share, summed], 0)
+        (weight_grads,) = call(
+            make_last(members), [like((6 * width, width), F32)], [mine, exchanged(mine, "blk", 1)]
         )
-        summed = (summed.astype(F32) + other[-2 * width :].astype(F32)).astype(BF16)
-        step //= 2
-    chain = jnp.concatenate([share, summed], 0)
-    other = exchanged(chain, "grp", 1)
-    (weight_grads,) = call(
-        last_kernel,
-        [like((6, width, width), F32)],
-        [chain, other],
-        scratch=[pltpu.VMEM((4 * width, width), F32)],
-    )
-    return (new_latent, latent_grad, weight_grads)
+    return (new_latent, latent_grad, weight_grads.reshape(6, width, width))
 
 
 def solution(mesh):

time: 84.6 us -> 83.8 us (level); the launches traced: 85.2 us -> 82.8 us
  waiting for transfers between devices: 26.8 us -> 23.2 us
  starting transfers between devices: 26.6 us -> 28.4 us
    ppermute x7 -> x8, waiting for transfers between devices: 14 us -> 11.4 us  [exchanged(): lax.ppermute(value, axis, [(source, source ^ step) for source in range(co...]
    ppermute x12 -> x14, starting transfers between devices: 19 us -> 20.1 us  [shifted(): return lax.ppermute(value, axis, pairs)]
    ppermute x12 -> x14, waiting for transfers between devices: 12.7 us -> 11.8 us  [shifted(): return lax.ppermute(value, axis, pairs)]
    ppermute x7 -> x8, starting transfers between devices: 7.6 us -> 8.33 us  [exchanged(): lax.ppermute(value, axis, [(source, source ^ step) for source in range(co...]
    pallas_call x12 -> x13, Pallas kernels: 27.9 us -> 27.3 us  [call(): pl.pallas_call(kernel, out_shape=[jax.ShapeDtypeStruct(o.shape, o.dtype)...]
  transfers between devices with their start and end apart: 19 -> 22, of which waited for: 8 -> 10; matrix products, arithmetic and copies ran while one was open for 0% -> 0% of each run, Pallas kernels for 13% -> 15%
where the time goes in v6:
time: 83.8 us; the launch traced here: 82.8 us
  starting transfers between devices  28.4 us (34%)
  Pallas kernels  27.3 us (33%)
  waiting for transfers between devices  23.2 us (28%)
  local copies, waits for them, and re-layouts  2.1 us (3%)
  between operations  1.65 us (2%)
    pallas_call x13, Pallas kernels, call(): pl.pallas_call(kernel, out_shape=[jax.ShapeDtypeStruct(o.shape, o.dtype)...  27.3 us
    ppermute x14, starting transfers between devices, shifted(): return lax.ppermute(value, axis, pairs)  20.1 us
    ppermute x14, waiting for transfers between devices, shifted(): return lax.ppermute(value, axis, pairs)  11.8 us
    ppermute x8, waiting for transfers between devices, exchanged(): lax.ppermute(value, axis, [(source, source ^ step) for source in range(co...  11.4 us
    ppermute x8, starting transfers between devices, exchanged(): lax.ppermute(value, axis, [(source, source ^ step) for source in range(co...  8.33 us
    unnamed x36, local copies, waits for them, and re-layouts  2.09 us
  transfers between devices with their start and end apart: 22, of which 10 were waited for; matrix products, arithmetic and copies ran while one was open for 0% of the time, Pallas kernels for 15%

profile of v6, /device:TPU:0, one launch (start us, length us, event | category | flops | bytes accessed | tf_op | source)
XLA Modules:
  0.0 82.8 jit_solution(312621343111486941)
XLA Ops:
  0.6 1.6 %shard_map.185 = (bf16[576,128]{1,0:T(8,128)(2,1)}, bf16[16,384]{1,0:T(8,128)(2,1)}) custom-call(bf16[512,128]{1,0:T(8,128)(2,1)} %latent.5, f32[3,512]{1,0:T(4,128)} %positions.1, f32[3,128]{1,0:T(4,128)} %pos_weight.1), custom_call_target="tpu_custom_call" | custom-call | bytes 298496 | tf_op jit(solution)/shard_map/pallas_call | solution.py:45
  2.2 0.5 collective-permute-start
  2.7 2.9 %collective-permute-start.1 = (bf16[576,128]{1,0:T(8,128)(2,1)}, bf16[576,128]{1,0:T(8,128)(2,1)S(1)}, u32[]{:S(2)}, u32[]{:S(2)}) collective-permute-start(bf16[576,128]{1,0:T(8,128)(2,1)} %get-tuple-element.47.message.refs_3_.own), channel_id=1, source_target_pairs={{0,28},{4,0},{8,4},{12,8},{16,12},{20,16},{24,20},{28,24},{1,29},{... | collective-permute-start | bytes 442376 | tf_op jit(solution)/shard_map/ppermute | solution.py:23
  5.6 2.3 %collective-permute-start.2 = (bf16[576,128]{1,0:T(8,128)(2,1)}, bf16[576,128]{1,0:T(8,128)(2,1)S(1)}, u32[]{:S(2)}, u32[]{:S(2)}) collective-permute-start(bf16[576,128]{1,0:T(8,128)(2,1)} %get-tuple-element.47.message.refs_3_.own), channel_id=1, source_target_pairs={{0,1},{1,2},{2,3},{3,0},{4,5},{5,6},{6,7},{7,4},{8,9},{9,10},{10,1... | collective-permute-start | bytes 442376 | tf_op jit(solution)/shard_map/ppermute | solution.py:23
  7.9 2.6 %collective-permute-start.3 = (bf16[576,128]{1,0:T(8,128)(2,1)}, bf16[576,128]{1,0:T(8,128)(2,1)S(1)}, u32[]{:S(2)}, u32[]{:S(2)}) collective-permute-start(bf16[576,128]{1,0:T(8,128)(2,1)} %get-tuple-element.47.message.refs_3_.own), channel_id=1, source_target_pairs={{0,2},{1,3},{2,0},{3,1},{4,6},{5,7},{6,4},{7,5},{8,10},{9,11},{10,... | collective-permute-start | bytes 442376 | tf_op jit(solution)/shard_map/ppermute | solution.py:23
  10.5 1.3 %collective-permute-start.4 = (bf16[576,128]{1,0:T(8,128)(2,1)}, bf16[576,128]{1,0:T(8,128)(2,1)S(1)}, u32[]{:S(2)}, u32[]{:S(2)}) collective-permute-start(bf16[576,128]{1,0:T(8,128)(2,1)} %get-tuple-element.47.message.refs_3_.own), channel_id=1, source_target_pairs={{0,3},{1,0},{2,1},{3,2},{4,7},{5,4},{6,5},{7,6},{8,11},{9,8},{10,9... | collective-permute-start | bytes 442376 | tf_op jit(solution)/shard_map/ppermute | solution.py:23
  12.6 0.6 copy-done.13
  13.2 0.0 copy-done.14
  13.2 0.0 copy-done.10
  13.2 0.0 copy-done.11
  13.2 1.2 %copy-done.1 = s32[1,1,16,128,128]{4,3,2,1,0:T(8,128)S(1)} copy-done((s32[1,1,16,128,128]{4,3,2,1,0:T(8,128)S(1)}, s32[1,1,16,128,128]{4,3,2,1,0:T(8,128)}, u32[]{:S(2)}) %copy-start.1) | copy-done | bytes 1048600
  14.5 0.7 shard_map.184
  15.2 0.1 copy-done.3
  15.4 3.5 %shard_map.186 = (bf16[4,128,128]{2,1,0:T(8,128)(2,1)S(1)}, bf16[12,128,128]{2,1,0:T(8,128)(2,1)S(1)}, f32[12,128,128]{2,1,0:T(8,128)S(1)}, f32[12,128,128]{2,1,0:T(8,128)S(1)}) custom-call(s32[1,1]{1,0:T(1,128)S(6)} %copy.20.tile_count, s32[3,24,128]{2,1,0:T(8,128)S(1)} %get-tuple-element.43.most, bf16[17,128,128]{2,1,0:T(8,128)(2,1)S(1)} %get-tuple-element.44.row_rank, ...), custom_call_target="tpu_custom_call" | custom-call | flops 1073741824 | bytes 3772416 | tf_op jit(solution)/shard_map/pallas_call | solution.py:45
  18.9 0.7 collective-permute-done.3.refs_4_.refs_5_
  19.6 4.8 %shard_map.187 = (bf16[512,128]{1,0:T(8,128)(2,1)S(1)}, bf16[512,128]{1,0:T(8,128)(2,1)S(1)}, bf16[512,128]{1,0:T(8,128)(2,1)S(1)}, bf16[512,128]{1,0:T(8,128)(2,1)S(1)}, bf16[16,128,128]{2,1,0:T(8,128)(2,1)S(1)}) custom-call(s32[1,1]{1,0:T(1,128)S(6)} %copy.20.tile_count, s32[3,24,128]{2,1,0:T(8,128)S(1)} %get-tuple-element.43.most, ...), custom_call_target="tpu_custom_call" | custom-call | flops 2147483648 | bytes 4784128 | tf_op jit(solution)/shard_map/pallas_call | solution.py:45
  24.4 0.5 collective-permute-start.5
  24.9 2.2 %collective-permute-start.6 = (bf16[512,128]{1,0:T(8,128)(2,1)S(1)}, bf16[512,128]{1,0:T(8,128)(2,1)S(1)}, u32[]{:S(2)}, u32[]{:S(2)}) collective-permute-start(bf16[512,128]{1,0:T(8,128)(2,1)S(1)} %get-tuple-element.55), channel_id=1, source_target_pairs={{0,28},{4,0},{8,4},{12,8},{16,12},{20,16},{24,20},{28,24},{1,29},{... | collective-permute-start | bytes 393224 | tf_op jit(solution)/shard_map/ppermute | solution.py:23
  27.1 3.4 %shard_map.188 = (f32[512,128]{1,0:T(8,128)S(1)}, f32[512,128]{1,0:T(8,128)S(1)}) custom-call(s32[1,1]{1,0:T(1,128)S(6)} %copy.20.tile_count, s32[3,24,128]{2,1,0:T(8,128)S(1)} %get-tuple-element.43.most, bf16[17,128,128]{2,1,0:T(8,128)(2,1)S(1)} %get-tuple-element.44.row_rank, bf16[17,128,128]{2,1,0:T(8,128)(2,1)S(1)} %get-tuple-element.45.row_degree, ...), custom_call_target="tpu_custom_call" | custom-call | flops 1073741824 | bytes 4165632 | tf_op jit(solution)/shard_map/pallas_call | solution.py:45
  30.5 0.3 collective-permute-done.5.sum_low
  30.9 1.7 %shard_map.189 = (bf16[512,128]{1,0:T(8,128)(2,1)}, bf16[512,128]{1,0:T(8,128)(2,1)S(1)}, bf16[512,128]{1,0:T(8,128)(2,1)S(1)}, bf16[512,128]{1,0:T(8,128)(2,1)S...) custom-call(f32[8,128]{1,0:T(8,128)S(1)} %get-tuple-element.42.vecto, ...), custom_call_target="tpu_custom_call" | custom-call | flops 117440512 | bytes 1970176 | tf_op jit(solution)/shard_map/pallas_call | solution.py:45
  32.6 0.4 shard_map.190
  33.0 3.6 %collective-permute-start.7 = (bf16[256,128]{1,0:T(8,128)(2,1)S(1)}, bf16[256,128]{1,0:T(8,128)(2,1)S(1)}, u32[]{:S(2)}, u32[]{:S(2)}) collective-permute-start(bf16[256,128]{1,0:T(8,128)(2,1)S(1)} %get-tuple-element.64), channel_id=1, source_target_pairs={{0,1},{1,0},{2,3},{3,2},{4,5},{5,4},{6,7},{7,6},{8,9},{9,8},{10,11... | collective-permute-start | bytes 196616 | tf_op jit(solution)/shard_map/ppermute | solution.py:553
  36.6 1.7 %collective-permute-start.10 = (bf16[512,128]{1,0:T(8,128)(2,1)S(1)}, bf16[512,128]{1,0:T(8,128)(2,1)S(1)}, u32[]{:S(2)}, u32[]{:S(2)}) collective-permute-start(bf16[512,128]{1,0:T(8,128)(2,1)S(1)} %get-tuple-element.68.refs_0_.d_own), channel_id=1, source_target_pairs={{0,28},{4,0},{8,4},{12,8},{16,12},{20,16},{24,20},{28,24},{1,29},{... | collective-permute-start | bytes 393224 | tf_op jit(solution)/shard_map/ppermute | solution.py:23
  38.2 0.6 collective-permute-done.7
  38.9 1.6 %collective-permute-start.8 = (bf16[128,128]{1,0:T(8,128)(2,1)S(1)}, bf16[128,128]{1,0:T(8,128)(2,1)S(1)}, u32[]{:S(2)}, u32[]{:S(2)}) collective-permute-start(bf16[128,128]{1,0:T(8,128)(2,1)S(1)} %select_convert_fusion), channel_id=1, source_target_pairs={{0,2},{1,3},{2,0},{3,1},{4,6},{5,7},{6,4},{7,5},{8,10},{9,11},{10,... | collective-permute-start | bytes 98312 | tf_op jit(solution)/shard_map/ppermute | solution.py:553
  40.5 3.5 %shard_map.191.refs_2_ = f32[16,128,128]{2,1,0:T(8,128)S(1)} custom-call(s32[1,1]{1,0:T(1,128)S(6)} %copy.20.tile_count, s32[3,24,128]{2,1,0:T(8,128)S(1)} %get-tuple-element.43.most, bf16[17,128,128]{2,1,0:T(8,128)(2,1)S(1)} %get-tuple-element.67.col_rank, bf16[16,128,128]{2,1,0:T(8,128)(2,1)S(1)} %get-tuple-element.52.refs_0_.senders, ...), custom_call_target="tpu_custom_call" | custom-call | flops 1073741824 | bytes 2691072 | tf_op jit(solution)/shard_map/pallas_call | solution.py:45
  44.0 5.3 %shard_map.192 = (f32[512,128]{1,0:T(8,128)S(1)}, bf16[512,128]{1,0:T(8,128)(2,1)S(1)}, bf16[512,128]{1,0:T(8,128)(2,1)S(1)}, bf16[512,128]{1,0:T(8,128)(2,1)S(1)}, bf16[128,128]{1,0:T(8,128)(2,1)S(1)}) custom-call(s32[1,1]{1,0:T(1,128)S(6)} %copy.20.tile_count, s32[3,24,128]{2,1,0:T(8,128)S(1)} %get-tuple-element.43.most, ...), custom_call_target="tpu_custom_call" | custom-call | flops 2147483648 | bytes 4100096 | tf_op jit(solution)/shard_map/pallas_call | solution.py:45
  49.3 0.3 shard_map.193
  49.7 0.1 collective-permute-start.11
  49.8 1.2 %collective-permute-done.11 = bf16[192,128]{1,0:T(8,128)(2,1)S(1)} collective-permute-done((bf16[192,128]{1,0:T(8,128)(2,1)S(1)}, bf16[192,128]{1,0:T(8,128)(2,1)S(1)}, u32[]{:S(2)}, u32[]{:S(2)}) %collective-permute-start.11) | collective-permute-done | bytes 49184 | tf_op jit(solution)/shard_map/ppermute | solution.py:553
  51.0 0.1 collective-permute-start.12
  51.1 4.1 %collective-permute-done.12 = bf16[192,128]{1,0:T(8,128)(2,1)S(1)} collective-permute-done((bf16[192,128]{1,0:T(8,128)(2,1)S(1)}, bf16[192,128]{1,0:T(8,128)(2,1)S(1)}, u32[]{:S(2)}, u32[]{:S(2)}) %collective-permute-start.12) | collective-permute-done | bytes 49184 | tf_op jit(solution)/shard_map/ppermute | solution.py:553
  55.2 1.3 %collective-permute-start.13 = (bf16[192,128]{1,0:T(8,128)(2,1)S(1)}, bf16[192,128]{1,0:T(8,128)(2,1)S(1)}, u32[]{:S(2)}, u32[]{:S(2)}) collective-permute-start(bf16[192,128]{1,0:T(8,128)(2,1)S(1)} %add_convert_fusion.1), channel_id=1, source_target_pairs={{0,16},{4,20},{8,24},{12,28},{16,0},{20,4},{24,8},{28,12},{1,17},{... | collective-permute-start | bytes 147464 | tf_op jit(solution)/shard_map/ppermute | solution.py:553
  56.5 2.6 %collective-permute-start.16 = (bf16[512,128]{1,0:T(8,128)(2,1)S(1)}, bf16[512,128]{1,0:T(8,128)(2,1)S(1)}, u32[]{:S(2)}, u32[]{:S(2)}) collective-permute-start(bf16[512,128]{1,0:T(8,128)(2,1)S(1)} %get-tuple-element.73.n_low), channel_id=1, source_target_pairs={{0,28},{4,0},{8,4},{12,8},{16,12},{20,16},{24,20},{28,24},{1,29},{... | collective-permute-start | bytes 393224 | tf_op jit(solution)/shard_map/ppermute | solution.py:23
  59.1 2.4 %collective-permute-start.17 = (bf16[512,128]{1,0:T(8,128)(2,1)S(1)}, bf16[512,128]{1,0:T(8,128)(2,1)S(1)}, u32[]{:S(2)}, u32[]{:S(2)}) collective-permute-start(bf16[512,128]{1,0:T(8,128)(2,1)S(1)} %get-tuple-element.75), channel_id=1, source_target_pairs={{0,3},{1,0},{2,1},{3,2},{4,7},{5,4},{6,5},{7,6},{8,11},{9,8},{10,9... | collective-permute-start | bytes 393224 | tf_op jit(solution)/shard_map/ppermute | solution.py:23
  61.6 1.0 %collective-permute-start.18 = (bf16[512,128]{1,0:T(8,128)(2,1)S(1)}, bf16[512,128]{1,0:T(8,128)(2,1)S(1)}, u32[]{:S(2)}, u32[]{:S(2)}) collective-permute-start(bf16[512,128]{1,0:T(8,128)(2,1)S(1)} %get-tuple-element.76), channel_id=1, source_target_pairs={{0,2},{1,3},{2,0},{3,1},{4,6},{5,7},{6,4},{7,5},{8,10},{9,11},{10,... | collective-permute-start | bytes 393224 | tf_op jit(solution)/shard_map/ppermute | solution.py:23
  62.6 0.4 collective-permute-done.15.from_low
  63.1 1.5 %collective-permute-start.14 = (bf16[192,128]{1,0:T(8,128)(2,1)S(1)}, bf16[192,128]{1,0:T(8,128)(2,1)S(1)}, u32[]{:S(2)}, u32[]{:S(2)}) collective-permute-start(bf16[192,128]{1,0:T(8,128)(2,1)S(1)} %add_convert_fusion), channel_id=1, source_target_pairs={{0,2},{1,3},{2,0},{3,1},{4,6},{5,7},{6,4},{7,5},{8,10},{9,11},{10,... | collective-permute-start | bytes 147464 | tf_op jit(solution)/shard_map/ppermute | solution.py:553
  64.6 0.3 shard_map.194.direct
  65.0 0.5 collective-permute-done.17.refs_0_
  65.5 9.8 %collective-permute-done.18.refs_1_ = bf16[512,128]{1,0:T(8,128)(2,1)S(1)} collective-permute-done((bf16[512,128]{1,0:T(8,128)(2,1)S(1)}, bf16[512,128]{1,0:T(8,128)(2,1)S(1)}, u32[]{:S(2)}, u32[]{:S(2)}) %collective-permute-start.18) | collective-permute-done | bytes 131104 | tf_op jit(solution)/shard_map/ppermute | solution.py:23
  75.3 0.9 %shard_map.195 = f32[512,128]{1,0:T(8,128)} custom-call(f32[512,128]{1,0:T(8,128)S(1)} %shard_map.194.direct, bf16[128,128]{1,0:T(8,128)(2,1)S(1)} %copy-done.9, f32[512,128]{1,0:T(8,128)S(1)} %get-tuple-element.74.own, bf16[512,128]{1,0:T(8,128)(2,1)S(1)} %collective-permute-done.17.refs_0_, bf16[512,128]{1,0:T(8,128)(2,1)S(1)} %collective-permute-done.18.refs_1_, ...), custom_call_target="tpu_custom_call" | custom-call | flops 16777216 | bytes 1212416 | tf_op jit(solution)/shard_map/pallas_call | solution.py:45
  76.3 0.1 collective-permute-start.20
  76.3 4.3 %collective-permute-done.20 = bf16[256,128]{1,0:T(8,128)(2,1)S(1)} collective-permute-done((bf16[256,128]{1,0:T(8,128)(2,1)S(1)}, bf16[256,128]{1,0:T(8,128)(2,1)S(1)}, u32[]{:S(2)}, u32[]{:S(2)}) %collective-permute-start.20) | collective-permute-done | bytes 65568 | tf_op jit(solution)/shard_map/ppermute | solution.py:553
  80.7 0.1 collective-permute-start.21
  80.7 1.3 %collective-permute-done.21.other = bf16[384,128]{1,0:T(8,128)(2,1)S(1)} collective-permute-done((bf16[384,128]{1,0:T(8,128)(2,1)S(1)}, bf16[384,128]{1,0:T(8,128)(2,1)S(1)}, u32[]{:S(2)}, u32[]{:S(2)}) %collective-permute-start.21) | collective-permute-done | bytes 98336 | tf_op jit(solution)/shard_map/ppermute | solution.py:553
  82.0 0.8 shard_map.196
  (61 shorter events, 0.3 us)
Async XLA Ops:
  2.2 13.0 %collective-permute-start = (bf16[576,128]{1,0:T(8,128)(2,1)}, bf16[576,128]{1,0:T(8,128)(2,1)S(1)}, u32[]{:S(2)}, u32[]{:S(2)}) collective-permute-start(bf16[576,128]{1,0:T(8,128)(2,1)} %get-tuple-element.47.message.refs_3_.own), channel_id=1, source_target_pairs={{0,4},{4,8},{8,12},{12,16},{16,20},{20,24},{24,28},{28,0},{1,5},{5... | collective-permute-start | bytes 442376 | tf_op jit(solution)/shard_map/ppermute | solution.py:23
  2.7 12.5 %collective-permute-start.1 = (bf16[576,128]{1,0:T(8,128)(2,1)}, bf16[576,128]{1,0:T(8,128)(2,1)S(1)}, u32[]{:S(2)}, u32[]{:S(2)}) collective-permute-start(bf16[576,128]{1,0:T(8,128)(2,1)} %get-tuple-element.47.message.refs_3_.own), channel_id=1, source_target_pairs={{0,28},{4,0},{8,4},{12,8},{16,12},{20,16},{24,20},{28,24},{1,29},{... | collective-permute-start | bytes 442376 | tf_op jit(solution)/shard_map/ppermute | solution.py:23
  5.6 13.3 %collective-permute-start.2 = (bf16[576,128]{1,0:T(8,128)(2,1)}, bf16[576,128]{1,0:T(8,128)(2,1)S(1)}, u32[]{:S(2)}, u32[]{:S(2)}) collective-permute-start(bf16[576,128]{1,0:T(8,128)(2,1)} %get-tuple-element.47.message.refs_3_.own), channel_id=1, source_target_pairs={{0,1},{1,2},{2,3},{3,0},{4,5},{5,6},{6,7},{7,4},{8,9},{9,10},{10,1... | collective-permute-start | bytes 442376 | tf_op jit(solution)/shard_map/ppermute | solution.py:23
  7.9 11.7 %collective-permute-start.3 = (bf16[576,128]{1,0:T(8,128)(2,1)}, bf16[576,128]{1,0:T(8,128)(2,1)S(1)}, u32[]{:S(2)}, u32[]{:S(2)}) collective-permute-start(bf16[576,128]{1,0:T(8,128)(2,1)} %get-tuple-element.47.message.refs_3_.own), channel_id=1, source_target_pairs={{0,2},{1,3},{2,0},{3,1},{4,6},{5,7},{6,4},{7,5},{8,10},{9,11},{10,... | collective-permute-start | bytes 442376 | tf_op jit(solution)/shard_map/ppermute | solution.py:23
  10.5 9.1 %collective-permute-start.4 = (bf16[576,128]{1,0:T(8,128)(2,1)}, bf16[576,128]{1,0:T(8,128)(2,1)S(1)}, u32[]{:S(2)}, u32[]{:S(2)}) collective-permute-start(bf16[576,128]{1,0:T(8,128)(2,1)} %get-tuple-element.47.message.refs_3_.own), channel_id=1, source_target_pairs={{0,3},{1,0},{2,1},{3,2},{4,7},{5,4},{6,5},{7,6},{8,11},{9,8},{10,9... | collective-permute-start | bytes 442376 | tf_op jit(solution)/shard_map/ppermute | solution.py:23
  12.5 0.7 copy-start.13
  12.5 0.7 copy-start.14
  12.5 0.7 copy-start.10
  12.5 0.7 copy-start.11
  12.5 0.7 copy-start.12
  13.2 1.2 %copy-start.1 = (s32[1,1,16,128,128]{4,3,2,1,0:T(8,128)S(1)}, s32[1,1,16,128,128]{4,3,2,1,0:T(8,128)}, u32[]{:S(2)}) copy-start(s32[1,1,16,128,128]{4,3,2,1,0:T(8,128)} %param.21) | copy-start | bytes 3145732
  14.4 0.9 %copy-start.3 = (bf16[576,128]{1,0:T(8,128)(2,1)S(1)}, bf16[576,128]{1,0:T(8,128)(2,1)}, u32[]{:S(2)}) copy-start(bf16[576,128]{1,0:T(8,128)(2,1)} %get-tuple-element.47.message.refs_3_.own) | copy-start | bytes 442372
  14.5 0.9 %copy-start.8 = (bf16[128,128]{1,0:T(8,128)(2,1)S(1)}, bf16[128,128]{1,0:T(8,128)(2,1)}, u32[]{:S(2)}) copy-start(bf16[128,128]{1,0:T(8,128)(2,1)} %w_recv.3) | copy-start | bytes 98308
  14.5 0.9 %copy-start.9 = (bf16[128,128]{1,0:T(8,128)(2,1)S(1)}, bf16[128,128]{1,0:T(8,128)(2,1)}, u32[]{:S(2)}) copy-start(bf16[128,128]{1,0:T(8,128)(2,1)} %w_send.3) | copy-start | bytes 98308
  14.5 0.9 %copy-start.15 = (bf16[16,384]{1,0:T(8,128)(2,1)S(1)}, bf16[16,384]{1,0:T(8,128)(2,1)}, u32[]{:S(2)}) copy-start(bf16[16,384]{1,0:T(8,128)(2,1)} %get-tuple-element.46.weight_parts.refs_2_) | copy-start | bytes 36868
  18.9 8.2 %copy-start.16 = (bf16[12,128,128]{2,1,0:T(8,128)(2,1)}, bf16[12,128,128]{2,1,0:T(8,128)(2,1)S(1)}, u32[]{:S(2)}) copy-start(bf16[12,128,128]{2,1,0:T(8,128)(2,1)S(1)} %get-tuple-element.48.receivers) | copy-start | bytes 1179652
  24.4 6.5 %collective-permute-start.5 = (bf16[512,128]{1,0:T(8,128)(2,1)S(1)}, bf16[512,128]{1,0:T(8,128)(2,1)S(1)}, u32[]{:S(2)}, u32[]{:S(2)}) collective-permute-start(bf16[512,128]{1,0:T(8,128)(2,1)S(1)} %get-tuple-element.54), channel_id=1, source_target_pairs={{0,4},{4,8},{8,12},{12,16},{16,20},{20,24},{24,28},{28,0},{1,5},{5... | collective-permute-start | bytes 393224 | tf_op jit(solution)/shard_map/ppermute | solution.py:23
  24.9 6.0 %collective-permute-start.6 = (bf16[512,128]{1,0:T(8,128)(2,1)S(1)}, bf16[512,128]{1,0:T(8,128)(2,1)S(1)}, u32[]{:S(2)}, u32[]{:S(2)}) collective-permute-start(bf16[512,128]{1,0:T(8,128)(2,1)S(1)} %get-tuple-element.55), channel_id=1, source_target_pairs={{0,28},{4,0},{8,4},{12,8},{16,12},{20,16},{24,20},{28,24},{1,29},{... | collective-permute-start | bytes 393224 | tf_op jit(solution)/shard_map/ppermute | solution.py:23
  27.1 3.8 %copy-start = (bf16[512,128]{1,0:T(8,128)(2,1)S(1)}, bf16[512,128]{1,0:T(8,128)(2,1)}, u32[]{:S(2)}) copy-start(bf16[512,128]{1,0:T(8,128)(2,1)} %latent.5) | copy-start | bytes 393220
  27.1 3.8 %copy-start.2 = (bf16[512,128]{1,0:T(8,128)(2,1)S(1)}, bf16[512,128]{1,0:T(8,128)(2,1)}, u32[]{:S(2)}) copy-start(bf16[512,128]{1,0:T(8,128)(2,1)} %cotangent.3) | copy-start | bytes 393220
  27.1 3.8 %copy-start.4 = (bf16[128,128]{1,0:T(8,128)(2,1)S(1)}, bf16[128,128]{1,0:T(8,128)(2,1)}, u32[]{:S(2)}) copy-start(bf16[128,128]{1,0:T(8,128)(2,1)} %w_edge_out.3) | copy-start | bytes 98308
  27.1 3.8 %copy-start.5 = (bf16[128,128]{1,0:T(8,128)(2,1)S(1)}, bf16[128,128]{1,0:T(8,128)(2,1)}, u32[]{:S(2)}) copy-start(bf16[128,128]{1,0:T(8,128)(2,1)} %w_node_self.3) | copy-start | bytes 98308
  27.1 3.8 %copy-start.6 = (bf16[128,128]{1,0:T(8,128)(2,1)S(1)}, bf16[128,128]{1,0:T(8,128)(2,1)}, u32[]{:S(2)}) copy-start(bf16[128,128]{1,0:T(8,128)(2,1)} %w_node_msg.1) | copy-start | bytes 98308
  27.1 3.8 %copy-start.7 = (bf16[128,128]{1,0:T(8,128)(2,1)S(1)}, bf16[128,128]{1,0:T(8,128)(2,1)}, u32[]{:S(2)}) copy-start(bf16[128,128]{1,0:T(8,128)(2,1)} %w_node_out.1) | copy-start | bytes 98308
  33.0 5.8 %collective-permute-start.7 = (bf16[256,128]{1,0:T(8,128)(2,1)S(1)}, bf16[256,128]{1,0:T(8,128)(2,1)S(1)}, u32[]{:S(2)}, u32[]{:S(2)}) collective-permute-start(bf16[256,128]{1,0:T(8,128)(2,1)S(1)} %get-tuple-element.64), channel_id=1, source_target_pairs={{0,1},{1,0},{2,3},{3,2},{4,5},{5,4},{6,7},{7,6},{8,9},{9,8},{10,11... | collective-permute-start | bytes 196616 | tf_op jit(solution)/shard_map/ppermute | solution.py:553
  36.6 3.9 %copy-start.17 = (bf16[12,128,128]{2,1,0:T(8,128)(2,1)S(1)}, bf16[12,128,128]{2,1,0:T(8,128)(2,1)}, u32[]{:S(2)}) copy-start(bf16[12,128,128]{2,1,0:T(8,128)(2,1)} %copy-done.16) | copy-start | bytes 1179652
  36.6 7.4 %collective-permute-start.10 = (bf16[512,128]{1,0:T(8,128)(2,1)S(1)}, bf16[512,128]{1,0:T(8,128)(2,1)S(1)}, u32[]{:S(2)}, u32[]{:S(2)}) collective-permute-start(bf16[512,128]{1,0:T(8,128)(2,1)S(1)} %get-tuple-element.68.refs_0_.d_own), channel_id=1, source_target_pairs={{0,28},{4,0},{8,4},{12,8},{16,12},{20,16},{24,20},{28,24},{1,29},{... | collective-permute-start | bytes 393224 | tf_op jit(solution)/shard_map/ppermute | solution.py:23
  38.2 5.8 %collective-permute-start.9 = (bf16[512,128]{1,0:T(8,128)(2,1)S(1)}, bf16[512,128]{1,0:T(8,128)(2,1)S(1)}, u32[]{:S(2)}, u32[]{:S(2)}) collective-permute-start(bf16[512,128]{1,0:T(8,128)(2,1)S(1)} %get-tuple-element.68.refs_0_.d_own), channel_id=1, source_target_pairs={{0,4},{4,8},{8,12},{12,16},{16,20},{20,24},{24,28},{28,0},{1,5},{5... | collective-permute-start | bytes 393224 | tf_op jit(solution)/shard_map/ppermute | solution.py:23
  38.9 5.1 %collective-permute-start.8 = (bf16[128,128]{1,0:T(8,128)(2,1)S(1)}, bf16[128,128]{1,0:T(8,128)(2,1)S(1)}, u32[]{:S(2)}, u32[]{:S(2)}) collective-permute-start(bf16[128,128]{1,0:T(8,128)(2,1)S(1)} %select_convert_fusion), channel_id=1, source_target_pairs={{0,2},{1,3},{2,0},{3,1},{4,6},{5,7},{6,4},{7,5},{8,10},{9,11},{10,... | collective-permute-start | bytes 98312 | tf_op jit(solution)/shard_map/ppermute | solution.py:553
  49.7 1.3 %collective-permute-start.11 = (bf16[192,128]{1,0:T(8,128)(2,1)S(1)}, bf16[192,128]{1,0:T(8,128)(2,1)S(1)}, u32[]{:S(2)}, u32[]{:S(2)}) collective-permute-start(bf16[192,128]{1,0:T(8,128)(2,1)S(1)} %broadcast_select_fusion), channel_id=1, source_target_pairs={{0,4},{4,0},{8,12},{12,8},{16,20},{20,16},{24,28},{28,24},{1,5},{5... | collective-permute-start | bytes 147464 | tf_op jit(solution)/shard_map/ppermute | solution.py:553
  51.0 4.2 %collective-permute-start.12 = (bf16[192,128]{1,0:T(8,128)(2,1)S(1)}, bf16[192,128]{1,0:T(8,128)(2,1)S(1)}, u32[]{:S(2)}, u32[]{:S(2)}) collective-permute-start(bf16[192,128]{1,0:T(8,128)(2,1)S(1)} %add_convert_fusion.2), channel_id=1, source_target_pairs={{0,8},{4,12},{8,0},{12,4},{16,24},{20,28},{24,16},{28,20},{1,9},{5... | collective-permute-start | bytes 147464 | tf_op jit(solution)/shard_map/ppermute | solution.py:553
  55.2 7.4 %collective-permute-start.13 = (bf16[192,128]{1,0:T(8,128)(2,1)S(1)}, bf16[192,128]{1,0:T(8,128)(2,1)S(1)}, u32[]{:S(2)}, u32[]{:S(2)}) collective-permute-start(bf16[192,128]{1,0:T(8,128)(2,1)S(1)} %add_convert_fusion.1), channel_id=1, source_target_pairs={{0,16},{4,20},{8,24},{12,28},{16,0},{20,4},{24,8},{28,12},{1,17},{... | collective-permute-start | bytes 147464 | tf_op jit(solution)/shard_map/ppermute | solution.py:553
  56.5 6.6 %collective-permute-start.15 = (bf16[512,128]{1,0:T(8,128)(2,1)S(1)}, bf16[512,128]{1,0:T(8,128)(2,1)S(1)}, u32[]{:S(2)}, u32[]{:S(2)}) collective-permute-start(bf16[512,128]{1,0:T(8,128)(2,1)S(1)} %get-tuple-element.72.n_high), channel_id=1, source_target_pairs={{0,4},{4,8},{8,12},{12,16},{16,20},{20,24},{24,28},{28,0},{1,5},{5... | collective-permute-start | bytes 393224 | tf_op jit(solution)/shard_map/ppermute | solution.py:23
  56.5 8.1 %collective-permute-start.16 = (bf16[512,128]{1,0:T(8,128)(2,1)S(1)}, bf16[512,128]{1,0:T(8,128)(2,1)S(1)}, u32[]{:S(2)}, u32[]{:S(2)}) collective-permute-start(bf16[512,128]{1,0:T(8,128)(2,1)S(1)} %get-tuple-element.73.n_low), channel_id=1, source_target_pairs={{0,28},{4,0},{8,4},{12,8},{16,12},{20,16},{24,20},{28,24},{1,29},{... | collective-permute-start | bytes 393224 | tf_op jit(solution)/shard_map/ppermute | solution.py:23
  59.1 6.4 %collective-permute-start.17 = (bf16[512,128]{1,0:T(8,128)(2,1)S(1)}, bf16[512,128]{1,0:T(8,128)(2,1)S(1)}, u32[]{:S(2)}, u32[]{:S(2)}) collective-permute-start(bf16[512,128]{1,0:T(8,128)(2,1)S(1)} %get-tuple-element.75), channel_id=1, source_target_pairs={{0,3},{1,0},{2,1},{3,2},{4,7},{5,4},{6,5},{7,6},{8,11},{9,8},{10,9... | collective-permute-start | bytes 393224 | tf_op jit(solution)/shard_map/ppermute | solution.py:23
  61.6 13.7 %collective-permute-start.18 = (bf16[512,128]{1,0:T(8,128)(2,1)S(1)}, bf16[512,128]{1,0:T(8,128)(2,1)S(1)}, u32[]{:S(2)}, u32[]{:S(2)}) collective-permute-start(bf16[512,128]{1,0:T(8,128)(2,1)S(1)} %get-tuple-element.76), channel_id=1, source_target_pairs={{0,2},{1,3},{2,0},{3,1},{4,6},{5,7},{6,4},{7,5},{8,10},{9,11},{10,... | collective-permute-start | bytes 393224 | tf_op jit(solution)/shard_map/ppermute | solution.py:23
  62.6 12.7 %collective-permute-start.19 = (bf16[512,128]{1,0:T(8,128)(2,1)S(1)}, bf16[512,128]{1,0:T(8,128)(2,1)S(1)}, u32[]{:S(2)}, u32[]{:S(2)}) collective-permute-start(bf16[512,128]{1,0:T(8,128)(2,1)S(1)} %get-tuple-element.77), channel_id=1, source_target_pairs={{0,1},{1,2},{2,3},{3,0},{4,5},{5,6},{6,7},{7,4},{8,9},{9,10},{10,1... | collective-permute-start | bytes 393224 | tf_op jit(solution)/shard_map/ppermute | solution.py:23
  63.1 13.2 %collective-permute-start.14 = (bf16[192,128]{1,0:T(8,128)(2,1)S(1)}, bf16[192,128]{1,0:T(8,128)(2,1)S(1)}, u32[]{:S(2)}, u32[]{:S(2)}) collective-permute-start(bf16[192,128]{1,0:T(8,128)(2,1)S(1)} %add_convert_fusion), channel_id=1, source_target_pairs={{0,2},{1,3},{2,0},{3,1},{4,6},{5,7},{6,4},{7,5},{8,10},{9,11},{10,... | collective-permute-start | bytes 147464 | tf_op jit(solution)/shard_map/ppermute | solution.py:553
  76.3 4.3 %collective-permute-start.20 = (bf16[256,128]{1,0:T(8,128)(2,1)S(1)}, bf16[256,128]{1,0:T(8,128)(2,1)S(1)}, u32[]{:S(2)}, u32[]{:S(2)}) collective-permute-start(bf16[256,128]{1,0:T(8,128)(2,1)S(1)} %pad_maximum_fusion.1), channel_id=1, source_target_pairs={{0,1},{1,0},{2,3},{3,2},{4,5},{5,4},{6,7},{7,6},{8,9},{9,8},{10,11... | collective-permute-start | bytes 196616 | tf_op jit(solution)/shard_map/ppermute | solution.py:553
  80.7 1.4 %collective-permute-start.21 = (bf16[384,128]{1,0:T(8,128)(2,1)S(1)}, bf16[384,128]{1,0:T(8,128)(2,1)S(1)}, u32[]{:S(2)}, u32[]{:S(2)}) collective-permute-start(bf16[384,128]{1,0:T(8,128)(2,1)S(1)} %pad_maximum_fusion.mine), channel_id=1, source_target_pairs={{0,4},{4,0},{8,12},{12,8},{16,20},{20,16},{24,28},{28,24},{1,5},{5... | collective-permute-start | bytes 294920 | tf_op jit(solution)/shard_map/ppermute | solution.py:553

commit v7 on v6

--- a/solution.py
+++ b/solution.py
@@ -7,7 +7,7 @@
 
 F32 = jnp.float32
 BF16 = jnp.bfloat16
-FORWARD = (8, 8)
+FORWARD = (16,)
 BACKWARD = (16,)
 LOOPED = 4
 ROWS, COLUMNS, TABLES = 0, 1, 2
@@ -145,12 +145,12 @@
     return (found + 1) // 2
 
 
-def pair_of(pair, order, table, tiles, member, members, blocks):
+def pair_of(pair, order, table, tiles, member, blocks):
     pair_tiles = [order[2 * pair], order[2 * pair + 1]]
     named = [pair_tiles[0], jnp.where(pair_tiles[1] == tiles, pair_tiles[0], pair_tiles[1])]
     recv_places = [table[RECEIVERS, tile] for tile in named]
     send_places = [
-        sender_place(table[SENDERS, tile], member, members, blocks) for tile in named
+        sender_place(table[SENDERS, tile], member, blocks) for tile in named
     ]
     return pair_tiles, recv_places, send_places
 
@@ -190,12 +190,6 @@
     return first + steps * LOOPED
 
 
-def eye_of(size):
-    row_index = lax.broadcasted_iota(jnp.int32, (size, size), 0)
-    col_index = lax.broadcasted_iota(jnp.int32, (size, size), 1)
-    return (row_index == col_index).astype(F32).astype(BF16)
-
-
 def lay_blocks(table, parts):
     size = table.shape[1]
     place = 0
@@ -205,8 +199,8 @@
             place += 1
 
 
-def sender_place(block, member, members, blocks):
-    distance = lax.rem(member - block // blocks + members, members)
+def sender_place(block, member, blocks):
+    distance = member ^ (block // blocks)
     return distance * blocks + lax.rem(block, blocks)
 
 
@@ -227,7 +221,7 @@
         table[start + block] = found[block * size : (block + 1) * size, :].astype(BF16)
 
 
-def forward_tiles(member, members, tables, ranks_in, rows_in, sums, counts, wanted):
+def forward_tiles(member, tables, ranks_in, rows_in, sums, counts, wanted):
     tile_count, row_most, table, order, total, count = tables
     row_rank, row_degree = ranks_in
     senders, receivers = rows_in
@@ -237,7 +231,7 @@
 
     def one_pair(pair, carry):
         pair_tiles, recv_places, send_places = pair_of(
-            pair, order, table, tiles, member, members, blocks
+            pair, order, table, tiles, member, blocks
         )
         nothing = jnp.zeros((size, width), BF16)
         upper = jnp.concatenate([senders[send_places[0]], nothing], 1)
@@ -317,7 +311,6 @@
         member = lax.axis_index("grp")
         forward_tiles(
             member,
-            members,
             (tile_count, row_most, table, order, total, count),
             (row_rank, row_degree),
             (senders, receivers),
@@ -358,7 +351,6 @@
         member = lax.axis_index("grp")
         forward_tiles(
             member,
-            members,
             (tile_count, row_most, table, order, total, count),
             (row_rank, row_degree),
             (senders, receivers),
@@ -451,7 +443,7 @@
     grad_out[...] = total.astype(BF16)
 
 
-def direct_kernel(
+def latent_grad_kernel(
     cotangent,
     count_own,
     from_low,
@@ -461,88 +453,141 @@
     w_edge_out,
     w_node_self,
     w_recv,
-    direct_out,
+    from_send,
+    latent_grad,
 ):
     count = count_own[...] + from_low[...].astype(F32) + from_high[...].astype(F32)
     d_recv = (dot_t(d_message[...], w_edge_out[...]) * count).astype(BF16)
-    direct_out[...] = (
+    latent_grad[...] = (
         cotangent[...].astype(F32)
         + dot_t(d_hidden_pre[...], w_node_self[...])
+        + from_send[...]
         + dot_t(d_recv, w_recv[...])
     )
 
 
-def make_backward(members, blocks, own):
-    def kernel(tile_count, most, col_rank, senders, receivers, *refs):
-        if own:
-            grad_parts, grads, refs = (None, refs[0], None), refs[1], refs[2:]
-            d_sums = refs[0]
-        else:
-            grad_parts, started, refs = (refs[0], None, refs[1]), refs[2], refs[3:]
-            messages, refs = refs[:members], refs[members:]
-            grads_out, late_out, refs = refs[:members], refs[members], refs[members + 1 :]
-            d_sums, grads = refs[0], refs[-1]
-        totals, col_most, table, order, sem = refs[1:6]
-        size, width = senders.shape[1:]
-        rows = blocks * size
-        tiles = col_rank.shape[0] - 1
+def backward_tiles(member, tables, col_rank, rows_in, d_sums, grads, wanted):
+    tile_count, col_most, table, order, totals = tables
+    senders, receivers = rows_in
+    size, width = senders.shape[1:]
+    blocks = receivers.shape[0] // 3
+    tiles = col_rank.shape[0] - 1
+
+    def one_pair(pair, carry):
+        pair_tiles, recv_places, send_places = pair_of(pair, order, table, tiles, member, blocks)
+        rights = [
+            jnp.concatenate([receivers[place], d_sums[place]], 1) for place in recv_places
+        ]
+        send_rows = [senders[place].astype(F32) for place in send_places]
+        ranks_of = [col_rank[tile] for tile in pair_tiles]
+
+        def one_group(first, ranks, fresh):
+            for place in range(2):
+                left = jnp.concatenate(one_hots(ranks_of[place], first, ranks), 0)
+                found = dot(left, rights[place])
+                for chunk in range(0, size, CHUNK):
+                    span = slice(chunk, chunk + CHUNK)
+                    rows = send_rows[place][span, :]
+                    added = jnp.zeros((CHUNK, width), F32)
+                    for item in range(ranks):
+                        part = found[item * size + chunk : item * size + chunk + CHUNK, :]
+                        positive = part[:, :width] + rows > 0.0
+                        added = added + jnp.where(positive, part[:, width:], 0.0)
+                    totals[place, span, :] = added if fresh else totals[place, span, :] + added
+
+        last = size - 1
+        most = jnp.maximum(col_most[pair_tiles[0], last], col_most[pair_tiles[1], last])
+        run_groups(BACKWARD, one_group, most)
+        for item, send_place in enumerate(send_places):
+            grads[send_place] += totals[item]
+        return carry
+
+    pairs = list_tiles(order, table, tile_count, tiles, wanted)
+    lax.fori_loop(0, pairs, one_pair, 0)
+
+
+def lay_grads(d_sums, parts):
+    blocks, size = d_sums.shape[0] // 3, d_sums.shape[1]
+    for side, part in parts:
+        for block in range(blocks):
+            d_sums[side * blocks + block] = part[block * size : (block + 1) * size, :]
+
+
+def back_own(
+    tile_count, most, col_rank, senders, receivers, d_own, grads, d_sums, totals, col_most, table, order, sem
+):
+    copies = start_tables(most, COLUMNS, col_most, table, sem)
+    blocks = receivers.shape[0] // 3
+    lay_grads(d_sums, [(1, d_own)])
+    grads[...] = jnp.zeros_like(grads)
+    for copy in copies:
+        copy.wait()
+    backward_tiles(
+        lax.axis_index("grp"),
+        (tile_count, col_most, table, order, totals),
+        col_rank,
+        (senders, receivers),
+        d_sums,
+        grads,
+        lambda send, recv: recv // blocks == 1,
+    )
+
+
+def make_back_far(members):
+    def kernel(tile_count, most, col_rank, senders, receivers, d_low, d_high, started, *refs):
+        outs, refs = refs[: members - 1], refs[members - 1 :]
+        d_sums, totals, col_most, table, order, sem, grads = refs
         copies = start_tables(most, COLUMNS, col_most, table, sem)
-        member = lax.axis_index("grp")
-        for side, part in enumerate(grad_parts):
-            if part is not None:
-                for block in range(blocks):
-                    span = slice(block * size, (block + 1) * size)
-                    d_sums[side * blocks + block] = part[span, :]
-        grads[...] = jnp.zeros_like(grads) if own else started[...]
-        unit = eye_of(size)
-        nothing = jnp.zeros((size, width), BF16)
+        blocks, size = receivers.shape[0] // 3, receivers.shape[1]
+        lay_grads(d_sums, [(0, d_low), (2, d_high)])
+        grads[blocks:] = started[blocks:]
         for copy in copies:
             copy.wait()
-
-        def one_pair(pair, carry):
-            pair_tiles, recv_places, send_places = pair_of(
-                pair, order, table, tiles, member, members, blocks
-            )
-            rights = []
-            for recv_place, send_place in zip(recv_places, send_places):
-                upper = jnp.concatenate([receivers[recv_place], d_sums[recv_place]], 1)
-                lower = jnp.concatenate([senders[send_place], nothing], 1)
-                rights.append(jnp.concatenate([upper, lower], 0))
-            ranks_of = [col_rank[tile] for tile in pair_tiles]
-
-            def one_group(first, ranks, fresh):
-                for place in range(2):
-                    hots = one_hots(ranks_of[place], first, ranks)
-                    left = jnp.concatenate([jnp.concatenate([hot, unit], 1) for hot in hots], 0)
-                    found = dot(left, rights[place])
-                    for chunk in range(0, size, CHUNK):
-                        span = slice(chunk, chunk + CHUNK)
-                        added = jnp.zeros((CHUNK, width), F32)
-                        for item in range(ranks):
-                            part = found[item * size + chunk : item * size + chunk + CHUNK, :]
-                            added = added + jnp.where(part[:, :width] > 0.0, part[:, width:], 0.0)
-                        totals[place, span, :] = added if fresh else totals[place, span, :] + added
-
-            last = size - 1
-            most = jnp.maximum(col_most[pair_tiles[0], last], col_most[pair_tiles[1], last])
-            run_groups(BACKWARD, one_group, most)
-            for item, send_place in enumerate(send_places):
-                grads[send_place] += totals[item]
-            return carry
-
-        pairs = list_tiles(
-            order, table, tile_count, tiles, lambda send, recv: (recv // blocks == 1) == own
+        member = lax.axis_index("grp")
+        backward_tiles(
+            member,
+            (tile_count, col_most, table, order, totals),
+            col_rank,
+            (senders, receivers),
+            d_sums,
+            grads,
+            lambda send, recv: (recv // blocks != 1) & (send // blocks != member),
         )
-        lax.fori_loop(0, pairs, one_pair, 0)
-        if own:
-            return
-        late = jnp.zeros((width, width), F32)
-        for distance, out in enumerate(grads_out):
+        for distance, out in enumerate(outs):
             for block in range(blocks):
                 span = slice(block * size, (block + 1) * size)
-                found = grads[distance * blocks + block]
-                out[span, :] = found.astype(out.dtype)
-                late = late + contract_rows(messages[distance][span, :], found.astype(BF16))
+                out[span, :] = grads[(distance + 1) * blocks + block].astype(BF16)
+
+    return kernel
+
+
+def make_back_near(members):
+    def kernel(tile_count, most, col_rank, senders, receivers, d_low, d_high, started, *refs):
+        far, refs = refs[: members - 1], refs[members - 1 :]
+        messages, refs = refs[:members], refs[members:]
+        own_out, late_out, d_sums, totals, col_most, table, order, sem, grads = refs
+        copies = start_tables(most, COLUMNS, col_most, table, sem)
+        blocks, size = receivers.shape[0] // 3, receivers.shape[1]
+        lay_grads(d_sums, [(0, d_low), (2, d_high)])
+        grads[0:blocks] = started[0:blocks]
+        for copy in copies:
+            copy.wait()
+        member = lax.axis_index("grp")
+        backward_tiles(
+            member,
+            (tile_count, col_most, table, order, totals),
+            col_rank,
+            (senders, receivers),
+            d_sums,
+            grads,
+            lambda send, recv: (recv // blocks != 1) & (send // blocks == member),
+        )
+        rows = blocks * size
+        for block in range(blocks):
+            own_out[block * size : (block + 1) * size, :] = grads[block]
+        late = contract_rows(messages[0][0:rows, :], own_out[...].astype(BF16))
+        for message, part in zip(messages[1:], far):
+            late = late + contract_rows(message[0:rows, :], part[...])
         late_out[...] = late.astype(BF16)
 
     return kernel
@@ -567,12 +612,12 @@
     return value
 
 
-def return_kernel(direct, w_send, own, *refs):
-    back, latent_grad = refs[:-1], refs[-1]
+def return_kernel(w_send, own, *refs):
+    back, out = refs[:-1], refs[-1]
     d_send = own[...]
     for part in back:
         d_send = d_send + part[...].astype(F32)
-    latent_grad[...] = direct[...] + dot_t(d_send.astype(BF16), w_send[...])
+    out[...] = dot_t(d_send.astype(BF16), w_send[...])
 
 
 def make_last(members):
@@ -613,7 +658,7 @@
     step = lax.axis_size("grp") // 2
     rows = share.shape[0]
     while step:
-        if step == 1:
+        if 2 * step == lax.axis_size("grp"):
             share, summed, tied = lax.optimization_barrier((share, summed, tied))
         other = exchanged(jnp.concatenate([share, summed], 0), "grp", step)
         others = other[:rows]
@@ -661,7 +706,7 @@
         [latent, positions, pos_weight],
         grant=60,
     )
-    messages = [message] + [shifted(message, "grp", distance) for distance in range(1, members)]
+    messages = [message] + [exchanged(message, "grp", distance) for distance in range(1, members)]
     row_rank, row_degree, col_rank, most, vectors = call(
         ranks_kernel,
         [tile_like] * 3 + [most_like, vectors_like],
@@ -751,6 +796,22 @@
         flops=14 * own_rows * width * width,
     )
     d_low, d_high = shifted(d_aggregate, "blk", 1), shifted(d_aggregate, "blk", -1)
+    back_scratch = [
+        pltpu.VMEM((3 * blocks, size, width), BF16),
+        pltpu.VMEM((2, size, width), F32),
+        *tables,
+    ]
+    grads_scratch = pltpu.VMEM((members * blocks, size, width), F32)
+    (started,) = call(
+        back_own,
+        [like((members * blocks, size, width), F32)],
+        [col_rank, senders, receivers, d_aggregate],
+        scalars=[tile_count],
+        far=[most],
+        scratch=back_scratch,
+        flops=tile_flops // 2,
+    )
+    aggregate, started = lax.optimization_barrier((aggregate, started))
     half = 4 * width // 2
     share, given = call(
         early_kernel,
@@ -768,19 +829,26 @@
         share = jnp.where(high, share[half:], share[:half])
         share = share + exchanged(given, "grp", step).astype(F32)
         step *= 2
-    back_scratch = [
-        pltpu.VMEM((3 * blocks, size, width), BF16),
-        pltpu.VMEM((2, size, width), F32),
-        *tables,
-    ]
-    (started,) = call(
-        make_backward(members, blocks, True),
-        [like((members * blocks, size, width), F32)],
-        [col_rank, senders, receivers, d_aggregate],
+    far_grads = call(
+        make_back_far(members),
+        [node_like] * (members - 1),
+        [col_rank, senders, receivers, d_low, d_high, started],
         scalars=[tile_count],
         far=[most],
-        scratch=back_scratch,
-        flops=tile_flops // 2,
+        scratch=back_scratch + [grads_scratch],
+        flops=tile_flops,
+    )
+    back = [
+        exchanged(part, "grp", distance + 1) for distance, part in enumerate(far_grads)
+    ]
+    own_grad, late = call(
+        make_back_near(members),
+        [node_float, like((width, width), BF16)],
+        [col_rank, senders, receivers, d_low, d_high, started, *far_grads, *messages],
+        scalars=[tile_count],
+        far=[most],
+        scratch=back_scratch + [grads_scratch],
+        flops=tile_flops // 4,
     )
     (recv_grad,) = call(
         recv_kernel,
@@ -798,19 +866,33 @@
         ],
         flops=6 * own_rows * width * width,
     )
-    *send_grads, late = call(
-        make_backward(members, blocks, False),
-        [node_float] + [node_like] * (members - 1) + [like((width, width), BF16)],
-        [col_rank, senders, receivers, d_low, d_high, started, *messages],
-        scalars=[tile_count],
-        far=[most],
-        scratch=back_scratch + [pltpu.VMEM((members * blocks, size, width), F32)],
-        flops=tile_flops,
-    )
-    back = [shifted(send_grads[distance], "grp", -distance) for distance in range(1, members)]
+    (from_send,) = call(
+        return_kernel,
+        [node_float],
+        [w_send, own_grad, *back],
+        flops=2 * own_rows * width * width,
+    )
     count_low, count_high, late = lax.optimization_barrier((count_low, count_high, late))
-    (direct,) = call(
-        direct_kernel,
+    share = share.astype(BF16)
+    chain = jnp.concatenate([share, late, recv_grad], 0)
+    slabs = lax.axis_size("blk")
+    if slabs & (slabs - 1) or slabs == 1:
+        chain = pairwise_sum(chain, "blk")
+        rows = share.shape[0]
+        share, summed, from_send = gather_shares(chain[:rows], chain[rows:], from_send)
+        weight_grads = jnp.concatenate([summed, share], 0).astype(F32)
+    else:
+        mine, given = halves(chain, (share.shape[0], width, width))
+        mine = (mine.astype(F32) + exchanged(given, "blk", 1).astype(F32)).astype(BF16)
+        chain = pairwise_sum(mine, "blk", 2)
+        rows = share.shape[0] // 2
+        share, summed, from_send = gather_shares(chain[:rows], chain[rows:], from_send)
+        mine = jnp.concatenate([share, summed], 0)
+        (weight_grads,) = call(
+            make_last(members), [like((6 * width, width), F32)], [mine, exchanged(mine, "blk", 1)]
+        )
+    (latent_grad,) = call(
+        latent_grad_kernel,
         [node_float],
         [
             cotangent,
@@ -822,33 +904,10 @@
             w_edge_out,
             w_node_self,
             w_recv,
+            from_send,
         ],
         flops=6 * own_rows * width * width,
     )
-    (latent_grad,) = call(
-        return_kernel,
-        [node_float],
-        [direct, w_send, send_grads[0], *back],
-        flops=2 * own_rows * width * width,
-    )
-    share = share.astype(BF16)
-    chain = jnp.concatenate([share, late, recv_grad], 0)
-    slabs = lax.axis_size("blk")
-    if slabs & (slabs - 1) or slabs == 1:
-        chain = pairwise_sum(chain, "blk")
-        rows = share.shape[0]
-        share, summed, latent_grad = gather_shares(chain[:rows], chain[rows:], latent_grad)
-        weight_grads = jnp.concatenate([summed, share], 0).astype(F32)
-    else:
-        mine, given = halves(chain, (share.shape[0], width, width))
-        mine = (mine.astype(F32) + exchanged(given, "blk", 1).astype(F32)).astype(BF16)
-        chain = pairwise_sum(mine, "blk", 2)
-        rows = share.shape[0] // 2
-        share, summed, latent_grad = gather_shares(chain[:rows], chain[rows:], latent_grad)
-        mine = jnp.concatenate([share, summed], 0)
-        (weight_grads,) = call(
-            make_last(members), [like((6 * width, width), F32)], [mine, exchanged(mine, "blk", 1)]
-        )
     return (new_latent, latent_grad, weight_grads.reshape(6, width, width))
 
 

time: 83.8 us -> 95.4 us (1.14)
  waiting for transfers between devices: 23.2 us -> 30.8 us
  starting transfers between devices: 28.4 us -> 23.2 us
  Pallas kernels: 27.3 us -> 31.2 us
  local copies, waits for them, and re-layouts: 2.1 us -> 5.28 us
  other arithmetic: 0.19 us -> 2.6 us
    ppermute x8 -> x14, waiting for transfers between devices: 11.4 us -> 27.6 us  [exchanged(): lax.ppermute(value, axis, [(source, source ^ step) for source in range(co...]
    ppermute x14 -> x8, starting transfers between devices: 20.1 us -> 9.13 us  [shifted(): return lax.ppermute(value, axis, pairs)]
    ppermute x14 -> x8, waiting for transfers between devices: 11.8 us -> 3.13 us  [shifted(): return lax.ppermute(value, axis, pairs)]
    ppermute x8 -> x14, starting transfers between devices: 8.33 us -> 14.1 us  [exchanged(): lax.ppermute(value, axis, [(source, source ^ step) for source in range(co...]
    pallas_call x13 -> x14, Pallas kernels: 27.3 us -> 31.2 us  [call(): pl.pallas_call(kernel, out_shape=[jax.ShapeDtypeStruct(o.shape, o.dtype)...]
    unnamed x36 -> x76, local copies, waits for them, and re-layouts: 2.09 us -> 5.26 us
  transfers between devices with their start and end apart: 22 -> 22, of which waited for: 10 -> 11; matrix products, arithmetic and copies ran while one was open for 0% -> 1% of each run, Pallas kernels for 15% -> 9%
where the time goes in v7:
time: 95.4 us; the launch traced here: 94.9 us
  Pallas kernels  31.2 us (33%)
  waiting for transfers between devices  30.8 us (32%)
  starting transfers between devices  23.2 us (24%)
  local copies, waits for them, and re-layouts  5.28 us (6%)
  other arithmetic  2.6 us (3%)
  between operations  1.89 us (2%)
    pallas_call x14, Pallas kernels, call(): pl.pallas_call(kernel, out_shape=[jax.ShapeDtypeStruct(o.shape, o.dtype)...  31.2 us
    ppermute x14, waiting for transfers between devices, exchanged(): lax.ppermute(value, axis, [(source, source ^ step) for source in range(co...  27.6 us
    ppermute x14, starting transfers between devices, exchanged(): lax.ppermute(value, axis, [(source, source ^ step) for source in range(co...  14.1 us
    ppermute x8, starting transfers between devices, shifted(): return lax.ppermute(value, axis, pairs)  9.13 us
    unnamed x76, local copies, waits for them, and re-layouts  5.26 us
    ppermute x8, waiting for transfers between devices, shifted(): return lax.ppermute(value, axis, pairs)  3.13 us
  transfers between devices with their start and end apart: 22, of which 11 were waited for; matrix products, arithmetic and copies ran while one was open for 1% of the time, Pallas kernels for 9%

profile of v7, /device:TPU:0, one launch (start us, length us, event | category | flops | bytes accessed | tf_op | source)
XLA Modules:
  0.0 94.9 jit_solution(3872870065325414454)
XLA Ops:
  0.6 1.6 %shard_map.185 = (bf16[576,128]{1,0:T(8,128)(2,1)}, bf16[16,384]{1,0:T(8,128)(2,1)}) custom-call(bf16[512,128]{1,0:T(8,128)(2,1)} %latent.5, f32[3,512]{1,0:T(4,128)} %positions.1, f32[3,128]{1,0:T(4,128)} %pos_weight.1), custom_call_target="tpu_custom_call" | custom-call | bytes 298496 | tf_op jit(solution)/shard_map/pallas_call | solution.py:45
  2.2 0.5 collective-permute-start
  2.7 2.9 %collective-permute-start.1 = (bf16[576,128]{1,0:T(8,128)(2,1)}, bf16[576,128]{1,0:T(8,128)(2,1)S(1)}, u32[]{:S(2)}, u32[]{:S(2)}) collective-permute-start(bf16[576,128]{1,0:T(8,128)(2,1)} %get-tuple-element.49.message.refs_3_.own), channel_id=1, source_target_pairs={{0,28},{4,0},{8,4},{12,8},{16,12},{20,16},{24,20},{28,24},{1,29},{... | collective-permute-start | bytes 442376 | tf_op jit(solution)/shard_map/ppermute | solution.py:23
  5.6 2.3 %collective-permute-start.2 = (bf16[576,128]{1,0:T(8,128)(2,1)}, bf16[576,128]{1,0:T(8,128)(2,1)S(1)}, u32[]{:S(2)}, u32[]{:S(2)}) collective-permute-start(bf16[576,128]{1,0:T(8,128)(2,1)} %get-tuple-element.49.message.refs_3_.own), channel_id=1, source_target_pairs={{0,1},{1,0},{2,3},{3,2},{4,5},{5,4},{6,7},{7,6},{8,9},{9,8},{10,11... | collective-permute-start | bytes 442376 | tf_op jit(solution)/shard_map/ppermute | solution.py:598
  7.9 2.6 %collective-permute-start.3 = (bf16[576,128]{1,0:T(8,128)(2,1)}, bf16[576,128]{1,0:T(8,128)(2,1)S(1)}, u32[]{:S(2)}, u32[]{:S(2)}) collective-permute-start(bf16[576,128]{1,0:T(8,128)(2,1)} %get-tuple-element.49.message.refs_3_.own), channel_id=1, source_target_pairs={{0,2},{1,3},{2,0},{3,1},{4,6},{5,7},{6,4},{7,5},{8,10},{9,11},{10,... | collective-permute-start | bytes 442376 | tf_op jit(solution)/shard_map/ppermute | solution.py:598
  11.2 0.6 copy-done.34
  11.9 1.2 %copy-done.1 = s32[1,1,16,128,128]{4,3,2,1,0:T(8,128)S(1)} copy-done((s32[1,1,16,128,128]{4,3,2,1,0:T(8,128)S(1)}, s32[1,1,16,128,128]{4,3,2,1,0:T(8,128)}, u32[]{:S(2)}) %copy-start.1) | copy-done | bytes 1048600
  13.1 0.7 shard_map.184
  14.0 3.6 %shard_map.186 = (bf16[4,128,128]{2,1,0:T(8,128)(2,1)S(1)}, bf16[12,128,128]{2,1,0:T(8,128)(2,1)S(1)}, f32[12,128,128]{2,1,0:T(8,128)S(1)}, f32[12,128,128]{2,1,0:T(8,128)S(1)}) custom-call(s32[1,1]{1,0:T(1,128)S(6)} %copy.20.tile_count, s32[3,24,128]{2,1,0:T(8,128)S(1)} %get-tuple-element.45.most, bf16[17,128,128]{2,1,0:T(8,128)(2,1)S(1)} %get-tuple-element.46.row_rank, ...), custom_call_target="tpu_custom_call" | custom-call | flops 1073741824 | bytes 3772416 | tf_op jit(solution)/shard_map/pallas_call | solution.py:45
  17.6 3.8 %collective-permute-done.3.refs_4_.refs_5_ = bf16[576,128]{1,0:T(8,128)(2,1)S(1)} collective-permute-done((bf16[576,128]{1,0:T(8,128)(2,1)}, bf16[576,128]{1,0:T(8,128)(2,1)S(1)}, u32[]{:S(2)}, u32[]{:S(2)}) %collective-permute-start.3) | collective-permute-done | bytes 147488 | tf_op jit(solution)/shard_map/ppermute | solution.py:598
  21.4 6.0 %shard_map.187 = (bf16[512,128]{1,0:T(8,128)(2,1)S(1)}, bf16[512,128]{1,0:T(8,128)(2,1)S(1)}, bf16[512,128]{1,0:T(8,128)(2,1)S(1)}, bf16[512,128]{1,0:T(8,128)(2,1)S(1)}, bf16[16,128,128]{2,1,0:T(8,128)(2,1)S(1)}) custom-call(s32[1,1]{1,0:T(1,128)S(6)} %copy.20.tile_count, s32[3,24,128]{2,1,0:T(8,128)S(1)} %get-tuple-element.45.most, ...), custom_call_target="tpu_custom_call" | custom-call | flops 2147483648 | bytes 4784128 | tf_op jit(solution)/shard_map/pallas_call | solution.py:45
  27.5 0.6 copy-done.15
  28.1 0.7 copy-done.18
  28.7 2.6 %collective-permute-start.6 = (bf16[512,128]{1,0:T(8,128)(2,1)S(1)}, bf16[512,128]{1,0:T(8,128)(2,1)S(1)}, u32[]{:S(2)}, u32[]{:S(2)}) collective-permute-start(bf16[512,128]{1,0:T(8,128)(2,1)S(1)} %get-tuple-element.57), channel_id=1, source_target_pairs={{0,28},{4,0},{8,4},{12,8},{16,12},{20,16},{24,20},{28,24},{1,29},{... | collective-permute-start | bytes 393224 | tf_op jit(solution)/shard_map/ppermute | solution.py:23
  31.4 3.3 %shard_map.188 = (f32[512,128]{1,0:T(8,128)S(1)}, f32[512,128]{1,0:T(8,128)S(1)}) custom-call(s32[1,1]{1,0:T(1,128)S(6)} %copy.20.tile_count, s32[3,24,128]{2,1,0:T(8,128)S(1)} %get-tuple-element.45.most, bf16[17,128,128]{2,1,0:T(8,128)(2,1)S(1)} %get-tuple-element.46.row_rank, bf16[17,128,128]{2,1,0:T(8,128)(2,1)S(1)} %get-tuple-element.47.row_degree, ...), custom_call_target="tpu_custom_call" | custom-call | flops 1073741824 | bytes 4165632 | tf_op jit(solution)/shard_map/pallas_call | solution.py:45
  34.8 1.7 %shard_map.189 = (bf16[512,128]{1,0:T(8,128)(2,1)}, bf16[512,128]{1,0:T(8,128)(2,1)S(1)}, bf16[512,128]{1,0:T(8,128)(2,1)S(1)}, bf16[512,128]{1,0:T(8,128)(2,1)S...) custom-call(f32[8,128]{1,0:T(8,128)S(1)} %get-tuple-element.44.vecto, ...), custom_call_target="tpu_custom_call" | custom-call | flops 117440512 | bytes 1970176 | tf_op jit(solution)/shard_map/pallas_call | solution.py:45
  36.5 3.7 %shard_map.190.started = f32[16,128,128]{2,1,0:T(8,128)S(1)} custom-call(s32[1,1]{1,0:T(1,128)S(6)} %copy.20.tile_count, s32[3,24,128]{2,1,0:T(8,128)S(1)} %get-tuple-element.45.most, bf16[17,128,128]{2,1,0:T(8,128)(2,1)S(1)} %get-tuple-element.62.col_rank, bf16[16,128,128]{2,1,0:T(8,128)(2,1)S(1)} %get-tuple-element.54.refs_0_.senders, ...), custom_call_target="tpu_custom_call" | custom-call | flops 1073741824 | bytes 2691072 | tf_op jit(solution)/shard_map/pallas_call | solution.py:45
  40.1 1.0 %shard_map.193 = (f32[256,128]{1,0:T(8,128)S(1)}, bf16[256,128]{1,0:T(8,128)(2,1)}) custom-call(bf16[512,128]{1,0:T(8,128)(2,1)S(1)} %copy-done, bf16[512,128]{1,0:T(8,128)(2,1)S(1)} %get-tuple-element.74.aggregate, bf16[512,128]{1,0:T(8,128)(2,1)S(1)} %get-tuple-element.75.message, bf16[512,128]{1,0:T(8,128)(2,1)S(1)} %get-tuple-element.76.hidden, ...), custom_call_target="tpu_custom_call" | custom-call | flops 67108864 | bytes 1114112 | tf_op jit(solution)/shard_map/pallas_call | solution.py:45
  41.2 0.7 copy-done.14
  41.8 5.1 %collective-permute-done.11 = bf16[256,128]{1,0:T(8,128)(2,1)} collective-permute-done((bf16[256,128]{1,0:T(8,128)(2,1)}, bf16[256,128]{1,0:T(8,128)(2,1)}, u32[]{:S(2)}, u32[]{:S(2)}) %collective-permute-start.11) | collective-permute-done | bytes 65568 | tf_op jit(solution)/shard_map/ppermute | solution.py:598
  46.9 0.9 convert_add_fusion
  47.8 0.6 copy-done.37
  48.5 0.6 select_convert_fusion
  49.1 0.1 collective-permute-start.7
  49.2 2.5 %collective-permute-start.8 = (bf16[512,128]{1,0:T(8,128)(2,1)}, bf16[512,128]{1,0:T(8,128)(2,1)S(1)}, u32[]{:S(2)}, u32[]{:S(2)}) collective-permute-start(bf16[512,128]{1,0:T(8,128)(2,1)} %copy-done.21), channel_id=1, source_target_pairs={{0,28},{4,0},{8,4},{12,8},{16,12},{20,16},{24,20},{28,24},{1,29},{... | collective-permute-start | bytes 393224 | tf_op jit(solution)/shard_map/ppermute | solution.py:23
  51.7 2.6 %collective-permute-done.12 = bf16[128,128]{1,0:T(8,128)(2,1)} collective-permute-done((bf16[128,128]{1,0:T(8,128)(2,1)}, bf16[128,128]{1,0:T(8,128)(2,1)}, u32[]{:S(2)}, u32[]{:S(2)}) %collective-permute-start.12) | collective-permute-done | bytes 32800 | tf_op jit(solution)/shard_map/ppermute | solution.py:598
  54.3 0.9 add_convert_fusion.5
  55.3 0.2 collective-permute-done.7.d_low
  55.5 0.6 copy-done.24
  56.0 5.2 %shard_map.191 = (bf16[512,128]{1,0:T(8,128)(2,1)S(1)}, bf16[512,128]{1,0:T(8,128)(2,1)S(1)}, bf16[512,128]{1,0:T(8,128)(2,1)S(1)}) custom-call(s32[1,1]{1,0:T(1,128)S(6)} %copy.20.tile_count, s32[3,24,128]{2,1,0:T(8,128)S(1)} %copy-done.24, bf16[17,128,128]{2,1,0:T(8,128)(2,1)S(1)} %get-tuple-element.62.col_rank, ...), custom_call_target="tpu_custom_call" | custom-call | flops 2147483648 | bytes 3215360 | tf_op jit(solution)/shard_map/pallas_call | solution.py:45
  61.3 2.1 %shard_map.192 = (f32[512,128]{1,0:T(8,128)S(1)}, bf16[128,128]{1,0:T(8,128)(2,1)S(1)}) custom-call(s32[1,1]{1,0:T(1,128)S(6)} %copy.20.tile_count, s32[3,24,128]{2,1,0:T(8,128)S(1)} %copy-done.24, bf16[17,128,128]{2,1,0:T(8,128)(2,1)S(1)} %get-tuple-element.62.col_rank, bf16[16,128,128]{2,1,0:T(8,128)(2,1)S(1)} %get-tuple-element.54.refs_0_.senders, ...), custom_call_target="tpu_custom_call" | custom-call | flops 536870912 | bytes 4100096 | tf_op jit(solution)/shard_map/pallas_call | solution.py:45
  63.5 0.3 shard_map.194
  63.9 1.2 %collective-permute-done.13 = bf16[192,128]{1,0:T(8,128)(2,1)S(1)} collective-permute-done((bf16[192,128]{1,0:T(8,128)(2,1)S(1)}, bf16[192,128]{1,0:T(8,128)(2,1)S(1)}, u32[]{:S(2)}, u32[]{:S(2)}) %collective-permute-start.13) | collective-permute-done | bytes 49184 | tf_op jit(solution)/shard_map/ppermute | solution.py:598
  65.3 2.2 %collective-permute-start.16 = (bf16[512,128]{1,0:T(8,128)(2,1)S(1)}, bf16[512,128]{1,0:T(8,128)(2,1)S(1)}, u32[]{:S(2)}, u32[]{:S(2)}) collective-permute-start(bf16[512,128]{1,0:T(8,128)(2,1)S(1)} %get-tuple-element.66.refs_0_), channel_id=1, source_target_pairs={{0,1},{1,0},{2,3},{3,2},{4,5},{5,4},{6,7},{7,6},{8,9},{9,8},{10,11... | collective-permute-start | bytes 393224 | tf_op jit(solution)/shard_map/ppermute | solution.py:598
  67.4 2.4 %collective-permute-start.18 = (bf16[512,128]{1,0:T(8,128)(2,1)S(1)}, bf16[512,128]{1,0:T(8,128)(2,1)S(1)}, u32[]{:S(2)}, u32[]{:S(2)}) collective-permute-start(bf16[512,128]{1,0:T(8,128)(2,1)S(1)} %get-tuple-element.68.refs_2_), channel_id=1, source_target_pairs={{0,3},{1,2},{2,1},{3,0},{4,7},{5,6},{6,5},{7,4},{8,11},{9,10},{10,... | collective-permute-start | bytes 393224 | tf_op jit(solution)/shard_map/ppermute | solution.py:598
  69.8 0.3 collective-permute-start.15
  70.1 1.4 %collective-permute-done.16.refs_0_ = bf16[512,128]{1,0:T(8,128)(2,1)S(1)} collective-permute-done((bf16[512,128]{1,0:T(8,128)(2,1)S(1)}, bf16[512,128]{1,0:T(8,128)(2,1)S(1)}, u32[]{:S(2)}, u32[]{:S(2)}) %collective-permute-start.16) | collective-permute-done | bytes 131104 | tf_op jit(solution)/shard_map/ppermute | solution.py:598
  71.5 8.2 %collective-permute-done.17.refs_1_ = bf16[512,128]{1,0:T(8,128)(2,1)S(1)} collective-permute-done((bf16[512,128]{1,0:T(8,128)(2,1)S(1)}, bf16[512,128]{1,0:T(8,128)(2,1)S(1)}, u32[]{:S(2)}, u32[]{:S(2)}) %collective-permute-start.17) | collective-permute-done | bytes 131104 | tf_op jit(solution)/shard_map/ppermute | solution.py:598
  79.7 0.2 shard_map.195.from_send
  80.0 2.0 %collective-permute-start.19 = (bf16[192,128]{1,0:T(8,128)(2,1)S(1)}, bf16[192,128]{1,0:T(8,128)(2,1)S(1)}, u32[]{:S(2)}, u32[]{:S(2)}) collective-permute-start(bf16[192,128]{1,0:T(8,128)(2,1)S(1)} %pad_maximum_fusion.4), channel_id=1, source_target_pairs={{0,2},{1,3},{2,0},{3,1},{4,6},{5,7},{6,4},{7,5},{8,10},{9,11},{10,... | collective-permute-start | bytes 147464 | tf_op jit(solution)/shard_map/ppermute | solution.py:598
  82.0 3.6 %collective-permute-done.19 = bf16[192,128]{1,0:T(8,128)(2,1)S(1)} collective-permute-done((bf16[192,128]{1,0:T(8,128)(2,1)S(1)}, bf16[192,128]{1,0:T(8,128)(2,1)S(1)}, u32[]{:S(2)}, u32[]{:S(2)}) %collective-permute-start.19) | collective-permute-done | bytes 49184 | tf_op jit(solution)/shard_map/ppermute | solution.py:598
  85.6 2.1 %collective-permute-start.20 = (bf16[256,128]{1,0:T(8,128)(2,1)S(1)}, bf16[256,128]{1,0:T(8,128)(2,1)S(1)}, u32[]{:S(2)}, u32[]{:S(2)}) collective-permute-start(bf16[256,128]{1,0:T(8,128)(2,1)S(1)} %pad_maximum_fusion.1), channel_id=1, source_target_pairs={{0,1},{1,0},{2,3},{3,2},{4,5},{5,4},{6,7},{7,6},{8,9},{9,8},{10,11... | collective-permute-start | bytes 196616 | tf_op jit(solution)/shard_map/ppermute | solution.py:598
  87.8 0.5 collective-permute-start.9
  88.3 1.7 %collective-permute-done.20 = bf16[256,128]{1,0:T(8,128)(2,1)S(1)} collective-permute-done((bf16[256,128]{1,0:T(8,128)(2,1)S(1)}, bf16[256,128]{1,0:T(8,128)(2,1)S(1)}, u32[]{:S(2)}, u32[]{:S(2)}) %collective-permute-start.20) | collective-permute-done | bytes 65568 | tf_op jit(solution)/shard_map/ppermute | solution.py:598
  90.2 1.4 %collective-permute-done.10.from_high = bf16[512,128]{1,0:T(8,128)(2,1)S(1)} collective-permute-done((bf16[512,128]{1,0:T(8,128)(2,1)S(1)}, bf16[512,128]{1,0:T(8,128)(2,1)S(1)}, u32[]{:S(2)}, u32[]{:S(2)}) %collective-permute-start.10) | collective-permute-done | bytes 131104 | tf_op jit(solution)/shard_map/ppermute | solution.py:23
  91.5 1.6 %collective-permute-done.9.from_low = bf16[512,128]{1,0:T(8,128)(2,1)S(1)} collective-permute-done((bf16[512,128]{1,0:T(8,128)(2,1)S(1)}, bf16[512,128]{1,0:T(8,128)(2,1)S(1)}, u32[]{:S(2)}, u32[]{:S(2)}) %collective-permute-start.9) | collective-permute-done | bytes 131104 | tf_op jit(solution)/shard_map/ppermute | solution.py:23
  93.1 1.0 %shard_map.196 = f32[512,128]{1,0:T(8,128)} custom-call(bf16[512,128]{1,0:T(8,128)(2,1)S(1)} %copy-done.3, f32[512,128]{1,0:T(8,128)S(1)} %get-tuple-element.59.n_own.count_own, bf16[512,128]{1,0:T(8,128)(2,1)S(1)} %collective-permute-done.9.from_low, bf16[512,128]{1,0:T(8,128)(2,1)S(1)} %collective-permute-done.10.from_high, ...), custom_call_target="tpu_custom_call" | custom-call | flops 50331648 | bytes 1540096 | tf_op jit(solution)/shard_map/pallas_call | solution.py:45
  94.2 0.8 shard_map.197
  (104 shorter events, 0.7 us)
Async XLA Ops:
  2.2 11.6 %collective-permute-start = (bf16[576,128]{1,0:T(8,128)(2,1)}, bf16[576,128]{1,0:T(8,128)(2,1)S(1)}, u32[]{:S(2)}, u32[]{:S(2)}) collective-permute-start(bf16[576,128]{1,0:T(8,128)(2,1)} %get-tuple-element.49.message.refs_3_.own), channel_id=1, source_target_pairs={{0,4},{4,8},{8,12},{12,16},{16,20},{20,24},{24,28},{28,0},{1,5},{5... | collective-permute-start | bytes 442376 | tf_op jit(solution)/shard_map/ppermute | solution.py:23
  2.7 11.2 %collective-permute-start.1 = (bf16[576,128]{1,0:T(8,128)(2,1)}, bf16[576,128]{1,0:T(8,128)(2,1)S(1)}, u32[]{:S(2)}, u32[]{:S(2)}) collective-permute-start(bf16[576,128]{1,0:T(8,128)(2,1)} %get-tuple-element.49.message.refs_3_.own), channel_id=1, source_target_pairs={{0,28},{4,0},{8,4},{12,8},{16,12},{20,16},{24,20},{28,24},{1,29},{... | collective-permute-start | bytes 442376 | tf_op jit(solution)/shard_map/ppermute | solution.py:23
  5.6 12.0 %collective-permute-start.2 = (bf16[576,128]{1,0:T(8,128)(2,1)}, bf16[576,128]{1,0:T(8,128)(2,1)S(1)}, u32[]{:S(2)}, u32[]{:S(2)}) collective-permute-start(bf16[576,128]{1,0:T(8,128)(2,1)} %get-tuple-element.49.message.refs_3_.own), channel_id=1, source_target_pairs={{0,1},{1,0},{2,3},{3,2},{4,5},{5,4},{6,7},{7,6},{8,9},{9,8},{10,11... | collective-permute-start | bytes 442376 | tf_op jit(solution)/shard_map/ppermute | solution.py:598
  7.9 13.5 %collective-permute-start.3 = (bf16[576,128]{1,0:T(8,128)(2,1)}, bf16[576,128]{1,0:T(8,128)(2,1)S(1)}, u32[]{:S(2)}, u32[]{:S(2)}) collective-permute-start(bf16[576,128]{1,0:T(8,128)(2,1)} %get-tuple-element.49.message.refs_3_.own), channel_id=1, source_target_pairs={{0,2},{1,3},{2,0},{3,1},{4,6},{5,7},{6,4},{7,5},{8,10},{9,11},{10,... | collective-permute-start | bytes 442376 | tf_op jit(solution)/shard_map/ppermute | solution.py:598
  10.5 10.9 %collective-permute-start.4 = (bf16[576,128]{1,0:T(8,128)(2,1)}, bf16[576,128]{1,0:T(8,128)(2,1)S(1)}, u32[]{:S(2)}, u32[]{:S(2)}) collective-permute-start(bf16[576,128]{1,0:T(8,128)(2,1)} %get-tuple-element.49.message.refs_3_.own), channel_id=1, source_target_pairs={{0,3},{1,2},{2,1},{3,0},{4,7},{5,6},{6,5},{7,4},{8,11},{9,10},{10,... | collective-permute-start | bytes 442376 | tf_op jit(solution)/shard_map/ppermute | solution.py:598
  11.9 1.2 %copy-start.1 = (s32[1,1,16,128,128]{4,3,2,1,0:T(8,128)S(1)}, s32[1,1,16,128,128]{4,3,2,1,0:T(8,128)}, u32[]{:S(2)}) copy-start(s32[1,1,16,128,128]{4,3,2,1,0:T(8,128)} %param.21) | copy-start | bytes 3145732
  13.1 0.9 copy-start.29
  13.1 0.9 copy-start.36
  13.9 22.6 %copy-start.23 = (s32[3,24,128]{2,1,0:T(8,128)}, s32[3,24,128]{2,1,0:T(8,128)S(1)}, u32[]{:S(2)}) copy-start(s32[3,24,128]{2,1,0:T(8,128)S(1)} %get-tuple-element.45.most) | copy-start | bytes 110596
  13.9 3.7 %copy-start.8 = (bf16[576,128]{1,0:T(8,128)(2,1)}, bf16[576,128]{1,0:T(8,128)(2,1)S(1)}, u32[]{:S(2)}) copy-start(bf16[576,128]{1,0:T(8,128)(2,1)S(1)} %collective-permute-done.low) | copy-start | bytes 442372
  13.9 3.7 %copy-start.10 = (bf16[576,128]{1,0:T(8,128)(2,1)}, bf16[576,128]{1,0:T(8,128)(2,1)S(1)}, u32[]{:S(2)}) copy-start(bf16[576,128]{1,0:T(8,128)(2,1)S(1)} %collective-permute-done.1.high) | copy-start | bytes 442372
  21.4 6.0 %copy-start.4 = (bf16[576,128]{1,0:T(8,128)(2,1)}, bf16[576,128]{1,0:T(8,128)(2,1)S(1)}, u32[]{:S(2)}) copy-start(bf16[576,128]{1,0:T(8,128)(2,1)S(1)} %collective-permute-done.3.refs_4_.refs_5_) | copy-start | bytes 442372
  21.4 6.0 %copy-start.6 = (bf16[576,128]{1,0:T(8,128)(2,1)}, bf16[576,128]{1,0:T(8,128)(2,1)S(1)}, u32[]{:S(2)}) copy-start(bf16[576,128]{1,0:T(8,128)(2,1)S(1)} %collective-permute-done.4.refs_5_.refs_6_) | copy-start | bytes 442372
  28.7 6.0 %collective-permute-start.5 = (bf16[512,128]{1,0:T(8,128)(2,1)S(1)}, bf16[512,128]{1,0:T(8,128)(2,1)S(1)}, u32[]{:S(2)}, u32[]{:S(2)}) collective-permute-start(bf16[512,128]{1,0:T(8,128)(2,1)S(1)} %get-tuple-element.56), channel_id=1, source_target_pairs={{0,4},{4,8},{8,12},{12,16},{16,20},{20,24},{24,28},{28,0},{1,5},{5... | collective-permute-start | bytes 393224 | tf_op jit(solution)/shard_map/ppermute | solution.py:23
  28.7 6.0 %collective-permute-start.6 = (bf16[512,128]{1,0:T(8,128)(2,1)S(1)}, bf16[512,128]{1,0:T(8,128)(2,1)S(1)}, u32[]{:S(2)}, u32[]{:S(2)}) collective-permute-start(bf16[512,128]{1,0:T(8,128)(2,1)S(1)} %get-tuple-element.57), channel_id=1, source_target_pairs={{0,28},{4,0},{8,4},{12,8},{16,12},{20,16},{24,20},{28,24},{1,29},{... | collective-permute-start | bytes 393224 | tf_op jit(solution)/shard_map/ppermute | solution.py:23
  31.4 3.3 %copy-start = (bf16[512,128]{1,0:T(8,128)(2,1)S(1)}, bf16[512,128]{1,0:T(8,128)(2,1)}, u32[]{:S(2)}) copy-start(bf16[512,128]{1,0:T(8,128)(2,1)} %latent.5) | copy-start | bytes 393220
  31.4 3.3 %copy-start.3 = (bf16[512,128]{1,0:T(8,128)(2,1)S(1)}, bf16[512,128]{1,0:T(8,128)(2,1)}, u32[]{:S(2)}) copy-start(bf16[512,128]{1,0:T(8,128)(2,1)} %cotangent.3) | copy-start | bytes 393220
  31.4 3.3 %copy-start.12 = (bf16[128,128]{1,0:T(8,128)(2,1)S(1)}, bf16[128,128]{1,0:T(8,128)(2,1)}, u32[]{:S(2)}) copy-start(bf16[128,128]{1,0:T(8,128)(2,1)} %w_edge_out.3) | copy-start | bytes 98308
  31.4 3.3 %copy-start.13 = (bf16[128,128]{1,0:T(8,128)(2,1)S(1)}, bf16[128,128]{1,0:T(8,128)(2,1)}, u32[]{:S(2)}) copy-start(bf16[128,128]{1,0:T(8,128)(2,1)} %w_node_self.3) | copy-start | bytes 98308
  31.4 3.4 %copy-start.25 = (bf16[128,128]{1,0:T(8,128)(2,1)S(1)}, bf16[128,128]{1,0:T(8,128)(2,1)}, u32[]{:S(2)}) copy-start(bf16[128,128]{1,0:T(8,128)(2,1)} %w_node_msg.1) | copy-start | bytes 98308
  31.4 3.4 %copy-start.26 = (bf16[128,128]{1,0:T(8,128)(2,1)S(1)}, bf16[128,128]{1,0:T(8,128)(2,1)}, u32[]{:S(2)}) copy-start(bf16[128,128]{1,0:T(8,128)(2,1)} %w_node_out.1) | copy-start | bytes 98308
  36.5 3.7 %copy-start.21 = (bf16[512,128]{1,0:T(8,128)(2,1)}, bf16[512,128]{1,0:T(8,128)(2,1)S(1)}, u32[]{:S(2)}) copy-start(bf16[512,128]{1,0:T(8,128)(2,1)S(1)} %get-tuple-element.63.d_own) | copy-start | bytes 393220
  41.8 5.1 %collective-permute-start.11 = (bf16[256,128]{1,0:T(8,128)(2,1)}, bf16[256,128]{1,0:T(8,128)(2,1)}, u32[]{:S(2)}, u32[]{:S(2)}) collective-permute-start(bf16[256,128]{1,0:T(8,128)(2,1)} %get-tuple-element.79), channel_id=1, source_target_pairs={{0,1},{1,0},{2,3},{3,2},{4,5},{5,4},{6,7},{7,6},{8,9},{9,8},{10,11... | collective-permute-start | bytes 196616 | tf_op jit(solution)/shard_map/ppermute | solution.py:598
  49.1 5.2 %collective-permute-start.12 = (bf16[128,128]{1,0:T(8,128)(2,1)}, bf16[128,128]{1,0:T(8,128)(2,1)}, u32[]{:S(2)}, u32[]{:S(2)}) collective-permute-start(bf16[128,128]{1,0:T(8,128)(2,1)} %select_convert_fusion), channel_id=1, source_target_pairs={{0,2},{1,3},{2,0},{3,1},{4,6},{5,7},{6,4},{7,5},{8,10},{9,11},{10,... | collective-permute-start | bytes 98312 | tf_op jit(solution)/shard_map/ppermute | solution.py:598
  49.1 6.4 %collective-permute-start.7 = (bf16[512,128]{1,0:T(8,128)(2,1)}, bf16[512,128]{1,0:T(8,128)(2,1)S(1)}, u32[]{:S(2)}, u32[]{:S(2)}) collective-permute-start(bf16[512,128]{1,0:T(8,128)(2,1)} %copy-done.21), channel_id=1, source_target_pairs={{0,4},{4,8},{8,12},{12,16},{16,20},{20,24},{24,28},{28,0},{1,5},{5... | collective-permute-start | bytes 393224 | tf_op jit(solution)/shard_map/ppermute | solution.py:23
  49.2 6.2 %collective-permute-start.8 = (bf16[512,128]{1,0:T(8,128)(2,1)}, bf16[512,128]{1,0:T(8,128)(2,1)S(1)}, u32[]{:S(2)}, u32[]{:S(2)}) collective-permute-start(bf16[512,128]{1,0:T(8,128)(2,1)} %copy-done.21), channel_id=1, source_target_pairs={{0,28},{4,0},{8,4},{12,8},{16,12},{20,16},{24,20},{28,24},{1,29},{... | collective-permute-start | bytes 393224 | tf_op jit(solution)/shard_map/ppermute | solution.py:23
  55.3 6.0 %copy-start.5 = (bf16[576,128]{1,0:T(8,128)(2,1)S(1)}, bf16[576,128]{1,0:T(8,128)(2,1)}, u32[]{:S(2)}) copy-start(bf16[576,128]{1,0:T(8,128)(2,1)} %copy-done.4) | copy-start | bytes 442372
  55.3 6.0 %copy-start.7 = (bf16[576,128]{1,0:T(8,128)(2,1)S(1)}, bf16[576,128]{1,0:T(8,128)(2,1)}, u32[]{:S(2)}) copy-start(bf16[576,128]{1,0:T(8,128)(2,1)} %copy-done.6) | copy-start | bytes 442372
  61.3 2.2 %copy-start.9 = (bf16[576,128]{1,0:T(8,128)(2,1)S(1)}, bf16[576,128]{1,0:T(8,128)(2,1)}, u32[]{:S(2)}) copy-start(bf16[576,128]{1,0:T(8,128)(2,1)} %copy-done.8) | copy-start | bytes 442372
  61.3 2.2 %copy-start.11 = (bf16[576,128]{1,0:T(8,128)(2,1)S(1)}, bf16[576,128]{1,0:T(8,128)(2,1)}, u32[]{:S(2)}) copy-start(bf16[576,128]{1,0:T(8,128)(2,1)} %copy-done.10) | copy-start | bytes 442372
  61.3 2.2 %copy-start.16 = (bf16[512,128]{1,0:T(8,128)(2,1)S(1)}, bf16[512,128]{1,0:T(8,128)(2,1)}, u32[]{:S(2)}) copy-start(bf16[512,128]{1,0:T(8,128)(2,1)} %copy-done.15) | copy-start | bytes 393220
  61.3 2.2 %copy-start.19 = (bf16[512,128]{1,0:T(8,128)(2,1)S(1)}, bf16[512,128]{1,0:T(8,128)(2,1)}, u32[]{:S(2)}) copy-start(bf16[512,128]{1,0:T(8,128)(2,1)} %copy-done.18) | copy-start | bytes 393220
  61.3 2.2 %copy-start.22 = (bf16[512,128]{1,0:T(8,128)(2,1)S(1)}, bf16[512,128]{1,0:T(8,128)(2,1)}, u32[]{:S(2)}) copy-start(bf16[512,128]{1,0:T(8,128)(2,1)} %copy-done.21) | copy-start | bytes 393220
  63.9 1.3 %collective-permute-start.13 = (bf16[192,128]{1,0:T(8,128)(2,1)S(1)}, bf16[192,128]{1,0:T(8,128)(2,1)S(1)}, u32[]{:S(2)}, u32[]{:S(2)}) collective-permute-start(bf16[192,128]{1,0:T(8,128)(2,1)S(1)} %broadcast_select_fusion), channel_id=1, source_target_pairs={{0,4},{4,0},{8,12},{12,8},{16,20},{20,16},{24,28},{28,24},{1,5},{5... | collective-permute-start | bytes 147464 | tf_op jit(solution)/shard_map/ppermute | solution.py:598
  65.2 14.6 %copy-start.30 = (bf16[128,128]{1,0:T(8,128)(2,1)S(1)}, bf16[128,128]{1,0:T(8,128)(2,1)}, u32[]{:S(2)}) copy-start(bf16[128,128]{1,0:T(8,128)(2,1)} %w_send.3) | copy-start | bytes 98308
  65.2 4.6 %collective-permute-start.14 = (bf16[192,128]{1,0:T(8,128)(2,1)S(1)}, bf16[192,128]{1,0:T(8,128)(2,1)S(1)}, u32[]{:S(2)}, u32[]{:S(2)}) collective-permute-start(bf16[192,128]{1,0:T(8,128)(2,1)S(1)} %add_convert_fusion.2), channel_id=1, source_target_pairs={{0,8},{4,12},{8,0},{12,4},{16,24},{20,28},{24,16},{28,20},{1,9},{5... | collective-permute-start | bytes 147464 | tf_op jit(solution)/shard_map/ppermute | solution.py:598
  65.3 6.2 %collective-permute-start.16 = (bf16[512,128]{1,0:T(8,128)(2,1)S(1)}, bf16[512,128]{1,0:T(8,128)(2,1)S(1)}, u32[]{:S(2)}, u32[]{:S(2)}) collective-permute-start(bf16[512,128]{1,0:T(8,128)(2,1)S(1)} %get-tuple-element.66.refs_0_), channel_id=1, source_target_pairs={{0,1},{1,0},{2,3},{3,2},{4,5},{5,4},{6,7},{7,6},{8,9},{9,8},{10,11... | collective-permute-start | bytes 393224 | tf_op jit(solution)/shard_map/ppermute | solution.py:598
  67.4 12.3 %collective-permute-start.17 = (bf16[512,128]{1,0:T(8,128)(2,1)S(1)}, bf16[512,128]{1,0:T(8,128)(2,1)S(1)}, u32[]{:S(2)}, u32[]{:S(2)}) collective-permute-start(bf16[512,128]{1,0:T(8,128)(2,1)S(1)} %get-tuple-element.67.refs_1_), channel_id=1, source_target_pairs={{0,2},{1,3},{2,0},{3,1},{4,6},{5,7},{6,4},{7,5},{8,10},{9,11},{10,... | collective-permute-start | bytes 393224 | tf_op jit(solution)/shard_map/ppermute | solution.py:598
  67.4 12.3 %collective-permute-start.18 = (bf16[512,128]{1,0:T(8,128)(2,1)S(1)}, bf16[512,128]{1,0:T(8,128)(2,1)S(1)}, u32[]{:S(2)}, u32[]{:S(2)}) collective-permute-start(bf16[512,128]{1,0:T(8,128)(2,1)S(1)} %get-tuple-element.68.refs_2_), channel_id=1, source_target_pairs={{0,3},{1,2},{2,1},{3,0},{4,7},{5,6},{6,5},{7,4},{8,11},{9,10},{10,... | collective-permute-start | bytes 393224 | tf_op jit(solution)/shard_map/ppermute | solution.py:598
  69.8 10.1 %collective-permute-start.15 = (bf16[192,128]{1,0:T(8,128)(2,1)S(1)}, bf16[192,128]{1,0:T(8,128)(2,1)S(1)}, u32[]{:S(2)}, u32[]{:S(2)}) collective-permute-start(bf16[192,128]{1,0:T(8,128)(2,1)S(1)} %add_convert_fusion.1), channel_id=1, source_target_pairs={{0,16},{4,20},{8,24},{12,28},{16,0},{20,4},{24,8},{28,12},{1,17},{... | collective-permute-start | bytes 147464 | tf_op jit(solution)/shard_map/ppermute | solution.py:598
  80.0 5.6 %collective-permute-start.19 = (bf16[192,128]{1,0:T(8,128)(2,1)S(1)}, bf16[192,128]{1,0:T(8,128)(2,1)S(1)}, u32[]{:S(2)}, u32[]{:S(2)}) collective-permute-start(bf16[192,128]{1,0:T(8,128)(2,1)S(1)} %pad_maximum_fusion.4), channel_id=1, source_target_pairs={{0,2},{1,3},{2,0},{3,1},{4,6},{5,7},{6,4},{7,5},{8,10},{9,11},{10,... | collective-permute-start | bytes 147464 | tf_op jit(solution)/shard_map/ppermute | solution.py:598
  85.6 2.2 %copy-start.20 = (bf16[512,128]{1,0:T(8,128)(2,1)S(1)}, bf16[512,128]{1,0:T(8,128)(2,1)}, u32[]{:S(2)}) copy-start(bf16[512,128]{1,0:T(8,128)(2,1)} %copy-done.18) | copy-start | bytes 393220
  85.6 2.2 %copy-start.17 = (bf16[512,128]{1,0:T(8,128)(2,1)S(1)}, bf16[512,128]{1,0:T(8,128)(2,1)}, u32[]{:S(2)}) copy-start(bf16[512,128]{1,0:T(8,128)(2,1)} %copy-done.15) | copy-start | bytes 393220
  85.6 4.4 %collective-permute-start.20 = (bf16[256,128]{1,0:T(8,128)(2,1)S(1)}, bf16[256,128]{1,0:T(8,128)(2,1)S(1)}, u32[]{:S(2)}, u32[]{:S(2)}) collective-permute-start(bf16[256,128]{1,0:T(8,128)(2,1)S(1)} %pad_maximum_fusion.1), channel_id=1, source_target_pairs={{0,1},{1,0},{2,3},{3,2},{4,5},{5,4},{6,7},{7,6},{8,9},{9,8},{10,11... | collective-permute-start | bytes 196616 | tf_op jit(solution)/shard_map/ppermute | solution.py:598
  87.8 3.8 %collective-permute-start.10 = (bf16[512,128]{1,0:T(8,128)(2,1)S(1)}, bf16[512,128]{1,0:T(8,128)(2,1)S(1)}, u32[]{:S(2)}, u32[]{:S(2)}) collective-permute-start(bf16[512,128]{1,0:T(8,128)(2,1)S(1)} %copy-done.20), channel_id=1, source_target_pairs={{0,28},{4,0},{8,4},{12,8},{16,12},{20,16},{24,20},{28,24},{1,29},{... | collective-permute-start | bytes 393224 | tf_op jit(solution)/shard_map/ppermute | solution.py:23
  87.8 5.3 %collective-permute-start.9 = (bf16[512,128]{1,0:T(8,128)(2,1)S(1)}, bf16[512,128]{1,0:T(8,128)(2,1)S(1)}, u32[]{:S(2)}, u32[]{:S(2)}) collective-permute-start(bf16[512,128]{1,0:T(8,128)(2,1)S(1)} %copy-done.17), channel_id=1, source_target_pairs={{0,4},{4,8},{8,12},{12,16},{16,20},{20,24},{24,28},{28,0},{1,5},{5... | collective-permute-start | bytes 393224 | tf_op jit(solution)/shard_map/ppermute | solution.py:23
  90.0 3.1 %copy-start.28 = (bf16[128,128]{1,0:T(8,128)(2,1)S(1)}, bf16[128,128]{1,0:T(8,128)(2,1)}, u32[]{:S(2)}) copy-start(bf16[128,128]{1,0:T(8,128)(2,1)} %w_recv.3) | copy-start | bytes 98308
  90.1 4.1 %collective-permute-start.21 = (bf16[384,128]{1,0:T(8,128)(2,1)S(1)}, bf16[384,128]{1,0:T(8,128)(2,1)S(1)}, u32[]{:S(2)}, u32[]{:S(2)}) collective-permute-start(bf16[384,128]{1,0:T(8,128)(2,1)S(1)} %pad_maximum_fusion.mine), channel_id=1, source_target_pairs={{0,4},{4,0},{8,12},{12,8},{16,20},{20,16},{24,28},{28,24},{1,5},{5... | collective-permute-start | bytes 294920 | tf_op jit(solution)/shard_map/ppermute | solution.py:598
  (12 other events, 8.5 us)

commit v8 on v6

--- a/solution.py
+++ b/solution.py
@@ -145,12 +145,12 @@
     return (found + 1) // 2
 
 
-def pair_of(pair, order, table, tiles, member, members, blocks):
+def pair_of(pair, order, table, tiles, member, blocks):
     pair_tiles = [order[2 * pair], order[2 * pair + 1]]
     named = [pair_tiles[0], jnp.where(pair_tiles[1] == tiles, pair_tiles[0], pair_tiles[1])]
     recv_places = [table[RECEIVERS, tile] for tile in named]
     send_places = [
-        sender_place(table[SENDERS, tile], member, members, blocks) for tile in named
+        sender_place(table[SENDERS, tile], member, blocks) for tile in named
     ]
     return pair_tiles, recv_places, send_places
 
@@ -205,8 +205,8 @@
             place += 1
 
 
-def sender_place(block, member, members, blocks):
-    distance = lax.rem(member - block // blocks + members, members)
+def sender_place(block, member, blocks):
+    distance = member ^ (block // blocks)
     return distance * blocks + lax.rem(block, blocks)
 
 
@@ -227,7 +227,7 @@
         table[start + block] = found[block * size : (block + 1) * size, :].astype(BF16)
 
 
-def forward_tiles(member, members, tables, ranks_in, rows_in, sums, counts, wanted):
+def forward_tiles(member, tables, ranks_in, rows_in, sums, counts, wanted):
     tile_count, row_most, table, order, total, count = tables
     row_rank, row_degree = ranks_in
     senders, receivers = rows_in
@@ -237,7 +237,7 @@
 
     def one_pair(pair, carry):
         pair_tiles, recv_places, send_places = pair_of(
-            pair, order, table, tiles, member, members, blocks
+            pair, order, table, tiles, member, blocks
         )
         nothing = jnp.zeros((size, width), BF16)
         upper = jnp.concatenate([senders[send_places[0]], nothing], 1)
@@ -317,7 +317,6 @@
         member = lax.axis_index("grp")
         forward_tiles(
             member,
-            members,
             (tile_count, row_most, table, order, total, count),
             (row_rank, row_degree),
             (senders, receivers),
@@ -358,7 +357,6 @@
         member = lax.axis_index("grp")
         forward_tiles(
             member,
-            members,
             (tile_count, row_most, table, order, total, count),
             (row_rank, row_degree),
             (senders, receivers),
@@ -429,18 +427,18 @@
     d_message_out[...] = d_message
 
 
-def early_kernel(
-    latent, aggregate, message, hidden, d_update, d_hidden_pre, d_message, keep, give, grads
-):
+def early_kernel(latent, aggregate, message, hidden, d_update, d_hidden_pre, d_message, *refs):
+    shares, grads = refs[:-1], refs[-1]
     width = latent.shape[1]
     grads[0:width, :] = contract_rows(aggregate[...], d_message[...])
     grads[width : 2 * width, :] = contract_rows(latent[...], d_hidden_pre[...])
     grads[2 * width : 3 * width, :] = contract_rows(message[...], d_hidden_pre[...])
     grads[3 * width : 4 * width, :] = contract_rows(hidden[...], d_update[...])
-    half = keep.shape[0]
-    bit = lax.axis_index("grp") & 1
-    keep[...] = grads[pl.ds(pl.multiple_of(bit * half, half), half), :]
-    give[...] = grads[pl.ds(pl.multiple_of((1 - bit) * half, half), half), :].astype(BF16)
+    rows = shares[0].shape[0]
+    member = lax.axis_index("grp")
+    for distance, share in enumerate(shares):
+        start = pl.multiple_of((member ^ distance) * rows, rows)
+        share[...] = grads[pl.ds(start, rows), :].astype(share.dtype)
 
 
 def recv_kernel(low, own, high, d_low, d_own, d_high, n_low, n_own, n_high, grad_out):
@@ -451,7 +449,7 @@
     grad_out[...] = total.astype(BF16)
 
 
-def direct_kernel(
+def latent_grad_kernel(
     cotangent,
     count_own,
     from_low,
@@ -461,13 +459,15 @@
     w_edge_out,
     w_node_self,
     w_recv,
-    direct_out,
+    from_send,
+    latent_grad,
 ):
     count = count_own[...] + from_low[...].astype(F32) + from_high[...].astype(F32)
     d_recv = (dot_t(d_message[...], w_edge_out[...]) * count).astype(BF16)
-    direct_out[...] = (
+    latent_grad[...] = (
         cotangent[...].astype(F32)
         + dot_t(d_hidden_pre[...], w_node_self[...])
+        + from_send[...]
         + dot_t(d_recv, w_recv[...])
     )
 
@@ -501,7 +501,7 @@
 
         def one_pair(pair, carry):
             pair_tiles, recv_places, send_places = pair_of(
-                pair, order, table, tiles, member, members, blocks
+                pair, order, table, tiles, member, blocks
             )
             rights = []
             for recv_place, send_place in zip(recv_places, send_places):
@@ -537,12 +537,12 @@
         if own:
             return
         late = jnp.zeros((width, width), F32)
-        for distance, out in enumerate(grads_out):
+        for distance, (message, out) in enumerate(zip(messages, grads_out)):
             for block in range(blocks):
                 span = slice(block * size, (block + 1) * size)
                 found = grads[distance * blocks + block]
                 out[span, :] = found.astype(out.dtype)
-                late = late + contract_rows(messages[distance][span, :], found.astype(BF16))
+                late = late + contract_rows(message[span, :], found.astype(BF16))
         late_out[...] = late.astype(BF16)
 
     return kernel
@@ -557,34 +557,47 @@
     return (lax.axis_index(axis) & step) != 0
 
 
-def pairwise_sum(value, axis, step=1):
+def tree_sum(parts):
+    while len(parts) > 1:
+        parts = [parts[item] + parts[item + 1] for item in range(0, len(parts), 2)]
+    return parts[0]
+
+
+def all_parts(value, axis, least=1):
     count = lax.axis_size(axis)
-    if count & (count - 1):
-        return lax.psum(value.astype(F32), axis).astype(BF16)
-    while step < count:
-        value = (value.astype(F32) + exchanged(value, axis, step).astype(F32)).astype(BF16)
-        step *= 2
-    return value
-
-
-def return_kernel(direct, w_send, own, *refs):
-    back, latent_grad = refs[:-1], refs[-1]
+    return [value] + [exchanged(value, axis, step) for step in range(least, count, least)]
+
+
+def return_kernel(w_send, own, *refs):
+    back, out = refs[:-1], refs[-1]
     d_send = own[...]
     for part in back:
         d_send = d_send + part[...].astype(F32)
-    latent_grad[...] = direct[...] + dot_t(d_send.astype(BF16), w_send[...])
+    out[...] = dot_t(d_send.astype(BF16), w_send[...])
+
+
+def make_gather(rows):
+    def kernel(*refs):
+        parts, out = refs[:-1], refs[-1]
+        for distance, part in enumerate(parts):
+            out[distance * rows : (distance + 1) * rows, :] = part[0:rows, :]
+        rest = [part[rows:, :].astype(F32) for part in parts]
+        out[len(parts) * rows :, :] = tree_sum(rest).astype(BF16)
+
+    return kernel
 
 
 def make_last(members):
     def kernel(mine, other, weight_grads):
         bit = lax.axis_index("blk") & 1
+        member = lax.axis_index("grp")
         for part, place in ((mine, bit), (other, 1 - bit)):
             early = 2 * weight_grads.shape[0] // 6
             half = (weight_grads.shape[0] - early) // (2 * members)
             quarter = early // 4
-            for item in range(members):
-                start = pl.multiple_of(early + (2 * item + place) * half, half)
-                span = slice(item * half, (item + 1) * half)
+            for distance in range(members):
+                start = pl.multiple_of(early + (2 * (member ^ distance) + place) * half, half)
+                span = slice(distance * half, (distance + 1) * half)
                 weight_grads[pl.ds(start, half), :] = part[span, :].astype(F32)
             for item in range(2):
                 start = pl.multiple_of((2 * item + place) * quarter, quarter)
@@ -607,22 +620,6 @@
     lows = jnp.concatenate([part[0] for part in parts], 0)
     highs = jnp.concatenate([part[1] for part in parts], 0)
     return jnp.where(high, highs, lows), jnp.where(high, lows, highs)
-
-
-def gather_shares(share, summed, tied):
-    step = lax.axis_size("grp") // 2
-    rows = share.shape[0]
-    while step:
-        if step == 1:
-            share, summed, tied = lax.optimization_barrier((share, summed, tied))
-        other = exchanged(jnp.concatenate([share, summed], 0), "grp", step)
-        others = other[:rows]
-        high = bit_set("grp", step)
-        share = jnp.concatenate([jnp.where(high, others, share), jnp.where(high, share, others)], 0)
-        summed = (summed.astype(F32) + other[rows:].astype(F32)).astype(BF16)
-        rows *= 2
-        step //= 2
-    return share, summed, tied
 
 
 def body(
@@ -661,7 +658,7 @@
         [latent, positions, pos_weight],
         grant=60,
     )
-    messages = [message] + [shifted(message, "grp", distance) for distance in range(1, members)]
+    messages = [message] + [exchanged(message, "grp", distance) for distance in range(1, members)]
     row_rank, row_degree, col_rank, most, vectors = call(
         ranks_kernel,
         [tile_like] * 3 + [most_like, vectors_like],
@@ -751,23 +748,16 @@
         flops=14 * own_rows * width * width,
     )
     d_low, d_high = shifted(d_aggregate, "blk", 1), shifted(d_aggregate, "blk", -1)
-    half = 4 * width // 2
-    share, given = call(
+    rows = 4 * width // members
+    share, *given = call(
         early_kernel,
-        [like((half, width), F32), like((half, width), BF16)],
+        [like((rows, width), F32)] + [like((rows, width), BF16)] * (members - 1),
         [latent, aggregate, message_out, hidden, d_update, d_hidden_pre, d_message],
-        scratch=[pltpu.VMEM((2 * half, width), F32)],
+        scratch=[pltpu.VMEM((4 * width, width), F32)],
         flops=8 * own_rows * width * width,
     )
-    share = share + exchanged(given, "grp", 1).astype(F32)
-    step = 2
-    while step < members:
-        half = share.shape[0] // 2
-        high = bit_set("grp", step)
-        given = jnp.where(high, share[:half], share[half:]).astype(BF16)
-        share = jnp.where(high, share[half:], share[:half])
-        share = share + exchanged(given, "grp", step).astype(F32)
-        step *= 2
+    for distance, part in enumerate(given):
+        share = share + exchanged(part, "grp", distance + 1).astype(F32)
     back_scratch = [
         pltpu.VMEM((3 * blocks, size, width), BF16),
         pltpu.VMEM((2, size, width), F32),
@@ -807,10 +797,50 @@
         scratch=back_scratch + [pltpu.VMEM((members * blocks, size, width), F32)],
         flops=tile_flops,
     )
-    back = [shifted(send_grads[distance], "grp", -distance) for distance in range(1, members)]
+    back = [exchanged(send_grads[distance], "grp", distance) for distance in range(1, members)]
     count_low, count_high, late = lax.optimization_barrier((count_low, count_high, late))
-    (direct,) = call(
-        direct_kernel,
+    share = share.astype(BF16)
+    chain = jnp.concatenate([share, late, recv_grad], 0)
+    rows = share.shape[0]
+    slabs = lax.axis_size("blk")
+    paired = slabs & (slabs - 1) == 0 and slabs > 1
+    if paired:
+        chain, given = halves(chain, (rows, width, width))
+        chain = (chain.astype(F32) + exchanged(given, "blk", 1).astype(F32)).astype(BF16)
+        rows //= 2
+        parts = [part.astype(F32) for part in all_parts(chain, "blk", 2)]
+        chain = tree_sum(parts).astype(BF16)
+    else:
+        chain = lax.psum(chain.astype(F32), "blk").astype(BF16)
+    parts = all_parts(chain, "grp")
+    summed_rows = chain.shape[0] - rows
+    (chain,) = call(
+        make_gather(rows),
+        [like((members * rows + summed_rows, width), BF16)],
+        parts,
+        flops=members * chain.size,
+    )
+    chain, own_grad, count_low, count_high = lax.optimization_barrier(
+        (chain, send_grads[0], count_low, count_high)
+    )
+    (from_send,) = call(
+        return_kernel,
+        [node_float],
+        [w_send, own_grad, *back],
+        flops=2 * own_rows * width * width,
+    )
+    chain, from_send = lax.optimization_barrier((chain, from_send))
+    if paired:
+        (weight_grads,) = call(
+            make_last(members), [like((6 * width, width), F32)], [chain, exchanged(chain, "blk", 1)]
+        )
+    else:
+        member = lax.axis_index("grp")
+        shares = chain[: members * rows].reshape(members, rows, width)
+        shares = shares[member ^ jnp.arange(members)].reshape(members * rows, width)
+        weight_grads = jnp.concatenate([chain[members * rows :], shares], 0).astype(F32)
+    (latent_grad,) = call(
+        latent_grad_kernel,
         [node_float],
         [
             cotangent,
@@ -822,33 +852,10 @@
             w_edge_out,
             w_node_self,
             w_recv,
+            from_send,
         ],
         flops=6 * own_rows * width * width,
     )
-    (latent_grad,) = call(
-        return_kernel,
-        [node_float],
-        [direct, w_send, send_grads[0], *back],
-        flops=2 * own_rows * width * width,
-    )
-    share = share.astype(BF16)
-    chain = jnp.concatenate([share, late, recv_grad], 0)
-    slabs = lax.axis_size("blk")
-    if slabs & (slabs - 1) or slabs == 1:
-        chain = pairwise_sum(chain, "blk")
-        rows = share.shape[0]
-        share, summed, latent_grad = gather_shares(chain[:rows], chain[rows:], latent_grad)
-        weight_grads = jnp.concatenate([summed, share], 0).astype(F32)
-    else:
-        mine, given = halves(chain, (share.shape[0], width, width))
-        mine = (mine.astype(F32) + exchanged(given, "blk", 1).astype(F32)).astype(BF16)
-        chain = pairwise_sum(mine, "blk", 2)
-        rows = share.shape[0] // 2
-        share, summed, latent_grad = gather_shares(chain[:rows], chain[rows:], latent_grad)
-        mine = jnp.concatenate([share, summed], 0)
-        (weight_grads,) = call(
-            make_last(members), [like((6 * width, width), F32)], [mine, exchanged(mine, "blk", 1)]
-        )
     return (new_latent, latent_grad, weight_grads.reshape(6, width, width))
 
 

time: 83.8 us -> 88.8 us (1.060); the launches traced: 82.8 us -> 89.6 us
  local copies, waits for them, and re-layouts: 2.1 us -> 7.21 us
  starting transfers between devices: 28.4 us -> 30.8 us
  waiting for transfers between devices: 23.2 us -> 21.1 us
  Pallas kernels: 27.3 us -> 28.7 us
    ppermute x8 -> x17, starting transfers between devices: 8.33 us -> 19.5 us  [exchanged(): lax.ppermute(value, axis, [(source, source ^ step) for source in range(co...]
    ppermute x14 -> x8, waiting for transfers between devices: 11.8 us -> 1.4 us  [shifted(): return lax.ppermute(value, axis, pairs)]
    ppermute x14 -> x8, starting transfers between devices: 20.1 us -> 11.3 us  [shifted(): return lax.ppermute(value, axis, pairs)]
    ppermute x8 -> x17, waiting for transfers between devices: 11.4 us -> 19.7 us  [exchanged(): lax.ppermute(value, axis, [(source, source ^ step) for source in range(co...]
    unnamed x36 -> x52, local copies, waits for them, and re-layouts: 2.09 us -> 7.2 us
    pallas_call x13 -> x14, Pallas kernels: 27.3 us -> 28.7 us  [call(): pl.pallas_call(kernel, out_shape=[jax.ShapeDtypeStruct(o.shape, o.dtype)...]
  transfers between devices with their start and end apart: 22 -> 25, of which waited for: 10 -> 7; matrix products, arithmetic and copies ran while one was open for 0% -> 0% of each run, Pallas kernels for 15% -> 13%
where the time goes in v8:
time: 88.8 us; the launch traced here: 89.6 us
  starting transfers between devices  30.8 us (35%)
  Pallas kernels  28.7 us (32%)
  waiting for transfers between devices  21.1 us (24%)
  local copies, waits for them, and re-layouts  7.21 us (8%)
  between operations  1.71 us (2%)
    pallas_call x14, Pallas kernels, call(): pl.pallas_call(kernel, out_shape=[jax.ShapeDtypeStruct(o.shape, o.dtype)...  28.7 us
    ppermute x17, waiting for transfers between devices, exchanged(): lax.ppermute(value, axis, [(source, source ^ step) for source in range(co...  19.7 us
    ppermute x17, starting transfers between devices, exchanged(): lax.ppermute(value, axis, [(source, source ^ step) for source in range(co...  19.5 us
    ppermute x8, starting transfers between devices, shifted(): return lax.ppermute(value, axis, pairs)  11.3 us
    unnamed x52, local copies, waits for them, and re-layouts  7.2 us
  transfers between devices with their start and end apart: 25, of which 7 were waited for; matrix products, arithmetic and copies ran while one was open for 0% of the time, Pallas kernels for 13%

profile of v8, /device:TPU:0, one launch (start us, length us, event | category | flops | bytes accessed | tf_op | source)
XLA Modules:
  0.0 89.6 jit_solution(8938929114853991907)
XLA Ops:
  0.6 1.6 %shard_map.185 = (bf16[576,128]{1,0:T(8,128)(2,1)}, bf16[16,384]{1,0:T(8,128)(2,1)}) custom-call(bf16[512,128]{1,0:T(8,128)(2,1)} %latent.5, f32[3,512]{1,0:T(4,128)} %positions.1, f32[3,128]{1,0:T(4,128)} %pos_weight.1), custom_call_target="tpu_custom_call" | custom-call | bytes 298496 | tf_op jit(solution)/shard_map/pallas_call | solution.py:45
  2.2 0.5 collective-permute-start
  2.7 2.9 %collective-permute-start.1 = (bf16[576,128]{1,0:T(8,128)(2,1)}, bf16[576,128]{1,0:T(8,128)(2,1)S(1)}, u32[]{:S(2)}, u32[]{:S(2)}) collective-permute-start(bf16[576,128]{1,0:T(8,128)(2,1)} %get-tuple-element.52.message.refs_3_.own), channel_id=1, source_target_pairs={{0,28},{4,0},{8,4},{12,8},{16,12},{20,16},{24,20},{28,24},{1,29},{... | collective-permute-start | bytes 442376 | tf_op jit(solution)/shard_map/ppermute | solution.py:23
  5.6 2.3 %collective-permute-start.2 = (bf16[576,128]{1,0:T(8,128)(2,1)}, bf16[576,128]{1,0:T(8,128)(2,1)S(1)}, u32[]{:S(2)}, u32[]{:S(2)}) collective-permute-start(bf16[576,128]{1,0:T(8,128)(2,1)} %get-tuple-element.52.message.refs_3_.own), channel_id=1, source_target_pairs={{0,1},{1,0},{2,3},{3,2},{4,5},{5,4},{6,7},{7,6},{8,9},{9,8},{10,11... | collective-permute-start | bytes 442376 | tf_op jit(solution)/shard_map/ppermute | solution.py:553
  7.9 2.6 %collective-permute-start.3 = (bf16[576,128]{1,0:T(8,128)(2,1)}, bf16[576,128]{1,0:T(8,128)(2,1)S(1)}, u32[]{:S(2)}, u32[]{:S(2)}) collective-permute-start(bf16[576,128]{1,0:T(8,128)(2,1)} %get-tuple-element.52.message.refs_3_.own), channel_id=1, source_target_pairs={{0,2},{1,3},{2,0},{3,1},{4,6},{5,7},{6,4},{7,5},{8,10},{9,11},{10,... | collective-permute-start | bytes 442376 | tf_op jit(solution)/shard_map/ppermute | solution.py:553
  11.2 0.6 copy-done.13
  11.9 1.2 %copy-done.1 = s32[1,1,16,128,128]{4,3,2,1,0:T(8,128)S(1)} copy-done((s32[1,1,16,128,128]{4,3,2,1,0:T(8,128)S(1)}, s32[1,1,16,128,128]{4,3,2,1,0:T(8,128)}, u32[]{:S(2)}) %copy-start.1) | copy-done | bytes 1048600
  13.1 0.7 shard_map.184
  13.9 0.1 copy-done.3
  14.0 3.2 %shard_map.186 = (bf16[4,128,128]{2,1,0:T(8,128)(2,1)S(1)}, bf16[12,128,128]{2,1,0:T(8,128)(2,1)S(1)}, f32[12,128,128]{2,1,0:T(8,128)S(1)}, f32[12,128,128]{2,1,0:T(8,128)S(1)}) custom-call(s32[1,1]{1,0:T(1,128)S(6)} %copy.20.tile_count, s32[3,24,128]{2,1,0:T(8,128)S(1)} %get-tuple-element.48.most, bf16[17,128,128]{2,1,0:T(8,128)(2,1)S(1)} %get-tuple-element.49.row_rank, ...), custom_call_target="tpu_custom_call" | custom-call | flops 1073741824 | bytes 3772416 | tf_op jit(solution)/shard_map/pallas_call | solution.py:45
  17.3 4.1 %collective-permute-done.3.refs_4_.refs_5_ = bf16[576,128]{1,0:T(8,128)(2,1)S(1)} collective-permute-done((bf16[576,128]{1,0:T(8,128)(2,1)}, bf16[576,128]{1,0:T(8,128)(2,1)S(1)}, u32[]{:S(2)}, u32[]{:S(2)}) %collective-permute-start.3) | collective-permute-done | bytes 147488 | tf_op jit(solution)/shard_map/ppermute | solution.py:553
  21.4 4.8 %shard_map.187 = (bf16[512,128]{1,0:T(8,128)(2,1)S(1)}, bf16[512,128]{1,0:T(8,128)(2,1)S(1)}, bf16[512,128]{1,0:T(8,128)(2,1)S(1)}, bf16[512,128]{1,0:T(8,128)(2,1)S(1)}, bf16[16,128,128]{2,1,0:T(8,128)(2,1)S(1)}) custom-call(s32[1,1]{1,0:T(1,128)S(6)} %copy.20.tile_count, s32[3,24,128]{2,1,0:T(8,128)S(1)} %get-tuple-element.48.most, ...), custom_call_target="tpu_custom_call" | custom-call | flops 2147483648 | bytes 4784128 | tf_op jit(solution)/shard_map/pallas_call | solution.py:45
  26.3 0.8 copy-done.20
  27.1 2.6 %collective-permute-start.6 = (bf16[512,128]{1,0:T(8,128)(2,1)S(1)}, bf16[512,128]{1,0:T(8,128)(2,1)S(1)}, u32[]{:S(2)}, u32[]{:S(2)}) collective-permute-start(bf16[512,128]{1,0:T(8,128)(2,1)S(1)} %get-tuple-element.60), channel_id=1, source_target_pairs={{0,28},{4,0},{8,4},{12,8},{16,12},{20,16},{24,20},{28,24},{1,29},{... | collective-permute-start | bytes 393224 | tf_op jit(solution)/shard_map/ppermute | solution.py:23
  29.7 1.1 %copy-done.17 = f32[12,128,128]{2,1,0:T(8,128)S(1)} copy-done((f32[12,128,128]{2,1,0:T(8,128)S(1)}, f32[12,128,128]{2,1,0:T(8,128)}, u32[]{:S(2)}) %copy-start.17) | copy-done | bytes 786456
  30.9 1.1 %copy-done.19 = f32[12,128,128]{2,1,0:T(8,128)S(1)} copy-done((f32[12,128,128]{2,1,0:T(8,128)S(1)}, f32[12,128,128]{2,1,0:T(8,128)}, u32[]{:S(2)}) %copy-start.19) | copy-done | bytes 786456
  32.0 1.0 %copy-done.21 = bf16[16,128,128]{2,1,0:T(8,128)(2,1)S(1)} copy-done((bf16[16,128,128]{2,1,0:T(8,128)(2,1)S(1)}, bf16[16,128,128]{2,1,0:T(8,128)(2,1)}, u32[]{:S(2)}) %copy-start.21) | copy-done | bytes 524312
  33.0 1.0 %copy-done.24 = bf16[12,128,128]{2,1,0:T(8,128)(2,1)S(1)} copy-done((bf16[12,128,128]{2,1,0:T(8,128)(2,1)S(1)}, bf16[12,128,128]{2,1,0:T(8,128)(2,1)}, u32[]{:S(2)}) %copy-start.24) | copy-done | bytes 393240
  34.1 3.2 %shard_map.188 = (f32[512,128]{1,0:T(8,128)S(1)}, f32[512,128]{1,0:T(8,128)S(1)}) custom-call(s32[1,1]{1,0:T(1,128)S(6)} %copy.20.tile_count, s32[3,24,128]{2,1,0:T(8,128)S(1)} %get-tuple-element.48.most, bf16[17,128,128]{2,1,0:T(8,128)(2,1)S(1)} %get-tuple-element.49.row_rank, bf16[17,128,128]{2,1,0:T(8,128)(2,1)S(1)} %get-tuple-element.50.row_degree, ...), custom_call_target="tpu_custom_call" | custom-call | flops 1073741824 | bytes 4165632 | tf_op jit(solution)/shard_map/pallas_call | solution.py:45
  37.4 1.7 %shard_map.189 = (bf16[512,128]{1,0:T(8,128)(2,1)}, bf16[512,128]{1,0:T(8,128)(2,1)S(1)}, bf16[512,128]{1,0:T(8,128)(2,1)S(1)}, bf16[512,128]{1,0:T(8,128)(2,1)S...) custom-call(f32[8,128]{1,0:T(8,128)S(1)} %get-tuple-element.47.vecto, ...), custom_call_target="tpu_custom_call" | custom-call | flops 117440512 | bytes 1970176 | tf_op jit(solution)/shard_map/pallas_call | solution.py:45
  39.1 2.6 %collective-permute-start.11 = (bf16[512,128]{1,0:T(8,128)(2,1)S(1)}, bf16[512,128]{1,0:T(8,128)(2,1)S(1)}, u32[]{:S(2)}, u32[]{:S(2)}) collective-permute-start(bf16[512,128]{1,0:T(8,128)(2,1)S(1)} %get-tuple-element.76.refs_0_.d_own), channel_id=1, source_target_pairs={{0,28},{4,0},{8,4},{12,8},{16,12},{20,16},{24,20},{28,24},{1,29},{... | collective-permute-start | bytes 393224 | tf_op jit(solution)/shard_map/ppermute | solution.py:23
  41.7 0.4 shard_map.190
  42.1 0.1 collective-permute-start.7
  42.1 3.9 %collective-permute-start.8 = (bf16[128,128]{1,0:T(8,128)(2,1)S(1)}, bf16[128,128]{1,0:T(8,128)(2,1)S(1)}, u32[]{:S(2)}, u32[]{:S(2)}) collective-permute-start(bf16[128,128]{1,0:T(8,128)(2,1)S(1)} %get-tuple-element.71), channel_id=1, source_target_pairs={{0,2},{1,3},{2,0},{3,1},{4,6},{5,7},{6,4},{7,5},{8,10},{9,11},{10,... | collective-permute-start | bytes 98312 | tf_op jit(solution)/shard_map/ppermute | solution.py:553
  46.0 0.5 collective-permute-start.9
  46.5 3.5 %shard_map.191.refs_2_ = f32[16,128,128]{2,1,0:T(8,128)S(1)} custom-call(s32[1,1]{1,0:T(1,128)S(6)} %copy.20.tile_count, s32[3,24,128]{2,1,0:T(8,128)S(1)} %get-tuple-element.48.most, bf16[17,128,128]{2,1,0:T(8,128)(2,1)S(1)} %get-tuple-element.75.col_rank, bf16[16,128,128]{2,1,0:T(8,128)(2,1)S(1)} %copy-done.22, bf16[12,128,128]{2,1,0:T(8,128)(2,1)S(1)} %copy-done.25, ...), custom_call_target="tpu_custom_call" | custom-call | flops 1073741824 | bytes 2691072 | tf_op jit(solution)/shard_map/pallas_call | solution.py:45
  50.0 1.7 %collective-permute-done.9 = bf16[128,128]{1,0:T(8,128)(2,1)S(1)} collective-permute-done((bf16[128,128]{1,0:T(8,128)(2,1)S(1)}, bf16[128,128]{1,0:T(8,128)(2,1)S(1)}, u32[]{:S(2)}, u32[]{:S(2)}) %collective-permute-start.9) | collective-permute-done | bytes 32800 | tf_op jit(solution)/shard_map/ppermute | solution.py:553
  51.8 7.2 %shard_map.192 = (f32[512,128]{1,0:T(8,128)S(1)}, bf16[512,128]{1,0:T(8,128)(2,1)S(1)}, bf16[512,128]{1,0:T(8,128)(2,1)S(1)}, bf16[512,128]{1,0:T(8,128)(2,1)S(1)}, bf16[128,128]{1,0:T(8,128)(2,1)S(1)}) custom-call(s32[1,1]{1,0:T(1,128)S(6)} %copy.20.tile_count, s32[3,24,128]{2,1,0:T(8,128)S(1)} %get-tuple-element.48.most, ...), custom_call_target="tpu_custom_call" | custom-call | flops 2147483648 | bytes 4100096 | tf_op jit(solution)/shard_map/pallas_call | solution.py:45
  59.0 0.3 shard_map.193
  59.4 0.1 collective-permute-start.12
  59.5 1.2 %collective-permute-done.12 = bf16[192,128]{1,0:T(8,128)(2,1)S(1)} collective-permute-done((bf16[192,128]{1,0:T(8,128)(2,1)S(1)}, bf16[192,128]{1,0:T(8,128)(2,1)S(1)}, u32[]{:S(2)}, u32[]{:S(2)}) %collective-permute-start.12) | collective-permute-done | bytes 49184 | tf_op jit(solution)/shard_map/ppermute | solution.py:553
  60.7 0.1 collective-permute-start.13
  60.8 0.1 collective-permute-start.14
  60.9 3.4 %collective-permute-start.15 = (bf16[192,128]{1,0:T(8,128)(2,1)S(1)}, bf16[192,128]{1,0:T(8,128)(2,1)S(1)}, u32[]{:S(2)}, u32[]{:S(2)}) collective-permute-start(bf16[192,128]{1,0:T(8,128)(2,1)S(1)} %add_convert_fusion.1), channel_id=1, source_target_pairs={{0,24},{4,28},{8,16},{12,20},{16,8},{20,12},{24,0},{28,4},{1,25},{... | collective-permute-start | bytes 147464 | tf_op jit(solution)/shard_map/ppermute | solution.py:553
  64.3 1.4 %collective-permute-start.22 = (bf16[512,128]{1,0:T(8,128)(2,1)S(1)}, bf16[512,128]{1,0:T(8,128)(2,1)S(1)}, u32[]{:S(2)}, u32[]{:S(2)}) collective-permute-start(bf16[512,128]{1,0:T(8,128)(2,1)S(1)} %get-tuple-element.87), channel_id=1, source_target_pairs={{0,2},{1,3},{2,0},{3,1},{4,6},{5,7},{6,4},{7,5},{8,10},{9,11},{10,... | collective-permute-start | bytes 393224 | tf_op jit(solution)/shard_map/ppermute | solution.py:553
  65.7 3.0 %collective-permute-start.23 = (bf16[512,128]{1,0:T(8,128)(2,1)S(1)}, bf16[512,128]{1,0:T(8,128)(2,1)S(1)}, u32[]{:S(2)}, u32[]{:S(2)}) collective-permute-start(bf16[512,128]{1,0:T(8,128)(2,1)S(1)} %get-tuple-element.88), channel_id=1, source_target_pairs={{0,3},{1,2},{2,1},{3,0},{4,7},{5,6},{6,5},{7,4},{8,11},{9,10},{10,... | collective-permute-start | bytes 393224 | tf_op jit(solution)/shard_map/ppermute | solution.py:553
  68.7 0.1 collective-permute-start.16
  68.8 1.4 %collective-permute-start.17 = (bf16[192,128]{1,0:T(8,128)(2,1)S(1)}, bf16[192,128]{1,0:T(8,128)(2,1)S(1)}, u32[]{:S(2)}, u32[]{:S(2)}) collective-permute-start(bf16[192,128]{1,0:T(8,128)(2,1)S(1)} %add_convert_fusion.refs_0_), channel_id=1, source_target_pairs={{0,2},{1,3},{2,0},{3,1},{4,6},{5,7},{6,4},{7,5},{8,10},{9,11},{10,... | collective-permute-start | bytes 147464 | tf_op jit(solution)/shard_map/ppermute | solution.py:553
  70.2 4.3 %collective-permute-done.16.refs_1_ = bf16[192,128]{1,0:T(8,128)(2,1)S(1)} collective-permute-done((bf16[192,128]{1,0:T(8,128)(2,1)S(1)}, bf16[192,128]{1,0:T(8,128)(2,1)S(1)}, u32[]{:S(2)}, u32[]{:S(2)}) %collective-permute-start.16) | collective-permute-done | bytes 49184 | tf_op jit(solution)/shard_map/ppermute | solution.py:553
  74.5 0.5 collective-permute-start.18
  75.1 7.0 %collective-permute-done.17.refs_2_ = bf16[192,128]{1,0:T(8,128)(2,1)S(1)} collective-permute-done((bf16[192,128]{1,0:T(8,128)(2,1)S(1)}, bf16[192,128]{1,0:T(8,128)(2,1)S(1)}, u32[]{:S(2)}, u32[]{:S(2)}) %collective-permute-start.17) | collective-permute-done | bytes 49184 | tf_op jit(solution)/shard_map/ppermute | solution.py:553
  82.2 2.6 %collective-permute-start.20 = (bf16[512,128]{1,0:T(8,128)(2,1)S(1)}, bf16[512,128]{1,0:T(8,128)(2,1)S(1)}, u32[]{:S(2)}, u32[]{:S(2)}) collective-permute-start(bf16[512,128]{1,0:T(8,128)(2,1)S(1)} %get-tuple-element.83.n_low), channel_id=1, source_target_pairs={{0,28},{4,0},{8,4},{12,8},{16,12},{20,16},{24,20},{28,24},{1,29},{... | collective-permute-start | bytes 393224 | tf_op jit(solution)/shard_map/ppermute | solution.py:23
  84.8 0.2 shard_map.195.from_send
  85.0 0.1 collective-permute-start.24
  85.1 1.3 %collective-permute-done.24.other = bf16[384,128]{1,0:T(8,128)(2,1)S(1)} collective-permute-done((bf16[384,128]{1,0:T(8,128)(2,1)S(1)}, bf16[384,128]{1,0:T(8,128)(2,1)S(1)}, u32[]{:S(2)}, u32[]{:S(2)}) %collective-permute-start.24) | collective-permute-done | bytes 98336 | tf_op jit(solution)/shard_map/ppermute | solution.py:553
  86.4 0.8 shard_map.197
  87.1 1.4 %collective-permute-done.19.from_low = bf16[512,128]{1,0:T(8,128)(2,1)S(1)} collective-permute-done((bf16[512,128]{1,0:T(8,128)(2,1)S(1)}, bf16[512,128]{1,0:T(8,128)(2,1)S(1)}, u32[]{:S(2)}, u32[]{:S(2)}) %collective-permute-start.19) | collective-permute-done | bytes 131104 | tf_op jit(solution)/shard_map/ppermute | solution.py:23
  88.5 1.0 %shard_map.196 = f32[512,128]{1,0:T(8,128)} custom-call(bf16[512,128]{1,0:T(8,128)(2,1)S(1)} %copy-done.2, f32[512,128]{1,0:T(8,128)S(1)} %get-tuple-element.62.n_own.count_own, bf16[512,128]{1,0:T(8,128)(2,1)S(1)} %collective-permute-done.19.from_low, bf16[512,128]{1,0:T(8,128)(2,1)S(1)} %collective-permute-done.20.from_high, ...), custom_call_target="tpu_custom_call" | custom-call | flops 50331648 | bytes 1540096 | tf_op jit(solution)/shard_map/pallas_call | solution.py:45
  (74 shorter events, 0.4 us)
Async XLA Ops:
  2.2 11.6 %collective-permute-start = (bf16[576,128]{1,0:T(8,128)(2,1)}, bf16[576,128]{1,0:T(8,128)(2,1)S(1)}, u32[]{:S(2)}, u32[]{:S(2)}) collective-permute-start(bf16[576,128]{1,0:T(8,128)(2,1)} %get-tuple-element.52.message.refs_3_.own), channel_id=1, source_target_pairs={{0,4},{4,8},{8,12},{12,16},{16,20},{20,24},{24,28},{28,0},{1,5},{5... | collective-permute-start | bytes 442376 | tf_op jit(solution)/shard_map/ppermute | solution.py:23
  2.7 11.2 %collective-permute-start.1 = (bf16[576,128]{1,0:T(8,128)(2,1)}, bf16[576,128]{1,0:T(8,128)(2,1)S(1)}, u32[]{:S(2)}, u32[]{:S(2)}) collective-permute-start(bf16[576,128]{1,0:T(8,128)(2,1)} %get-tuple-element.52.message.refs_3_.own), channel_id=1, source_target_pairs={{0,28},{4,0},{8,4},{12,8},{16,12},{20,16},{24,20},{28,24},{1,29},{... | collective-permute-start | bytes 442376 | tf_op jit(solution)/shard_map/ppermute | solution.py:23
  5.6 11.7 %collective-permute-start.2 = (bf16[576,128]{1,0:T(8,128)(2,1)}, bf16[576,128]{1,0:T(8,128)(2,1)S(1)}, u32[]{:S(2)}, u32[]{:S(2)}) collective-permute-start(bf16[576,128]{1,0:T(8,128)(2,1)} %get-tuple-element.52.message.refs_3_.own), channel_id=1, source_target_pairs={{0,1},{1,0},{2,3},{3,2},{4,5},{5,4},{6,7},{7,6},{8,9},{9,8},{10,11... | collective-permute-start | bytes 442376 | tf_op jit(solution)/shard_map/ppermute | solution.py:553
  7.9 13.5 %collective-permute-start.3 = (bf16[576,128]{1,0:T(8,128)(2,1)}, bf16[576,128]{1,0:T(8,128)(2,1)S(1)}, u32[]{:S(2)}, u32[]{:S(2)}) collective-permute-start(bf16[576,128]{1,0:T(8,128)(2,1)} %get-tuple-element.52.message.refs_3_.own), channel_id=1, source_target_pairs={{0,2},{1,3},{2,0},{3,1},{4,6},{5,7},{6,4},{7,5},{8,10},{9,11},{10,... | collective-permute-start | bytes 442376 | tf_op jit(solution)/shard_map/ppermute | solution.py:553
  10.5 10.9 %collective-permute-start.4 = (bf16[576,128]{1,0:T(8,128)(2,1)}, bf16[576,128]{1,0:T(8,128)(2,1)S(1)}, u32[]{:S(2)}, u32[]{:S(2)}) collective-permute-start(bf16[576,128]{1,0:T(8,128)(2,1)} %get-tuple-element.52.message.refs_3_.own), channel_id=1, source_target_pairs={{0,3},{1,2},{2,1},{3,0},{4,7},{5,6},{6,5},{7,4},{8,11},{9,10},{10,... | collective-permute-start | bytes 442376 | tf_op jit(solution)/shard_map/ppermute | solution.py:553
  11.2 0.7 copy-start.11
  11.2 0.7 copy-start.12
  11.9 1.2 %copy-start.1 = (s32[1,1,16,128,128]{4,3,2,1,0:T(8,128)S(1)}, s32[1,1,16,128,128]{4,3,2,1,0:T(8,128)}, u32[]{:S(2)}) copy-start(s32[1,1,16,128,128]{4,3,2,1,0:T(8,128)} %param.21) | copy-start | bytes 3145732
  13.1 0.9 %copy-start.3 = (bf16[576,128]{1,0:T(8,128)(2,1)S(1)}, bf16[576,128]{1,0:T(8,128)(2,1)}, u32[]{:S(2)}) copy-start(bf16[576,128]{1,0:T(8,128)(2,1)} %get-tuple-element.52.message.refs_3_.own) | copy-start | bytes 442372
  13.1 0.9 %copy-start.8 = (bf16[128,128]{1,0:T(8,128)(2,1)S(1)}, bf16[128,128]{1,0:T(8,128)(2,1)}, u32[]{:S(2)}) copy-start(bf16[128,128]{1,0:T(8,128)(2,1)} %w_recv.3) | copy-start | bytes 98308
  13.1 0.9 %copy-start.9 = (bf16[128,128]{1,0:T(8,128)(2,1)S(1)}, bf16[128,128]{1,0:T(8,128)(2,1)}, u32[]{:S(2)}) copy-start(bf16[128,128]{1,0:T(8,128)(2,1)} %w_send.3) | copy-start | bytes 98308
  13.1 0.9 %copy-start.15 = (bf16[16,384]{1,0:T(8,128)(2,1)S(1)}, bf16[16,384]{1,0:T(8,128)(2,1)}, u32[]{:S(2)}) copy-start(bf16[16,384]{1,0:T(8,128)(2,1)} %get-tuple-element.51.weight_parts.refs_2_) | copy-start | bytes 36868
  17.3 9.0 %copy-start.16 = (f32[12,128,128]{2,1,0:T(8,128)}, f32[12,128,128]{2,1,0:T(8,128)S(1)}, u32[]{:S(2)}) copy-start(f32[12,128,128]{2,1,0:T(8,128)S(1)} %get-tuple-element.54.sums_in) | copy-start | bytes 2359300
  17.3 9.0 %copy-start.18 = (f32[12,128,128]{2,1,0:T(8,128)}, f32[12,128,128]{2,1,0:T(8,128)S(1)}, u32[]{:S(2)}) copy-start(f32[12,128,128]{2,1,0:T(8,128)S(1)} %get-tuple-element.55.counts_in) | copy-start | bytes 2359300
  17.3 9.0 %copy-start.23 = (bf16[12,128,128]{2,1,0:T(8,128)(2,1)}, bf16[12,128,128]{2,1,0:T(8,128)(2,1)S(1)}, u32[]{:S(2)}) copy-start(bf16[12,128,128]{2,1,0:T(8,128)(2,1)S(1)} %get-tuple-element.53.receivers) | copy-start | bytes 1179652
  26.3 0.8 copy-start.20
  27.1 10.2 %collective-permute-start.5 = (bf16[512,128]{1,0:T(8,128)(2,1)S(1)}, bf16[512,128]{1,0:T(8,128)(2,1)S(1)}, u32[]{:S(2)}, u32[]{:S(2)}) collective-permute-start(bf16[512,128]{1,0:T(8,128)(2,1)S(1)} %get-tuple-element.59), channel_id=1, source_target_pairs={{0,4},{4,8},{8,12},{12,16},{16,20},{20,24},{24,28},{28,0},{1,5},{5... | collective-permute-start | bytes 393224 | tf_op jit(solution)/shard_map/ppermute | solution.py:23
  27.1 10.2 %collective-permute-start.6 = (bf16[512,128]{1,0:T(8,128)(2,1)S(1)}, bf16[512,128]{1,0:T(8,128)(2,1)S(1)}, u32[]{:S(2)}, u32[]{:S(2)}) collective-permute-start(bf16[512,128]{1,0:T(8,128)(2,1)S(1)} %get-tuple-element.60), channel_id=1, source_target_pairs={{0,28},{4,0},{8,4},{12,8},{16,12},{20,16},{24,20},{28,24},{1,29},{... | collective-permute-start | bytes 393224 | tf_op jit(solution)/shard_map/ppermute | solution.py:23
  29.7 1.1 %copy-start.17 = (f32[12,128,128]{2,1,0:T(8,128)S(1)}, f32[12,128,128]{2,1,0:T(8,128)}, u32[]{:S(2)}) copy-start(f32[12,128,128]{2,1,0:T(8,128)} %copy-done.16) | copy-start | bytes 2359300
  30.9 1.1 %copy-start.19 = (f32[12,128,128]{2,1,0:T(8,128)S(1)}, f32[12,128,128]{2,1,0:T(8,128)}, u32[]{:S(2)}) copy-start(f32[12,128,128]{2,1,0:T(8,128)} %copy-done.18) | copy-start | bytes 2359300
  32.0 1.0 %copy-start.21 = (bf16[16,128,128]{2,1,0:T(8,128)(2,1)S(1)}, bf16[16,128,128]{2,1,0:T(8,128)(2,1)}, u32[]{:S(2)}) copy-start(bf16[16,128,128]{2,1,0:T(8,128)(2,1)} %copy-done.20) | copy-start | bytes 1572868
  33.0 1.0 %copy-start.24 = (bf16[12,128,128]{2,1,0:T(8,128)(2,1)S(1)}, bf16[12,128,128]{2,1,0:T(8,128)(2,1)}, u32[]{:S(2)}) copy-start(bf16[12,128,128]{2,1,0:T(8,128)(2,1)} %copy-done.23) | copy-start | bytes 1179652
  34.0 3.3 %copy-start = (bf16[512,128]{1,0:T(8,128)(2,1)S(1)}, bf16[512,128]{1,0:T(8,128)(2,1)}, u32[]{:S(2)}) copy-start(bf16[512,128]{1,0:T(8,128)(2,1)} %latent.5) | copy-start | bytes 393220
  34.0 3.3 %copy-start.2 = (bf16[512,128]{1,0:T(8,128)(2,1)S(1)}, bf16[512,128]{1,0:T(8,128)(2,1)}, u32[]{:S(2)}) copy-start(bf16[512,128]{1,0:T(8,128)(2,1)} %cotangent.3) | copy-start | bytes 393220
  34.0 3.3 %copy-start.4 = (bf16[128,128]{1,0:T(8,128)(2,1)S(1)}, bf16[128,128]{1,0:T(8,128)(2,1)}, u32[]{:S(2)}) copy-start(bf16[128,128]{1,0:T(8,128)(2,1)} %w_edge_out.3) | copy-start | bytes 98308
  34.0 3.3 %copy-start.5 = (bf16[128,128]{1,0:T(8,128)(2,1)S(1)}, bf16[128,128]{1,0:T(8,128)(2,1)}, u32[]{:S(2)}) copy-start(bf16[128,128]{1,0:T(8,128)(2,1)} %w_node_self.3) | copy-start | bytes 98308
  34.0 3.3 %copy-start.6 = (bf16[128,128]{1,0:T(8,128)(2,1)S(1)}, bf16[128,128]{1,0:T(8,128)(2,1)}, u32[]{:S(2)}) copy-start(bf16[128,128]{1,0:T(8,128)(2,1)} %w_node_msg.1) | copy-start | bytes 98308
  34.0 3.3 %copy-start.7 = (bf16[128,128]{1,0:T(8,128)(2,1)S(1)}, bf16[128,128]{1,0:T(8,128)(2,1)}, u32[]{:S(2)}) copy-start(bf16[128,128]{1,0:T(8,128)(2,1)} %w_node_out.1) | copy-start | bytes 98308
  39.1 7.5 %copy-start.22 = (bf16[16,128,128]{2,1,0:T(8,128)(2,1)S(1)}, bf16[16,128,128]{2,1,0:T(8,128)(2,1)}, u32[]{:S(2)}) copy-start(bf16[16,128,128]{2,1,0:T(8,128)(2,1)} %copy-done.20) | copy-start | bytes 1572868
  39.1 12.7 %collective-permute-start.10 = (bf16[512,128]{1,0:T(8,128)(2,1)S(1)}, bf16[512,128]{1,0:T(8,128)(2,1)S(1)}, u32[]{:S(2)}, u32[]{:S(2)}) collective-permute-start(bf16[512,128]{1,0:T(8,128)(2,1)S(1)} %get-tuple-element.76.refs_0_.d_own), channel_id=1, source_target_pairs={{0,4},{4,8},{8,12},{12,16},{16,20},{20,24},{24,28},{28,0},{1,5},{5... | collective-permute-start | bytes 393224 | tf_op jit(solution)/shard_map/ppermute | solution.py:23
  39.1 12.7 %collective-permute-start.11 = (bf16[512,128]{1,0:T(8,128)(2,1)S(1)}, bf16[512,128]{1,0:T(8,128)(2,1)S(1)}, u32[]{:S(2)}, u32[]{:S(2)}) collective-permute-start(bf16[512,128]{1,0:T(8,128)(2,1)S(1)} %get-tuple-element.76.refs_0_.d_own), channel_id=1, source_target_pairs={{0,28},{4,0},{8,4},{12,8},{16,12},{20,16},{24,20},{28,24},{1,29},{... | collective-permute-start | bytes 393224 | tf_op jit(solution)/shard_map/ppermute | solution.py:23
  41.7 4.8 %copy-start.25 = (bf16[12,128,128]{2,1,0:T(8,128)(2,1)S(1)}, bf16[12,128,128]{2,1,0:T(8,128)(2,1)}, u32[]{:S(2)}) copy-start(bf16[12,128,128]{2,1,0:T(8,128)(2,1)} %copy-done.23) | copy-start | bytes 1179652
  42.1 7.9 %collective-permute-start.7 = (bf16[128,128]{1,0:T(8,128)(2,1)S(1)}, bf16[128,128]{1,0:T(8,128)(2,1)S(1)}, u32[]{:S(2)}, u32[]{:S(2)}) collective-permute-start(bf16[128,128]{1,0:T(8,128)(2,1)S(1)} %get-tuple-element.70), channel_id=1, source_target_pairs={{0,1},{1,0},{2,3},{3,2},{4,5},{5,4},{6,7},{7,6},{8,9},{9,8},{10,11... | collective-permute-start | bytes 98312 | tf_op jit(solution)/shard_map/ppermute | solution.py:553
  42.1 7.9 %collective-permute-start.8 = (bf16[128,128]{1,0:T(8,128)(2,1)S(1)}, bf16[128,128]{1,0:T(8,128)(2,1)S(1)}, u32[]{:S(2)}, u32[]{:S(2)}) collective-permute-start(bf16[128,128]{1,0:T(8,128)(2,1)S(1)} %get-tuple-element.71), channel_id=1, source_target_pairs={{0,2},{1,3},{2,0},{3,1},{4,6},{5,7},{6,4},{7,5},{8,10},{9,11},{10,... | collective-permute-start | bytes 98312 | tf_op jit(solution)/shard_map/ppermute | solution.py:553
  46.0 5.7 %collective-permute-start.9 = (bf16[128,128]{1,0:T(8,128)(2,1)S(1)}, bf16[128,128]{1,0:T(8,128)(2,1)S(1)}, u32[]{:S(2)}, u32[]{:S(2)}) collective-permute-start(bf16[128,128]{1,0:T(8,128)(2,1)S(1)} %get-tuple-element.72), channel_id=1, source_target_pairs={{0,3},{1,2},{2,1},{3,0},{4,7},{5,6},{6,5},{7,4},{8,11},{9,10},{10,... | collective-permute-start | bytes 98312 | tf_op jit(solution)/shard_map/ppermute | solution.py:553
  59.4 1.3 %collective-permute-start.12 = (bf16[192,128]{1,0:T(8,128)(2,1)S(1)}, bf16[192,128]{1,0:T(8,128)(2,1)S(1)}, u32[]{:S(2)}, u32[]{:S(2)}) collective-permute-start(bf16[192,128]{1,0:T(8,128)(2,1)S(1)} %broadcast_select_fusion), channel_id=1, source_target_pairs={{0,4},{4,0},{8,12},{12,8},{16,20},{20,16},{24,28},{28,24},{1,5},{5... | collective-permute-start | bytes 147464 | tf_op jit(solution)/shard_map/ppermute | solution.py:553
  60.7 5.0 %collective-permute-start.13 = (bf16[192,128]{1,0:T(8,128)(2,1)S(1)}, bf16[192,128]{1,0:T(8,128)(2,1)S(1)}, u32[]{:S(2)}, u32[]{:S(2)}) collective-permute-start(bf16[192,128]{1,0:T(8,128)(2,1)S(1)} %add_convert_fusion.1), channel_id=1, source_target_pairs={{0,8},{4,12},{8,0},{12,4},{16,24},{20,28},{24,16},{28,20},{1,9},{5... | collective-permute-start | bytes 147464 | tf_op jit(solution)/shard_map/ppermute | solution.py:553
  60.8 7.9 %collective-permute-start.14 = (bf16[192,128]{1,0:T(8,128)(2,1)S(1)}, bf16[192,128]{1,0:T(8,128)(2,1)S(1)}, u32[]{:S(2)}, u32[]{:S(2)}) collective-permute-start(bf16[192,128]{1,0:T(8,128)(2,1)S(1)} %add_convert_fusion.1), channel_id=1, source_target_pairs={{0,16},{4,20},{8,24},{12,28},{16,0},{20,4},{24,8},{28,12},{1,17},{... | collective-permute-start | bytes 147464 | tf_op jit(solution)/shard_map/ppermute | solution.py:553
  60.9 7.8 %collective-permute-start.15 = (bf16[192,128]{1,0:T(8,128)(2,1)S(1)}, bf16[192,128]{1,0:T(8,128)(2,1)S(1)}, u32[]{:S(2)}, u32[]{:S(2)}) collective-permute-start(bf16[192,128]{1,0:T(8,128)(2,1)S(1)} %add_convert_fusion.1), channel_id=1, source_target_pairs={{0,24},{4,28},{8,16},{12,20},{16,8},{20,12},{24,0},{28,4},{1,25},{... | collective-permute-start | bytes 147464 | tf_op jit(solution)/shard_map/ppermute | solution.py:553
  64.3 20.5 %collective-permute-start.21 = (bf16[512,128]{1,0:T(8,128)(2,1)S(1)}, bf16[512,128]{1,0:T(8,128)(2,1)S(1)}, u32[]{:S(2)}, u32[]{:S(2)}) collective-permute-start(bf16[512,128]{1,0:T(8,128)(2,1)S(1)} %get-tuple-element.86), channel_id=1, source_target_pairs={{0,1},{1,0},{2,3},{3,2},{4,5},{5,4},{6,7},{7,6},{8,9},{9,8},{10,11... | collective-permute-start | bytes 393224 | tf_op jit(solution)/shard_map/ppermute | solution.py:553
  64.3 20.5 %collective-permute-start.22 = (bf16[512,128]{1,0:T(8,128)(2,1)S(1)}, bf16[512,128]{1,0:T(8,128)(2,1)S(1)}, u32[]{:S(2)}, u32[]{:S(2)}) collective-permute-start(bf16[512,128]{1,0:T(8,128)(2,1)S(1)} %get-tuple-element.87), channel_id=1, source_target_pairs={{0,2},{1,3},{2,0},{3,1},{4,6},{5,7},{6,4},{7,5},{8,10},{9,11},{10,... | collective-permute-start | bytes 393224 | tf_op jit(solution)/shard_map/ppermute | solution.py:553
  65.7 19.1 %collective-permute-start.23 = (bf16[512,128]{1,0:T(8,128)(2,1)S(1)}, bf16[512,128]{1,0:T(8,128)(2,1)S(1)}, u32[]{:S(2)}, u32[]{:S(2)}) collective-permute-start(bf16[512,128]{1,0:T(8,128)(2,1)S(1)} %get-tuple-element.88), channel_id=1, source_target_pairs={{0,3},{1,2},{2,1},{3,0},{4,7},{5,6},{6,5},{7,4},{8,11},{9,10},{10,... | collective-permute-start | bytes 393224 | tf_op jit(solution)/shard_map/ppermute | solution.py:553
  68.7 5.8 %collective-permute-start.16 = (bf16[192,128]{1,0:T(8,128)(2,1)S(1)}, bf16[192,128]{1,0:T(8,128)(2,1)S(1)}, u32[]{:S(2)}, u32[]{:S(2)}) collective-permute-start(bf16[192,128]{1,0:T(8,128)(2,1)S(1)} %add_convert_fusion.refs_0_), channel_id=1, source_target_pairs={{0,1},{1,0},{2,3},{3,2},{4,5},{5,4},{6,7},{7,6},{8,9},{9,8},{10,11... | collective-permute-start | bytes 147464 | tf_op jit(solution)/shard_map/ppermute | solution.py:553
  68.8 13.3 %collective-permute-start.17 = (bf16[192,128]{1,0:T(8,128)(2,1)S(1)}, bf16[192,128]{1,0:T(8,128)(2,1)S(1)}, u32[]{:S(2)}, u32[]{:S(2)}) collective-permute-start(bf16[192,128]{1,0:T(8,128)(2,1)S(1)} %add_convert_fusion.refs_0_), channel_id=1, source_target_pairs={{0,2},{1,3},{2,0},{3,1},{4,6},{5,7},{6,4},{7,5},{8,10},{9,11},{10,... | collective-permute-start | bytes 147464 | tf_op jit(solution)/shard_map/ppermute | solution.py:553
  74.5 7.5 %collective-permute-start.18 = (bf16[192,128]{1,0:T(8,128)(2,1)S(1)}, bf16[192,128]{1,0:T(8,128)(2,1)S(1)}, u32[]{:S(2)}, u32[]{:S(2)}) collective-permute-start(bf16[192,128]{1,0:T(8,128)(2,1)S(1)} %add_convert_fusion.refs_0_), channel_id=1, source_target_pairs={{0,3},{1,2},{2,1},{3,0},{4,7},{5,6},{6,5},{7,4},{8,11},{9,10},{10,... | collective-permute-start | bytes 147464 | tf_op jit(solution)/shard_map/ppermute | solution.py:553
  82.1 6.4 %collective-permute-start.19 = (bf16[512,128]{1,0:T(8,128)(2,1)S(1)}, bf16[512,128]{1,0:T(8,128)(2,1)S(1)}, u32[]{:S(2)}, u32[]{:S(2)}) collective-permute-start(bf16[512,128]{1,0:T(8,128)(2,1)S(1)} %get-tuple-element.82.n_high), channel_id=1, source_target_pairs={{0,4},{4,8},{8,12},{12,16},{16,20},{20,24},{24,28},{28,0},{1,5},{5... | collective-permute-start | bytes 393224 | tf_op jit(solution)/shard_map/ppermute | solution.py:23
  82.2 6.4 %collective-permute-start.20 = (bf16[512,128]{1,0:T(8,128)(2,1)S(1)}, bf16[512,128]{1,0:T(8,128)(2,1)S(1)}, u32[]{:S(2)}, u32[]{:S(2)}) collective-permute-start(bf16[512,128]{1,0:T(8,128)(2,1)S(1)} %get-tuple-element.83.n_low), channel_id=1, source_target_pairs={{0,28},{4,0},{8,4},{12,8},{16,12},{20,16},{24,20},{28,24},{1,29},{... | collective-permute-start | bytes 393224 | tf_op jit(solution)/shard_map/ppermute | solution.py:23
  85.0 1.4 %collective-permute-start.24 = (bf16[384,128]{1,0:T(8,128)(2,1)S(1)}, bf16[384,128]{1,0:T(8,128)(2,1)S(1)}, u32[]{:S(2)}, u32[]{:S(2)}) collective-permute-start(bf16[384,128]{1,0:T(8,128)(2,1)S(1)} %shard_map.194.mine), channel_id=1, source_target_pairs={{0,4},{4,0},{8,12},{12,8},{16,20},{20,16},{24,28},{28,24},{1,5},{5... | collective-permute-start | bytes 294920 | tf_op jit(solution)/shard_map/ppermute | solution.py:553
  (3 other events, 2.0 us)

commit v9 on v8

--- a/solution.py
+++ b/solution.py
@@ -427,18 +427,18 @@
     d_message_out[...] = d_message
 
 
-def early_kernel(latent, aggregate, message, hidden, d_update, d_hidden_pre, d_message, *refs):
-    shares, grads = refs[:-1], refs[-1]
+def early_kernel(
+    latent, aggregate, message, hidden, d_update, d_hidden_pre, d_message, keep, give, grads
+):
     width = latent.shape[1]
     grads[0:width, :] = contract_rows(aggregate[...], d_message[...])
     grads[width : 2 * width, :] = contract_rows(latent[...], d_hidden_pre[...])
     grads[2 * width : 3 * width, :] = contract_rows(message[...], d_hidden_pre[...])
     grads[3 * width : 4 * width, :] = contract_rows(hidden[...], d_update[...])
-    rows = shares[0].shape[0]
-    member = lax.axis_index("grp")
-    for distance, share in enumerate(shares):
-        start = pl.multiple_of((member ^ distance) * rows, rows)
-        share[...] = grads[pl.ds(start, rows), :].astype(share.dtype)
+    half = keep.shape[0]
+    bit = lax.axis_index("grp") & 1
+    keep[...] = grads[pl.ds(pl.multiple_of(bit * half, half), half), :]
+    give[...] = grads[pl.ds(pl.multiple_of((1 - bit) * half, half), half), :].astype(BF16)
 
 
 def recv_kernel(low, own, high, d_low, d_own, d_high, n_low, n_own, n_high, grad_out):
@@ -480,7 +480,7 @@
         else:
             grad_parts, started, refs = (refs[0], None, refs[1]), refs[2], refs[3:]
             messages, refs = refs[:members], refs[members:]
-            grads_out, late_out, refs = refs[:members], refs[members], refs[members + 1 :]
+            own_out, stay_out, away_out, late_out, refs = *refs[:4], refs[4:]
             d_sums, grads = refs[0], refs[-1]
         totals, col_most, table, order, sem = refs[1:6]
         size, width = senders.shape[1:]
@@ -537,12 +537,19 @@
         if own:
             return
         late = jnp.zeros((width, width), F32)
-        for distance, (message, out) in enumerate(zip(messages, grads_out)):
+        for distance, message in enumerate(messages):
             for block in range(blocks):
                 span = slice(block * size, (block + 1) * size)
                 found = grads[distance * blocks + block]
-                out[span, :] = found.astype(out.dtype)
                 late = late + contract_rows(message[span, :], found.astype(BF16))
+                if distance == 0:
+                    own_out[span, :] = found
+                elif distance % 2:
+                    start = distance // 2 * rows + block * size
+                    away_out[start : start + size, :] = found.astype(BF16)
+                else:
+                    start = (distance // 2 - 1) * rows + block * size
+                    stay_out[start : start + size, :] = found.astype(BF16)
         late_out[...] = late.astype(BF16)
 
     return kernel
@@ -557,47 +564,40 @@
     return (lax.axis_index(axis) & step) != 0
 
 
-def tree_sum(parts):
-    while len(parts) > 1:
-        parts = [parts[item] + parts[item + 1] for item in range(0, len(parts), 2)]
-    return parts[0]
-
-
-def all_parts(value, axis, least=1):
-    count = lax.axis_size(axis)
-    return [value] + [exchanged(value, axis, step) for step in range(least, count, least)]
+def gather_shares(share, summed, tied):
+    step = lax.axis_size("grp") // 2
+    rows = share.shape[0]
+    while step:
+        if step == 1:
+            share, summed, tied = lax.optimization_barrier((share, summed, tied))
+        other = exchanged(jnp.concatenate([share, summed], 0), "grp", step)
+        others = other[:rows]
+        high = bit_set("grp", step)
+        share = jnp.concatenate([jnp.where(high, others, share), jnp.where(high, share, others)], 0)
+        summed = (summed.astype(F32) + other[rows:].astype(F32)).astype(BF16)
+        rows *= 2
+        step //= 2
+    return share, summed, tied
 
 
 def return_kernel(w_send, own, *refs):
     back, out = refs[:-1], refs[-1]
     d_send = own[...]
     for part in back:
-        d_send = d_send + part[...].astype(F32)
+        d_send = d_send + part[0 : out.shape[0], :].astype(F32)
     out[...] = dot_t(d_send.astype(BF16), w_send[...])
-
-
-def make_gather(rows):
-    def kernel(*refs):
-        parts, out = refs[:-1], refs[-1]
-        for distance, part in enumerate(parts):
-            out[distance * rows : (distance + 1) * rows, :] = part[0:rows, :]
-        rest = [part[rows:, :].astype(F32) for part in parts]
-        out[len(parts) * rows :, :] = tree_sum(rest).astype(BF16)
-
-    return kernel
 
 
 def make_last(members):
     def kernel(mine, other, weight_grads):
         bit = lax.axis_index("blk") & 1
-        member = lax.axis_index("grp")
         for part, place in ((mine, bit), (other, 1 - bit)):
             early = 2 * weight_grads.shape[0] // 6
             half = (weight_grads.shape[0] - early) // (2 * members)
             quarter = early // 4
-            for distance in range(members):
-                start = pl.multiple_of(early + (2 * (member ^ distance) + place) * half, half)
-                span = slice(distance * half, (distance + 1) * half)
+            for item in range(members):
+                start = pl.multiple_of(early + (2 * item + place) * half, half)
+                span = slice(item * half, (item + 1) * half)
                 weight_grads[pl.ds(start, half), :] = part[span, :].astype(F32)
             for item in range(2):
                 start = pl.multiple_of((2 * item + place) * quarter, quarter)
@@ -748,16 +748,26 @@
         flops=14 * own_rows * width * width,
     )
     d_low, d_high = shifted(d_aggregate, "blk", 1), shifted(d_aggregate, "blk", -1)
-    rows = 4 * width // members
-    share, *given = call(
+    half = 4 * width // 2
+    share, given = call(
         early_kernel,
-        [like((rows, width), F32)] + [like((rows, width), BF16)] * (members - 1),
+        [like((half, width), F32), like((half, width), BF16)],
         [latent, aggregate, message_out, hidden, d_update, d_hidden_pre, d_message],
-        scratch=[pltpu.VMEM((4 * width, width), F32)],
+        scratch=[pltpu.VMEM((2 * half, width), F32)],
         flops=8 * own_rows * width * width,
     )
-    for distance, part in enumerate(given):
-        share = share + exchanged(part, "grp", distance + 1).astype(F32)
+    share = share + exchanged(given, "grp", 1).astype(F32)
+    arrived = jnp.zeros_like(share)
+    step = 2
+    while step < members:
+        half = share.shape[0] // 2
+        high = bit_set("grp", step)
+        given = jnp.where(high, share[:half], share[half:]).astype(BF16)
+        share = jnp.where(high, share[half:], share[:half])
+        arrived = exchanged(given, "grp", step)
+        step *= 2
+        if step < members:
+            share = share + arrived.astype(F32)
     back_scratch = [
         pltpu.VMEM((3 * blocks, size, width), BF16),
         pltpu.VMEM((2, size, width), F32),
@@ -788,17 +798,23 @@
         ],
         flops=6 * own_rows * width * width,
     )
-    *send_grads, late = call(
+    apart = (members // 2) * own_rows
+    own_grad, stay, away, late = call(
         make_backward(members, blocks, False),
-        [node_float] + [node_like] * (members - 1) + [like((width, width), BF16)],
+        [
+            node_float,
+            like((apart - own_rows, width), BF16),
+            like((apart, width), BF16),
+            like((width, width), BF16),
+        ],
         [col_rank, senders, receivers, d_low, d_high, started, *messages],
         scalars=[tile_count],
         far=[most],
         scratch=back_scratch + [pltpu.VMEM((members * blocks, size, width), F32)],
         flops=tile_flops,
     )
-    back = [exchanged(send_grads[distance], "grp", distance) for distance in range(1, members)]
-    count_low, count_high, late = lax.optimization_barrier((count_low, count_high, late))
+    first = exchanged(away, "grp", 1)
+    share = share + lax.optimization_barrier((arrived, late))[0].astype(F32)
     share = share.astype(BF16)
     chain = jnp.concatenate([share, late, recv_grad], 0)
     rows = share.shape[0]
@@ -808,37 +824,39 @@
         chain, given = halves(chain, (rows, width, width))
         chain = (chain.astype(F32) + exchanged(given, "blk", 1).astype(F32)).astype(BF16)
         rows //= 2
-        parts = [part.astype(F32) for part in all_parts(chain, "blk", 2)]
-        chain = tree_sum(parts).astype(BF16)
+        step = 2
+        while step < slabs:
+            if 2 * step == slabs:
+                chain, first = lax.optimization_barrier((chain, first))
+            chain = (chain.astype(F32) + exchanged(chain, "blk", step).astype(F32)).astype(BF16)
+            step *= 2
     else:
         chain = lax.psum(chain.astype(F32), "blk").astype(BF16)
-    parts = all_parts(chain, "grp")
-    summed_rows = chain.shape[0] - rows
-    (chain,) = call(
-        make_gather(rows),
-        [like((members * rows + summed_rows, width), BF16)],
-        parts,
-        flops=members * chain.size,
-    )
-    chain, own_grad, count_low, count_high = lax.optimization_barrier(
-        (chain, send_grads[0], count_low, count_high)
-    )
+    back = [first]
+    stay = stay.astype(F32) + back[0][own_rows:].astype(F32)
+    step = 2
+    while step < members:
+        kept = [stay[start : start + own_rows] for start in range(0, stay.shape[0], own_rows)]
+        given = jnp.concatenate(kept[0::2], 0).astype(BF16)
+        back.append(exchanged(given, "grp", step))
+        if kept[1::2]:
+            stay = jnp.concatenate(kept[1::2], 0) + back[-1][own_rows:].astype(F32)
+        step *= 2
     (from_send,) = call(
         return_kernel,
         [node_float],
         [w_send, own_grad, *back],
         flops=2 * own_rows * width * width,
     )
-    chain, from_send = lax.optimization_barrier((chain, from_send))
+    share, summed, from_send = gather_shares(chain[:rows], chain[rows:], from_send)
+    chain = jnp.concatenate([share, summed], 0)
     if paired:
         (weight_grads,) = call(
             make_last(members), [like((6 * width, width), F32)], [chain, exchanged(chain, "blk", 1)]
         )
     else:
-        member = lax.axis_index("grp")
-        shares = chain[: members * rows].reshape(members, rows, width)
-        shares = shares[member ^ jnp.arange(members)].reshape(members * rows, width)
-        weight_grads = jnp.concatenate([chain[members * rows :], shares], 0).astype(F32)
+        gathered = members * rows
+        weight_grads = jnp.concatenate([chain[gathered:], chain[:gathered]], 0).astype(F32)
     (latent_grad,) = call(
         latent_grad_kernel,
         [node_float],

time: 88.8 us -> 90.7 us (1.021)
  the two profiles are of different devices: /device:TPU:0 before, /device:TPU:1 now
where the time goes in v9:
time: 90.7 us; the launch traced here: 89.5 us
  starting transfers between devices  32.1 us (35%)
  waiting for transfers between devices  27.1 us (30%)
  Pallas kernels  20 us (22%)
  local copies, waits for them, and re-layouts  8.25 us (9%)
  between operations  1.74 us (2%)
    ppermute x13, waiting for transfers between devices, exchanged(): lax.ppermute(value, axis, [(source, source ^ step) for source in range(co...  25.4 us
    pallas_call x13, Pallas kernels, call(): pl.pallas_call(kernel, out_shape=[jax.ShapeDtypeStruct(o.shape, o.dtype)...  20 us
    ppermute x13, starting transfers between devices, exchanged(): lax.ppermute(value, axis, [(source, source ^ step) for source in range(co...  17 us
    ppermute x8, starting transfers between devices, shifted(): return lax.ppermute(value, axis, pairs)  15.1 us
    unnamed x60, local copies, waits for them, and re-layouts  8.24 us
  transfers between devices with their start and end apart: 21, of which 10 were waited for; matrix products, arithmetic and copies ran while one was open for 0% of the time, Pallas kernels for 14%

profile of v9, /device:TPU:1, one launch (start us, length us, event | category | flops | bytes accessed | tf_op | source)
XLA Modules:
  0.0 89.5 jit_solution(5068766639555021166)
XLA Ops:
  0.6 1.6 %shard_map.185 = (bf16[576,128]{1,0:T(8,128)(2,1)}, bf16[16,384]{1,0:T(8,128)(2,1)}) custom-call(bf16[512,128]{1,0:T(8,128)(2,1)} %latent.5, f32[3,512]{1,0:T(4,128)} %positions.1, f32[3,128]{1,0:T(4,128)} %pos_weight.1), custom_call_target="tpu_custom_call" | custom-call | bytes 298496 | tf_op jit(solution)/shard_map/pallas_call | solution.py:45
  2.2 2.6 %collective-permute-start = (bf16[576,128]{1,0:T(8,128)(2,1)}, bf16[576,128]{1,0:T(8,128)(2,1)S(1)}, u32[]{:S(2)}, u32[]{:S(2)}) collective-permute-start(bf16[576,128]{1,0:T(8,128)(2,1)} %get-tuple-element.46.message.refs_3_.own), channel_id=1, source_target_pairs={{0,4},{4,8},{8,12},{12,16},{16,20},{20,24},{24,28},{28,0},{1,5},{5... | collective-permute-start | bytes 442376 | tf_op jit(solution)/shard_map/ppermute | solution.py:23
  4.8 1.3 %collective-permute-start.2 = (bf16[576,128]{1,0:T(8,128)(2,1)}, bf16[576,128]{1,0:T(8,128)(2,1)S(1)}, u32[]{:S(2)}, u32[]{:S(2)}) collective-permute-start(bf16[576,128]{1,0:T(8,128)(2,1)} %get-tuple-element.46.message.refs_3_.own), channel_id=1, source_target_pairs={{0,1},{1,0},{2,3},{3,2},{4,5},{5,4},{6,7},{7,6},{8,9},{9,8},{10,11... | collective-permute-start | bytes 442376 | tf_op jit(solution)/shard_map/ppermute | solution.py:560
  6.1 2.3 %collective-permute-start.3 = (bf16[576,128]{1,0:T(8,128)(2,1)}, bf16[576,128]{1,0:T(8,128)(2,1)S(1)}, u32[]{:S(2)}, u32[]{:S(2)}) collective-permute-start(bf16[576,128]{1,0:T(8,128)(2,1)} %get-tuple-element.46.message.refs_3_.own), channel_id=1, source_target_pairs={{0,2},{1,3},{2,0},{3,1},{4,6},{5,7},{6,4},{7,5},{8,10},{9,11},{10,... | collective-permute-start | bytes 442376 | tf_op jit(solution)/shard_map/ppermute | solution.py:560
  9.2 0.6 copy-done.13
  9.8 1.2 %copy-done.1 = s32[1,1,16,128,128]{4,3,2,1,0:T(8,128)S(1)} copy-done((s32[1,1,16,128,128]{4,3,2,1,0:T(8,128)S(1)}, s32[1,1,16,128,128]{4,3,2,1,0:T(8,128)}, u32[]{:S(2)}) %copy-start.1) | copy-done | bytes 1048600
  11.1 0.7 shard_map.184
  11.8 0.1 copy-done.3
  12.0 2.4 %shard_map.186 = (bf16[4,128,128]{2,1,0:T(8,128)(2,1)S(1)}, bf16[12,128,128]{2,1,0:T(8,128)(2,1)S(1)}, f32[12,128,128]{2,1,0:T(8,128)S(1)}, f32[12,128,128]{2,1,0:T(8,128)S(1)}) custom-call(s32[1,1]{1,0:T(1,128)S(6)} %copy.20.tile_count, s32[3,24,128]{2,1,0:T(8,128)S(1)} %get-tuple-element.42.most, bf16[17,128,128]{2,1,0:T(8,128)(2,1)S(1)} %get-tuple-element.43.row_rank, ...), custom_call_target="tpu_custom_call" | custom-call | flops 1073741824 | bytes 3772416 | tf_op jit(solution)/shard_map/pallas_call | solution.py:45
  14.5 2.4 %collective-permute-done.4.refs_5_.refs_6_ = bf16[576,128]{1,0:T(8,128)(2,1)S(1)} collective-permute-done((bf16[576,128]{1,0:T(8,128)(2,1)}, bf16[576,128]{1,0:T(8,128)(2,1)S(1)}, u32[]{:S(2)}, u32[]{:S(2)}) %collective-permute-start.4) | collective-permute-done | bytes 147488 | tf_op jit(solution)/shard_map/ppermute | solution.py:560
  16.9 3.2 %shard_map.187 = (bf16[512,128]{1,0:T(8,128)(2,1)S(1)}, bf16[512,128]{1,0:T(8,128)(2,1)S(1)}, bf16[512,128]{1,0:T(8,128)(2,1)S(1)}, bf16[512,128]{1,0:T(8,128)(2,1)S(1)}, bf16[16,128,128]{2,1,0:T(8,128)(2,1)S(1)}) custom-call(s32[1,1]{1,0:T(1,128)S(6)} %copy.20.tile_count, s32[3,24,128]{2,1,0:T(8,128)S(1)} %get-tuple-element.42.most, ...), custom_call_target="tpu_custom_call" | custom-call | flops 2147483648 | bytes 4784128 | tf_op jit(solution)/shard_map/pallas_call | solution.py:45
  20.2 0.8 copy-done.24
  21.0 6.3 %collective-permute-start.5 = (bf16[512,128]{1,0:T(8,128)(2,1)S(1)}, bf16[512,128]{1,0:T(8,128)(2,1)S(1)}, u32[]{:S(2)}, u32[]{:S(2)}) collective-permute-start(bf16[512,128]{1,0:T(8,128)(2,1)S(1)} %get-tuple-element.53), channel_id=1, source_target_pairs={{0,4},{4,8},{8,12},{12,16},{16,20},{20,24},{24,28},{28,0},{1,5},{5... | collective-permute-start | bytes 393224 | tf_op jit(solution)/shard_map/ppermute | solution.py:23
  27.2 0.2 collective-permute-start.6
  27.4 1.1 %copy-done.16 = bf16[17,128,128]{2,1,0:T(8,128)(2,1)S(1)} copy-done((bf16[17,128,128]{2,1,0:T(8,128)(2,1)S(1)}, bf16[17,128,128]{2,1,0:T(8,128)(2,1)}, u32[]{:S(2)}) %copy-start.16) | copy-done | bytes 557080
  28.5 1.1 %copy-done.21 = f32[12,128,128]{2,1,0:T(8,128)S(1)} copy-done((f32[12,128,128]{2,1,0:T(8,128)S(1)}, f32[12,128,128]{2,1,0:T(8,128)}, u32[]{:S(2)}) %copy-start.21) | copy-done | bytes 786456
  29.6 1.1 %copy-done.23 = f32[12,128,128]{2,1,0:T(8,128)S(1)} copy-done((f32[12,128,128]{2,1,0:T(8,128)S(1)}, f32[12,128,128]{2,1,0:T(8,128)}, u32[]{:S(2)}) %copy-start.23) | copy-done | bytes 786456
  30.7 1.0 %copy-done.25 = bf16[16,128,128]{2,1,0:T(8,128)(2,1)S(1)} copy-done((bf16[16,128,128]{2,1,0:T(8,128)(2,1)S(1)}, bf16[16,128,128]{2,1,0:T(8,128)(2,1)}, u32[]{:S(2)}) %copy-start.25) | copy-done | bytes 524312
  31.8 1.0 %copy-done.28 = bf16[12,128,128]{2,1,0:T(8,128)(2,1)S(1)} copy-done((bf16[12,128,128]{2,1,0:T(8,128)(2,1)S(1)}, bf16[12,128,128]{2,1,0:T(8,128)(2,1)}, u32[]{:S(2)}) %copy-start.28) | copy-done | bytes 393240
  32.8 1.9 %shard_map.188 = (f32[512,128]{1,0:T(8,128)S(1)}, f32[512,128]{1,0:T(8,128)S(1)}) custom-call(s32[1,1]{1,0:T(1,128)S(6)} %copy.20.tile_count, s32[3,24,128]{2,1,0:T(8,128)S(1)} %get-tuple-element.42.most, bf16[17,128,128]{2,1,0:T(8,128)(2,1)S(1)} %get-tuple-element.43.row_rank, bf16[17,128,128]{2,1,0:T(8,128)(2,1)S(1)} %copy-done.16, ...), custom_call_target="tpu_custom_call" | custom-call | flops 1073741824 | bytes 4165632 | tf_op jit(solution)/shard_map/pallas_call | solution.py:45
  34.8 1.7 %shard_map.189 = (bf16[512,128]{1,0:T(8,128)(2,1)}, bf16[512,128]{1,0:T(8,128)(2,1)S(1)}, bf16[512,128]{1,0:T(8,128)(2,1)S(1)}, bf16[512,128]{1,0:T(8,128)(2,1)S...) custom-call(f32[8,128]{1,0:T(8,128)S(1)} %get-tuple-element.41.vecto, ...), custom_call_target="tpu_custom_call" | custom-call | flops 117440512 | bytes 1970176 | tf_op jit(solution)/shard_map/pallas_call | solution.py:45
  36.4 4.0 %collective-permute-start.11 = (bf16[512,128]{1,0:T(8,128)(2,1)S(1)}, bf16[512,128]{1,0:T(8,128)(2,1)S(1)}, u32[]{:S(2)}, u32[]{:S(2)}) collective-permute-start(bf16[512,128]{1,0:T(8,128)(2,1)S(1)} %get-tuple-element.68.refs_0_.d_own), channel_id=1, source_target_pairs={{0,4},{4,8},{8,12},{12,16},{16,20},{20,24},{24,28},{28,0},{1,5},{5... | collective-permute-start | bytes 393224 | tf_op jit(solution)/shard_map/ppermute | solution.py:23
  40.4 0.4 shard_map.190
  40.8 0.2 collective-permute-start.9
  41.0 1.7 %shard_map.191.refs_2_ = f32[16,128,128]{2,1,0:T(8,128)S(1)} custom-call(s32[1,1]{1,0:T(1,128)S(6)} %copy.20.tile_count, s32[3,24,128]{2,1,0:T(8,128)S(1)} %get-tuple-element.42.most, bf16[17,128,128]{2,1,0:T(8,128)(2,1)S(1)} %get-tuple-element.67.col_rank, bf16[16,128,128]{2,1,0:T(8,128)(2,1)S(1)} %copy-done.26, bf16[12,128,128]{2,1,0:T(8,128)(2,1)S(1)} %copy-done.28, ...), custom_call_target="tpu_custom_call" | custom-call | flops 1073741824 | bytes 2691072 | tf_op jit(solution)/shard_map/pallas_call | solution.py:45
  42.7 1.6 %collective-permute-done.9 = bf16[256,128]{1,0:T(8,128)(2,1)S(1)} collective-permute-done((bf16[256,128]{1,0:T(8,128)(2,1)S(1)}, bf16[256,128]{1,0:T(8,128)(2,1)S(1)}, u32[]{:S(2)}, u32[]{:S(2)}) %collective-permute-start.9) | collective-permute-done | bytes 65568 | tf_op jit(solution)/shard_map/ppermute | solution.py:560
  44.3 2.6 %collective-permute-start.10 = (bf16[128,128]{1,0:T(8,128)(2,1)S(1)}, bf16[128,128]{1,0:T(8,128)(2,1)S(1)}, u32[]{:S(2)}, u32[]{:S(2)}) collective-permute-start(bf16[128,128]{1,0:T(8,128)(2,1)S(1)} %select_convert_fusion), channel_id=1, source_target_pairs={{0,2},{1,3},{2,0},{3,1},{4,6},{5,7},{6,4},{7,5},{8,10},{9,11},{10,... | collective-permute-start | bytes 98312 | tf_op jit(solution)/shard_map/ppermute | solution.py:560
  47.0 4.1 %shard_map.192 = (f32[512,128]{1,0:T(8,128)S(1)}, bf16[512,128]{1,0:T(8,128)(2,1)S(1)}, bf16[1024,128]{1,0:T(8,128)(2,1)S(1)}, bf16[128,128]{1,0:T(8,128)(2,1)S(1)}) custom-call(s32[1,1]{1,0:T(1,128)S(6)} %copy.20.tile_count, s32[3,24,128]{2,1,0:T(8,128)S(1)} %get-tuple-element.42.most, bf16[17,128,128]{2,1,0:T(8,128)(2,1)S(1)} %get-tuple-element.67.col_rank, ...), custom_call_target="tpu_custom_call" | custom-call | flops 2147483648 | bytes 4100096 | tf_op jit(solution)/shard_map/pallas_call | solution.py:45
  51.1 0.3 shard_map.193
  51.5 5.0 %collective-permute-start.13 = (bf16[192,128]{1,0:T(8,128)(2,1)S(1)}, bf16[192,128]{1,0:T(8,128)(2,1)S(1)}, u32[]{:S(2)}, u32[]{:S(2)}) collective-permute-start(bf16[192,128]{1,0:T(8,128)(2,1)S(1)} %broadcast_select_fusion), channel_id=1, source_target_pairs={{0,4},{4,0},{8,12},{12,8},{16,20},{20,16},{24,28},{28,24},{1,5},{5... | collective-permute-start | bytes 147464 | tf_op jit(solution)/shard_map/ppermute | solution.py:560
  56.5 0.9 collective-permute-done.13
  57.4 0.3 collective-permute-start.14
  57.7 2.7 %collective-permute-done.14 = bf16[192,128]{1,0:T(8,128)(2,1)S(1)} collective-permute-done((bf16[192,128]{1,0:T(8,128)(2,1)S(1)}, bf16[192,128]{1,0:T(8,128)(2,1)S(1)}, u32[]{:S(2)}, u32[]{:S(2)}) %collective-permute-start.14) | collective-permute-done | bytes 49184 | tf_op jit(solution)/shard_map/ppermute | solution.py:560
  60.5 4.7 %collective-permute-done.15.refs_0_ = bf16[1024,128]{1,0:T(8,128)(2,1)S(1)} collective-permute-done((bf16[1024,128]{1,0:T(8,128)(2,1)S(1)}, bf16[1024,128]{1,0:T(8,128)(2,1)S(1)}, u32[]{:S(2)}, u32[]{:S(2)}) %collective-permute-start.15) | collective-permute-done | bytes 262176 | tf_op jit(solution)/shard_map/ppermute | solution.py:560
  65.2 0.4 collective-permute-start.16
  65.6 2.5 %collective-permute-done.16 = bf16[192,128]{1,0:T(8,128)(2,1)S(1)} collective-permute-done((bf16[192,128]{1,0:T(8,128)(2,1)S(1)}, bf16[192,128]{1,0:T(8,128)(2,1)S(1)}, u32[]{:S(2)}, u32[]{:S(2)}) %collective-permute-start.16) | collective-permute-done | bytes 49184 | tf_op jit(solution)/shard_map/ppermute | solution.py:560
  68.1 2.4 %collective-permute-start.17 = (bf16[192,128]{1,0:T(8,128)(2,1)S(1)}, bf16[192,128]{1,0:T(8,128)(2,1)S(1)}, u32[]{:S(2)}, u32[]{:S(2)}) collective-permute-start(bf16[192,128]{1,0:T(8,128)(2,1)S(1)} %add_convert_fusion.1), channel_id=1, source_target_pairs={{0,2},{1,3},{2,0},{3,1},{4,6},{5,7},{6,4},{7,5},{8,10},{9,11},{10,... | collective-permute-start | bytes 147464 | tf_op jit(solution)/shard_map/ppermute | solution.py:560
  70.6 0.1 collective-permute-start.18
  70.7 1.9 %collective-permute-done.17 = bf16[192,128]{1,0:T(8,128)(2,1)S(1)} collective-permute-done((bf16[192,128]{1,0:T(8,128)(2,1)S(1)}, bf16[192,128]{1,0:T(8,128)(2,1)S(1)}, u32[]{:S(2)}, u32[]{:S(2)}) %collective-permute-start.17) | collective-permute-done | bytes 49184 | tf_op jit(solution)/shard_map/ppermute | solution.py:560
  72.6 7.6 %collective-permute-done.18.refs_1_ = bf16[512,128]{1,0:T(8,128)(2,1)S(1)} collective-permute-done((bf16[512,128]{1,0:T(8,128)(2,1)S(1)}, bf16[512,128]{1,0:T(8,128)(2,1)S(1)}, u32[]{:S(2)}, u32[]{:S(2)}) %collective-permute-start.18) | collective-permute-done | bytes 131104 | tf_op jit(solution)/shard_map/ppermute | solution.py:560
  80.2 0.2 shard_map.194.from_send
  80.4 0.1 collective-permute-start.19
  80.5 2.1 %collective-permute-start.7 = (bf16[512,128]{1,0:T(8,128)(2,1)S(1)}, bf16[512,128]{1,0:T(8,128)(2,1)S(1)}, u32[]{:S(2)}, u32[]{:S(2)}) collective-permute-start(bf16[512,128]{1,0:T(8,128)(2,1)S(1)} %get-tuple-element.57.n_high), channel_id=1, source_target_pairs={{0,4},{4,8},{8,12},{12,16},{16,20},{20,24},{24,28},{28,0},{1,5},{5... | collective-permute-start | bytes 393224 | tf_op jit(solution)/shard_map/ppermute | solution.py:23
  82.6 1.0 %collective-permute-done.19 = bf16[256,128]{1,0:T(8,128)(2,1)S(1)} collective-permute-done((bf16[256,128]{1,0:T(8,128)(2,1)S(1)}, bf16[256,128]{1,0:T(8,128)(2,1)S(1)}, u32[]{:S(2)}, u32[]{:S(2)}) %collective-permute-start.19) | collective-permute-done | bytes 65568 | tf_op jit(solution)/shard_map/ppermute | solution.py:560
  83.7 2.3 %collective-permute-start.20 = (bf16[384,128]{1,0:T(8,128)(2,1)S(1)}, bf16[384,128]{1,0:T(8,128)(2,1)S(1)}, u32[]{:S(2)}, u32[]{:S(2)}) collective-permute-start(bf16[384,128]{1,0:T(8,128)(2,1)S(1)} %pad_maximum_fusion.mine), channel_id=1, source_target_pairs={{0,4},{4,0},{8,12},{12,8},{16,20},{20,16},{24,28},{28,24},{1,5},{5... | collective-permute-start | bytes 294920 | tf_op jit(solution)/shard_map/ppermute | solution.py:560
  86.0 1.7 %collective-permute-done.8.from_high = bf16[512,128]{1,0:T(8,128)(2,1)S(1)} collective-permute-done((bf16[512,128]{1,0:T(8,128)(2,1)S(1)}, bf16[512,128]{1,0:T(8,128)(2,1)S(1)}, u32[]{:S(2)}, u32[]{:S(2)}) %collective-permute-start.8) | collective-permute-done | bytes 131104 | tf_op jit(solution)/shard_map/ppermute | solution.py:23
  87.7 1.0 %shard_map.195 = f32[512,128]{1,0:T(8,128)} custom-call(bf16[512,128]{1,0:T(8,128)(2,1)S(1)} %copy-done.2, f32[512,128]{1,0:T(8,128)S(1)} %get-tuple-element.56.n_own.count_own, bf16[512,128]{1,0:T(8,128)(2,1)S(1)} %collective-permute-done.7.from_low, bf16[512,128]{1,0:T(8,128)(2,1)S(1)} %collective-permute-done.8.from_high, ...), custom_call_target="tpu_custom_call" | custom-call | flops 50331648 | bytes 1540096 | tf_op jit(solution)/shard_map/pallas_call | solution.py:45
  88.7 0.8 shard_map.196
  (85 shorter events, 0.4 us)
Async XLA Ops:
  2.2 9.6 %collective-permute-start = (bf16[576,128]{1,0:T(8,128)(2,1)}, bf16[576,128]{1,0:T(8,128)(2,1)S(1)}, u32[]{:S(2)}, u32[]{:S(2)}) collective-permute-start(bf16[576,128]{1,0:T(8,128)(2,1)} %get-tuple-element.46.message.refs_3_.own), channel_id=1, source_target_pairs={{0,4},{4,8},{8,12},{12,16},{16,20},{20,24},{24,28},{28,0},{1,5},{5... | collective-permute-start | bytes 442376 | tf_op jit(solution)/shard_map/ppermute | solution.py:23
  4.8 7.0 %collective-permute-start.1 = (bf16[576,128]{1,0:T(8,128)(2,1)}, bf16[576,128]{1,0:T(8,128)(2,1)S(1)}, u32[]{:S(2)}, u32[]{:S(2)}) collective-permute-start(bf16[576,128]{1,0:T(8,128)(2,1)} %get-tuple-element.46.message.refs_3_.own), channel_id=1, source_target_pairs={{0,28},{4,0},{8,4},{12,8},{16,12},{20,16},{24,20},{28,24},{1,29},{... | collective-permute-start | bytes 442376 | tf_op jit(solution)/shard_map/ppermute | solution.py:23
  4.8 9.6 %collective-permute-start.2 = (bf16[576,128]{1,0:T(8,128)(2,1)}, bf16[576,128]{1,0:T(8,128)(2,1)S(1)}, u32[]{:S(2)}, u32[]{:S(2)}) collective-permute-start(bf16[576,128]{1,0:T(8,128)(2,1)} %get-tuple-element.46.message.refs_3_.own), channel_id=1, source_target_pairs={{0,1},{1,0},{2,3},{3,2},{4,5},{5,4},{6,7},{7,6},{8,9},{9,8},{10,11... | collective-permute-start | bytes 442376 | tf_op jit(solution)/shard_map/ppermute | solution.py:560
  6.1 8.3 %collective-permute-start.3 = (bf16[576,128]{1,0:T(8,128)(2,1)}, bf16[576,128]{1,0:T(8,128)(2,1)S(1)}, u32[]{:S(2)}, u32[]{:S(2)}) collective-permute-start(bf16[576,128]{1,0:T(8,128)(2,1)} %get-tuple-element.46.message.refs_3_.own), channel_id=1, source_target_pairs={{0,2},{1,3},{2,0},{3,1},{4,6},{5,7},{6,4},{7,5},{8,10},{9,11},{10,... | collective-permute-start | bytes 442376 | tf_op jit(solution)/shard_map/ppermute | solution.py:560
  8.5 8.5 %collective-permute-start.4 = (bf16[576,128]{1,0:T(8,128)(2,1)}, bf16[576,128]{1,0:T(8,128)(2,1)S(1)}, u32[]{:S(2)}, u32[]{:S(2)}) collective-permute-start(bf16[576,128]{1,0:T(8,128)(2,1)} %get-tuple-element.46.message.refs_3_.own), channel_id=1, source_target_pairs={{0,3},{1,2},{2,1},{3,0},{4,7},{5,6},{6,5},{7,4},{8,11},{9,10},{10,... | collective-permute-start | bytes 442376 | tf_op jit(solution)/shard_map/ppermute | solution.py:560
  9.1 0.7 copy-start.11
  9.2 0.7 copy-start.12
  9.8 1.2 %copy-start.1 = (s32[1,1,16,128,128]{4,3,2,1,0:T(8,128)S(1)}, s32[1,1,16,128,128]{4,3,2,1,0:T(8,128)}, u32[]{:S(2)}) copy-start(s32[1,1,16,128,128]{4,3,2,1,0:T(8,128)} %param.21) | copy-start | bytes 3145732
  11.1 0.9 %copy-start.3 = (bf16[576,128]{1,0:T(8,128)(2,1)S(1)}, bf16[576,128]{1,0:T(8,128)(2,1)}, u32[]{:S(2)}) copy-start(bf16[576,128]{1,0:T(8,128)(2,1)} %get-tuple-element.46.message.refs_3_.own) | copy-start | bytes 442372
  11.1 0.9 %copy-start.8 = (bf16[128,128]{1,0:T(8,128)(2,1)S(1)}, bf16[128,128]{1,0:T(8,128)(2,1)}, u32[]{:S(2)}) copy-start(bf16[128,128]{1,0:T(8,128)(2,1)} %w_recv.3) | copy-start | bytes 98308
  11.1 0.9 %copy-start.9 = (bf16[128,128]{1,0:T(8,128)(2,1)S(1)}, bf16[128,128]{1,0:T(8,128)(2,1)}, u32[]{:S(2)}) copy-start(bf16[128,128]{1,0:T(8,128)(2,1)} %w_send.3) | copy-start | bytes 98308
  11.1 0.9 %copy-start.19 = (bf16[16,384]{1,0:T(8,128)(2,1)S(1)}, bf16[16,384]{1,0:T(8,128)(2,1)}, u32[]{:S(2)}) copy-start(bf16[16,384]{1,0:T(8,128)(2,1)} %get-tuple-element.45.weight_parts.refs_2_) | copy-start | bytes 36868
  11.8 5.1 %copy-start.15 = (bf16[17,128,128]{2,1,0:T(8,128)(2,1)}, bf16[17,128,128]{2,1,0:T(8,128)(2,1)S(1)}, u32[]{:S(2)}) copy-start(bf16[17,128,128]{2,1,0:T(8,128)(2,1)S(1)} %get-tuple-element.44.row_degree) | copy-start | bytes 1671172
  14.4 5.7 %copy-start.20 = (f32[12,128,128]{2,1,0:T(8,128)}, f32[12,128,128]{2,1,0:T(8,128)S(1)}, u32[]{:S(2)}) copy-start(f32[12,128,128]{2,1,0:T(8,128)S(1)} %get-tuple-element.48.sums_in) | copy-start | bytes 2359300
  14.4 5.7 %copy-start.22 = (f32[12,128,128]{2,1,0:T(8,128)}, f32[12,128,128]{2,1,0:T(8,128)S(1)}, u32[]{:S(2)}) copy-start(f32[12,128,128]{2,1,0:T(8,128)S(1)} %get-tuple-element.49.counts_in) | copy-start | bytes 2359300
  14.4 5.7 %copy-start.27 = (bf16[12,128,128]{2,1,0:T(8,128)(2,1)}, bf16[12,128,128]{2,1,0:T(8,128)(2,1)S(1)}, u32[]{:S(2)}) copy-start(bf16[12,128,128]{2,1,0:T(8,128)(2,1)S(1)} %get-tuple-element.47.receivers) | copy-start | bytes 1179652
  16.9 3.3 %copy-start.17 = (bf16[576,128]{1,0:T(8,128)(2,1)}, bf16[576,128]{1,0:T(8,128)(2,1)S(1)}, u32[]{:S(2)}) copy-start(bf16[576,128]{1,0:T(8,128)(2,1)S(1)} %collective-permute-done.4.refs_5_.refs_6_) | copy-start | bytes 442372
  20.2 0.8 copy-start.24
  21.0 13.7 %collective-permute-start.5 = (bf16[512,128]{1,0:T(8,128)(2,1)S(1)}, bf16[512,128]{1,0:T(8,128)(2,1)S(1)}, u32[]{:S(2)}, u32[]{:S(2)}) collective-permute-start(bf16[512,128]{1,0:T(8,128)(2,1)S(1)} %get-tuple-element.53), channel_id=1, source_target_pairs={{0,4},{4,8},{8,12},{12,16},{16,20},{20,24},{24,28},{28,0},{1,5},{5... | collective-permute-start | bytes 393224 | tf_op jit(solution)/shard_map/ppermute | solution.py:23
  27.2 7.5 %collective-permute-start.6 = (bf16[512,128]{1,0:T(8,128)(2,1)S(1)}, bf16[512,128]{1,0:T(8,128)(2,1)S(1)}, u32[]{:S(2)}, u32[]{:S(2)}) collective-permute-start(bf16[512,128]{1,0:T(8,128)(2,1)S(1)} %get-tuple-element.54), channel_id=1, source_target_pairs={{0,28},{4,0},{8,4},{12,8},{16,12},{20,16},{24,20},{28,24},{1,29},{... | collective-permute-start | bytes 393224 | tf_op jit(solution)/shard_map/ppermute | solution.py:23
  27.4 1.1 %copy-start.16 = (bf16[17,128,128]{2,1,0:T(8,128)(2,1)S(1)}, bf16[17,128,128]{2,1,0:T(8,128)(2,1)}, u32[]{:S(2)}) copy-start(bf16[17,128,128]{2,1,0:T(8,128)(2,1)} %copy-done.15) | copy-start | bytes 1671172
  28.5 1.1 %copy-start.21 = (f32[12,128,128]{2,1,0:T(8,128)S(1)}, f32[12,128,128]{2,1,0:T(8,128)}, u32[]{:S(2)}) copy-start(f32[12,128,128]{2,1,0:T(8,128)} %copy-done.20) | copy-start | bytes 2359300
  29.6 1.1 %copy-start.23 = (f32[12,128,128]{2,1,0:T(8,128)S(1)}, f32[12,128,128]{2,1,0:T(8,128)}, u32[]{:S(2)}) copy-start(f32[12,128,128]{2,1,0:T(8,128)} %copy-done.22) | copy-start | bytes 2359300
  30.7 1.0 %copy-start.25 = (bf16[16,128,128]{2,1,0:T(8,128)(2,1)S(1)}, bf16[16,128,128]{2,1,0:T(8,128)(2,1)}, u32[]{:S(2)}) copy-start(bf16[16,128,128]{2,1,0:T(8,128)(2,1)} %copy-done.24) | copy-start | bytes 1572868
  31.8 1.0 %copy-start.28 = (bf16[12,128,128]{2,1,0:T(8,128)(2,1)S(1)}, bf16[12,128,128]{2,1,0:T(8,128)(2,1)}, u32[]{:S(2)}) copy-start(bf16[12,128,128]{2,1,0:T(8,128)(2,1)} %copy-done.27) | copy-start | bytes 1179652
  32.8 1.9 %copy-start = (bf16[512,128]{1,0:T(8,128)(2,1)S(1)}, bf16[512,128]{1,0:T(8,128)(2,1)}, u32[]{:S(2)}) copy-start(bf16[512,128]{1,0:T(8,128)(2,1)} %latent.5) | copy-start | bytes 393220
  32.8 1.9 %copy-start.2 = (bf16[512,128]{1,0:T(8,128)(2,1)S(1)}, bf16[512,128]{1,0:T(8,128)(2,1)}, u32[]{:S(2)}) copy-start(bf16[512,128]{1,0:T(8,128)(2,1)} %cotangent.3) | copy-start | bytes 393220
  32.8 1.9 %copy-start.4 = (bf16[128,128]{1,0:T(8,128)(2,1)S(1)}, bf16[128,128]{1,0:T(8,128)(2,1)}, u32[]{:S(2)}) copy-start(bf16[128,128]{1,0:T(8,128)(2,1)} %w_edge_out.3) | copy-start | bytes 98308
  32.8 1.9 %copy-start.5 = (bf16[128,128]{1,0:T(8,128)(2,1)S(1)}, bf16[128,128]{1,0:T(8,128)(2,1)}, u32[]{:S(2)}) copy-start(bf16[128,128]{1,0:T(8,128)(2,1)} %w_node_self.3) | copy-start | bytes 98308
  32.8 1.9 %copy-start.6 = (bf16[128,128]{1,0:T(8,128)(2,1)S(1)}, bf16[128,128]{1,0:T(8,128)(2,1)}, u32[]{:S(2)}) copy-start(bf16[128,128]{1,0:T(8,128)(2,1)} %w_node_msg.1) | copy-start | bytes 98308
  32.8 1.9 %copy-start.7 = (bf16[128,128]{1,0:T(8,128)(2,1)S(1)}, bf16[128,128]{1,0:T(8,128)(2,1)}, u32[]{:S(2)}) copy-start(bf16[128,128]{1,0:T(8,128)(2,1)} %w_node_out.1) | copy-start | bytes 98308
  36.4 4.6 %copy-start.26 = (bf16[16,128,128]{2,1,0:T(8,128)(2,1)S(1)}, bf16[16,128,128]{2,1,0:T(8,128)(2,1)}, u32[]{:S(2)}) copy-start(bf16[16,128,128]{2,1,0:T(8,128)(2,1)} %copy-done.24) | copy-start | bytes 1572868
  36.4 10.5 %collective-permute-start.11 = (bf16[512,128]{1,0:T(8,128)(2,1)S(1)}, bf16[512,128]{1,0:T(8,128)(2,1)S(1)}, u32[]{:S(2)}, u32[]{:S(2)}) collective-permute-start(bf16[512,128]{1,0:T(8,128)(2,1)S(1)} %get-tuple-element.68.refs_0_.d_own), channel_id=1, source_target_pairs={{0,4},{4,8},{8,12},{12,16},{16,20},{20,24},{24,28},{28,0},{1,5},{5... | collective-permute-start | bytes 393224 | tf_op jit(solution)/shard_map/ppermute | solution.py:23
  40.4 6.5 %collective-permute-start.12 = (bf16[512,128]{1,0:T(8,128)(2,1)S(1)}, bf16[512,128]{1,0:T(8,128)(2,1)S(1)}, u32[]{:S(2)}, u32[]{:S(2)}) collective-permute-start(bf16[512,128]{1,0:T(8,128)(2,1)S(1)} %get-tuple-element.68.refs_0_.d_own), channel_id=1, source_target_pairs={{0,28},{4,0},{8,4},{12,8},{16,12},{20,16},{24,20},{28,24},{1,29},{... | collective-permute-start | bytes 393224 | tf_op jit(solution)/shard_map/ppermute | solution.py:23
  40.8 3.5 %collective-permute-start.9 = (bf16[256,128]{1,0:T(8,128)(2,1)S(1)}, bf16[256,128]{1,0:T(8,128)(2,1)S(1)}, u32[]{:S(2)}, u32[]{:S(2)}) collective-permute-start(bf16[256,128]{1,0:T(8,128)(2,1)S(1)} %get-tuple-element.66), channel_id=1, source_target_pairs={{0,1},{1,0},{2,3},{3,2},{4,5},{5,4},{6,7},{7,6},{8,9},{9,8},{10,11... | collective-permute-start | bytes 196616 | tf_op jit(solution)/shard_map/ppermute | solution.py:560
  41.0 5.9 %copy-start.29 = (bf16[12,128,128]{2,1,0:T(8,128)(2,1)S(1)}, bf16[12,128,128]{2,1,0:T(8,128)(2,1)}, u32[]{:S(2)}) copy-start(bf16[12,128,128]{2,1,0:T(8,128)(2,1)} %copy-done.27) | copy-start | bytes 1179652
  44.3 2.7 %copy-start.18 = (bf16[576,128]{1,0:T(8,128)(2,1)S(1)}, bf16[576,128]{1,0:T(8,128)(2,1)}, u32[]{:S(2)}) copy-start(bf16[576,128]{1,0:T(8,128)(2,1)} %copy-done.17) | copy-start | bytes 442372
  44.3 6.8 %collective-permute-start.10 = (bf16[128,128]{1,0:T(8,128)(2,1)S(1)}, bf16[128,128]{1,0:T(8,128)(2,1)S(1)}, u32[]{:S(2)}, u32[]{:S(2)}) collective-permute-start(bf16[128,128]{1,0:T(8,128)(2,1)S(1)} %select_convert_fusion), channel_id=1, source_target_pairs={{0,2},{1,3},{2,0},{3,1},{4,6},{5,7},{6,4},{7,5},{8,10},{9,11},{10,... | collective-permute-start | bytes 98312 | tf_op jit(solution)/shard_map/ppermute | solution.py:560
  51.5 5.9 %collective-permute-start.13 = (bf16[192,128]{1,0:T(8,128)(2,1)S(1)}, bf16[192,128]{1,0:T(8,128)(2,1)S(1)}, u32[]{:S(2)}, u32[]{:S(2)}) collective-permute-start(bf16[192,128]{1,0:T(8,128)(2,1)S(1)} %broadcast_select_fusion), channel_id=1, source_target_pairs={{0,4},{4,0},{8,12},{12,8},{16,20},{20,16},{24,28},{28,24},{1,5},{5... | collective-permute-start | bytes 147464 | tf_op jit(solution)/shard_map/ppermute | solution.py:560
  57.4 3.0 %collective-permute-start.14 = (bf16[192,128]{1,0:T(8,128)(2,1)S(1)}, bf16[192,128]{1,0:T(8,128)(2,1)S(1)}, u32[]{:S(2)}, u32[]{:S(2)}) collective-permute-start(bf16[192,128]{1,0:T(8,128)(2,1)S(1)} %add_convert_fusion.3), channel_id=1, source_target_pairs={{0,8},{4,12},{8,0},{12,4},{16,24},{20,28},{24,16},{28,20},{1,9},{5... | collective-permute-start | bytes 147464 | tf_op jit(solution)/shard_map/ppermute | solution.py:560
  57.7 7.4 %collective-permute-start.15 = (bf16[1024,128]{1,0:T(8,128)(2,1)S(1)}, bf16[1024,128]{1,0:T(8,128)(2,1)S(1)}, u32[]{:S(2)}, u32[]{:S(2)}) collective-permute-start(bf16[1024,128]{1,0:T(8,128)(2,1)S(1)} %get-tuple-element.71), channel_id=1, source_target_pairs={{0,1},{1,0},{2,3},{3,2},{4,5},{5,4},{6,7},{7,6},{8,9},{9,8},{10,11... | collective-permute-start | bytes 786440 | tf_op jit(solution)/shard_map/ppermute | solution.py:560
  65.2 2.9 %collective-permute-start.16 = (bf16[192,128]{1,0:T(8,128)(2,1)S(1)}, bf16[192,128]{1,0:T(8,128)(2,1)S(1)}, u32[]{:S(2)}, u32[]{:S(2)}) collective-permute-start(bf16[192,128]{1,0:T(8,128)(2,1)S(1)} %add_convert_fusion.2), channel_id=1, source_target_pairs={{0,16},{4,20},{8,24},{12,28},{16,0},{20,4},{24,8},{28,12},{1,17},{... | collective-permute-start | bytes 147464 | tf_op jit(solution)/shard_map/ppermute | solution.py:560
  68.1 4.4 %collective-permute-start.17 = (bf16[192,128]{1,0:T(8,128)(2,1)S(1)}, bf16[192,128]{1,0:T(8,128)(2,1)S(1)}, u32[]{:S(2)}, u32[]{:S(2)}) collective-permute-start(bf16[192,128]{1,0:T(8,128)(2,1)S(1)} %add_convert_fusion.1), channel_id=1, source_target_pairs={{0,2},{1,3},{2,0},{3,1},{4,6},{5,7},{6,4},{7,5},{8,10},{9,11},{10,... | collective-permute-start | bytes 147464 | tf_op jit(solution)/shard_map/ppermute | solution.py:560
  70.6 9.7 %collective-permute-start.18 = (bf16[512,128]{1,0:T(8,128)(2,1)S(1)}, bf16[512,128]{1,0:T(8,128)(2,1)S(1)}, u32[]{:S(2)}, u32[]{:S(2)}) collective-permute-start(bf16[512,128]{1,0:T(8,128)(2,1)S(1)} %add_convert_fusion), channel_id=1, source_target_pairs={{0,2},{1,3},{2,0},{3,1},{4,6},{5,7},{6,4},{7,5},{8,10},{9,11},{10,... | collective-permute-start | bytes 393224 | tf_op jit(solution)/shard_map/ppermute | solution.py:560
  80.4 3.2 %collective-permute-start.19 = (bf16[256,128]{1,0:T(8,128)(2,1)S(1)}, bf16[256,128]{1,0:T(8,128)(2,1)S(1)}, u32[]{:S(2)}, u32[]{:S(2)}) collective-permute-start(bf16[256,128]{1,0:T(8,128)(2,1)S(1)} %pad_maximum_fusion.1), channel_id=1, source_target_pairs={{0,1},{1,0},{2,3},{3,2},{4,5},{5,4},{6,7},{7,6},{8,9},{9,8},{10,11... | collective-permute-start | bytes 196616 | tf_op jit(solution)/shard_map/ppermute | solution.py:560
  80.5 5.4 %collective-permute-start.7 = (bf16[512,128]{1,0:T(8,128)(2,1)S(1)}, bf16[512,128]{1,0:T(8,128)(2,1)S(1)}, u32[]{:S(2)}, u32[]{:S(2)}) collective-permute-start(bf16[512,128]{1,0:T(8,128)(2,1)S(1)} %get-tuple-element.57.n_high), channel_id=1, source_target_pairs={{0,4},{4,8},{8,12},{12,16},{16,20},{20,24},{24,28},{28,0},{1,5},{5... | collective-permute-start | bytes 393224 | tf_op jit(solution)/shard_map/ppermute | solution.py:23
  82.6 5.1 %collective-permute-start.8 = (bf16[512,128]{1,0:T(8,128)(2,1)S(1)}, bf16[512,128]{1,0:T(8,128)(2,1)S(1)}, u32[]{:S(2)}, u32[]{:S(2)}) collective-permute-start(bf16[512,128]{1,0:T(8,128)(2,1)S(1)} %get-tuple-element.58.n_low), channel_id=1, source_target_pairs={{0,28},{4,0},{8,4},{12,8},{16,12},{20,16},{24,20},{28,24},{1,29},{... | collective-permute-start | bytes 393224 | tf_op jit(solution)/shard_map/ppermute | solution.py:23
  83.7 5.1 %collective-permute-start.20 = (bf16[384,128]{1,0:T(8,128)(2,1)S(1)}, bf16[384,128]{1,0:T(8,128)(2,1)S(1)}, u32[]{:S(2)}, u32[]{:S(2)}) collective-permute-start(bf16[384,128]{1,0:T(8,128)(2,1)S(1)} %pad_maximum_fusion.mine), channel_id=1, source_target_pairs={{0,4},{4,0},{8,12},{12,8},{16,20},{20,16},{24,28},{28,24},{1,5},{5... | collective-permute-start | bytes 294920 | tf_op jit(solution)/shard_map/ppermute | solution.py:560
  (3 other events, 2.0 us)

commit v10 on v5

--- a/solution.py
+++ b/solution.py
@@ -7,8 +7,8 @@
 
 F32 = jnp.float32
 BF16 = jnp.bfloat16
-FORWARD = (4, 4, 4, 4)
-BACKWARD = (2, 2, 2, 2, 2, 2, 2, 2)
+FORWARD = (8, 8)
+BACKWARD = (16,)
 LOOPED = 4
 ROWS, COLUMNS, TABLES = 0, 1, 2
 SENDERS, RECEIVERS = 0, 1
@@ -145,12 +145,12 @@
     return (found + 1) // 2
 
 
-def pair_of(pair, order, table, tiles, member, members, blocks):
+def pair_of(pair, order, table, tiles, member, blocks):
     pair_tiles = [order[2 * pair], order[2 * pair + 1]]
     named = [pair_tiles[0], jnp.where(pair_tiles[1] == tiles, pair_tiles[0], pair_tiles[1])]
     recv_places = [table[RECEIVERS, tile] for tile in named]
     send_places = [
-        sender_place(table[SENDERS, tile], member, members, blocks) for tile in named
+        sender_place(table[SENDERS, tile], member, blocks) for tile in named
     ]
     return pair_tiles, recv_places, send_places
 
@@ -205,8 +205,8 @@
             place += 1
 
 
-def sender_place(block, member, members, blocks):
-    distance = lax.rem(member - block // blocks + members, members)
+def sender_place(block, member, blocks):
+    distance = member ^ (block // blocks)
     return distance * blocks + lax.rem(block, blocks)
 
 
@@ -227,7 +227,7 @@
         table[start + block] = found[block * size : (block + 1) * size, :].astype(BF16)
 
 
-def forward_tiles(member, members, tables, ranks_in, rows_in, sums, counts, wanted):
+def forward_tiles(member, tables, ranks_in, rows_in, sums, counts, wanted):
     tile_count, row_most, table, order, total, count = tables
     row_rank, row_degree = ranks_in
     senders, receivers = rows_in
@@ -237,7 +237,7 @@
 
     def one_pair(pair, carry):
         pair_tiles, recv_places, send_places = pair_of(
-            pair, order, table, tiles, member, members, blocks
+            pair, order, table, tiles, member, blocks
         )
         nothing = jnp.zeros((size, width), BF16)
         upper = jnp.concatenate([senders[send_places[0]], nothing], 1)
@@ -317,7 +317,6 @@
         member = lax.axis_index("grp")
         forward_tiles(
             member,
-            members,
             (tile_count, row_most, table, order, total, count),
             (row_rank, row_degree),
             (senders, receivers),
@@ -358,7 +357,6 @@
         member = lax.axis_index("grp")
         forward_tiles(
             member,
-            members,
             (tile_count, row_most, table, order, total, count),
             (row_rank, row_degree),
             (senders, receivers),
@@ -425,10 +423,9 @@
     d_message = dot_t(d_hidden_pre, w_node_msg[...]).astype(BF16)
     d_aggregate = dot_t(d_message, w_edge_out[...]).astype(BF16)
     own_rows = latent.shape[0]
-    to_low[0:own_rows, :] = d_aggregate
-    to_low[own_rows:, :] = count_low[...]
-    to_high[0:own_rows, :] = d_aggregate
-    to_high[own_rows:, :] = count_high[...]
+    for out, counts in ((to_low, count_low), (to_high, count_high)):
+        out[0:own_rows, :] = d_aggregate
+        out[own_rows:, :] = counts[...]
     aggregate_out[...] = aggregate
     message_out[...] = message
     hidden_out[...] = hidden
@@ -437,18 +434,12 @@
     d_message_out[...] = d_message
 
 
-def early_kernel(
-    latent, aggregate, message, hidden, d_update, d_hidden_pre, d_message, keep, give, grads
-):
+def early_kernel(latent, aggregate, message, hidden, d_update, d_hidden_pre, d_message, grads):
     width = latent.shape[1]
-    grads[0:width, :] = contract_rows(aggregate[...], d_message[...])
-    grads[width : 2 * width, :] = contract_rows(latent[...], d_hidden_pre[...])
-    grads[2 * width : 3 * width, :] = contract_rows(message[...], d_hidden_pre[...])
-    grads[3 * width : 4 * width, :] = contract_rows(hidden[...], d_update[...])
-    half = keep.shape[0]
-    bit = lax.axis_index("grp") & 1
-    keep[...] = grads[pl.ds(pl.multiple_of(bit * half, half), half), :]
-    give[...] = grads[pl.ds(pl.multiple_of((1 - bit) * half, half), half), :].astype(BF16)
+    grads[0:width, :] = contract_rows(aggregate[...], d_message[...]).astype(BF16)
+    grads[width : 2 * width, :] = contract_rows(latent[...], d_hidden_pre[...]).astype(BF16)
+    grads[2 * width : 3 * width, :] = contract_rows(message[...], d_hidden_pre[...]).astype(BF16)
+    grads[3 * width : 4 * width, :] = contract_rows(hidden[...], d_update[...]).astype(BF16)
 
 
 def recv_kernel(
@@ -485,7 +476,8 @@
         else:
             grad_parts, started, refs = (refs[0], None, refs[1]), refs[2], refs[3:]
             messages, refs = refs[:members], refs[members:]
-            grads_out, late_out, refs = refs[:members], refs[members], refs[members + 1 :]
+            recv_grad, early, refs = refs[0], refs[1], refs[2:]
+            grads_out, weights_out, refs = refs[:members], refs[members], refs[members + 1 :]
             d_sums, grads = refs[0], refs[-1]
         totals, col_most, table, order, sem = refs[1:6]
         size, width = senders.shape[1:]
@@ -506,7 +498,7 @@
 
         def one_pair(pair, carry):
             pair_tiles, recv_places, send_places = pair_of(
-                pair, order, table, tiles, member, members, blocks
+                pair, order, table, tiles, member, blocks
             )
             rights = []
             for recv_place, send_place in zip(recv_places, send_places):
@@ -542,13 +534,15 @@
         if own:
             return
         late = jnp.zeros((width, width), F32)
-        for distance, out in enumerate(grads_out):
+        for distance, (message, out) in enumerate(zip(messages, grads_out)):
             for block in range(blocks):
                 span = slice(block * size, (block + 1) * size)
                 found = grads[distance * blocks + block]
                 out[span, :] = found.astype(out.dtype)
-                late = late + contract_rows(messages[distance][span, :], found.astype(BF16))
-        late_out[...] = late.astype(BF16)
+                late = late + contract_rows(message[span, :], found.astype(BF16))
+        weights_out[0:width, :] = late.astype(BF16)
+        weights_out[width : 2 * width, :] = recv_grad[...]
+        weights_out[2 * width :, :] = early[...]
 
     return kernel
 
@@ -556,21 +550,6 @@
 def exchanged(value, axis, step):
     count = lax.axis_size(axis)
     return lax.ppermute(value, axis, [(source, source ^ step) for source in range(count)])
-
-
-def bit_set(axis, step):
-    return (lax.axis_index(axis) & step) != 0
-
-
-def pairwise_sum(value, axis):
-    count = lax.axis_size(axis)
-    if count & (count - 1):
-        return lax.psum(value.astype(F32), axis).astype(BF16)
-    step = 1
-    while step < count:
-        value = (value.astype(F32) + exchanged(value, axis, step).astype(F32)).astype(BF16)
-        step *= 2
-    return value
 
 
 def return_kernel(direct, w_send, own, *refs):
@@ -581,18 +560,34 @@
     latent_grad[...] = direct[...] + dot_t(d_send.astype(BF16), w_send[...])
 
 
-def last_kernel(mine, other, weight_grads, table):
-    summed = mine.shape[0] - table.shape[0] // 2
-    half = table.shape[0] // 2
-    width = mine.shape[1]
-    bit = lax.axis_index("grp") & 1
-    table[pl.ds(pl.multiple_of(bit * half, half), half), :] = mine[0:half, :].astype(F32)
-    table[pl.ds(pl.multiple_of((1 - bit) * half, half), half), :] = other[0:half, :].astype(F32)
-    for item in range(summed // width):
-        span = slice(half + item * width, half + (item + 1) * width)
-        weight_grads[item] = mine[span, :].astype(F32) + other[span, :].astype(F32)
-    for item in range(table.shape[0] // width):
-        weight_grads[summed // width + item] = table[item * width : (item + 1) * width, :]
+def sum_kernel(parts, copies):
+    total = parts[0].astype(F32)
+    for place in range(1, parts.shape[0]):
+        total = total + parts[place].astype(F32)
+    total = total.astype(BF16)
+    for place in range(copies.shape[0]):
+        copies[place] = total
+
+
+def last_kernel(parts, weight_grads):
+    rows = parts.shape[1]
+    for place in range(parts.shape[0]):
+        weight_grads[place * rows : (place + 1) * rows, :] = parts[place].astype(F32)
+
+
+def sum_everywhere(value):
+    axes = ("blk", "grp")
+    devices = lax.axis_size("blk") * lax.axis_size("grp")
+    rows, width = value.shape
+    share = rows // devices
+    if share * devices != rows or share % 8:
+        return lax.psum(value.astype(F32), axes)
+    shares = value.reshape(devices, share, width)
+    shares = lax.all_to_all(shares, axes, split_axis=0, concat_axis=0, tiled=True)
+    (copies,) = call(sum_kernel, [like(shares.shape, BF16)], [shares], flops=value.size)
+    shares = lax.all_to_all(copies, axes, split_axis=0, concat_axis=0, tiled=True)
+    (total,) = call(last_kernel, [like((rows, width), F32)], [shares], flops=value.size)
+    return total
 
 
 def body(
@@ -619,8 +614,8 @@
     blocks = own_rows // size
     members = lax.axis_size("grp")
     node_like = like((own_rows, width), BF16)
+    pair_like = like((2 * own_rows, width), BF16)
     node_float = like((own_rows, width), F32)
-    pair_like = like((2 * own_rows, width), BF16)
     tile_like = like((tiles + 1, size, size), BF16)
     most_like = like((3, tiles + 8, size), jnp.int32)
     vectors_like = like((8, width), F32)
@@ -632,7 +627,7 @@
         [latent, positions, pos_weight],
         grant=60,
     )
-    messages = [message] + [shifted(message, "grp", distance) for distance in range(1, members)]
+    messages = [message] + [exchanged(message, "grp", distance) for distance in range(1, members)]
     row_rank, row_degree, col_rank, most, vectors = call(
         ranks_kernel,
         [tile_like] * 3 + [most_like, vectors_like],
@@ -647,8 +642,7 @@
         scalars=[tile_count],
         flops=8 * tiles * size * size * size,
     )
-    near, most = lax.optimization_barrier((message, most))
-    sides = [shifted(near, "blk", 1), shifted(near, "blk", -1)]
+    sides = [shifted(message, "blk", 1), shifted(message, "blk", -1)]
     tables = [
         pltpu.SMEM(most.shape[1:], jnp.int32),
         pltpu.SMEM((8, size), jnp.int32),
@@ -726,23 +720,12 @@
         flops=14 * own_rows * width * width,
     )
     from_low, from_high = shifted(to_high, "blk", 1), shifted(to_low, "blk", -1)
-    half = 4 * width // 2
-    share, given = call(
+    (early,) = call(
         early_kernel,
-        [like((half, width), F32), like((half, width), BF16)],
+        [like((4 * width, width), BF16)],
         [latent, aggregate, message_out, hidden, d_update, d_hidden_pre, d_message],
-        scratch=[pltpu.VMEM((2 * half, width), F32)],
         flops=8 * own_rows * width * width,
     )
-    share = share + exchanged(given, "grp", 1).astype(F32)
-    step = 2
-    while step < members:
-        half = share.shape[0] // 2
-        high = bit_set("grp", step)
-        given = jnp.where(high, share[:half], share[half:]).astype(BF16)
-        share = jnp.where(high, share[half:], share[:half])
-        share = share + exchanged(given, "grp", step).astype(F32)
-        step *= 2
     back_scratch = [
         pltpu.VMEM((3 * blocks, size, width), BF16),
         pltpu.VMEM((2, size, width), F32),
@@ -774,45 +757,24 @@
         ],
         flops=8 * own_rows * width * width,
     )
-    *send_grads, late = call(
+    *send_grads, weights = call(
         make_backward(members, blocks, False),
-        [node_float] + [node_like] * (members - 1) + [like((width, width), BF16)],
-        [col_rank, senders, receivers, from_low, from_high, started, *messages],
+        [node_float] + [node_like] * (members - 1) + [like((6 * width, width), BF16)],
+        [col_rank, senders, receivers, from_low, from_high, started, *messages, recv_grad, early],
         scalars=[tile_count],
         far=[most],
         scratch=back_scratch + [pltpu.VMEM((members * blocks, size, width), F32)],
         flops=tile_flops,
     )
-    back = [shifted(send_grads[distance], "grp", -distance) for distance in range(1, members)]
-    chain = jnp.concatenate([share.astype(BF16), late, recv_grad], 0)
-    chain = pairwise_sum(chain, "blk")
+    back = [exchanged(send_grads[distance], "grp", distance) for distance in range(1, members)]
+    weight_grads = sum_everywhere(weights)
     (latent_grad,) = call(
         return_kernel,
         [node_float],
         [direct, w_send, send_grads[0], *back],
         flops=2 * own_rows * width * width,
     )
-    chain, latent_grad = lax.optimization_barrier((chain, latent_grad))
-    share, summed = chain[: -2 * width], chain[-2 * width :]
-    step = members // 2
-    while step > 1:
-        other = exchanged(jnp.concatenate([share, summed], 0), "grp", step)
-        others = other[: -2 * width]
-        high = bit_set("grp", step)
-        share = jnp.concatenate(
-            [jnp.where(high, others, share), jnp.where(high, share, others)], 0
-        )
-        summed = (summed.astype(F32) + other[-2 * width :].astype(F32)).astype(BF16)
-        step //= 2
-    chain = jnp.concatenate([share, summed], 0)
-    other = exchanged(chain, "grp", 1)
-    (weight_grads,) = call(
-        last_kernel,
-        [like((6, width, width), F32)],
-        [chain, other],
-        scratch=[pltpu.VMEM((4 * width, width), F32)],
-    )
-    return (new_latent, latent_grad, weight_grads)
+    return (new_latent, latent_grad, weight_grads.reshape(6, width, width))
 
 
 def solution(mesh):

time: 84.6 us -> 84.7 us (level); the launches traced: 85.2 us -> 83.4 us
  blocking collectives: 0 us -> 11 us
  waiting for transfers between devices: 26.8 us -> 19.8 us
  starting transfers between devices: 26.6 us -> 20.1 us
  Pallas kernels: 27.9 us -> 28.9 us
    all_to_all x0 -> x1, blocking collectives: none -> 11 us  [sum_everywhere(): lax.all_to_all(shares, axes, split_axis=0, concat_axis=0, tiled=True)]
    ppermute x12 -> x6, starting transfers between devices: 19 us -> 8.67 us  [shifted(): return lax.ppermute(value, axis, pairs)]
    ppermute x12 -> x6, waiting for transfers between devices: 12.7 us -> 3.15 us  [shifted(): return lax.ppermute(value, axis, pairs)]
    all_to_all x0 -> x1, starting transfers between devices: none -> 2.58 us  [sum_everywhere(): lax.all_to_all(copies, axes, split_axis=0, concat_axis=0, tiled=True)]
    ppermute x7 -> x6, waiting for transfers between devices: 14 us -> 16.6 us  [exchanged(): lax.ppermute(value, axis, [(source, source ^ step) for source in range(co...]
    ppermute x7 -> x6, starting transfers between devices: 7.6 us -> 8.84 us  [exchanged(): lax.ppermute(value, axis, [(source, source ^ step) for source in range(co...]
    pallas_call x12 -> x13, Pallas kernels: 27.9 us -> 28.9 us  [call(): pl.pallas_call(kernel, out_shape=[jax.ShapeDtypeStruct(o.shape, o.dtype)...]
    unnamed x36 -> x32, local copies, waits for them, and re-layouts: 2.13 us -> 2.1 us
  transfers between devices with their start and end apart: 19 -> 13, of which waited for: 8 -> 5; matrix products, arithmetic and copies ran while one was open for 0% -> 0% of each run, Pallas kernels for 13% -> 15%
where the time goes in v10:
time: 84.7 us; the launch traced here: 83.4 us
  Pallas kernels  28.9 us (34%)
  starting transfers between devices  20.1 us (24%)
  waiting for transfers between devices  19.8 us (23%)
  blocking collectives  11 us (13%)
  local copies, waits for them, and re-layouts  2.1 us (2%)
  between operations  1.51 us (2%)
    pallas_call x13, Pallas kernels, call(): pl.pallas_call(kernel, out_shape=[jax.ShapeDtypeStruct(o.shape, o.dtype)...  28.9 us
    ppermute x6, waiting for transfers between devices, exchanged(): lax.ppermute(value, axis, [(source, source ^ step) for source in range(co...  16.6 us
    all_to_all x1, blocking collectives, sum_everywhere(): lax.all_to_all(shares, axes, split_axis=0, concat_axis=0, tiled=True)  11 us
    ppermute x6, starting transfers between devices, exchanged(): lax.ppermute(value, axis, [(source, source ^ step) for source in range(co...  8.84 us
    ppermute x6, starting transfers between devices, shifted(): return lax.ppermute(value, axis, pairs)  8.67 us
    ppermute x6, waiting for transfers between devices, shifted(): return lax.ppermute(value, axis, pairs)  3.15 us
    all_to_all x1, starting transfers between devices, sum_everywhere(): lax.all_to_all(copies, axes, split_axis=0, concat_axis=0, tiled=True)  2.58 us
    unnamed x32, local copies, waits for them, and re-layouts  2.1 us
  transfers between devices with their start and end apart: 13, of which 5 were waited for; matrix products, arithmetic and copies ran while one was open for 0% of the time, Pallas kernels for 15%

profile of v10, /device:TPU:0, one launch (start us, length us, event | category | flops | bytes accessed | tf_op | source)
XLA Modules:
  0.0 83.4 jit_solution(12945258348392393204)
XLA Ops:
  0.6 1.6 %shard_map.185 = (bf16[576,128]{1,0:T(8,128)(2,1)}, bf16[16,384]{1,0:T(8,128)(2,1)}) custom-call(bf16[512,128]{1,0:T(8,128)(2,1)} %latent.7, f32[3,512]{1,0:T(4,128)} %positions.1, f32[3,128]{1,0:T(4,128)} %pos_weight.1), custom_call_target="tpu_custom_call" | custom-call | bytes 298496 | tf_op jit(solution)/shard_map/pallas_call | solution.py:45
  2.2 3.3 %collective-permute-start.1 = (bf16[576,128]{1,0:T(8,128)(2,1)}, bf16[576,128]{1,0:T(8,128)(2,1)S(1)}, u32[]{:S(2)}, u32[]{:S(2)}) collective-permute-start(bf16[576,128]{1,0:T(8,128)(2,1)} %get-tuple-element.42.message.refs_3_), channel_id=1, source_target_pairs={{0,28},{4,0},{8,4},{12,8},{16,12},{20,16},{24,20},{28,24},{1,29},{... | collective-permute-start | bytes 442376 | tf_op jit(solution)/shard_map/ppermute | solution.py:23
  5.6 0.0 collective-permute-start
  5.6 3.6 %collective-permute-start.4 = (bf16[576,128]{1,0:T(8,128)(2,1)}, bf16[576,128]{1,0:T(8,128)(2,1)S(1)}, u32[]{:S(2)}, u32[]{:S(2)}) collective-permute-start(bf16[576,128]{1,0:T(8,128)(2,1)} %get-tuple-element.42.message.refs_3_), channel_id=1, source_target_pairs={{0,3},{1,2},{2,1},{3,0},{4,7},{5,6},{6,5},{7,4},{8,11},{9,10},{10,... | collective-permute-start | bytes 442376 | tf_op jit(solution)/shard_map/ppermute | solution.py:552
  9.2 0.0 collective-permute-start.3
  9.2 0.8 collective-permute-start.2
  10.6 0.0 copy-start.12
  10.6 0.0 copy-start.13
  10.6 0.0 copy-start.9
  10.7 0.0 copy-start.10
  10.7 0.0 copy-start.11
  10.7 0.6 copy-done.12
  11.3 0.0 copy-done.13
  11.3 0.0 copy-done.9
  11.3 0.0 copy-done.10
  11.3 0.0 copy-done.11
  11.3 1.2 %copy-done.1 = s32[1,1,16,128,128]{4,3,2,1,0:T(8,128)S(1)} copy-done((s32[1,1,16,128,128]{4,3,2,1,0:T(8,128)S(1)}, s32[1,1,16,128,128]{4,3,2,1,0:T(8,128)}, u32[]{:S(2)}) %copy-start.1) | copy-done | bytes 1048600
  12.6 0.7 shard_map.184
  13.3 0.0 collective-permute-done.1.high
  13.4 0.2 copy-done.14
  13.5 4.0 %shard_map.186 = (bf16[4,128,128]{2,1,0:T(8,128)(2,1)S(1)}, bf16[12,128,128]{2,1,0:T(8,128)(2,1)S(1)}, f32[12,128,128]{2,1,0:T(8,128)S(1)}, f32[12,128,128]{2,1,0:T(8,128)S(1)}) custom-call(s32[1,1]{1,0:T(1,128)S(6)} %copy.20.tile_count, s32[3,24,128]{2,1,0:T(8,128)S(1)} %get-tuple-element.38.most, bf16[17,128,128]{2,1,0:T(8,128)(2,1)S(1)} %get-tuple-element.39.row_rank, ...), custom_call_target="tpu_custom_call" | custom-call | flops 1073741824 | bytes 3772416 | tf_op jit(solution)/shard_map/pallas_call | solution.py:45
  17.6 4.2 %collective-permute-done.3.refs_4_.refs_5_ = bf16[576,128]{1,0:T(8,128)(2,1)S(1)} collective-permute-done((bf16[576,128]{1,0:T(8,128)(2,1)}, bf16[576,128]{1,0:T(8,128)(2,1)S(1)}, u32[]{:S(2)}, u32[]{:S(2)}) %collective-permute-start.3) | collective-permute-done | bytes 147488 | tf_op jit(solution)/shard_map/ppermute | solution.py:552
  21.8 0.0 collective-permute-done.2.refs_3_.refs_4_
  21.8 5.4 %shard_map.187 = (bf16[512,128]{1,0:T(8,128)(2,1)S(1)}, bf16[512,128]{1,0:T(8,128)(2,1)S(1)}, bf16[512,128]{1,0:T(8,128)(2,1)S(1)}, bf16[512,128]{1,0:T(8,128)(2,1)S(1)}, bf16[16,128,128]{2,1,0:T(8,128)(2,1)S(1)}) custom-call(s32[1,1]{1,0:T(1,128)S(6)} %copy.20.tile_count, s32[3,24,128]{2,1,0:T(8,128)S(1)} %get-tuple-element.38.most, ...), custom_call_target="tpu_custom_call" | custom-call | flops 2147483648 | bytes 4784128 | tf_op jit(solution)/shard_map/pallas_call | solution.py:45
  27.1 0.1 collective-permute-start.5
  27.2 2.6 %collective-permute-start.6 = (bf16[512,128]{1,0:T(8,128)(2,1)S(1)}, bf16[512,128]{1,0:T(8,128)(2,1)S(1)}, u32[]{:S(2)}, u32[]{:S(2)}) collective-permute-start(bf16[512,128]{1,0:T(8,128)(2,1)S(1)} %get-tuple-element.50), channel_id=1, source_target_pairs={{0,28},{4,0},{8,4},{12,8},{16,12},{20,16},{24,20},{28,24},{1,29},{... | collective-permute-start | bytes 393224 | tf_op jit(solution)/shard_map/ppermute | solution.py:23
  29.8 0.0 copy-start.5
  29.9 0.0 copy-start.6
  29.9 2.9 %shard_map.188 = (f32[512,128]{1,0:T(8,128)S(1)}, f32[512,128]{1,0:T(8,128)S(1)}) custom-call(s32[1,1]{1,0:T(1,128)S(6)} %copy.20.tile_count, s32[3,24,128]{2,1,0:T(8,128)S(1)} %get-tuple-element.38.most, bf16[17,128,128]{2,1,0:T(8,128)(2,1)S(1)} %get-tuple-element.39.row_rank, bf16[17,128,128]{2,1,0:T(8,128)(2,1)S(1)} %get-tuple-element.40.row_degree, ...), custom_call_target="tpu_custom_call" | custom-call | flops 1073741824 | bytes 4165632 | tf_op jit(solution)/shard_map/pallas_call | solution.py:45
  32.8 0.4 collective-permute-done.5.sum_low
  33.2 0.0 collective-permute-done.6.sum_high
  33.3 1.4 %shard_map.189 = (bf16[512,128]{1,0:T(8,128)(2,1)}, bf16[1024,128]{1,0:T(8,128)(2,1)S(1)}, bf16[1024,128]{1,0:T(8,128)(2,1)S(1)}, bf16[512,128]{1,0:T(8,128)(2,1...) custom-call(f32[8,128]{1,0:T(8,128)S(1)} %get-tuple-element.37.vecto, ...), custom_call_target="tpu_custom_call" | custom-call | flops 117440512 | bytes 2625536 | tf_op jit(solution)/shard_map/pallas_call | solution.py:45
  34.7 2.6 %collective-permute-start.8 = (bf16[1024,128]{1,0:T(8,128)(2,1)S(1)}, bf16[1024,128]{1,0:T(8,128)(2,1)S(1)}, u32[]{:S(2)}, u32[]{:S(2)}) collective-permute-start(bf16[1024,128]{1,0:T(8,128)(2,1)S(1)} %get-tuple-element.56.refs_0_), channel_id=1, source_target_pairs={{0,28},{4,0},{8,4},{12,8},{16,12},{20,16},{24,20},{28,24},{1,29},{... | collective-permute-start | bytes 786440 | tf_op jit(solution)/shard_map/ppermute | solution.py:23
  37.3 0.3 shard_map.192.refs_8_
  37.6 3.4 %shard_map.191.refs_2_ = f32[16,128,128]{2,1,0:T(8,128)S(1)} custom-call(s32[1,1]{1,0:T(1,128)S(6)} %copy.20.tile_count, s32[3,24,128]{2,1,0:T(8,128)S(1)} %get-tuple-element.38.most, bf16[17,128,128]{2,1,0:T(8,128)(2,1)S(1)} %get-tuple-element.60.col_rank, bf16[16,128,128]{2,1,0:T(8,128)(2,1)S(1)} %get-tuple-element.47.refs_0_.senders, ...), custom_call_target="tpu_custom_call" | custom-call | flops 1073741824 | bytes 2822144 | tf_op jit(solution)/shard_map/pallas_call | solution.py:45
  41.1 2.7 %collective-permute-done.7.from_low.refs_0_ = bf16[1024,128]{1,0:T(8,128)(2,1)S(1)} collective-permute-done((bf16[1024,128]{1,0:T(8,128)(2,1)S(1)}, bf16[1024,128]{1,0:T(8,128)(2,1)S(1)}, u32[]{:S(2)}, u32[]{:S(2)}) %collective-permute-start.7) | collective-permute-done | bytes 262176 | tf_op jit(solution)/shard_map/ppermute | solution.py:23
  43.8 0.4 shard_map.190
  44.2 6.3 %shard_map.193 = (f32[512,128]{1,0:T(8,128)S(1)}, bf16[512,128]{1,0:T(8,128)(2,1)S(1)}, bf16[512,128]{1,0:T(8,128)(2,1)S(1)}, bf16[512,128]{1,0:T(8,128)(2,1)S(1)}, bf16[768,128]{1,0:T(8,128)(2,1)S(1)}) custom-call(s32[1,1]{1,0:T(1,128)S(6)} %copy.20.tile_count, s32[3,24,128]{2,1,0:T(8,128)S(1)} %get-tuple-element.38.most, ...), custom_call_target="tpu_custom_call" | custom-call | flops 2147483648 | bytes 4689920 | tf_op jit(solution)/shard_map/pallas_call | solution.py:45
  50.5 11.0 %all_to_all.10.parts = bf16[32,24,128]{2,1,0:T(8,128)(2,1)S(1)} all-to-all(bf16[32,24,128]{2,1,0:T(8,128)(2,1)S(1)} %bitcast.7), channel_id=1, replica_groups=mesh['blk'=8,'grp'=4] {'blk','grp'}, dimensions={0} | all-to-all | bytes 393216 | tf_op jit(solution)/shard_map/all_to_all | solution.py:586
  61.6 0.7 shard_map.195
  62.3 2.6 %all-to-all-start.1 = ((bf16[32,24,128]{2,1,0:T(8,128)(2,1)}), bf16[32,24,128]{2,1,0:T(8,128)(2,1)S(1)}, u32[]{:S(2)}, u32[]{:S(2)}) async-start(bf16[32,24,128]{2,1,0:T(8,128)(2,1)} %shard_map.195), calls=%async_computation.1 | async-start | bytes 393216 | tf_op jit(solution)/shard_map/all_to_all | solution.py:588
  64.9 1.8 %collective-permute-start.9 = (bf16[512,128]{1,0:T(8,128)(2,1)S(1)}, bf16[512,128]{1,0:T(8,128)(2,1)S(1)}, u32[]{:S(2)}, u32[]{:S(2)}) collective-permute-start(bf16[512,128]{1,0:T(8,128)(2,1)S(1)} %get-tuple-element.67), channel_id=1, source_target_pairs={{0,1},{1,0},{2,3},{3,2},{4,5},{5,4},{6,7},{7,6},{8,9},{9,8},{10,11... | collective-permute-start | bytes 393224 | tf_op jit(solution)/shard_map/ppermute | solution.py:552
  66.6 2.5 %collective-permute-start.10 = (bf16[512,128]{1,0:T(8,128)(2,1)S(1)}, bf16[512,128]{1,0:T(8,128)(2,1)S(1)}, u32[]{:S(2)}, u32[]{:S(2)}) collective-permute-start(bf16[512,128]{1,0:T(8,128)(2,1)S(1)} %get-tuple-element.68), channel_id=1, source_target_pairs={{0,2},{1,3},{2,0},{3,1},{4,6},{5,7},{6,4},{7,5},{8,10},{9,11},{10,... | collective-permute-start | bytes 393224 | tf_op jit(solution)/shard_map/ppermute | solution.py:552
  69.1 0.2 collective-permute-start.11
  69.3 6.9 %collective-permute-done.9.refs_0_ = bf16[512,128]{1,0:T(8,128)(2,1)S(1)} collective-permute-done((bf16[512,128]{1,0:T(8,128)(2,1)S(1)}, bf16[512,128]{1,0:T(8,128)(2,1)S(1)}, u32[]{:S(2)}, u32[]{:S(2)}) %collective-permute-start.9) | collective-permute-done | bytes 131104 | tf_op jit(solution)/shard_map/ppermute | solution.py:552
  76.2 5.5 %collective-permute-done.10.refs_1_ = bf16[512,128]{1,0:T(8,128)(2,1)S(1)} collective-permute-done((bf16[512,128]{1,0:T(8,128)(2,1)S(1)}, bf16[512,128]{1,0:T(8,128)(2,1)S(1)}, u32[]{:S(2)}, u32[]{:S(2)}) %collective-permute-start.10) | collective-permute-done | bytes 131104 | tf_op jit(solution)/shard_map/ppermute | solution.py:552
  81.7 0.9 %shard_map.194 = f32[512,128]{1,0:T(8,128)} custom-call(f32[512,128]{1,0:T(8,128)S(1)} %get-tuple-element.59.direct, bf16[128,128]{1,0:T(8,128)(2,1)S(1)} %copy-done.8, f32[512,128]{1,0:T(8,128)S(1)} %get-tuple-element.66.own, bf16[512,128]{1,0:T(8,128)(2,1)S(1)} %collective-permute-done.9.refs_0_, bf16[512,128]{1,0:T(8,128)(2,1)S(1)} %collective-permute-done.10.refs_1_, ...), custom_call_target="tpu_custom_call" | custom-call | flops 16777216 | bytes 1212416 | tf_op jit(solution)/shard_map/pallas_call | solution.py:45
  82.6 0.8 shard_map.196
  (24 shorter events, 0.0 us)
Async XLA Ops:
  2.2 11.1 %collective-permute-start.1 = (bf16[576,128]{1,0:T(8,128)(2,1)}, bf16[576,128]{1,0:T(8,128)(2,1)S(1)}, u32[]{:S(2)}, u32[]{:S(2)}) collective-permute-start(bf16[576,128]{1,0:T(8,128)(2,1)} %get-tuple-element.42.message.refs_3_), channel_id=1, source_target_pairs={{0,28},{4,0},{8,4},{12,8},{16,12},{20,16},{24,20},{28,24},{1,29},{... | collective-permute-start | bytes 442376 | tf_op jit(solution)/shard_map/ppermute | solution.py:23
  5.6 7.8 %collective-permute-start = (bf16[576,128]{1,0:T(8,128)(2,1)}, bf16[576,128]{1,0:T(8,128)(2,1)S(1)}, u32[]{:S(2)}, u32[]{:S(2)}) collective-permute-start(bf16[576,128]{1,0:T(8,128)(2,1)} %get-tuple-element.42.message.refs_3_), channel_id=1, source_target_pairs={{0,4},{4,8},{8,12},{12,16},{16,20},{20,24},{24,28},{28,0},{1,5},{5... | collective-permute-start | bytes 442376 | tf_op jit(solution)/shard_map/ppermute | solution.py:23
  5.6 12.0 %collective-permute-start.4 = (bf16[576,128]{1,0:T(8,128)(2,1)}, bf16[576,128]{1,0:T(8,128)(2,1)S(1)}, u32[]{:S(2)}, u32[]{:S(2)}) collective-permute-start(bf16[576,128]{1,0:T(8,128)(2,1)} %get-tuple-element.42.message.refs_3_), channel_id=1, source_target_pairs={{0,3},{1,2},{2,1},{3,0},{4,7},{5,6},{6,5},{7,4},{8,11},{9,10},{10,... | collective-permute-start | bytes 442376 | tf_op jit(solution)/shard_map/ppermute | solution.py:552
  9.2 12.6 %collective-permute-start.3 = (bf16[576,128]{1,0:T(8,128)(2,1)}, bf16[576,128]{1,0:T(8,128)(2,1)S(1)}, u32[]{:S(2)}, u32[]{:S(2)}) collective-permute-start(bf16[576,128]{1,0:T(8,128)(2,1)} %get-tuple-element.42.message.refs_3_), channel_id=1, source_target_pairs={{0,2},{1,3},{2,0},{3,1},{4,6},{5,7},{6,4},{7,5},{8,10},{9,11},{10,... | collective-permute-start | bytes 442376 | tf_op jit(solution)/shard_map/ppermute | solution.py:552
  9.2 12.6 %collective-permute-start.2 = (bf16[576,128]{1,0:T(8,128)(2,1)}, bf16[576,128]{1,0:T(8,128)(2,1)S(1)}, u32[]{:S(2)}, u32[]{:S(2)}) collective-permute-start(bf16[576,128]{1,0:T(8,128)(2,1)} %get-tuple-element.42.message.refs_3_), channel_id=1, source_target_pairs={{0,1},{1,0},{2,3},{3,2},{4,5},{5,4},{6,7},{7,6},{8,9},{9,8},{10,11... | collective-permute-start | bytes 442376 | tf_op jit(solution)/shard_map/ppermute | solution.py:552
  10.6 0.7 copy-start.12
  10.6 0.7 copy-start.13
  10.6 0.7 copy-start.9
  10.7 0.7 copy-start.10
  10.7 0.7 copy-start.11
  11.3 1.2 %copy-start.1 = (s32[1,1,16,128,128]{4,3,2,1,0:T(8,128)S(1)}, s32[1,1,16,128,128]{4,3,2,1,0:T(8,128)}, u32[]{:S(2)}) copy-start(s32[1,1,16,128,128]{4,3,2,1,0:T(8,128)} %param.21) | copy-start | bytes 3145732
  12.6 0.8 copy-start.7
  12.6 0.8 copy-start.8
  12.6 0.9 %copy-start.14 = (bf16[576,128]{1,0:T(8,128)(2,1)S(1)}, bf16[576,128]{1,0:T(8,128)(2,1)}, u32[]{:S(2)}) copy-start(bf16[576,128]{1,0:T(8,128)(2,1)} %get-tuple-element.42.message.refs_3_) | copy-start | bytes 442372
  12.6 0.9 %copy-start.15 = (bf16[16,384]{1,0:T(8,128)(2,1)S(1)}, bf16[16,384]{1,0:T(8,128)(2,1)}, u32[]{:S(2)}) copy-start(bf16[16,384]{1,0:T(8,128)(2,1)} %get-tuple-element.41.weight_parts.refs_2_) | copy-start | bytes 36868
  27.1 6.1 %collective-permute-start.5 = (bf16[512,128]{1,0:T(8,128)(2,1)S(1)}, bf16[512,128]{1,0:T(8,128)(2,1)S(1)}, u32[]{:S(2)}, u32[]{:S(2)}) collective-permute-start(bf16[512,128]{1,0:T(8,128)(2,1)S(1)} %get-tuple-element.49), channel_id=1, source_target_pairs={{0,4},{4,8},{8,12},{12,16},{16,20},{20,24},{24,28},{28,0},{1,5},{5... | collective-permute-start | bytes 393224 | tf_op jit(solution)/shard_map/ppermute | solution.py:23
  27.2 6.0 %collective-permute-start.6 = (bf16[512,128]{1,0:T(8,128)(2,1)S(1)}, bf16[512,128]{1,0:T(8,128)(2,1)S(1)}, u32[]{:S(2)}, u32[]{:S(2)}) collective-permute-start(bf16[512,128]{1,0:T(8,128)(2,1)S(1)} %get-tuple-element.50), channel_id=1, source_target_pairs={{0,28},{4,0},{8,4},{12,8},{16,12},{20,16},{24,20},{28,24},{1,29},{... | collective-permute-start | bytes 393224 | tf_op jit(solution)/shard_map/ppermute | solution.py:23
  29.8 3.4 %copy-start = (bf16[512,128]{1,0:T(8,128)(2,1)S(1)}, bf16[512,128]{1,0:T(8,128)(2,1)}, u32[]{:S(2)}) copy-start(bf16[512,128]{1,0:T(8,128)(2,1)} %latent.7) | copy-start | bytes 393220
  29.8 3.4 %copy-start.2 = (bf16[512,128]{1,0:T(8,128)(2,1)S(1)}, bf16[512,128]{1,0:T(8,128)(2,1)}, u32[]{:S(2)}) copy-start(bf16[512,128]{1,0:T(8,128)(2,1)} %cotangent.3) | copy-start | bytes 393220
  29.8 3.4 %copy-start.3 = (bf16[128,128]{1,0:T(8,128)(2,1)S(1)}, bf16[128,128]{1,0:T(8,128)(2,1)}, u32[]{:S(2)}) copy-start(bf16[128,128]{1,0:T(8,128)(2,1)} %w_edge_out.3) | copy-start | bytes 98308
  29.8 3.4 %copy-start.4 = (bf16[128,128]{1,0:T(8,128)(2,1)S(1)}, bf16[128,128]{1,0:T(8,128)(2,1)}, u32[]{:S(2)}) copy-start(bf16[128,128]{1,0:T(8,128)(2,1)} %w_node_self.3) | copy-start | bytes 98308
  29.8 3.4 %copy-start.5 = (bf16[128,128]{1,0:T(8,128)(2,1)S(1)}, bf16[128,128]{1,0:T(8,128)(2,1)}, u32[]{:S(2)}) copy-start(bf16[128,128]{1,0:T(8,128)(2,1)} %w_node_msg.1) | copy-start | bytes 98308
  29.9 3.4 %copy-start.6 = (bf16[128,128]{1,0:T(8,128)(2,1)S(1)}, bf16[128,128]{1,0:T(8,128)(2,1)}, u32[]{:S(2)}) copy-start(bf16[128,128]{1,0:T(8,128)(2,1)} %w_node_out.1) | copy-start | bytes 98308
  34.7 9.2 %collective-permute-start.7 = (bf16[1024,128]{1,0:T(8,128)(2,1)S(1)}, bf16[1024,128]{1,0:T(8,128)(2,1)S(1)}, u32[]{:S(2)}, u32[]{:S(2)}) collective-permute-start(bf16[1024,128]{1,0:T(8,128)(2,1)S(1)} %get-tuple-element.55), channel_id=1, source_target_pairs={{0,4},{4,8},{8,12},{12,16},{16,20},{20,24},{24,28},{28,0},{1,5},{5... | collective-permute-start | bytes 786440 | tf_op jit(solution)/shard_map/ppermute | solution.py:23
  34.7 9.2 %collective-permute-start.8 = (bf16[1024,128]{1,0:T(8,128)(2,1)S(1)}, bf16[1024,128]{1,0:T(8,128)(2,1)S(1)}, u32[]{:S(2)}, u32[]{:S(2)}) collective-permute-start(bf16[1024,128]{1,0:T(8,128)(2,1)S(1)} %get-tuple-element.56.refs_0_), channel_id=1, source_target_pairs={{0,28},{4,0},{8,4},{12,8},{16,12},{20,16},{24,20},{28,24},{1,29},{... | collective-permute-start | bytes 786440 | tf_op jit(solution)/shard_map/ppermute | solution.py:23
  62.3 20.3 %all-to-all-start.1 = ((bf16[32,24,128]{2,1,0:T(8,128)(2,1)}), bf16[32,24,128]{2,1,0:T(8,128)(2,1)S(1)}, u32[]{:S(2)}, u32[]{:S(2)}) async-start(bf16[32,24,128]{2,1,0:T(8,128)(2,1)} %shard_map.195), calls=%async_computation.1 | async-start | bytes 393216 | tf_op jit(solution)/shard_map/all_to_all | solution.py:588
  64.9 11.3 %collective-permute-start.9 = (bf16[512,128]{1,0:T(8,128)(2,1)S(1)}, bf16[512,128]{1,0:T(8,128)(2,1)S(1)}, u32[]{:S(2)}, u32[]{:S(2)}) collective-permute-start(bf16[512,128]{1,0:T(8,128)(2,1)S(1)} %get-tuple-element.67), channel_id=1, source_target_pairs={{0,1},{1,0},{2,3},{3,2},{4,5},{5,4},{6,7},{7,6},{8,9},{9,8},{10,11... | collective-permute-start | bytes 393224 | tf_op jit(solution)/shard_map/ppermute | solution.py:552
  66.6 15.1 %collective-permute-start.10 = (bf16[512,128]{1,0:T(8,128)(2,1)S(1)}, bf16[512,128]{1,0:T(8,128)(2,1)S(1)}, u32[]{:S(2)}, u32[]{:S(2)}) collective-permute-start(bf16[512,128]{1,0:T(8,128)(2,1)S(1)} %get-tuple-element.68), channel_id=1, source_target_pairs={{0,2},{1,3},{2,0},{3,1},{4,6},{5,7},{6,4},{7,5},{8,10},{9,11},{10,... | collective-permute-start | bytes 393224 | tf_op jit(solution)/shard_map/ppermute | solution.py:552
  69.1 12.6 %collective-permute-start.11 = (bf16[512,128]{1,0:T(8,128)(2,1)S(1)}, bf16[512,128]{1,0:T(8,128)(2,1)S(1)}, u32[]{:S(2)}, u32[]{:S(2)}) collective-permute-start(bf16[512,128]{1,0:T(8,128)(2,1)S(1)} %get-tuple-element.69), channel_id=1, source_target_pairs={{0,3},{1,2},{2,1},{3,0},{4,7},{5,6},{6,5},{7,4},{8,11},{9,10},{10,... | collective-permute-start | bytes 393224 | tf_op jit(solution)/shard_map/ppermute | solution.py:552

commit v11 on v10

--- a/solution.py
+++ b/solution.py
@@ -10,8 +10,7 @@
 FORWARD = (8, 8)
 BACKWARD = (16,)
 LOOPED = 4
-ROWS, COLUMNS, TABLES = 0, 1, 2
-SENDERS, RECEIVERS = 0, 1
+SENDERS, RECEIVERS, ROWS, COLUMNS = 0, 1, 2, 3
 TOGETHER = 4
 CHUNK = 32
 PARTS = 16
@@ -107,8 +106,11 @@
     for_rows = jnp.concatenate([upper, ones], 1)
     for_cols = jnp.concatenate([upper, eye], 1)
     most[...] = jnp.zeros_like(most)
-    most[2, SENDERS : SENDERS + 1, 0:tiles] = tile_send[0]
-    most[2, RECEIVERS : RECEIVERS + 1, 0:tiles] = tile_recv[0]
+    most[SENDERS : SENDERS + 1, 0:tiles] = tile_send[0]
+    most[RECEIVERS : RECEIVERS + 1, 0:tiles] = tile_recv[0]
+    lane = lax.broadcasted_iota(jnp.int32, (1, size), 1)
+    row_most = jnp.zeros((1, size), F32)
+    col_most = jnp.zeros((1, size), F32)
     vectors[...] = jnp.zeros_like(vectors)
     for place, vector in enumerate((edge_bias, node_bias, gain)):
         vectors[place : place + 1, :] = vector[...]
@@ -127,12 +129,16 @@
             row_rank[tile] = (found[span, :size] * values[item]).astype(BF16)
             degree = found[span, size:]
             row_degree[tile] = degree.astype(BF16)
-            most[0, tile : tile + 1, :] = jnp.max(degree, axis=0, keepdims=True).astype(jnp.int32)
+            longest = jnp.max(degree, axis=0, keepdims=True)
+            row_most = jnp.where(lane == tile, longest, row_most)
         for item, tile in enumerate(here):
             found = contract_rows(values_b[item], for_cols)
             ranks = found[:, :size]
             col_rank[tile] = (ranks * found[:, size:]).astype(BF16)
-            most[1, tile : tile + 1, :] = jnp.max(ranks, axis=0, keepdims=True).astype(jnp.int32)
+            longest = jnp.max(jnp.max(ranks, axis=0, keepdims=True), axis=1, keepdims=True)
+            col_most = jnp.where(lane == tile, longest, col_most)
+    most[ROWS : ROWS + 1, :] = row_most.astype(jnp.int32)
+    most[COLUMNS : COLUMNS + 1, :] = col_most.astype(jnp.int32)
 
 
 def list_tiles(order, table, tile_count, tiles, wanted):
@@ -153,17 +159,6 @@
         sender_place(table[SENDERS, tile], member, blocks) for tile in named
     ]
     return pair_tiles, recv_places, send_places
-
-
-def start_tables(most, part, extremes, table, sem):
-    sources = (most.at[part], most.at[TABLES, 0 : table.shape[0]])
-    copies = [
-        pltpu.make_async_copy(source, target, sem.at[item])
-        for item, (source, target) in enumerate(zip(sources, (extremes, table)))
-    ]
-    for copy in copies:
-        copy.start()
-    return copies
 
 
 def one_hots(rank_block, first, ranks):
@@ -228,7 +223,7 @@
 
 
 def forward_tiles(member, tables, ranks_in, rows_in, sums, counts, wanted):
-    tile_count, row_most, table, order, total, count = tables
+    tile_count, table, order, total, count = tables
     row_rank, row_degree = ranks_in
     senders, receivers = rows_in
     size, width = senders.shape[1:]
@@ -262,8 +257,9 @@
                 total[span, :] = added if fresh else total[span, :] + added
                 count[span, :] = seen if fresh else count[span, :] + seen
 
-        most = jnp.maximum(row_most[pair_tiles[0], size - 1], row_most[pair_tiles[1], size - 1])
-        done = jnp.asarray(run_groups(FORWARD, one_group, most), jnp.int32).astype(F32)
+        longest = [table[ROWS, tile] for tile in pair_tiles]
+        longest = jnp.maximum(longest[0], longest[1])
+        done = jnp.asarray(run_groups(FORWARD, one_group, longest), jnp.int32).astype(F32)
         for item, tile in enumerate(pair_tiles):
             half = slice(item * width, (item + 1) * width)
             spare = done - row_degree[tile].astype(F32)
@@ -296,12 +292,12 @@
         counts,
         total,
         count,
-        row_most,
         table,
         order,
         sem,
     ):
-        copies = start_tables(most, ROWS, row_most, table, sem)
+        copy = pltpu.make_async_copy(most, table, sem)
+        copy.start()
         blocks = senders.shape[0]
         rows = blocks * senders.shape[1]
         sums[...] = jnp.zeros_like(sums)
@@ -312,12 +308,11 @@
             lay(receivers, side * blocks, dot(latents, w_recv[...]) - placed + vectors[0:1, :])
             if side == 1:
                 lay(senders, 0, dot(latents, w_send[...]) + placed)
-        for copy in copies:
-            copy.wait()
+        copy.wait()
         member = lax.axis_index("grp")
         forward_tiles(
             member,
-            (tile_count, row_most, table, order, total, count),
+            (tile_count, table, order, total, count),
             (row_rank, row_degree),
             (senders, receivers),
             sums,
@@ -338,8 +333,9 @@
             messages, refs = refs[: members - 1], refs[members - 1 :]
             sides = ((0, refs[0], refs[2]), (2, refs[1], refs[3]))
             senders, refs = refs[4], refs[5:]
-        total, count, row_most, table, order, sem, sums, counts = refs
-        copies = start_tables(most, ROWS, row_most, table, sem)
+        total, count, table, order, sem, sums, counts = refs
+        copy = pltpu.make_async_copy(most, table, sem)
+        copy.start()
         blocks = receivers.shape[0] // 3
         size = receivers.shape[1]
         for side, *unused in sides:
@@ -352,12 +348,11 @@
                 placed = placed_of(message, weight_parts, blocks)
                 rows = dot(message[0 : blocks * size, :], w_send[...]) + placed
                 lay(senders, (distance + 1) * blocks, rows)
-        for copy in copies:
-            copy.wait()
+        copy.wait()
         member = lax.axis_index("grp")
         forward_tiles(
             member,
-            (tile_count, row_most, table, order, total, count),
+            (tile_count, table, order, total, count),
             (row_rank, row_degree),
             (senders, receivers),
             sums,
@@ -479,11 +474,12 @@
             recv_grad, early, refs = refs[0], refs[1], refs[2:]
             grads_out, weights_out, refs = refs[:members], refs[members], refs[members + 1 :]
             d_sums, grads = refs[0], refs[-1]
-        totals, col_most, table, order, sem = refs[1:6]
+        totals, table, order, sem = refs[1:5]
+        copy = pltpu.make_async_copy(most, table, sem)
+        copy.start()
         size, width = senders.shape[1:]
         rows = blocks * size
         tiles = col_rank.shape[0] - 1
-        copies = start_tables(most, COLUMNS, col_most, table, sem)
         member = lax.axis_index("grp")
         for side, part in enumerate(grad_parts):
             if part is not None:
@@ -493,8 +489,7 @@
         grads[...] = jnp.zeros_like(grads) if own else started[...]
         unit = eye_of(size)
         nothing = jnp.zeros((size, width), BF16)
-        for copy in copies:
-            copy.wait()
+        copy.wait()
 
         def one_pair(pair, carry):
             pair_tiles, recv_places, send_places = pair_of(
@@ -520,9 +515,8 @@
                             added = added + jnp.where(part[:, :width] > 0.0, part[:, width:], 0.0)
                         totals[place, span, :] = added if fresh else totals[place, span, :] + added
 
-            last = size - 1
-            most = jnp.maximum(col_most[pair_tiles[0], last], col_most[pair_tiles[1], last])
-            run_groups(BACKWARD, one_group, most)
+            longest = [table[COLUMNS, tile] for tile in pair_tiles]
+            run_groups(BACKWARD, one_group, jnp.maximum(longest[0], longest[1]))
             for item, send_place in enumerate(send_places):
                 grads[send_place] += totals[item]
             return carry
@@ -575,19 +569,20 @@
         weight_grads[place * rows : (place + 1) * rows, :] = parts[place].astype(F32)
 
 
-def sum_everywhere(value):
+def sum_everywhere(value, tied):
     axes = ("blk", "grp")
     devices = lax.axis_size("blk") * lax.axis_size("grp")
     rows, width = value.shape
     share = rows // devices
     if share * devices != rows or share % 8:
-        return lax.psum(value.astype(F32), axes)
+        return lax.psum(value.astype(F32), axes), tied
     shares = value.reshape(devices, share, width)
     shares = lax.all_to_all(shares, axes, split_axis=0, concat_axis=0, tiled=True)
     (copies,) = call(sum_kernel, [like(shares.shape, BF16)], [shares], flops=value.size)
+    copies, tied = lax.optimization_barrier((copies, tied))
     shares = lax.all_to_all(copies, axes, split_axis=0, concat_axis=0, tiled=True)
     (total,) = call(last_kernel, [like((rows, width), F32)], [shares], flops=value.size)
-    return total
+    return total, tied
 
 
 def body(
@@ -617,7 +612,7 @@
     pair_like = like((2 * own_rows, width), BF16)
     node_float = like((own_rows, width), F32)
     tile_like = like((tiles + 1, size, size), BF16)
-    most_like = like((3, tiles + 8, size), jnp.int32)
+    most_like = like((8, size), jnp.int32)
     vectors_like = like((8, width), F32)
     slab_like = like((members * blocks, size, width), BF16)
     near_like = like((3 * blocks, size, width), BF16)
@@ -644,10 +639,9 @@
     )
     sides = [shifted(message, "blk", 1), shifted(message, "blk", -1)]
     tables = [
-        pltpu.SMEM(most.shape[1:], jnp.int32),
-        pltpu.SMEM((8, size), jnp.int32),
+        pltpu.SMEM(most.shape, jnp.int32),
         pltpu.SMEM((tiles + 2,), jnp.int32),
-        pltpu.SemaphoreType.DMA((2,)),
+        pltpu.SemaphoreType.DMA,
     ]
     pair_scratch = [pltpu.VMEM((size, 2 * width), F32)] * 2 + tables
     window = pltpu.VMEM((3 * blocks, size, width), F32)
@@ -767,7 +761,7 @@
         flops=tile_flops,
     )
     back = [exchanged(send_grads[distance], "grp", distance) for distance in range(1, members)]
-    weight_grads = sum_everywhere(weights)
+    weight_grads, back = sum_everywhere(weights, back)
     (latent_grad,) = call(
         return_kernel,
         [node_float],

time: 84.7 us -> 85.6 us (1.011)
  blocking collectives: 11 us -> 0 us
  waiting for transfers between devices: 19.8 us -> 27.8 us
  starting transfers between devices: 20.1 us -> 25.2 us
  Pallas kernels: 28.9 us -> 27.7 us
    all_to_all x1 -> x0, blocking collectives: 11 us -> none  [sum_everywhere(): lax.all_to_all(shares, axes, split_axis=0, concat_axis=0, tiled=True)]
    all_to_all x1, waiting for transfers between devices: 0.01 us -> 8.43 us  [sum_everywhere(): lax.all_to_all(copies, axes, split_axis=0, concat_axis=0, tiled=True)]
    all_to_all x0 -> x1, waiting for transfers between devices: none -> 4.96 us  [sum_everywhere(): lax.all_to_all(shares, axes, split_axis=0, concat_axis=0, tiled=True)]
    ppermute x6, waiting for transfers between devices: 16.6 us -> 11.8 us  [exchanged(): lax.ppermute(value, axis, [(source, source ^ step) for source in range(co...]
    all_to_all x0 -> x1, starting transfers between devices: none -> 2.6 us  [sum_everywhere(): lax.all_to_all(shares, axes, split_axis=0, concat_axis=0, tiled=True)]
    all_to_all x1, starting transfers between devices: 2.58 us -> 5.11 us  [sum_everywhere(): lax.all_to_all(copies, axes, split_axis=0, concat_axis=0, tiled=True)]
    pallas_call x13, Pallas kernels: 28.9 us -> 27.7 us  [call(): pl.pallas_call(kernel, out_shape=[jax.ShapeDtypeStruct(o.shape, o.dtype)...]
  transfers between devices with their start and end apart: 13 -> 14, of which waited for: 5 -> 6; matrix products, arithmetic and copies ran while one was open for 0% -> 0% of each run, Pallas kernels for 15% -> 16%
where the time goes in v11:
time: 85.6 us; the launch traced here: 84.2 us
  waiting for transfers between devices  27.8 us (32%)
  Pallas kernels  27.7 us (32%)
  starting transfers between devices  25.2 us (29%)
  local copies, waits for them, and re-layouts  1.95 us (2%)
  between operations  1.53 us (2%)
    pallas_call x13, Pallas kernels, call(): pl.pallas_call(kernel, out_shape=[jax.ShapeDtypeStruct(o.shape, o.dtype)...  27.7 us
    ppermute x6, waiting for transfers between devices, exchanged(): lax.ppermute(value, axis, [(source, source ^ step) for source in range(co...  11.8 us
    ppermute x6, starting transfers between devices, exchanged(): lax.ppermute(value, axis, [(source, source ^ step) for source in range(co...  8.84 us
    ppermute x6, starting transfers between devices, shifted(): return lax.ppermute(value, axis, pairs)  8.68 us
    all_to_all x1, waiting for transfers between devices, sum_everywhere(): lax.all_to_all(copies, axes, split_axis=0, concat_axis=0, tiled=True)  8.43 us
    all_to_all x1, starting transfers between devices, sum_everywhere(): lax.all_to_all(copies, axes, split_axis=0, concat_axis=0, tiled=True)  5.11 us
    all_to_all x1, waiting for transfers between devices, sum_everywhere(): lax.all_to_all(shares, axes, split_axis=0, concat_axis=0, tiled=True)  4.96 us
    ppermute x6, waiting for transfers between devices, shifted(): return lax.ppermute(value, axis, pairs)  2.63 us
  transfers between devices with their start and end apart: 14, of which 6 were waited for; matrix products, arithmetic and copies ran while one was open for 0% of the time, Pallas kernels for 16%

profile of v11, /device:TPU:0, one launch (start us, length us, event | category | flops | bytes accessed | tf_op | source)
XLA Modules:
  0.0 84.2 jit_solution(6102841747353847926)
XLA Ops:
  0.6 1.6 %shard_map.185 = (bf16[576,128]{1,0:T(8,128)(2,1)}, bf16[16,384]{1,0:T(8,128)(2,1)}) custom-call(bf16[512,128]{1,0:T(8,128)(2,1)} %latent.7, f32[3,512]{1,0:T(4,128)} %positions.1, f32[3,128]{1,0:T(4,128)} %pos_weight.1), custom_call_target="tpu_custom_call" | custom-call | bytes 298496 | tf_op jit(solution)/shard_map/pallas_call | solution.py:44
  2.2 3.3 %collective-permute-start.1 = (bf16[576,128]{1,0:T(8,128)(2,1)}, bf16[576,128]{1,0:T(8,128)(2,1)S(1)}, u32[]{:S(2)}, u32[]{:S(2)}) collective-permute-start(bf16[576,128]{1,0:T(8,128)(2,1)} %get-tuple-element.46.message.refs_3_), channel_id=1, source_target_pairs={{0,28},{4,0},{8,4},{12,8},{16,12},{20,16},{24,20},{28,24},{1,29},{... | collective-permute-start | bytes 442376 | tf_op jit(solution)/shard_map/ppermute | solution.py:22
  5.6 0.0 collective-permute-start
  5.6 3.6 %collective-permute-start.4 = (bf16[576,128]{1,0:T(8,128)(2,1)}, bf16[576,128]{1,0:T(8,128)(2,1)S(1)}, u32[]{:S(2)}, u32[]{:S(2)}) collective-permute-start(bf16[576,128]{1,0:T(8,128)(2,1)} %get-tuple-element.46.message.refs_3_), channel_id=1, source_target_pairs={{0,3},{1,2},{2,1},{3,0},{4,7},{5,6},{6,5},{7,4},{8,11},{9,10},{10,... | collective-permute-start | bytes 442376 | tf_op jit(solution)/shard_map/ppermute | solution.py:546
  9.2 0.8 collective-permute-start.2
  10.6 0.0 copy-start.12
  10.6 0.0 copy-start.13
  10.6 0.0 copy-start.9
  10.7 0.0 copy-start.10
  10.7 0.0 copy-start.11
  10.7 0.6 copy-done.12
  11.3 0.0 copy-done.13
  11.3 0.0 copy-done.9
  11.3 0.0 copy-done.10
  11.3 0.0 copy-done.11
  11.3 1.2 %copy-done.1 = s32[1,1,16,128,128]{4,3,2,1,0:T(8,128)S(1)} copy-done((s32[1,1,16,128,128]{4,3,2,1,0:T(8,128)S(1)}, s32[1,1,16,128,128]{4,3,2,1,0:T(8,128)}, u32[]{:S(2)}) %copy-start.1) | copy-done | bytes 1048600
  12.6 1.0 %shard_map.184 = (bf16[17,128,128]{2,1,0:T(8,128)(2,1)S(1)}, bf16[17,128,128]{2,1,0:T(8,128)(2,1)S(1)}, bf16[17,128,128]{2,1,0:T(8,128)(2,1)S(1)}, s32[8,128]{1,0:T(8,128)S(1)}, f32[8,128]{1,0:T(8,128)S(1)}) custom-call(s32[1,1]{1,0:T(1,128)S(6)} %copy.20.tile_count, s32[16,128,128]{2,1,0:T(8,128)S(1)} %bitcast.6, s32[1,1,16]{2,1,0:T(1,128)S(1)} %copy-done.9, ...), custom_call_target="tpu_custom_call" | custom-call | flops 268435456 | bytes 2729600 | tf_op jit(solution)/shard_map/pallas_call | solution.py:44
  13.6 0.0 copy-done.7
  13.6 3.0 %shard_map.186 = (bf16[4,128,128]{2,1,0:T(8,128)(2,1)S(1)}, bf16[12,128,128]{2,1,0:T(8,128)(2,1)S(1)}, f32[12,128,128]{2,1,0:T(8,128)S(1)}, f32[12,128,128]{2,1,0:T(8,128)S(1)}) custom-call(s32[1,1]{1,0:T(1,128)S(6)} %copy.20.tile_count, s32[8,128]{1,0:T(8,128)S(1)} %get-tuple-element.42.most, bf16[17,128,128]{2,1,0:T(8,128)(2,1)S(1)} %get-tuple-element.43.row_rank, ...), custom_call_target="tpu_custom_call" | custom-call | flops 1073741824 | bytes 3739648 | tf_op jit(solution)/shard_map/pallas_call | solution.py:44
  16.7 5.1 %collective-permute-done.3.refs_4_.refs_5_ = bf16[576,128]{1,0:T(8,128)(2,1)S(1)} collective-permute-done((bf16[576,128]{1,0:T(8,128)(2,1)}, bf16[576,128]{1,0:T(8,128)(2,1)S(1)}, u32[]{:S(2)}, u32[]{:S(2)}) %collective-permute-start.3) | collective-permute-done | bytes 147488 | tf_op jit(solution)/shard_map/ppermute | solution.py:546
  21.8 4.4 %shard_map.187 = (bf16[512,128]{1,0:T(8,128)(2,1)S(1)}, bf16[512,128]{1,0:T(8,128)(2,1)S(1)}, bf16[512,128]{1,0:T(8,128)(2,1)S(1)}, bf16[512,128]{1,0:T(8,128)(2,1)S(1)}, bf16[16,128,128]{2,1,0:T(8,128)(2,1)S(1)}) custom-call(s32[1,1]{1,0:T(1,128)S(6)} %copy.20.tile_count, s32[8,128]{1,0:T(8,128)S(1)} %get-tuple-element.42.most, ...), custom_call_target="tpu_custom_call" | custom-call | flops 2147483648 | bytes 4751360 | tf_op jit(solution)/shard_map/pallas_call | solution.py:44
  26.1 0.2 collective-permute-start.5
  26.4 2.5 %collective-permute-start.6 = (bf16[512,128]{1,0:T(8,128)(2,1)S(1)}, bf16[512,128]{1,0:T(8,128)(2,1)S(1)}, u32[]{:S(2)}, u32[]{:S(2)}) collective-permute-start(bf16[512,128]{1,0:T(8,128)(2,1)S(1)} %get-tuple-element.54), channel_id=1, source_target_pairs={{0,28},{4,0},{8,4},{12,8},{16,12},{20,16},{24,20},{28,24},{1,29},{... | collective-permute-start | bytes 393224 | tf_op jit(solution)/shard_map/ppermute | solution.py:22
  28.9 0.0 copy-start.5
  28.9 0.0 copy-start.6
  28.9 3.2 %shard_map.188 = (f32[512,128]{1,0:T(8,128)S(1)}, f32[512,128]{1,0:T(8,128)S(1)}) custom-call(s32[1,1]{1,0:T(1,128)S(6)} %copy.20.tile_count, s32[8,128]{1,0:T(8,128)S(1)} %get-tuple-element.42.most, bf16[17,128,128]{2,1,0:T(8,128)(2,1)S(1)} %get-tuple-element.43.row_rank, bf16[17,128,128]{2,1,0:T(8,128)(2,1)S(1)} %get-tuple-element.44.row_degree, ...), custom_call_target="tpu_custom_call" | custom-call | flops 1073741824 | bytes 4132864 | tf_op jit(solution)/shard_map/pallas_call | solution.py:44
  32.1 0.0 collective-permute-done.5.sum_low
  32.2 1.4 %shard_map.189 = (bf16[512,128]{1,0:T(8,128)(2,1)}, bf16[1024,128]{1,0:T(8,128)(2,1)S(1)}, bf16[1024,128]{1,0:T(8,128)(2,1)S(1)}, bf16[512,128]{1,0:T(8,128)(2,1...) custom-call(f32[8,128]{1,0:T(8,128)S(1)} %get-tuple-element.41.vecto, ...), custom_call_target="tpu_custom_call" | custom-call | flops 117440512 | bytes 2625536 | tf_op jit(solution)/shard_map/pallas_call | solution.py:44
  33.6 2.6 %collective-permute-start.8 = (bf16[1024,128]{1,0:T(8,128)(2,1)S(1)}, bf16[1024,128]{1,0:T(8,128)(2,1)S(1)}, u32[]{:S(2)}, u32[]{:S(2)}) collective-permute-start(bf16[1024,128]{1,0:T(8,128)(2,1)S(1)} %get-tuple-element.60.refs_0_), channel_id=1, source_target_pairs={{0,28},{4,0},{8,4},{12,8},{16,12},{20,16},{24,20},{28,24},{1,29},{... | collective-permute-start | bytes 786440 | tf_op jit(solution)/shard_map/ppermute | solution.py:22
  36.2 0.3 shard_map.192.refs_8_
  36.6 3.9 %shard_map.191.refs_2_ = f32[16,128,128]{2,1,0:T(8,128)S(1)} custom-call(s32[1,1]{1,0:T(1,128)S(6)} %copy.20.tile_count, s32[8,128]{1,0:T(8,128)S(1)} %get-tuple-element.42.most, bf16[17,128,128]{2,1,0:T(8,128)(2,1)S(1)} %get-tuple-element.64.col_rank, bf16[16,128,128]{2,1,0:T(8,128)(2,1)S(1)} %get-tuple-element.51.refs_0_.senders, ...), custom_call_target="tpu_custom_call" | custom-call | flops 1073741824 | bytes 2789376 | tf_op jit(solution)/shard_map/pallas_call | solution.py:44
  40.4 2.6 %collective-permute-done.7.from_low.refs_0_ = bf16[1024,128]{1,0:T(8,128)(2,1)S(1)} collective-permute-done((bf16[1024,128]{1,0:T(8,128)(2,1)S(1)}, bf16[1024,128]{1,0:T(8,128)(2,1)S(1)}, u32[]{:S(2)}, u32[]{:S(2)}) %collective-permute-start.7) | collective-permute-done | bytes 262176 | tf_op jit(solution)/shard_map/ppermute | solution.py:22
  43.1 0.0 collective-permute-done.8.from_high.refs_1_
  43.1 0.4 shard_map.190
  43.4 6.1 %shard_map.193 = (f32[512,128]{1,0:T(8,128)S(1)}, bf16[512,128]{1,0:T(8,128)(2,1)S(1)}, bf16[512,128]{1,0:T(8,128)(2,1)S(1)}, bf16[512,128]{1,0:T(8,128)(2,1)S(1)}, bf16[768,128]{1,0:T(8,128)(2,1)}) custom-call(s32[1,1]{1,0:T(1,128)S(6)} %copy.20.tile_count, s32[8,128]{1,0:T(8,128)S(1)} %get-tuple-element.42.most, ...), custom_call_target="tpu_custom_call" | custom-call | flops 2147483648 | bytes 4657152 | tf_op jit(solution)/shard_map/pallas_call | solution.py:44
  49.5 2.6 %all-to-all-start = ((bf16[32,24,128]{2,1,0:T(8,128)(2,1)}), bf16[32,24,128]{2,1,0:T(8,128)(2,1)S(1)}, u32[]{:S(2)}, u32[]{:S(2)}) async-start(bf16[32,24,128]{2,1,0:T(8,128)(2,1)} %bitcast.4), calls=%async_computation | async-start | bytes 393216 | tf_op jit(solution)/shard_map/all_to_all | solution.py:580
  52.1 1.8 %collective-permute-start.9 = (bf16[512,128]{1,0:T(8,128)(2,1)S(1)}, bf16[512,128]{1,0:T(8,128)(2,1)S(1)}, u32[]{:S(2)}, u32[]{:S(2)}) collective-permute-start(bf16[512,128]{1,0:T(8,128)(2,1)S(1)} %get-tuple-element.72), channel_id=1, source_target_pairs={{0,1},{1,0},{2,3},{3,2},{4,5},{5,4},{6,7},{7,6},{8,9},{9,8},{10,11... | collective-permute-start | bytes 393224 | tf_op jit(solution)/shard_map/ppermute | solution.py:546
  53.9 2.5 %collective-permute-start.10 = (bf16[512,128]{1,0:T(8,128)(2,1)S(1)}, bf16[512,128]{1,0:T(8,128)(2,1)S(1)}, u32[]{:S(2)}, u32[]{:S(2)}) collective-permute-start(bf16[512,128]{1,0:T(8,128)(2,1)S(1)} %get-tuple-element.73), channel_id=1, source_target_pairs={{0,2},{1,3},{2,0},{3,1},{4,6},{5,7},{6,4},{7,5},{8,10},{9,11},{10,... | collective-permute-start | bytes 393224 | tf_op jit(solution)/shard_map/ppermute | solution.py:546
  56.4 0.2 collective-permute-start.11
  56.6 5.0 %all-to-all-done.parts = bf16[32,24,128]{2,1,0:T(8,128)(2,1)S(1)} async-done(((bf16[32,24,128]{2,1,0:T(8,128)(2,1)}), bf16[32,24,128]{2,1,0:T(8,128)(2,1)S(1)}, u32[]{:S(2)}, u32[]{:S(2)}) %all-to-all-start) | async-done | bytes 196640 | tf_op jit(solution)/shard_map/all_to_all | solution.py:580
  61.6 0.7 shard_map.194
  62.3 1.2 %collective-permute-done.9.refs_0_ = bf16[512,128]{1,0:T(8,128)(2,1)S(1)} collective-permute-done((bf16[512,128]{1,0:T(8,128)(2,1)S(1)}, bf16[512,128]{1,0:T(8,128)(2,1)S(1)}, u32[]{:S(2)}, u32[]{:S(2)}) %collective-permute-start.9) | collective-permute-done | bytes 131104 | tf_op jit(solution)/shard_map/ppermute | solution.py:546
  63.5 5.5 %collective-permute-done.10.refs_1_ = bf16[512,128]{1,0:T(8,128)(2,1)S(1)} collective-permute-done((bf16[512,128]{1,0:T(8,128)(2,1)S(1)}, bf16[512,128]{1,0:T(8,128)(2,1)S(1)}, u32[]{:S(2)}, u32[]{:S(2)}) %collective-permute-start.10) | collective-permute-done | bytes 131104 | tf_op jit(solution)/shard_map/ppermute | solution.py:546
  69.0 0.0 collective-permute-done.11.refs_2_
  69.0 5.1 %all-to-all-start.1 = ((bf16[32,24,128]{2,1,0:T(8,128)(2,1)}), bf16[32,24,128]{2,1,0:T(8,128)(2,1)S(1)}, u32[]{:S(2)}, u32[]{:S(2)}) async-start(bf16[32,24,128]{2,1,0:T(8,128)(2,1)} %shard_map.194), calls=%async_computation.1 | async-start | bytes 393216 | tf_op jit(solution)/shard_map/all_to_all | solution.py:583
  74.1 0.9 %shard_map.195 = f32[512,128]{1,0:T(8,128)} custom-call(f32[512,128]{1,0:T(8,128)S(1)} %get-tuple-element.63.direct, bf16[128,128]{1,0:T(8,128)(2,1)S(1)} %copy-done.8, f32[512,128]{1,0:T(8,128)S(1)} %get-tuple-element.70.own, bf16[512,128]{1,0:T(8,128)(2,1)S(1)} %collective-permute-done.9.refs_0_, bf16[512,128]{1,0:T(8,128)(2,1)S(1)} %collective-permute-done.10.refs_1_, ...), custom_call_target="tpu_custom_call" | custom-call | flops 16777216 | bytes 1212416 | tf_op jit(solution)/shard_map/pallas_call | solution.py:44
  75.0 8.4 %all-to-all-done.1.parts = bf16[32,24,128]{2,1,0:T(8,128)(2,1)S(1)} async-done(((bf16[32,24,128]{2,1,0:T(8,128)(2,1)}), bf16[32,24,128]{2,1,0:T(8,128)(2,1)S(1)}, u32[]{:S(2)}, u32[]{:S(2)}) %all-to-all-start.1) | async-done | bytes 196640 | tf_op jit(solution)/shard_map/all_to_all | solution.py:583
  83.5 0.8 shard_map.196
  (25 shorter events, 0.1 us)
Async XLA Ops:
  2.2 11.3 %collective-permute-start.1 = (bf16[576,128]{1,0:T(8,128)(2,1)}, bf16[576,128]{1,0:T(8,128)(2,1)S(1)}, u32[]{:S(2)}, u32[]{:S(2)}) collective-permute-start(bf16[576,128]{1,0:T(8,128)(2,1)} %get-tuple-element.46.message.refs_3_), channel_id=1, source_target_pairs={{0,28},{4,0},{8,4},{12,8},{16,12},{20,16},{24,20},{28,24},{1,29},{... | collective-permute-start | bytes 442376 | tf_op jit(solution)/shard_map/ppermute | solution.py:22
  5.6 8.0 %collective-permute-start = (bf16[576,128]{1,0:T(8,128)(2,1)}, bf16[576,128]{1,0:T(8,128)(2,1)S(1)}, u32[]{:S(2)}, u32[]{:S(2)}) collective-permute-start(bf16[576,128]{1,0:T(8,128)(2,1)} %get-tuple-element.46.message.refs_3_), channel_id=1, source_target_pairs={{0,4},{4,8},{8,12},{12,16},{16,20},{20,24},{24,28},{28,0},{1,5},{5... | collective-permute-start | bytes 442376 | tf_op jit(solution)/shard_map/ppermute | solution.py:22
  5.6 11.1 %collective-permute-start.4 = (bf16[576,128]{1,0:T(8,128)(2,1)}, bf16[576,128]{1,0:T(8,128)(2,1)S(1)}, u32[]{:S(2)}, u32[]{:S(2)}) collective-permute-start(bf16[576,128]{1,0:T(8,128)(2,1)} %get-tuple-element.46.message.refs_3_), channel_id=1, source_target_pairs={{0,3},{1,2},{2,1},{3,0},{4,7},{5,6},{6,5},{7,4},{8,11},{9,10},{10,... | collective-permute-start | bytes 442376 | tf_op jit(solution)/shard_map/ppermute | solution.py:546
  9.2 12.6 %collective-permute-start.3 = (bf16[576,128]{1,0:T(8,128)(2,1)}, bf16[576,128]{1,0:T(8,128)(2,1)S(1)}, u32[]{:S(2)}, u32[]{:S(2)}) collective-permute-start(bf16[576,128]{1,0:T(8,128)(2,1)} %get-tuple-element.46.message.refs_3_), channel_id=1, source_target_pairs={{0,2},{1,3},{2,0},{3,1},{4,6},{5,7},{6,4},{7,5},{8,10},{9,11},{10,... | collective-permute-start | bytes 442376 | tf_op jit(solution)/shard_map/ppermute | solution.py:546
  9.2 12.6 %collective-permute-start.2 = (bf16[576,128]{1,0:T(8,128)(2,1)}, bf16[576,128]{1,0:T(8,128)(2,1)S(1)}, u32[]{:S(2)}, u32[]{:S(2)}) collective-permute-start(bf16[576,128]{1,0:T(8,128)(2,1)} %get-tuple-element.46.message.refs_3_), channel_id=1, source_target_pairs={{0,1},{1,0},{2,3},{3,2},{4,5},{5,4},{6,7},{7,6},{8,9},{9,8},{10,11... | collective-permute-start | bytes 442376 | tf_op jit(solution)/shard_map/ppermute | solution.py:546
  10.6 0.7 copy-start.12
  10.6 0.7 copy-start.13
  10.6 0.7 copy-start.9
  10.7 0.7 copy-start.10
  10.7 0.7 copy-start.11
  11.3 1.2 %copy-start.1 = (s32[1,1,16,128,128]{4,3,2,1,0:T(8,128)S(1)}, s32[1,1,16,128,128]{4,3,2,1,0:T(8,128)}, u32[]{:S(2)}) copy-start(s32[1,1,16,128,128]{4,3,2,1,0:T(8,128)} %param.21) | copy-start | bytes 3145732
  12.6 1.0 %copy-start.7 = (bf16[128,128]{1,0:T(8,128)(2,1)S(1)}, bf16[128,128]{1,0:T(8,128)(2,1)}, u32[]{:S(2)}) copy-start(bf16[128,128]{1,0:T(8,128)(2,1)} %w_recv.3) | copy-start | bytes 98308
  12.6 1.0 %copy-start.8 = (bf16[128,128]{1,0:T(8,128)(2,1)S(1)}, bf16[128,128]{1,0:T(8,128)(2,1)}, u32[]{:S(2)}) copy-start(bf16[128,128]{1,0:T(8,128)(2,1)} %w_send.3) | copy-start | bytes 98308
  12.6 1.0 %copy-start.14 = (bf16[576,128]{1,0:T(8,128)(2,1)S(1)}, bf16[576,128]{1,0:T(8,128)(2,1)}, u32[]{:S(2)}) copy-start(bf16[576,128]{1,0:T(8,128)(2,1)} %get-tuple-element.46.message.refs_3_) | copy-start | bytes 442372
  12.6 1.0 %copy-start.15 = (bf16[16,384]{1,0:T(8,128)(2,1)S(1)}, bf16[16,384]{1,0:T(8,128)(2,1)}, u32[]{:S(2)}) copy-start(bf16[16,384]{1,0:T(8,128)(2,1)} %get-tuple-element.45.weight_parts.refs_2_) | copy-start | bytes 36868
  26.1 6.0 %collective-permute-start.5 = (bf16[512,128]{1,0:T(8,128)(2,1)S(1)}, bf16[512,128]{1,0:T(8,128)(2,1)S(1)}, u32[]{:S(2)}, u32[]{:S(2)}) collective-permute-start(bf16[512,128]{1,0:T(8,128)(2,1)S(1)} %get-tuple-element.53), channel_id=1, source_target_pairs={{0,4},{4,8},{8,12},{12,16},{16,20},{20,24},{24,28},{28,0},{1,5},{5... | collective-permute-start | bytes 393224 | tf_op jit(solution)/shard_map/ppermute | solution.py:22
  26.4 5.8 %collective-permute-start.6 = (bf16[512,128]{1,0:T(8,128)(2,1)S(1)}, bf16[512,128]{1,0:T(8,128)(2,1)S(1)}, u32[]{:S(2)}, u32[]{:S(2)}) collective-permute-start(bf16[512,128]{1,0:T(8,128)(2,1)S(1)} %get-tuple-element.54), channel_id=1, source_target_pairs={{0,28},{4,0},{8,4},{12,8},{16,12},{20,16},{24,20},{28,24},{1,29},{... | collective-permute-start | bytes 393224 | tf_op jit(solution)/shard_map/ppermute | solution.py:22
  28.8 3.3 %copy-start = (bf16[512,128]{1,0:T(8,128)(2,1)S(1)}, bf16[512,128]{1,0:T(8,128)(2,1)}, u32[]{:S(2)}) copy-start(bf16[512,128]{1,0:T(8,128)(2,1)} %latent.7) | copy-start | bytes 393220
  28.8 3.3 %copy-start.2 = (bf16[512,128]{1,0:T(8,128)(2,1)S(1)}, bf16[512,128]{1,0:T(8,128)(2,1)}, u32[]{:S(2)}) copy-start(bf16[512,128]{1,0:T(8,128)(2,1)} %cotangent.3) | copy-start | bytes 393220
  28.8 3.3 %copy-start.3 = (bf16[128,128]{1,0:T(8,128)(2,1)S(1)}, bf16[128,128]{1,0:T(8,128)(2,1)}, u32[]{:S(2)}) copy-start(bf16[128,128]{1,0:T(8,128)(2,1)} %w_edge_out.3) | copy-start | bytes 98308
  28.9 3.3 %copy-start.4 = (bf16[128,128]{1,0:T(8,128)(2,1)S(1)}, bf16[128,128]{1,0:T(8,128)(2,1)}, u32[]{:S(2)}) copy-start(bf16[128,128]{1,0:T(8,128)(2,1)} %w_node_self.3) | copy-start | bytes 98308
  28.9 3.3 %copy-start.5 = (bf16[128,128]{1,0:T(8,128)(2,1)S(1)}, bf16[128,128]{1,0:T(8,128)(2,1)}, u32[]{:S(2)}) copy-start(bf16[128,128]{1,0:T(8,128)(2,1)} %w_node_msg.1) | copy-start | bytes 98308
  28.9 3.3 %copy-start.6 = (bf16[128,128]{1,0:T(8,128)(2,1)S(1)}, bf16[128,128]{1,0:T(8,128)(2,1)}, u32[]{:S(2)}) copy-start(bf16[128,128]{1,0:T(8,128)(2,1)} %w_node_out.1) | copy-start | bytes 98308
  33.6 9.5 %collective-permute-start.7 = (bf16[1024,128]{1,0:T(8,128)(2,1)S(1)}, bf16[1024,128]{1,0:T(8,128)(2,1)S(1)}, u32[]{:S(2)}, u32[]{:S(2)}) collective-permute-start(bf16[1024,128]{1,0:T(8,128)(2,1)S(1)} %get-tuple-element.59), channel_id=1, source_target_pairs={{0,4},{4,8},{8,12},{12,16},{16,20},{20,24},{24,28},{28,0},{1,5},{5... | collective-permute-start | bytes 786440 | tf_op jit(solution)/shard_map/ppermute | solution.py:22
  33.6 9.5 %collective-permute-start.8 = (bf16[1024,128]{1,0:T(8,128)(2,1)S(1)}, bf16[1024,128]{1,0:T(8,128)(2,1)S(1)}, u32[]{:S(2)}, u32[]{:S(2)}) collective-permute-start(bf16[1024,128]{1,0:T(8,128)(2,1)S(1)} %get-tuple-element.60.refs_0_), channel_id=1, source_target_pairs={{0,28},{4,0},{8,4},{12,8},{16,12},{20,16},{24,20},{28,24},{1,29},{... | collective-permute-start | bytes 786440 | tf_op jit(solution)/shard_map/ppermute | solution.py:22
  49.5 12.0 %all-to-all-start = ((bf16[32,24,128]{2,1,0:T(8,128)(2,1)}), bf16[32,24,128]{2,1,0:T(8,128)(2,1)S(1)}, u32[]{:S(2)}, u32[]{:S(2)}) async-start(bf16[32,24,128]{2,1,0:T(8,128)(2,1)} %bitcast.4), calls=%async_computation | async-start | bytes 393216 | tf_op jit(solution)/shard_map/all_to_all | solution.py:580
  52.1 11.3 %collective-permute-start.9 = (bf16[512,128]{1,0:T(8,128)(2,1)S(1)}, bf16[512,128]{1,0:T(8,128)(2,1)S(1)}, u32[]{:S(2)}, u32[]{:S(2)}) collective-permute-start(bf16[512,128]{1,0:T(8,128)(2,1)S(1)} %get-tuple-element.72), channel_id=1, source_target_pairs={{0,1},{1,0},{2,3},{3,2},{4,5},{5,4},{6,7},{7,6},{8,9},{9,8},{10,11... | collective-permute-start | bytes 393224 | tf_op jit(solution)/shard_map/ppermute | solution.py:546
  53.9 15.1 %collective-permute-start.10 = (bf16[512,128]{1,0:T(8,128)(2,1)S(1)}, bf16[512,128]{1,0:T(8,128)(2,1)S(1)}, u32[]{:S(2)}, u32[]{:S(2)}) collective-permute-start(bf16[512,128]{1,0:T(8,128)(2,1)S(1)} %get-tuple-element.73), channel_id=1, source_target_pairs={{0,2},{1,3},{2,0},{3,1},{4,6},{5,7},{6,4},{7,5},{8,10},{9,11},{10,... | collective-permute-start | bytes 393224 | tf_op jit(solution)/shard_map/ppermute | solution.py:546
  56.4 12.6 %collective-permute-start.11 = (bf16[512,128]{1,0:T(8,128)(2,1)S(1)}, bf16[512,128]{1,0:T(8,128)(2,1)S(1)}, u32[]{:S(2)}, u32[]{:S(2)}) collective-permute-start(bf16[512,128]{1,0:T(8,128)(2,1)S(1)} %get-tuple-element.74), channel_id=1, source_target_pairs={{0,3},{1,2},{2,1},{3,0},{4,7},{5,6},{6,5},{7,4},{8,11},{9,10},{10,... | collective-permute-start | bytes 393224 | tf_op jit(solution)/shard_map/ppermute | solution.py:546
  69.0 14.4 %all-to-all-start.1 = ((bf16[32,24,128]{2,1,0:T(8,128)(2,1)}), bf16[32,24,128]{2,1,0:T(8,128)(2,1)S(1)}, u32[]{:S(2)}, u32[]{:S(2)}) async-start(bf16[32,24,128]{2,1,0:T(8,128)(2,1)} %shard_map.194), calls=%async_computation.1 | async-start | bytes 393216 | tf_op jit(solution)/shard_map/all_to_all | solution.py:583

commit v12 on v11

--- a/solution.py
+++ b/solution.py
@@ -429,12 +429,18 @@
     d_message_out[...] = d_message
 
 
-def early_kernel(latent, aggregate, message, hidden, d_update, d_hidden_pre, d_message, grads):
+def early_kernel(
+    latent, aggregate, message, hidden, d_update, d_hidden_pre, d_message, keep, give, grads
+):
     width = latent.shape[1]
-    grads[0:width, :] = contract_rows(aggregate[...], d_message[...]).astype(BF16)
-    grads[width : 2 * width, :] = contract_rows(latent[...], d_hidden_pre[...]).astype(BF16)
-    grads[2 * width : 3 * width, :] = contract_rows(message[...], d_hidden_pre[...]).astype(BF16)
-    grads[3 * width : 4 * width, :] = contract_rows(hidden[...], d_update[...]).astype(BF16)
+    grads[0:width, :] = contract_rows(aggregate[...], d_message[...])
+    grads[width : 2 * width, :] = contract_rows(latent[...], d_hidden_pre[...])
+    grads[2 * width : 3 * width, :] = contract_rows(message[...], d_hidden_pre[...])
+    grads[3 * width : 4 * width, :] = contract_rows(hidden[...], d_update[...])
+    half = keep.shape[0]
+    bit = lax.axis_index("grp") & 1
+    keep[...] = grads[pl.ds(pl.multiple_of(bit * half, half), half), :]
+    give[...] = grads[pl.ds(pl.multiple_of((1 - bit) * half, half), half), :].astype(BF16)
 
 
 def recv_kernel(
@@ -471,8 +477,7 @@
         else:
             grad_parts, started, refs = (refs[0], None, refs[1]), refs[2], refs[3:]
             messages, refs = refs[:members], refs[members:]
-            recv_grad, early, refs = refs[0], refs[1], refs[2:]
-            grads_out, weights_out, refs = refs[:members], refs[members], refs[members + 1 :]
+            grads_out, late_out, refs = refs[:members], refs[members], refs[members + 1 :]
             d_sums, grads = refs[0], refs[-1]
         totals, table, order, sem = refs[1:5]
         copy = pltpu.make_async_copy(most, table, sem)
@@ -534,9 +539,7 @@
                 found = grads[distance * blocks + block]
                 out[span, :] = found.astype(out.dtype)
                 late = late + contract_rows(message[span, :], found.astype(BF16))
-        weights_out[0:width, :] = late.astype(BF16)
-        weights_out[width : 2 * width, :] = recv_grad[...]
-        weights_out[2 * width :, :] = early[...]
+        late_out[...] = late.astype(BF16)
 
     return kernel
 
@@ -554,35 +557,58 @@
     latent_grad[...] = direct[...] + dot_t(d_send.astype(BF16), w_send[...])
 
 
-def sum_kernel(parts, copies):
-    total = parts[0].astype(F32)
-    for place in range(1, parts.shape[0]):
-        total = total + parts[place].astype(F32)
-    total = total.astype(BF16)
-    for place in range(copies.shape[0]):
-        copies[place] = total
-
-
-def last_kernel(parts, weight_grads):
-    rows = parts.shape[1]
-    for place in range(parts.shape[0]):
-        weight_grads[place * rows : (place + 1) * rows, :] = parts[place].astype(F32)
-
-
-def sum_everywhere(value, tied):
-    axes = ("blk", "grp")
-    devices = lax.axis_size("blk") * lax.axis_size("grp")
+def bit_set(axis, step):
+    return (lax.axis_index(axis) & step) != 0
+
+
+def gather_shares(share, summed, tied):
+    step = lax.axis_size("grp") // 2
+    rows = share.shape[0]
+    while step:
+        if step == 1:
+            share, summed, tied = lax.optimization_barrier((share, summed, tied))
+        other = exchanged(jnp.concatenate([share, summed], 0), "grp", step)
+        others = other[:rows]
+        high = bit_set("grp", step)
+        share = jnp.concatenate([jnp.where(high, others, share), jnp.where(high, share, others)], 0)
+        summed = (summed.astype(F32) + other[rows:].astype(F32)).astype(BF16)
+        rows *= 2
+        step //= 2
+    return share, summed, tied
+
+
+def make_last(members):
+    def kernel(mine, other, weight_grads):
+        bit = lax.axis_index("blk") & 1
+        for part, place in ((mine, bit), (other, 1 - bit)):
+            early = 2 * weight_grads.shape[0] // 6
+            half = (weight_grads.shape[0] - early) // (2 * members)
+            quarter = early // 4
+            for item in range(members):
+                start = pl.multiple_of(early + (2 * item + place) * half, half)
+                span = slice(item * half, (item + 1) * half)
+                weight_grads[pl.ds(start, half), :] = part[span, :].astype(F32)
+            for item in range(2):
+                start = pl.multiple_of((2 * item + place) * quarter, quarter)
+                first = members * half + item * quarter
+                weight_grads[pl.ds(start, quarter), :] = part[
+                    first : first + quarter, :
+                ].astype(F32)
+
+    return kernel
+
+
+def halves(value, pieces):
     rows, width = value.shape
-    share = rows // devices
-    if share * devices != rows or share % 8:
-        return lax.psum(value.astype(F32), axes), tied
-    shares = value.reshape(devices, share, width)
-    shares = lax.all_to_all(shares, axes, split_axis=0, concat_axis=0, tiled=True)
-    (copies,) = call(sum_kernel, [like(shares.shape, BF16)], [shares], flops=value.size)
-    copies, tied = lax.optimization_barrier((copies, tied))
-    shares = lax.all_to_all(copies, axes, split_axis=0, concat_axis=0, tiled=True)
-    (total,) = call(last_kernel, [like((rows, width), F32)], [shares], flops=value.size)
-    return total, tied
+    parts = []
+    start = 0
+    for piece in pieces:
+        parts.append((value[start : start + piece // 2], value[start + piece // 2 : start + piece]))
+        start += piece
+    high = bit_set("blk", 1)
+    lows = jnp.concatenate([part[0] for part in parts], 0)
+    highs = jnp.concatenate([part[1] for part in parts], 0)
+    return jnp.where(high, highs, lows), jnp.where(high, lows, highs)
 
 
 def body(
@@ -714,12 +740,26 @@
         flops=14 * own_rows * width * width,
     )
     from_low, from_high = shifted(to_high, "blk", 1), shifted(to_low, "blk", -1)
-    (early,) = call(
+    half = 4 * width // 2
+    share, given = call(
         early_kernel,
-        [like((4 * width, width), BF16)],
+        [like((half, width), F32), like((half, width), BF16)],
         [latent, aggregate, message_out, hidden, d_update, d_hidden_pre, d_message],
+        scratch=[pltpu.VMEM((2 * half, width), F32)],
         flops=8 * own_rows * width * width,
     )
+    share = share + exchanged(given, "grp", 1).astype(F32)
+    arrived = jnp.zeros_like(share)
+    step = 2
+    while step < members:
+        half = share.shape[0] // 2
+        high = bit_set("grp", step)
+        given = jnp.where(high, share[:half], share[half:]).astype(BF16)
+        share = jnp.where(high, share[half:], share[:half])
+        arrived = exchanged(given, "grp", step)
+        step *= 2
+        if step < members:
+            share = share + arrived.astype(F32)
     back_scratch = [
         pltpu.VMEM((3 * blocks, size, width), BF16),
         pltpu.VMEM((2, size, width), F32),
@@ -751,23 +791,47 @@
         ],
         flops=8 * own_rows * width * width,
     )
-    *send_grads, weights = call(
+    *send_grads, late = call(
         make_backward(members, blocks, False),
-        [node_float] + [node_like] * (members - 1) + [like((6 * width, width), BF16)],
-        [col_rank, senders, receivers, from_low, from_high, started, *messages, recv_grad, early],
+        [node_float] + [node_like] * (members - 1) + [like((width, width), BF16)],
+        [col_rank, senders, receivers, from_low, from_high, started, *messages],
         scalars=[tile_count],
         far=[most],
         scratch=back_scratch + [pltpu.VMEM((members * blocks, size, width), F32)],
         flops=tile_flops,
     )
     back = [exchanged(send_grads[distance], "grp", distance) for distance in range(1, members)]
-    weight_grads, back = sum_everywhere(weights, back)
     (latent_grad,) = call(
         return_kernel,
         [node_float],
         [direct, w_send, send_grads[0], *back],
         flops=2 * own_rows * width * width,
     )
+    share = share + lax.optimization_barrier((arrived, late))[0].astype(F32)
+    share = share.astype(BF16)
+    chain = jnp.concatenate([share, late, recv_grad], 0)
+    rows = share.shape[0]
+    slabs = lax.axis_size("blk")
+    paired = slabs & (slabs - 1) == 0 and slabs > 1
+    if paired:
+        chain, given = halves(chain, (rows, width, width))
+        chain = (chain.astype(F32) + exchanged(given, "blk", 1).astype(F32)).astype(BF16)
+        rows //= 2
+        step = 2
+        while step < slabs:
+            chain = (chain.astype(F32) + exchanged(chain, "blk", step).astype(F32)).astype(BF16)
+            step *= 2
+    else:
+        chain = lax.psum(chain.astype(F32), "blk").astype(BF16)
+    share, summed, latent_grad = gather_shares(chain[:rows], chain[rows:], latent_grad)
+    chain = jnp.concatenate([share, summed], 0)
+    if paired:
+        (weight_grads,) = call(
+            make_last(members), [like((6 * width, width), F32)], [chain, exchanged(chain, "blk", 1)]
+        )
+    else:
+        gathered = members * rows
+        weight_grads = jnp.concatenate([chain[gathered:], chain[:gathered]], 0).astype(F32)
     return (new_latent, latent_grad, weight_grads.reshape(6, width, width))
 
 

time: 85.6 us -> 83.3 us (0.973); the launches traced: 84.2 us -> 83 us
  waiting for transfers between devices: 27.8 us -> 23.7 us
  local copies, waits for them, and re-layouts: 1.95 us -> 6.05 us
    all_to_all x2 -> x0, waiting for transfers between devices: 13.4 us -> none  [the longest x1 8.43 us: sum_everywhere(): lax.all_to_all(copies, axes, split_axis=0, concat_axis=0, tiled=True)]
    ppermute x6 -> x14, waiting for transfers between devices: 11.8 us -> 23.7 us  [exchanged(): lax.ppermute(value, axis, [(source, source ^ step) for source in range(co...]
    ppermute x6 -> x14, starting transfers between devices: 8.84 us -> 17.9 us  [exchanged(): lax.ppermute(value, axis, [(source, source ^ step) for source in range(co...]
    all_to_all x2 -> x0, starting transfers between devices: 7.71 us -> none  [the longest x1 5.11 us: sum_everywhere(): lax.all_to_all(copies, axes, split_axis=0, concat_axis=0, tiled=True)]
    unnamed x32 -> x46, local copies, waits for them, and re-layouts: 1.95 us -> 6.04 us
    ppermute x6, waiting for transfers between devices: 2.63 us -> 0.02 us  [shifted(): return lax.ppermute(value, axis, pairs)]
    ppermute x6, starting transfers between devices: 8.68 us -> 6.49 us  [shifted(): return lax.ppermute(value, axis, pairs)]
    pallas_call x13 -> x12, Pallas kernels: 27.7 us -> 27 us  [call(): pl.pallas_call(kernel, out_shape=[jax.ShapeDtypeStruct(o.shape, o.dtype)...]
  transfers between devices with their start and end apart: 14 -> 20, of which waited for: 6 -> 8; matrix products, arithmetic and copies ran while one was open for 0% -> 0% of each run, Pallas kernels for 16% -> 22%
where the time goes in v12:
time: 83.3 us; the launch traced here: 83 us
  Pallas kernels  27 us (32%)
  starting transfers between devices  24.4 us (29%)
  waiting for transfers between devices  23.7 us (28%)
  local copies, waits for them, and re-layouts  6.05 us (7%)
  between operations  1.69 us (2%)
    pallas_call x12, Pallas kernels, call(): pl.pallas_call(kernel, out_shape=[jax.ShapeDtypeStruct(o.shape, o.dtype)...  27 us
    ppermute x14, waiting for transfers between devices, exchanged(): lax.ppermute(value, axis, [(source, source ^ step) for source in range(co...  23.7 us
    ppermute x14, starting transfers between devices, exchanged(): lax.ppermute(value, axis, [(source, source ^ step) for source in range(co...  17.9 us
    ppermute x6, starting transfers between devices, shifted(): return lax.ppermute(value, axis, pairs)  6.49 us
    unnamed x46, local copies, waits for them, and re-layouts  6.04 us
  transfers between devices with their start and end apart: 20, of which 8 were waited for; matrix products, arithmetic and copies ran while one was open for 0% of the time, Pallas kernels for 22%

profile of v12, /device:TPU:0, one launch (start us, length us, event | category | flops | bytes accessed | tf_op | source)
XLA Modules:
  0.0 83.0 jit_solution(5110421944852204762)
XLA Ops:
  0.6 1.6 %shard_map.185 = (bf16[576,128]{1,0:T(8,128)(2,1)}, bf16[16,384]{1,0:T(8,128)(2,1)}) custom-call(bf16[512,128]{1,0:T(8,128)(2,1)} %latent.7, f32[3,512]{1,0:T(4,128)} %positions.1, f32[3,128]{1,0:T(4,128)} %pos_weight.1), custom_call_target="tpu_custom_call" | custom-call | bytes 298496 | tf_op jit(solution)/shard_map/pallas_call | solution.py:44
  2.2 0.5 collective-permute-start
  2.7 2.9 %collective-permute-start.1 = (bf16[576,128]{1,0:T(8,128)(2,1)}, bf16[576,128]{1,0:T(8,128)(2,1)S(1)}, u32[]{:S(2)}, u32[]{:S(2)}) collective-permute-start(bf16[576,128]{1,0:T(8,128)(2,1)} %get-tuple-element.48.message.refs_3_), channel_id=1, source_target_pairs={{0,28},{4,0},{8,4},{12,8},{16,12},{20,16},{24,20},{28,24},{1,29},{... | collective-permute-start | bytes 442376 | tf_op jit(solution)/shard_map/ppermute | solution.py:22
  5.6 2.3 %collective-permute-start.2 = (bf16[576,128]{1,0:T(8,128)(2,1)}, bf16[576,128]{1,0:T(8,128)(2,1)S(1)}, u32[]{:S(2)}, u32[]{:S(2)}) collective-permute-start(bf16[576,128]{1,0:T(8,128)(2,1)} %get-tuple-element.48.message.refs_3_), channel_id=1, source_target_pairs={{0,1},{1,0},{2,3},{3,2},{4,5},{5,4},{6,7},{7,6},{8,9},{9,8},{10,11... | collective-permute-start | bytes 442376 | tf_op jit(solution)/shard_map/ppermute | solution.py:549
  7.9 2.6 %collective-permute-start.3 = (bf16[576,128]{1,0:T(8,128)(2,1)}, bf16[576,128]{1,0:T(8,128)(2,1)S(1)}, u32[]{:S(2)}, u32[]{:S(2)}) collective-permute-start(bf16[576,128]{1,0:T(8,128)(2,1)} %get-tuple-element.48.message.refs_3_), channel_id=1, source_target_pairs={{0,2},{1,3},{2,0},{3,1},{4,6},{5,7},{6,4},{7,5},{8,10},{9,11},{10,... | collective-permute-start | bytes 442376 | tf_op jit(solution)/shard_map/ppermute | solution.py:549
  11.2 0.0 copy-start.13
  11.2 0.6 copy-done.12
  11.8 0.0 copy-done.13
  11.8 0.0 copy-done.9
  11.8 0.0 copy-done.10
  11.9 0.0 copy-done.11
  11.9 1.2 %copy-done.1 = s32[1,1,16,128,128]{4,3,2,1,0:T(8,128)S(1)} copy-done((s32[1,1,16,128,128]{4,3,2,1,0:T(8,128)S(1)}, s32[1,1,16,128,128]{4,3,2,1,0:T(8,128)}, u32[]{:S(2)}) %copy-start.1) | copy-done | bytes 1048600
  13.1 1.0 %shard_map.184 = (bf16[17,128,128]{2,1,0:T(8,128)(2,1)S(1)}, bf16[17,128,128]{2,1,0:T(8,128)(2,1)S(1)}, bf16[17,128,128]{2,1,0:T(8,128)(2,1)S(1)}, s32[8,128]{1,0:T(8,128)S(1)}, f32[8,128]{1,0:T(8,128)S(1)}) custom-call(s32[1,1]{1,0:T(1,128)S(6)} %copy.20.tile_count, s32[16,128,128]{2,1,0:T(8,128)S(1)} %bitcast.5, s32[1,1,16]{2,1,0:T(1,128)S(1)} %copy-done.9, ...), custom_call_target="tpu_custom_call" | custom-call | flops 268435456 | bytes 2729600 | tf_op jit(solution)/shard_map/pallas_call | solution.py:44
  14.1 3.0 %shard_map.186 = (bf16[4,128,128]{2,1,0:T(8,128)(2,1)S(1)}, bf16[12,128,128]{2,1,0:T(8,128)(2,1)S(1)}, f32[12,128,128]{2,1,0:T(8,128)S(1)}, f32[12,128,128]{2,1,0:T(8,128)S(1)}) custom-call(s32[1,1]{1,0:T(1,128)S(6)} %copy.20.tile_count, s32[8,128]{1,0:T(8,128)S(1)} %get-tuple-element.44.most, bf16[17,128,128]{2,1,0:T(8,128)(2,1)S(1)} %get-tuple-element.45.row_rank, ...), custom_call_target="tpu_custom_call" | custom-call | flops 1073741824 | bytes 3739648 | tf_op jit(solution)/shard_map/pallas_call | solution.py:44
  17.2 4.2 %collective-permute-done.3.refs_4_.refs_5_ = bf16[576,128]{1,0:T(8,128)(2,1)S(1)} collective-permute-done((bf16[576,128]{1,0:T(8,128)(2,1)}, bf16[576,128]{1,0:T(8,128)(2,1)S(1)}, u32[]{:S(2)}, u32[]{:S(2)}) %collective-permute-start.3) | collective-permute-done | bytes 147488 | tf_op jit(solution)/shard_map/ppermute | solution.py:549
  21.4 4.4 %shard_map.187 = (bf16[512,128]{1,0:T(8,128)(2,1)S(1)}, bf16[512,128]{1,0:T(8,128)(2,1)S(1)}, bf16[512,128]{1,0:T(8,128)(2,1)S(1)}, bf16[512,128]{1,0:T(8,128)(2,1)S(1)}, bf16[16,128,128]{2,1,0:T(8,128)(2,1)S(1)}) custom-call(s32[1,1]{1,0:T(1,128)S(6)} %copy.20.tile_count, s32[8,128]{1,0:T(8,128)S(1)} %get-tuple-element.44.most, ...), custom_call_target="tpu_custom_call" | custom-call | flops 2147483648 | bytes 4751360 | tf_op jit(solution)/shard_map/pallas_call | solution.py:44
  25.8 0.8 copy-done.20
  26.6 2.6 %collective-permute-start.6 = (bf16[512,128]{1,0:T(8,128)(2,1)S(1)}, bf16[512,128]{1,0:T(8,128)(2,1)S(1)}, u32[]{:S(2)}, u32[]{:S(2)}) collective-permute-start(bf16[512,128]{1,0:T(8,128)(2,1)S(1)} %get-tuple-element.56), channel_id=1, source_target_pairs={{0,28},{4,0},{8,4},{12,8},{16,12},{20,16},{24,20},{28,24},{1,29},{... | collective-permute-start | bytes 393224 | tf_op jit(solution)/shard_map/ppermute | solution.py:22
  29.3 1.1 %copy-done.17 = f32[12,128,128]{2,1,0:T(8,128)S(1)} copy-done((f32[12,128,128]{2,1,0:T(8,128)S(1)}, f32[12,128,128]{2,1,0:T(8,128)}, u32[]{:S(2)}) %copy-start.17) | copy-done | bytes 786456
  30.4 1.1 %copy-done.19 = f32[12,128,128]{2,1,0:T(8,128)S(1)} copy-done((f32[12,128,128]{2,1,0:T(8,128)S(1)}, f32[12,128,128]{2,1,0:T(8,128)}, u32[]{:S(2)}) %copy-start.19) | copy-done | bytes 786456
  31.5 1.0 %copy-done.21 = bf16[16,128,128]{2,1,0:T(8,128)(2,1)S(1)} copy-done((bf16[16,128,128]{2,1,0:T(8,128)(2,1)S(1)}, bf16[16,128,128]{2,1,0:T(8,128)(2,1)}, u32[]{:S(2)}) %copy-start.21) | copy-done | bytes 524312
  32.6 3.5 %shard_map.188 = (f32[512,128]{1,0:T(8,128)S(1)}, f32[512,128]{1,0:T(8,128)S(1)}) custom-call(s32[1,1]{1,0:T(1,128)S(6)} %copy.20.tile_count, s32[8,128]{1,0:T(8,128)S(1)} %get-tuple-element.44.most, bf16[17,128,128]{2,1,0:T(8,128)(2,1)S(1)} %get-tuple-element.45.row_rank, bf16[17,128,128]{2,1,0:T(8,128)(2,1)S(1)} %get-tuple-element.46.row_degree, ...), custom_call_target="tpu_custom_call" | custom-call | flops 1073741824 | bytes 4132864 | tf_op jit(solution)/shard_map/pallas_call | solution.py:44
  36.2 1.4 %shard_map.189 = (bf16[512,128]{1,0:T(8,128)(2,1)}, bf16[1024,128]{1,0:T(8,128)(2,1)S(1)}, bf16[1024,128]{1,0:T(8,128)(2,1)S(1)}, bf16[512,128]{1,0:T(8,128)(2,1...) custom-call(f32[8,128]{1,0:T(8,128)S(1)} %get-tuple-element.43.vecto, ...), custom_call_target="tpu_custom_call" | custom-call | flops 117440512 | bytes 2625536 | tf_op jit(solution)/shard_map/pallas_call | solution.py:44
  37.6 0.5 collective-permute-start.9
  38.1 0.4 shard_map.190
  38.5 0.7 collective-permute-start.7
  39.2 3.2 %shard_map.191.refs_2_ = f32[16,128,128]{2,1,0:T(8,128)S(1)} custom-call(s32[1,1]{1,0:T(1,128)S(6)} %copy.20.tile_count, s32[8,128]{1,0:T(8,128)S(1)} %get-tuple-element.44.most, bf16[17,128,128]{2,1,0:T(8,128)(2,1)S(1)} %get-tuple-element.68.col_rank, bf16[16,128,128]{2,1,0:T(8,128)(2,1)S(1)} %copy-done.21, ...), custom_call_target="tpu_custom_call" | custom-call | flops 1073741824 | bytes 2789376 | tf_op jit(solution)/shard_map/pallas_call | solution.py:44
  42.4 0.7 collective-permute-done.7
  43.2 2.2 %collective-permute-start.8 = (bf16[128,128]{1,0:T(8,128)(2,1)S(1)}, bf16[128,128]{1,0:T(8,128)(2,1)S(1)}, u32[]{:S(2)}, u32[]{:S(2)}) collective-permute-start(bf16[128,128]{1,0:T(8,128)(2,1)S(1)} %select_convert_fusion), channel_id=1, source_target_pairs={{0,2},{1,3},{2,0},{3,1},{4,6},{5,7},{6,4},{7,5},{8,10},{9,11},{10,... | collective-permute-start | bytes 98312 | tf_op jit(solution)/shard_map/ppermute | solution.py:549
  45.4 6.4 %shard_map.192 = (f32[512,128]{1,0:T(8,128)S(1)}, bf16[512,128]{1,0:T(8,128)(2,1)S(1)}, bf16[512,128]{1,0:T(8,128)(2,1)S(1)}, bf16[512,128]{1,0:T(8,128)(2,1)S(1)}, bf16[128,128]{1,0:T(8,128)(2,1)S(1)}) custom-call(s32[1,1]{1,0:T(1,128)S(6)} %copy.20.tile_count, s32[8,128]{1,0:T(8,128)S(1)} %get-tuple-element.44.most, ...), custom_call_target="tpu_custom_call" | custom-call | flops 2147483648 | bytes 4329472 | tf_op jit(solution)/shard_map/pallas_call | solution.py:44
  51.8 0.4 shard_map.193
  52.3 0.1 collective-permute-start.11
  52.3 1.2 %collective-permute-done.11 = bf16[192,128]{1,0:T(8,128)(2,1)S(1)} collective-permute-done((bf16[192,128]{1,0:T(8,128)(2,1)S(1)}, bf16[192,128]{1,0:T(8,128)(2,1)S(1)}, u32[]{:S(2)}, u32[]{:S(2)}) %collective-permute-start.11) | collective-permute-done | bytes 49184 | tf_op jit(solution)/shard_map/ppermute | solution.py:549
  53.6 0.3 collective-permute-start.12
  53.9 3.9 %collective-permute-done.12 = bf16[192,128]{1,0:T(8,128)(2,1)S(1)} collective-permute-done((bf16[192,128]{1,0:T(8,128)(2,1)S(1)}, bf16[192,128]{1,0:T(8,128)(2,1)S(1)}, u32[]{:S(2)}, u32[]{:S(2)}) %collective-permute-start.12) | collective-permute-done | bytes 49184 | tf_op jit(solution)/shard_map/ppermute | solution.py:549
  57.8 0.1 collective-permute-start.13
  57.8 0.4 collective-permute-start.15
  58.2 4.7 %collective-permute-start.16 = (bf16[512,128]{1,0:T(8,128)(2,1)S(1)}, bf16[512,128]{1,0:T(8,128)(2,1)S(1)}, u32[]{:S(2)}, u32[]{:S(2)}) collective-permute-start(bf16[512,128]{1,0:T(8,128)(2,1)S(1)} %get-tuple-element.78), channel_id=1, source_target_pairs={{0,2},{1,3},{2,0},{3,1},{4,6},{5,7},{6,4},{7,5},{8,10},{9,11},{10,... | collective-permute-start | bytes 393224 | tf_op jit(solution)/shard_map/ppermute | solution.py:549
  62.9 1.5 %collective-permute-start.17 = (bf16[512,128]{1,0:T(8,128)(2,1)S(1)}, bf16[512,128]{1,0:T(8,128)(2,1)S(1)}, u32[]{:S(2)}, u32[]{:S(2)}) collective-permute-start(bf16[512,128]{1,0:T(8,128)(2,1)S(1)} %get-tuple-element.79), channel_id=1, source_target_pairs={{0,3},{1,2},{2,1},{3,0},{4,7},{5,6},{6,5},{7,4},{8,11},{9,10},{10,... | collective-permute-start | bytes 393224 | tf_op jit(solution)/shard_map/ppermute | solution.py:549
  64.4 2.1 %collective-permute-start.14 = (bf16[192,128]{1,0:T(8,128)(2,1)S(1)}, bf16[192,128]{1,0:T(8,128)(2,1)S(1)}, u32[]{:S(2)}, u32[]{:S(2)}) collective-permute-start(bf16[192,128]{1,0:T(8,128)(2,1)S(1)} %add_convert_fusion), channel_id=1, source_target_pairs={{0,2},{1,3},{2,0},{3,1},{4,6},{5,7},{6,4},{7,5},{8,10},{9,11},{10,... | collective-permute-start | bytes 147464 | tf_op jit(solution)/shard_map/ppermute | solution.py:549
  66.5 6.8 %collective-permute-done.16.refs_1_ = bf16[512,128]{1,0:T(8,128)(2,1)S(1)} collective-permute-done((bf16[512,128]{1,0:T(8,128)(2,1)S(1)}, bf16[512,128]{1,0:T(8,128)(2,1)S(1)}, u32[]{:S(2)}, u32[]{:S(2)}) %collective-permute-start.16) | collective-permute-done | bytes 131104 | tf_op jit(solution)/shard_map/ppermute | solution.py:549
  73.3 0.9 %shard_map.194 = f32[512,128]{1,0:T(8,128)} custom-call(f32[512,128]{1,0:T(8,128)S(1)} %get-tuple-element.75.direct, bf16[128,128]{1,0:T(8,128)(2,1)S(1)} %copy-done.8, f32[512,128]{1,0:T(8,128)S(1)} %get-tuple-element.76.own, bf16[512,128]{1,0:T(8,128)(2,1)S(1)} %collective-permute-done.15.refs_0_, bf16[512,128]{1,0:T(8,128)(2,1)S(1)} %collective-permute-done.16.refs_1_, ...), custom_call_target="tpu_custom_call" | custom-call | flops 16777216 | bytes 1212416 | tf_op jit(solution)/shard_map/pallas_call | solution.py:44
  74.2 2.2 %collective-permute-done.14 = bf16[192,128]{1,0:T(8,128)(2,1)S(1)} collective-permute-done((bf16[192,128]{1,0:T(8,128)(2,1)S(1)}, bf16[192,128]{1,0:T(8,128)(2,1)S(1)}, u32[]{:S(2)}, u32[]{:S(2)}) %collective-permute-start.14) | collective-permute-done | bytes 49184 | tf_op jit(solution)/shard_map/ppermute | solution.py:549
  76.5 1.0 %collective-permute-start.18 = (bf16[256,128]{1,0:T(8,128)(2,1)S(1)}, bf16[256,128]{1,0:T(8,128)(2,1)S(1)}, u32[]{:S(2)}, u32[]{:S(2)}) collective-permute-start(bf16[256,128]{1,0:T(8,128)(2,1)S(1)} %pad_maximum_fusion.1), channel_id=1, source_target_pairs={{0,1},{1,0},{2,3},{3,2},{4,5},{5,4},{6,7},{7,6},{8,9},{9,8},{10,11... | collective-permute-start | bytes 196616 | tf_op jit(solution)/shard_map/ppermute | solution.py:549
  77.5 3.3 %collective-permute-done.18 = bf16[256,128]{1,0:T(8,128)(2,1)S(1)} collective-permute-done((bf16[256,128]{1,0:T(8,128)(2,1)S(1)}, bf16[256,128]{1,0:T(8,128)(2,1)S(1)}, u32[]{:S(2)}, u32[]{:S(2)}) %collective-permute-start.18) | collective-permute-done | bytes 65568 | tf_op jit(solution)/shard_map/ppermute | solution.py:549
  80.8 0.1 collective-permute-start.19
  80.9 1.3 %collective-permute-done.19.other = bf16[384,128]{1,0:T(8,128)(2,1)S(1)} collective-permute-done((bf16[384,128]{1,0:T(8,128)(2,1)S(1)}, bf16[384,128]{1,0:T(8,128)(2,1)S(1)}, u32[]{:S(2)}, u32[]{:S(2)}) %collective-permute-start.19) | collective-permute-done | bytes 98336 | tf_op jit(solution)/shard_map/ppermute | solution.py:549
  82.2 0.8 shard_map.195
  (66 shorter events, 0.3 us)
Async XLA Ops:
  2.2 11.9 %collective-permute-start = (bf16[576,128]{1,0:T(8,128)(2,1)}, bf16[576,128]{1,0:T(8,128)(2,1)S(1)}, u32[]{:S(2)}, u32[]{:S(2)}) collective-permute-start(bf16[576,128]{1,0:T(8,128)(2,1)} %get-tuple-element.48.message.refs_3_), channel_id=1, source_target_pairs={{0,4},{4,8},{8,12},{12,16},{16,20},{20,24},{24,28},{28,0},{1,5},{5... | collective-permute-start | bytes 442376 | tf_op jit(solution)/shard_map/ppermute | solution.py:22
  2.7 11.4 %collective-permute-start.1 = (bf16[576,128]{1,0:T(8,128)(2,1)}, bf16[576,128]{1,0:T(8,128)(2,1)S(1)}, u32[]{:S(2)}, u32[]{:S(2)}) collective-permute-start(bf16[576,128]{1,0:T(8,128)(2,1)} %get-tuple-element.48.message.refs_3_), channel_id=1, source_target_pairs={{0,28},{4,0},{8,4},{12,8},{16,12},{20,16},{24,20},{28,24},{1,29},{... | collective-permute-start | bytes 442376 | tf_op jit(solution)/shard_map/ppermute | solution.py:22
  5.6 11.6 %collective-permute-start.2 = (bf16[576,128]{1,0:T(8,128)(2,1)}, bf16[576,128]{1,0:T(8,128)(2,1)S(1)}, u32[]{:S(2)}, u32[]{:S(2)}) collective-permute-start(bf16[576,128]{1,0:T(8,128)(2,1)} %get-tuple-element.48.message.refs_3_), channel_id=1, source_target_pairs={{0,1},{1,0},{2,3},{3,2},{4,5},{5,4},{6,7},{7,6},{8,9},{9,8},{10,11... | collective-permute-start | bytes 442376 | tf_op jit(solution)/shard_map/ppermute | solution.py:549
  7.9 13.5 %collective-permute-start.3 = (bf16[576,128]{1,0:T(8,128)(2,1)}, bf16[576,128]{1,0:T(8,128)(2,1)S(1)}, u32[]{:S(2)}, u32[]{:S(2)}) collective-permute-start(bf16[576,128]{1,0:T(8,128)(2,1)} %get-tuple-element.48.message.refs_3_), channel_id=1, source_target_pairs={{0,2},{1,3},{2,0},{3,1},{4,6},{5,7},{6,4},{7,5},{8,10},{9,11},{10,... | collective-permute-start | bytes 442376 | tf_op jit(solution)/shard_map/ppermute | solution.py:549
  10.5 10.9 %collective-permute-start.4 = (bf16[576,128]{1,0:T(8,128)(2,1)}, bf16[576,128]{1,0:T(8,128)(2,1)S(1)}, u32[]{:S(2)}, u32[]{:S(2)}) collective-permute-start(bf16[576,128]{1,0:T(8,128)(2,1)} %get-tuple-element.48.message.refs_3_), channel_id=1, source_target_pairs={{0,3},{1,2},{2,1},{3,0},{4,7},{5,6},{6,5},{7,4},{8,11},{9,10},{10,... | collective-permute-start | bytes 442376 | tf_op jit(solution)/shard_map/ppermute | solution.py:549
  11.2 0.7 copy-start.12
  11.2 0.7 copy-start.13
  11.2 0.7 copy-start.9
  11.2 0.7 copy-start.10
  11.2 0.7 copy-start.11
  11.9 1.2 %copy-start.1 = (s32[1,1,16,128,128]{4,3,2,1,0:T(8,128)S(1)}, s32[1,1,16,128,128]{4,3,2,1,0:T(8,128)}, u32[]{:S(2)}) copy-start(s32[1,1,16,128,128]{4,3,2,1,0:T(8,128)} %param.21) | copy-start | bytes 3145732
  13.1 1.0 %copy-start.7 = (bf16[128,128]{1,0:T(8,128)(2,1)S(1)}, bf16[128,128]{1,0:T(8,128)(2,1)}, u32[]{:S(2)}) copy-start(bf16[128,128]{1,0:T(8,128)(2,1)} %w_recv.3) | copy-start | bytes 98308
  13.1 1.0 %copy-start.8 = (bf16[128,128]{1,0:T(8,128)(2,1)S(1)}, bf16[128,128]{1,0:T(8,128)(2,1)}, u32[]{:S(2)}) copy-start(bf16[128,128]{1,0:T(8,128)(2,1)} %w_send.3) | copy-start | bytes 98308
  13.1 1.0 %copy-start.14 = (bf16[576,128]{1,0:T(8,128)(2,1)S(1)}, bf16[576,128]{1,0:T(8,128)(2,1)}, u32[]{:S(2)}) copy-start(bf16[576,128]{1,0:T(8,128)(2,1)} %get-tuple-element.48.message.refs_3_) | copy-start | bytes 442372
  13.1 1.0 %copy-start.15 = (bf16[16,384]{1,0:T(8,128)(2,1)S(1)}, bf16[16,384]{1,0:T(8,128)(2,1)}, u32[]{:S(2)}) copy-start(bf16[16,384]{1,0:T(8,128)(2,1)} %get-tuple-element.47.weight_parts.refs_2_) | copy-start | bytes 36868
  17.2 8.6 %copy-start.16 = (f32[12,128,128]{2,1,0:T(8,128)}, f32[12,128,128]{2,1,0:T(8,128)S(1)}, u32[]{:S(2)}) copy-start(f32[12,128,128]{2,1,0:T(8,128)S(1)} %get-tuple-element.50.sums_in) | copy-start | bytes 2359300
  17.2 8.6 %copy-start.18 = (f32[12,128,128]{2,1,0:T(8,128)}, f32[12,128,128]{2,1,0:T(8,128)S(1)}, u32[]{:S(2)}) copy-start(f32[12,128,128]{2,1,0:T(8,128)S(1)} %get-tuple-element.51.counts_in) | copy-start | bytes 2359300
  25.8 0.8 copy-start.20
  26.6 9.5 %collective-permute-start.5 = (bf16[512,128]{1,0:T(8,128)(2,1)S(1)}, bf16[512,128]{1,0:T(8,128)(2,1)S(1)}, u32[]{:S(2)}, u32[]{:S(2)}) collective-permute-start(bf16[512,128]{1,0:T(8,128)(2,1)S(1)} %get-tuple-element.55), channel_id=1, source_target_pairs={{0,4},{4,8},{8,12},{12,16},{16,20},{20,24},{24,28},{28,0},{1,5},{5... | collective-permute-start | bytes 393224 | tf_op jit(solution)/shard_map/ppermute | solution.py:22
  26.6 9.5 %collective-permute-start.6 = (bf16[512,128]{1,0:T(8,128)(2,1)S(1)}, bf16[512,128]{1,0:T(8,128)(2,1)S(1)}, u32[]{:S(2)}, u32[]{:S(2)}) collective-permute-start(bf16[512,128]{1,0:T(8,128)(2,1)S(1)} %get-tuple-element.56), channel_id=1, source_target_pairs={{0,28},{4,0},{8,4},{12,8},{16,12},{20,16},{24,20},{28,24},{1,29},{... | collective-permute-start | bytes 393224 | tf_op jit(solution)/shard_map/ppermute | solution.py:22
  29.3 1.1 %copy-start.17 = (f32[12,128,128]{2,1,0:T(8,128)S(1)}, f32[12,128,128]{2,1,0:T(8,128)}, u32[]{:S(2)}) copy-start(f32[12,128,128]{2,1,0:T(8,128)} %copy-done.16) | copy-start | bytes 2359300
  30.4 1.1 %copy-start.19 = (f32[12,128,128]{2,1,0:T(8,128)S(1)}, f32[12,128,128]{2,1,0:T(8,128)}, u32[]{:S(2)}) copy-start(f32[12,128,128]{2,1,0:T(8,128)} %copy-done.18) | copy-start | bytes 2359300
  31.5 1.0 %copy-start.21 = (bf16[16,128,128]{2,1,0:T(8,128)(2,1)S(1)}, bf16[16,128,128]{2,1,0:T(8,128)(2,1)}, u32[]{:S(2)}) copy-start(bf16[16,128,128]{2,1,0:T(8,128)(2,1)} %copy-done.20) | copy-start | bytes 1572868
  32.6 3.6 %copy-start = (bf16[512,128]{1,0:T(8,128)(2,1)S(1)}, bf16[512,128]{1,0:T(8,128)(2,1)}, u32[]{:S(2)}) copy-start(bf16[512,128]{1,0:T(8,128)(2,1)} %latent.7) | copy-start | bytes 393220
  32.6 3.6 %copy-start.2 = (bf16[512,128]{1,0:T(8,128)(2,1)S(1)}, bf16[512,128]{1,0:T(8,128)(2,1)}, u32[]{:S(2)}) copy-start(bf16[512,128]{1,0:T(8,128)(2,1)} %cotangent.3) | copy-start | bytes 393220
  32.6 3.6 %copy-start.3 = (bf16[128,128]{1,0:T(8,128)(2,1)S(1)}, bf16[128,128]{1,0:T(8,128)(2,1)}, u32[]{:S(2)}) copy-start(bf16[128,128]{1,0:T(8,128)(2,1)} %w_edge_out.3) | copy-start | bytes 98308
  32.6 3.6 %copy-start.4 = (bf16[128,128]{1,0:T(8,128)(2,1)S(1)}, bf16[128,128]{1,0:T(8,128)(2,1)}, u32[]{:S(2)}) copy-start(bf16[128,128]{1,0:T(8,128)(2,1)} %w_node_self.3) | copy-start | bytes 98308
  32.6 3.6 %copy-start.5 = (bf16[128,128]{1,0:T(8,128)(2,1)S(1)}, bf16[128,128]{1,0:T(8,128)(2,1)}, u32[]{:S(2)}) copy-start(bf16[128,128]{1,0:T(8,128)(2,1)} %w_node_msg.1) | copy-start | bytes 98308
  32.6 3.6 %copy-start.6 = (bf16[128,128]{1,0:T(8,128)(2,1)S(1)}, bf16[128,128]{1,0:T(8,128)(2,1)}, u32[]{:S(2)}) copy-start(bf16[128,128]{1,0:T(8,128)(2,1)} %w_node_out.1) | copy-start | bytes 98308
  37.6 7.8 %collective-permute-start.10 = (bf16[1024,128]{1,0:T(8,128)(2,1)S(1)}, bf16[1024,128]{1,0:T(8,128)(2,1)S(1)}, u32[]{:S(2)}, u32[]{:S(2)}) collective-permute-start(bf16[1024,128]{1,0:T(8,128)(2,1)S(1)} %get-tuple-element.70.refs_0_), channel_id=1, source_target_pairs={{0,28},{4,0},{8,4},{12,8},{16,12},{20,16},{24,20},{28,24},{1,29},{... | collective-permute-start | bytes 786440 | tf_op jit(solution)/shard_map/ppermute | solution.py:22
  37.6 7.8 %collective-permute-start.9 = (bf16[1024,128]{1,0:T(8,128)(2,1)S(1)}, bf16[1024,128]{1,0:T(8,128)(2,1)S(1)}, u32[]{:S(2)}, u32[]{:S(2)}) collective-permute-start(bf16[1024,128]{1,0:T(8,128)(2,1)S(1)} %get-tuple-element.69), channel_id=1, source_target_pairs={{0,4},{4,8},{8,12},{12,16},{16,20},{20,24},{24,28},{28,0},{1,5},{5... | collective-permute-start | bytes 786440 | tf_op jit(solution)/shard_map/ppermute | solution.py:22
  38.5 4.7 %collective-permute-start.7 = (bf16[256,128]{1,0:T(8,128)(2,1)S(1)}, bf16[256,128]{1,0:T(8,128)(2,1)S(1)}, u32[]{:S(2)}, u32[]{:S(2)}) collective-permute-start(bf16[256,128]{1,0:T(8,128)(2,1)S(1)} %get-tuple-element.67), channel_id=1, source_target_pairs={{0,1},{1,0},{2,3},{3,2},{4,5},{5,4},{6,7},{7,6},{8,9},{9,8},{10,11... | collective-permute-start | bytes 196616 | tf_op jit(solution)/shard_map/ppermute | solution.py:549
  39.2 6.2 %copy-start.22 = (bf16[16,128,128]{2,1,0:T(8,128)(2,1)S(1)}, bf16[16,128,128]{2,1,0:T(8,128)(2,1)}, u32[]{:S(2)}) copy-start(bf16[16,128,128]{2,1,0:T(8,128)(2,1)} %copy-done.20) | copy-start | bytes 1572868
  43.2 8.6 %collective-permute-start.8 = (bf16[128,128]{1,0:T(8,128)(2,1)S(1)}, bf16[128,128]{1,0:T(8,128)(2,1)S(1)}, u32[]{:S(2)}, u32[]{:S(2)}) collective-permute-start(bf16[128,128]{1,0:T(8,128)(2,1)S(1)} %select_convert_fusion), channel_id=1, source_target_pairs={{0,2},{1,3},{2,0},{3,1},{4,6},{5,7},{6,4},{7,5},{8,10},{9,11},{10,... | collective-permute-start | bytes 98312 | tf_op jit(solution)/shard_map/ppermute | solution.py:549
  52.3 1.3 %collective-permute-start.11 = (bf16[192,128]{1,0:T(8,128)(2,1)S(1)}, bf16[192,128]{1,0:T(8,128)(2,1)S(1)}, u32[]{:S(2)}, u32[]{:S(2)}) collective-permute-start(bf16[192,128]{1,0:T(8,128)(2,1)S(1)} %broadcast_select_fusion), channel_id=1, source_target_pairs={{0,4},{4,0},{8,12},{12,8},{16,20},{20,16},{24,28},{28,24},{1,5},{5... | collective-permute-start | bytes 147464 | tf_op jit(solution)/shard_map/ppermute | solution.py:549
  53.6 4.2 %collective-permute-start.12 = (bf16[192,128]{1,0:T(8,128)(2,1)S(1)}, bf16[192,128]{1,0:T(8,128)(2,1)S(1)}, u32[]{:S(2)}, u32[]{:S(2)}) collective-permute-start(bf16[192,128]{1,0:T(8,128)(2,1)S(1)} %add_convert_fusion.2), channel_id=1, source_target_pairs={{0,8},{4,12},{8,0},{12,4},{16,24},{20,28},{24,16},{28,20},{1,9},{5... | collective-permute-start | bytes 147464 | tf_op jit(solution)/shard_map/ppermute | solution.py:549
  57.8 6.6 %collective-permute-start.13 = (bf16[192,128]{1,0:T(8,128)(2,1)S(1)}, bf16[192,128]{1,0:T(8,128)(2,1)S(1)}, u32[]{:S(2)}, u32[]{:S(2)}) collective-permute-start(bf16[192,128]{1,0:T(8,128)(2,1)S(1)} %add_convert_fusion.1), channel_id=1, source_target_pairs={{0,16},{4,20},{8,24},{12,28},{16,0},{20,4},{24,8},{28,12},{1,17},{... | collective-permute-start | bytes 147464 | tf_op jit(solution)/shard_map/ppermute | solution.py:549
  57.8 8.7 %collective-permute-start.15 = (bf16[512,128]{1,0:T(8,128)(2,1)S(1)}, bf16[512,128]{1,0:T(8,128)(2,1)S(1)}, u32[]{:S(2)}, u32[]{:S(2)}) collective-permute-start(bf16[512,128]{1,0:T(8,128)(2,1)S(1)} %get-tuple-element.77), channel_id=1, source_target_pairs={{0,1},{1,0},{2,3},{3,2},{4,5},{5,4},{6,7},{7,6},{8,9},{9,8},{10,11... | collective-permute-start | bytes 393224 | tf_op jit(solution)/shard_map/ppermute | solution.py:549
  58.2 15.1 %collective-permute-start.16 = (bf16[512,128]{1,0:T(8,128)(2,1)S(1)}, bf16[512,128]{1,0:T(8,128)(2,1)S(1)}, u32[]{:S(2)}, u32[]{:S(2)}) collective-permute-start(bf16[512,128]{1,0:T(8,128)(2,1)S(1)} %get-tuple-element.78), channel_id=1, source_target_pairs={{0,2},{1,3},{2,0},{3,1},{4,6},{5,7},{6,4},{7,5},{8,10},{9,11},{10,... | collective-permute-start | bytes 393224 | tf_op jit(solution)/shard_map/ppermute | solution.py:549
  62.9 10.4 %collective-permute-start.17 = (bf16[512,128]{1,0:T(8,128)(2,1)S(1)}, bf16[512,128]{1,0:T(8,128)(2,1)S(1)}, u32[]{:S(2)}, u32[]{:S(2)}) collective-permute-start(bf16[512,128]{1,0:T(8,128)(2,1)S(1)} %get-tuple-element.79), channel_id=1, source_target_pairs={{0,3},{1,2},{2,1},{3,0},{4,7},{5,6},{6,5},{7,4},{8,11},{9,10},{10,... | collective-permute-start | bytes 393224 | tf_op jit(solution)/shard_map/ppermute | solution.py:549
  64.4 12.0 %collective-permute-start.14 = (bf16[192,128]{1,0:T(8,128)(2,1)S(1)}, bf16[192,128]{1,0:T(8,128)(2,1)S(1)}, u32[]{:S(2)}, u32[]{:S(2)}) collective-permute-start(bf16[192,128]{1,0:T(8,128)(2,1)S(1)} %add_convert_fusion), channel_id=1, source_target_pairs={{0,2},{1,3},{2,0},{3,1},{4,6},{5,7},{6,4},{7,5},{8,10},{9,11},{10,... | collective-permute-start | bytes 147464 | tf_op jit(solution)/shard_map/ppermute | solution.py:549
  76.5 4.3 %collective-permute-start.18 = (bf16[256,128]{1,0:T(8,128)(2,1)S(1)}, bf16[256,128]{1,0:T(8,128)(2,1)S(1)}, u32[]{:S(2)}, u32[]{:S(2)}) collective-permute-start(bf16[256,128]{1,0:T(8,128)(2,1)S(1)} %pad_maximum_fusion.1), channel_id=1, source_target_pairs={{0,1},{1,0},{2,3},{3,2},{4,5},{5,4},{6,7},{7,6},{8,9},{9,8},{10,11... | collective-permute-start | bytes 196616 | tf_op jit(solution)/shard_map/ppermute | solution.py:549
  80.8 1.4 %collective-permute-start.19 = (bf16[384,128]{1,0:T(8,128)(2,1)S(1)}, bf16[384,128]{1,0:T(8,128)(2,1)S(1)}, u32[]{:S(2)}, u32[]{:S(2)}) collective-permute-start(bf16[384,128]{1,0:T(8,128)(2,1)S(1)} %pad_maximum_fusion.mine), channel_id=1, source_target_pairs={{0,4},{4,0},{8,12},{12,8},{16,20},{20,16},{24,28},{28,24},{1,5},{5... | collective-permute-start | bytes 294920 | tf_op jit(solution)/shard_map/ppermute | solution.py:549

commit v13 on v12

--- a/solution.py
+++ b/solution.py
@@ -288,13 +288,17 @@
         high,
         senders,
         receivers,
-        sums,
-        counts,
+        sums_own,
+        counts_own,
+        sums_near,
+        counts_near,
         total,
         count,
         table,
         order,
         sem,
+        sums,
+        counts,
     ):
         copy = pltpu.make_async_copy(most, table, sem)
         copy.start()
@@ -319,6 +323,10 @@
             counts,
             lambda send, recv: send // blocks == member,
         )
+        for values, own, near in ((sums, sums_own, sums_near), (counts, counts_own, counts_near)):
+            near[0:blocks] = values[0:blocks]
+            own[...] = values[blocks : 2 * blocks]
+            near[blocks:] = values[2 * blocks :]
 
     return kernel
 
@@ -338,10 +346,11 @@
         copy.start()
         blocks = receivers.shape[0] // 3
         size = receivers.shape[1]
-        for side, *unused in sides:
-            span = slice(side * blocks, (side + 1) * blocks)
-            sums[span] = sums_in[span]
-            counts[span] = counts_in[span]
+        for item, (side, *unused) in enumerate(sides):
+            source = slice(item * blocks, (item + 1) * blocks)
+            target = slice(side * blocks, (side + 1) * blocks)
+            sums[target] = sums_in[source]
+            counts[target] = counts_in[source]
         if not own:
             senders[0:blocks] = own_senders[...]
             for distance, message in enumerate(messages):
@@ -561,32 +570,47 @@
     return (lax.axis_index(axis) & step) != 0
 
 
-def gather_shares(share, summed, tied):
-    step = lax.axis_size("grp") // 2
-    rows = share.shape[0]
-    while step:
-        if step == 1:
-            share, summed, tied = lax.optimization_barrier((share, summed, tied))
-        other = exchanged(jnp.concatenate([share, summed], 0), "grp", step)
-        others = other[:rows]
-        high = bit_set("grp", step)
-        share = jnp.concatenate([jnp.where(high, others, share), jnp.where(high, share, others)], 0)
-        summed = (summed.astype(F32) + other[rows:].astype(F32)).astype(BF16)
-        rows *= 2
-        step //= 2
-    return share, summed, tied
+def tree_sum(parts):
+    while len(parts) > 1:
+        parts = [parts[item] + parts[item + 1] for item in range(0, len(parts), 2)]
+    return parts[0]
+
+
+def all_parts(value, axis):
+    return [value] + [exchanged(value, axis, step) for step in range(1, lax.axis_size(axis))]
+
+
+def make_gather(rows):
+    def kernel(*refs):
+        parts, out = refs[:-1], refs[-1]
+        for distance, part in enumerate(parts):
+            out[distance * rows : (distance + 1) * rows, :] = part[0:rows, :]
+        rest = [part[rows:, :].astype(F32) for part in parts]
+        out[len(parts) * rows :, :] = tree_sum(rest).astype(BF16)
+
+    return kernel
+
+
+def reversed_bits(place, count):
+    result, low, high = 0, 1, count // 2
+    while high:
+        result = result + jnp.where((place & low) != 0, high, 0)
+        low, high = low * 2, high // 2
+    return result
 
 
 def make_last(members):
     def kernel(mine, other, weight_grads):
         bit = lax.axis_index("blk") & 1
+        member = lax.axis_index("grp")
         for part, place in ((mine, bit), (other, 1 - bit)):
             early = 2 * weight_grads.shape[0] // 6
             half = (weight_grads.shape[0] - early) // (2 * members)
             quarter = early // 4
-            for item in range(members):
+            for distance in range(members):
+                item = reversed_bits(member ^ distance, members)
                 start = pl.multiple_of(early + (2 * item + place) * half, half)
-                span = slice(item * half, (item + 1) * half)
+                span = slice(distance * half, (distance + 1) * half)
                 weight_grads[pl.ds(start, half), :] = part[span, :].astype(F32)
             for item in range(2):
                 start = pl.multiple_of((2 * item + place) * quarter, quarter)
@@ -672,13 +696,15 @@
     pair_scratch = [pltpu.VMEM((size, 2 * width), F32)] * 2 + tables
     window = pltpu.VMEM((3 * blocks, size, width), F32)
     tile_flops = 64 * tiles * size * size * width
-    own_senders, receivers, sums, counts = call(
+    own_senders, receivers, sums_own, counts_own, sums_near, counts_near = call(
         make_first(members),
-        [like((blocks, size, width), BF16), near_like] + [like(window.shape, F32)] * 2,
+        [like((blocks, size, width), BF16), near_like]
+        + [like((blocks, size, width), F32)] * 2
+        + [like((2 * blocks, size, width), F32)] * 2,
         [row_rank, row_degree, w_send, w_recv, weight_parts, vectors, message, *sides],
         scalars=[tile_count],
         far=[most],
-        scratch=pair_scratch,
+        scratch=pair_scratch + [window] * 2,
         flops=tile_flops // 2,
     )
     sum_low, sum_high, count_low, count_high, senders = call(
@@ -688,8 +714,8 @@
             row_rank,
             row_degree,
             receivers,
-            sums,
-            counts,
+            sums_near,
+            counts_near,
             own_senders,
             w_send,
             weight_parts,
@@ -704,7 +730,7 @@
     sum_own, count_own = call(
         make_forward(members, True),
         [node_float] * 2,
-        [row_rank, row_degree, receivers, sums, counts, senders],
+        [row_rank, row_degree, receivers, sums_own, counts_own, senders],
         scalars=[tile_count],
         far=[most],
         scratch=pair_scratch + [window] * 2,
@@ -772,7 +798,7 @@
         scalars=[tile_count],
         far=[most],
         scratch=back_scratch,
-        flops=tile_flops // 2,
+        flops=tile_flops // 16,
     )
     direct, recv_grad = call(
         recv_kernel,
@@ -823,15 +849,24 @@
             step *= 2
     else:
         chain = lax.psum(chain.astype(F32), "blk").astype(BF16)
-    share, summed, latent_grad = gather_shares(chain[:rows], chain[rows:], latent_grad)
-    chain = jnp.concatenate([share, summed], 0)
+    chain, latent_grad = lax.optimization_barrier((chain, latent_grad))
+    summed_rows = chain.shape[0] - rows
+    (chain,) = call(
+        make_gather(rows),
+        [like((members * rows + summed_rows, width), BF16)],
+        all_parts(chain, "grp"),
+        flops=members * chain.size,
+    )
     if paired:
         (weight_grads,) = call(
             make_last(members), [like((6 * width, width), F32)], [chain, exchanged(chain, "blk", 1)]
         )
     else:
-        gathered = members * rows
-        weight_grads = jnp.concatenate([chain[gathered:], chain[:gathered]], 0).astype(F32)
+        member = lax.axis_index("grp")
+        shares = chain[: members * rows].reshape(members, rows, width)
+        shares = shares[member ^ reversed_bits(jnp.arange(members), members)]
+        shares = shares.reshape(members * rows, width)
+        weight_grads = jnp.concatenate([chain[members * rows :], shares], 0).astype(F32)
     return (new_latent, latent_grad, weight_grads.reshape(6, width, width))
 
 

time: 83.3 us -> 80.1 us (0.962)
  local copies, waits for them, and re-layouts: 6.05 us -> 1.97 us
  starting transfers between devices: 24.4 us -> 28.2 us
  waiting for transfers between devices: 23.7 us -> 20.1 us
    ppermute x14 -> x15, waiting for transfers between devices: 23.7 us -> 19 us  [exchanged(): lax.ppermute(value, axis, [(source, source ^ step) for source in range(co...]
    unnamed x46 -> x36, local copies, waits for them, and re-layouts: 6.04 us -> 1.96 us
    ppermute x6, starting transfers between devices: 6.49 us -> 8.67 us  [shifted(): return lax.ppermute(value, axis, pairs)]
    ppermute x14 -> x15, starting transfers between devices: 17.9 us -> 19.6 us  [exchanged(): lax.ppermute(value, axis, [(source, source ^ step) for source in range(co...]
    ppermute x6, waiting for transfers between devices: 0.02 us -> 1.09 us  [shifted(): return lax.ppermute(value, axis, pairs)]
    add x1, other arithmetic: 0.01 us -> 0.89 us  [body(): share = share + exchanged(given, 'grp', 1).astype(F32)]
    pallas_call x12 -> x13, Pallas kernels: 27 us -> 27.4 us  [call(): pl.pallas_call(kernel, out_shape=[jax.ShapeDtypeStruct(o.shape, o.dtype)...]
  transfers between devices with their start and end apart: 20 -> 21, of which waited for: 8 -> 8; matrix products, arithmetic and copies ran while one was open for 0% -> 1% of each run, Pallas kernels for 22% -> 23%
where the time goes in v13:
time: 80.1 us; the launch traced here: 80.3 us
  starting transfers between devices  28.2 us (35%)
  Pallas kernels  27.4 us (34%)
  waiting for transfers between devices  20.1 us (25%)
  local copies, waits for them, and re-layouts  1.97 us (2%)
  between operations  1.62 us (2%)
  other arithmetic  0.99 us (1%)
    pallas_call x13, Pallas kernels, call(): pl.pallas_call(kernel, out_shape=[jax.ShapeDtypeStruct(o.shape, o.dtype)...  27.4 us
    ppermute x15, starting transfers between devices, exchanged(): lax.ppermute(value, axis, [(source, source ^ step) for source in range(co...  19.6 us
    ppermute x15, waiting for transfers between devices, exchanged(): lax.ppermute(value, axis, [(source, source ^ step) for source in range(co...  19 us
    ppermute x6, starting transfers between devices, shifted(): return lax.ppermute(value, axis, pairs)  8.67 us
    unnamed x36, local copies, waits for them, and re-layouts  1.96 us
  transfers between devices with their start and end apart: 21, of which 8 were waited for; matrix products, arithmetic and copies ran while one was open for 1% of the time, Pallas kernels for 23%

profile of v13, /device:TPU:0, one launch (start us, length us, event | category | flops | bytes accessed | tf_op | source)
XLA Modules:
  0.0 80.3 jit_solution(15991991937573284185)
XLA Ops:
  0.6 1.6 %shard_map.185 = (bf16[576,128]{1,0:T(8,128)(2,1)}, bf16[16,384]{1,0:T(8,128)(2,1)}) custom-call(bf16[512,128]{1,0:T(8,128)(2,1)} %latent.7, f32[3,512]{1,0:T(4,128)} %positions.1, f32[3,128]{1,0:T(4,128)} %pos_weight.1), custom_call_target="tpu_custom_call" | custom-call | bytes 298496 | tf_op jit(solution)/shard_map/pallas_call | solution.py:44
  2.2 0.5 collective-permute-start
  2.7 2.9 %collective-permute-start.1 = (bf16[576,128]{1,0:T(8,128)(2,1)}, bf16[576,128]{1,0:T(8,128)(2,1)S(1)}, u32[]{:S(2)}, u32[]{:S(2)}) collective-permute-start(bf16[576,128]{1,0:T(8,128)(2,1)} %get-tuple-element.49.message.refs_3_), channel_id=1, source_target_pairs={{0,28},{4,0},{8,4},{12,8},{16,12},{20,16},{24,20},{28,24},{1,29},{... | collective-permute-start | bytes 442376 | tf_op jit(solution)/shard_map/ppermute | solution.py:22
  5.6 2.3 %collective-permute-start.2 = (bf16[576,128]{1,0:T(8,128)(2,1)}, bf16[576,128]{1,0:T(8,128)(2,1)S(1)}, u32[]{:S(2)}, u32[]{:S(2)}) collective-permute-start(bf16[576,128]{1,0:T(8,128)(2,1)} %get-tuple-element.49.message.refs_3_), channel_id=1, source_target_pairs={{0,1},{1,0},{2,3},{3,2},{4,5},{5,4},{6,7},{7,6},{8,9},{9,8},{10,11... | collective-permute-start | bytes 442376 | tf_op jit(solution)/shard_map/ppermute | solution.py:558
  7.9 2.6 %collective-permute-start.3 = (bf16[576,128]{1,0:T(8,128)(2,1)}, bf16[576,128]{1,0:T(8,128)(2,1)S(1)}, u32[]{:S(2)}, u32[]{:S(2)}) collective-permute-start(bf16[576,128]{1,0:T(8,128)(2,1)} %get-tuple-element.49.message.refs_3_), channel_id=1, source_target_pairs={{0,2},{1,3},{2,0},{3,1},{4,6},{5,7},{6,4},{7,5},{8,10},{9,11},{10,... | collective-permute-start | bytes 442376 | tf_op jit(solution)/shard_map/ppermute | solution.py:558
  11.2 0.0 copy-start.9
  11.2 0.0 copy-start.10
  11.2 0.6 copy-done.12
  11.8 0.0 copy-done.13
  11.8 0.0 copy-done.9
  11.8 0.0 copy-done.10
  11.9 0.0 copy-done.11
  11.9 1.2 %copy-done.1 = s32[1,1,16,128,128]{4,3,2,1,0:T(8,128)S(1)} copy-done((s32[1,1,16,128,128]{4,3,2,1,0:T(8,128)S(1)}, s32[1,1,16,128,128]{4,3,2,1,0:T(8,128)}, u32[]{:S(2)}) %copy-start.1) | copy-done | bytes 1048600
  13.1 1.0 %shard_map.184 = (bf16[17,128,128]{2,1,0:T(8,128)(2,1)S(1)}, bf16[17,128,128]{2,1,0:T(8,128)(2,1)S(1)}, bf16[17,128,128]{2,1,0:T(8,128)(2,1)S(1)}, s32[8,128]{1,0:T(8,128)S(1)}, f32[8,128]{1,0:T(8,128)S(1)}) custom-call(s32[1,1]{1,0:T(1,128)S(6)} %copy.20.tile_count, s32[16,128,128]{2,1,0:T(8,128)S(1)} %bitcast.5, s32[1,1,16]{2,1,0:T(1,128)S(1)} %copy-done.9, ...), custom_call_target="tpu_custom_call" | custom-call | flops 268435456 | bytes 2729600 | tf_op jit(solution)/shard_map/pallas_call | solution.py:44
  14.1 3.9 %shard_map.186 = (bf16[4,128,128]{2,1,0:T(8,128)(2,1)S(1)}, bf16[12,128,128]{2,1,0:T(8,128)(2,1)S(1)}, f32[4,128,128]{2,1,0:T(8,128)S(1)}, f32[4,128,128]{2,1,0:...) custom-call(s32[1,1]{1,0:T(1,128)S(6)} %copy.20.tile_count, s32[8,128]{1,0:T(8,128)S(1)} %get-tuple-element.45.most, ...), custom_call_target="tpu_custom_call" | custom-call | flops 1073741824 | bytes 3739648 | tf_op jit(solution)/shard_map/pallas_call | solution.py:44
  18.0 3.4 %collective-permute-done.3.refs_4_.refs_5_ = bf16[576,128]{1,0:T(8,128)(2,1)S(1)} collective-permute-done((bf16[576,128]{1,0:T(8,128)(2,1)}, bf16[576,128]{1,0:T(8,128)(2,1)S(1)}, u32[]{:S(2)}, u32[]{:S(2)}) %collective-permute-start.3) | collective-permute-done | bytes 147488 | tf_op jit(solution)/shard_map/ppermute | solution.py:558
  21.4 4.1 %shard_map.187 = (bf16[512,128]{1,0:T(8,128)(2,1)S(1)}, bf16[512,128]{1,0:T(8,128)(2,1)S(1)}, bf16[512,128]{1,0:T(8,128)(2,1)S(1)}, bf16[512,128]{1,0:T(8,128)(2,1)S(1)}, bf16[16,128,128]{2,1,0:T(8,128)(2,1)S(1)}) custom-call(s32[1,1]{1,0:T(1,128)S(6)} %copy.20.tile_count, s32[8,128]{1,0:T(8,128)S(1)} %get-tuple-element.45.most, ...), custom_call_target="tpu_custom_call" | custom-call | flops 2147483648 | bytes 4227072 | tf_op jit(solution)/shard_map/pallas_call | solution.py:44
  25.5 0.1 collective-permute-start.5
  25.6 2.6 %collective-permute-start.6 = (bf16[512,128]{1,0:T(8,128)(2,1)S(1)}, bf16[512,128]{1,0:T(8,128)(2,1)S(1)}, u32[]{:S(2)}, u32[]{:S(2)}) collective-permute-start(bf16[512,128]{1,0:T(8,128)(2,1)S(1)} %get-tuple-element.59), channel_id=1, source_target_pairs={{0,28},{4,0},{8,4},{12,8},{16,12},{20,16},{24,20},{28,24},{1,29},{... | collective-permute-start | bytes 393224 | tf_op jit(solution)/shard_map/ppermute | solution.py:22
  28.2 0.0 copy-start.5
  28.3 2.4 %shard_map.188 = (f32[512,128]{1,0:T(8,128)S(1)}, f32[512,128]{1,0:T(8,128)S(1)}) custom-call(s32[1,1]{1,0:T(1,128)S(6)} %copy.20.tile_count, s32[8,128]{1,0:T(8,128)S(1)} %get-tuple-element.45.most, bf16[17,128,128]{2,1,0:T(8,128)(2,1)S(1)} %get-tuple-element.46.row_rank, bf16[17,128,128]{2,1,0:T(8,128)(2,1)S(1)} %get-tuple-element.47.row_degree, ...), custom_call_target="tpu_custom_call" | custom-call | flops 1073741824 | bytes 3084288 | tf_op jit(solution)/shard_map/pallas_call | solution.py:44
  30.7 1.1 %collective-permute-done.5.sum_low = bf16[512,128]{1,0:T(8,128)(2,1)S(1)} collective-permute-done((bf16[512,128]{1,0:T(8,128)(2,1)S(1)}, bf16[512,128]{1,0:T(8,128)(2,1)S(1)}, u32[]{:S(2)}, u32[]{:S(2)}) %collective-permute-start.5) | collective-permute-done | bytes 131104 | tf_op jit(solution)/shard_map/ppermute | solution.py:22
  31.9 1.4 %shard_map.189 = (bf16[512,128]{1,0:T(8,128)(2,1)}, bf16[1024,128]{1,0:T(8,128)(2,1)S(1)}, bf16[1024,128]{1,0:T(8,128)(2,1)S(1)}, bf16[512,128]{1,0:T(8,128)(2,1...) custom-call(f32[8,128]{1,0:T(8,128)S(1)} %get-tuple-element.44.vecto, ...), custom_call_target="tpu_custom_call" | custom-call | flops 117440512 | bytes 2625536 | tf_op jit(solution)/shard_map/pallas_call | solution.py:44
  33.2 1.0 %shard_map.190 = (f32[256,128]{1,0:T(8,128)S(1)}, bf16[256,128]{1,0:T(8,128)(2,1)}) custom-call(bf16[512,128]{1,0:T(8,128)(2,1)S(1)} %copy-done, bf16[512,128]{1,0:T(8,128)(2,1)S(1)} %get-tuple-element.63.aggregate, bf16[512,128]{1,0:T(8,128)(2,1)S(1)} %get-tuple-element.64.message, bf16[512,128]{1,0:T(8,128)(2,1)S(1)} %get-tuple-element.65.hidden, ...), custom_call_target="tpu_custom_call" | custom-call | flops 67108864 | bytes 1114112 | tf_op jit(solution)/shard_map/pallas_call | solution.py:44
  34.2 2.5 %collective-permute-start.9 = (bf16[1024,128]{1,0:T(8,128)(2,1)S(1)}, bf16[1024,128]{1,0:T(8,128)(2,1)S(1)}, u32[]{:S(2)}, u32[]{:S(2)}) collective-permute-start(bf16[1024,128]{1,0:T(8,128)(2,1)S(1)} %get-tuple-element.72), channel_id=1, source_target_pairs={{0,4},{4,8},{8,12},{12,16},{16,20},{20,24},{24,28},{28,0},{1,5},{5... | collective-permute-start | bytes 786440 | tf_op jit(solution)/shard_map/ppermute | solution.py:22
  36.7 0.2 collective-permute-start.10
  36.9 3.2 %shard_map.191.refs_2_ = f32[16,128,128]{2,1,0:T(8,128)S(1)} custom-call(s32[1,1]{1,0:T(1,128)S(6)} %copy.20.tile_count, s32[8,128]{1,0:T(8,128)S(1)} %get-tuple-element.45.most, bf16[17,128,128]{2,1,0:T(8,128)(2,1)S(1)} %get-tuple-element.71.col_rank, bf16[16,128,128]{2,1,0:T(8,128)(2,1)S(1)} %get-tuple-element.56.refs_0_.senders, ...), custom_call_target="tpu_custom_call" | custom-call | flops 134217728 | bytes 2789376 | tf_op jit(solution)/shard_map/pallas_call | solution.py:44
  40.2 0.9 %convert_add_fusion = f32[256,128]{1,0:T(8,128)S(1)} fusion(f32[256,128]{1,0:T(8,128)S(1)} %get-tuple-element.69, bf16[256,128]{1,0:T(8,128)(2,1)} %collective-permute-done.7), kind=kLoop, calls=%fused_computation | loop fusion | flops 65536 | bytes 327680 | tf_op jit(solution)/shard_map/add | solution.py:777
  41.1 3.6 %collective-permute-start.8 = (bf16[128,128]{1,0:T(8,128)(2,1)S(1)}, bf16[128,128]{1,0:T(8,128)(2,1)S(1)}, u32[]{:S(2)}, u32[]{:S(2)}) collective-permute-start(bf16[128,128]{1,0:T(8,128)(2,1)S(1)} %select_convert_fusion), channel_id=1, source_target_pairs={{0,2},{1,3},{2,0},{3,1},{4,6},{5,7},{6,4},{7,5},{8,10},{9,11},{10,... | collective-permute-start | bytes 98312 | tf_op jit(solution)/shard_map/ppermute | solution.py:558
  44.6 6.7 %shard_map.192 = (f32[512,128]{1,0:T(8,128)S(1)}, bf16[512,128]{1,0:T(8,128)(2,1)S(1)}, bf16[512,128]{1,0:T(8,128)(2,1)S(1)}, bf16[512,128]{1,0:T(8,128)(2,1)S(1)}, bf16[128,128]{1,0:T(8,128)(2,1)S(1)}) custom-call(s32[1,1]{1,0:T(1,128)S(6)} %copy.20.tile_count, s32[8,128]{1,0:T(8,128)S(1)} %get-tuple-element.45.most, ...), custom_call_target="tpu_custom_call" | custom-call | flops 2147483648 | bytes 4329472 | tf_op jit(solution)/shard_map/pallas_call | solution.py:44
  51.4 0.4 shard_map.193
  51.9 0.1 collective-permute-start.11
  51.9 1.2 %collective-permute-done.11 = bf16[192,128]{1,0:T(8,128)(2,1)S(1)} collective-permute-done((bf16[192,128]{1,0:T(8,128)(2,1)S(1)}, bf16[192,128]{1,0:T(8,128)(2,1)S(1)}, u32[]{:S(2)}, u32[]{:S(2)}) %collective-permute-start.11) | collective-permute-done | bytes 49184 | tf_op jit(solution)/shard_map/ppermute | solution.py:558
  53.2 0.9 %collective-permute-start.12 = (bf16[192,128]{1,0:T(8,128)(2,1)S(1)}, bf16[192,128]{1,0:T(8,128)(2,1)S(1)}, u32[]{:S(2)}, u32[]{:S(2)}) collective-permute-start(bf16[192,128]{1,0:T(8,128)(2,1)S(1)} %add_convert_fusion.2), channel_id=1, source_target_pairs={{0,8},{4,12},{8,0},{12,4},{16,24},{20,28},{24,16},{28,20},{1,9},{5... | collective-permute-start | bytes 147464 | tf_op jit(solution)/shard_map/ppermute | solution.py:558
  54.1 1.9 %collective-permute-start.15 = (bf16[512,128]{1,0:T(8,128)(2,1)S(1)}, bf16[512,128]{1,0:T(8,128)(2,1)S(1)}, u32[]{:S(2)}, u32[]{:S(2)}) collective-permute-start(bf16[512,128]{1,0:T(8,128)(2,1)S(1)} %get-tuple-element.81), channel_id=1, source_target_pairs={{0,2},{1,3},{2,0},{3,1},{4,6},{5,7},{6,4},{7,5},{8,10},{9,11},{10,... | collective-permute-start | bytes 393224 | tf_op jit(solution)/shard_map/ppermute | solution.py:558
  56.0 2.5 %collective-permute-start.16 = (bf16[512,128]{1,0:T(8,128)(2,1)S(1)}, bf16[512,128]{1,0:T(8,128)(2,1)S(1)}, u32[]{:S(2)}, u32[]{:S(2)}) collective-permute-start(bf16[512,128]{1,0:T(8,128)(2,1)S(1)} %get-tuple-element.82), channel_id=1, source_target_pairs={{0,3},{1,2},{2,1},{3,0},{4,7},{5,6},{6,5},{7,4},{8,11},{9,10},{10,... | collective-permute-start | bytes 393224 | tf_op jit(solution)/shard_map/ppermute | solution.py:558
  58.5 0.1 collective-permute-start.13
  58.6 3.6 %collective-permute-done.14.refs_0_ = bf16[512,128]{1,0:T(8,128)(2,1)S(1)} collective-permute-done((bf16[512,128]{1,0:T(8,128)(2,1)S(1)}, bf16[512,128]{1,0:T(8,128)(2,1)S(1)}, u32[]{:S(2)}, u32[]{:S(2)}) %collective-permute-start.14) | collective-permute-done | bytes 131104 | tf_op jit(solution)/shard_map/ppermute | solution.py:558
  62.2 4.9 %collective-permute-done.15.refs_1_ = bf16[512,128]{1,0:T(8,128)(2,1)S(1)} collective-permute-done((bf16[512,128]{1,0:T(8,128)(2,1)S(1)}, bf16[512,128]{1,0:T(8,128)(2,1)S(1)}, u32[]{:S(2)}, u32[]{:S(2)}) %collective-permute-start.15) | collective-permute-done | bytes 131104 | tf_op jit(solution)/shard_map/ppermute | solution.py:558
  67.0 0.9 %shard_map.194 = f32[512,128]{1,0:T(8,128)} custom-call(f32[512,128]{1,0:T(8,128)S(1)} %get-tuple-element.78.direct, bf16[128,128]{1,0:T(8,128)(2,1)S(1)} %copy-done.8, f32[512,128]{1,0:T(8,128)S(1)} %get-tuple-element.79.own, bf16[512,128]{1,0:T(8,128)(2,1)S(1)} %collective-permute-done.14.refs_0_, bf16[512,128]{1,0:T(8,128)(2,1)S(1)} %collective-permute-done.15.refs_1_, ...), custom_call_target="tpu_custom_call" | custom-call | flops 16777216 | bytes 1212416 | tf_op jit(solution)/shard_map/pallas_call | solution.py:44
  68.0 2.6 %collective-permute-start.17 = (bf16[192,128]{1,0:T(8,128)(2,1)S(1)}, bf16[192,128]{1,0:T(8,128)(2,1)S(1)}, u32[]{:S(2)}, u32[]{:S(2)}) collective-permute-start(bf16[192,128]{1,0:T(8,128)(2,1)S(1)} %add_convert_fusion.refs_0_), channel_id=1, source_target_pairs={{0,1},{1,0},{2,3},{3,2},{4,5},{5,4},{6,7},{7,6},{8,9},{9,8},{10,11... | collective-permute-start | bytes 147464 | tf_op jit(solution)/shard_map/ppermute | solution.py:558
  70.5 1.6 %collective-permute-start.18 = (bf16[192,128]{1,0:T(8,128)(2,1)S(1)}, bf16[192,128]{1,0:T(8,128)(2,1)S(1)}, u32[]{:S(2)}, u32[]{:S(2)}) collective-permute-start(bf16[192,128]{1,0:T(8,128)(2,1)S(1)} %add_convert_fusion.refs_0_), channel_id=1, source_target_pairs={{0,2},{1,3},{2,0},{3,1},{4,6},{5,7},{6,4},{7,5},{8,10},{9,11},{10,... | collective-permute-start | bytes 147464 | tf_op jit(solution)/shard_map/ppermute | solution.py:558
  72.1 1.4 %collective-permute-start.19 = (bf16[192,128]{1,0:T(8,128)(2,1)S(1)}, bf16[192,128]{1,0:T(8,128)(2,1)S(1)}, u32[]{:S(2)}, u32[]{:S(2)}) collective-permute-start(bf16[192,128]{1,0:T(8,128)(2,1)S(1)} %add_convert_fusion.refs_0_), channel_id=1, source_target_pairs={{0,3},{1,2},{2,1},{3,0},{4,7},{5,6},{6,5},{7,4},{8,11},{9,10},{10,... | collective-permute-start | bytes 147464 | tf_op jit(solution)/shard_map/ppermute | solution.py:558
  73.5 3.4 %collective-permute-done.18.refs_2_ = bf16[192,128]{1,0:T(8,128)(2,1)S(1)} collective-permute-done((bf16[192,128]{1,0:T(8,128)(2,1)S(1)}, bf16[192,128]{1,0:T(8,128)(2,1)S(1)}, u32[]{:S(2)}, u32[]{:S(2)}) %collective-permute-start.18) | collective-permute-done | bytes 49184 | tf_op jit(solution)/shard_map/ppermute | solution.py:558
  77.0 1.2 %collective-permute-done.19.refs_3_ = bf16[192,128]{1,0:T(8,128)(2,1)S(1)} collective-permute-done((bf16[192,128]{1,0:T(8,128)(2,1)S(1)}, bf16[192,128]{1,0:T(8,128)(2,1)S(1)}, u32[]{:S(2)}, u32[]{:S(2)}) %collective-permute-start.19) | collective-permute-done | bytes 49184 | tf_op jit(solution)/shard_map/ppermute | solution.py:558
  78.1 0.1 collective-permute-start.20
  78.2 1.3 %collective-permute-done.20.other = bf16[384,128]{1,0:T(8,128)(2,1)S(1)} collective-permute-done((bf16[384,128]{1,0:T(8,128)(2,1)S(1)}, bf16[384,128]{1,0:T(8,128)(2,1)S(1)}, u32[]{:S(2)}, u32[]{:S(2)}) %collective-permute-start.20) | collective-permute-done | bytes 98336 | tf_op jit(solution)/shard_map/ppermute | solution.py:558
  79.5 0.8 shard_map.196
  (52 shorter events, 0.2 us)
Async XLA Ops:
  2.2 11.9 %collective-permute-start = (bf16[576,128]{1,0:T(8,128)(2,1)}, bf16[576,128]{1,0:T(8,128)(2,1)S(1)}, u32[]{:S(2)}, u32[]{:S(2)}) collective-permute-start(bf16[576,128]{1,0:T(8,128)(2,1)} %get-tuple-element.49.message.refs_3_), channel_id=1, source_target_pairs={{0,4},{4,8},{8,12},{12,16},{16,20},{20,24},{24,28},{28,0},{1,5},{5... | collective-permute-start | bytes 442376 | tf_op jit(solution)/shard_map/ppermute | solution.py:22
  2.7 11.4 %collective-permute-start.1 = (bf16[576,128]{1,0:T(8,128)(2,1)}, bf16[576,128]{1,0:T(8,128)(2,1)S(1)}, u32[]{:S(2)}, u32[]{:S(2)}) collective-permute-start(bf16[576,128]{1,0:T(8,128)(2,1)} %get-tuple-element.49.message.refs_3_), channel_id=1, source_target_pairs={{0,28},{4,0},{8,4},{12,8},{16,12},{20,16},{24,20},{28,24},{1,29},{... | collective-permute-start | bytes 442376 | tf_op jit(solution)/shard_map/ppermute | solution.py:22
  5.6 12.4 %collective-permute-start.2 = (bf16[576,128]{1,0:T(8,128)(2,1)}, bf16[576,128]{1,0:T(8,128)(2,1)S(1)}, u32[]{:S(2)}, u32[]{:S(2)}) collective-permute-start(bf16[576,128]{1,0:T(8,128)(2,1)} %get-tuple-element.49.message.refs_3_), channel_id=1, source_target_pairs={{0,1},{1,0},{2,3},{3,2},{4,5},{5,4},{6,7},{7,6},{8,9},{9,8},{10,11... | collective-permute-start | bytes 442376 | tf_op jit(solution)/shard_map/ppermute | solution.py:558
  7.9 13.5 %collective-permute-start.3 = (bf16[576,128]{1,0:T(8,128)(2,1)}, bf16[576,128]{1,0:T(8,128)(2,1)S(1)}, u32[]{:S(2)}, u32[]{:S(2)}) collective-permute-start(bf16[576,128]{1,0:T(8,128)(2,1)} %get-tuple-element.49.message.refs_3_), channel_id=1, source_target_pairs={{0,2},{1,3},{2,0},{3,1},{4,6},{5,7},{6,4},{7,5},{8,10},{9,11},{10,... | collective-permute-start | bytes 442376 | tf_op jit(solution)/shard_map/ppermute | solution.py:558
  10.5 10.9 %collective-permute-start.4 = (bf16[576,128]{1,0:T(8,128)(2,1)}, bf16[576,128]{1,0:T(8,128)(2,1)S(1)}, u32[]{:S(2)}, u32[]{:S(2)}) collective-permute-start(bf16[576,128]{1,0:T(8,128)(2,1)} %get-tuple-element.49.message.refs_3_), channel_id=1, source_target_pairs={{0,3},{1,2},{2,1},{3,0},{4,7},{5,6},{6,5},{7,4},{8,11},{9,10},{10,... | collective-permute-start | bytes 442376 | tf_op jit(solution)/shard_map/ppermute | solution.py:558
  11.2 0.7 copy-start.12
  11.2 0.7 copy-start.13
  11.2 0.7 copy-start.9
  11.2 0.7 copy-start.10
  11.2 0.7 copy-start.11
  11.9 1.2 %copy-start.1 = (s32[1,1,16,128,128]{4,3,2,1,0:T(8,128)S(1)}, s32[1,1,16,128,128]{4,3,2,1,0:T(8,128)}, u32[]{:S(2)}) copy-start(s32[1,1,16,128,128]{4,3,2,1,0:T(8,128)} %param.21) | copy-start | bytes 3145732
  13.1 1.0 %copy-start.7 = (bf16[128,128]{1,0:T(8,128)(2,1)S(1)}, bf16[128,128]{1,0:T(8,128)(2,1)}, u32[]{:S(2)}) copy-start(bf16[128,128]{1,0:T(8,128)(2,1)} %w_recv.3) | copy-start | bytes 98308
  13.1 1.0 %copy-start.8 = (bf16[128,128]{1,0:T(8,128)(2,1)S(1)}, bf16[128,128]{1,0:T(8,128)(2,1)}, u32[]{:S(2)}) copy-start(bf16[128,128]{1,0:T(8,128)(2,1)} %w_send.3) | copy-start | bytes 98308
  13.1 1.0 %copy-start.14 = (bf16[576,128]{1,0:T(8,128)(2,1)S(1)}, bf16[576,128]{1,0:T(8,128)(2,1)}, u32[]{:S(2)}) copy-start(bf16[576,128]{1,0:T(8,128)(2,1)} %get-tuple-element.49.message.refs_3_) | copy-start | bytes 442372
  13.1 1.0 %copy-start.17 = (bf16[16,384]{1,0:T(8,128)(2,1)S(1)}, bf16[16,384]{1,0:T(8,128)(2,1)}, u32[]{:S(2)}) copy-start(bf16[16,384]{1,0:T(8,128)(2,1)} %get-tuple-element.48.weight_parts.refs_2_) | copy-start | bytes 36868
  21.4 4.1 %copy-start.15 = (bf16[576,128]{1,0:T(8,128)(2,1)}, bf16[576,128]{1,0:T(8,128)(2,1)S(1)}, u32[]{:S(2)}) copy-start(bf16[576,128]{1,0:T(8,128)(2,1)S(1)} %collective-permute-done.4.refs_5_.refs_6_) | copy-start | bytes 442372
  25.5 6.3 %collective-permute-start.5 = (bf16[512,128]{1,0:T(8,128)(2,1)S(1)}, bf16[512,128]{1,0:T(8,128)(2,1)S(1)}, u32[]{:S(2)}, u32[]{:S(2)}) collective-permute-start(bf16[512,128]{1,0:T(8,128)(2,1)S(1)} %get-tuple-element.58), channel_id=1, source_target_pairs={{0,4},{4,8},{8,12},{12,16},{16,20},{20,24},{24,28},{28,0},{1,5},{5... | collective-permute-start | bytes 393224 | tf_op jit(solution)/shard_map/ppermute | solution.py:22
  25.6 6.2 %collective-permute-start.6 = (bf16[512,128]{1,0:T(8,128)(2,1)S(1)}, bf16[512,128]{1,0:T(8,128)(2,1)S(1)}, u32[]{:S(2)}, u32[]{:S(2)}) collective-permute-start(bf16[512,128]{1,0:T(8,128)(2,1)S(1)} %get-tuple-element.59), channel_id=1, source_target_pairs={{0,28},{4,0},{8,4},{12,8},{16,12},{20,16},{24,20},{28,24},{1,29},{... | collective-permute-start | bytes 393224 | tf_op jit(solution)/shard_map/ppermute | solution.py:22
  28.2 3.6 %copy-start = (bf16[512,128]{1,0:T(8,128)(2,1)S(1)}, bf16[512,128]{1,0:T(8,128)(2,1)}, u32[]{:S(2)}) copy-start(bf16[512,128]{1,0:T(8,128)(2,1)} %latent.7) | copy-start | bytes 393220
  28.2 3.6 %copy-start.2 = (bf16[512,128]{1,0:T(8,128)(2,1)S(1)}, bf16[512,128]{1,0:T(8,128)(2,1)}, u32[]{:S(2)}) copy-start(bf16[512,128]{1,0:T(8,128)(2,1)} %cotangent.3) | copy-start | bytes 393220
  28.2 3.6 %copy-start.3 = (bf16[128,128]{1,0:T(8,128)(2,1)S(1)}, bf16[128,128]{1,0:T(8,128)(2,1)}, u32[]{:S(2)}) copy-start(bf16[128,128]{1,0:T(8,128)(2,1)} %w_edge_out.3) | copy-start | bytes 98308
  28.2 3.6 %copy-start.4 = (bf16[128,128]{1,0:T(8,128)(2,1)S(1)}, bf16[128,128]{1,0:T(8,128)(2,1)}, u32[]{:S(2)}) copy-start(bf16[128,128]{1,0:T(8,128)(2,1)} %w_node_self.3) | copy-start | bytes 98308
  28.2 3.6 %copy-start.5 = (bf16[128,128]{1,0:T(8,128)(2,1)S(1)}, bf16[128,128]{1,0:T(8,128)(2,1)}, u32[]{:S(2)}) copy-start(bf16[128,128]{1,0:T(8,128)(2,1)} %w_node_msg.1) | copy-start | bytes 98308
  28.3 3.6 %copy-start.6 = (bf16[128,128]{1,0:T(8,128)(2,1)S(1)}, bf16[128,128]{1,0:T(8,128)(2,1)}, u32[]{:S(2)}) copy-start(bf16[128,128]{1,0:T(8,128)(2,1)} %w_node_out.1) | copy-start | bytes 98308
  34.2 5.9 %collective-permute-start.7 = (bf16[256,128]{1,0:T(8,128)(2,1)}, bf16[256,128]{1,0:T(8,128)(2,1)}, u32[]{:S(2)}, u32[]{:S(2)}) collective-permute-start(bf16[256,128]{1,0:T(8,128)(2,1)} %get-tuple-element.70), channel_id=1, source_target_pairs={{0,1},{1,0},{2,3},{3,2},{4,5},{5,4},{6,7},{7,6},{8,9},{9,8},{10,11... | collective-permute-start | bytes 196616 | tf_op jit(solution)/shard_map/ppermute | solution.py:558
  34.2 10.4 %collective-permute-start.9 = (bf16[1024,128]{1,0:T(8,128)(2,1)S(1)}, bf16[1024,128]{1,0:T(8,128)(2,1)S(1)}, u32[]{:S(2)}, u32[]{:S(2)}) collective-permute-start(bf16[1024,128]{1,0:T(8,128)(2,1)S(1)} %get-tuple-element.72), channel_id=1, source_target_pairs={{0,4},{4,8},{8,12},{12,16},{16,20},{20,24},{24,28},{28,0},{1,5},{5... | collective-permute-start | bytes 786440 | tf_op jit(solution)/shard_map/ppermute | solution.py:22
  36.7 7.9 %collective-permute-start.10 = (bf16[1024,128]{1,0:T(8,128)(2,1)S(1)}, bf16[1024,128]{1,0:T(8,128)(2,1)S(1)}, u32[]{:S(2)}, u32[]{:S(2)}) collective-permute-start(bf16[1024,128]{1,0:T(8,128)(2,1)S(1)} %get-tuple-element.73.refs_0_), channel_id=1, source_target_pairs={{0,28},{4,0},{8,4},{12,8},{16,12},{20,16},{24,20},{28,24},{1,29},{... | collective-permute-start | bytes 786440 | tf_op jit(solution)/shard_map/ppermute | solution.py:22
  40.2 4.5 %copy-start.16 = (bf16[576,128]{1,0:T(8,128)(2,1)S(1)}, bf16[576,128]{1,0:T(8,128)(2,1)}, u32[]{:S(2)}) copy-start(bf16[576,128]{1,0:T(8,128)(2,1)} %copy-done.15) | copy-start | bytes 442372
  41.1 10.3 %collective-permute-start.8 = (bf16[128,128]{1,0:T(8,128)(2,1)S(1)}, bf16[128,128]{1,0:T(8,128)(2,1)S(1)}, u32[]{:S(2)}, u32[]{:S(2)}) collective-permute-start(bf16[128,128]{1,0:T(8,128)(2,1)S(1)} %select_convert_fusion), channel_id=1, source_target_pairs={{0,2},{1,3},{2,0},{3,1},{4,6},{5,7},{6,4},{7,5},{8,10},{9,11},{10,... | collective-permute-start | bytes 98312 | tf_op jit(solution)/shard_map/ppermute | solution.py:558
  51.9 1.3 %collective-permute-start.11 = (bf16[192,128]{1,0:T(8,128)(2,1)S(1)}, bf16[192,128]{1,0:T(8,128)(2,1)S(1)}, u32[]{:S(2)}, u32[]{:S(2)}) collective-permute-start(bf16[192,128]{1,0:T(8,128)(2,1)S(1)} %broadcast_select_fusion), channel_id=1, source_target_pairs={{0,4},{4,0},{8,12},{12,8},{16,20},{20,16},{24,28},{28,24},{1,5},{5... | collective-permute-start | bytes 147464 | tf_op jit(solution)/shard_map/ppermute | solution.py:558
  53.2 5.3 %collective-permute-start.12 = (bf16[192,128]{1,0:T(8,128)(2,1)S(1)}, bf16[192,128]{1,0:T(8,128)(2,1)S(1)}, u32[]{:S(2)}, u32[]{:S(2)}) collective-permute-start(bf16[192,128]{1,0:T(8,128)(2,1)S(1)} %add_convert_fusion.2), channel_id=1, source_target_pairs={{0,8},{4,12},{8,0},{12,4},{16,24},{20,28},{24,16},{28,20},{1,9},{5... | collective-permute-start | bytes 147464 | tf_op jit(solution)/shard_map/ppermute | solution.py:558
  54.1 8.1 %collective-permute-start.14 = (bf16[512,128]{1,0:T(8,128)(2,1)S(1)}, bf16[512,128]{1,0:T(8,128)(2,1)S(1)}, u32[]{:S(2)}, u32[]{:S(2)}) collective-permute-start(bf16[512,128]{1,0:T(8,128)(2,1)S(1)} %get-tuple-element.80), channel_id=1, source_target_pairs={{0,1},{1,0},{2,3},{3,2},{4,5},{5,4},{6,7},{7,6},{8,9},{9,8},{10,11... | collective-permute-start | bytes 393224 | tf_op jit(solution)/shard_map/ppermute | solution.py:558
  54.1 12.9 %collective-permute-start.15 = (bf16[512,128]{1,0:T(8,128)(2,1)S(1)}, bf16[512,128]{1,0:T(8,128)(2,1)S(1)}, u32[]{:S(2)}, u32[]{:S(2)}) collective-permute-start(bf16[512,128]{1,0:T(8,128)(2,1)S(1)} %get-tuple-element.81), channel_id=1, source_target_pairs={{0,2},{1,3},{2,0},{3,1},{4,6},{5,7},{6,4},{7,5},{8,10},{9,11},{10,... | collective-permute-start | bytes 393224 | tf_op jit(solution)/shard_map/ppermute | solution.py:558
  56.0 11.1 %collective-permute-start.16 = (bf16[512,128]{1,0:T(8,128)(2,1)S(1)}, bf16[512,128]{1,0:T(8,128)(2,1)S(1)}, u32[]{:S(2)}, u32[]{:S(2)}) collective-permute-start(bf16[512,128]{1,0:T(8,128)(2,1)S(1)} %get-tuple-element.82), channel_id=1, source_target_pairs={{0,3},{1,2},{2,1},{3,0},{4,7},{5,6},{6,5},{7,4},{8,11},{9,10},{10,... | collective-permute-start | bytes 393224 | tf_op jit(solution)/shard_map/ppermute | solution.py:558
  58.5 9.4 %collective-permute-start.13 = (bf16[192,128]{1,0:T(8,128)(2,1)S(1)}, bf16[192,128]{1,0:T(8,128)(2,1)S(1)}, u32[]{:S(2)}, u32[]{:S(2)}) collective-permute-start(bf16[192,128]{1,0:T(8,128)(2,1)S(1)} %add_convert_fusion.1), channel_id=1, source_target_pairs={{0,16},{4,20},{8,24},{12,28},{16,0},{20,4},{24,8},{28,12},{1,17},{... | collective-permute-start | bytes 147464 | tf_op jit(solution)/shard_map/ppermute | solution.py:558
  68.0 5.5 %collective-permute-start.17 = (bf16[192,128]{1,0:T(8,128)(2,1)S(1)}, bf16[192,128]{1,0:T(8,128)(2,1)S(1)}, u32[]{:S(2)}, u32[]{:S(2)}) collective-permute-start(bf16[192,128]{1,0:T(8,128)(2,1)S(1)} %add_convert_fusion.refs_0_), channel_id=1, source_target_pairs={{0,1},{1,0},{2,3},{3,2},{4,5},{5,4},{6,7},{7,6},{8,9},{9,8},{10,11... | collective-permute-start | bytes 147464 | tf_op jit(solution)/shard_map/ppermute | solution.py:558
  70.5 6.4 %collective-permute-start.18 = (bf16[192,128]{1,0:T(8,128)(2,1)S(1)}, bf16[192,128]{1,0:T(8,128)(2,1)S(1)}, u32[]{:S(2)}, u32[]{:S(2)}) collective-permute-start(bf16[192,128]{1,0:T(8,128)(2,1)S(1)} %add_convert_fusion.refs_0_), channel_id=1, source_target_pairs={{0,2},{1,3},{2,0},{3,1},{4,6},{5,7},{6,4},{7,5},{8,10},{9,11},{10,... | collective-permute-start | bytes 147464 | tf_op jit(solution)/shard_map/ppermute | solution.py:558
  72.1 6.0 %collective-permute-start.19 = (bf16[192,128]{1,0:T(8,128)(2,1)S(1)}, bf16[192,128]{1,0:T(8,128)(2,1)S(1)}, u32[]{:S(2)}, u32[]{:S(2)}) collective-permute-start(bf16[192,128]{1,0:T(8,128)(2,1)S(1)} %add_convert_fusion.refs_0_), channel_id=1, source_target_pairs={{0,3},{1,2},{2,1},{3,0},{4,7},{5,6},{6,5},{7,4},{8,11},{9,10},{10,... | collective-permute-start | bytes 147464 | tf_op jit(solution)/shard_map/ppermute | solution.py:558
  78.1 1.4 %collective-permute-start.20 = (bf16[384,128]{1,0:T(8,128)(2,1)S(1)}, bf16[384,128]{1,0:T(8,128)(2,1)S(1)}, u32[]{:S(2)}, u32[]{:S(2)}) collective-permute-start(bf16[384,128]{1,0:T(8,128)(2,1)S(1)} %shard_map.195.mine), channel_id=1, source_target_pairs={{0,4},{4,0},{8,12},{12,8},{16,20},{20,16},{24,28},{28,24},{1,5},{5... | collective-permute-start | bytes 294920 | tf_op jit(solution)/shard_map/ppermute | solution.py:558

commit v14 on v13

--- a/solution.py
+++ b/solution.py
@@ -452,6 +452,17 @@
     give[...] = grads[pl.ds(pl.multiple_of((1 - bit) * half, half), half), :].astype(BF16)
 
 
+def make_half(step):
+    def kernel(mine, arrived, keep, give):
+        half = keep.shape[0]
+        high = jnp.where((lax.axis_index("grp") & step) != 0, 1, 0)
+        for out, place in ((keep, high), (give, 1 - high)):
+            span = pl.ds(pl.multiple_of(place * half, half), half)
+            out[...] = (mine[span, :] + arrived[span, :].astype(F32)).astype(out.dtype)
+
+    return kernel
+
+
 def recv_kernel(
     latent,
     cotangent,
@@ -576,8 +587,9 @@
     return parts[0]
 
 
-def all_parts(value, axis):
-    return [value] + [exchanged(value, axis, step) for step in range(1, lax.axis_size(axis))]
+def all_parts(value, axis, least=1):
+    steps = range(least, lax.axis_size(axis), least)
+    return [value] + [exchanged(value, axis, step) for step in steps]
 
 
 def make_gather(rows):
@@ -774,18 +786,19 @@
         scratch=[pltpu.VMEM((2 * half, width), F32)],
         flops=8 * own_rows * width * width,
     )
-    share = share + exchanged(given, "grp", 1).astype(F32)
-    arrived = jnp.zeros_like(share)
+    arrived = exchanged(given, "grp", 1)
+    arrived, from_low, from_high = lax.optimization_barrier((arrived, from_low, from_high))
     step = 2
     while step < members:
-        half = share.shape[0] // 2
-        high = bit_set("grp", step)
-        given = jnp.where(high, share[:half], share[half:]).astype(BF16)
-        share = jnp.where(high, share[half:], share[:half])
+        half //= 2
+        share, given = call(
+            make_half(step),
+            [like((half, width), F32), like((half, width), BF16)],
+            [share, arrived],
+            flops=share.size,
+        )
         arrived = exchanged(given, "grp", step)
         step *= 2
-        if step < members:
-            share = share + arrived.astype(F32)
     back_scratch = [
         pltpu.VMEM((3 * blocks, size, width), BF16),
         pltpu.VMEM((2, size, width), F32),
@@ -843,13 +856,6 @@
         chain, given = halves(chain, (rows, width, width))
         chain = (chain.astype(F32) + exchanged(given, "blk", 1).astype(F32)).astype(BF16)
         rows //= 2
-        step = 2
-        while step < slabs:
-            chain = (chain.astype(F32) + exchanged(chain, "blk", step).astype(F32)).astype(BF16)
-            step *= 2
-    else:
-        chain = lax.psum(chain.astype(F32), "blk").astype(BF16)
-    chain, latent_grad = lax.optimization_barrier((chain, latent_grad))
     summed_rows = chain.shape[0] - rows
     (chain,) = call(
         make_gather(rows),
@@ -857,6 +863,11 @@
         all_parts(chain, "grp"),
         flops=members * chain.size,
     )
+    if paired:
+        chain = tree_sum([part.astype(F32) for part in all_parts(chain, "blk", 2)]).astype(BF16)
+    else:
+        chain = lax.psum(chain.astype(F32), "blk").astype(BF16)
+    chain, latent_grad = lax.optimization_barrier((chain, latent_grad))
     if paired:
         (weight_grads,) = call(
             make_last(members), [like((6 * width, width), F32)], [chain, exchanged(chain, "blk", 1)]

time: 80.1 us -> 75.6 us (0.944)
  starting transfers between devices: 28.2 us -> 23.6 us
  other arithmetic: 0.99 us -> 0.11 us
    ppermute x15 -> x16, starting transfers between devices: 19.6 us -> 14.9 us  [exchanged(): lax.ppermute(value, axis, [(source, source ^ step) for source in range(co...]
    add x1 -> x0, other arithmetic: 0.89 us -> none  [body(): share = share + exchanged(given, 'grp', 1).astype(F32)]
    pallas_call x13 -> x14, Pallas kernels: 27.4 us -> 28 us  [call(): pl.pallas_call(kernel, out_shape=[jax.ShapeDtypeStruct(o.shape, o.dtype)...]
    ppermute x15 -> x16, waiting for transfers between devices: 19 us -> 18.7 us  [exchanged(): lax.ppermute(value, axis, [(source, source ^ step) for source in range(co...]
    unnamed x36 -> x44, local copies, waits for them, and re-layouts: 1.96 us -> 1.97 us
  transfers between devices with their start and end apart: 21 -> 22, of which waited for: 8 -> 10; matrix products, arithmetic and copies ran while one was open for 1% -> 0% of each run, Pallas kernels for 23% -> 25%
where the time goes in v14:
time: 75.6 us; the launch traced here: 75.1 us
  Pallas kernels  28 us (37%)
  starting transfers between devices  23.6 us (31%)
  waiting for transfers between devices  19.8 us (26%)
  local copies, waits for them, and re-layouts  1.99 us (3%)
  between operations  1.66 us (2%)
    pallas_call x14, Pallas kernels, call(): pl.pallas_call(kernel, out_shape=[jax.ShapeDtypeStruct(o.shape, o.dtype)...  28 us
    ppermute x16, waiting for transfers between devices, exchanged(): lax.ppermute(value, axis, [(source, source ^ step) for source in range(co...  18.7 us
    ppermute x16, starting transfers between devices, exchanged(): lax.ppermute(value, axis, [(source, source ^ step) for source in range(co...  14.9 us
    ppermute x6, starting transfers between devices, shifted(): return lax.ppermute(value, axis, pairs)  8.67 us
    unnamed x44, local copies, waits for them, and re-layouts  1.97 us
  transfers between devices with their start and end apart: 22, of which 10 were waited for; matrix products, arithmetic and copies ran while one was open for 0% of the time, Pallas kernels for 25%

profile of v14, /device:TPU:0, one launch (start us, length us, event | category | flops | bytes accessed | tf_op | source)
XLA Modules:
  0.0 75.1 jit_solution(18106414878620813655)
XLA Ops:
  0.6 1.6 %shard_map.185 = (bf16[576,128]{1,0:T(8,128)(2,1)}, bf16[16,384]{1,0:T(8,128)(2,1)}) custom-call(bf16[512,128]{1,0:T(8,128)(2,1)} %latent.7, f32[3,512]{1,0:T(4,128)} %positions.1, f32[3,128]{1,0:T(4,128)} %pos_weight.1), custom_call_target="tpu_custom_call" | custom-call | bytes 298496 | tf_op jit(solution)/shard_map/pallas_call | solution.py:44
  2.2 0.5 collective-permute-start
  2.7 2.9 %collective-permute-start.1 = (bf16[576,128]{1,0:T(8,128)(2,1)}, bf16[576,128]{1,0:T(8,128)(2,1)S(1)}, u32[]{:S(2)}, u32[]{:S(2)}) collective-permute-start(bf16[576,128]{1,0:T(8,128)(2,1)} %get-tuple-element.54.message.refs_3_), channel_id=1, source_target_pairs={{0,28},{4,0},{8,4},{12,8},{16,12},{20,16},{24,20},{28,24},{1,29},{... | collective-permute-start | bytes 442376 | tf_op jit(solution)/shard_map/ppermute | solution.py:22
  5.6 2.3 %collective-permute-start.2 = (bf16[576,128]{1,0:T(8,128)(2,1)}, bf16[576,128]{1,0:T(8,128)(2,1)S(1)}, u32[]{:S(2)}, u32[]{:S(2)}) collective-permute-start(bf16[576,128]{1,0:T(8,128)(2,1)} %get-tuple-element.54.message.refs_3_), channel_id=1, source_target_pairs={{0,1},{1,0},{2,3},{3,2},{4,5},{5,4},{6,7},{7,6},{8,9},{9,8},{10,11... | collective-permute-start | bytes 442376 | tf_op jit(solution)/shard_map/ppermute | solution.py:569
  7.9 2.6 %collective-permute-start.3 = (bf16[576,128]{1,0:T(8,128)(2,1)}, bf16[576,128]{1,0:T(8,128)(2,1)S(1)}, u32[]{:S(2)}, u32[]{:S(2)}) collective-permute-start(bf16[576,128]{1,0:T(8,128)(2,1)} %get-tuple-element.54.message.refs_3_), channel_id=1, source_target_pairs={{0,2},{1,3},{2,0},{3,1},{4,6},{5,7},{6,4},{7,5},{8,10},{9,11},{10,... | collective-permute-start | bytes 442376 | tf_op jit(solution)/shard_map/ppermute | solution.py:569
  11.2 0.0 copy-start.12
  11.2 0.0 copy-start.10
  11.2 0.0 copy-start.11
  11.2 0.6 copy-done.12
  11.8 0.0 copy-done.13
  11.8 0.0 copy-done.9
  11.8 0.0 copy-done.10
  11.9 0.0 copy-done.11
  11.9 1.2 %copy-done.1 = s32[1,1,16,128,128]{4,3,2,1,0:T(8,128)S(1)} copy-done((s32[1,1,16,128,128]{4,3,2,1,0:T(8,128)S(1)}, s32[1,1,16,128,128]{4,3,2,1,0:T(8,128)}, u32[]{:S(2)}) %copy-start.1) | copy-done | bytes 1048600
  13.1 1.0 %shard_map.184 = (bf16[17,128,128]{2,1,0:T(8,128)(2,1)S(1)}, bf16[17,128,128]{2,1,0:T(8,128)(2,1)S(1)}, bf16[17,128,128]{2,1,0:T(8,128)(2,1)S(1)}, s32[8,128]{1,0:T(8,128)S(1)}, f32[8,128]{1,0:T(8,128)S(1)}) custom-call(s32[1,1]{1,0:T(1,128)S(6)} %copy.20.tile_count, s32[16,128,128]{2,1,0:T(8,128)S(1)} %bitcast.5, s32[1,1,16]{2,1,0:T(1,128)S(1)} %copy-done.9, ...), custom_call_target="tpu_custom_call" | custom-call | flops 268435456 | bytes 2729600 | tf_op jit(solution)/shard_map/pallas_call | solution.py:44
  14.1 2.8 %shard_map.186 = (bf16[4,128,128]{2,1,0:T(8,128)(2,1)S(1)}, bf16[12,128,128]{2,1,0:T(8,128)(2,1)S(1)}, f32[4,128,128]{2,1,0:T(8,128)S(1)}, f32[4,128,128]{2,1,0:...) custom-call(s32[1,1]{1,0:T(1,128)S(6)} %copy.20.tile_count, s32[8,128]{1,0:T(8,128)S(1)} %get-tuple-element.50.most, ...), custom_call_target="tpu_custom_call" | custom-call | flops 1073741824 | bytes 3739648 | tf_op jit(solution)/shard_map/pallas_call | solution.py:44
  16.9 4.5 %collective-permute-done.3.refs_4_.refs_5_ = bf16[576,128]{1,0:T(8,128)(2,1)S(1)} collective-permute-done((bf16[576,128]{1,0:T(8,128)(2,1)}, bf16[576,128]{1,0:T(8,128)(2,1)S(1)}, u32[]{:S(2)}, u32[]{:S(2)}) %collective-permute-start.3) | collective-permute-done | bytes 147488 | tf_op jit(solution)/shard_map/ppermute | solution.py:569
  21.4 4.9 %shard_map.187 = (bf16[512,128]{1,0:T(8,128)(2,1)S(1)}, bf16[512,128]{1,0:T(8,128)(2,1)S(1)}, bf16[512,128]{1,0:T(8,128)(2,1)S(1)}, bf16[512,128]{1,0:T(8,128)(2,1)S(1)}, bf16[16,128,128]{2,1,0:T(8,128)(2,1)S(1)}) custom-call(s32[1,1]{1,0:T(1,128)S(6)} %copy.20.tile_count, s32[8,128]{1,0:T(8,128)S(1)} %get-tuple-element.50.most, ...), custom_call_target="tpu_custom_call" | custom-call | flops 2147483648 | bytes 4227072 | tf_op jit(solution)/shard_map/pallas_call | solution.py:44
  26.4 0.1 collective-permute-start.5
  26.5 2.6 %collective-permute-start.6 = (bf16[512,128]{1,0:T(8,128)(2,1)S(1)}, bf16[512,128]{1,0:T(8,128)(2,1)S(1)}, u32[]{:S(2)}, u32[]{:S(2)}) collective-permute-start(bf16[512,128]{1,0:T(8,128)(2,1)S(1)} %get-tuple-element.64), channel_id=1, source_target_pairs={{0,28},{4,0},{8,4},{12,8},{16,12},{20,16},{24,20},{28,24},{1,29},{... | collective-permute-start | bytes 393224 | tf_op jit(solution)/shard_map/ppermute | solution.py:22
  29.1 3.5 %shard_map.188 = (f32[512,128]{1,0:T(8,128)S(1)}, f32[512,128]{1,0:T(8,128)S(1)}) custom-call(s32[1,1]{1,0:T(1,128)S(6)} %copy.20.tile_count, s32[8,128]{1,0:T(8,128)S(1)} %get-tuple-element.50.most, bf16[17,128,128]{2,1,0:T(8,128)(2,1)S(1)} %get-tuple-element.51.row_rank, bf16[17,128,128]{2,1,0:T(8,128)(2,1)S(1)} %get-tuple-element.52.row_degree, ...), custom_call_target="tpu_custom_call" | custom-call | flops 1073741824 | bytes 3084288 | tf_op jit(solution)/shard_map/pallas_call | solution.py:44
  32.8 1.8 %shard_map.189 = (bf16[512,128]{1,0:T(8,128)(2,1)}, bf16[1024,128]{1,0:T(8,128)(2,1)S(1)}, bf16[1024,128]{1,0:T(8,128)(2,1)}, bf16[512,128]{1,0:T(8,128)(2,1)S(1...) custom-call(f32[8,128]{1,0:T(8,128)S(1)} %get-tuple-element.49.vecto, ...), custom_call_target="tpu_custom_call" | custom-call | flops 117440512 | bytes 2625536 | tf_op jit(solution)/shard_map/pallas_call | solution.py:44
  34.6 2.6 %collective-permute-start.9 = (bf16[1024,128]{1,0:T(8,128)(2,1)S(1)}, bf16[1024,128]{1,0:T(8,128)(2,1)S(1)}, u32[]{:S(2)}, u32[]{:S(2)}) collective-permute-start(bf16[1024,128]{1,0:T(8,128)(2,1)S(1)} %get-tuple-element.77.refs_0_), channel_id=1, source_target_pairs={{0,28},{4,0},{8,4},{12,8},{16,12},{20,16},{24,20},{28,24},{1,29},{... | collective-permute-start | bytes 786440 | tf_op jit(solution)/shard_map/ppermute | solution.py:22
  37.2 1.0 %shard_map.190 = (f32[256,128]{1,0:T(8,128)S(1)}, bf16[256,128]{1,0:T(8,128)(2,1)}) custom-call(bf16[512,128]{1,0:T(8,128)(2,1)S(1)} %copy-done, bf16[512,128]{1,0:T(8,128)(2,1)S(1)} %get-tuple-element.68.aggregate, bf16[512,128]{1,0:T(8,128)(2,1)S(1)} %get-tuple-element.69.message, bf16[512,128]{1,0:T(8,128)(2,1)S(1)} %get-tuple-element.70.hidden, ...), custom_call_target="tpu_custom_call" | custom-call | flops 67108864 | bytes 1114112 | tf_op jit(solution)/shard_map/pallas_call | solution.py:44
  38.3 3.5 %shard_map.192.refs_2_ = f32[16,128,128]{2,1,0:T(8,128)S(1)} custom-call(s32[1,1]{1,0:T(1,128)S(6)} %copy.20.tile_count, s32[8,128]{1,0:T(8,128)S(1)} %get-tuple-element.50.most, bf16[17,128,128]{2,1,0:T(8,128)(2,1)S(1)} %get-tuple-element.81.col_rank, bf16[16,128,128]{2,1,0:T(8,128)(2,1)S(1)} %get-tuple-element.61.refs_0_.senders, ...), custom_call_target="tpu_custom_call" | custom-call | flops 134217728 | bytes 2789376 | tf_op jit(solution)/shard_map/pallas_call | solution.py:44
  41.8 0.9 %collective-permute-done.7.arrived = bf16[256,128]{1,0:T(8,128)(2,1)S(1)} collective-permute-done((bf16[256,128]{1,0:T(8,128)(2,1)}, bf16[256,128]{1,0:T(8,128)(2,1)S(1)}, u32[]{:S(2)}, u32[]{:S(2)}) %collective-permute-start.7) | collective-permute-done | bytes 65568 | tf_op jit(solution)/shard_map/ppermute | solution.py:569
  42.7 1.1 %collective-permute-done.8.refs_0_.from_low = bf16[1024,128]{1,0:T(8,128)(2,1)S(1)} collective-permute-done((bf16[1024,128]{1,0:T(8,128)(2,1)}, bf16[1024,128]{1,0:T(8,128)(2,1)S(1)}, u32[]{:S(2)}, u32[]{:S(2)}) %collective-permute-start.8) | collective-permute-done | bytes 262176 | tf_op jit(solution)/shard_map/ppermute | solution.py:22
  43.9 1.8 %collective-permute-start.10 = (bf16[128,128]{1,0:T(8,128)(2,1)S(1)}, bf16[128,128]{1,0:T(8,128)(2,1)S(1)}, u32[]{:S(2)}, u32[]{:S(2)}) collective-permute-start(bf16[128,128]{1,0:T(8,128)(2,1)S(1)} %get-tuple-element.80), channel_id=1, source_target_pairs={{0,2},{1,3},{2,0},{3,1},{4,6},{5,7},{6,4},{7,5},{8,10},{9,11},{10,... | collective-permute-start | bytes 98312 | tf_op jit(solution)/shard_map/ppermute | solution.py:569
  45.7 5.7 %shard_map.193 = (f32[512,128]{1,0:T(8,128)S(1)}, bf16[512,128]{1,0:T(8,128)(2,1)S(1)}, bf16[512,128]{1,0:T(8,128)(2,1)S(1)}, bf16[512,128]{1,0:T(8,128)(2,1)S(1)}, bf16[128,128]{1,0:T(8,128)(2,1)S(1)}) custom-call(s32[1,1]{1,0:T(1,128)S(6)} %copy.20.tile_count, s32[8,128]{1,0:T(8,128)S(1)} %get-tuple-element.50.most, ...), custom_call_target="tpu_custom_call" | custom-call | flops 2147483648 | bytes 4329472 | tf_op jit(solution)/shard_map/pallas_call | solution.py:44
  51.3 0.4 shard_map.194
  51.8 0.1 collective-permute-start.11
  51.9 0.1 collective-permute-start.18
  52.0 1.1 %collective-permute-done.11 = bf16[192,128]{1,0:T(8,128)(2,1)S(1)} collective-permute-done((bf16[192,128]{1,0:T(8,128)(2,1)S(1)}, bf16[192,128]{1,0:T(8,128)(2,1)S(1)}, u32[]{:S(2)}, u32[]{:S(2)}) %collective-permute-start.11) | collective-permute-done | bytes 49184 | tf_op jit(solution)/shard_map/ppermute | solution.py:569
  53.1 0.9 %collective-permute-start.12 = (bf16[192,128]{1,0:T(8,128)(2,1)S(1)}, bf16[192,128]{1,0:T(8,128)(2,1)S(1)}, u32[]{:S(2)}, u32[]{:S(2)}) collective-permute-start(bf16[192,128]{1,0:T(8,128)(2,1)S(1)} %add_convert_fusion.1.refs_0_), channel_id=1, source_target_pairs={{0,1},{1,0},{2,3},{3,2},{4,5},{5,4},{6,7},{7,6},{8,9},{9,8},{10,11... | collective-permute-start | bytes 147464 | tf_op jit(solution)/shard_map/ppermute | solution.py:569
  54.1 3.5 %collective-permute-start.14 = (bf16[192,128]{1,0:T(8,128)(2,1)S(1)}, bf16[192,128]{1,0:T(8,128)(2,1)S(1)}, u32[]{:S(2)}, u32[]{:S(2)}) collective-permute-start(bf16[192,128]{1,0:T(8,128)(2,1)S(1)} %add_convert_fusion.1.refs_0_), channel_id=1, source_target_pairs={{0,3},{1,2},{2,1},{3,0},{4,7},{5,6},{6,5},{7,4},{8,11},{9,10},{10,... | collective-permute-start | bytes 147464 | tf_op jit(solution)/shard_map/ppermute | solution.py:569
  57.6 2.6 %collective-permute-done.12.refs_1_ = bf16[192,128]{1,0:T(8,128)(2,1)S(1)} collective-permute-done((bf16[192,128]{1,0:T(8,128)(2,1)S(1)}, bf16[192,128]{1,0:T(8,128)(2,1)S(1)}, u32[]{:S(2)}, u32[]{:S(2)}) %collective-permute-start.12) | collective-permute-done | bytes 49184 | tf_op jit(solution)/shard_map/ppermute | solution.py:569
  60.2 5.3 %collective-permute-done.13.refs_2_ = bf16[192,128]{1,0:T(8,128)(2,1)S(1)} collective-permute-done((bf16[192,128]{1,0:T(8,128)(2,1)S(1)}, bf16[192,128]{1,0:T(8,128)(2,1)S(1)}, u32[]{:S(2)}, u32[]{:S(2)}) %collective-permute-start.13) | collective-permute-done | bytes 49184 | tf_op jit(solution)/shard_map/ppermute | solution.py:569
  65.5 0.1 collective-permute-start.17
  65.6 2.7 %collective-permute-start.16 = (bf16[384,128]{1,0:T(8,128)(2,1)S(1)}, bf16[384,128]{1,0:T(8,128)(2,1)S(1)}, u32[]{:S(2)}, u32[]{:S(2)}) collective-permute-start(bf16[384,128]{1,0:T(8,128)(2,1)S(1)} %shard_map.195), channel_id=1, source_target_pairs={{0,16},{4,20},{8,24},{12,28},{16,0},{20,4},{24,8},{28,12},{1,17},{... | collective-permute-start | bytes 294920 | tf_op jit(solution)/shard_map/ppermute | solution.py:569
  68.3 0.8 %collective-permute-start.15 = (bf16[384,128]{1,0:T(8,128)(2,1)S(1)}, bf16[384,128]{1,0:T(8,128)(2,1)S(1)}, u32[]{:S(2)}, u32[]{:S(2)}) collective-permute-start(bf16[384,128]{1,0:T(8,128)(2,1)S(1)} %shard_map.195), channel_id=1, source_target_pairs={{0,8},{4,12},{8,0},{12,4},{16,24},{20,28},{24,16},{28,20},{1,9},{5... | collective-permute-start | bytes 294920 | tf_op jit(solution)/shard_map/ppermute | solution.py:569
  69.1 1.7 %collective-permute-done.19.refs_1_ = bf16[512,128]{1,0:T(8,128)(2,1)S(1)} collective-permute-done((bf16[512,128]{1,0:T(8,128)(2,1)S(1)}, bf16[512,128]{1,0:T(8,128)(2,1)S(1)}, u32[]{:S(2)}, u32[]{:S(2)}) %collective-permute-start.19) | collective-permute-done | bytes 131104 | tf_op jit(solution)/shard_map/ppermute | solution.py:569
  70.8 0.9 %shard_map.196 = f32[512,128]{1,0:T(8,128)} custom-call(f32[512,128]{1,0:T(8,128)S(1)} %get-tuple-element.88.direct, bf16[128,128]{1,0:T(8,128)(2,1)S(1)} %copy-done.8, f32[512,128]{1,0:T(8,128)S(1)} %get-tuple-element.89.own, bf16[512,128]{1,0:T(8,128)(2,1)S(1)} %collective-permute-done.18.refs_0_, bf16[512,128]{1,0:T(8,128)(2,1)S(1)} %collective-permute-done.19.refs_1_, ...), custom_call_target="tpu_custom_call" | custom-call | flops 16777216 | bytes 1212416 | tf_op jit(solution)/shard_map/pallas_call | solution.py:44
  71.7 0.3 collective-permute-done.16
  72.0 1.0 %collective-permute-done.15 = bf16[384,128]{1,0:T(8,128)(2,1)S(1)} collective-permute-done((bf16[384,128]{1,0:T(8,128)(2,1)S(1)}, bf16[384,128]{1,0:T(8,128)(2,1)S(1)}, u32[]{:S(2)}, u32[]{:S(2)}) %collective-permute-start.15) | collective-permute-done | bytes 98336 | tf_op jit(solution)/shard_map/ppermute | solution.py:569
  72.9 0.1 add_convert_fusion.mine
  73.0 0.1 collective-permute-start.21
  73.1 1.3 %collective-permute-done.21.other = bf16[384,128]{1,0:T(8,128)(2,1)S(1)} collective-permute-done((bf16[384,128]{1,0:T(8,128)(2,1)S(1)}, bf16[384,128]{1,0:T(8,128)(2,1)S(1)}, u32[]{:S(2)}, u32[]{:S(2)}) %collective-permute-start.21) | collective-permute-done | bytes 98336 | tf_op jit(solution)/shard_map/ppermute | solution.py:569
  74.4 0.8 %shard_map.197 = f32[768,128]{1,0:T(8,128)} custom-call(bf16[384,128]{1,0:T(8,128)(2,1)S(1)} %add_convert_fusion.mine, bf16[384,128]{1,0:T(8,128)(2,1)S(1)} %collective-permute-done.21.other), custom_call_target="tpu_custom_call" | custom-call | bytes 589824 | tf_op jit(solution)/shard_map/pallas_call | solution.py:44
  (60 shorter events, 0.2 us)
Async XLA Ops:
  2.2 11.9 %collective-permute-start = (bf16[576,128]{1,0:T(8,128)(2,1)}, bf16[576,128]{1,0:T(8,128)(2,1)S(1)}, u32[]{:S(2)}, u32[]{:S(2)}) collective-permute-start(bf16[576,128]{1,0:T(8,128)(2,1)} %get-tuple-element.54.message.refs_3_), channel_id=1, source_target_pairs={{0,4},{4,8},{8,12},{12,16},{16,20},{20,24},{24,28},{28,0},{1,5},{5... | collective-permute-start | bytes 442376 | tf_op jit(solution)/shard_map/ppermute | solution.py:22
  2.7 11.4 %collective-permute-start.1 = (bf16[576,128]{1,0:T(8,128)(2,1)}, bf16[576,128]{1,0:T(8,128)(2,1)S(1)}, u32[]{:S(2)}, u32[]{:S(2)}) collective-permute-start(bf16[576,128]{1,0:T(8,128)(2,1)} %get-tuple-element.54.message.refs_3_), channel_id=1, source_target_pairs={{0,28},{4,0},{8,4},{12,8},{16,12},{20,16},{24,20},{28,24},{1,29},{... | collective-permute-start | bytes 442376 | tf_op jit(solution)/shard_map/ppermute | solution.py:22
  5.6 11.3 %collective-permute-start.2 = (bf16[576,128]{1,0:T(8,128)(2,1)}, bf16[576,128]{1,0:T(8,128)(2,1)S(1)}, u32[]{:S(2)}, u32[]{:S(2)}) collective-permute-start(bf16[576,128]{1,0:T(8,128)(2,1)} %get-tuple-element.54.message.refs_3_), channel_id=1, source_target_pairs={{0,1},{1,0},{2,3},{3,2},{4,5},{5,4},{6,7},{7,6},{8,9},{9,8},{10,11... | collective-permute-start | bytes 442376 | tf_op jit(solution)/shard_map/ppermute | solution.py:569
  7.9 13.5 %collective-permute-start.3 = (bf16[576,128]{1,0:T(8,128)(2,1)}, bf16[576,128]{1,0:T(8,128)(2,1)S(1)}, u32[]{:S(2)}, u32[]{:S(2)}) collective-permute-start(bf16[576,128]{1,0:T(8,128)(2,1)} %get-tuple-element.54.message.refs_3_), channel_id=1, source_target_pairs={{0,2},{1,3},{2,0},{3,1},{4,6},{5,7},{6,4},{7,5},{8,10},{9,11},{10,... | collective-permute-start | bytes 442376 | tf_op jit(solution)/shard_map/ppermute | solution.py:569
  10.5 10.9 %collective-permute-start.4 = (bf16[576,128]{1,0:T(8,128)(2,1)}, bf16[576,128]{1,0:T(8,128)(2,1)S(1)}, u32[]{:S(2)}, u32[]{:S(2)}) collective-permute-start(bf16[576,128]{1,0:T(8,128)(2,1)} %get-tuple-element.54.message.refs_3_), channel_id=1, source_target_pairs={{0,3},{1,2},{2,1},{3,0},{4,7},{5,6},{6,5},{7,4},{8,11},{9,10},{10,... | collective-permute-start | bytes 442376 | tf_op jit(solution)/shard_map/ppermute | solution.py:569
  11.2 0.7 copy-start.12
  11.2 0.7 copy-start.13
  11.2 0.7 copy-start.9
  11.2 0.7 copy-start.10
  11.2 0.7 copy-start.11
  11.9 1.2 %copy-start.1 = (s32[1,1,16,128,128]{4,3,2,1,0:T(8,128)S(1)}, s32[1,1,16,128,128]{4,3,2,1,0:T(8,128)}, u32[]{:S(2)}) copy-start(s32[1,1,16,128,128]{4,3,2,1,0:T(8,128)} %param.21) | copy-start | bytes 3145732
  13.1 1.0 %copy-start.7 = (bf16[128,128]{1,0:T(8,128)(2,1)S(1)}, bf16[128,128]{1,0:T(8,128)(2,1)}, u32[]{:S(2)}) copy-start(bf16[128,128]{1,0:T(8,128)(2,1)} %w_recv.3) | copy-start | bytes 98308
  13.1 1.0 %copy-start.8 = (bf16[128,128]{1,0:T(8,128)(2,1)S(1)}, bf16[128,128]{1,0:T(8,128)(2,1)}, u32[]{:S(2)}) copy-start(bf16[128,128]{1,0:T(8,128)(2,1)} %w_send.3) | copy-start | bytes 98308
  13.1 1.0 %copy-start.14 = (bf16[576,128]{1,0:T(8,128)(2,1)S(1)}, bf16[576,128]{1,0:T(8,128)(2,1)}, u32[]{:S(2)}) copy-start(bf16[576,128]{1,0:T(8,128)(2,1)} %get-tuple-element.54.message.refs_3_) | copy-start | bytes 442372
  13.1 1.0 %copy-start.21 = (bf16[16,384]{1,0:T(8,128)(2,1)S(1)}, bf16[16,384]{1,0:T(8,128)(2,1)}, u32[]{:S(2)}) copy-start(bf16[16,384]{1,0:T(8,128)(2,1)} %get-tuple-element.53.weight_parts.refs_2_) | copy-start | bytes 36868
  16.9 9.4 %copy-start.15 = (bf16[576,128]{1,0:T(8,128)(2,1)}, bf16[576,128]{1,0:T(8,128)(2,1)S(1)}, u32[]{:S(2)}) copy-start(bf16[576,128]{1,0:T(8,128)(2,1)S(1)} %collective-permute-done.2.refs_3_.refs_4_) | copy-start | bytes 442372
  21.4 5.0 %copy-start.17 = (bf16[576,128]{1,0:T(8,128)(2,1)}, bf16[576,128]{1,0:T(8,128)(2,1)S(1)}, u32[]{:S(2)}) copy-start(bf16[576,128]{1,0:T(8,128)(2,1)S(1)} %collective-permute-done.3.refs_4_.refs_5_) | copy-start | bytes 442372
  21.4 5.0 %copy-start.19 = (bf16[576,128]{1,0:T(8,128)(2,1)}, bf16[576,128]{1,0:T(8,128)(2,1)S(1)}, u32[]{:S(2)}) copy-start(bf16[576,128]{1,0:T(8,128)(2,1)S(1)} %collective-permute-done.4.refs_5_.refs_6_) | copy-start | bytes 442372
  26.4 6.3 %collective-permute-start.5 = (bf16[512,128]{1,0:T(8,128)(2,1)S(1)}, bf16[512,128]{1,0:T(8,128)(2,1)S(1)}, u32[]{:S(2)}, u32[]{:S(2)}) collective-permute-start(bf16[512,128]{1,0:T(8,128)(2,1)S(1)} %get-tuple-element.63), channel_id=1, source_target_pairs={{0,4},{4,8},{8,12},{12,16},{16,20},{20,24},{24,28},{28,0},{1,5},{5... | collective-permute-start | bytes 393224 | tf_op jit(solution)/shard_map/ppermute | solution.py:22
  26.5 6.2 %collective-permute-start.6 = (bf16[512,128]{1,0:T(8,128)(2,1)S(1)}, bf16[512,128]{1,0:T(8,128)(2,1)S(1)}, u32[]{:S(2)}, u32[]{:S(2)}) collective-permute-start(bf16[512,128]{1,0:T(8,128)(2,1)S(1)} %get-tuple-element.64), channel_id=1, source_target_pairs={{0,28},{4,0},{8,4},{12,8},{16,12},{20,16},{24,20},{28,24},{1,29},{... | collective-permute-start | bytes 393224 | tf_op jit(solution)/shard_map/ppermute | solution.py:22
  29.1 3.6 %copy-start = (bf16[512,128]{1,0:T(8,128)(2,1)S(1)}, bf16[512,128]{1,0:T(8,128)(2,1)}, u32[]{:S(2)}) copy-start(bf16[512,128]{1,0:T(8,128)(2,1)} %latent.7) | copy-start | bytes 393220
  29.1 3.6 %copy-start.2 = (bf16[512,128]{1,0:T(8,128)(2,1)S(1)}, bf16[512,128]{1,0:T(8,128)(2,1)}, u32[]{:S(2)}) copy-start(bf16[512,128]{1,0:T(8,128)(2,1)} %cotangent.3) | copy-start | bytes 393220
  29.1 3.6 %copy-start.3 = (bf16[128,128]{1,0:T(8,128)(2,1)S(1)}, bf16[128,128]{1,0:T(8,128)(2,1)}, u32[]{:S(2)}) copy-start(bf16[128,128]{1,0:T(8,128)(2,1)} %w_edge_out.3) | copy-start | bytes 98308
  29.1 3.6 %copy-start.4 = (bf16[128,128]{1,0:T(8,128)(2,1)S(1)}, bf16[128,128]{1,0:T(8,128)(2,1)}, u32[]{:S(2)}) copy-start(bf16[128,128]{1,0:T(8,128)(2,1)} %w_node_self.3) | copy-start | bytes 98308
  29.1 3.6 %copy-start.5 = (bf16[128,128]{1,0:T(8,128)(2,1)S(1)}, bf16[128,128]{1,0:T(8,128)(2,1)}, u32[]{:S(2)}) copy-start(bf16[128,128]{1,0:T(8,128)(2,1)} %w_node_msg.1) | copy-start | bytes 98308
  29.1 3.6 %copy-start.6 = (bf16[128,128]{1,0:T(8,128)(2,1)S(1)}, bf16[128,128]{1,0:T(8,128)(2,1)}, u32[]{:S(2)}) copy-start(bf16[128,128]{1,0:T(8,128)(2,1)} %w_node_out.1) | copy-start | bytes 98308
  34.6 9.2 %collective-permute-start.8 = (bf16[1024,128]{1,0:T(8,128)(2,1)}, bf16[1024,128]{1,0:T(8,128)(2,1)S(1)}, u32[]{:S(2)}, u32[]{:S(2)}) collective-permute-start(bf16[1024,128]{1,0:T(8,128)(2,1)} %get-tuple-element.76), channel_id=1, source_target_pairs={{0,4},{4,8},{8,12},{12,16},{16,20},{20,24},{24,28},{28,0},{1,5},{5... | collective-permute-start | bytes 786440 | tf_op jit(solution)/shard_map/ppermute | solution.py:22
  34.6 9.2 %collective-permute-start.9 = (bf16[1024,128]{1,0:T(8,128)(2,1)S(1)}, bf16[1024,128]{1,0:T(8,128)(2,1)S(1)}, u32[]{:S(2)}, u32[]{:S(2)}) collective-permute-start(bf16[1024,128]{1,0:T(8,128)(2,1)S(1)} %get-tuple-element.77.refs_0_), channel_id=1, source_target_pairs={{0,28},{4,0},{8,4},{12,8},{16,12},{20,16},{24,20},{28,24},{1,29},{... | collective-permute-start | bytes 786440 | tf_op jit(solution)/shard_map/ppermute | solution.py:22
  38.3 4.5 %collective-permute-start.7 = (bf16[256,128]{1,0:T(8,128)(2,1)}, bf16[256,128]{1,0:T(8,128)(2,1)S(1)}, u32[]{:S(2)}, u32[]{:S(2)}) collective-permute-start(bf16[256,128]{1,0:T(8,128)(2,1)} %get-tuple-element.75), channel_id=1, source_target_pairs={{0,1},{1,0},{2,3},{3,2},{4,5},{5,4},{6,7},{7,6},{8,9},{9,8},{10,11... | collective-permute-start | bytes 196616 | tf_op jit(solution)/shard_map/ppermute | solution.py:569
  38.3 7.4 %copy-start.18 = (bf16[576,128]{1,0:T(8,128)(2,1)S(1)}, bf16[576,128]{1,0:T(8,128)(2,1)}, u32[]{:S(2)}) copy-start(bf16[576,128]{1,0:T(8,128)(2,1)} %copy-done.17) | copy-start | bytes 442372
  38.3 7.4 %copy-start.20 = (bf16[576,128]{1,0:T(8,128)(2,1)S(1)}, bf16[576,128]{1,0:T(8,128)(2,1)}, u32[]{:S(2)}) copy-start(bf16[576,128]{1,0:T(8,128)(2,1)} %copy-done.19) | copy-start | bytes 442372
  41.8 3.8 %copy-start.16 = (bf16[576,128]{1,0:T(8,128)(2,1)S(1)}, bf16[576,128]{1,0:T(8,128)(2,1)}, u32[]{:S(2)}) copy-start(bf16[576,128]{1,0:T(8,128)(2,1)} %copy-done.15) | copy-start | bytes 442372
  43.9 7.9 %collective-permute-start.10 = (bf16[128,128]{1,0:T(8,128)(2,1)S(1)}, bf16[128,128]{1,0:T(8,128)(2,1)S(1)}, u32[]{:S(2)}, u32[]{:S(2)}) collective-permute-start(bf16[128,128]{1,0:T(8,128)(2,1)S(1)} %get-tuple-element.80), channel_id=1, source_target_pairs={{0,2},{1,3},{2,0},{3,1},{4,6},{5,7},{6,4},{7,5},{8,10},{9,11},{10,... | collective-permute-start | bytes 98312 | tf_op jit(solution)/shard_map/ppermute | solution.py:569
  51.8 1.3 %collective-permute-start.11 = (bf16[192,128]{1,0:T(8,128)(2,1)S(1)}, bf16[192,128]{1,0:T(8,128)(2,1)S(1)}, u32[]{:S(2)}, u32[]{:S(2)}) collective-permute-start(bf16[192,128]{1,0:T(8,128)(2,1)S(1)} %broadcast_select_fusion), channel_id=1, source_target_pairs={{0,4},{4,0},{8,12},{12,8},{16,20},{20,16},{24,28},{28,24},{1,5},{5... | collective-permute-start | bytes 147464 | tf_op jit(solution)/shard_map/ppermute | solution.py:569
  51.9 16.4 %collective-permute-start.18 = (bf16[512,128]{1,0:T(8,128)(2,1)S(1)}, bf16[512,128]{1,0:T(8,128)(2,1)S(1)}, u32[]{:S(2)}, u32[]{:S(2)}) collective-permute-start(bf16[512,128]{1,0:T(8,128)(2,1)S(1)} %get-tuple-element.90), channel_id=1, source_target_pairs={{0,1},{1,0},{2,3},{3,2},{4,5},{5,4},{6,7},{7,6},{8,9},{9,8},{10,11... | collective-permute-start | bytes 393224 | tf_op jit(solution)/shard_map/ppermute | solution.py:569
  53.1 7.1 %collective-permute-start.12 = (bf16[192,128]{1,0:T(8,128)(2,1)S(1)}, bf16[192,128]{1,0:T(8,128)(2,1)S(1)}, u32[]{:S(2)}, u32[]{:S(2)}) collective-permute-start(bf16[192,128]{1,0:T(8,128)(2,1)S(1)} %add_convert_fusion.1.refs_0_), channel_id=1, source_target_pairs={{0,1},{1,0},{2,3},{3,2},{4,5},{5,4},{6,7},{7,6},{8,9},{9,8},{10,11... | collective-permute-start | bytes 147464 | tf_op jit(solution)/shard_map/ppermute | solution.py:569
  54.1 11.4 %collective-permute-start.13 = (bf16[192,128]{1,0:T(8,128)(2,1)S(1)}, bf16[192,128]{1,0:T(8,128)(2,1)S(1)}, u32[]{:S(2)}, u32[]{:S(2)}) collective-permute-start(bf16[192,128]{1,0:T(8,128)(2,1)S(1)} %add_convert_fusion.1.refs_0_), channel_id=1, source_target_pairs={{0,2},{1,3},{2,0},{3,1},{4,6},{5,7},{6,4},{7,5},{8,10},{9,11},{10,... | collective-permute-start | bytes 147464 | tf_op jit(solution)/shard_map/ppermute | solution.py:569
  54.1 11.4 %collective-permute-start.14 = (bf16[192,128]{1,0:T(8,128)(2,1)S(1)}, bf16[192,128]{1,0:T(8,128)(2,1)S(1)}, u32[]{:S(2)}, u32[]{:S(2)}) collective-permute-start(bf16[192,128]{1,0:T(8,128)(2,1)S(1)} %add_convert_fusion.1.refs_0_), channel_id=1, source_target_pairs={{0,3},{1,2},{2,1},{3,0},{4,7},{5,6},{6,5},{7,4},{8,11},{9,10},{10,... | collective-permute-start | bytes 147464 | tf_op jit(solution)/shard_map/ppermute | solution.py:569
  57.6 13.2 %collective-permute-start.19 = (bf16[512,128]{1,0:T(8,128)(2,1)S(1)}, bf16[512,128]{1,0:T(8,128)(2,1)S(1)}, u32[]{:S(2)}, u32[]{:S(2)}) collective-permute-start(bf16[512,128]{1,0:T(8,128)(2,1)S(1)} %get-tuple-element.91), channel_id=1, source_target_pairs={{0,2},{1,3},{2,0},{3,1},{4,6},{5,7},{6,4},{7,5},{8,10},{9,11},{10,... | collective-permute-start | bytes 393224 | tf_op jit(solution)/shard_map/ppermute | solution.py:569
  60.2 10.6 %collective-permute-start.20 = (bf16[512,128]{1,0:T(8,128)(2,1)S(1)}, bf16[512,128]{1,0:T(8,128)(2,1)S(1)}, u32[]{:S(2)}, u32[]{:S(2)}) collective-permute-start(bf16[512,128]{1,0:T(8,128)(2,1)S(1)} %get-tuple-element.92), channel_id=1, source_target_pairs={{0,3},{1,2},{2,1},{3,0},{4,7},{5,6},{6,5},{7,4},{8,11},{9,10},{10,... | collective-permute-start | bytes 393224 | tf_op jit(solution)/shard_map/ppermute | solution.py:569
  65.5 6.1 %collective-permute-start.17 = (bf16[384,128]{1,0:T(8,128)(2,1)S(1)}, bf16[384,128]{1,0:T(8,128)(2,1)S(1)}, u32[]{:S(2)}, u32[]{:S(2)}) collective-permute-start(bf16[384,128]{1,0:T(8,128)(2,1)S(1)} %shard_map.195), channel_id=1, source_target_pairs={{0,24},{4,28},{8,16},{12,20},{16,8},{20,12},{24,0},{28,4},{1,25},{... | collective-permute-start | bytes 294920 | tf_op jit(solution)/shard_map/ppermute | solution.py:569
  65.6 6.3 %collective-permute-start.16 = (bf16[384,128]{1,0:T(8,128)(2,1)S(1)}, bf16[384,128]{1,0:T(8,128)(2,1)S(1)}, u32[]{:S(2)}, u32[]{:S(2)}) collective-permute-start(bf16[384,128]{1,0:T(8,128)(2,1)S(1)} %shard_map.195), channel_id=1, source_target_pairs={{0,16},{4,20},{8,24},{12,28},{16,0},{20,4},{24,8},{28,12},{1,17},{... | collective-permute-start | bytes 294920 | tf_op jit(solution)/shard_map/ppermute | solution.py:569
  68.3 4.6 %collective-permute-start.15 = (bf16[384,128]{1,0:T(8,128)(2,1)S(1)}, bf16[384,128]{1,0:T(8,128)(2,1)S(1)}, u32[]{:S(2)}, u32[]{:S(2)}) collective-permute-start(bf16[384,128]{1,0:T(8,128)(2,1)S(1)} %shard_map.195), channel_id=1, source_target_pairs={{0,8},{4,12},{8,0},{12,4},{16,24},{20,28},{24,16},{28,20},{1,9},{5... | collective-permute-start | bytes 294920 | tf_op jit(solution)/shard_map/ppermute | solution.py:569
  73.0 1.4 %collective-permute-start.21 = (bf16[384,128]{1,0:T(8,128)(2,1)S(1)}, bf16[384,128]{1,0:T(8,128)(2,1)S(1)}, u32[]{:S(2)}, u32[]{:S(2)}) collective-permute-start(bf16[384,128]{1,0:T(8,128)(2,1)S(1)} %add_convert_fusion.mine), channel_id=1, source_target_pairs={{0,4},{4,0},{8,12},{12,8},{16,20},{20,16},{24,28},{28,24},{1,5},{5... | collective-permute-start | bytes 294920 | tf_op jit(solution)/shard_map/ppermute | solution.py:569

commit v15 on v14

--- a/solution.py
+++ b/solution.py
@@ -9,7 +9,7 @@
 BF16 = jnp.bfloat16
 FORWARD = (8, 8)
 BACKWARD = (16,)
-LOOPED = 4
+LOOPED = 2
 SENDERS, RECEIVERS, ROWS, COLUMNS = 0, 1, 2, 3
 TOGETHER = 4
 CHUNK = 32
@@ -497,7 +497,7 @@
         else:
             grad_parts, started, refs = (refs[0], None, refs[1]), refs[2], refs[3:]
             messages, refs = refs[:members], refs[members:]
-            grads_out, late_out, refs = refs[:members], refs[members], refs[members + 1 :]
+            own_out, stay_out, away_out, late_out, refs = *refs[:4], refs[4:]
             d_sums, grads = refs[0], refs[-1]
         totals, table, order, sem = refs[1:5]
         copy = pltpu.make_async_copy(most, table, sem)
@@ -553,12 +553,19 @@
         if own:
             return
         late = jnp.zeros((width, width), F32)
-        for distance, (message, out) in enumerate(zip(messages, grads_out)):
+        for distance, message in enumerate(messages):
             for block in range(blocks):
                 span = slice(block * size, (block + 1) * size)
                 found = grads[distance * blocks + block]
-                out[span, :] = found.astype(out.dtype)
                 late = late + contract_rows(message[span, :], found.astype(BF16))
+                if distance == 0:
+                    own_out[span, :] = found
+                elif distance % 2:
+                    start = distance // 2 * rows + block * size
+                    away_out[start : start + size, :] = found.astype(BF16)
+                else:
+                    start = (distance // 2 - 1) * rows + block * size
+                    stay_out[start : start + size, :] = found.astype(BF16)
         late_out[...] = late.astype(BF16)
 
     return kernel
@@ -573,7 +580,7 @@
     back, latent_grad = refs[:-1], refs[-1]
     d_send = own[...]
     for part in back:
-        d_send = d_send + part[...].astype(F32)
+        d_send = d_send + part[0 : own.shape[0], :].astype(F32)
     latent_grad[...] = direct[...] + dot_t(d_send.astype(BF16), w_send[...])
 
 
@@ -830,22 +837,22 @@
         ],
         flops=8 * own_rows * width * width,
     )
-    *send_grads, late = call(
+    apart = (members // 2) * own_rows
+    own_grad, stay, away, late = call(
         make_backward(members, blocks, False),
-        [node_float] + [node_like] * (members - 1) + [like((width, width), BF16)],
+        [
+            node_float,
+            like((apart - own_rows, width), BF16),
+            like((apart, width), BF16),
+            like((width, width), BF16),
+        ],
         [col_rank, senders, receivers, from_low, from_high, started, *messages],
         scalars=[tile_count],
         far=[most],
         scratch=back_scratch + [pltpu.VMEM((members * blocks, size, width), F32)],
         flops=tile_flops,
     )
-    back = [exchanged(send_grads[distance], "grp", distance) for distance in range(1, members)]
-    (latent_grad,) = call(
-        return_kernel,
-        [node_float],
-        [direct, w_send, send_grads[0], *back],
-        flops=2 * own_rows * width * width,
-    )
+    first = exchanged(away, "grp", 1)
     share = share + lax.optimization_barrier((arrived, late))[0].astype(F32)
     share = share.astype(BF16)
     chain = jnp.concatenate([share, late, recv_grad], 0)
@@ -862,6 +869,23 @@
         [like((members * rows + summed_rows, width), BF16)],
         all_parts(chain, "grp"),
         flops=members * chain.size,
+    )
+    chain, first = lax.optimization_barrier((chain, first))
+    back = [first]
+    stay = stay.astype(F32) + first[own_rows:].astype(F32)
+    step = 2
+    while step < members:
+        kept = [stay[start : start + own_rows] for start in range(0, stay.shape[0], own_rows)]
+        given = jnp.concatenate(kept[0::2], 0).astype(BF16)
+        back.append(exchanged(given, "grp", step))
+        if kept[1::2]:
+            stay = jnp.concatenate(kept[1::2], 0) + back[-1][own_rows:].astype(F32)
+        step *= 2
+    (latent_grad,) = call(
+        return_kernel,
+        [node_float],
+        [direct, w_send, own_grad, *back],
+        flops=2 * own_rows * width * width,
     )
     if paired:
         chain = tree_sum([part.astype(F32) for part in all_parts(chain, "blk", 2)]).astype(BF16)

time: 75.6 us -> 79.3 us (1.049)
  waiting for transfers between devices: 19.8 us -> 24.1 us
  Pallas kernels: 28 us -> 26.7 us
  starting transfers between devices: 23.6 us -> 24.8 us
    ppermute x16 -> x15, waiting for transfers between devices: 18.7 us -> 22.9 us  [exchanged(): lax.ppermute(value, axis, [(source, source ^ step) for source in range(co...]
    pallas_call x14, Pallas kernels: 28 us -> 26.7 us  [call(): pl.pallas_call(kernel, out_shape=[jax.ShapeDtypeStruct(o.shape, o.dtype)...]
    ppermute x16 -> x15, starting transfers between devices: 14.9 us -> 16.2 us  [exchanged(): lax.ppermute(value, axis, [(source, source ^ step) for source in range(co...]
  transfers between devices with their start and end apart: 22 -> 21, of which waited for: 10 -> 9; matrix products, arithmetic and copies ran while one was open for 0% -> 0% of each run, Pallas kernels for 25% -> 20%
where the time goes in v15:
time: 79.3 us; the launch traced here: 79.5 us
  Pallas kernels  26.7 us (34%)
  starting transfers between devices  24.8 us (31%)
  waiting for transfers between devices  24.1 us (30%)
  local copies, waits for them, and re-layouts  1.99 us (3%)
  between operations  1.67 us (2%)
    pallas_call x14, Pallas kernels, call(): pl.pallas_call(kernel, out_shape=[jax.ShapeDtypeStruct(o.shape, o.dtype)...  26.7 us
    ppermute x15, waiting for transfers between devices, exchanged(): lax.ppermute(value, axis, [(source, source ^ step) for source in range(co...  22.9 us
    ppermute x15, starting transfers between devices, exchanged(): lax.ppermute(value, axis, [(source, source ^ step) for source in range(co...  16.2 us
    ppermute x6, starting transfers between devices, shifted(): return lax.ppermute(value, axis, pairs)  8.67 us
    unnamed x44, local copies, waits for them, and re-layouts  1.97 us
  transfers between devices with their start and end apart: 21, of which 9 were waited for; matrix products, arithmetic and copies ran while one was open for 0% of the time, Pallas kernels for 20%

profile of v15, /device:TPU:0, one launch (start us, length us, event | category | flops | bytes accessed | tf_op | source)
XLA Modules:
  0.0 79.5 jit_solution(501870275304652046)
XLA Ops:
  0.6 1.6 %shard_map.185 = (bf16[576,128]{1,0:T(8,128)(2,1)}, bf16[16,384]{1,0:T(8,128)(2,1)}) custom-call(bf16[512,128]{1,0:T(8,128)(2,1)} %latent.7, f32[3,512]{1,0:T(4,128)} %positions.1, f32[3,128]{1,0:T(4,128)} %pos_weight.1), custom_call_target="tpu_custom_call" | custom-call | bytes 298496 | tf_op jit(solution)/shard_map/pallas_call | solution.py:44
  2.2 0.5 collective-permute-start
  2.7 2.9 %collective-permute-start.1 = (bf16[576,128]{1,0:T(8,128)(2,1)}, bf16[576,128]{1,0:T(8,128)(2,1)S(1)}, u32[]{:S(2)}, u32[]{:S(2)}) collective-permute-start(bf16[576,128]{1,0:T(8,128)(2,1)} %get-tuple-element.55.message.refs_3_), channel_id=1, source_target_pairs={{0,28},{4,0},{8,4},{12,8},{16,12},{20,16},{24,20},{28,24},{1,29},{... | collective-permute-start | bytes 442376 | tf_op jit(solution)/shard_map/ppermute | solution.py:22
  5.6 2.3 %collective-permute-start.2 = (bf16[576,128]{1,0:T(8,128)(2,1)}, bf16[576,128]{1,0:T(8,128)(2,1)S(1)}, u32[]{:S(2)}, u32[]{:S(2)}) collective-permute-start(bf16[576,128]{1,0:T(8,128)(2,1)} %get-tuple-element.55.message.refs_3_), channel_id=1, source_target_pairs={{0,1},{1,0},{2,3},{3,2},{4,5},{5,4},{6,7},{7,6},{8,9},{9,8},{10,11... | collective-permute-start | bytes 442376 | tf_op jit(solution)/shard_map/ppermute | solution.py:576
  7.9 2.6 %collective-permute-start.3 = (bf16[576,128]{1,0:T(8,128)(2,1)}, bf16[576,128]{1,0:T(8,128)(2,1)S(1)}, u32[]{:S(2)}, u32[]{:S(2)}) collective-permute-start(bf16[576,128]{1,0:T(8,128)(2,1)} %get-tuple-element.55.message.refs_3_), channel_id=1, source_target_pairs={{0,2},{1,3},{2,0},{3,1},{4,6},{5,7},{6,4},{7,5},{8,10},{9,11},{10,... | collective-permute-start | bytes 442376 | tf_op jit(solution)/shard_map/ppermute | solution.py:576
  11.2 0.0 copy-start.9
  11.2 0.0 copy-start.10
  11.2 0.6 copy-done.12
  11.8 0.0 copy-done.13
  11.8 0.0 copy-done.9
  11.8 0.0 copy-done.10
  11.9 0.0 copy-done.11
  11.9 1.2 %copy-done.1 = s32[1,1,16,128,128]{4,3,2,1,0:T(8,128)S(1)} copy-done((s32[1,1,16,128,128]{4,3,2,1,0:T(8,128)S(1)}, s32[1,1,16,128,128]{4,3,2,1,0:T(8,128)}, u32[]{:S(2)}) %copy-start.1) | copy-done | bytes 1048600
  13.1 1.0 %shard_map.184 = (bf16[17,128,128]{2,1,0:T(8,128)(2,1)S(1)}, bf16[17,128,128]{2,1,0:T(8,128)(2,1)S(1)}, bf16[17,128,128]{2,1,0:T(8,128)(2,1)S(1)}, s32[8,128]{1,0:T(8,128)S(1)}, f32[8,128]{1,0:T(8,128)S(1)}) custom-call(s32[1,1]{1,0:T(1,128)S(6)} %copy.20.tile_count, s32[16,128,128]{2,1,0:T(8,128)S(1)} %bitcast.5, s32[1,1,16]{2,1,0:T(1,128)S(1)} %copy-done.9, ...), custom_call_target="tpu_custom_call" | custom-call | flops 268435456 | bytes 2729600 | tf_op jit(solution)/shard_map/pallas_call | solution.py:44
  14.1 1.9 %shard_map.186 = (bf16[4,128,128]{2,1,0:T(8,128)(2,1)S(1)}, bf16[12,128,128]{2,1,0:T(8,128)(2,1)S(1)}, f32[4,128,128]{2,1,0:T(8,128)S(1)}, f32[4,128,128]{2,1,0:...) custom-call(s32[1,1]{1,0:T(1,128)S(6)} %copy.20.tile_count, s32[8,128]{1,0:T(8,128)S(1)} %get-tuple-element.51.most, ...), custom_call_target="tpu_custom_call" | custom-call | flops 1073741824 | bytes 3739648 | tf_op jit(solution)/shard_map/pallas_call | solution.py:44
  16.1 0.0 copy-start.15
  16.1 5.3 %collective-permute-done.3.refs_4_.refs_5_ = bf16[576,128]{1,0:T(8,128)(2,1)S(1)} collective-permute-done((bf16[576,128]{1,0:T(8,128)(2,1)}, bf16[576,128]{1,0:T(8,128)(2,1)S(1)}, u32[]{:S(2)}, u32[]{:S(2)}) %collective-permute-start.3) | collective-permute-done | bytes 147488 | tf_op jit(solution)/shard_map/ppermute | solution.py:576
  21.4 5.7 %shard_map.187 = (bf16[512,128]{1,0:T(8,128)(2,1)S(1)}, bf16[512,128]{1,0:T(8,128)(2,1)S(1)}, bf16[512,128]{1,0:T(8,128)(2,1)S(1)}, bf16[512,128]{1,0:T(8,128)(2,1)S(1)}, bf16[16,128,128]{2,1,0:T(8,128)(2,1)S(1)}) custom-call(s32[1,1]{1,0:T(1,128)S(6)} %copy.20.tile_count, s32[8,128]{1,0:T(8,128)S(1)} %get-tuple-element.51.most, ...), custom_call_target="tpu_custom_call" | custom-call | flops 2147483648 | bytes 4227072 | tf_op jit(solution)/shard_map/pallas_call | solution.py:44
  27.2 0.1 collective-permute-start.5
  27.3 2.6 %collective-permute-start.6 = (bf16[512,128]{1,0:T(8,128)(2,1)S(1)}, bf16[512,128]{1,0:T(8,128)(2,1)S(1)}, u32[]{:S(2)}, u32[]{:S(2)}) collective-permute-start(bf16[512,128]{1,0:T(8,128)(2,1)S(1)} %get-tuple-element.65), channel_id=1, source_target_pairs={{0,28},{4,0},{8,4},{12,8},{16,12},{20,16},{24,20},{28,24},{1,29},{... | collective-permute-start | bytes 393224 | tf_op jit(solution)/shard_map/ppermute | solution.py:22
  29.9 2.7 %shard_map.188 = (f32[512,128]{1,0:T(8,128)S(1)}, f32[512,128]{1,0:T(8,128)S(1)}) custom-call(s32[1,1]{1,0:T(1,128)S(6)} %copy.20.tile_count, s32[8,128]{1,0:T(8,128)S(1)} %get-tuple-element.51.most, bf16[17,128,128]{2,1,0:T(8,128)(2,1)S(1)} %get-tuple-element.52.row_rank, bf16[17,128,128]{2,1,0:T(8,128)(2,1)S(1)} %get-tuple-element.53.row_degree, ...), custom_call_target="tpu_custom_call" | custom-call | flops 1073741824 | bytes 3084288 | tf_op jit(solution)/shard_map/pallas_call | solution.py:44
  32.7 1.8 %shard_map.189 = (bf16[512,128]{1,0:T(8,128)(2,1)}, bf16[1024,128]{1,0:T(8,128)(2,1)S(1)}, bf16[1024,128]{1,0:T(8,128)(2,1)}, bf16[512,128]{1,0:T(8,128)(2,1)S(1...) custom-call(f32[8,128]{1,0:T(8,128)S(1)} %get-tuple-element.50.vecto, ...), custom_call_target="tpu_custom_call" | custom-call | flops 117440512 | bytes 2625536 | tf_op jit(solution)/shard_map/pallas_call | solution.py:44
  34.5 0.0 collective-permute-start.8
  34.6 2.6 %collective-permute-start.9 = (bf16[1024,128]{1,0:T(8,128)(2,1)S(1)}, bf16[1024,128]{1,0:T(8,128)(2,1)S(1)}, u32[]{:S(2)}, u32[]{:S(2)}) collective-permute-start(bf16[1024,128]{1,0:T(8,128)(2,1)S(1)} %get-tuple-element.78.refs_0_), channel_id=1, source_target_pairs={{0,28},{4,0},{8,4},{12,8},{16,12},{20,16},{24,20},{28,24},{1,29},{... | collective-permute-start | bytes 786440 | tf_op jit(solution)/shard_map/ppermute | solution.py:22
  37.2 1.0 %shard_map.190 = (f32[256,128]{1,0:T(8,128)S(1)}, bf16[256,128]{1,0:T(8,128)(2,1)}) custom-call(bf16[512,128]{1,0:T(8,128)(2,1)S(1)} %copy-done, bf16[512,128]{1,0:T(8,128)(2,1)S(1)} %get-tuple-element.69.aggregate, bf16[512,128]{1,0:T(8,128)(2,1)S(1)} %get-tuple-element.70.message, bf16[512,128]{1,0:T(8,128)(2,1)S(1)} %get-tuple-element.71.hidden, ...), custom_call_target="tpu_custom_call" | custom-call | flops 67108864 | bytes 1114112 | tf_op jit(solution)/shard_map/pallas_call | solution.py:44
  38.2 2.7 %shard_map.192.refs_2_ = f32[16,128,128]{2,1,0:T(8,128)S(1)} custom-call(s32[1,1]{1,0:T(1,128)S(6)} %copy.20.tile_count, s32[8,128]{1,0:T(8,128)S(1)} %get-tuple-element.51.most, bf16[17,128,128]{2,1,0:T(8,128)(2,1)S(1)} %get-tuple-element.82.col_rank, bf16[16,128,128]{2,1,0:T(8,128)(2,1)S(1)} %get-tuple-element.62.refs_0_.senders, ...), custom_call_target="tpu_custom_call" | custom-call | flops 134217728 | bytes 2789376 | tf_op jit(solution)/shard_map/pallas_call | solution.py:44
  40.9 1.8 %collective-permute-done.7.arrived = bf16[256,128]{1,0:T(8,128)(2,1)S(1)} collective-permute-done((bf16[256,128]{1,0:T(8,128)(2,1)}, bf16[256,128]{1,0:T(8,128)(2,1)S(1)}, u32[]{:S(2)}, u32[]{:S(2)}) %collective-permute-start.7) | collective-permute-done | bytes 65568 | tf_op jit(solution)/shard_map/ppermute | solution.py:576
  42.7 1.3 %collective-permute-done.8.refs_0_.from_low = bf16[1024,128]{1,0:T(8,128)(2,1)S(1)} collective-permute-done((bf16[1024,128]{1,0:T(8,128)(2,1)}, bf16[1024,128]{1,0:T(8,128)(2,1)S(1)}, u32[]{:S(2)}, u32[]{:S(2)}) %collective-permute-start.8) | collective-permute-done | bytes 262176 | tf_op jit(solution)/shard_map/ppermute | solution.py:22
  44.0 2.7 %collective-permute-start.10 = (bf16[128,128]{1,0:T(8,128)(2,1)S(1)}, bf16[128,128]{1,0:T(8,128)(2,1)S(1)}, u32[]{:S(2)}, u32[]{:S(2)}) collective-permute-start(bf16[128,128]{1,0:T(8,128)(2,1)S(1)} %get-tuple-element.81), channel_id=1, source_target_pairs={{0,2},{1,3},{2,0},{3,1},{4,6},{5,7},{6,4},{7,5},{8,10},{9,11},{10,... | collective-permute-start | bytes 98312 | tf_op jit(solution)/shard_map/ppermute | solution.py:576
  46.7 6.2 %shard_map.193 = (f32[512,128]{1,0:T(8,128)S(1)}, bf16[512,128]{1,0:T(8,128)(2,1)S(1)}, bf16[1024,128]{1,0:T(8,128)(2,1)S(1)}, bf16[128,128]{1,0:T(8,128)(2,1)S(1)}) custom-call(s32[1,1]{1,0:T(1,128)S(6)} %copy.20.tile_count, s32[8,128]{1,0:T(8,128)S(1)} %get-tuple-element.51.most, bf16[17,128,128]{2,1,0:T(8,128)(2,1)S(1)} %get-tuple-element.82.col_rank, ...), custom_call_target="tpu_custom_call" | custom-call | flops 2147483648 | bytes 4329472 | tf_op jit(solution)/shard_map/pallas_call | solution.py:44
  52.9 0.4 shard_map.194
  53.3 0.1 collective-permute-start.11
  53.4 0.1 collective-permute-start.15
  53.5 1.1 %collective-permute-done.11 = bf16[192,128]{1,0:T(8,128)(2,1)S(1)} collective-permute-done((bf16[192,128]{1,0:T(8,128)(2,1)S(1)}, bf16[192,128]{1,0:T(8,128)(2,1)S(1)}, u32[]{:S(2)}, u32[]{:S(2)}) %collective-permute-start.11) | collective-permute-done | bytes 49184 | tf_op jit(solution)/shard_map/ppermute | solution.py:576
  54.7 0.9 %collective-permute-start.12 = (bf16[192,128]{1,0:T(8,128)(2,1)S(1)}, bf16[192,128]{1,0:T(8,128)(2,1)S(1)}, u32[]{:S(2)}, u32[]{:S(2)}) collective-permute-start(bf16[192,128]{1,0:T(8,128)(2,1)S(1)} %add_convert_fusion.2.refs_0_), channel_id=1, source_target_pairs={{0,1},{1,0},{2,3},{3,2},{4,5},{5,4},{6,7},{7,6},{8,9},{9,8},{10,11... | collective-permute-start | bytes 147464 | tf_op jit(solution)/shard_map/ppermute | solution.py:576
  55.6 3.5 %collective-permute-start.14 = (bf16[192,128]{1,0:T(8,128)(2,1)S(1)}, bf16[192,128]{1,0:T(8,128)(2,1)S(1)}, u32[]{:S(2)}, u32[]{:S(2)}) collective-permute-start(bf16[192,128]{1,0:T(8,128)(2,1)S(1)} %add_convert_fusion.2.refs_0_), channel_id=1, source_target_pairs={{0,3},{1,2},{2,1},{3,0},{4,7},{5,6},{6,5},{7,4},{8,11},{9,10},{10,... | collective-permute-start | bytes 147464 | tf_op jit(solution)/shard_map/ppermute | solution.py:576
  59.1 6.2 %collective-permute-done.12.refs_1_ = bf16[192,128]{1,0:T(8,128)(2,1)S(1)} collective-permute-done((bf16[192,128]{1,0:T(8,128)(2,1)S(1)}, bf16[192,128]{1,0:T(8,128)(2,1)S(1)}, u32[]{:S(2)}, u32[]{:S(2)}) %collective-permute-start.12) | collective-permute-done | bytes 49184 | tf_op jit(solution)/shard_map/ppermute | solution.py:576
  65.4 0.1 collective-permute-start.18
  65.4 0.1 collective-permute-start.17
  65.5 3.4 %collective-permute-start.16 = (bf16[384,128]{1,0:T(8,128)(2,1)S(1)}, bf16[384,128]{1,0:T(8,128)(2,1)S(1)}, u32[]{:S(2)}, u32[]{:S(2)}) collective-permute-start(bf16[384,128]{1,0:T(8,128)(2,1)S(1)} %shard_map.195), channel_id=1, source_target_pairs={{0,8},{4,12},{8,0},{12,4},{16,24},{20,28},{24,16},{28,20},{1,9},{5... | collective-permute-start | bytes 294920 | tf_op jit(solution)/shard_map/ppermute | solution.py:576
  68.9 0.4 collective-permute-start.19
  69.4 2.4 %collective-permute-done.18 = bf16[384,128]{1,0:T(8,128)(2,1)S(1)} collective-permute-done((bf16[384,128]{1,0:T(8,128)(2,1)S(1)}, bf16[384,128]{1,0:T(8,128)(2,1)S(1)}, u32[]{:S(2)}, u32[]{:S(2)}) %collective-permute-start.18) | collective-permute-done | bytes 98336 | tf_op jit(solution)/shard_map/ppermute | solution.py:576
  71.8 0.2 collective-permute-done.17
  72.0 0.1 add_convert_fusion.1.mine
  72.0 4.5 %collective-permute-done.19.refs_1_ = bf16[512,128]{1,0:T(8,128)(2,1)S(1)} collective-permute-done((bf16[512,128]{1,0:T(8,128)(2,1)S(1)}, bf16[512,128]{1,0:T(8,128)(2,1)S(1)}, u32[]{:S(2)}, u32[]{:S(2)}) %collective-permute-start.19) | collective-permute-done | bytes 131104 | tf_op jit(solution)/shard_map/ppermute | solution.py:576
  76.6 0.9 %shard_map.196 = f32[512,128]{1,0:T(8,128)} custom-call(f32[512,128]{1,0:T(8,128)S(1)} %get-tuple-element.91.direct, bf16[128,128]{1,0:T(8,128)(2,1)S(1)} %copy-done.8, f32[512,128]{1,0:T(8,128)S(1)} %get-tuple-element.92.own, bf16[1024,128]{1,0:T(8,128)(2,1)S(1)} %collective-permute-done.15.refs_0_, bf16[512,128]{1,0:T(8,128)(2,1)S(1)} %collective-permute-done.19.refs_1_), custom_call_target="tpu_custom_call" | custom-call | flops 16777216 | bytes 1212416 | tf_op jit(solution)/shard_map/pallas_call | solution.py:44
  77.5 1.3 %collective-permute-done.20.other = bf16[384,128]{1,0:T(8,128)(2,1)S(1)} collective-permute-done((bf16[384,128]{1,0:T(8,128)(2,1)S(1)}, bf16[384,128]{1,0:T(8,128)(2,1)S(1)}, u32[]{:S(2)}, u32[]{:S(2)}) %collective-permute-start.20) | collective-permute-done | bytes 98336 | tf_op jit(solution)/shard_map/ppermute | solution.py:576
  78.8 0.8 shard_map.197
  (59 shorter events, 0.3 us)
Async XLA Ops:
  2.2 11.9 %collective-permute-start = (bf16[576,128]{1,0:T(8,128)(2,1)}, bf16[576,128]{1,0:T(8,128)(2,1)S(1)}, u32[]{:S(2)}, u32[]{:S(2)}) collective-permute-start(bf16[576,128]{1,0:T(8,128)(2,1)} %get-tuple-element.55.message.refs_3_), channel_id=1, source_target_pairs={{0,4},{4,8},{8,12},{12,16},{16,20},{20,24},{24,28},{28,0},{1,5},{5... | collective-permute-start | bytes 442376 | tf_op jit(solution)/shard_map/ppermute | solution.py:22
  2.7 11.4 %collective-permute-start.1 = (bf16[576,128]{1,0:T(8,128)(2,1)}, bf16[576,128]{1,0:T(8,128)(2,1)S(1)}, u32[]{:S(2)}, u32[]{:S(2)}) collective-permute-start(bf16[576,128]{1,0:T(8,128)(2,1)} %get-tuple-element.55.message.refs_3_), channel_id=1, source_target_pairs={{0,28},{4,0},{8,4},{12,8},{16,12},{20,16},{24,20},{28,24},{1,29},{... | collective-permute-start | bytes 442376 | tf_op jit(solution)/shard_map/ppermute | solution.py:22
  5.6 10.5 %collective-permute-start.2 = (bf16[576,128]{1,0:T(8,128)(2,1)}, bf16[576,128]{1,0:T(8,128)(2,1)S(1)}, u32[]{:S(2)}, u32[]{:S(2)}) collective-permute-start(bf16[576,128]{1,0:T(8,128)(2,1)} %get-tuple-element.55.message.refs_3_), channel_id=1, source_target_pairs={{0,1},{1,0},{2,3},{3,2},{4,5},{5,4},{6,7},{7,6},{8,9},{9,8},{10,11... | collective-permute-start | bytes 442376 | tf_op jit(solution)/shard_map/ppermute | solution.py:576
  7.9 13.5 %collective-permute-start.3 = (bf16[576,128]{1,0:T(8,128)(2,1)}, bf16[576,128]{1,0:T(8,128)(2,1)S(1)}, u32[]{:S(2)}, u32[]{:S(2)}) collective-permute-start(bf16[576,128]{1,0:T(8,128)(2,1)} %get-tuple-element.55.message.refs_3_), channel_id=1, source_target_pairs={{0,2},{1,3},{2,0},{3,1},{4,6},{5,7},{6,4},{7,5},{8,10},{9,11},{10,... | collective-permute-start | bytes 442376 | tf_op jit(solution)/shard_map/ppermute | solution.py:576
  10.5 10.9 %collective-permute-start.4 = (bf16[576,128]{1,0:T(8,128)(2,1)}, bf16[576,128]{1,0:T(8,128)(2,1)S(1)}, u32[]{:S(2)}, u32[]{:S(2)}) collective-permute-start(bf16[576,128]{1,0:T(8,128)(2,1)} %get-tuple-element.55.message.refs_3_), channel_id=1, source_target_pairs={{0,3},{1,2},{2,1},{3,0},{4,7},{5,6},{6,5},{7,4},{8,11},{9,10},{10,... | collective-permute-start | bytes 442376 | tf_op jit(solution)/shard_map/ppermute | solution.py:576
  11.2 0.7 copy-start.12
  11.2 0.7 copy-start.13
  11.2 0.7 copy-start.9
  11.2 0.7 copy-start.10
  11.2 0.7 copy-start.11
  11.9 1.2 %copy-start.1 = (s32[1,1,16,128,128]{4,3,2,1,0:T(8,128)S(1)}, s32[1,1,16,128,128]{4,3,2,1,0:T(8,128)}, u32[]{:S(2)}) copy-start(s32[1,1,16,128,128]{4,3,2,1,0:T(8,128)} %param.21) | copy-start | bytes 3145732
  13.1 1.0 %copy-start.7 = (bf16[128,128]{1,0:T(8,128)(2,1)S(1)}, bf16[128,128]{1,0:T(8,128)(2,1)}, u32[]{:S(2)}) copy-start(bf16[128,128]{1,0:T(8,128)(2,1)} %w_recv.3) | copy-start | bytes 98308
  13.1 1.0 %copy-start.8 = (bf16[128,128]{1,0:T(8,128)(2,1)S(1)}, bf16[128,128]{1,0:T(8,128)(2,1)}, u32[]{:S(2)}) copy-start(bf16[128,128]{1,0:T(8,128)(2,1)} %w_send.3) | copy-start | bytes 98308
  13.1 1.0 %copy-start.14 = (bf16[576,128]{1,0:T(8,128)(2,1)S(1)}, bf16[576,128]{1,0:T(8,128)(2,1)}, u32[]{:S(2)}) copy-start(bf16[576,128]{1,0:T(8,128)(2,1)} %get-tuple-element.55.message.refs_3_) | copy-start | bytes 442372
  13.1 1.0 %copy-start.21 = (bf16[16,384]{1,0:T(8,128)(2,1)S(1)}, bf16[16,384]{1,0:T(8,128)(2,1)}, u32[]{:S(2)}) copy-start(bf16[16,384]{1,0:T(8,128)(2,1)} %get-tuple-element.54.weight_parts.refs_2_) | copy-start | bytes 36868
  16.1 11.1 %copy-start.15 = (bf16[576,128]{1,0:T(8,128)(2,1)}, bf16[576,128]{1,0:T(8,128)(2,1)S(1)}, u32[]{:S(2)}) copy-start(bf16[576,128]{1,0:T(8,128)(2,1)S(1)} %collective-permute-done.2.refs_3_.refs_4_) | copy-start | bytes 442372
  21.4 5.8 %copy-start.17 = (bf16[576,128]{1,0:T(8,128)(2,1)}, bf16[576,128]{1,0:T(8,128)(2,1)S(1)}, u32[]{:S(2)}) copy-start(bf16[576,128]{1,0:T(8,128)(2,1)S(1)} %collective-permute-done.3.refs_4_.refs_5_) | copy-start | bytes 442372
  21.4 5.8 %copy-start.19 = (bf16[576,128]{1,0:T(8,128)(2,1)}, bf16[576,128]{1,0:T(8,128)(2,1)S(1)}, u32[]{:S(2)}) copy-start(bf16[576,128]{1,0:T(8,128)(2,1)S(1)} %collective-permute-done.4.refs_5_.refs_6_) | copy-start | bytes 442372
  27.2 5.4 %collective-permute-start.5 = (bf16[512,128]{1,0:T(8,128)(2,1)S(1)}, bf16[512,128]{1,0:T(8,128)(2,1)S(1)}, u32[]{:S(2)}, u32[]{:S(2)}) collective-permute-start(bf16[512,128]{1,0:T(8,128)(2,1)S(1)} %get-tuple-element.64), channel_id=1, source_target_pairs={{0,4},{4,8},{8,12},{12,16},{16,20},{20,24},{24,28},{28,0},{1,5},{5... | collective-permute-start | bytes 393224 | tf_op jit(solution)/shard_map/ppermute | solution.py:22
  27.3 5.3 %collective-permute-start.6 = (bf16[512,128]{1,0:T(8,128)(2,1)S(1)}, bf16[512,128]{1,0:T(8,128)(2,1)S(1)}, u32[]{:S(2)}, u32[]{:S(2)}) collective-permute-start(bf16[512,128]{1,0:T(8,128)(2,1)S(1)} %get-tuple-element.65), channel_id=1, source_target_pairs={{0,28},{4,0},{8,4},{12,8},{16,12},{20,16},{24,20},{28,24},{1,29},{... | collective-permute-start | bytes 393224 | tf_op jit(solution)/shard_map/ppermute | solution.py:22
  29.9 2.7 %copy-start = (bf16[512,128]{1,0:T(8,128)(2,1)S(1)}, bf16[512,128]{1,0:T(8,128)(2,1)}, u32[]{:S(2)}) copy-start(bf16[512,128]{1,0:T(8,128)(2,1)} %latent.7) | copy-start | bytes 393220
  29.9 2.7 %copy-start.2 = (bf16[512,128]{1,0:T(8,128)(2,1)S(1)}, bf16[512,128]{1,0:T(8,128)(2,1)}, u32[]{:S(2)}) copy-start(bf16[512,128]{1,0:T(8,128)(2,1)} %cotangent.3) | copy-start | bytes 393220
  29.9 2.7 %copy-start.3 = (bf16[128,128]{1,0:T(8,128)(2,1)S(1)}, bf16[128,128]{1,0:T(8,128)(2,1)}, u32[]{:S(2)}) copy-start(bf16[128,128]{1,0:T(8,128)(2,1)} %w_edge_out.3) | copy-start | bytes 98308
  29.9 2.7 %copy-start.4 = (bf16[128,128]{1,0:T(8,128)(2,1)S(1)}, bf16[128,128]{1,0:T(8,128)(2,1)}, u32[]{:S(2)}) copy-start(bf16[128,128]{1,0:T(8,128)(2,1)} %w_node_self.3) | copy-start | bytes 98308
  29.9 2.8 %copy-start.5 = (bf16[128,128]{1,0:T(8,128)(2,1)S(1)}, bf16[128,128]{1,0:T(8,128)(2,1)}, u32[]{:S(2)}) copy-start(bf16[128,128]{1,0:T(8,128)(2,1)} %w_node_msg.1) | copy-start | bytes 98308
  29.9 2.7 %copy-start.6 = (bf16[128,128]{1,0:T(8,128)(2,1)S(1)}, bf16[128,128]{1,0:T(8,128)(2,1)}, u32[]{:S(2)}) copy-start(bf16[128,128]{1,0:T(8,128)(2,1)} %w_node_out.1) | copy-start | bytes 98308
  34.5 9.4 %collective-permute-start.8 = (bf16[1024,128]{1,0:T(8,128)(2,1)}, bf16[1024,128]{1,0:T(8,128)(2,1)S(1)}, u32[]{:S(2)}, u32[]{:S(2)}) collective-permute-start(bf16[1024,128]{1,0:T(8,128)(2,1)} %get-tuple-element.77), channel_id=1, source_target_pairs={{0,4},{4,8},{8,12},{12,16},{16,20},{20,24},{24,28},{28,0},{1,5},{5... | collective-permute-start | bytes 786440 | tf_op jit(solution)/shard_map/ppermute | solution.py:22
  34.6 9.4 %collective-permute-start.9 = (bf16[1024,128]{1,0:T(8,128)(2,1)S(1)}, bf16[1024,128]{1,0:T(8,128)(2,1)S(1)}, u32[]{:S(2)}, u32[]{:S(2)}) collective-permute-start(bf16[1024,128]{1,0:T(8,128)(2,1)S(1)} %get-tuple-element.78.refs_0_), channel_id=1, source_target_pairs={{0,28},{4,0},{8,4},{12,8},{16,12},{20,16},{24,20},{28,24},{1,29},{... | collective-permute-start | bytes 786440 | tf_op jit(solution)/shard_map/ppermute | solution.py:22
  38.2 4.5 %collective-permute-start.7 = (bf16[256,128]{1,0:T(8,128)(2,1)}, bf16[256,128]{1,0:T(8,128)(2,1)S(1)}, u32[]{:S(2)}, u32[]{:S(2)}) collective-permute-start(bf16[256,128]{1,0:T(8,128)(2,1)} %get-tuple-element.76), channel_id=1, source_target_pairs={{0,1},{1,0},{2,3},{3,2},{4,5},{5,4},{6,7},{7,6},{8,9},{9,8},{10,11... | collective-permute-start | bytes 196616 | tf_op jit(solution)/shard_map/ppermute | solution.py:576
  38.2 8.5 %copy-start.18 = (bf16[576,128]{1,0:T(8,128)(2,1)S(1)}, bf16[576,128]{1,0:T(8,128)(2,1)}, u32[]{:S(2)}) copy-start(bf16[576,128]{1,0:T(8,128)(2,1)} %copy-done.17) | copy-start | bytes 442372
  38.2 8.5 %copy-start.20 = (bf16[576,128]{1,0:T(8,128)(2,1)S(1)}, bf16[576,128]{1,0:T(8,128)(2,1)}, u32[]{:S(2)}) copy-start(bf16[576,128]{1,0:T(8,128)(2,1)} %copy-done.19) | copy-start | bytes 442372
  40.9 5.8 %copy-start.16 = (bf16[576,128]{1,0:T(8,128)(2,1)S(1)}, bf16[576,128]{1,0:T(8,128)(2,1)}, u32[]{:S(2)}) copy-start(bf16[576,128]{1,0:T(8,128)(2,1)} %copy-done.15) | copy-start | bytes 442372
  44.0 9.3 %collective-permute-start.10 = (bf16[128,128]{1,0:T(8,128)(2,1)S(1)}, bf16[128,128]{1,0:T(8,128)(2,1)S(1)}, u32[]{:S(2)}, u32[]{:S(2)}) collective-permute-start(bf16[128,128]{1,0:T(8,128)(2,1)S(1)} %get-tuple-element.81), channel_id=1, source_target_pairs={{0,2},{1,3},{2,0},{3,1},{4,6},{5,7},{6,4},{7,5},{8,10},{9,11},{10,... | collective-permute-start | bytes 98312 | tf_op jit(solution)/shard_map/ppermute | solution.py:576
  53.3 1.3 %collective-permute-start.11 = (bf16[192,128]{1,0:T(8,128)(2,1)S(1)}, bf16[192,128]{1,0:T(8,128)(2,1)S(1)}, u32[]{:S(2)}, u32[]{:S(2)}) collective-permute-start(bf16[192,128]{1,0:T(8,128)(2,1)S(1)} %broadcast_select_fusion), channel_id=1, source_target_pairs={{0,4},{4,0},{8,12},{12,8},{16,20},{20,16},{24,28},{28,24},{1,5},{5... | collective-permute-start | bytes 147464 | tf_op jit(solution)/shard_map/ppermute | solution.py:576
  53.4 11.9 %collective-permute-start.15 = (bf16[1024,128]{1,0:T(8,128)(2,1)S(1)}, bf16[1024,128]{1,0:T(8,128)(2,1)S(1)}, u32[]{:S(2)}, u32[]{:S(2)}) collective-permute-start(bf16[1024,128]{1,0:T(8,128)(2,1)S(1)} %get-tuple-element.89), channel_id=1, source_target_pairs={{0,1},{1,0},{2,3},{3,2},{4,5},{5,4},{6,7},{7,6},{8,9},{9,8},{10,11... | collective-permute-start | bytes 786440 | tf_op jit(solution)/shard_map/ppermute | solution.py:576
  54.7 10.6 %collective-permute-start.12 = (bf16[192,128]{1,0:T(8,128)(2,1)S(1)}, bf16[192,128]{1,0:T(8,128)(2,1)S(1)}, u32[]{:S(2)}, u32[]{:S(2)}) collective-permute-start(bf16[192,128]{1,0:T(8,128)(2,1)S(1)} %add_convert_fusion.2.refs_0_), channel_id=1, source_target_pairs={{0,1},{1,0},{2,3},{3,2},{4,5},{5,4},{6,7},{7,6},{8,9},{9,8},{10,11... | collective-permute-start | bytes 147464 | tf_op jit(solution)/shard_map/ppermute | solution.py:576
  55.6 9.7 %collective-permute-start.13 = (bf16[192,128]{1,0:T(8,128)(2,1)S(1)}, bf16[192,128]{1,0:T(8,128)(2,1)S(1)}, u32[]{:S(2)}, u32[]{:S(2)}) collective-permute-start(bf16[192,128]{1,0:T(8,128)(2,1)S(1)} %add_convert_fusion.2.refs_0_), channel_id=1, source_target_pairs={{0,2},{1,3},{2,0},{3,1},{4,6},{5,7},{6,4},{7,5},{8,10},{9,11},{10,... | collective-permute-start | bytes 147464 | tf_op jit(solution)/shard_map/ppermute | solution.py:576
  55.6 9.7 %collective-permute-start.14 = (bf16[192,128]{1,0:T(8,128)(2,1)S(1)}, bf16[192,128]{1,0:T(8,128)(2,1)S(1)}, u32[]{:S(2)}, u32[]{:S(2)}) collective-permute-start(bf16[192,128]{1,0:T(8,128)(2,1)S(1)} %add_convert_fusion.2.refs_0_), channel_id=1, source_target_pairs={{0,3},{1,2},{2,1},{3,0},{4,7},{5,6},{6,5},{7,4},{8,11},{9,10},{10,... | collective-permute-start | bytes 147464 | tf_op jit(solution)/shard_map/ppermute | solution.py:576
  65.4 6.5 %collective-permute-start.18 = (bf16[384,128]{1,0:T(8,128)(2,1)S(1)}, bf16[384,128]{1,0:T(8,128)(2,1)S(1)}, u32[]{:S(2)}, u32[]{:S(2)}) collective-permute-start(bf16[384,128]{1,0:T(8,128)(2,1)S(1)} %shard_map.195), channel_id=1, source_target_pairs={{0,24},{4,28},{8,16},{12,20},{16,8},{20,12},{24,0},{28,4},{1,25},{... | collective-permute-start | bytes 294920 | tf_op jit(solution)/shard_map/ppermute | solution.py:576
  65.4 6.5 %collective-permute-start.17 = (bf16[384,128]{1,0:T(8,128)(2,1)S(1)}, bf16[384,128]{1,0:T(8,128)(2,1)S(1)}, u32[]{:S(2)}, u32[]{:S(2)}) collective-permute-start(bf16[384,128]{1,0:T(8,128)(2,1)S(1)} %shard_map.195), channel_id=1, source_target_pairs={{0,16},{4,20},{8,24},{12,28},{16,0},{20,4},{24,8},{28,12},{1,17},{... | collective-permute-start | bytes 294920 | tf_op jit(solution)/shard_map/ppermute | solution.py:576
  65.5 6.5 %collective-permute-start.16 = (bf16[384,128]{1,0:T(8,128)(2,1)S(1)}, bf16[384,128]{1,0:T(8,128)(2,1)S(1)}, u32[]{:S(2)}, u32[]{:S(2)}) collective-permute-start(bf16[384,128]{1,0:T(8,128)(2,1)S(1)} %shard_map.195), channel_id=1, source_target_pairs={{0,8},{4,12},{8,0},{12,4},{16,24},{20,28},{24,16},{28,20},{1,9},{5... | collective-permute-start | bytes 294920 | tf_op jit(solution)/shard_map/ppermute | solution.py:576
  68.9 7.6 %collective-permute-start.19 = (bf16[512,128]{1,0:T(8,128)(2,1)S(1)}, bf16[512,128]{1,0:T(8,128)(2,1)S(1)}, u32[]{:S(2)}, u32[]{:S(2)}) collective-permute-start(bf16[512,128]{1,0:T(8,128)(2,1)S(1)} %add_convert_fusion), channel_id=1, source_target_pairs={{0,2},{1,3},{2,0},{3,1},{4,6},{5,7},{6,4},{7,5},{8,10},{9,11},{10,... | collective-permute-start | bytes 393224 | tf_op jit(solution)/shard_map/ppermute | solution.py:576
  77.5 1.3 %collective-permute-start.20 = (bf16[384,128]{1,0:T(8,128)(2,1)S(1)}, bf16[384,128]{1,0:T(8,128)(2,1)S(1)}, u32[]{:S(2)}, u32[]{:S(2)}) collective-permute-start(bf16[384,128]{1,0:T(8,128)(2,1)S(1)} %add_convert_fusion.1.mine), channel_id=1, source_target_pairs={{0,4},{4,0},{8,12},{12,8},{16,20},{20,16},{24,28},{28,24},{1,5},{5... | collective-permute-start | bytes 294920 | tf_op jit(solution)/shard_map/ppermute | solution.py:576

commit v16 on v15

--- a/solution.py
+++ b/solution.py
@@ -888,7 +888,9 @@
         flops=2 * own_rows * width * width,
     )
     if paired:
-        chain = tree_sum([part.astype(F32) for part in all_parts(chain, "blk", 2)]).astype(BF16)
+        parts = all_parts(chain, "blk", 2)
+        parts, latent_grad = lax.optimization_barrier((parts, latent_grad))
+        chain = tree_sum([part.astype(F32) for part in parts]).astype(BF16)
     else:
         chain = lax.psum(chain.astype(F32), "blk").astype(BF16)
     chain, latent_grad = lax.optimization_barrier((chain, latent_grad))

time: 79.3 us -> 75.4 us (0.951)
  waiting for transfers between devices: 24.1 us -> 20.1 us
  starting transfers between devices: 24.8 us -> 23.4 us
  Pallas kernels: 26.7 us -> 27.7 us
    ppermute x15, waiting for transfers between devices: 22.9 us -> 19.4 us  [exchanged(): lax.ppermute(value, axis, [(source, source ^ step) for source in range(co...]
    ppermute x15, starting transfers between devices: 16.2 us -> 14.7 us  [exchanged(): lax.ppermute(value, axis, [(source, source ^ step) for source in range(co...]
    pallas_call x14, Pallas kernels: 26.7 us -> 27.7 us  [call(): pl.pallas_call(kernel, out_shape=[jax.ShapeDtypeStruct(o.shape, o.dtype)...]
  transfers between devices with their start and end apart: 21 -> 21, of which waited for: 9 -> 7; matrix products, arithmetic and copies ran while one was open for 0% -> 0% of each run, Pallas kernels for 20% -> 25%
where the time goes in v16:
time: 75.4 us; the launch traced here: 75 us
  Pallas kernels  27.7 us (37%)
  starting transfers between devices  23.4 us (31%)
  waiting for transfers between devices  20.1 us (27%)
  local copies, waits for them, and re-layouts  1.99 us (3%)
  between operations  1.66 us (2%)
    pallas_call x14, Pallas kernels, call(): pl.pallas_call(kernel, out_shape=[jax.ShapeDtypeStruct(o.shape, o.dtype)...  27.7 us
    ppermute x15, waiting for transfers between devices, exchanged(): lax.ppermute(value, axis, [(source, source ^ step) for source in range(co...  19.4 us
    ppermute x15, starting transfers between devices, exchanged(): lax.ppermute(value, axis, [(source, source ^ step) for source in range(co...  14.7 us
    ppermute x6, starting transfers between devices, shifted(): return lax.ppermute(value, axis, pairs)  8.67 us
    unnamed x44, local copies, waits for them, and re-layouts  1.97 us
  transfers between devices with their start and end apart: 21, of which 7 were waited for; matrix products, arithmetic and copies ran while one was open for 0% of the time, Pallas kernels for 25%

profile of v16, /device:TPU:0, one launch (start us, length us, event | category | flops | bytes accessed | tf_op | source)
XLA Modules:
  0.0 75.0 jit_solution(16745752844368728227)
XLA Ops:
  0.6 1.6 %shard_map.185 = (bf16[576,128]{1,0:T(8,128)(2,1)}, bf16[16,384]{1,0:T(8,128)(2,1)}) custom-call(bf16[512,128]{1,0:T(8,128)(2,1)} %latent.7, f32[3,512]{1,0:T(4,128)} %positions.1, f32[3,128]{1,0:T(4,128)} %pos_weight.1), custom_call_target="tpu_custom_call" | custom-call | bytes 298496 | tf_op jit(solution)/shard_map/pallas_call | solution.py:44
  2.2 0.5 collective-permute-start
  2.7 2.9 %collective-permute-start.1 = (bf16[576,128]{1,0:T(8,128)(2,1)}, bf16[576,128]{1,0:T(8,128)(2,1)S(1)}, u32[]{:S(2)}, u32[]{:S(2)}) collective-permute-start(bf16[576,128]{1,0:T(8,128)(2,1)} %get-tuple-element.60.message.refs_3_), channel_id=1, source_target_pairs={{0,28},{4,0},{8,4},{12,8},{16,12},{20,16},{24,20},{28,24},{1,29},{... | collective-permute-start | bytes 442376 | tf_op jit(solution)/shard_map/ppermute | solution.py:22
  5.6 2.3 %collective-permute-start.2 = (bf16[576,128]{1,0:T(8,128)(2,1)}, bf16[576,128]{1,0:T(8,128)(2,1)S(1)}, u32[]{:S(2)}, u32[]{:S(2)}) collective-permute-start(bf16[576,128]{1,0:T(8,128)(2,1)} %get-tuple-element.60.message.refs_3_), channel_id=1, source_target_pairs={{0,1},{1,0},{2,3},{3,2},{4,5},{5,4},{6,7},{7,6},{8,9},{9,8},{10,11... | collective-permute-start | bytes 442376 | tf_op jit(solution)/shard_map/ppermute | solution.py:576
  7.9 2.6 %collective-permute-start.3 = (bf16[576,128]{1,0:T(8,128)(2,1)}, bf16[576,128]{1,0:T(8,128)(2,1)S(1)}, u32[]{:S(2)}, u32[]{:S(2)}) collective-permute-start(bf16[576,128]{1,0:T(8,128)(2,1)} %get-tuple-element.60.message.refs_3_), channel_id=1, source_target_pairs={{0,2},{1,3},{2,0},{3,1},{4,6},{5,7},{6,4},{7,5},{8,10},{9,11},{10,... | collective-permute-start | bytes 442376 | tf_op jit(solution)/shard_map/ppermute | solution.py:576
  11.2 0.0 copy-start.12
  11.2 0.0 copy-start.13
  11.2 0.0 copy-start.11
  11.2 0.6 copy-done.12
  11.8 0.0 copy-done.13
  11.8 0.0 copy-done.9
  11.8 0.0 copy-done.10
  11.9 0.0 copy-done.11
  11.9 1.2 %copy-done.1 = s32[1,1,16,128,128]{4,3,2,1,0:T(8,128)S(1)} copy-done((s32[1,1,16,128,128]{4,3,2,1,0:T(8,128)S(1)}, s32[1,1,16,128,128]{4,3,2,1,0:T(8,128)}, u32[]{:S(2)}) %copy-start.1) | copy-done | bytes 1048600
  13.1 1.0 %shard_map.184 = (bf16[17,128,128]{2,1,0:T(8,128)(2,1)S(1)}, bf16[17,128,128]{2,1,0:T(8,128)(2,1)S(1)}, bf16[17,128,128]{2,1,0:T(8,128)(2,1)S(1)}, s32[8,128]{1,0:T(8,128)S(1)}, f32[8,128]{1,0:T(8,128)S(1)}) custom-call(s32[1,1]{1,0:T(1,128)S(6)} %copy.20.tile_count, s32[16,128,128]{2,1,0:T(8,128)S(1)} %bitcast.5, s32[1,1,16]{2,1,0:T(1,128)S(1)} %copy-done.9, ...), custom_call_target="tpu_custom_call" | custom-call | flops 268435456 | bytes 2729600 | tf_op jit(solution)/shard_map/pallas_call | solution.py:44
  14.1 2.5 %shard_map.186 = (bf16[4,128,128]{2,1,0:T(8,128)(2,1)S(1)}, bf16[12,128,128]{2,1,0:T(8,128)(2,1)S(1)}, f32[4,128,128]{2,1,0:T(8,128)S(1)}, f32[4,128,128]{2,1,0:...) custom-call(s32[1,1]{1,0:T(1,128)S(6)} %copy.20.tile_count, s32[8,128]{1,0:T(8,128)S(1)} %get-tuple-element.56.most, ...), custom_call_target="tpu_custom_call" | custom-call | flops 1073741824 | bytes 3739648 | tf_op jit(solution)/shard_map/pallas_call | solution.py:44
  16.7 4.8 %collective-permute-done.3.refs_4_.refs_5_ = bf16[576,128]{1,0:T(8,128)(2,1)S(1)} collective-permute-done((bf16[576,128]{1,0:T(8,128)(2,1)}, bf16[576,128]{1,0:T(8,128)(2,1)S(1)}, u32[]{:S(2)}, u32[]{:S(2)}) %collective-permute-start.3) | collective-permute-done | bytes 147488 | tf_op jit(solution)/shard_map/ppermute | solution.py:576
  21.4 4.7 %shard_map.187 = (bf16[512,128]{1,0:T(8,128)(2,1)S(1)}, bf16[512,128]{1,0:T(8,128)(2,1)S(1)}, bf16[512,128]{1,0:T(8,128)(2,1)S(1)}, bf16[512,128]{1,0:T(8,128)(2,1)S(1)}, bf16[16,128,128]{2,1,0:T(8,128)(2,1)S(1)}) custom-call(s32[1,1]{1,0:T(1,128)S(6)} %copy.20.tile_count, s32[8,128]{1,0:T(8,128)S(1)} %get-tuple-element.56.most, ...), custom_call_target="tpu_custom_call" | custom-call | flops 2147483648 | bytes 4227072 | tf_op jit(solution)/shard_map/pallas_call | solution.py:44
  26.2 0.1 collective-permute-start.5
  26.3 2.6 %collective-permute-start.6 = (bf16[512,128]{1,0:T(8,128)(2,1)S(1)}, bf16[512,128]{1,0:T(8,128)(2,1)S(1)}, u32[]{:S(2)}, u32[]{:S(2)}) collective-permute-start(bf16[512,128]{1,0:T(8,128)(2,1)S(1)} %get-tuple-element.70), channel_id=1, source_target_pairs={{0,28},{4,0},{8,4},{12,8},{16,12},{20,16},{24,20},{28,24},{1,29},{... | collective-permute-start | bytes 393224 | tf_op jit(solution)/shard_map/ppermute | solution.py:22
  28.9 0.0 copy-start.5
  28.9 4.1 %shard_map.188 = (f32[512,128]{1,0:T(8,128)S(1)}, f32[512,128]{1,0:T(8,128)S(1)}) custom-call(s32[1,1]{1,0:T(1,128)S(6)} %copy.20.tile_count, s32[8,128]{1,0:T(8,128)S(1)} %get-tuple-element.56.most, bf16[17,128,128]{2,1,0:T(8,128)(2,1)S(1)} %get-tuple-element.57.row_rank, bf16[17,128,128]{2,1,0:T(8,128)(2,1)S(1)} %get-tuple-element.58.row_degree, ...), custom_call_target="tpu_custom_call" | custom-call | flops 1073741824 | bytes 3084288 | tf_op jit(solution)/shard_map/pallas_call | solution.py:44
  33.1 1.8 %shard_map.189 = (bf16[512,128]{1,0:T(8,128)(2,1)}, bf16[1024,128]{1,0:T(8,128)(2,1)S(1)}, bf16[1024,128]{1,0:T(8,128)(2,1)}, bf16[512,128]{1,0:T(8,128)(2,1)S(1...) custom-call(f32[8,128]{1,0:T(8,128)S(1)} %get-tuple-element.55.vecto, ...), custom_call_target="tpu_custom_call" | custom-call | flops 117440512 | bytes 2625536 | tf_op jit(solution)/shard_map/pallas_call | solution.py:44
  34.9 2.6 %collective-permute-start.9 = (bf16[1024,128]{1,0:T(8,128)(2,1)S(1)}, bf16[1024,128]{1,0:T(8,128)(2,1)S(1)}, u32[]{:S(2)}, u32[]{:S(2)}) collective-permute-start(bf16[1024,128]{1,0:T(8,128)(2,1)S(1)} %get-tuple-element.83.refs_0_), channel_id=1, source_target_pairs={{0,28},{4,0},{8,4},{12,8},{16,12},{20,16},{24,20},{28,24},{1,29},{... | collective-permute-start | bytes 786440 | tf_op jit(solution)/shard_map/ppermute | solution.py:22
  37.6 1.0 %shard_map.190 = (f32[256,128]{1,0:T(8,128)S(1)}, bf16[256,128]{1,0:T(8,128)(2,1)}) custom-call(bf16[512,128]{1,0:T(8,128)(2,1)S(1)} %copy-done, bf16[512,128]{1,0:T(8,128)(2,1)S(1)} %get-tuple-element.74.aggregate, bf16[512,128]{1,0:T(8,128)(2,1)S(1)} %get-tuple-element.75.message, bf16[512,128]{1,0:T(8,128)(2,1)S(1)} %get-tuple-element.76.hidden, ...), custom_call_target="tpu_custom_call" | custom-call | flops 67108864 | bytes 1114112 | tf_op jit(solution)/shard_map/pallas_call | solution.py:44
  38.6 2.9 %shard_map.192.refs_2_ = f32[16,128,128]{2,1,0:T(8,128)S(1)} custom-call(s32[1,1]{1,0:T(1,128)S(6)} %copy.20.tile_count, s32[8,128]{1,0:T(8,128)S(1)} %get-tuple-element.56.most, bf16[17,128,128]{2,1,0:T(8,128)(2,1)S(1)} %get-tuple-element.87.col_rank, bf16[16,128,128]{2,1,0:T(8,128)(2,1)S(1)} %get-tuple-element.67.refs_0_.senders, ...), custom_call_target="tpu_custom_call" | custom-call | flops 134217728 | bytes 2789376 | tf_op jit(solution)/shard_map/pallas_call | solution.py:44
  41.6 1.5 %collective-permute-done.7.arrived = bf16[256,128]{1,0:T(8,128)(2,1)S(1)} collective-permute-done((bf16[256,128]{1,0:T(8,128)(2,1)}, bf16[256,128]{1,0:T(8,128)(2,1)S(1)}, u32[]{:S(2)}, u32[]{:S(2)}) %collective-permute-start.7) | collective-permute-done | bytes 65568 | tf_op jit(solution)/shard_map/ppermute | solution.py:576
  43.1 0.7 collective-permute-done.8.refs_0_.from_low
  43.8 1.2 %collective-permute-start.10 = (bf16[128,128]{1,0:T(8,128)(2,1)S(1)}, bf16[128,128]{1,0:T(8,128)(2,1)S(1)}, u32[]{:S(2)}, u32[]{:S(2)}) collective-permute-start(bf16[128,128]{1,0:T(8,128)(2,1)S(1)} %get-tuple-element.86), channel_id=1, source_target_pairs={{0,2},{1,3},{2,0},{3,1},{4,6},{5,7},{6,4},{7,5},{8,10},{9,11},{10,... | collective-permute-start | bytes 98312 | tf_op jit(solution)/shard_map/ppermute | solution.py:576
  45.0 5.9 %shard_map.193 = (f32[512,128]{1,0:T(8,128)S(1)}, bf16[512,128]{1,0:T(8,128)(2,1)S(1)}, bf16[1024,128]{1,0:T(8,128)(2,1)S(1)}, bf16[128,128]{1,0:T(8,128)(2,1)S(1)}) custom-call(s32[1,1]{1,0:T(1,128)S(6)} %copy.20.tile_count, s32[8,128]{1,0:T(8,128)S(1)} %get-tuple-element.56.most, bf16[17,128,128]{2,1,0:T(8,128)(2,1)S(1)} %get-tuple-element.87.col_rank, ...), custom_call_target="tpu_custom_call" | custom-call | flops 2147483648 | bytes 4329472 | tf_op jit(solution)/shard_map/pallas_call | solution.py:44
  50.9 0.4 shard_map.194
  51.4 0.1 collective-permute-start.11
  51.5 0.1 collective-permute-start.15
  51.6 1.1 %collective-permute-done.11 = bf16[192,128]{1,0:T(8,128)(2,1)S(1)} collective-permute-done((bf16[192,128]{1,0:T(8,128)(2,1)S(1)}, bf16[192,128]{1,0:T(8,128)(2,1)S(1)}, u32[]{:S(2)}, u32[]{:S(2)}) %collective-permute-start.11) | collective-permute-done | bytes 49184 | tf_op jit(solution)/shard_map/ppermute | solution.py:576
  52.7 0.9 %collective-permute-start.12 = (bf16[192,128]{1,0:T(8,128)(2,1)S(1)}, bf16[192,128]{1,0:T(8,128)(2,1)S(1)}, u32[]{:S(2)}, u32[]{:S(2)}) collective-permute-start(bf16[192,128]{1,0:T(8,128)(2,1)S(1)} %add_convert_fusion.2.refs_0_), channel_id=1, source_target_pairs={{0,1},{1,0},{2,3},{3,2},{4,5},{5,4},{6,7},{7,6},{8,9},{9,8},{10,11... | collective-permute-start | bytes 147464 | tf_op jit(solution)/shard_map/ppermute | solution.py:576
  53.7 1.0 %collective-permute-start.13 = (bf16[192,128]{1,0:T(8,128)(2,1)S(1)}, bf16[192,128]{1,0:T(8,128)(2,1)S(1)}, u32[]{:S(2)}, u32[]{:S(2)}) collective-permute-start(bf16[192,128]{1,0:T(8,128)(2,1)S(1)} %add_convert_fusion.2.refs_0_), channel_id=1, source_target_pairs={{0,2},{1,3},{2,0},{3,1},{4,6},{5,7},{6,4},{7,5},{8,10},{9,11},{10,... | collective-permute-start | bytes 147464 | tf_op jit(solution)/shard_map/ppermute | solution.py:576
  54.7 2.5 %collective-permute-start.14 = (bf16[192,128]{1,0:T(8,128)(2,1)S(1)}, bf16[192,128]{1,0:T(8,128)(2,1)S(1)}, u32[]{:S(2)}, u32[]{:S(2)}) collective-permute-start(bf16[192,128]{1,0:T(8,128)(2,1)S(1)} %add_convert_fusion.2.refs_0_), channel_id=1, source_target_pairs={{0,3},{1,2},{2,1},{3,0},{4,7},{5,6},{6,5},{7,4},{8,11},{9,10},{10,... | collective-permute-start | bytes 147464 | tf_op jit(solution)/shard_map/ppermute | solution.py:576
  57.2 6.2 %collective-permute-done.12.refs_1_ = bf16[192,128]{1,0:T(8,128)(2,1)S(1)} collective-permute-done((bf16[192,128]{1,0:T(8,128)(2,1)S(1)}, bf16[192,128]{1,0:T(8,128)(2,1)S(1)}, u32[]{:S(2)}, u32[]{:S(2)}) %collective-permute-start.12) | collective-permute-done | bytes 49184 | tf_op jit(solution)/shard_map/ppermute | solution.py:576
  63.5 0.4 collective-permute-start.19
  63.9 1.6 %collective-permute-start.16 = (bf16[384,128]{1,0:T(8,128)(2,1)S(1)}, bf16[384,128]{1,0:T(8,128)(2,1)S(1)}, u32[]{:S(2)}, u32[]{:S(2)}) collective-permute-start(bf16[384,128]{1,0:T(8,128)(2,1)S(1)} %shard_map.195), channel_id=1, source_target_pairs={{0,8},{4,12},{8,0},{12,4},{16,24},{20,28},{24,16},{28,20},{1,9},{5... | collective-permute-start | bytes 294920 | tf_op jit(solution)/shard_map/ppermute | solution.py:576
  65.5 1.0 %collective-permute-start.17 = (bf16[384,128]{1,0:T(8,128)(2,1)S(1)}, bf16[384,128]{1,0:T(8,128)(2,1)S(1)}, u32[]{:S(2)}, u32[]{:S(2)}) collective-permute-start(bf16[384,128]{1,0:T(8,128)(2,1)S(1)} %shard_map.195), channel_id=1, source_target_pairs={{0,16},{4,20},{8,24},{12,28},{16,0},{20,4},{24,8},{28,12},{1,17},{... | collective-permute-start | bytes 294920 | tf_op jit(solution)/shard_map/ppermute | solution.py:576
  66.5 0.9 %collective-permute-start.18 = (bf16[384,128]{1,0:T(8,128)(2,1)S(1)}, bf16[384,128]{1,0:T(8,128)(2,1)S(1)}, u32[]{:S(2)}, u32[]{:S(2)}) collective-permute-start(bf16[384,128]{1,0:T(8,128)(2,1)S(1)} %shard_map.195), channel_id=1, source_target_pairs={{0,24},{4,28},{8,16},{12,20},{16,8},{20,12},{24,0},{28,4},{1,25},{... | collective-permute-start | bytes 294920 | tf_op jit(solution)/shard_map/ppermute | solution.py:576
  67.4 4.5 %collective-permute-done.19.refs_1_ = bf16[512,128]{1,0:T(8,128)(2,1)S(1)} collective-permute-done((bf16[512,128]{1,0:T(8,128)(2,1)S(1)}, bf16[512,128]{1,0:T(8,128)(2,1)S(1)}, u32[]{:S(2)}, u32[]{:S(2)}) %collective-permute-start.19) | collective-permute-done | bytes 131104 | tf_op jit(solution)/shard_map/ppermute | solution.py:576
  71.9 0.9 %shard_map.196 = f32[512,128]{1,0:T(8,128)} custom-call(f32[512,128]{1,0:T(8,128)S(1)} %get-tuple-element.96.direct, bf16[128,128]{1,0:T(8,128)(2,1)S(1)} %copy-done.8, f32[512,128]{1,0:T(8,128)S(1)} %get-tuple-element.97.own, bf16[1024,128]{1,0:T(8,128)(2,1)S(1)} %collective-permute-done.15.refs_0_, bf16[512,128]{1,0:T(8,128)(2,1)S(1)} %collective-permute-done.19.refs_1_), custom_call_target="tpu_custom_call" | custom-call | flops 16777216 | bytes 1212416 | tf_op jit(solution)/shard_map/pallas_call | solution.py:44
  72.8 0.1 add_convert_fusion.1.mine
  72.9 0.1 collective-permute-start.20
  73.0 1.3 %collective-permute-done.20.other = bf16[384,128]{1,0:T(8,128)(2,1)S(1)} collective-permute-done((bf16[384,128]{1,0:T(8,128)(2,1)S(1)}, bf16[384,128]{1,0:T(8,128)(2,1)S(1)}, u32[]{:S(2)}, u32[]{:S(2)}) %collective-permute-start.20) | collective-permute-done | bytes 98336 | tf_op jit(solution)/shard_map/ppermute | solution.py:576
  74.3 0.8 %shard_map.197 = f32[768,128]{1,0:T(8,128)} custom-call(bf16[384,128]{1,0:T(8,128)(2,1)S(1)} %add_convert_fusion.1.mine, bf16[384,128]{1,0:T(8,128)(2,1)S(1)} %collective-permute-done.20.other), custom_call_target="tpu_custom_call" | custom-call | bytes 589824 | tf_op jit(solution)/shard_map/pallas_call | solution.py:44
  (59 shorter events, 0.3 us)
Async XLA Ops:
  2.2 11.9 %collective-permute-start = (bf16[576,128]{1,0:T(8,128)(2,1)}, bf16[576,128]{1,0:T(8,128)(2,1)S(1)}, u32[]{:S(2)}, u32[]{:S(2)}) collective-permute-start(bf16[576,128]{1,0:T(8,128)(2,1)} %get-tuple-element.60.message.refs_3_), channel_id=1, source_target_pairs={{0,4},{4,8},{8,12},{12,16},{16,20},{20,24},{24,28},{28,0},{1,5},{5... | collective-permute-start | bytes 442376 | tf_op jit(solution)/shard_map/ppermute | solution.py:22
  2.7 11.4 %collective-permute-start.1 = (bf16[576,128]{1,0:T(8,128)(2,1)}, bf16[576,128]{1,0:T(8,128)(2,1)S(1)}, u32[]{:S(2)}, u32[]{:S(2)}) collective-permute-start(bf16[576,128]{1,0:T(8,128)(2,1)} %get-tuple-element.60.message.refs_3_), channel_id=1, source_target_pairs={{0,28},{4,0},{8,4},{12,8},{16,12},{20,16},{24,20},{28,24},{1,29},{... | collective-permute-start | bytes 442376 | tf_op jit(solution)/shard_map/ppermute | solution.py:22
  5.6 11.1 %collective-permute-start.2 = (bf16[576,128]{1,0:T(8,128)(2,1)}, bf16[576,128]{1,0:T(8,128)(2,1)S(1)}, u32[]{:S(2)}, u32[]{:S(2)}) collective-permute-start(bf16[576,128]{1,0:T(8,128)(2,1)} %get-tuple-element.60.message.refs_3_), channel_id=1, source_target_pairs={{0,1},{1,0},{2,3},{3,2},{4,5},{5,4},{6,7},{7,6},{8,9},{9,8},{10,11... | collective-permute-start | bytes 442376 | tf_op jit(solution)/shard_map/ppermute | solution.py:576
  7.9 13.5 %collective-permute-start.3 = (bf16[576,128]{1,0:T(8,128)(2,1)}, bf16[576,128]{1,0:T(8,128)(2,1)S(1)}, u32[]{:S(2)}, u32[]{:S(2)}) collective-permute-start(bf16[576,128]{1,0:T(8,128)(2,1)} %get-tuple-element.60.message.refs_3_), channel_id=1, source_target_pairs={{0,2},{1,3},{2,0},{3,1},{4,6},{5,7},{6,4},{7,5},{8,10},{9,11},{10,... | collective-permute-start | bytes 442376 | tf_op jit(solution)/shard_map/ppermute | solution.py:576
  10.5 10.9 %collective-permute-start.4 = (bf16[576,128]{1,0:T(8,128)(2,1)}, bf16[576,128]{1,0:T(8,128)(2,1)S(1)}, u32[]{:S(2)}, u32[]{:S(2)}) collective-permute-start(bf16[576,128]{1,0:T(8,128)(2,1)} %get-tuple-element.60.message.refs_3_), channel_id=1, source_target_pairs={{0,3},{1,2},{2,1},{3,0},{4,7},{5,6},{6,5},{7,4},{8,11},{9,10},{10,... | collective-permute-start | bytes 442376 | tf_op jit(solution)/shard_map/ppermute | solution.py:576
  11.2 0.7 copy-start.12
  11.2 0.7 copy-start.13
  11.2 0.7 copy-start.9
  11.2 0.7 copy-start.10
  11.2 0.7 copy-start.11
  11.9 1.2 %copy-start.1 = (s32[1,1,16,128,128]{4,3,2,1,0:T(8,128)S(1)}, s32[1,1,16,128,128]{4,3,2,1,0:T(8,128)}, u32[]{:S(2)}) copy-start(s32[1,1,16,128,128]{4,3,2,1,0:T(8,128)} %param.21) | copy-start | bytes 3145732
  13.1 1.0 %copy-start.7 = (bf16[128,128]{1,0:T(8,128)(2,1)S(1)}, bf16[128,128]{1,0:T(8,128)(2,1)}, u32[]{:S(2)}) copy-start(bf16[128,128]{1,0:T(8,128)(2,1)} %w_recv.3) | copy-start | bytes 98308
  13.1 1.0 %copy-start.8 = (bf16[128,128]{1,0:T(8,128)(2,1)S(1)}, bf16[128,128]{1,0:T(8,128)(2,1)}, u32[]{:S(2)}) copy-start(bf16[128,128]{1,0:T(8,128)(2,1)} %w_send.3) | copy-start | bytes 98308
  13.1 1.0 %copy-start.14 = (bf16[576,128]{1,0:T(8,128)(2,1)S(1)}, bf16[576,128]{1,0:T(8,128)(2,1)}, u32[]{:S(2)}) copy-start(bf16[576,128]{1,0:T(8,128)(2,1)} %get-tuple-element.60.message.refs_3_) | copy-start | bytes 442372
  13.1 1.0 %copy-start.21 = (bf16[16,384]{1,0:T(8,128)(2,1)S(1)}, bf16[16,384]{1,0:T(8,128)(2,1)}, u32[]{:S(2)}) copy-start(bf16[16,384]{1,0:T(8,128)(2,1)} %get-tuple-element.59.weight_parts.refs_2_) | copy-start | bytes 36868
  16.6 9.5 %copy-start.15 = (bf16[576,128]{1,0:T(8,128)(2,1)}, bf16[576,128]{1,0:T(8,128)(2,1)S(1)}, u32[]{:S(2)}) copy-start(bf16[576,128]{1,0:T(8,128)(2,1)S(1)} %collective-permute-done.2.refs_3_.refs_4_) | copy-start | bytes 442372
  21.4 4.8 %copy-start.17 = (bf16[576,128]{1,0:T(8,128)(2,1)}, bf16[576,128]{1,0:T(8,128)(2,1)S(1)}, u32[]{:S(2)}) copy-start(bf16[576,128]{1,0:T(8,128)(2,1)S(1)} %collective-permute-done.3.refs_4_.refs_5_) | copy-start | bytes 442372
  21.4 4.8 %copy-start.19 = (bf16[576,128]{1,0:T(8,128)(2,1)}, bf16[576,128]{1,0:T(8,128)(2,1)S(1)}, u32[]{:S(2)}) copy-start(bf16[576,128]{1,0:T(8,128)(2,1)S(1)} %collective-permute-done.4.refs_5_.refs_6_) | copy-start | bytes 442372
  26.2 6.8 %collective-permute-start.5 = (bf16[512,128]{1,0:T(8,128)(2,1)S(1)}, bf16[512,128]{1,0:T(8,128)(2,1)S(1)}, u32[]{:S(2)}, u32[]{:S(2)}) collective-permute-start(bf16[512,128]{1,0:T(8,128)(2,1)S(1)} %get-tuple-element.69), channel_id=1, source_target_pairs={{0,4},{4,8},{8,12},{12,16},{16,20},{20,24},{24,28},{28,0},{1,5},{5... | collective-permute-start | bytes 393224 | tf_op jit(solution)/shard_map/ppermute | solution.py:22
  26.3 6.8 %collective-permute-start.6 = (bf16[512,128]{1,0:T(8,128)(2,1)S(1)}, bf16[512,128]{1,0:T(8,128)(2,1)S(1)}, u32[]{:S(2)}, u32[]{:S(2)}) collective-permute-start(bf16[512,128]{1,0:T(8,128)(2,1)S(1)} %get-tuple-element.70), channel_id=1, source_target_pairs={{0,28},{4,0},{8,4},{12,8},{16,12},{20,16},{24,20},{28,24},{1,29},{... | collective-permute-start | bytes 393224 | tf_op jit(solution)/shard_map/ppermute | solution.py:22
  28.9 4.1 %copy-start = (bf16[512,128]{1,0:T(8,128)(2,1)S(1)}, bf16[512,128]{1,0:T(8,128)(2,1)}, u32[]{:S(2)}) copy-start(bf16[512,128]{1,0:T(8,128)(2,1)} %latent.7) | copy-start | bytes 393220
  28.9 4.2 %copy-start.2 = (bf16[512,128]{1,0:T(8,128)(2,1)S(1)}, bf16[512,128]{1,0:T(8,128)(2,1)}, u32[]{:S(2)}) copy-start(bf16[512,128]{1,0:T(8,128)(2,1)} %cotangent.3) | copy-start | bytes 393220
  28.9 4.2 %copy-start.3 = (bf16[128,128]{1,0:T(8,128)(2,1)S(1)}, bf16[128,128]{1,0:T(8,128)(2,1)}, u32[]{:S(2)}) copy-start(bf16[128,128]{1,0:T(8,128)(2,1)} %w_edge_out.3) | copy-start | bytes 98308
  28.9 4.2 %copy-start.4 = (bf16[128,128]{1,0:T(8,128)(2,1)S(1)}, bf16[128,128]{1,0:T(8,128)(2,1)}, u32[]{:S(2)}) copy-start(bf16[128,128]{1,0:T(8,128)(2,1)} %w_node_self.3) | copy-start | bytes 98308
  28.9 4.2 %copy-start.5 = (bf16[128,128]{1,0:T(8,128)(2,1)S(1)}, bf16[128,128]{1,0:T(8,128)(2,1)}, u32[]{:S(2)}) copy-start(bf16[128,128]{1,0:T(8,128)(2,1)} %w_node_msg.1) | copy-start | bytes 98308
  28.9 4.2 %copy-start.6 = (bf16[128,128]{1,0:T(8,128)(2,1)S(1)}, bf16[128,128]{1,0:T(8,128)(2,1)}, u32[]{:S(2)}) copy-start(bf16[128,128]{1,0:T(8,128)(2,1)} %w_node_out.1) | copy-start | bytes 98308
  34.9 8.8 %collective-permute-start.8 = (bf16[1024,128]{1,0:T(8,128)(2,1)}, bf16[1024,128]{1,0:T(8,128)(2,1)S(1)}, u32[]{:S(2)}, u32[]{:S(2)}) collective-permute-start(bf16[1024,128]{1,0:T(8,128)(2,1)} %get-tuple-element.82), channel_id=1, source_target_pairs={{0,4},{4,8},{8,12},{12,16},{16,20},{20,24},{24,28},{28,0},{1,5},{5... | collective-permute-start | bytes 786440 | tf_op jit(solution)/shard_map/ppermute | solution.py:22
  34.9 8.8 %collective-permute-start.9 = (bf16[1024,128]{1,0:T(8,128)(2,1)S(1)}, bf16[1024,128]{1,0:T(8,128)(2,1)S(1)}, u32[]{:S(2)}, u32[]{:S(2)}) collective-permute-start(bf16[1024,128]{1,0:T(8,128)(2,1)S(1)} %get-tuple-element.83.refs_0_), channel_id=1, source_target_pairs={{0,28},{4,0},{8,4},{12,8},{16,12},{20,16},{24,20},{28,24},{1,29},{... | collective-permute-start | bytes 786440 | tf_op jit(solution)/shard_map/ppermute | solution.py:22
  38.6 4.5 %collective-permute-start.7 = (bf16[256,128]{1,0:T(8,128)(2,1)}, bf16[256,128]{1,0:T(8,128)(2,1)S(1)}, u32[]{:S(2)}, u32[]{:S(2)}) collective-permute-start(bf16[256,128]{1,0:T(8,128)(2,1)} %get-tuple-element.81), channel_id=1, source_target_pairs={{0,1},{1,0},{2,3},{3,2},{4,5},{5,4},{6,7},{7,6},{8,9},{9,8},{10,11... | collective-permute-start | bytes 196616 | tf_op jit(solution)/shard_map/ppermute | solution.py:576
  38.6 6.4 %copy-start.18 = (bf16[576,128]{1,0:T(8,128)(2,1)S(1)}, bf16[576,128]{1,0:T(8,128)(2,1)}, u32[]{:S(2)}) copy-start(bf16[576,128]{1,0:T(8,128)(2,1)} %copy-done.17) | copy-start | bytes 442372
  38.6 6.4 %copy-start.20 = (bf16[576,128]{1,0:T(8,128)(2,1)S(1)}, bf16[576,128]{1,0:T(8,128)(2,1)}, u32[]{:S(2)}) copy-start(bf16[576,128]{1,0:T(8,128)(2,1)} %copy-done.19) | copy-start | bytes 442372
  41.6 3.4 %copy-start.16 = (bf16[576,128]{1,0:T(8,128)(2,1)S(1)}, bf16[576,128]{1,0:T(8,128)(2,1)}, u32[]{:S(2)}) copy-start(bf16[576,128]{1,0:T(8,128)(2,1)} %copy-done.15) | copy-start | bytes 442372
  43.8 7.6 %collective-permute-start.10 = (bf16[128,128]{1,0:T(8,128)(2,1)S(1)}, bf16[128,128]{1,0:T(8,128)(2,1)S(1)}, u32[]{:S(2)}, u32[]{:S(2)}) collective-permute-start(bf16[128,128]{1,0:T(8,128)(2,1)S(1)} %get-tuple-element.86), channel_id=1, source_target_pairs={{0,2},{1,3},{2,0},{3,1},{4,6},{5,7},{6,4},{7,5},{8,10},{9,11},{10,... | collective-permute-start | bytes 98312 | tf_op jit(solution)/shard_map/ppermute | solution.py:576
  51.4 1.3 %collective-permute-start.11 = (bf16[192,128]{1,0:T(8,128)(2,1)S(1)}, bf16[192,128]{1,0:T(8,128)(2,1)S(1)}, u32[]{:S(2)}, u32[]{:S(2)}) collective-permute-start(bf16[192,128]{1,0:T(8,128)(2,1)S(1)} %broadcast_select_fusion), channel_id=1, source_target_pairs={{0,4},{4,0},{8,12},{12,8},{16,20},{20,16},{24,28},{28,24},{1,5},{5... | collective-permute-start | bytes 147464 | tf_op jit(solution)/shard_map/ppermute | solution.py:576
  51.5 11.9 %collective-permute-start.15 = (bf16[1024,128]{1,0:T(8,128)(2,1)S(1)}, bf16[1024,128]{1,0:T(8,128)(2,1)S(1)}, u32[]{:S(2)}, u32[]{:S(2)}) collective-permute-start(bf16[1024,128]{1,0:T(8,128)(2,1)S(1)} %get-tuple-element.94), channel_id=1, source_target_pairs={{0,1},{1,0},{2,3},{3,2},{4,5},{5,4},{6,7},{7,6},{8,9},{9,8},{10,11... | collective-permute-start | bytes 786440 | tf_op jit(solution)/shard_map/ppermute | solution.py:576
  52.7 10.6 %collective-permute-start.12 = (bf16[192,128]{1,0:T(8,128)(2,1)S(1)}, bf16[192,128]{1,0:T(8,128)(2,1)S(1)}, u32[]{:S(2)}, u32[]{:S(2)}) collective-permute-start(bf16[192,128]{1,0:T(8,128)(2,1)S(1)} %add_convert_fusion.2.refs_0_), channel_id=1, source_target_pairs={{0,1},{1,0},{2,3},{3,2},{4,5},{5,4},{6,7},{7,6},{8,9},{9,8},{10,11... | collective-permute-start | bytes 147464 | tf_op jit(solution)/shard_map/ppermute | solution.py:576
  53.7 9.7 %collective-permute-start.13 = (bf16[192,128]{1,0:T(8,128)(2,1)S(1)}, bf16[192,128]{1,0:T(8,128)(2,1)S(1)}, u32[]{:S(2)}, u32[]{:S(2)}) collective-permute-start(bf16[192,128]{1,0:T(8,128)(2,1)S(1)} %add_convert_fusion.2.refs_0_), channel_id=1, source_target_pairs={{0,2},{1,3},{2,0},{3,1},{4,6},{5,7},{6,4},{7,5},{8,10},{9,11},{10,... | collective-permute-start | bytes 147464 | tf_op jit(solution)/shard_map/ppermute | solution.py:576
  54.7 8.7 %collective-permute-start.14 = (bf16[192,128]{1,0:T(8,128)(2,1)S(1)}, bf16[192,128]{1,0:T(8,128)(2,1)S(1)}, u32[]{:S(2)}, u32[]{:S(2)}) collective-permute-start(bf16[192,128]{1,0:T(8,128)(2,1)S(1)} %add_convert_fusion.2.refs_0_), channel_id=1, source_target_pairs={{0,3},{1,2},{2,1},{3,0},{4,7},{5,6},{6,5},{7,4},{8,11},{9,10},{10,... | collective-permute-start | bytes 147464 | tf_op jit(solution)/shard_map/ppermute | solution.py:576
  63.5 8.4 %collective-permute-start.19 = (bf16[512,128]{1,0:T(8,128)(2,1)S(1)}, bf16[512,128]{1,0:T(8,128)(2,1)S(1)}, u32[]{:S(2)}, u32[]{:S(2)}) collective-permute-start(bf16[512,128]{1,0:T(8,128)(2,1)S(1)} %add_convert_fusion), channel_id=1, source_target_pairs={{0,2},{1,3},{2,0},{3,1},{4,6},{5,7},{6,4},{7,5},{8,10},{9,11},{10,... | collective-permute-start | bytes 393224 | tf_op jit(solution)/shard_map/ppermute | solution.py:576
  63.9 8.9 %collective-permute-start.16 = (bf16[384,128]{1,0:T(8,128)(2,1)S(1)}, bf16[384,128]{1,0:T(8,128)(2,1)S(1)}, u32[]{:S(2)}, u32[]{:S(2)}) collective-permute-start(bf16[384,128]{1,0:T(8,128)(2,1)S(1)} %shard_map.195), channel_id=1, source_target_pairs={{0,8},{4,12},{8,0},{12,4},{16,24},{20,28},{24,16},{28,20},{1,9},{5... | collective-permute-start | bytes 294920 | tf_op jit(solution)/shard_map/ppermute | solution.py:576
  65.5 7.3 %collective-permute-start.17 = (bf16[384,128]{1,0:T(8,128)(2,1)S(1)}, bf16[384,128]{1,0:T(8,128)(2,1)S(1)}, u32[]{:S(2)}, u32[]{:S(2)}) collective-permute-start(bf16[384,128]{1,0:T(8,128)(2,1)S(1)} %shard_map.195), channel_id=1, source_target_pairs={{0,16},{4,20},{8,24},{12,28},{16,0},{20,4},{24,8},{28,12},{1,17},{... | collective-permute-start | bytes 294920 | tf_op jit(solution)/shard_map/ppermute | solution.py:576
  66.5 6.4 %collective-permute-start.18 = (bf16[384,128]{1,0:T(8,128)(2,1)S(1)}, bf16[384,128]{1,0:T(8,128)(2,1)S(1)}, u32[]{:S(2)}, u32[]{:S(2)}) collective-permute-start(bf16[384,128]{1,0:T(8,128)(2,1)S(1)} %shard_map.195), channel_id=1, source_target_pairs={{0,24},{4,28},{8,16},{12,20},{16,8},{20,12},{24,0},{28,4},{1,25},{... | collective-permute-start | bytes 294920 | tf_op jit(solution)/shard_map/ppermute | solution.py:576
  72.9 1.4 %collective-permute-start.20 = (bf16[384,128]{1,0:T(8,128)(2,1)S(1)}, bf16[384,128]{1,0:T(8,128)(2,1)S(1)}, u32[]{:S(2)}, u32[]{:S(2)}) collective-permute-start(bf16[384,128]{1,0:T(8,128)(2,1)S(1)} %add_convert_fusion.1.mine), channel_id=1, source_target_pairs={{0,4},{4,0},{8,12},{12,8},{16,20},{20,16},{24,28},{28,24},{1,5},{5... | collective-permute-start | bytes 294920 | tf_op jit(solution)/shard_map/ppermute | solution.py:576

commit v17 on v16

--- a/solution.py
+++ b/solution.py
@@ -36,7 +36,7 @@
     )
 
 
-def call(kernel, outs, args, scalars=(), far=(), scratch=(), flops=0, smem_outs=(), grant=20):
+def call(kernel, outs, args, scalars=(), far=(), scratch=(), flops=0, smem_outs=(), grant=12):
     vmem = pl.BlockSpec(memory_space=pltpu.VMEM)
     smem = pl.BlockSpec(memory_space=pltpu.SMEM)
     hbm = pl.BlockSpec(memory_space=pltpu.HBM)

time: 75.4 us -> 76.5 us (1.015); the launches traced: 75 us -> 77.7 us
  waiting for transfers between devices: 20.1 us -> 21.9 us
  starting transfers between devices: 23.4 us -> 24.9 us
    ppermute x6, waiting for transfers between devices: 0.67 us -> 3.02 us  [shifted(): return lax.ppermute(value, axis, pairs)]
    ppermute x15, starting transfers between devices: 14.7 us -> 16.3 us  [exchanged(): lax.ppermute(value, axis, [(source, source ^ step) for source in range(co...]
  transfers between devices with their start and end apart: 21 -> 21, of which waited for: 7 -> 8; matrix products, arithmetic and copies ran while one was open for 0% -> 0% of each run, Pallas kernels for 25% -> 24%
where the time goes in v17:
time: 76.5 us; the launch traced here: 77.7 us
  Pallas kernels  27.1 us (35%)
  starting transfers between devices  24.9 us (33%)
  waiting for transfers between devices  21.9 us (29%)
  local copies, waits for them, and re-layouts  1.99 us (3%)
  between operations  1.64 us (2%)
    pallas_call x14, Pallas kernels, call(): pl.pallas_call(kernel, out_shape=[jax.ShapeDtypeStruct(o.shape, o.dtype)...  27.1 us
    ppermute x15, waiting for transfers between devices, exchanged(): lax.ppermute(value, axis, [(source, source ^ step) for source in range(co...  18.9 us
    ppermute x15, starting transfers between devices, exchanged(): lax.ppermute(value, axis, [(source, source ^ step) for source in range(co...  16.3 us
    ppermute x6, starting transfers between devices, shifted(): return lax.ppermute(value, axis, pairs)  8.67 us
    ppermute x6, waiting for transfers between devices, shifted(): return lax.ppermute(value, axis, pairs)  3.02 us
    unnamed x44, local copies, waits for them, and re-layouts  1.97 us
  transfers between devices with their start and end apart: 21, of which 8 were waited for; matrix products, arithmetic and copies ran while one was open for 0% of the time, Pallas kernels for 24%

profile of v17, /device:TPU:0, one launch (start us, length us, event | category | flops | bytes accessed | tf_op | source)
XLA Modules:
  0.0 77.7 jit_solution(5893658579321025409)
XLA Ops:
  0.6 1.6 %shard_map.185 = (bf16[576,128]{1,0:T(8,128)(2,1)}, bf16[16,384]{1,0:T(8,128)(2,1)}) custom-call(bf16[512,128]{1,0:T(8,128)(2,1)} %latent.7, f32[3,512]{1,0:T(4,128)} %positions.1, f32[3,128]{1,0:T(4,128)} %pos_weight.1), custom_call_target="tpu_custom_call" | custom-call | bytes 298496 | tf_op jit(solution)/shard_map/pallas_call | solution.py:44
  2.2 0.5 collective-permute-start
  2.7 2.9 %collective-permute-start.1 = (bf16[576,128]{1,0:T(8,128)(2,1)}, bf16[576,128]{1,0:T(8,128)(2,1)S(1)}, u32[]{:S(2)}, u32[]{:S(2)}) collective-permute-start(bf16[576,128]{1,0:T(8,128)(2,1)} %get-tuple-element.60.message.refs_3_), channel_id=1, source_target_pairs={{0,28},{4,0},{8,4},{12,8},{16,12},{20,16},{24,20},{28,24},{1,29},{... | collective-permute-start | bytes 442376 | tf_op jit(solution)/shard_map/ppermute | solution.py:22
  5.6 2.3 %collective-permute-start.2 = (bf16[576,128]{1,0:T(8,128)(2,1)}, bf16[576,128]{1,0:T(8,128)(2,1)S(1)}, u32[]{:S(2)}, u32[]{:S(2)}) collective-permute-start(bf16[576,128]{1,0:T(8,128)(2,1)} %get-tuple-element.60.message.refs_3_), channel_id=1, source_target_pairs={{0,1},{1,0},{2,3},{3,2},{4,5},{5,4},{6,7},{7,6},{8,9},{9,8},{10,11... | collective-permute-start | bytes 442376 | tf_op jit(solution)/shard_map/ppermute | solution.py:576
  7.9 2.6 %collective-permute-start.3 = (bf16[576,128]{1,0:T(8,128)(2,1)}, bf16[576,128]{1,0:T(8,128)(2,1)S(1)}, u32[]{:S(2)}, u32[]{:S(2)}) collective-permute-start(bf16[576,128]{1,0:T(8,128)(2,1)} %get-tuple-element.60.message.refs_3_), channel_id=1, source_target_pairs={{0,2},{1,3},{2,0},{3,1},{4,6},{5,7},{6,4},{7,5},{8,10},{9,11},{10,... | collective-permute-start | bytes 442376 | tf_op jit(solution)/shard_map/ppermute | solution.py:576
  11.2 0.0 copy-start.12
  11.2 0.0 copy-start.9
  11.2 0.0 copy-start.10
  11.2 0.6 copy-done.12
  11.8 0.0 copy-done.13
  11.8 0.0 copy-done.9
  11.8 0.0 copy-done.10
  11.9 0.0 copy-done.11
  11.9 1.2 %copy-done.1 = s32[1,1,16,128,128]{4,3,2,1,0:T(8,128)S(1)} copy-done((s32[1,1,16,128,128]{4,3,2,1,0:T(8,128)S(1)}, s32[1,1,16,128,128]{4,3,2,1,0:T(8,128)}, u32[]{:S(2)}) %copy-start.1) | copy-done | bytes 1048600
  13.1 1.0 %shard_map.184 = (bf16[17,128,128]{2,1,0:T(8,128)(2,1)S(1)}, bf16[17,128,128]{2,1,0:T(8,128)(2,1)S(1)}, bf16[17,128,128]{2,1,0:T(8,128)(2,1)S(1)}, s32[8,128]{1,0:T(8,128)S(1)}, f32[8,128]{1,0:T(8,128)S(1)}) custom-call(s32[1,1]{1,0:T(1,128)S(6)} %copy.20.tile_count, s32[16,128,128]{2,1,0:T(8,128)S(1)} %bitcast.5, s32[1,1,16]{2,1,0:T(1,128)S(1)} %copy-done.9, ...), custom_call_target="tpu_custom_call" | custom-call | flops 268435456 | bytes 2729600 | tf_op jit(solution)/shard_map/pallas_call | solution.py:44
  14.1 4.5 %shard_map.186 = (bf16[4,128,128]{2,1,0:T(8,128)(2,1)S(1)}, bf16[12,128,128]{2,1,0:T(8,128)(2,1)S(1)}, f32[4,128,128]{2,1,0:T(8,128)S(1)}, f32[4,128,128]{2,1,0:...) custom-call(s32[1,1]{1,0:T(1,128)S(6)} %copy.20.tile_count, s32[8,128]{1,0:T(8,128)S(1)} %get-tuple-element.56.most, ...), custom_call_target="tpu_custom_call" | custom-call | flops 1073741824 | bytes 3739648 | tf_op jit(solution)/shard_map/pallas_call | solution.py:44
  18.7 0.0 copy-start.15
  18.7 2.7 %collective-permute-done.3.refs_4_.refs_5_ = bf16[576,128]{1,0:T(8,128)(2,1)S(1)} collective-permute-done((bf16[576,128]{1,0:T(8,128)(2,1)}, bf16[576,128]{1,0:T(8,128)(2,1)S(1)}, u32[]{:S(2)}, u32[]{:S(2)}) %collective-permute-start.3) | collective-permute-done | bytes 147488 | tf_op jit(solution)/shard_map/ppermute | solution.py:576
  21.4 4.3 %shard_map.187 = (bf16[512,128]{1,0:T(8,128)(2,1)S(1)}, bf16[512,128]{1,0:T(8,128)(2,1)S(1)}, bf16[512,128]{1,0:T(8,128)(2,1)S(1)}, bf16[512,128]{1,0:T(8,128)(2,1)S(1)}, bf16[16,128,128]{2,1,0:T(8,128)(2,1)S(1)}) custom-call(s32[1,1]{1,0:T(1,128)S(6)} %copy.20.tile_count, s32[8,128]{1,0:T(8,128)S(1)} %get-tuple-element.56.most, ...), custom_call_target="tpu_custom_call" | custom-call | flops 2147483648 | bytes 4227072 | tf_op jit(solution)/shard_map/pallas_call | solution.py:44
  25.8 0.1 collective-permute-start.5
  25.8 2.6 %collective-permute-start.6 = (bf16[512,128]{1,0:T(8,128)(2,1)S(1)}, bf16[512,128]{1,0:T(8,128)(2,1)S(1)}, u32[]{:S(2)}, u32[]{:S(2)}) collective-permute-start(bf16[512,128]{1,0:T(8,128)(2,1)S(1)} %get-tuple-element.70), channel_id=1, source_target_pairs={{0,28},{4,0},{8,4},{12,8},{16,12},{20,16},{24,20},{28,24},{1,29},{... | collective-permute-start | bytes 393224 | tf_op jit(solution)/shard_map/ppermute | solution.py:22
  28.5 0.0 copy-start.5
  28.5 1.6 %shard_map.188 = (f32[512,128]{1,0:T(8,128)S(1)}, f32[512,128]{1,0:T(8,128)S(1)}) custom-call(s32[1,1]{1,0:T(1,128)S(6)} %copy.20.tile_count, s32[8,128]{1,0:T(8,128)S(1)} %get-tuple-element.56.most, bf16[17,128,128]{2,1,0:T(8,128)(2,1)S(1)} %get-tuple-element.57.row_rank, bf16[17,128,128]{2,1,0:T(8,128)(2,1)S(1)} %get-tuple-element.58.row_degree, ...), custom_call_target="tpu_custom_call" | custom-call | flops 1073741824 | bytes 3084288 | tf_op jit(solution)/shard_map/pallas_call | solution.py:44
  30.2 2.3 %collective-permute-done.5.sum_low = bf16[512,128]{1,0:T(8,128)(2,1)S(1)} collective-permute-done((bf16[512,128]{1,0:T(8,128)(2,1)S(1)}, bf16[512,128]{1,0:T(8,128)(2,1)S(1)}, u32[]{:S(2)}, u32[]{:S(2)}) %collective-permute-start.5) | collective-permute-done | bytes 131104 | tf_op jit(solution)/shard_map/ppermute | solution.py:22
  32.5 1.8 %shard_map.189 = (bf16[512,128]{1,0:T(8,128)(2,1)}, bf16[1024,128]{1,0:T(8,128)(2,1)S(1)}, bf16[1024,128]{1,0:T(8,128)(2,1)}, bf16[512,128]{1,0:T(8,128)(2,1)S(1...) custom-call(f32[8,128]{1,0:T(8,128)S(1)} %get-tuple-element.55.vecto, ...), custom_call_target="tpu_custom_call" | custom-call | flops 117440512 | bytes 2625536 | tf_op jit(solution)/shard_map/pallas_call | solution.py:44
  34.4 2.6 %collective-permute-start.9 = (bf16[1024,128]{1,0:T(8,128)(2,1)S(1)}, bf16[1024,128]{1,0:T(8,128)(2,1)S(1)}, u32[]{:S(2)}, u32[]{:S(2)}) collective-permute-start(bf16[1024,128]{1,0:T(8,128)(2,1)S(1)} %get-tuple-element.83.refs_0_), channel_id=1, source_target_pairs={{0,28},{4,0},{8,4},{12,8},{16,12},{20,16},{24,20},{28,24},{1,29},{... | collective-permute-start | bytes 786440 | tf_op jit(solution)/shard_map/ppermute | solution.py:22
  37.0 1.0 %shard_map.190 = (f32[256,128]{1,0:T(8,128)S(1)}, bf16[256,128]{1,0:T(8,128)(2,1)}) custom-call(bf16[512,128]{1,0:T(8,128)(2,1)S(1)} %copy-done, bf16[512,128]{1,0:T(8,128)(2,1)S(1)} %get-tuple-element.74.aggregate, bf16[512,128]{1,0:T(8,128)(2,1)S(1)} %get-tuple-element.75.message, bf16[512,128]{1,0:T(8,128)(2,1)S(1)} %get-tuple-element.76.hidden, ...), custom_call_target="tpu_custom_call" | custom-call | flops 67108864 | bytes 1114112 | tf_op jit(solution)/shard_map/pallas_call | solution.py:44
  38.1 1.5 %shard_map.192.refs_2_ = f32[16,128,128]{2,1,0:T(8,128)S(1)} custom-call(s32[1,1]{1,0:T(1,128)S(6)} %copy.20.tile_count, s32[8,128]{1,0:T(8,128)S(1)} %get-tuple-element.56.most, bf16[17,128,128]{2,1,0:T(8,128)(2,1)S(1)} %get-tuple-element.87.col_rank, bf16[16,128,128]{2,1,0:T(8,128)(2,1)S(1)} %get-tuple-element.67.refs_0_.senders, ...), custom_call_target="tpu_custom_call" | custom-call | flops 134217728 | bytes 2789376 | tf_op jit(solution)/shard_map/pallas_call | solution.py:44
  39.5 0.0 copy-start.16
  39.6 3.0 %collective-permute-done.7.arrived = bf16[256,128]{1,0:T(8,128)(2,1)S(1)} collective-permute-done((bf16[256,128]{1,0:T(8,128)(2,1)}, bf16[256,128]{1,0:T(8,128)(2,1)S(1)}, u32[]{:S(2)}, u32[]{:S(2)}) %collective-permute-start.7) | collective-permute-done | bytes 65568 | tf_op jit(solution)/shard_map/ppermute | solution.py:576
  42.5 0.7 collective-permute-done.8.refs_0_.from_low
  43.2 2.7 %collective-permute-start.10 = (bf16[128,128]{1,0:T(8,128)(2,1)S(1)}, bf16[128,128]{1,0:T(8,128)(2,1)S(1)}, u32[]{:S(2)}, u32[]{:S(2)}) collective-permute-start(bf16[128,128]{1,0:T(8,128)(2,1)S(1)} %get-tuple-element.86), channel_id=1, source_target_pairs={{0,2},{1,3},{2,0},{3,1},{4,6},{5,7},{6,4},{7,5},{8,10},{9,11},{10,... | collective-permute-start | bytes 98312 | tf_op jit(solution)/shard_map/ppermute | solution.py:576
  46.0 7.6 %shard_map.193 = (f32[512,128]{1,0:T(8,128)S(1)}, bf16[512,128]{1,0:T(8,128)(2,1)S(1)}, bf16[1024,128]{1,0:T(8,128)(2,1)S(1)}, bf16[128,128]{1,0:T(8,128)(2,1)S(1)}) custom-call(s32[1,1]{1,0:T(1,128)S(6)} %copy.20.tile_count, s32[8,128]{1,0:T(8,128)S(1)} %get-tuple-element.56.most, bf16[17,128,128]{2,1,0:T(8,128)(2,1)S(1)} %get-tuple-element.87.col_rank, ...), custom_call_target="tpu_custom_call" | custom-call | flops 2147483648 | bytes 4329472 | tf_op jit(solution)/shard_map/pallas_call | solution.py:44
  53.6 0.4 shard_map.194
  54.1 0.1 collective-permute-start.11
  54.2 0.1 collective-permute-start.15
  54.3 1.1 %collective-permute-done.11 = bf16[192,128]{1,0:T(8,128)(2,1)S(1)} collective-permute-done((bf16[192,128]{1,0:T(8,128)(2,1)S(1)}, bf16[192,128]{1,0:T(8,128)(2,1)S(1)}, u32[]{:S(2)}, u32[]{:S(2)}) %collective-permute-start.11) | collective-permute-done | bytes 49184 | tf_op jit(solution)/shard_map/ppermute | solution.py:576
  55.4 0.9 %collective-permute-start.12 = (bf16[192,128]{1,0:T(8,128)(2,1)S(1)}, bf16[192,128]{1,0:T(8,128)(2,1)S(1)}, u32[]{:S(2)}, u32[]{:S(2)}) collective-permute-start(bf16[192,128]{1,0:T(8,128)(2,1)S(1)} %add_convert_fusion.2.refs_0_), channel_id=1, source_target_pairs={{0,1},{1,0},{2,3},{3,2},{4,5},{5,4},{6,7},{7,6},{8,9},{9,8},{10,11... | collective-permute-start | bytes 147464 | tf_op jit(solution)/shard_map/ppermute | solution.py:576
  56.4 3.5 %collective-permute-start.14 = (bf16[192,128]{1,0:T(8,128)(2,1)S(1)}, bf16[192,128]{1,0:T(8,128)(2,1)S(1)}, u32[]{:S(2)}, u32[]{:S(2)}) collective-permute-start(bf16[192,128]{1,0:T(8,128)(2,1)S(1)} %add_convert_fusion.2.refs_0_), channel_id=1, source_target_pairs={{0,3},{1,2},{2,1},{3,0},{4,7},{5,6},{6,5},{7,4},{8,11},{9,10},{10,... | collective-permute-start | bytes 147464 | tf_op jit(solution)/shard_map/ppermute | solution.py:576
  59.9 6.2 %collective-permute-done.12.refs_1_ = bf16[192,128]{1,0:T(8,128)(2,1)S(1)} collective-permute-done((bf16[192,128]{1,0:T(8,128)(2,1)S(1)}, bf16[192,128]{1,0:T(8,128)(2,1)S(1)}, u32[]{:S(2)}, u32[]{:S(2)}) %collective-permute-start.12) | collective-permute-done | bytes 49184 | tf_op jit(solution)/shard_map/ppermute | solution.py:576
  66.2 0.4 collective-permute-start.19
  66.6 3.5 %collective-permute-start.18 = (bf16[384,128]{1,0:T(8,128)(2,1)S(1)}, bf16[384,128]{1,0:T(8,128)(2,1)S(1)}, u32[]{:S(2)}, u32[]{:S(2)}) collective-permute-start(bf16[384,128]{1,0:T(8,128)(2,1)S(1)} %shard_map.195), channel_id=1, source_target_pairs={{0,24},{4,28},{8,16},{12,20},{16,8},{20,12},{24,0},{28,4},{1,25},{... | collective-permute-start | bytes 294920 | tf_op jit(solution)/shard_map/ppermute | solution.py:576
  70.1 4.5 %collective-permute-done.19.refs_1_ = bf16[512,128]{1,0:T(8,128)(2,1)S(1)} collective-permute-done((bf16[512,128]{1,0:T(8,128)(2,1)S(1)}, bf16[512,128]{1,0:T(8,128)(2,1)S(1)}, u32[]{:S(2)}, u32[]{:S(2)}) %collective-permute-start.19) | collective-permute-done | bytes 131104 | tf_op jit(solution)/shard_map/ppermute | solution.py:576
  74.6 0.9 %shard_map.196 = f32[512,128]{1,0:T(8,128)} custom-call(f32[512,128]{1,0:T(8,128)S(1)} %get-tuple-element.96.direct, bf16[128,128]{1,0:T(8,128)(2,1)S(1)} %copy-done.8, f32[512,128]{1,0:T(8,128)S(1)} %get-tuple-element.97.own, bf16[1024,128]{1,0:T(8,128)(2,1)S(1)} %collective-permute-done.15.refs_0_, bf16[512,128]{1,0:T(8,128)(2,1)S(1)} %collective-permute-done.19.refs_1_), custom_call_target="tpu_custom_call" | custom-call | flops 16777216 | bytes 1212416 | tf_op jit(solution)/shard_map/pallas_call | solution.py:44
  75.5 0.1 add_convert_fusion.1.mine
  75.6 0.1 collective-permute-start.20
  75.7 1.3 %collective-permute-done.20.other = bf16[384,128]{1,0:T(8,128)(2,1)S(1)} collective-permute-done((bf16[384,128]{1,0:T(8,128)(2,1)S(1)}, bf16[384,128]{1,0:T(8,128)(2,1)S(1)}, u32[]{:S(2)}, u32[]{:S(2)}) %collective-permute-start.20) | collective-permute-done | bytes 98336 | tf_op jit(solution)/shard_map/ppermute | solution.py:576
  77.0 0.8 shard_map.197
  (59 shorter events, 0.3 us)
Async XLA Ops:
  2.2 11.9 %collective-permute-start = (bf16[576,128]{1,0:T(8,128)(2,1)}, bf16[576,128]{1,0:T(8,128)(2,1)S(1)}, u32[]{:S(2)}, u32[]{:S(2)}) collective-permute-start(bf16[576,128]{1,0:T(8,128)(2,1)} %get-tuple-element.60.message.refs_3_), channel_id=1, source_target_pairs={{0,4},{4,8},{8,12},{12,16},{16,20},{20,24},{24,28},{28,0},{1,5},{5... | collective-permute-start | bytes 442376 | tf_op jit(solution)/shard_map/ppermute | solution.py:22
  2.7 11.4 %collective-permute-start.1 = (bf16[576,128]{1,0:T(8,128)(2,1)}, bf16[576,128]{1,0:T(8,128)(2,1)S(1)}, u32[]{:S(2)}, u32[]{:S(2)}) collective-permute-start(bf16[576,128]{1,0:T(8,128)(2,1)} %get-tuple-element.60.message.refs_3_), channel_id=1, source_target_pairs={{0,28},{4,0},{8,4},{12,8},{16,12},{20,16},{24,20},{28,24},{1,29},{... | collective-permute-start | bytes 442376 | tf_op jit(solution)/shard_map/ppermute | solution.py:22
  5.6 13.1 %collective-permute-start.2 = (bf16[576,128]{1,0:T(8,128)(2,1)}, bf16[576,128]{1,0:T(8,128)(2,1)S(1)}, u32[]{:S(2)}, u32[]{:S(2)}) collective-permute-start(bf16[576,128]{1,0:T(8,128)(2,1)} %get-tuple-element.60.message.refs_3_), channel_id=1, source_target_pairs={{0,1},{1,0},{2,3},{3,2},{4,5},{5,4},{6,7},{7,6},{8,9},{9,8},{10,11... | collective-permute-start | bytes 442376 | tf_op jit(solution)/shard_map/ppermute | solution.py:576
  7.9 13.5 %collective-permute-start.3 = (bf16[576,128]{1,0:T(8,128)(2,1)}, bf16[576,128]{1,0:T(8,128)(2,1)S(1)}, u32[]{:S(2)}, u32[]{:S(2)}) collective-permute-start(bf16[576,128]{1,0:T(8,128)(2,1)} %get-tuple-element.60.message.refs_3_), channel_id=1, source_target_pairs={{0,2},{1,3},{2,0},{3,1},{4,6},{5,7},{6,4},{7,5},{8,10},{9,11},{10,... | collective-permute-start | bytes 442376 | tf_op jit(solution)/shard_map/ppermute | solution.py:576
  10.5 10.9 %collective-permute-start.4 = (bf16[576,128]{1,0:T(8,128)(2,1)}, bf16[576,128]{1,0:T(8,128)(2,1)S(1)}, u32[]{:S(2)}, u32[]{:S(2)}) collective-permute-start(bf16[576,128]{1,0:T(8,128)(2,1)} %get-tuple-element.60.message.refs_3_), channel_id=1, source_target_pairs={{0,3},{1,2},{2,1},{3,0},{4,7},{5,6},{6,5},{7,4},{8,11},{9,10},{10,... | collective-permute-start | bytes 442376 | tf_op jit(solution)/shard_map/ppermute | solution.py:576
  11.2 0.7 copy-start.12
  11.2 0.7 copy-start.13
  11.2 0.7 copy-start.9
  11.2 0.7 copy-start.10
  11.2 0.7 copy-start.11
  11.9 1.2 %copy-start.1 = (s32[1,1,16,128,128]{4,3,2,1,0:T(8,128)S(1)}, s32[1,1,16,128,128]{4,3,2,1,0:T(8,128)}, u32[]{:S(2)}) copy-start(s32[1,1,16,128,128]{4,3,2,1,0:T(8,128)} %param.21) | copy-start | bytes 3145732
  13.1 1.0 %copy-start.7 = (bf16[128,128]{1,0:T(8,128)(2,1)S(1)}, bf16[128,128]{1,0:T(8,128)(2,1)}, u32[]{:S(2)}) copy-start(bf16[128,128]{1,0:T(8,128)(2,1)} %w_recv.3) | copy-start | bytes 98308
  13.1 1.0 %copy-start.8 = (bf16[128,128]{1,0:T(8,128)(2,1)S(1)}, bf16[128,128]{1,0:T(8,128)(2,1)}, u32[]{:S(2)}) copy-start(bf16[128,128]{1,0:T(8,128)(2,1)} %w_send.3) | copy-start | bytes 98308
  13.1 1.0 %copy-start.14 = (bf16[576,128]{1,0:T(8,128)(2,1)S(1)}, bf16[576,128]{1,0:T(8,128)(2,1)}, u32[]{:S(2)}) copy-start(bf16[576,128]{1,0:T(8,128)(2,1)} %get-tuple-element.60.message.refs_3_) | copy-start | bytes 442372
  13.1 1.0 %copy-start.21 = (bf16[16,384]{1,0:T(8,128)(2,1)S(1)}, bf16[16,384]{1,0:T(8,128)(2,1)}, u32[]{:S(2)}) copy-start(bf16[16,384]{1,0:T(8,128)(2,1)} %get-tuple-element.59.weight_parts.refs_2_) | copy-start | bytes 36868
  18.7 7.1 %copy-start.15 = (bf16[576,128]{1,0:T(8,128)(2,1)}, bf16[576,128]{1,0:T(8,128)(2,1)S(1)}, u32[]{:S(2)}) copy-start(bf16[576,128]{1,0:T(8,128)(2,1)S(1)} %collective-permute-done.2.refs_3_.refs_4_) | copy-start | bytes 442372
  21.4 4.3 %copy-start.17 = (bf16[576,128]{1,0:T(8,128)(2,1)}, bf16[576,128]{1,0:T(8,128)(2,1)S(1)}, u32[]{:S(2)}) copy-start(bf16[576,128]{1,0:T(8,128)(2,1)S(1)} %collective-permute-done.3.refs_4_.refs_5_) | copy-start | bytes 442372
  21.4 4.3 %copy-start.19 = (bf16[576,128]{1,0:T(8,128)(2,1)}, bf16[576,128]{1,0:T(8,128)(2,1)S(1)}, u32[]{:S(2)}) copy-start(bf16[576,128]{1,0:T(8,128)(2,1)S(1)} %collective-permute-done.4.refs_5_.refs_6_) | copy-start | bytes 442372
  25.8 6.7 %collective-permute-start.5 = (bf16[512,128]{1,0:T(8,128)(2,1)S(1)}, bf16[512,128]{1,0:T(8,128)(2,1)S(1)}, u32[]{:S(2)}, u32[]{:S(2)}) collective-permute-start(bf16[512,128]{1,0:T(8,128)(2,1)S(1)} %get-tuple-element.69), channel_id=1, source_target_pairs={{0,4},{4,8},{8,12},{12,16},{16,20},{20,24},{24,28},{28,0},{1,5},{5... | collective-permute-start | bytes 393224 | tf_op jit(solution)/shard_map/ppermute | solution.py:22
  25.8 6.7 %collective-permute-start.6 = (bf16[512,128]{1,0:T(8,128)(2,1)S(1)}, bf16[512,128]{1,0:T(8,128)(2,1)S(1)}, u32[]{:S(2)}, u32[]{:S(2)}) collective-permute-start(bf16[512,128]{1,0:T(8,128)(2,1)S(1)} %get-tuple-element.70), channel_id=1, source_target_pairs={{0,28},{4,0},{8,4},{12,8},{16,12},{20,16},{24,20},{28,24},{1,29},{... | collective-permute-start | bytes 393224 | tf_op jit(solution)/shard_map/ppermute | solution.py:22
  28.5 4.0 %copy-start = (bf16[512,128]{1,0:T(8,128)(2,1)S(1)}, bf16[512,128]{1,0:T(8,128)(2,1)}, u32[]{:S(2)}) copy-start(bf16[512,128]{1,0:T(8,128)(2,1)} %latent.7) | copy-start | bytes 393220
  28.5 4.0 %copy-start.2 = (bf16[512,128]{1,0:T(8,128)(2,1)S(1)}, bf16[512,128]{1,0:T(8,128)(2,1)}, u32[]{:S(2)}) copy-start(bf16[512,128]{1,0:T(8,128)(2,1)} %cotangent.3) | copy-start | bytes 393220
  28.5 4.0 %copy-start.3 = (bf16[128,128]{1,0:T(8,128)(2,1)S(1)}, bf16[128,128]{1,0:T(8,128)(2,1)}, u32[]{:S(2)}) copy-start(bf16[128,128]{1,0:T(8,128)(2,1)} %w_edge_out.3) | copy-start | bytes 98308
  28.5 4.0 %copy-start.4 = (bf16[128,128]{1,0:T(8,128)(2,1)S(1)}, bf16[128,128]{1,0:T(8,128)(2,1)}, u32[]{:S(2)}) copy-start(bf16[128,128]{1,0:T(8,128)(2,1)} %w_node_self.3) | copy-start | bytes 98308
  28.5 4.0 %copy-start.5 = (bf16[128,128]{1,0:T(8,128)(2,1)S(1)}, bf16[128,128]{1,0:T(8,128)(2,1)}, u32[]{:S(2)}) copy-start(bf16[128,128]{1,0:T(8,128)(2,1)} %w_node_msg.1) | copy-start | bytes 98308
  28.5 4.0 %copy-start.6 = (bf16[128,128]{1,0:T(8,128)(2,1)S(1)}, bf16[128,128]{1,0:T(8,128)(2,1)}, u32[]{:S(2)}) copy-start(bf16[128,128]{1,0:T(8,128)(2,1)} %w_node_out.1) | copy-start | bytes 98308
  34.4 8.8 %collective-permute-start.8 = (bf16[1024,128]{1,0:T(8,128)(2,1)}, bf16[1024,128]{1,0:T(8,128)(2,1)S(1)}, u32[]{:S(2)}, u32[]{:S(2)}) collective-permute-start(bf16[1024,128]{1,0:T(8,128)(2,1)} %get-tuple-element.82), channel_id=1, source_target_pairs={{0,4},{4,8},{8,12},{12,16},{16,20},{20,24},{24,28},{28,0},{1,5},{5... | collective-permute-start | bytes 786440 | tf_op jit(solution)/shard_map/ppermute | solution.py:22
  34.4 8.8 %collective-permute-start.9 = (bf16[1024,128]{1,0:T(8,128)(2,1)S(1)}, bf16[1024,128]{1,0:T(8,128)(2,1)S(1)}, u32[]{:S(2)}, u32[]{:S(2)}) collective-permute-start(bf16[1024,128]{1,0:T(8,128)(2,1)S(1)} %get-tuple-element.83.refs_0_), channel_id=1, source_target_pairs={{0,28},{4,0},{8,4},{12,8},{16,12},{20,16},{24,20},{28,24},{1,29},{... | collective-permute-start | bytes 786440 | tf_op jit(solution)/shard_map/ppermute | solution.py:22
  38.1 4.5 %collective-permute-start.7 = (bf16[256,128]{1,0:T(8,128)(2,1)}, bf16[256,128]{1,0:T(8,128)(2,1)S(1)}, u32[]{:S(2)}, u32[]{:S(2)}) collective-permute-start(bf16[256,128]{1,0:T(8,128)(2,1)} %get-tuple-element.81), channel_id=1, source_target_pairs={{0,1},{1,0},{2,3},{3,2},{4,5},{5,4},{6,7},{7,6},{8,9},{9,8},{10,11... | collective-permute-start | bytes 196616 | tf_op jit(solution)/shard_map/ppermute | solution.py:576
  38.1 7.9 %copy-start.18 = (bf16[576,128]{1,0:T(8,128)(2,1)S(1)}, bf16[576,128]{1,0:T(8,128)(2,1)}, u32[]{:S(2)}) copy-start(bf16[576,128]{1,0:T(8,128)(2,1)} %copy-done.17) | copy-start | bytes 442372
  38.1 7.9 %copy-start.20 = (bf16[576,128]{1,0:T(8,128)(2,1)S(1)}, bf16[576,128]{1,0:T(8,128)(2,1)}, u32[]{:S(2)}) copy-start(bf16[576,128]{1,0:T(8,128)(2,1)} %copy-done.19) | copy-start | bytes 442372
  39.5 6.4 %copy-start.16 = (bf16[576,128]{1,0:T(8,128)(2,1)S(1)}, bf16[576,128]{1,0:T(8,128)(2,1)}, u32[]{:S(2)}) copy-start(bf16[576,128]{1,0:T(8,128)(2,1)} %copy-done.15) | copy-start | bytes 442372
  43.2 10.8 %collective-permute-start.10 = (bf16[128,128]{1,0:T(8,128)(2,1)S(1)}, bf16[128,128]{1,0:T(8,128)(2,1)S(1)}, u32[]{:S(2)}, u32[]{:S(2)}) collective-permute-start(bf16[128,128]{1,0:T(8,128)(2,1)S(1)} %get-tuple-element.86), channel_id=1, source_target_pairs={{0,2},{1,3},{2,0},{3,1},{4,6},{5,7},{6,4},{7,5},{8,10},{9,11},{10,... | collective-permute-start | bytes 98312 | tf_op jit(solution)/shard_map/ppermute | solution.py:576
  54.1 1.3 %collective-permute-start.11 = (bf16[192,128]{1,0:T(8,128)(2,1)S(1)}, bf16[192,128]{1,0:T(8,128)(2,1)S(1)}, u32[]{:S(2)}, u32[]{:S(2)}) collective-permute-start(bf16[192,128]{1,0:T(8,128)(2,1)S(1)} %broadcast_select_fusion), channel_id=1, source_target_pairs={{0,4},{4,0},{8,12},{12,8},{16,20},{20,16},{24,28},{28,24},{1,5},{5... | collective-permute-start | bytes 147464 | tf_op jit(solution)/shard_map/ppermute | solution.py:576
  54.2 11.9 %collective-permute-start.15 = (bf16[1024,128]{1,0:T(8,128)(2,1)S(1)}, bf16[1024,128]{1,0:T(8,128)(2,1)S(1)}, u32[]{:S(2)}, u32[]{:S(2)}) collective-permute-start(bf16[1024,128]{1,0:T(8,128)(2,1)S(1)} %get-tuple-element.94), channel_id=1, source_target_pairs={{0,1},{1,0},{2,3},{3,2},{4,5},{5,4},{6,7},{7,6},{8,9},{9,8},{10,11... | collective-permute-start | bytes 786440 | tf_op jit(solution)/shard_map/ppermute | solution.py:576
  55.4 10.6 %collective-permute-start.12 = (bf16[192,128]{1,0:T(8,128)(2,1)S(1)}, bf16[192,128]{1,0:T(8,128)(2,1)S(1)}, u32[]{:S(2)}, u32[]{:S(2)}) collective-permute-start(bf16[192,128]{1,0:T(8,128)(2,1)S(1)} %add_convert_fusion.2.refs_0_), channel_id=1, source_target_pairs={{0,1},{1,0},{2,3},{3,2},{4,5},{5,4},{6,7},{7,6},{8,9},{9,8},{10,11... | collective-permute-start | bytes 147464 | tf_op jit(solution)/shard_map/ppermute | solution.py:576
  56.4 9.7 %collective-permute-start.13 = (bf16[192,128]{1,0:T(8,128)(2,1)S(1)}, bf16[192,128]{1,0:T(8,128)(2,1)S(1)}, u32[]{:S(2)}, u32[]{:S(2)}) collective-permute-start(bf16[192,128]{1,0:T(8,128)(2,1)S(1)} %add_convert_fusion.2.refs_0_), channel_id=1, source_target_pairs={{0,2},{1,3},{2,0},{3,1},{4,6},{5,7},{6,4},{7,5},{8,10},{9,11},{10,... | collective-permute-start | bytes 147464 | tf_op jit(solution)/shard_map/ppermute | solution.py:576
  56.4 9.7 %collective-permute-start.14 = (bf16[192,128]{1,0:T(8,128)(2,1)S(1)}, bf16[192,128]{1,0:T(8,128)(2,1)S(1)}, u32[]{:S(2)}, u32[]{:S(2)}) collective-permute-start(bf16[192,128]{1,0:T(8,128)(2,1)S(1)} %add_convert_fusion.2.refs_0_), channel_id=1, source_target_pairs={{0,3},{1,2},{2,1},{3,0},{4,7},{5,6},{6,5},{7,4},{8,11},{9,10},{10,... | collective-permute-start | bytes 147464 | tf_op jit(solution)/shard_map/ppermute | solution.py:576
  66.2 8.4 %collective-permute-start.19 = (bf16[512,128]{1,0:T(8,128)(2,1)S(1)}, bf16[512,128]{1,0:T(8,128)(2,1)S(1)}, u32[]{:S(2)}, u32[]{:S(2)}) collective-permute-start(bf16[512,128]{1,0:T(8,128)(2,1)S(1)} %add_convert_fusion), channel_id=1, source_target_pairs={{0,2},{1,3},{2,0},{3,1},{4,6},{5,7},{6,4},{7,5},{8,10},{9,11},{10,... | collective-permute-start | bytes 393224 | tf_op jit(solution)/shard_map/ppermute | solution.py:576
  66.6 8.9 %collective-permute-start.16 = (bf16[384,128]{1,0:T(8,128)(2,1)S(1)}, bf16[384,128]{1,0:T(8,128)(2,1)S(1)}, u32[]{:S(2)}, u32[]{:S(2)}) collective-permute-start(bf16[384,128]{1,0:T(8,128)(2,1)S(1)} %shard_map.195), channel_id=1, source_target_pairs={{0,8},{4,12},{8,0},{12,4},{16,24},{20,28},{24,16},{28,20},{1,9},{5... | collective-permute-start | bytes 294920 | tf_op jit(solution)/shard_map/ppermute | solution.py:576
  66.6 8.9 %collective-permute-start.17 = (bf16[384,128]{1,0:T(8,128)(2,1)S(1)}, bf16[384,128]{1,0:T(8,128)(2,1)S(1)}, u32[]{:S(2)}, u32[]{:S(2)}) collective-permute-start(bf16[384,128]{1,0:T(8,128)(2,1)S(1)} %shard_map.195), channel_id=1, source_target_pairs={{0,16},{4,20},{8,24},{12,28},{16,0},{20,4},{24,8},{28,12},{1,17},{... | collective-permute-start | bytes 294920 | tf_op jit(solution)/shard_map/ppermute | solution.py:576
  66.6 8.9 %collective-permute-start.18 = (bf16[384,128]{1,0:T(8,128)(2,1)S(1)}, bf16[384,128]{1,0:T(8,128)(2,1)S(1)}, u32[]{:S(2)}, u32[]{:S(2)}) collective-permute-start(bf16[384,128]{1,0:T(8,128)(2,1)S(1)} %shard_map.195), channel_id=1, source_target_pairs={{0,24},{4,28},{8,16},{12,20},{16,8},{20,12},{24,0},{28,4},{1,25},{... | collective-permute-start | bytes 294920 | tf_op jit(solution)/shard_map/ppermute | solution.py:576
  75.6 1.4 %collective-permute-start.20 = (bf16[384,128]{1,0:T(8,128)(2,1)S(1)}, bf16[384,128]{1,0:T(8,128)(2,1)S(1)}, u32[]{:S(2)}, u32[]{:S(2)}) collective-permute-start(bf16[384,128]{1,0:T(8,128)(2,1)S(1)} %add_convert_fusion.1.mine), channel_id=1, source_target_pairs={{0,4},{4,0},{8,12},{12,8},{16,20},{20,16},{24,28},{28,24},{1,5},{5... | collective-permute-start | bytes 294920 | tf_op jit(solution)/shard_map/ppermute | solution.py:576

commit v18 on v16

--- a/solution.py
+++ b/solution.py
@@ -12,7 +12,7 @@
 LOOPED = 2
 SENDERS, RECEIVERS, ROWS, COLUMNS = 0, 1, 2, 3
 TOGETHER = 4
-CHUNK = 32
+CHUNK = 16
 PARTS = 16
 
 

time: 75.4 us -> 75.3 us (level)
  waiting for transfers between devices: 20.1 us -> 18.6 us
  Pallas kernels: 27.7 us -> 28.8 us
    ppermute x15, waiting for transfers between devices: 19.4 us -> 17.4 us  [exchanged(): lax.ppermute(value, axis, [(source, source ^ step) for source in range(co...]
    pallas_call x14, Pallas kernels: 27.7 us -> 28.8 us  [call(): pl.pallas_call(kernel, out_shape=[jax.ShapeDtypeStruct(o.shape, o.dtype)...]
  transfers between devices with their start and end apart: 21 -> 21, of which waited for: 7 -> 8; matrix products, arithmetic and copies ran while one was open for 0% -> 0% of each run, Pallas kernels for 25% -> 25%
where the time goes in v18:
time: 75.3 us; the launch traced here: 75.2 us
  Pallas kernels  28.8 us (38%)
  starting transfers between devices  24 us (32%)
  waiting for transfers between devices  18.6 us (25%)
  local copies, waits for them, and re-layouts  1.99 us (3%)
  between operations  1.71 us (2%)
    pallas_call x14, Pallas kernels, call(): pl.pallas_call(kernel, out_shape=[jax.ShapeDtypeStruct(o.shape, o.dtype)...  28.8 us
    ppermute x15, waiting for transfers between devices, exchanged(): lax.ppermute(value, axis, [(source, source ^ step) for source in range(co...  17.4 us
    ppermute x15, starting transfers between devices, exchanged(): lax.ppermute(value, axis, [(source, source ^ step) for source in range(co...  15.4 us
    ppermute x6, starting transfers between devices, shifted(): return lax.ppermute(value, axis, pairs)  8.67 us
    unnamed x44, local copies, waits for them, and re-layouts  1.97 us
  transfers between devices with their start and end apart: 21, of which 8 were waited for; matrix products, arithmetic and copies ran while one was open for 0% of the time, Pallas kernels for 25%

profile of v18, /device:TPU:0, one launch (start us, length us, event | category | flops | bytes accessed | tf_op | source)
XLA Modules:
  0.0 75.2 jit_solution(16745752844368728227)
XLA Ops:
  0.6 1.6 %shard_map.185 = (bf16[576,128]{1,0:T(8,128)(2,1)}, bf16[16,384]{1,0:T(8,128)(2,1)}) custom-call(bf16[512,128]{1,0:T(8,128)(2,1)} %latent.7, f32[3,512]{1,0:T(4,128)} %positions.1, f32[3,128]{1,0:T(4,128)} %pos_weight.1), custom_call_target="tpu_custom_call" | custom-call | bytes 298496 | tf_op jit(solution)/shard_map/pallas_call | solution.py:44
  2.2 0.5 collective-permute-start
  2.7 2.9 %collective-permute-start.1 = (bf16[576,128]{1,0:T(8,128)(2,1)}, bf16[576,128]{1,0:T(8,128)(2,1)S(1)}, u32[]{:S(2)}, u32[]{:S(2)}) collective-permute-start(bf16[576,128]{1,0:T(8,128)(2,1)} %get-tuple-element.60.message.refs_3_), channel_id=1, source_target_pairs={{0,28},{4,0},{8,4},{12,8},{16,12},{20,16},{24,20},{28,24},{1,29},{... | collective-permute-start | bytes 442376 | tf_op jit(solution)/shard_map/ppermute | solution.py:22
  5.6 2.3 %collective-permute-start.2 = (bf16[576,128]{1,0:T(8,128)(2,1)}, bf16[576,128]{1,0:T(8,128)(2,1)S(1)}, u32[]{:S(2)}, u32[]{:S(2)}) collective-permute-start(bf16[576,128]{1,0:T(8,128)(2,1)} %get-tuple-element.60.message.refs_3_), channel_id=1, source_target_pairs={{0,1},{1,0},{2,3},{3,2},{4,5},{5,4},{6,7},{7,6},{8,9},{9,8},{10,11... | collective-permute-start | bytes 442376 | tf_op jit(solution)/shard_map/ppermute | solution.py:576
  7.9 2.6 %collective-permute-start.3 = (bf16[576,128]{1,0:T(8,128)(2,1)}, bf16[576,128]{1,0:T(8,128)(2,1)S(1)}, u32[]{:S(2)}, u32[]{:S(2)}) collective-permute-start(bf16[576,128]{1,0:T(8,128)(2,1)} %get-tuple-element.60.message.refs_3_), channel_id=1, source_target_pairs={{0,2},{1,3},{2,0},{3,1},{4,6},{5,7},{6,4},{7,5},{8,10},{9,11},{10,... | collective-permute-start | bytes 442376 | tf_op jit(solution)/shard_map/ppermute | solution.py:576
  11.2 0.0 copy-start.12
  11.2 0.0 copy-start.13
  11.2 0.6 copy-done.12
  11.8 0.0 copy-done.13
  11.8 0.0 copy-done.9
  11.8 0.0 copy-done.10
  11.9 0.0 copy-done.11
  11.9 1.2 %copy-done.1 = s32[1,1,16,128,128]{4,3,2,1,0:T(8,128)S(1)} copy-done((s32[1,1,16,128,128]{4,3,2,1,0:T(8,128)S(1)}, s32[1,1,16,128,128]{4,3,2,1,0:T(8,128)}, u32[]{:S(2)}) %copy-start.1) | copy-done | bytes 1048600
  13.1 1.0 %shard_map.184 = (bf16[17,128,128]{2,1,0:T(8,128)(2,1)S(1)}, bf16[17,128,128]{2,1,0:T(8,128)(2,1)S(1)}, bf16[17,128,128]{2,1,0:T(8,128)(2,1)S(1)}, s32[8,128]{1,0:T(8,128)S(1)}, f32[8,128]{1,0:T(8,128)S(1)}) custom-call(s32[1,1]{1,0:T(1,128)S(6)} %copy.20.tile_count, s32[16,128,128]{2,1,0:T(8,128)S(1)} %bitcast.5, s32[1,1,16]{2,1,0:T(1,128)S(1)} %copy-done.9, ...), custom_call_target="tpu_custom_call" | custom-call | flops 268435456 | bytes 2729600 | tf_op jit(solution)/shard_map/pallas_call | solution.py:44
  14.1 2.7 %shard_map.186 = (bf16[4,128,128]{2,1,0:T(8,128)(2,1)S(1)}, bf16[12,128,128]{2,1,0:T(8,128)(2,1)S(1)}, f32[4,128,128]{2,1,0:T(8,128)S(1)}, f32[4,128,128]{2,1,0:...) custom-call(s32[1,1]{1,0:T(1,128)S(6)} %copy.20.tile_count, s32[8,128]{1,0:T(8,128)S(1)} %get-tuple-element.56.most, ...), custom_call_target="tpu_custom_call" | custom-call | flops 1073741824 | bytes 3739648 | tf_op jit(solution)/shard_map/pallas_call | solution.py:44
  16.9 4.5 %collective-permute-done.3.refs_4_.refs_5_ = bf16[576,128]{1,0:T(8,128)(2,1)S(1)} collective-permute-done((bf16[576,128]{1,0:T(8,128)(2,1)}, bf16[576,128]{1,0:T(8,128)(2,1)S(1)}, u32[]{:S(2)}, u32[]{:S(2)}) %collective-permute-start.3) | collective-permute-done | bytes 147488 | tf_op jit(solution)/shard_map/ppermute | solution.py:576
  21.4 5.5 %shard_map.187 = (bf16[512,128]{1,0:T(8,128)(2,1)S(1)}, bf16[512,128]{1,0:T(8,128)(2,1)S(1)}, bf16[512,128]{1,0:T(8,128)(2,1)S(1)}, bf16[512,128]{1,0:T(8,128)(2,1)S(1)}, bf16[16,128,128]{2,1,0:T(8,128)(2,1)S(1)}) custom-call(s32[1,1]{1,0:T(1,128)S(6)} %copy.20.tile_count, s32[8,128]{1,0:T(8,128)S(1)} %get-tuple-element.56.most, ...), custom_call_target="tpu_custom_call" | custom-call | flops 2147483648 | bytes 4227072 | tf_op jit(solution)/shard_map/pallas_call | solution.py:44
  27.0 0.1 collective-permute-start.5
  27.1 2.6 %collective-permute-start.6 = (bf16[512,128]{1,0:T(8,128)(2,1)S(1)}, bf16[512,128]{1,0:T(8,128)(2,1)S(1)}, u32[]{:S(2)}, u32[]{:S(2)}) collective-permute-start(bf16[512,128]{1,0:T(8,128)(2,1)S(1)} %get-tuple-element.70), channel_id=1, source_target_pairs={{0,28},{4,0},{8,4},{12,8},{16,12},{20,16},{24,20},{28,24},{1,29},{... | collective-permute-start | bytes 393224 | tf_op jit(solution)/shard_map/ppermute | solution.py:22
  29.7 2.7 %shard_map.188 = (f32[512,128]{1,0:T(8,128)S(1)}, f32[512,128]{1,0:T(8,128)S(1)}) custom-call(s32[1,1]{1,0:T(1,128)S(6)} %copy.20.tile_count, s32[8,128]{1,0:T(8,128)S(1)} %get-tuple-element.56.most, bf16[17,128,128]{2,1,0:T(8,128)(2,1)S(1)} %get-tuple-element.57.row_rank, bf16[17,128,128]{2,1,0:T(8,128)(2,1)S(1)} %get-tuple-element.58.row_degree, ...), custom_call_target="tpu_custom_call" | custom-call | flops 1073741824 | bytes 3084288 | tf_op jit(solution)/shard_map/pallas_call | solution.py:44
  32.5 1.8 %shard_map.189 = (bf16[512,128]{1,0:T(8,128)(2,1)}, bf16[1024,128]{1,0:T(8,128)(2,1)S(1)}, bf16[1024,128]{1,0:T(8,128)(2,1)}, bf16[512,128]{1,0:T(8,128)(2,1)S(1...) custom-call(f32[8,128]{1,0:T(8,128)S(1)} %get-tuple-element.55.vecto, ...), custom_call_target="tpu_custom_call" | custom-call | flops 117440512 | bytes 2625536 | tf_op jit(solution)/shard_map/pallas_call | solution.py:44
  34.3 2.6 %collective-permute-start.9 = (bf16[1024,128]{1,0:T(8,128)(2,1)S(1)}, bf16[1024,128]{1,0:T(8,128)(2,1)S(1)}, u32[]{:S(2)}, u32[]{:S(2)}) collective-permute-start(bf16[1024,128]{1,0:T(8,128)(2,1)S(1)} %get-tuple-element.83.refs_0_), channel_id=1, source_target_pairs={{0,28},{4,0},{8,4},{12,8},{16,12},{20,16},{24,20},{28,24},{1,29},{... | collective-permute-start | bytes 786440 | tf_op jit(solution)/shard_map/ppermute | solution.py:22
  37.0 1.0 %shard_map.190 = (f32[256,128]{1,0:T(8,128)S(1)}, bf16[256,128]{1,0:T(8,128)(2,1)}) custom-call(bf16[512,128]{1,0:T(8,128)(2,1)S(1)} %copy-done, bf16[512,128]{1,0:T(8,128)(2,1)S(1)} %get-tuple-element.74.aggregate, bf16[512,128]{1,0:T(8,128)(2,1)S(1)} %get-tuple-element.75.message, bf16[512,128]{1,0:T(8,128)(2,1)S(1)} %get-tuple-element.76.hidden, ...), custom_call_target="tpu_custom_call" | custom-call | flops 67108864 | bytes 1114112 | tf_op jit(solution)/shard_map/pallas_call | solution.py:44
  38.0 0.9 %collective-permute-start.7 = (bf16[256,128]{1,0:T(8,128)(2,1)}, bf16[256,128]{1,0:T(8,128)(2,1)S(1)}, u32[]{:S(2)}, u32[]{:S(2)}) collective-permute-start(bf16[256,128]{1,0:T(8,128)(2,1)} %get-tuple-element.81), channel_id=1, source_target_pairs={{0,1},{1,0},{2,3},{3,2},{4,5},{5,4},{6,7},{7,6},{8,9},{9,8},{10,11... | collective-permute-start | bytes 196616 | tf_op jit(solution)/shard_map/ppermute | solution.py:576
  38.9 3.6 %shard_map.192.refs_2_ = f32[16,128,128]{2,1,0:T(8,128)S(1)} custom-call(s32[1,1]{1,0:T(1,128)S(6)} %copy.20.tile_count, s32[8,128]{1,0:T(8,128)S(1)} %get-tuple-element.56.most, bf16[17,128,128]{2,1,0:T(8,128)(2,1)S(1)} %get-tuple-element.87.col_rank, bf16[16,128,128]{2,1,0:T(8,128)(2,1)S(1)} %get-tuple-element.67.refs_0_.senders, ...), custom_call_target="tpu_custom_call" | custom-call | flops 134217728 | bytes 2789376 | tf_op jit(solution)/shard_map/pallas_call | solution.py:44
  42.6 1.2 %collective-permute-done.8.refs_0_.from_low = bf16[1024,128]{1,0:T(8,128)(2,1)S(1)} collective-permute-done((bf16[1024,128]{1,0:T(8,128)(2,1)}, bf16[1024,128]{1,0:T(8,128)(2,1)S(1)}, u32[]{:S(2)}, u32[]{:S(2)}) %collective-permute-start.8) | collective-permute-done | bytes 262176 | tf_op jit(solution)/shard_map/ppermute | solution.py:22
  43.7 0.1 collective-permute-start.10
  43.9 6.7 %shard_map.193 = (f32[512,128]{1,0:T(8,128)S(1)}, bf16[512,128]{1,0:T(8,128)(2,1)S(1)}, bf16[1024,128]{1,0:T(8,128)(2,1)S(1)}, bf16[128,128]{1,0:T(8,128)(2,1)S(1)}) custom-call(s32[1,1]{1,0:T(1,128)S(6)} %copy.20.tile_count, s32[8,128]{1,0:T(8,128)S(1)} %get-tuple-element.56.most, bf16[17,128,128]{2,1,0:T(8,128)(2,1)S(1)} %get-tuple-element.87.col_rank, ...), custom_call_target="tpu_custom_call" | custom-call | flops 2147483648 | bytes 4329472 | tf_op jit(solution)/shard_map/pallas_call | solution.py:44
  50.6 0.4 shard_map.194
  51.0 0.1 collective-permute-start.11
  51.1 0.1 collective-permute-start.15
  51.2 1.1 %collective-permute-done.11 = bf16[192,128]{1,0:T(8,128)(2,1)S(1)} collective-permute-done((bf16[192,128]{1,0:T(8,128)(2,1)S(1)}, bf16[192,128]{1,0:T(8,128)(2,1)S(1)}, u32[]{:S(2)}, u32[]{:S(2)}) %collective-permute-start.11) | collective-permute-done | bytes 49184 | tf_op jit(solution)/shard_map/ppermute | solution.py:576
  52.3 0.9 %collective-permute-start.12 = (bf16[192,128]{1,0:T(8,128)(2,1)S(1)}, bf16[192,128]{1,0:T(8,128)(2,1)S(1)}, u32[]{:S(2)}, u32[]{:S(2)}) collective-permute-start(bf16[192,128]{1,0:T(8,128)(2,1)S(1)} %add_convert_fusion.2.refs_0_), channel_id=1, source_target_pairs={{0,1},{1,0},{2,3},{3,2},{4,5},{5,4},{6,7},{7,6},{8,9},{9,8},{10,11... | collective-permute-start | bytes 147464 | tf_op jit(solution)/shard_map/ppermute | solution.py:576
  53.3 2.6 %collective-permute-start.13 = (bf16[192,128]{1,0:T(8,128)(2,1)S(1)}, bf16[192,128]{1,0:T(8,128)(2,1)S(1)}, u32[]{:S(2)}, u32[]{:S(2)}) collective-permute-start(bf16[192,128]{1,0:T(8,128)(2,1)S(1)} %add_convert_fusion.2.refs_0_), channel_id=1, source_target_pairs={{0,2},{1,3},{2,0},{3,1},{4,6},{5,7},{6,4},{7,5},{8,10},{9,11},{10,... | collective-permute-start | bytes 147464 | tf_op jit(solution)/shard_map/ppermute | solution.py:576
  55.9 0.9 %collective-permute-start.14 = (bf16[192,128]{1,0:T(8,128)(2,1)S(1)}, bf16[192,128]{1,0:T(8,128)(2,1)S(1)}, u32[]{:S(2)}, u32[]{:S(2)}) collective-permute-start(bf16[192,128]{1,0:T(8,128)(2,1)S(1)} %add_convert_fusion.2.refs_0_), channel_id=1, source_target_pairs={{0,3},{1,2},{2,1},{3,0},{4,7},{5,6},{6,5},{7,4},{8,11},{9,10},{10,... | collective-permute-start | bytes 147464 | tf_op jit(solution)/shard_map/ppermute | solution.py:576
  56.8 5.1 %collective-permute-done.12.refs_1_ = bf16[192,128]{1,0:T(8,128)(2,1)S(1)} collective-permute-done((bf16[192,128]{1,0:T(8,128)(2,1)S(1)}, bf16[192,128]{1,0:T(8,128)(2,1)S(1)}, u32[]{:S(2)}, u32[]{:S(2)}) %collective-permute-start.12) | collective-permute-done | bytes 49184 | tf_op jit(solution)/shard_map/ppermute | solution.py:576
  61.9 2.2 %collective-permute-done.14.refs_3_ = bf16[192,128]{1,0:T(8,128)(2,1)S(1)} collective-permute-done((bf16[192,128]{1,0:T(8,128)(2,1)S(1)}, bf16[192,128]{1,0:T(8,128)(2,1)S(1)}, u32[]{:S(2)}, u32[]{:S(2)}) %collective-permute-start.14) | collective-permute-done | bytes 49184 | tf_op jit(solution)/shard_map/ppermute | solution.py:576
  64.2 0.1 collective-permute-start.19
  64.3 0.9 %collective-permute-start.16 = (bf16[384,128]{1,0:T(8,128)(2,1)S(1)}, bf16[384,128]{1,0:T(8,128)(2,1)S(1)}, u32[]{:S(2)}, u32[]{:S(2)}) collective-permute-start(bf16[384,128]{1,0:T(8,128)(2,1)S(1)} %shard_map.195), channel_id=1, source_target_pairs={{0,8},{4,12},{8,0},{12,4},{16,24},{20,28},{24,16},{28,20},{1,9},{5... | collective-permute-start | bytes 294920 | tf_op jit(solution)/shard_map/ppermute | solution.py:576
  65.1 2.4 %collective-permute-start.17 = (bf16[384,128]{1,0:T(8,128)(2,1)S(1)}, bf16[384,128]{1,0:T(8,128)(2,1)S(1)}, u32[]{:S(2)}, u32[]{:S(2)}) collective-permute-start(bf16[384,128]{1,0:T(8,128)(2,1)S(1)} %shard_map.195), channel_id=1, source_target_pairs={{0,16},{4,20},{8,24},{12,28},{16,0},{20,4},{24,8},{28,12},{1,17},{... | collective-permute-start | bytes 294920 | tf_op jit(solution)/shard_map/ppermute | solution.py:576
  67.5 1.5 %collective-permute-start.18 = (bf16[384,128]{1,0:T(8,128)(2,1)S(1)}, bf16[384,128]{1,0:T(8,128)(2,1)S(1)}, u32[]{:S(2)}, u32[]{:S(2)}) collective-permute-start(bf16[384,128]{1,0:T(8,128)(2,1)S(1)} %shard_map.195), channel_id=1, source_target_pairs={{0,24},{4,28},{8,16},{12,20},{16,8},{20,12},{24,0},{28,4},{1,25},{... | collective-permute-start | bytes 294920 | tf_op jit(solution)/shard_map/ppermute | solution.py:576
  69.0 2.6 %collective-permute-done.19.refs_1_ = bf16[512,128]{1,0:T(8,128)(2,1)S(1)} collective-permute-done((bf16[512,128]{1,0:T(8,128)(2,1)S(1)}, bf16[512,128]{1,0:T(8,128)(2,1)S(1)}, u32[]{:S(2)}, u32[]{:S(2)}) %collective-permute-start.19) | collective-permute-done | bytes 131104 | tf_op jit(solution)/shard_map/ppermute | solution.py:576
  71.6 0.9 %shard_map.196 = f32[512,128]{1,0:T(8,128)} custom-call(f32[512,128]{1,0:T(8,128)S(1)} %get-tuple-element.96.direct, bf16[128,128]{1,0:T(8,128)(2,1)S(1)} %copy-done.8, f32[512,128]{1,0:T(8,128)S(1)} %get-tuple-element.97.own, bf16[1024,128]{1,0:T(8,128)(2,1)S(1)} %collective-permute-done.15.refs_0_, bf16[512,128]{1,0:T(8,128)(2,1)S(1)} %collective-permute-done.19.refs_1_), custom_call_target="tpu_custom_call" | custom-call | flops 16777216 | bytes 1212416 | tf_op jit(solution)/shard_map/pallas_call | solution.py:44
  72.5 0.6 collective-permute-done.18
  73.0 0.1 add_convert_fusion.1.mine
  73.1 0.1 collective-permute-start.20
  73.2 1.3 %collective-permute-done.20.other = bf16[384,128]{1,0:T(8,128)(2,1)S(1)} collective-permute-done((bf16[384,128]{1,0:T(8,128)(2,1)S(1)}, bf16[384,128]{1,0:T(8,128)(2,1)S(1)}, u32[]{:S(2)}, u32[]{:S(2)}) %collective-permute-start.20) | collective-permute-done | bytes 98336 | tf_op jit(solution)/shard_map/ppermute | solution.py:576
  74.5 0.8 %shard_map.197 = f32[768,128]{1,0:T(8,128)} custom-call(bf16[384,128]{1,0:T(8,128)(2,1)S(1)} %add_convert_fusion.1.mine, bf16[384,128]{1,0:T(8,128)(2,1)S(1)} %collective-permute-done.20.other), custom_call_target="tpu_custom_call" | custom-call | bytes 589824 | tf_op jit(solution)/shard_map/pallas_call | solution.py:44
  (59 shorter events, 0.3 us)
Async XLA Ops:
  2.2 11.9 %collective-permute-start = (bf16[576,128]{1,0:T(8,128)(2,1)}, bf16[576,128]{1,0:T(8,128)(2,1)S(1)}, u32[]{:S(2)}, u32[]{:S(2)}) collective-permute-start(bf16[576,128]{1,0:T(8,128)(2,1)} %get-tuple-element.60.message.refs_3_), channel_id=1, source_target_pairs={{0,4},{4,8},{8,12},{12,16},{16,20},{20,24},{24,28},{28,0},{1,5},{5... | collective-permute-start | bytes 442376 | tf_op jit(solution)/shard_map/ppermute | solution.py:22
  2.7 11.4 %collective-permute-start.1 = (bf16[576,128]{1,0:T(8,128)(2,1)}, bf16[576,128]{1,0:T(8,128)(2,1)S(1)}, u32[]{:S(2)}, u32[]{:S(2)}) collective-permute-start(bf16[576,128]{1,0:T(8,128)(2,1)} %get-tuple-element.60.message.refs_3_), channel_id=1, source_target_pairs={{0,28},{4,0},{8,4},{12,8},{16,12},{20,16},{24,20},{28,24},{1,29},{... | collective-permute-start | bytes 442376 | tf_op jit(solution)/shard_map/ppermute | solution.py:22
  5.6 11.3 %collective-permute-start.2 = (bf16[576,128]{1,0:T(8,128)(2,1)}, bf16[576,128]{1,0:T(8,128)(2,1)S(1)}, u32[]{:S(2)}, u32[]{:S(2)}) collective-permute-start(bf16[576,128]{1,0:T(8,128)(2,1)} %get-tuple-element.60.message.refs_3_), channel_id=1, source_target_pairs={{0,1},{1,0},{2,3},{3,2},{4,5},{5,4},{6,7},{7,6},{8,9},{9,8},{10,11... | collective-permute-start | bytes 442376 | tf_op jit(solution)/shard_map/ppermute | solution.py:576
  7.9 13.5 %collective-permute-start.3 = (bf16[576,128]{1,0:T(8,128)(2,1)}, bf16[576,128]{1,0:T(8,128)(2,1)S(1)}, u32[]{:S(2)}, u32[]{:S(2)}) collective-permute-start(bf16[576,128]{1,0:T(8,128)(2,1)} %get-tuple-element.60.message.refs_3_), channel_id=1, source_target_pairs={{0,2},{1,3},{2,0},{3,1},{4,6},{5,7},{6,4},{7,5},{8,10},{9,11},{10,... | collective-permute-start | bytes 442376 | tf_op jit(solution)/shard_map/ppermute | solution.py:576
  10.5 10.9 %collective-permute-start.4 = (bf16[576,128]{1,0:T(8,128)(2,1)}, bf16[576,128]{1,0:T(8,128)(2,1)S(1)}, u32[]{:S(2)}, u32[]{:S(2)}) collective-permute-start(bf16[576,128]{1,0:T(8,128)(2,1)} %get-tuple-element.60.message.refs_3_), channel_id=1, source_target_pairs={{0,3},{1,2},{2,1},{3,0},{4,7},{5,6},{6,5},{7,4},{8,11},{9,10},{10,... | collective-permute-start | bytes 442376 | tf_op jit(solution)/shard_map/ppermute | solution.py:576
  11.2 0.7 copy-start.12
  11.2 0.7 copy-start.13
  11.2 0.7 copy-start.9
  11.2 0.7 copy-start.10
  11.2 0.7 copy-start.11
  11.9 1.2 %copy-start.1 = (s32[1,1,16,128,128]{4,3,2,1,0:T(8,128)S(1)}, s32[1,1,16,128,128]{4,3,2,1,0:T(8,128)}, u32[]{:S(2)}) copy-start(s32[1,1,16,128,128]{4,3,2,1,0:T(8,128)} %param.21) | copy-start | bytes 3145732
  13.1 1.0 %copy-start.7 = (bf16[128,128]{1,0:T(8,128)(2,1)S(1)}, bf16[128,128]{1,0:T(8,128)(2,1)}, u32[]{:S(2)}) copy-start(bf16[128,128]{1,0:T(8,128)(2,1)} %w_recv.3) | copy-start | bytes 98308
  13.1 1.0 %copy-start.8 = (bf16[128,128]{1,0:T(8,128)(2,1)S(1)}, bf16[128,128]{1,0:T(8,128)(2,1)}, u32[]{:S(2)}) copy-start(bf16[128,128]{1,0:T(8,128)(2,1)} %w_send.3) | copy-start | bytes 98308
  13.1 1.0 %copy-start.14 = (bf16[576,128]{1,0:T(8,128)(2,1)S(1)}, bf16[576,128]{1,0:T(8,128)(2,1)}, u32[]{:S(2)}) copy-start(bf16[576,128]{1,0:T(8,128)(2,1)} %get-tuple-element.60.message.refs_3_) | copy-start | bytes 442372
  13.1 1.0 %copy-start.21 = (bf16[16,384]{1,0:T(8,128)(2,1)S(1)}, bf16[16,384]{1,0:T(8,128)(2,1)}, u32[]{:S(2)}) copy-start(bf16[16,384]{1,0:T(8,128)(2,1)} %get-tuple-element.59.weight_parts.refs_2_) | copy-start | bytes 36868
  16.9 10.1 %copy-start.15 = (bf16[576,128]{1,0:T(8,128)(2,1)}, bf16[576,128]{1,0:T(8,128)(2,1)S(1)}, u32[]{:S(2)}) copy-start(bf16[576,128]{1,0:T(8,128)(2,1)S(1)} %collective-permute-done.2.refs_3_.refs_4_) | copy-start | bytes 442372
  21.4 5.6 %copy-start.17 = (bf16[576,128]{1,0:T(8,128)(2,1)}, bf16[576,128]{1,0:T(8,128)(2,1)S(1)}, u32[]{:S(2)}) copy-start(bf16[576,128]{1,0:T(8,128)(2,1)S(1)} %collective-permute-done.3.refs_4_.refs_5_) | copy-start | bytes 442372
  21.4 5.6 %copy-start.19 = (bf16[576,128]{1,0:T(8,128)(2,1)}, bf16[576,128]{1,0:T(8,128)(2,1)S(1)}, u32[]{:S(2)}) copy-start(bf16[576,128]{1,0:T(8,128)(2,1)S(1)} %collective-permute-done.4.refs_5_.refs_6_) | copy-start | bytes 442372
  27.0 5.4 %collective-permute-start.5 = (bf16[512,128]{1,0:T(8,128)(2,1)S(1)}, bf16[512,128]{1,0:T(8,128)(2,1)S(1)}, u32[]{:S(2)}, u32[]{:S(2)}) collective-permute-start(bf16[512,128]{1,0:T(8,128)(2,1)S(1)} %get-tuple-element.69), channel_id=1, source_target_pairs={{0,4},{4,8},{8,12},{12,16},{16,20},{20,24},{24,28},{28,0},{1,5},{5... | collective-permute-start | bytes 393224 | tf_op jit(solution)/shard_map/ppermute | solution.py:22
  27.1 5.3 %collective-permute-start.6 = (bf16[512,128]{1,0:T(8,128)(2,1)S(1)}, bf16[512,128]{1,0:T(8,128)(2,1)S(1)}, u32[]{:S(2)}, u32[]{:S(2)}) collective-permute-start(bf16[512,128]{1,0:T(8,128)(2,1)S(1)} %get-tuple-element.70), channel_id=1, source_target_pairs={{0,28},{4,0},{8,4},{12,8},{16,12},{20,16},{24,20},{28,24},{1,29},{... | collective-permute-start | bytes 393224 | tf_op jit(solution)/shard_map/ppermute | solution.py:22
  29.7 2.7 %copy-start = (bf16[512,128]{1,0:T(8,128)(2,1)S(1)}, bf16[512,128]{1,0:T(8,128)(2,1)}, u32[]{:S(2)}) copy-start(bf16[512,128]{1,0:T(8,128)(2,1)} %latent.7) | copy-start | bytes 393220
  29.7 2.7 %copy-start.2 = (bf16[512,128]{1,0:T(8,128)(2,1)S(1)}, bf16[512,128]{1,0:T(8,128)(2,1)}, u32[]{:S(2)}) copy-start(bf16[512,128]{1,0:T(8,128)(2,1)} %cotangent.3) | copy-start | bytes 393220
  29.7 2.7 %copy-start.3 = (bf16[128,128]{1,0:T(8,128)(2,1)S(1)}, bf16[128,128]{1,0:T(8,128)(2,1)}, u32[]{:S(2)}) copy-start(bf16[128,128]{1,0:T(8,128)(2,1)} %w_edge_out.3) | copy-start | bytes 98308
  29.7 2.7 %copy-start.4 = (bf16[128,128]{1,0:T(8,128)(2,1)S(1)}, bf16[128,128]{1,0:T(8,128)(2,1)}, u32[]{:S(2)}) copy-start(bf16[128,128]{1,0:T(8,128)(2,1)} %w_node_self.3) | copy-start | bytes 98308
  29.7 2.8 %copy-start.5 = (bf16[128,128]{1,0:T(8,128)(2,1)S(1)}, bf16[128,128]{1,0:T(8,128)(2,1)}, u32[]{:S(2)}) copy-start(bf16[128,128]{1,0:T(8,128)(2,1)} %w_node_msg.1) | copy-start | bytes 98308
  29.7 2.7 %copy-start.6 = (bf16[128,128]{1,0:T(8,128)(2,1)S(1)}, bf16[128,128]{1,0:T(8,128)(2,1)}, u32[]{:S(2)}) copy-start(bf16[128,128]{1,0:T(8,128)(2,1)} %w_node_out.1) | copy-start | bytes 98308
  34.3 9.4 %collective-permute-start.8 = (bf16[1024,128]{1,0:T(8,128)(2,1)}, bf16[1024,128]{1,0:T(8,128)(2,1)S(1)}, u32[]{:S(2)}, u32[]{:S(2)}) collective-permute-start(bf16[1024,128]{1,0:T(8,128)(2,1)} %get-tuple-element.82), channel_id=1, source_target_pairs={{0,4},{4,8},{8,12},{12,16},{16,20},{20,24},{24,28},{28,0},{1,5},{5... | collective-permute-start | bytes 786440 | tf_op jit(solution)/shard_map/ppermute | solution.py:22
  34.3 9.4 %collective-permute-start.9 = (bf16[1024,128]{1,0:T(8,128)(2,1)S(1)}, bf16[1024,128]{1,0:T(8,128)(2,1)S(1)}, u32[]{:S(2)}, u32[]{:S(2)}) collective-permute-start(bf16[1024,128]{1,0:T(8,128)(2,1)S(1)} %get-tuple-element.83.refs_0_), channel_id=1, source_target_pairs={{0,28},{4,0},{8,4},{12,8},{16,12},{20,16},{24,20},{28,24},{1,29},{... | collective-permute-start | bytes 786440 | tf_op jit(solution)/shard_map/ppermute | solution.py:22
  38.0 4.6 %collective-permute-start.7 = (bf16[256,128]{1,0:T(8,128)(2,1)}, bf16[256,128]{1,0:T(8,128)(2,1)S(1)}, u32[]{:S(2)}, u32[]{:S(2)}) collective-permute-start(bf16[256,128]{1,0:T(8,128)(2,1)} %get-tuple-element.81), channel_id=1, source_target_pairs={{0,1},{1,0},{2,3},{3,2},{4,5},{5,4},{6,7},{7,6},{8,9},{9,8},{10,11... | collective-permute-start | bytes 196616 | tf_op jit(solution)/shard_map/ppermute | solution.py:576
  38.9 4.9 %copy-start.18 = (bf16[576,128]{1,0:T(8,128)(2,1)S(1)}, bf16[576,128]{1,0:T(8,128)(2,1)}, u32[]{:S(2)}) copy-start(bf16[576,128]{1,0:T(8,128)(2,1)} %copy-done.17) | copy-start | bytes 442372
  38.9 5.0 %copy-start.20 = (bf16[576,128]{1,0:T(8,128)(2,1)S(1)}, bf16[576,128]{1,0:T(8,128)(2,1)}, u32[]{:S(2)}) copy-start(bf16[576,128]{1,0:T(8,128)(2,1)} %copy-done.19) | copy-start | bytes 442372
  42.5 1.3 %copy-start.16 = (bf16[576,128]{1,0:T(8,128)(2,1)S(1)}, bf16[576,128]{1,0:T(8,128)(2,1)}, u32[]{:S(2)}) copy-start(bf16[576,128]{1,0:T(8,128)(2,1)} %copy-done.15) | copy-start | bytes 442372
  43.7 7.2 %collective-permute-start.10 = (bf16[128,128]{1,0:T(8,128)(2,1)S(1)}, bf16[128,128]{1,0:T(8,128)(2,1)S(1)}, u32[]{:S(2)}, u32[]{:S(2)}) collective-permute-start(bf16[128,128]{1,0:T(8,128)(2,1)S(1)} %get-tuple-element.86), channel_id=1, source_target_pairs={{0,2},{1,3},{2,0},{3,1},{4,6},{5,7},{6,4},{7,5},{8,10},{9,11},{10,... | collective-permute-start | bytes 98312 | tf_op jit(solution)/shard_map/ppermute | solution.py:576
  51.0 1.3 %collective-permute-start.11 = (bf16[192,128]{1,0:T(8,128)(2,1)S(1)}, bf16[192,128]{1,0:T(8,128)(2,1)S(1)}, u32[]{:S(2)}, u32[]{:S(2)}) collective-permute-start(bf16[192,128]{1,0:T(8,128)(2,1)S(1)} %broadcast_select_fusion), channel_id=1, source_target_pairs={{0,4},{4,0},{8,12},{12,8},{16,20},{20,16},{24,28},{28,24},{1,5},{5... | collective-permute-start | bytes 147464 | tf_op jit(solution)/shard_map/ppermute | solution.py:576
  51.1 13.0 %collective-permute-start.15 = (bf16[1024,128]{1,0:T(8,128)(2,1)S(1)}, bf16[1024,128]{1,0:T(8,128)(2,1)S(1)}, u32[]{:S(2)}, u32[]{:S(2)}) collective-permute-start(bf16[1024,128]{1,0:T(8,128)(2,1)S(1)} %get-tuple-element.94), channel_id=1, source_target_pairs={{0,1},{1,0},{2,3},{3,2},{4,5},{5,4},{6,7},{7,6},{8,9},{9,8},{10,11... | collective-permute-start | bytes 786440 | tf_op jit(solution)/shard_map/ppermute | solution.py:576
  52.3 9.6 %collective-permute-start.12 = (bf16[192,128]{1,0:T(8,128)(2,1)S(1)}, bf16[192,128]{1,0:T(8,128)(2,1)S(1)}, u32[]{:S(2)}, u32[]{:S(2)}) collective-permute-start(bf16[192,128]{1,0:T(8,128)(2,1)S(1)} %add_convert_fusion.2.refs_0_), channel_id=1, source_target_pairs={{0,1},{1,0},{2,3},{3,2},{4,5},{5,4},{6,7},{7,6},{8,9},{9,8},{10,11... | collective-permute-start | bytes 147464 | tf_op jit(solution)/shard_map/ppermute | solution.py:576
  53.3 8.6 %collective-permute-start.13 = (bf16[192,128]{1,0:T(8,128)(2,1)S(1)}, bf16[192,128]{1,0:T(8,128)(2,1)S(1)}, u32[]{:S(2)}, u32[]{:S(2)}) collective-permute-start(bf16[192,128]{1,0:T(8,128)(2,1)S(1)} %add_convert_fusion.2.refs_0_), channel_id=1, source_target_pairs={{0,2},{1,3},{2,0},{3,1},{4,6},{5,7},{6,4},{7,5},{8,10},{9,11},{10,... | collective-permute-start | bytes 147464 | tf_op jit(solution)/shard_map/ppermute | solution.py:576
  55.9 8.2 %collective-permute-start.14 = (bf16[192,128]{1,0:T(8,128)(2,1)S(1)}, bf16[192,128]{1,0:T(8,128)(2,1)S(1)}, u32[]{:S(2)}, u32[]{:S(2)}) collective-permute-start(bf16[192,128]{1,0:T(8,128)(2,1)S(1)} %add_convert_fusion.2.refs_0_), channel_id=1, source_target_pairs={{0,3},{1,2},{2,1},{3,0},{4,7},{5,6},{6,5},{7,4},{8,11},{9,10},{10,... | collective-permute-start | bytes 147464 | tf_op jit(solution)/shard_map/ppermute | solution.py:576
  64.2 7.4 %collective-permute-start.19 = (bf16[512,128]{1,0:T(8,128)(2,1)S(1)}, bf16[512,128]{1,0:T(8,128)(2,1)S(1)}, u32[]{:S(2)}, u32[]{:S(2)}) collective-permute-start(bf16[512,128]{1,0:T(8,128)(2,1)S(1)} %add_convert_fusion), channel_id=1, source_target_pairs={{0,2},{1,3},{2,0},{3,1},{4,6},{5,7},{6,4},{7,5},{8,10},{9,11},{10,... | collective-permute-start | bytes 393224 | tf_op jit(solution)/shard_map/ppermute | solution.py:576
  64.3 8.2 %collective-permute-start.16 = (bf16[384,128]{1,0:T(8,128)(2,1)S(1)}, bf16[384,128]{1,0:T(8,128)(2,1)S(1)}, u32[]{:S(2)}, u32[]{:S(2)}) collective-permute-start(bf16[384,128]{1,0:T(8,128)(2,1)S(1)} %shard_map.195), channel_id=1, source_target_pairs={{0,8},{4,12},{8,0},{12,4},{16,24},{20,28},{24,16},{28,20},{1,9},{5... | collective-permute-start | bytes 294920 | tf_op jit(solution)/shard_map/ppermute | solution.py:576
  65.1 7.4 %collective-permute-start.17 = (bf16[384,128]{1,0:T(8,128)(2,1)S(1)}, bf16[384,128]{1,0:T(8,128)(2,1)S(1)}, u32[]{:S(2)}, u32[]{:S(2)}) collective-permute-start(bf16[384,128]{1,0:T(8,128)(2,1)S(1)} %shard_map.195), channel_id=1, source_target_pairs={{0,16},{4,20},{8,24},{12,28},{16,0},{20,4},{24,8},{28,12},{1,17},{... | collective-permute-start | bytes 294920 | tf_op jit(solution)/shard_map/ppermute | solution.py:576
  67.5 5.5 %collective-permute-start.18 = (bf16[384,128]{1,0:T(8,128)(2,1)S(1)}, bf16[384,128]{1,0:T(8,128)(2,1)S(1)}, u32[]{:S(2)}, u32[]{:S(2)}) collective-permute-start(bf16[384,128]{1,0:T(8,128)(2,1)S(1)} %shard_map.195), channel_id=1, source_target_pairs={{0,24},{4,28},{8,16},{12,20},{16,8},{20,12},{24,0},{28,4},{1,25},{... | collective-permute-start | bytes 294920 | tf_op jit(solution)/shard_map/ppermute | solution.py:576
  73.1 1.4 %collective-permute-start.20 = (bf16[384,128]{1,0:T(8,128)(2,1)S(1)}, bf16[384,128]{1,0:T(8,128)(2,1)S(1)}, u32[]{:S(2)}, u32[]{:S(2)}) collective-permute-start(bf16[384,128]{1,0:T(8,128)(2,1)S(1)} %add_convert_fusion.1.mine), channel_id=1, source_target_pairs={{0,4},{4,0},{8,12},{12,8},{16,20},{20,16},{24,28},{28,24},{1,5},{5... | collective-permute-start | bytes 294920 | tf_op jit(solution)/shard_map/ppermute | solution.py:576
